TPU v7x, 32 devices: a whole 2x2x4 slice. The times are simulated.
32 devices in a mesh: grp: 2 (over y), row: 8 (over z, core), col: 2 (over x).
Axes of the slice: x: 2, y: 2, z: 4, core: 2. Of those that a mesh axis runs over, the one named last changes fastest.
Arguments:
- sketch_base: int32 [2], P('grp'), parts along dimension 0, may hold values from 0 to 999999
- states: bfloat16 [4096, 8192], P(('grp', 'row'), 'col'), parts along dimension 0
Outputs:
- loadings: float32 [8192, 128], P(('col', 'row'), 'grp'), parts along dimension 1
- sketch_factor: float32 [128, 64], P('grp'), parts along dimension 0
There are 2 independent parts, one for each index of `grp`. A program takes and returns all parts, laid end to end along the dimension named above; each array names one. Nothing has to cross between parts.
All inputs are finite; a program needn't handle non-finite values.
Results may differ from a plain program's by a relative error of at most 0.011.
Values may be sent and summed in bfloat16 or wider, within the bound.
No kernel may reach another device: no remote copies, remote signals or barrier semaphores. Data moves between devices by JAX's collectives and lax.ppermute only.
A program may use at most 64 MiB of HBM per device.

v0:
```python
import math

import jax
import jax.numpy as jnp
from jax import lax
from jax.sharding import PartitionSpec as P

RANK = 64
POWER = 4


shift_ratio = 0.005


def scramble(value):
    value = value ^ jnp.right_shift(value, 16) & 65535
    value = value * 73244475
    value = value ^ jnp.right_shift(value, 16) & 65535
    value = value * 73244475
    value = value ^ jnp.right_shift(value, 16) & 65535
    return value


def sketch_table(base_value, feature_index, rank):
    counter = feature_index[:, None] * rank + jnp.arange(rank, dtype=jnp.int32)[None, :]
    offset = scramble(base_value)
    total = jnp.zeros(counter.shape, jnp.float32)
    for j in range(4):
        hashed = scramble(counter * 4 + j + offset)
        total = total + (hashed & 16777215).astype(jnp.float32) * (1.0 / 16777216.0)
    return ((total - 2.0) * 1.7320508).astype(jnp.bfloat16)


def local_gram(basis):
    return jnp.dot(basis.T, basis, precision=lax.Precision.HIGHEST)


def shifted(whole_gram):
    identity = jnp.eye(whole_gram.shape[0], dtype=whole_gram.dtype)
    return whole_gram + shift_ratio * jnp.trace(whole_gram) * identity


def second_pass(first, second_gram):
    lower_two = jnp.linalg.cholesky(second_gram)
    return jax.scipy.linalg.solve_triangular(lower_two, first.T, lower=True).T


def orthonormal_block(sketch):
    whole_gram = lax.psum(local_gram(sketch), "row")
    lower = jnp.linalg.cholesky(shifted(whole_gram))
    first = jax.scipy.linalg.solve_triangular(lower, sketch.T, lower=True).T
    second_gram = lax.psum(local_gram(first), "row")
    return (second_pass(first, second_gram), lower)


def transposed_term(states, narrow_basis):
    return lax.dot_general(
        states, narrow_basis, (((0,), (0,)), ((), ())), preferred_element_type=jnp.float32
    )


def back_weights(states, narrow_basis):
    partial_back = lax.dot_general(
        states, narrow_basis, (((0,), (0,)), ((), ())), preferred_element_type=jnp.float32
    )
    return lax.psum(partial_back, "row").astype(jnp.bfloat16)


def per_device(sketch_base, states):
    width_local = states.shape[1]
    rows_total = states.shape[0] * lax.axis_size("row")
    width_total = width_local * lax.axis_size("col")
    feature_index = lax.axis_index("col") * width_local + jnp.arange(width_local, dtype=jnp.int32)
    omega = sketch_table(sketch_base[0], feature_index, RANK)

    def row_basis(right):
        partial_sketch = jnp.dot(states, right, preferred_element_type=jnp.float32)
        sketch = lax.psum(partial_sketch, "col")
        basis_new, lower = orthonormal_block(sketch)
        return (basis_new.astype(jnp.bfloat16), lower)

    basis, first_lower = row_basis(omega)
    factor = first_lower * (1.0 / math.sqrt(rows_total * width_total))
    for step in range(POWER):
        weights = back_weights(states, basis)
        basis, unused = row_basis(weights)
    return (
        lax.psum_scatter(transposed_term(states, basis), "row", scatter_dimension=0, tiled=True),
        factor,
    )


def solution(mesh):
    placed = (P("grp"), P(("grp", "row"), "col"))
    return jax.shard_map(
        per_device,
        mesh=mesh,
        in_specs=placed,
        out_specs=(P(("col", "row"), "grp"), P("grp", None)),
        check_vma=False,
    )
```

profile of v0, /device:TPU:0, one launch (start us, length us, event | category | flops | bytes accessed | tf_op | source)
XLA Modules:
  0.0 809.6 jit_solution(7497336272623781154)
XLA Ops:
  11.8 23.6 %all-reduce.10.cloned.1.call-done = f32[256,64]{0,1:T(8,128)} async-done(((f32[256,64]{0,1:T(8,128)}), f32[256,64]{0,1:T(8,128)}) %all-reduce.10.cloned.1.call-update) | async-done | bytes 65552 | tf_op jit(solution)/shard_map/psum | solution.py:78
  36.4 28.1 %psum.134 = f32[64,64]{0,1:T(8,128)S(1)} all-reduce(f32[64,64]{0,1:T(8,128)S(1)} %fusion.89), channel_id=1, replica_groups=mesh['grp'=2,'row'=8,'col'=2] {'row'}, use_global_device_ids=true, to_apply=%region_1.0 | all-reduce | flops 4096 | bytes 32768 | tf_op jit(solution)/shard_map/psum | solution.py:49
  66.0 5.8 cholesky.164
  80.0 25.9 %psum.135 = f32[64,64]{0,1:T(8,128)S(1)} all-reduce(f32[64,64]{0,1:T(8,128)S(1)} %fusion.90), channel_id=1, replica_groups=mesh['grp'=2,'row'=8,'col'=2] {'row'}, use_global_device_ids=true, to_apply=%region_5.8 | all-reduce | flops 4096 | bytes 32768 | tf_op jit(solution)/shard_map/psum | solution.py:52
  106.0 5.8 cholesky.175
  113.2 4.9 custom-call.15
  118.9 56.9 %all-reduce.19 = bf16[4096,64]{0,1:T(8,128)(2,1)} all-reduce(f32[4096,64]{0,1:T(8,128)S(1)} %convolution_bitcast_fusion.4), channel_id=1, replica_groups=mesh['grp'=2,'row'=8,'col'=2] {'row'}, use_global_device_ids=true, to_apply=%region_6.9 | all-reduce | flops 262144 | bytes 1572864 | tf_op jit(solution)/shard_map/psum | solution.py:66
  178.2 20.9 %all-reduce.12.cloned.1.call-done = f32[256,64]{0,1:T(8,128)} async-done(((f32[256,64]{0,1:T(8,128)}), f32[256,64]{0,1:T(8,128)}) %all-reduce.12.cloned.1.call-update) | async-done | bytes 65552 | tf_op jit(solution)/shard_map/psum | solution.py:78
  200.3 28.1 %psum.138 = f32[64,64]{0,1:T(8,128)S(1)} all-reduce(f32[64,64]{0,1:T(8,128)S(1)} %fusion.91), channel_id=1, replica_groups=mesh['grp'=2,'row'=8,'col'=2] {'row'}, use_global_device_ids=true, to_apply=%region_8.11 | all-reduce | flops 4096 | bytes 32768 | tf_op jit(solution)/shard_map/psum | solution.py:49
  229.8 5.8 cholesky.186
  243.2 26.1 %psum.139 = f32[64,64]{0,1:T(8,128)S(1)} all-reduce(f32[64,64]{0,1:T(8,128)S(1)} %fusion.92), channel_id=1, replica_groups=mesh['grp'=2,'row'=8,'col'=2] {'row'}, use_global_device_ids=true, to_apply=%region_10.13 | all-reduce | flops 4096 | bytes 32768 | tf_op jit(solution)/shard_map/psum | solution.py:52
  269.4 5.8 cholesky.197
  282.3 56.9 %all-reduce.20 = bf16[4096,64]{0,1:T(8,128)(2,1)} all-reduce(f32[4096,64]{0,1:T(8,128)S(1)} %convolution_bitcast_fusion.3), channel_id=1, replica_groups=mesh['grp'=2,'row'=8,'col'=2] {'row'}, use_global_device_ids=true, to_apply=%region_11.14 | all-reduce | flops 262144 | bytes 1572864 | tf_op jit(solution)/shard_map/psum | solution.py:66
  341.6 20.9 %all-reduce.14.cloned.1.call-done = f32[256,64]{0,1:T(8,128)} async-done(((f32[256,64]{0,1:T(8,128)}), f32[256,64]{0,1:T(8,128)}) %all-reduce.14.cloned.1.call-update) | async-done | bytes 65552 | tf_op jit(solution)/shard_map/psum | solution.py:78
  363.7 28.1 %psum.142 = f32[64,64]{0,1:T(8,128)S(1)} all-reduce(f32[64,64]{0,1:T(8,128)S(1)} %fusion.93), channel_id=1, replica_groups=mesh['grp'=2,'row'=8,'col'=2] {'row'}, use_global_device_ids=true, to_apply=%region_13.16 | all-reduce | flops 4096 | bytes 32768 | tf_op jit(solution)/shard_map/psum | solution.py:49
  393.2 5.8 cholesky.208
  406.6 25.9 %psum.143 = f32[64,64]{0,1:T(8,128)S(1)} all-reduce(f32[64,64]{0,1:T(8,128)S(1)} %fusion.94), channel_id=1, replica_groups=mesh['grp'=2,'row'=8,'col'=2] {'row'}, use_global_device_ids=true, to_apply=%region_15.18 | all-reduce | flops 4096 | bytes 32768 | tf_op jit(solution)/shard_map/psum | solution.py:52
  432.6 5.8 cholesky.219
  445.5 56.9 %all-reduce.21 = bf16[4096,64]{0,1:T(8,128)(2,1)} all-reduce(f32[4096,64]{0,1:T(8,128)S(1)} %convolution_bitcast_fusion.2), channel_id=1, replica_groups=mesh['grp'=2,'row'=8,'col'=2] {'row'}, use_global_device_ids=true, to_apply=%region_16.19 | all-reduce | flops 262144 | bytes 1572864 | tf_op jit(solution)/shard_map/psum | solution.py:66
  504.8 20.9 %all-reduce.16.cloned.1.call-done = f32[256,64]{0,1:T(8,128)} async-done(((f32[256,64]{0,1:T(8,128)}), f32[256,64]{0,1:T(8,128)}) %all-reduce.16.cloned.1.call-update) | async-done | bytes 65552 | tf_op jit(solution)/shard_map/psum | solution.py:78
  526.9 28.1 %psum.146 = f32[64,64]{0,1:T(8,128)S(1)} all-reduce(f32[64,64]{0,1:T(8,128)S(1)} %fusion.95), channel_id=1, replica_groups=mesh['grp'=2,'row'=8,'col'=2] {'row'}, use_global_device_ids=true, to_apply=%region_18.21 | all-reduce | flops 4096 | bytes 32768 | tf_op jit(solution)/shard_map/psum | solution.py:49
  556.4 5.8 cholesky.230
  569.8 26.2 %psum.147 = f32[64,64]{0,1:T(8,128)S(1)} all-reduce(f32[64,64]{0,1:T(8,128)S(1)} %fusion.96), channel_id=1, replica_groups=mesh['grp'=2,'row'=8,'col'=2] {'row'}, use_global_device_ids=true, to_apply=%region_20.23 | all-reduce | flops 4096 | bytes 32768 | tf_op jit(solution)/shard_map/psum | solution.py:52
  596.1 5.8 cholesky.241
  608.9 56.9 %all-reduce.22 = bf16[4096,64]{0,1:T(8,128)(2,1)} all-reduce(f32[4096,64]{0,1:T(8,128)S(1)} %convolution_bitcast_fusion.1), channel_id=1, replica_groups=mesh['grp'=2,'row'=8,'col'=2] {'row'}, use_global_device_ids=true, to_apply=%region_21.24 | all-reduce | flops 262144 | bytes 1572864 | tf_op jit(solution)/shard_map/psum | solution.py:66
  668.3 20.9 %all-reduce.18.cloned.1.call-done = f32[256,64]{0,1:T(8,128)} async-done(((f32[256,64]{0,1:T(8,128)}), f32[256,64]{0,1:T(8,128)}) %all-reduce.18.cloned.1.call-update) | async-done | bytes 65552 | tf_op jit(solution)/shard_map/psum | solution.py:78
  690.3 28.1 %psum.150 = f32[64,64]{0,1:T(8,128)S(1)} all-reduce(f32[64,64]{0,1:T(8,128)S(1)} %fusion.97), channel_id=1, replica_groups=mesh['grp'=2,'row'=8,'col'=2] {'row'}, use_global_device_ids=true, to_apply=%region_23.26 | all-reduce | flops 4096 | bytes 32768 | tf_op jit(solution)/shard_map/psum | solution.py:49
  719.8 5.8 cholesky.252
  733.2 25.9 %psum.151 = f32[64,64]{0,1:T(8,128)S(1)} all-reduce(f32[64,64]{0,1:T(8,128)S(1)} %fusion.98), channel_id=1, replica_groups=mesh['grp'=2,'row'=8,'col'=2] {'row'}, use_global_device_ids=true, to_apply=%region_25.28 | all-reduce | flops 4096 | bytes 32768 | tf_op jit(solution)/shard_map/psum | solution.py:52
  759.3 5.8 cholesky.263
  766.5 4.9 custom-call.23
  773.1 29.6 %reduce-scatter.2.cloned.1.call-done = f32[512,64]{0,1:T(8,128)} async-done(((f32[4096,64]{0,1:T(8,128)}), f32[512,64]{0,1:T(8,128)}) %reduce-scatter.2.cloned.1.call-update) | async-done | bytes 131088 | tf_op jit(solution)/shard_map/reduce_scatter | solution.py:88
  (113 shorter events, 87.6 us)
Async XLA Ops:
  7.2 1.6 copy-start
  7.2 28.1 %all-reduce.10.cloned.1.call-start = ((), (), s32[]{:S(2)}) async-start(), calls=%async_computation.1 | async-start | bytes 131072 | tf_op jit(solution)/shard_map/psum | solution.py:78
  11.7 187.4 %all-reduce.12.cloned.1.call-start = ((), (), s32[]{:S(2)}) async-start(), calls=%async_computation.2 | async-start | bytes 131072 | tf_op jit(solution)/shard_map/psum | solution.py:78
  178.2 184.4 %all-reduce.14.cloned.1.call-start = ((), (), s32[]{:S(2)}) async-start(), calls=%async_computation.3 | async-start | bytes 131072 | tf_op jit(solution)/shard_map/psum | solution.py:78
  341.6 184.2 %all-reduce.16.cloned.1.call-start = ((), (), s32[]{:S(2)}) async-start(), calls=%async_computation.4 | async-start | bytes 131072 | tf_op jit(solution)/shard_map/psum | solution.py:78
  504.8 184.4 %all-reduce.18.cloned.1.call-start = ((), (), s32[]{:S(2)}) async-start(), calls=%async_computation.5 | async-start | bytes 131072 | tf_op jit(solution)/shard_map/psum | solution.py:78
  668.2 134.5 %reduce-scatter.2.cloned.1.call-start = ((), (), s32[]{:S(2)}) async-start(), calls=%async_computation.6 | async-start | bytes 1179648 | tf_op jit(solution)/shard_map/reduce_scatter | solution.py:88
Sparse Core Ops, SparseCore 0:
  11.8 23.4 all-reduce.9
  178.3 20.8 all-reduce.11
  341.7 20.8 all-reduce.13
  504.9 20.8 all-reduce.15
  668.3 20.8 all-reduce.17
  773.3 29.4 reduce-scatter.1
where the time goes:
time: 811 us; the launch traced here: 810 us
  blocking collectives  498 us (61%)
  waiting for transfers between devices  137 us (17%)
  other arithmetic  125 us (15%)
  matrix products  29.5 us (4%)
  between operations  18.6 us (2%)
    psum x4, blocking collectives, back_weights(): return lax.psum(partial_back, 'row').astype(jnp.bfloat16)  227 us
    psum x5, blocking collectives, orthonormal_block(): whole_gram = lax.psum(local_gram(sketch), 'row')  141 us
    psum x5, blocking collectives, orthonormal_block(): second_gram = lax.psum(local_gram(first), 'row')  130 us
    psum x5, waiting for transfers between devices, row_basis(): sketch = lax.psum(partial_sketch, 'col')  107 us
    another operation x15, other arithmetic, second_pass(): lower_two = jnp.linalg.cholesky(second_gram)  32.6 us
    another operation x15, other arithmetic, orthonormal_block(): lower = jnp.linalg.cholesky(shifted(whole_gram))  32.6 us
    reduce_scatter x1, waiting for transfers between devices, per_device(): lax.psum_scatter(transposed_term(states, basis), 'row', scatter_dimension...  29.6 us
    another operation x10, other arithmetic, second_pass(): return jax.scipy.linalg.solve_triangular(lower_two, first.T, lower=True).T  27.8 us
  transfers between devices with their start and end apart: 6, of which 6 were waited for; matrix products, arithmetic and copies ran while one was open for 0% of the time, Pallas kernels for 0%

commit v1 on v0

v1 whole, which is shorter than its diff:
```python
import functools
import math

import jax
import jax.numpy as jnp
from jax import lax
from jax.experimental import pallas as pl
from jax.experimental.pallas import tpu as pltpu
from jax.sharding import PartitionSpec as P

RANK = 64
POWER = 4
LANES = 128
SUB = 8


shift_ratio = 0.005


def scramble(value):
    value = value ^ jnp.right_shift(value, 16) & 65535
    value = value * 73244475
    value = value ^ jnp.right_shift(value, 16) & 65535
    value = value * 73244475
    value = value ^ jnp.right_shift(value, 16) & 65535
    return value


def sketch_table(base_value, feature_index, rank):
    counter = feature_index[:, None] * rank + jnp.arange(rank, dtype=jnp.int32)[None, :]
    offset = scramble(base_value)
    total = jnp.zeros(counter.shape, jnp.float32)
    for j in range(4):
        hashed = scramble(counter * 4 + j + offset)
        total = total + (hashed & 16777215).astype(jnp.float32) * (1.0 / 16777216.0)
    return ((total - 2.0) * 1.7320508).astype(jnp.bfloat16)


def three_terms(value):
    high = value.astype(jnp.bfloat16)
    rest = value - high.astype(jnp.float32)
    middle = rest.astype(jnp.bfloat16)
    low = (rest - middle.astype(jnp.float32)).astype(jnp.bfloat16)
    return high, middle, low


def dot_nn(left, right):
    return lax.dot_general(
        left, right, (((1,), (0,)), ((), ())), preferred_element_type=jnp.float32
    )


def dot_nt(left, right):
    return lax.dot_general(
        left, right, (((1,), (1,)), ((), ())), preferred_element_type=jnp.float32
    )


def small_times_wide(small, wide):
    sh, sm, sl = three_terms(small)
    wh, wm, wl = three_terms(wide)
    first = dot_nn(sl, wh) + dot_nn(sm, wm) + dot_nn(sh, wl)
    second = dot_nn(sm, wh) + dot_nn(sh, wm)
    return (first + second) + dot_nn(sh, wh)


def gram_of(wide):
    wh, wm, wl = three_terms(wide)
    hm = dot_nt(wh, wm)
    hl = dot_nt(wh, wl)
    return dot_nt(wh, wh) + ((hm + hm.T) + ((hl + hl.T) + dot_nt(wm, wm)))


def eliminate(matrix):
    size = matrix.shape[0]
    blocks = size // SUB
    row_index = lax.broadcasted_iota(jnp.int32, (SUB, size), 0)
    col_index = lax.broadcasted_iota(jnp.int32, (SUB, size), 1)
    work = [matrix[SUB * i : SUB * (i + 1), :] for i in range(blocks)]
    inverse = [
        jnp.where(col_index == row_index + SUB * i, 1.0, 0.0).astype(jnp.float32)
        for i in range(blocks)
    ]
    upper_rows, inverse_rows = [], []
    for b in range(blocks):
        columns = [
            {
                i: jnp.broadcast_to(work[i][:, SUB * b + j : SUB * b + j + 1], (SUB, size))
                for i in range(b, blocks)
            }
            for j in range(SUB)
        ]
        pivots = jnp.zeros((SUB, size), jnp.float32)
        for k in range(SUB):
            pivot = jnp.broadcast_to(columns[k][b][k : k + 1, :], (SUB, size))
            reciprocal = 1.0 / pivot
            pivots = jnp.where(row_index == k, pivot, pivots)
            work_row = jnp.broadcast_to(work[b][k : k + 1, :], (SUB, size))
            inverse_row = jnp.broadcast_to(inverse[b][k : k + 1, :], (SUB, size))
            later = [
                jnp.broadcast_to(columns[j][b][k : k + 1, :], (SUB, size))
                for j in range(k + 1, SUB)
            ]
            for i in range(b, blocks):
                factor = columns[k][i] * reciprocal
                if i == b:
                    factor = jnp.where(row_index > k, factor, 0.0)
                for j in range(k + 1, SUB):
                    columns[j][i] = columns[j][i] - factor * later[j - k - 1]
                work[i] = work[i] - factor * work_row
                inverse[i] = inverse[i] - factor * inverse_row
        root = lax.rsqrt(pivots)
        upper = work[b] * root
        upper_rows.append(jnp.where(col_index >= row_index + SUB * b, upper, 0.0))
        inverse_rows.append(inverse[b] * root)
    return jnp.concatenate(upper_rows, axis=0), jnp.concatenate(inverse_rows, axis=0)


def shifted(whole_gram):
    size = whole_gram.shape[0]
    diagonal = lax.broadcasted_iota(jnp.int32, (size, size), 0) == lax.broadcasted_iota(
        jnp.int32, (size, size), 1
    )
    on_diagonal = jnp.where(diagonal, whole_gram, 0.0)
    trace = jnp.sum(jnp.sum(on_diagonal, axis=1, keepdims=True), axis=0, keepdims=True)
    return jnp.where(diagonal, whole_gram + shift_ratio * trace, whole_gram)


def both_passes(wide):
    upper, inverse_one = eliminate(shifted(gram_of(wide)))
    first = small_times_wide(inverse_one, wide)
    unused, inverse_two = eliminate(gram_of(first))
    return upper, inverse_one, first, inverse_two


def wide_of(z_ref):
    return jnp.concatenate([z_ref[i] for i in range(z_ref.shape[0])], axis=1)


def narrow_basis(z_ref):
    upper, inverse_one, first, inverse_two = both_passes(wide_of(z_ref))
    return small_times_wide(inverse_two, first).astype(jnp.bfloat16), upper


def power_body(basis, a_ref, p_ref):
    weights = dot_nn(basis, a_ref[...]).astype(jnp.bfloat16)
    forth = dot_nt(weights, a_ref[...])
    width = p_ref.shape[2]
    for i in range(p_ref.shape[0]):
        p_ref[i] = forth[:, width * i : width * (i + 1)]


def orth_kernel(z_ref, basis_ref, upper_ref):
    basis_ref[...], upper_ref[...] = narrow_basis(z_ref)


def power_kernel(basis_ref, a_ref, p_ref):
    power_body(basis_ref[...], a_ref, p_ref)


def orth_power_kernel(z_ref, a_ref, p_ref):
    basis, unused = narrow_basis(z_ref)
    power_body(basis, a_ref, p_ref)


def last_kernel(z_ref, a_ref, out_ref):
    basis, unused = narrow_basis(z_ref)
    out_ref[...] = dot_nn(basis, a_ref[...]).T


def call(kernel, out_shapes, flops, *operands):
    moved = sum(x.size * x.dtype.itemsize for x in operands)
    return pl.pallas_call(
        kernel,
        out_shape=out_shapes,
        in_specs=[pl.BlockSpec(memory_space=pltpu.VMEM)] * len(operands),
        out_specs=jax.tree.map(lambda _: pl.BlockSpec(memory_space=pltpu.VMEM), out_shapes),
        compiler_params=pltpu.CompilerParams(vmem_limit_bytes=40 * 1024 * 1024),
        cost_estimate=pl.CostEstimate(flops=flops, bytes_accessed=moved, transcendentals=0),
    )(*operands)


def from_xor(value, axis, offset):
    size = lax.axis_size(axis)
    return lax.ppermute(value, axis, [(i, i ^ offset) for i in range(size)])


def sum_scatter(parts, n_z, n_col):
    half = parts.shape[0] // 2
    total = parts[:half] + from_xor(parts[half:], "row", 1)
    step = half // n_col
    pieces = [from_xor(total[step * o : step * (o + 1)], "col", o) for o in range(1, n_col)]
    total = functools.reduce(jnp.add, pieces, total[:step])
    pieces = [from_xor(total[o], "row", 2 * o) for o in range(1, n_z)]
    return functools.reduce(jnp.add, pieces, total[0])


def gather_all(own, n_z, n_col):
    chunks = jnp.stack([own] + [from_xor(own, "row", 2 * o) for o in range(1, n_z)])
    chunks = jnp.concatenate([chunks] + [from_xor(chunks, "col", o) for o in range(1, n_col)])
    return jnp.concatenate([chunks, from_xor(chunks, "row", 1)])


def per_device_transposed(sketch_base, states):
    n_row, n_col = lax.axis_size("row"), lax.axis_size("col")
    n_z = n_row // 2
    row, col = lax.axis_index("row"), lax.axis_index("col")
    rows_local, width_local = states.shape
    rows_total, width_total = rows_local * n_row, width_local * n_col
    chunk = rows_local // n_col
    cols = width_local // n_row
    n_chunks = n_row * n_col

    order = [col ^ o for o in range(n_col)]
    relative = jnp.concatenate(
        [lax.dynamic_slice_in_dim(states, o * chunk, chunk, 0) for o in order]
    )

    def block(offset):
        return lax.dynamic_slice_in_dim(relative, (row ^ offset) * cols, cols, 1)

    received = {0: block(0)}
    for offset in sorted(range(1, n_row), reverse=True):
        received[offset] = from_xor(block(offset), "row", offset)

    feature_index = col * width_local + jnp.arange(width_local, dtype=jnp.int32)
    omega = sketch_table(sketch_base[0], feature_index, RANK)
    partial = lax.dot_general(
        omega, relative, (((0,), (1,)), ((), ())), preferred_element_type=jnp.float32
    )
    own = partial[:, :chunk]
    for o in range(1, n_col):
        own = own + from_xor(partial[:, o * chunk : (o + 1) * chunk], "col", o)
    z = gather_all(own, n_z, n_col)

    a = jnp.concatenate(
        [
            received[2 * zo + core][co * chunk : (co + 1) * chunk]
            for core in range(2)
            for co in range(n_col)
            for zo in range(n_z)
        ]
    )

    f32 = jnp.float32
    square = jax.ShapeDtypeStruct((RANK, RANK), f32)
    wide = jax.ShapeDtypeStruct((RANK, rows_total), jnp.bfloat16)
    chunks = jax.ShapeDtypeStruct((n_chunks, RANK, chunk), f32)
    orth_flops = 8 * 64 * 64 * rows_total * 6
    power_flops = 4 * 64 * rows_total * cols

    basis, upper = call(orth_kernel, (wide, square), orth_flops, z)
    factor = upper.T * (1.0 / math.sqrt(rows_total * width_total))
    parts = call(power_kernel, chunks, power_flops, basis, a)
    for step in range(POWER - 1):
        z = gather_all(sum_scatter(parts, n_z, n_col), n_z, n_col)
        parts = call(orth_power_kernel, chunks, orth_flops + power_flops, z, a)
    z = gather_all(sum_scatter(parts, n_z, n_col), n_z, n_col)
    loadings = call(
        last_kernel, jax.ShapeDtypeStruct((cols, RANK), f32), orth_flops + power_flops, z, a
    )
    return loadings, factor


def local_gram(basis):
    return jnp.dot(basis.T, basis, precision=lax.Precision.HIGHEST)


def orthonormal_block(sketch):
    whole_gram = lax.psum(local_gram(sketch), "row")
    identity = jnp.eye(RANK, dtype=jnp.float32)
    lower = jnp.linalg.cholesky(whole_gram + shift_ratio * jnp.trace(whole_gram) * identity)
    first = jax.scipy.linalg.solve_triangular(lower, sketch.T, lower=True).T
    lower_two = jnp.linalg.cholesky(lax.psum(local_gram(first), "row"))
    return jax.scipy.linalg.solve_triangular(lower_two, first.T, lower=True).T, lower


def per_device_slabs(sketch_base, states):
    width_local = states.shape[1]
    rows_total = states.shape[0] * lax.axis_size("row")
    width_total = width_local * lax.axis_size("col")
    feature_index = lax.axis_index("col") * width_local + jnp.arange(width_local, dtype=jnp.int32)
    omega = sketch_table(sketch_base[0], feature_index, RANK)

    def row_basis(right):
        partial_sketch = jnp.dot(states, right, preferred_element_type=jnp.float32)
        basis_new, lower = orthonormal_block(lax.psum(partial_sketch, "col"))
        return basis_new.astype(jnp.bfloat16), lower

    def back(basis):
        return lax.dot_general(
            states, basis, (((0,), (0,)), ((), ())), preferred_element_type=jnp.float32
        )

    basis, first_lower = row_basis(omega)
    factor = first_lower * (1.0 / math.sqrt(rows_total * width_total))
    for step in range(POWER):
        basis, unused = row_basis(lax.psum(back(basis), "row").astype(jnp.bfloat16))
    return lax.psum_scatter(back(basis), "row", scatter_dimension=0, tiled=True), factor


def per_device(sketch_base, states):
    n_row, n_col = lax.axis_size("row"), lax.axis_size("col")
    rows_local, width_local = states.shape
    powers = n_row & (n_row - 1) == 0 and n_col & (n_col - 1) == 0 and n_row > 1
    tiled = rows_local % (n_col * LANES) == 0 and width_local % (n_row * LANES) == 0
    if powers and tiled:
        return per_device_transposed(sketch_base, states)
    return per_device_slabs(sketch_base, states)


def solution(mesh):
    placed = (P("grp"), P(("grp", "row"), "col"))
    return jax.shard_map(
        per_device,
        mesh=mesh,
        in_specs=placed,
        out_specs=(P(("col", "row"), "grp"), P("grp", None)),
        check_vma=False,
    )
```

time: 811 us -> 218 us (0.27)
  blocking collectives: 498 us -> 0 us
  other arithmetic: 125 us -> 0.49 us
  starting transfers between devices: 0.25 us -> 60.7 us
  Pallas kernels: 0 us -> 35.8 us
  matrix products: 29.5 us -> 2.24 us
  waiting for transfers between devices: 137 us -> 113 us
  between operations: 18.6 us -> 1.85 us
    psum x14 -> x0, blocking collectives: 498 us -> none  [the longest x4 227 us: back_weights(): return lax.psum(partial_back, 'row').astype(jnp.bfloat16)]
    another operation x49 -> x5, other arithmetic: 120 us -> 0.05 us  [gather_all(): jnp.stack([own] + [from_xor(own, 'row', 2 * o) for o in range(1, n_z)])]
    ppermute x0 -> x53, waiting for transfers between devices: none -> 113 us  [from_xor(): return lax.ppermute(value, axis, [(i, i ^ offset) for i in range(size)])]
    psum x5 -> x0, waiting for transfers between devices: 107 us -> none  [row_basis(): sketch = lax.psum(partial_sketch, 'col')]
    ppermute x0 -> x53, starting transfers between devices: none -> 60.7 us  [from_xor(): return lax.ppermute(value, axis, [(i, i ^ offset) for i in range(size)])]
    pallas_call x0 -> x6, Pallas kernels: none -> 35.8 us  [call(): pl.pallas_call(kernel, out_shape=out_shapes, in_specs=[pl.BlockSpec(memor...]
    reduce_scatter x1 -> x0, waiting for transfers between devices: 29.6 us -> none  [per_device(): lax.psum_scatter(transposed_term(states, basis), 'row', scatter_dimension...]
    dot_general x20 -> x1, matrix products: 22.6 us -> 2.24 us  [per_device_transposed(): lax.dot_general(omega, relative, (((0,), (1,)), ((), ())), preferred_elem...]
  transfers between devices with their start and end apart: 6 -> 53, of which waited for: 6 -> 43; matrix products, arithmetic and copies ran while one was open for 0% -> 1% of each run, Pallas kernels for 0% -> 0%
where the time goes in v1:
time: 218 us
  waiting for transfers between devices  113 us (52%)
  starting transfers between devices  60.7 us (28%)
  Pallas kernels  35.8 us (16%)
  local copies, waits for them, and re-layouts  3.8 us (2%)
  matrix products  2.24 us (1%)
    ppermute x53, waiting for transfers between devices, from_xor(): return lax.ppermute(value, axis, [(i, i ^ offset) for i in range(size)])  113 us
    ppermute x53, starting transfers between devices, from_xor(): return lax.ppermute(value, axis, [(i, i ^ offset) for i in range(size)])  60.7 us
    pallas_call x6, Pallas kernels, call(): pl.pallas_call(kernel, out_shape=out_shapes, in_specs=[pl.BlockSpec(memor...  35.8 us
  transfers between devices with their start and end apart: 53, of which 43 were waited for; matrix products, arithmetic and copies ran while one was open for 1% of the time, Pallas kernels for 0%

profile of v1, /device:TPU:0, one launch (start us, length us, event | category | flops | bytes accessed | tf_op | source)
XLA Modules:
  0.0 217.9 jit_solution(7862392012292512966)
XLA Ops:
  3.0 2.2 %fusion = f32[64,256]{1,0:T(8,128)S(1)} fusion(bf16[128,4096]{1,0:T(8,128)(2,1)S(1)} %get-tuple-element.29, bf16[128,4096]{1,0:T(8,128)(2,1)S(1)} %get-tuple-element.28, s32[]{:T(128)S(6)} %xor.71, s32[4096]{0:T(1024)S(1)} %add_multiply_fusion), kind=kOutput, calls=%fused_computation.17 | convolution fusion | flops 156237824 | bytes 2179076 | tf_op jit(solution)/shard_map/dot_general | solution.py:228
  5.3 3.0 %collective-permute-start = (f32[64,128]{1,0:T(8,128)S(1)}, f32[64,128]{1,0:T(8,128)S(1)}, u32[]{:S(2)}, u32[]{:S(2)}) collective-permute-start(f32[64,128]{1,0:T(8,128)S(1)} %slice.201), channel_id=1, source_target_pairs={{0,1},{1,0},{2,3},{3,2},{4,5},{5,4},{6,7},{7,6},{8,9},{9,8},{10,11... | collective-permute-start | bytes 98312 | tf_op jit(solution)/shard_map/ppermute | solution.py:185
  10.1 2.1 collective-permute-start.10
  14.4 2.5 %collective-permute-start.1 = (f32[64,128]{1,0:T(8,128)S(1)}, f32[64,128]{1,0:T(8,128)S(1)}, u32[]{:S(2)}, u32[]{:S(2)}) collective-permute-start(f32[64,128]{1,0:T(8,128)S(1)} %get-tuple-element.19), channel_id=1, source_target_pairs={{0,4},{2,6},{4,0},{6,2},{8,12},{10,14},{12,8},{14,10},{1,5},{3,7},... | collective-permute-start | bytes 98312 | tf_op jit(solution)/shard_map/ppermute | solution.py:185
  16.9 8.7 %collective-permute-done.3 = f32[64,128]{1,0:T(8,128)S(1)} collective-permute-done((f32[64,128]{1,0:T(8,128)S(1)}, f32[64,128]{1,0:T(8,128)S(1)}, u32[]{:S(2)}, u32[]{:S(2)}) %collective-permute-start.3) | collective-permute-done | bytes 32800 | tf_op jit(solution)/shard_map/ppermute | solution.py:185
  28.9 5.0 %collective-permute-done.4 = f32[4,64,128]{2,1,0:T(8,128)S(1)} collective-permute-done((f32[4,64,128]{2,1,0:T(8,128)S(1)}, f32[4,64,128]{2,1,0:T(8,128)S(1)}, u32[]{:S(2)}, u32[]{:S(2)}) %collective-permute-start.4) | collective-permute-done | bytes 131104 | tf_op jit(solution)/shard_map/ppermute | solution.py:185
  35.5 7.1 %collective-permute-done.6 = bf16[256,512]{1,0:T(8,128)(2,1)S(1)} collective-permute-done((bf16[256,512]{1,0:T(8,128)(2,1)S(1)}, bf16[256,512]{1,0:T(8,128)(2,1)S(1)}, u32[]{:S(2)}, u32[]{:S(2)}) %collective-permute-start.6) | collective-permute-done | bytes 262176 | tf_op jit(solution)/shard_map/ppermute | solution.py:185
  43.7 13.8 %collective-permute-done.7 = bf16[256,512]{1,0:T(8,128)(2,1)S(1)} collective-permute-done((bf16[256,512]{1,0:T(8,128)(2,1)S(1)}, bf16[256,512]{1,0:T(8,128)(2,1)S(1)}, u32[]{:S(2)}, u32[]{:S(2)}) %collective-permute-start.7) | collective-permute-done | bytes 262176 | tf_op jit(solution)/shard_map/ppermute | solution.py:185
  59.4 6.2 %shard_map.41 = (bf16[64,2048]{1,0:T(8,128)(2,1)S(1)}, f32[64,64]{1,0:T(8,128)S(1)}) custom-call(f32[16,64,128]{2,1,0:T(8,128)S(1)} %constant_dynamic-update-slice_fusion.5.z_ref), custom_call_target="tpu_custom_call" | custom-call | flops 402653184 | bytes 524288 | tf_op jit(solution)/shard_map/pallas_call | solution.py:173
  69.1 5.1 %collective-permute-done.14 = f32[4,64,128]{2,1,0:T(8,128)S(1)} collective-permute-done((f32[4,64,128]{2,1,0:T(8,128)S(1)}, f32[4,64,128]{2,1,0:T(8,128)S(1)}, u32[]{:S(2)}, u32[]{:S(2)}) %collective-permute-start.14) | collective-permute-done | bytes 131104 | tf_op jit(solution)/shard_map/ppermute | solution.py:185
  74.2 5.3 %collective-permute-start.15 = (f32[64,128]{1,0:T(8,128)S(1)}, f32[64,128]{1,0:T(8,128)S(1)}, u32[]{:S(2)}, u32[]{:S(2)}) collective-permute-start(f32[64,128]{1,0:T(8,128)S(1)} %get-tuple-element.47), channel_id=1, source_target_pairs={{0,4},{2,6},{4,0},{6,2},{8,12},{10,14},{12,8},{14,10},{1,5},{3,7},... | collective-permute-start | bytes 98312 | tf_op jit(solution)/shard_map/ppermute | solution.py:185
  79.5 2.9 %collective-permute-start.17 = (f32[64,128]{1,0:T(8,128)S(1)}, f32[64,128]{1,0:T(8,128)S(1)}, u32[]{:S(2)}, u32[]{:S(2)}) collective-permute-start(f32[64,128]{1,0:T(8,128)S(1)} %get-tuple-element.48), channel_id=1, source_target_pairs={{0,12},{2,14},{4,8},{6,10},{8,4},{10,6},{12,0},{14,2},{1,13},{3,15... | collective-permute-start | bytes 98312 | tf_op jit(solution)/shard_map/ppermute | solution.py:185
  82.4 2.9 %collective-permute-done.17 = f32[64,128]{1,0:T(8,128)S(1)} collective-permute-done((f32[64,128]{1,0:T(8,128)S(1)}, f32[64,128]{1,0:T(8,128)S(1)}, u32[]{:S(2)}, u32[]{:S(2)}) %collective-permute-start.17) | collective-permute-done | bytes 32800 | tf_op jit(solution)/shard_map/ppermute | solution.py:185
  88.9 2.8 %collective-permute-start.18 = (f32[64,128]{1,0:T(8,128)S(1)}, f32[64,128]{1,0:T(8,128)S(1)}, u32[]{:S(2)}, u32[]{:S(2)}) collective-permute-start(f32[64,128]{1,0:T(8,128)S(1)} %get-tuple-element.17), channel_id=1, source_target_pairs={{0,4},{2,6},{4,0},{6,2},{8,12},{10,14},{12,8},{14,10},{1,5},{3,7},... | collective-permute-start | bytes 98312 | tf_op jit(solution)/shard_map/ppermute | solution.py:185
  94.6 4.4 %collective-permute-done.21 = f32[4,64,128]{2,1,0:T(8,128)S(1)} collective-permute-done((f32[4,64,128]{2,1,0:T(8,128)S(1)}, f32[4,64,128]{2,1,0:T(8,128)S(1)}, u32[]{:S(2)}, u32[]{:S(2)}) %collective-permute-start.21) | collective-permute-done | bytes 131104 | tf_op jit(solution)/shard_map/ppermute | solution.py:185
  100.6 7.4 %shard_map.43 = f32[16,64,128]{2,1,0:T(8,128)S(1)} custom-call(f32[16,64,128]{2,1,0:T(8,128)S(1)} %constant_dynamic-update-slice_fusion.32.z_ref, bf16[2048,512]{1,0:T(8,128)(2,1)S(1)} %constant_dynamic-update-slice_fusion.11.a_ref), custom_call_target="tpu_custom_call" | custom-call | flops 671088640 | bytes 2621440 | tf_op jit(solution)/shard_map/pallas_call | solution.py:173
  110.3 5.0 %collective-permute-done.24 = f32[4,64,128]{2,1,0:T(8,128)S(1)} collective-permute-done((f32[4,64,128]{2,1,0:T(8,128)S(1)}, f32[4,64,128]{2,1,0:T(8,128)S(1)}, u32[]{:S(2)}, u32[]{:S(2)}) %collective-permute-start.24) | collective-permute-done | bytes 131104 | tf_op jit(solution)/shard_map/ppermute | solution.py:185
  119.3 3.5 %collective-permute-done.27 = f32[64,128]{1,0:T(8,128)S(1)} collective-permute-done((f32[64,128]{1,0:T(8,128)S(1)}, f32[64,128]{1,0:T(8,128)S(1)}, u32[]{:S(2)}, u32[]{:S(2)}) %collective-permute-start.27) | collective-permute-done | bytes 32800 | tf_op jit(solution)/shard_map/ppermute | solution.py:185
  123.5 2.4 %collective-permute-start.30 = (f32[64,128]{1,0:T(8,128)S(1)}, f32[64,128]{1,0:T(8,128)S(1)}, u32[]{:S(2)}, u32[]{:S(2)}) collective-permute-start(f32[64,128]{1,0:T(8,128)S(1)} %get-tuple-element.15), channel_id=1, source_target_pairs={{0,12},{2,14},{4,8},{6,10},{8,4},{10,6},{12,0},{14,2},{1,13},{3,15... | collective-permute-start | bytes 98312 | tf_op jit(solution)/shard_map/ppermute | solution.py:185
  131.3 4.4 %collective-permute-done.31 = f32[4,64,128]{2,1,0:T(8,128)S(1)} collective-permute-done((f32[4,64,128]{2,1,0:T(8,128)S(1)}, f32[4,64,128]{2,1,0:T(8,128)S(1)}, u32[]{:S(2)}, u32[]{:S(2)}) %collective-permute-start.31) | collective-permute-done | bytes 131104 | tf_op jit(solution)/shard_map/ppermute | solution.py:185
  137.3 7.2 %shard_map.44 = f32[16,64,128]{2,1,0:T(8,128)S(1)} custom-call(f32[16,64,128]{2,1,0:T(8,128)S(1)} %constant_dynamic-update-slice_fusion.43.z_ref, bf16[2048,512]{1,0:T(8,128)(2,1)S(1)} %constant_dynamic-update-slice_fusion.11.a_ref), custom_call_target="tpu_custom_call" | custom-call | flops 671088640 | bytes 2621440 | tf_op jit(solution)/shard_map/pallas_call | solution.py:173
  146.9 5.0 %collective-permute-done.34 = f32[4,64,128]{2,1,0:T(8,128)S(1)} collective-permute-done((f32[4,64,128]{2,1,0:T(8,128)S(1)}, f32[4,64,128]{2,1,0:T(8,128)S(1)}, u32[]{:S(2)}, u32[]{:S(2)}) %collective-permute-start.34) | collective-permute-done | bytes 131104 | tf_op jit(solution)/shard_map/ppermute | solution.py:185
  153.2 2.3 %collective-permute-start.37 = (f32[64,128]{1,0:T(8,128)S(1)}, f32[64,128]{1,0:T(8,128)S(1)}, u32[]{:S(2)}, u32[]{:S(2)}) collective-permute-start(f32[64,128]{1,0:T(8,128)S(1)} %get-tuple-element.38), channel_id=1, source_target_pairs={{0,12},{2,14},{4,8},{6,10},{8,4},{10,6},{12,0},{14,2},{1,13},{3,15... | collective-permute-start | bytes 98312 | tf_op jit(solution)/shard_map/ppermute | solution.py:185
  155.9 3.0 %collective-permute-done.37 = f32[64,128]{1,0:T(8,128)S(1)} collective-permute-done((f32[64,128]{1,0:T(8,128)S(1)}, f32[64,128]{1,0:T(8,128)S(1)}, u32[]{:S(2)}, u32[]{:S(2)}) %collective-permute-start.37) | collective-permute-done | bytes 32800 | tf_op jit(solution)/shard_map/ppermute | solution.py:185
  161.9 2.9 %collective-permute-start.38 = (f32[64,128]{1,0:T(8,128)S(1)}, f32[64,128]{1,0:T(8,128)S(1)}, u32[]{:S(2)}, u32[]{:S(2)}) collective-permute-start(f32[64,128]{1,0:T(8,128)S(1)} %get-tuple-element.13), channel_id=1, source_target_pairs={{0,4},{2,6},{4,0},{6,2},{8,12},{10,14},{12,8},{14,10},{1,5},{3,7},... | collective-permute-start | bytes 98312 | tf_op jit(solution)/shard_map/ppermute | solution.py:185
  167.7 4.4 %collective-permute-done.41 = f32[4,64,128]{2,1,0:T(8,128)S(1)} collective-permute-done((f32[4,64,128]{2,1,0:T(8,128)S(1)}, f32[4,64,128]{2,1,0:T(8,128)S(1)}, u32[]{:S(2)}, u32[]{:S(2)}) %collective-permute-start.41) | collective-permute-done | bytes 131104 | tf_op jit(solution)/shard_map/ppermute | solution.py:185
  173.8 7.2 %shard_map.45 = f32[16,64,128]{2,1,0:T(8,128)S(1)} custom-call(f32[16,64,128]{2,1,0:T(8,128)S(1)} %constant_dynamic-update-slice_fusion.54.z_ref, bf16[2048,512]{1,0:T(8,128)(2,1)S(1)} %constant_dynamic-update-slice_fusion.11.a_ref), custom_call_target="tpu_custom_call" | custom-call | flops 671088640 | bytes 2621440 | tf_op jit(solution)/shard_map/pallas_call | solution.py:173
  183.3 5.0 %collective-permute-done.44 = f32[4,64,128]{2,1,0:T(8,128)S(1)} collective-permute-done((f32[4,64,128]{2,1,0:T(8,128)S(1)}, f32[4,64,128]{2,1,0:T(8,128)S(1)}, u32[]{:S(2)}, u32[]{:S(2)}) %collective-permute-start.44) | collective-permute-done | bytes 131104 | tf_op jit(solution)/shard_map/ppermute | solution.py:185
  192.3 3.5 %collective-permute-done.47 = f32[64,128]{1,0:T(8,128)S(1)} collective-permute-done((f32[64,128]{1,0:T(8,128)S(1)}, f32[64,128]{1,0:T(8,128)S(1)}, u32[]{:S(2)}, u32[]{:S(2)}) %collective-permute-start.47) | collective-permute-done | bytes 32800 | tf_op jit(solution)/shard_map/ppermute | solution.py:185
  196.5 2.5 %collective-permute-start.50 = (f32[64,128]{1,0:T(8,128)S(1)}, f32[64,128]{1,0:T(8,128)S(1)}, u32[]{:S(2)}, u32[]{:S(2)}) collective-permute-start(f32[64,128]{1,0:T(8,128)S(1)} %get-tuple-element.11), channel_id=1, source_target_pairs={{0,12},{2,14},{4,8},{6,10},{8,4},{10,6},{12,0},{14,2},{1,13},{3,15... | collective-permute-start | bytes 98312 | tf_op jit(solution)/shard_map/ppermute | solution.py:185
  204.4 4.4 %collective-permute-done.51 = f32[4,64,128]{2,1,0:T(8,128)S(1)} collective-permute-done((f32[4,64,128]{2,1,0:T(8,128)S(1)}, f32[4,64,128]{2,1,0:T(8,128)S(1)}, u32[]{:S(2)}, u32[]{:S(2)}) %collective-permute-start.51) | collective-permute-done | bytes 131104 | tf_op jit(solution)/shard_map/ppermute | solution.py:185
  210.5 6.7 %shard_map.46 = f32[512,64]{1,0:T(8,128)S(1)} custom-call(f32[16,64,128]{2,1,0:T(8,128)S(1)} %constant_dynamic-update-slice_fusion.65.z_ref, bf16[2048,512]{1,0:T(8,128)(2,1)S(1)} %constant_dynamic-update-slice_fusion.11.a_ref), custom_call_target="tpu_custom_call" | custom-call | flops 671088640 | bytes 2621440 | tf_op jit(solution)/shard_map/pallas_call | solution.py:173
  (165 shorter events, 65.5 us)
Async XLA Ops:
  5.3 7.2 %collective-permute-start = (f32[64,128]{1,0:T(8,128)S(1)}, f32[64,128]{1,0:T(8,128)S(1)}, u32[]{:S(2)}, u32[]{:S(2)}) collective-permute-start(f32[64,128]{1,0:T(8,128)S(1)} %slice.201), channel_id=1, source_target_pairs={{0,1},{1,0},{2,3},{3,2},{4,5},{5,4},{6,7},{7,6},{8,9},{9,8},{10,11... | collective-permute-start | bytes 98312 | tf_op jit(solution)/shard_map/ppermute | solution.py:185
  8.3 50.8 %collective-permute-start.11 = (bf16[256,512]{1,0:T(8,128)(2,1)S(1)}, bf16[256,512]{1,0:T(8,128)(2,1)S(1)}, u32[]{:S(2)}, u32[]{:S(2)}) collective-permute-start(bf16[256,512]{1,0:T(8,128)(2,1)S(1)} %get-tuple-element.26), channel_id=1, source_target_pairs={{0,10},{2,8},{4,14},{6,12},{8,2},{10,0},{12,6},{14,4},{1,11},{3,9}... | collective-permute-start | bytes 786440 | tf_op jit(solution)/shard_map/ppermute | solution.py:185
  10.1 48.9 %collective-permute-start.10 = (bf16[256,512]{1,0:T(8,128)(2,1)S(1)}, bf16[256,512]{1,0:T(8,128)(2,1)S(1)}, u32[]{:S(2)}, u32[]{:S(2)}) collective-permute-start(bf16[256,512]{1,0:T(8,128)(2,1)S(1)} %get-tuple-element.27), channel_id=1, source_target_pairs={{0,6},{2,4},{4,2},{6,0},{8,14},{10,12},{12,10},{14,8},{1,7},{3,5},... | collective-permute-start | bytes 786440 | tf_op jit(solution)/shard_map/ppermute | solution.py:185
  12.5 13.1 %collective-permute-start.3 = (f32[64,128]{1,0:T(8,128)S(1)}, f32[64,128]{1,0:T(8,128)S(1)}, u32[]{:S(2)}, u32[]{:S(2)}) collective-permute-start(f32[64,128]{1,0:T(8,128)S(1)} %get-tuple-element.19), channel_id=1, source_target_pairs={{0,12},{2,14},{4,8},{6,10},{8,4},{10,6},{12,0},{14,2},{1,13},{3,15... | collective-permute-start | bytes 98312 | tf_op jit(solution)/shard_map/ppermute | solution.py:185
  14.3 13.0 %collective-permute-start.2 = (f32[64,128]{1,0:T(8,128)S(1)}, f32[64,128]{1,0:T(8,128)S(1)}, u32[]{:S(2)}, u32[]{:S(2)}) collective-permute-start(f32[64,128]{1,0:T(8,128)S(1)} %get-tuple-element.19), channel_id=1, source_target_pairs={{0,8},{2,10},{4,12},{6,14},{8,0},{10,2},{12,4},{14,6},{1,9},{3,11}... | collective-permute-start | bytes 98312 | tf_op jit(solution)/shard_map/ppermute | solution.py:185
  14.4 13.8 %collective-permute-start.1 = (f32[64,128]{1,0:T(8,128)S(1)}, f32[64,128]{1,0:T(8,128)S(1)}, u32[]{:S(2)}, u32[]{:S(2)}) collective-permute-start(f32[64,128]{1,0:T(8,128)S(1)} %get-tuple-element.19), channel_id=1, source_target_pairs={{0,4},{2,6},{4,0},{6,2},{8,12},{10,14},{12,8},{14,10},{1,5},{3,7},... | collective-permute-start | bytes 98312 | tf_op jit(solution)/shard_map/ppermute | solution.py:185
  25.6 33.5 %collective-permute-start.12 = (bf16[256,512]{1,0:T(8,128)(2,1)S(1)}, bf16[256,512]{1,0:T(8,128)(2,1)S(1)}, u32[]{:S(2)}, u32[]{:S(2)}) collective-permute-start(bf16[256,512]{1,0:T(8,128)(2,1)S(1)} %get-tuple-element.20), channel_id=1, source_target_pairs={{0,14},{2,12},{4,10},{6,8},{8,6},{10,4},{12,2},{14,0},{1,15},{3,13... | collective-permute-start | bytes 786440 | tf_op jit(solution)/shard_map/ppermute | solution.py:185
  27.3 15.3 %collective-permute-start.6 = (bf16[256,512]{1,0:T(8,128)(2,1)S(1)}, bf16[256,512]{1,0:T(8,128)(2,1)S(1)}, u32[]{:S(2)}, u32[]{:S(2)}) collective-permute-start(bf16[256,512]{1,0:T(8,128)(2,1)S(1)} %get-tuple-element.22), channel_id=1, source_target_pairs={{0,4},{2,6},{4,0},{6,2},{8,12},{10,14},{12,8},{14,10},{1,5},{3,7},... | collective-permute-start | bytes 786440 | tf_op jit(solution)/shard_map/ppermute | solution.py:185
  28.2 5.6 %collective-permute-start.4 = (f32[4,64,128]{2,1,0:T(8,128)S(1)}, f32[4,64,128]{2,1,0:T(8,128)S(1)}, u32[]{:S(2)}, u32[]{:S(2)}) collective-permute-start(f32[4,64,128]{2,1,0:T(8,128)S(1)} %pad_maximum_fusion.2), channel_id=1, source_target_pairs={{0,1},{1,0},{2,3},{3,2},{4,5},{5,4},{6,7},{7,6},{8,9},{9,8},{10,11... | collective-permute-start | bytes 393224 | tf_op jit(solution)/shard_map/ppermute | solution.py:185
  33.9 23.6 %collective-permute-start.7 = (bf16[256,512]{1,0:T(8,128)(2,1)S(1)}, bf16[256,512]{1,0:T(8,128)(2,1)S(1)}, u32[]{:S(2)}, u32[]{:S(2)}) collective-permute-start(bf16[256,512]{1,0:T(8,128)(2,1)S(1)} %get-tuple-element.23), channel_id=1, source_target_pairs={{0,8},{2,10},{4,12},{6,14},{8,0},{10,2},{12,4},{14,6},{1,9},{3,11}... | collective-permute-start | bytes 786440 | tf_op jit(solution)/shard_map/ppermute | solution.py:185
  42.6 15.0 %collective-permute-start.8 = (bf16[256,512]{1,0:T(8,128)(2,1)S(1)}, bf16[256,512]{1,0:T(8,128)(2,1)S(1)}, u32[]{:S(2)}, u32[]{:S(2)}) collective-permute-start(bf16[256,512]{1,0:T(8,128)(2,1)S(1)} %get-tuple-element.24), channel_id=1, source_target_pairs={{0,12},{2,14},{4,8},{6,10},{8,4},{10,6},{12,0},{14,2},{1,13},{3,15... | collective-permute-start | bytes 786440 | tf_op jit(solution)/shard_map/ppermute | solution.py:185
  68.5 5.7 %collective-permute-start.14 = (f32[4,64,128]{2,1,0:T(8,128)S(1)}, f32[4,64,128]{2,1,0:T(8,128)S(1)}, u32[]{:S(2)}, u32[]{:S(2)}) collective-permute-start(f32[4,64,128]{2,1,0:T(8,128)S(1)} %slice.221), channel_id=1, source_target_pairs={{0,1},{1,0},{2,3},{3,2},{4,5},{5,4},{6,7},{7,6},{8,9},{9,8},{10,11... | collective-permute-start | bytes 393224 | tf_op jit(solution)/shard_map/ppermute | solution.py:185
  74.2 8.2 %collective-permute-start.15 = (f32[64,128]{1,0:T(8,128)S(1)}, f32[64,128]{1,0:T(8,128)S(1)}, u32[]{:S(2)}, u32[]{:S(2)}) collective-permute-start(f32[64,128]{1,0:T(8,128)S(1)} %get-tuple-element.47), channel_id=1, source_target_pairs={{0,4},{2,6},{4,0},{6,2},{8,12},{10,14},{12,8},{14,10},{1,5},{3,7},... | collective-permute-start | bytes 98312 | tf_op jit(solution)/shard_map/ppermute | solution.py:185
  79.5 5.8 %collective-permute-start.17 = (f32[64,128]{1,0:T(8,128)S(1)}, f32[64,128]{1,0:T(8,128)S(1)}, u32[]{:S(2)}, u32[]{:S(2)}) collective-permute-start(f32[64,128]{1,0:T(8,128)S(1)} %get-tuple-element.48), channel_id=1, source_target_pairs={{0,12},{2,14},{4,8},{6,10},{8,4},{10,6},{12,0},{14,2},{1,13},{3,15... | collective-permute-start | bytes 98312 | tf_op jit(solution)/shard_map/ppermute | solution.py:185
  87.2 5.8 %collective-permute-start.20 = (f32[64,128]{1,0:T(8,128)S(1)}, f32[64,128]{1,0:T(8,128)S(1)}, u32[]{:S(2)}, u32[]{:S(2)}) collective-permute-start(f32[64,128]{1,0:T(8,128)S(1)} %get-tuple-element.17), channel_id=1, source_target_pairs={{0,12},{2,14},{4,8},{6,10},{8,4},{10,6},{12,0},{14,2},{1,13},{3,15... | collective-permute-start | bytes 98312 | tf_op jit(solution)/shard_map/ppermute | solution.py:185
  88.9 5.0 %collective-permute-start.18 = (f32[64,128]{1,0:T(8,128)S(1)}, f32[64,128]{1,0:T(8,128)S(1)}, u32[]{:S(2)}, u32[]{:S(2)}) collective-permute-start(f32[64,128]{1,0:T(8,128)S(1)} %get-tuple-element.17), channel_id=1, source_target_pairs={{0,4},{2,6},{4,0},{6,2},{8,12},{10,14},{12,8},{14,10},{1,5},{3,7},... | collective-permute-start | bytes 98312 | tf_op jit(solution)/shard_map/ppermute | solution.py:185
  93.9 5.0 %collective-permute-start.21 = (f32[4,64,128]{2,1,0:T(8,128)S(1)}, f32[4,64,128]{2,1,0:T(8,128)S(1)}, u32[]{:S(2)}, u32[]{:S(2)}) collective-permute-start(f32[4,64,128]{2,1,0:T(8,128)S(1)} %pad_maximum_fusion.3), channel_id=1, source_target_pairs={{0,1},{1,0},{2,3},{3,2},{4,5},{5,4},{6,7},{7,6},{8,9},{9,8},{10,11... | collective-permute-start | bytes 393224 | tf_op jit(solution)/shard_map/ppermute | solution.py:185
  109.7 5.6 %collective-permute-start.24 = (f32[4,64,128]{2,1,0:T(8,128)S(1)}, f32[4,64,128]{2,1,0:T(8,128)S(1)}, u32[]{:S(2)}, u32[]{:S(2)}) collective-permute-start(f32[4,64,128]{2,1,0:T(8,128)S(1)} %slice.229), channel_id=1, source_target_pairs={{0,1},{1,0},{2,3},{3,2},{4,5},{5,4},{6,7},{7,6},{8,9},{9,8},{10,11... | collective-permute-start | bytes 393224 | tf_op jit(solution)/shard_map/ppermute | solution.py:185
  117.1 5.7 %collective-permute-start.27 = (f32[64,128]{1,0:T(8,128)S(1)}, f32[64,128]{1,0:T(8,128)S(1)}, u32[]{:S(2)}, u32[]{:S(2)}) collective-permute-start(f32[64,128]{1,0:T(8,128)S(1)} %get-tuple-element.43), channel_id=1, source_target_pairs={{0,12},{2,14},{4,8},{6,10},{8,4},{10,6},{12,0},{14,2},{1,13},{3,15... | collective-permute-start | bytes 98312 | tf_op jit(solution)/shard_map/ppermute | solution.py:185
  123.5 5.8 %collective-permute-start.30 = (f32[64,128]{1,0:T(8,128)S(1)}, f32[64,128]{1,0:T(8,128)S(1)}, u32[]{:S(2)}, u32[]{:S(2)}) collective-permute-start(f32[64,128]{1,0:T(8,128)S(1)} %get-tuple-element.15), channel_id=1, source_target_pairs={{0,12},{2,14},{4,8},{6,10},{8,4},{10,6},{12,0},{14,2},{1,13},{3,15... | collective-permute-start | bytes 98312 | tf_op jit(solution)/shard_map/ppermute | solution.py:185
  130.7 5.0 %collective-permute-start.31 = (f32[4,64,128]{2,1,0:T(8,128)S(1)}, f32[4,64,128]{2,1,0:T(8,128)S(1)}, u32[]{:S(2)}, u32[]{:S(2)}) collective-permute-start(f32[4,64,128]{2,1,0:T(8,128)S(1)} %pad_maximum_fusion.4), channel_id=1, source_target_pairs={{0,1},{1,0},{2,3},{3,2},{4,5},{5,4},{6,7},{7,6},{8,9},{9,8},{10,11... | collective-permute-start | bytes 393224 | tf_op jit(solution)/shard_map/ppermute | solution.py:185
  146.3 5.6 %collective-permute-start.34 = (f32[4,64,128]{2,1,0:T(8,128)S(1)}, f32[4,64,128]{2,1,0:T(8,128)S(1)}, u32[]{:S(2)}, u32[]{:S(2)}) collective-permute-start(f32[4,64,128]{2,1,0:T(8,128)S(1)} %slice.237), channel_id=1, source_target_pairs={{0,1},{1,0},{2,3},{3,2},{4,5},{5,4},{6,7},{7,6},{8,9},{9,8},{10,11... | collective-permute-start | bytes 393224 | tf_op jit(solution)/shard_map/ppermute | solution.py:185
  153.2 5.7 %collective-permute-start.37 = (f32[64,128]{1,0:T(8,128)S(1)}, f32[64,128]{1,0:T(8,128)S(1)}, u32[]{:S(2)}, u32[]{:S(2)}) collective-permute-start(f32[64,128]{1,0:T(8,128)S(1)} %get-tuple-element.38), channel_id=1, source_target_pairs={{0,12},{2,14},{4,8},{6,10},{8,4},{10,6},{12,0},{14,2},{1,13},{3,15... | collective-permute-start | bytes 98312 | tf_op jit(solution)/shard_map/ppermute | solution.py:185
  155.4 4.9 %collective-permute-start.36 = (f32[64,128]{1,0:T(8,128)S(1)}, f32[64,128]{1,0:T(8,128)S(1)}, u32[]{:S(2)}, u32[]{:S(2)}) collective-permute-start(f32[64,128]{1,0:T(8,128)S(1)} %get-tuple-element.39), channel_id=1, source_target_pairs={{0,8},{2,10},{4,12},{6,14},{8,0},{10,2},{12,4},{14,6},{1,9},{3,11}... | collective-permute-start | bytes 98312 | tf_op jit(solution)/shard_map/ppermute | solution.py:185
  160.4 5.8 %collective-permute-start.40 = (f32[64,128]{1,0:T(8,128)S(1)}, f32[64,128]{1,0:T(8,128)S(1)}, u32[]{:S(2)}, u32[]{:S(2)}) collective-permute-start(f32[64,128]{1,0:T(8,128)S(1)} %get-tuple-element.13), channel_id=1, source_target_pairs={{0,12},{2,14},{4,8},{6,10},{8,4},{10,6},{12,0},{14,2},{1,13},{3,15... | collective-permute-start | bytes 98312 | tf_op jit(solution)/shard_map/ppermute | solution.py:185
  161.9 5.0 %collective-permute-start.39 = (f32[64,128]{1,0:T(8,128)S(1)}, f32[64,128]{1,0:T(8,128)S(1)}, u32[]{:S(2)}, u32[]{:S(2)}) collective-permute-start(f32[64,128]{1,0:T(8,128)S(1)} %get-tuple-element.13), channel_id=1, source_target_pairs={{0,8},{2,10},{4,12},{6,14},{8,0},{10,2},{12,4},{14,6},{1,9},{3,11}... | collective-permute-start | bytes 98312 | tf_op jit(solution)/shard_map/ppermute | solution.py:185
  161.9 5.1 %collective-permute-start.38 = (f32[64,128]{1,0:T(8,128)S(1)}, f32[64,128]{1,0:T(8,128)S(1)}, u32[]{:S(2)}, u32[]{:S(2)}) collective-permute-start(f32[64,128]{1,0:T(8,128)S(1)} %get-tuple-element.13), channel_id=1, source_target_pairs={{0,4},{2,6},{4,0},{6,2},{8,12},{10,14},{12,8},{14,10},{1,5},{3,7},... | collective-permute-start | bytes 98312 | tf_op jit(solution)/shard_map/ppermute | solution.py:185
  167.1 5.0 %collective-permute-start.41 = (f32[4,64,128]{2,1,0:T(8,128)S(1)}, f32[4,64,128]{2,1,0:T(8,128)S(1)}, u32[]{:S(2)}, u32[]{:S(2)}) collective-permute-start(f32[4,64,128]{2,1,0:T(8,128)S(1)} %pad_maximum_fusion.5), channel_id=1, source_target_pairs={{0,1},{1,0},{2,3},{3,2},{4,5},{5,4},{6,7},{7,6},{8,9},{9,8},{10,11... | collective-permute-start | bytes 393224 | tf_op jit(solution)/shard_map/ppermute | solution.py:185
  182.7 5.6 %collective-permute-start.44 = (f32[4,64,128]{2,1,0:T(8,128)S(1)}, f32[4,64,128]{2,1,0:T(8,128)S(1)}, u32[]{:S(2)}, u32[]{:S(2)}) collective-permute-start(f32[4,64,128]{2,1,0:T(8,128)S(1)} %slice.245), channel_id=1, source_target_pairs={{0,1},{1,0},{2,3},{3,2},{4,5},{5,4},{6,7},{7,6},{8,9},{9,8},{10,11... | collective-permute-start | bytes 393224 | tf_op jit(solution)/shard_map/ppermute | solution.py:185
  190.1 5.7 %collective-permute-start.47 = (f32[64,128]{1,0:T(8,128)S(1)}, f32[64,128]{1,0:T(8,128)S(1)}, u32[]{:S(2)}, u32[]{:S(2)}) collective-permute-start(f32[64,128]{1,0:T(8,128)S(1)} %get-tuple-element.33), channel_id=1, source_target_pairs={{0,12},{2,14},{4,8},{6,10},{8,4},{10,6},{12,0},{14,2},{1,13},{3,15... | collective-permute-start | bytes 98312 | tf_op jit(solution)/shard_map/ppermute | solution.py:185
  196.5 5.8 %collective-permute-start.50 = (f32[64,128]{1,0:T(8,128)S(1)}, f32[64,128]{1,0:T(8,128)S(1)}, u32[]{:S(2)}, u32[]{:S(2)}) collective-permute-start(f32[64,128]{1,0:T(8,128)S(1)} %get-tuple-element.11), channel_id=1, source_target_pairs={{0,12},{2,14},{4,8},{6,10},{8,4},{10,6},{12,0},{14,2},{1,13},{3,15... | collective-permute-start | bytes 98312 | tf_op jit(solution)/shard_map/ppermute | solution.py:185
  203.8 5.0 %collective-permute-start.51 = (f32[4,64,128]{2,1,0:T(8,128)S(1)}, f32[4,64,128]{2,1,0:T(8,128)S(1)}, u32[]{:S(2)}, u32[]{:S(2)}) collective-permute-start(f32[4,64,128]{2,1,0:T(8,128)S(1)} %pad_maximum_fusion.6), channel_id=1, source_target_pairs={{0,1},{1,0},{2,3},{3,2},{4,5},{5,4},{6,7},{7,6},{8,9},{9,8},{10,11... | collective-permute-start | bytes 393224 | tf_op jit(solution)/shard_map/ppermute | solution.py:185
  (21 other events, 66.9 us)

commit v2 on v1

--- a/solution.py
+++ b/solution.py
@@ -133,131 +133,133 @@
     return upper, inverse_one, first, inverse_two
 
 
-def wide_of(z_ref):
-    return jnp.concatenate([z_ref[i] for i in range(z_ref.shape[0])], axis=1)
-
-
-def narrow_basis(z_ref):
-    upper, inverse_one, first, inverse_two = both_passes(wide_of(z_ref))
+def wide_of(z_ref, at_ref):
+    halves, n_z, n_col = z_ref.shape[:3]
+    return jnp.concatenate(
+        [
+            z_ref[h, at_ref[0] ^ zo, c]
+            for h in range(halves)
+            for zo in range(n_z)
+            for c in range(n_col)
+        ],
+        axis=1,
+    )
+
+
+def narrow_basis(z_ref, at_ref):
+    upper, inverse_one, first, inverse_two = both_passes(wide_of(z_ref, at_ref))
     return small_times_wide(inverse_two, first).astype(jnp.bfloat16), upper
 
 
-def power_body(basis, a_ref, p_ref):
+def power_body(basis, a_ref, at_ref, p_ref):
     weights = dot_nn(basis, a_ref[...]).astype(jnp.bfloat16)
     forth = dot_nt(weights, a_ref[...])
-    width = p_ref.shape[2]
-    for i in range(p_ref.shape[0]):
-        p_ref[i] = forth[:, width * i : width * (i + 1)]
-
-
-def orth_kernel(z_ref, basis_ref, upper_ref):
-    basis_ref[...], upper_ref[...] = narrow_basis(z_ref)
-
-
-def power_kernel(basis_ref, a_ref, p_ref):
-    power_body(basis_ref[...], a_ref, p_ref)
-
-
-def orth_power_kernel(z_ref, a_ref, p_ref):
-    basis, unused = narrow_basis(z_ref)
-    power_body(basis, a_ref, p_ref)
-
-
-def last_kernel(z_ref, a_ref, out_ref):
-    basis, unused = narrow_basis(z_ref)
+    halves, n_z, n_col, unused, width = p_ref.shape
+    for h in range(halves):
+        for zo in range(n_z):
+            for c in range(n_col):
+                i = (h * n_z + zo) * n_col + c
+                p_ref[h, at_ref[0] ^ zo, c] = forth[:, width * i : width * (i + 1)]
+
+
+def orth_kernel(at_ref, z_ref, basis_ref, upper_ref):
+    basis_ref[...], upper_ref[...] = narrow_basis(z_ref, at_ref)
+
+
+def power_kernel(at_ref, basis_ref, a_ref, p_ref):
+    power_body(basis_ref[...], a_ref, at_ref, p_ref)
+
+
+def orth_power_kernel(at_ref, z_ref, a_ref, p_ref):
+    basis, unused = narrow_basis(z_ref, at_ref)
+    power_body(basis, a_ref, at_ref, p_ref)
+
+
+def last_kernel(at_ref, z_ref, a_ref, out_ref):
+    basis, unused = narrow_basis(z_ref, at_ref)
     out_ref[...] = dot_nn(basis, a_ref[...]).T
 
 
-def call(kernel, out_shapes, flops, *operands):
+def call(kernel, out_shapes, flops, at, *operands):
     moved = sum(x.size * x.dtype.itemsize for x in operands)
     return pl.pallas_call(
         kernel,
         out_shape=out_shapes,
-        in_specs=[pl.BlockSpec(memory_space=pltpu.VMEM)] * len(operands),
+        in_specs=[pl.BlockSpec(memory_space=pltpu.SMEM)]
+        + [pl.BlockSpec(memory_space=pltpu.VMEM)] * len(operands),
         out_specs=jax.tree.map(lambda _: pl.BlockSpec(memory_space=pltpu.VMEM), out_shapes),
         compiler_params=pltpu.CompilerParams(vmem_limit_bytes=40 * 1024 * 1024),
         cost_estimate=pl.CostEstimate(flops=flops, bytes_accessed=moved, transcendentals=0),
-    )(*operands)
-
-
-def from_xor(value, axis, offset):
-    size = lax.axis_size(axis)
-    return lax.ppermute(value, axis, [(i, i ^ offset) for i in range(size)])
-
-
-def sum_scatter(parts, n_z, n_col):
-    half = parts.shape[0] // 2
-    total = parts[:half] + from_xor(parts[half:], "row", 1)
-    step = half // n_col
-    pieces = [from_xor(total[step * o : step * (o + 1)], "col", o) for o in range(1, n_col)]
-    total = functools.reduce(jnp.add, pieces, total[:step])
-    pieces = [from_xor(total[o], "row", 2 * o) for o in range(1, n_z)]
-    return functools.reduce(jnp.add, pieces, total[0])
-
-
-def gather_all(own, n_z, n_col):
-    chunks = jnp.stack([own] + [from_xor(own, "row", 2 * o) for o in range(1, n_z)])
-    chunks = jnp.concatenate([chunks] + [from_xor(chunks, "col", o) for o in range(1, n_col)])
-    return jnp.concatenate([chunks, from_xor(chunks, "row", 1)])
+    )(at, *operands)
+
+
+def swap_cores(value):
+    return lax.ppermute(value, "core", [(0, 1), (1, 0)])
+
+
+def sum_scatter(parts):
+    total = parts[0] + swap_cores(parts[1])
+    total = total.reshape((-1,) + total.shape[2:])
+    return jnp.sum(lax.all_to_all(total, ("z", "col"), 0, 0, tiled=True), axis=0)
+
+
+def gather_all(own):
+    n_z, n_col = lax.axis_size("z"), lax.axis_size("col")
+    copies = jnp.broadcast_to(own[None], (n_z * n_col,) + own.shape)
+    chunks = lax.all_to_all(copies, ("z", "col"), 0, 0, tiled=True)
+    chunks = chunks.reshape((n_z, n_col) + own.shape)
+    return jnp.stack([chunks, swap_cores(chunks)])
 
 
 def per_device_transposed(sketch_base, states):
-    n_row, n_col = lax.axis_size("row"), lax.axis_size("col")
-    n_z = n_row // 2
-    row, col = lax.axis_index("row"), lax.axis_index("col")
+    n_z, n_core, n_col = lax.axis_size("z"), lax.axis_size("core"), lax.axis_size("col")
+    n_row = n_z * n_core
+    z_at, core, col = lax.axis_index("z"), lax.axis_index("core"), lax.axis_index("col")
+    row = z_at * n_core + core
     rows_local, width_local = states.shape
     rows_total, width_total = rows_local * n_row, width_local * n_col
     chunk = rows_local // n_col
     cols = width_local // n_row
-    n_chunks = n_row * n_col
-
-    order = [col ^ o for o in range(n_col)]
-    relative = jnp.concatenate(
-        [lax.dynamic_slice_in_dim(states, o * chunk, chunk, 0) for o in order]
-    )
 
     def block(offset):
-        return lax.dynamic_slice_in_dim(relative, (row ^ offset) * cols, cols, 1)
+        return lax.dynamic_slice_in_dim(states, (row ^ offset) * cols, cols, 1)
+
+    def to_row(value, offset):
+        pairs = [(i, i ^ offset) for i in range(n_row)]
+        return lax.ppermute(value, ("z", "core"), pairs)
 
     received = {0: block(0)}
     for offset in sorted(range(1, n_row), reverse=True):
-        received[offset] = from_xor(block(offset), "row", offset)
+        received[offset] = to_row(block(offset), offset)
 
     feature_index = col * width_local + jnp.arange(width_local, dtype=jnp.int32)
     omega = sketch_table(sketch_base[0], feature_index, RANK)
     partial = lax.dot_general(
-        omega, relative, (((0,), (1,)), ((), ())), preferred_element_type=jnp.float32
-    )
-    own = partial[:, :chunk]
-    for o in range(1, n_col):
-        own = own + from_xor(partial[:, o * chunk : (o + 1) * chunk], "col", o)
-    z = gather_all(own, n_z, n_col)
-
-    a = jnp.concatenate(
-        [
-            received[2 * zo + core][co * chunk : (co + 1) * chunk]
-            for core in range(2)
-            for co in range(n_col)
-            for zo in range(n_z)
-        ]
-    )
+        omega, states, (((0,), (1,)), ((), ())), preferred_element_type=jnp.float32
+    )
+    partial = partial.reshape(RANK, n_col, chunk).transpose(1, 0, 2)
+    own = jnp.sum(lax.all_to_all(partial, "col", 0, 0, tiled=True), axis=0)
+    z = gather_all(own)
+
+    a = jnp.concatenate([received[2 * zo + other] for other in range(2) for zo in range(n_z)])
+    at = z_at[None].astype(jnp.int32)
 
     f32 = jnp.float32
     square = jax.ShapeDtypeStruct((RANK, RANK), f32)
     wide = jax.ShapeDtypeStruct((RANK, rows_total), jnp.bfloat16)
-    chunks = jax.ShapeDtypeStruct((n_chunks, RANK, chunk), f32)
+    chunks = jax.ShapeDtypeStruct((2, n_z, n_col, RANK, chunk), f32)
     orth_flops = 8 * 64 * 64 * rows_total * 6
     power_flops = 4 * 64 * rows_total * cols
 
-    basis, upper = call(orth_kernel, (wide, square), orth_flops, z)
+    basis, upper = call(orth_kernel, (wide, square), orth_flops, at, z)
     factor = upper.T * (1.0 / math.sqrt(rows_total * width_total))
-    parts = call(power_kernel, chunks, power_flops, basis, a)
+    parts = call(power_kernel, chunks, power_flops, at, basis, a)
     for step in range(POWER - 1):
-        z = gather_all(sum_scatter(parts, n_z, n_col), n_z, n_col)
-        parts = call(orth_power_kernel, chunks, orth_flops + power_flops, z, a)
-    z = gather_all(sum_scatter(parts, n_z, n_col), n_z, n_col)
+        z = gather_all(sum_scatter(parts))
+        parts = call(orth_power_kernel, chunks, orth_flops + power_flops, at, z, a)
+    z = gather_all(sum_scatter(parts))
     loadings = call(
-        last_kernel, jax.ShapeDtypeStruct((cols, RANK), f32), orth_flops + power_flops, z, a
+        last_kernel, jax.ShapeDtypeStruct((cols, RANK), f32), orth_flops + power_flops, at, z, a
     )
     return loadings, factor
 
@@ -299,22 +301,26 @@
     return lax.psum_scatter(back(basis), "row", scatter_dimension=0, tiled=True), factor
 
 
-def per_device(sketch_base, states):
-    n_row, n_col = lax.axis_size("row"), lax.axis_size("col")
-    rows_local, width_local = states.shape
-    powers = n_row & (n_row - 1) == 0 and n_col & (n_col - 1) == 0 and n_row > 1
-    tiled = rows_local % (n_col * LANES) == 0 and width_local % (n_row * LANES) == 0
-    if powers and tiled:
-        return per_device_transposed(sketch_base, states)
-    return per_device_slabs(sketch_base, states)
-
-
 def solution(mesh):
-    placed = (P("grp"), P(("grp", "row"), "col"))
-    return jax.shard_map(
-        per_device,
-        mesh=mesh,
-        in_specs=placed,
-        out_specs=(P(("col", "row"), "grp"), P("grp", None)),
-        check_vma=False,
-    )
+    n_grp, n_row, n_col = (mesh.shape[name] for name in ("grp", "row", "col"))
+    fits = n_row % 2 == 0 and n_row & (n_row - 1) == 0
+
+    def run(sketch_base, states):
+        rows_local = states.shape[0] // (n_grp * n_row)
+        width_local = states.shape[1] // n_col
+        tiled = rows_local % (n_col * LANES) == 0 and width_local % (n_row * LANES) == 0
+        if fits and tiled:
+            split = mesh.devices.reshape(n_grp, n_row // 2, 2, n_col)
+            inner = jax.sharding.Mesh(split, ("grp", "z", "core", "col"))
+            row, step = ("z", "core"), per_device_transposed
+        else:
+            inner, row, step = mesh, ("row",), per_device_slabs
+        return jax.shard_map(
+            step,
+            mesh=inner,
+            in_specs=(P("grp"), P(("grp",) + row, "col")),
+            out_specs=(P(("col",) + row, "grp"), P("grp", None)),
+            check_vma=False,
+        )(sketch_base, states)
+
+    return run

time: 218 us -> 210 us (0.963)
  blocking collectives: 0 us -> 103 us
  waiting for transfers between devices: 113 us -> 33.7 us
  starting transfers between devices: 60.7 us -> 18.5 us
  local copies, waits for them, and re-layouts: 3.8 us -> 12.4 us
    all_to_all x0 -> x8, blocking collectives: none -> 103 us  [the longest x4 55.2 us: sum_scatter(): lax.all_to_all(total, ('z', 'col'), 0, 0, tiled=True)]
    ppermute x53 -> x16, waiting for transfers between devices: 113 us -> 15.1 us  [the longest x9 10.8 us: swap_cores(): return lax.ppermute(value, 'core', [(0, 1), (1, 0)])]
    ppermute x53 -> x16, starting transfers between devices: 60.7 us -> 11.8 us  [the longest x7 10.7 us: to_row(): return lax.ppermute(value, ('z', 'core'), pairs)]
    all_to_all x0 -> x2, waiting for transfers between devices: none -> 18.6 us  [the longest x1 15.6 us: gather_all(): chunks = lax.all_to_all(copies, ('z', 'col'), 0, 0, tiled=True)]
    all_to_all x0 -> x2, starting transfers between devices: none -> 6.71 us  [the longest x1 3.41 us: gather_all(): chunks = lax.all_to_all(copies, ('z', 'col'), 0, 0, tiled=True)]
    unnamed x37 -> x8, local copies, waits for them, and re-layouts: 1.74 us -> 7.28 us
  transfers between devices with their start and end apart: 53 -> 18, of which waited for: 43 -> 11; matrix products, arithmetic and copies ran while one was open for 1% -> 6% of each run, Pallas kernels for 0% -> 0%
where the time goes in v2:
time: 210 us
  blocking collectives  103 us (49%)
  Pallas kernels  35.7 us (17%)
  waiting for transfers between devices  33.7 us (16%)
  starting transfers between devices  18.5 us (9%)
  local copies, waits for them, and re-layouts  12.4 us (6%)
  matrix products  3.83 us (2%)
    all_to_all x4, blocking collectives, sum_scatter(): lax.all_to_all(total, ('z', 'col'), 0, 0, tiled=True)  55.2 us
    all_to_all x4, blocking collectives, gather_all(): chunks = lax.all_to_all(copies, ('z', 'col'), 0, 0, tiled=True)  48.2 us
    pallas_call x6, Pallas kernels, call(): pl.pallas_call(kernel, out_shape=out_shapes, in_specs=[pl.BlockSpec(memor...  35.7 us
    all_to_all x1, waiting for transfers between devices, gather_all(): chunks = lax.all_to_all(copies, ('z', 'col'), 0, 0, tiled=True)  15.6 us
    ppermute x9, waiting for transfers between devices, swap_cores(): return lax.ppermute(value, 'core', [(0, 1), (1, 0)])  10.8 us
    ppermute x7, starting transfers between devices, to_row(): return lax.ppermute(value, ('z', 'core'), pairs)  10.7 us
    unnamed x8, local copies, waits for them, and re-layouts  7.28 us
    ppermute x7, waiting for transfers between devices, to_row(): return lax.ppermute(value, ('z', 'core'), pairs)  4.25 us
  transfers between devices with their start and end apart: 18, of which 11 were waited for; matrix products, arithmetic and copies ran while one was open for 6% of the time, Pallas kernels for 0%

profile of v2, /device:TPU:0, one launch (start us, length us, event | category | flops | bytes accessed | tf_op | source)
XLA Modules:
  0.0 209.5 jit_solution(1709798766002759672)
XLA Ops:
  0.7 2.6 %constant_dynamic-slice_fusion = (bf16[256,512]{1,0:T(8,128)(2,1)S(1)}, bf16[256,512]{1,0:T(8,128)(2,1)S(1)}, bf16[256,512]{1,0:T(8,128)(2,1)S(1)}, bf16[256,512...) fusion(bf16[256,4096]{1,0:T(8,128)(2,1)} %param.3, ...), kind=kLoop, calls=%fused_computation.43 | loop fusion | bytes 4194336 | tf_op jit(solution)/shard_map/dynamic_slice | solution.py:225
  3.2 3.0 %collective-permute-start.1 = (bf16[256,512]{1,0:T(8,128)(2,1)}, bf16[256,512]{1,0:T(8,128)(2,1)}, u32[]{:S(2)}, u32[]{:S(2)}) collective-permute-start(bf16[256,512]{1,0:T(8,128)(2,1)} %get-tuple-element.17), channel_id=1, source_target_pairs={{0,4},{2,6},{4,0},{6,2},{8,12},{10,14},{12,8},{14,10},{1,5},{3,7},... | collective-permute-start | bytes 786440 | tf_op jit(solution)/shard_map/ppermute | solution.py:229
  6.3 2.6 %collective-permute-start.2 = (bf16[256,512]{1,0:T(8,128)(2,1)}, bf16[256,512]{1,0:T(8,128)(2,1)}, u32[]{:S(2)}, u32[]{:S(2)}) collective-permute-start(bf16[256,512]{1,0:T(8,128)(2,1)} %get-tuple-element.16), channel_id=1, source_target_pairs={{0,8},{2,10},{4,12},{6,14},{8,0},{10,2},{12,4},{14,6},{1,9},{3,11}... | collective-permute-start | bytes 786440 | tf_op jit(solution)/shard_map/ppermute | solution.py:229
  9.5 3.8 %convolution_bitcast_fusion = f32[8,2,8,128]{3,2,1,0:T(8,128)S(1)} fusion(bf16[256,4096]{1,0:T(8,128)(2,1)} %param.3, s32[]{:T(128)S(6)} %xor.68, s32[4096]{0:T(1024)S(1)} %add_multiply_fusion), kind=kOutput, calls=%fused_computation | convolution fusion | flops 152043520 | bytes 2179076 | tf_op jit(solution)/shard_map/dot_general | solution.py:237
  14.0 3.3 %all-to-all-start = ((f32[2,64,128]{2,1,0:T(8,128)}), f32[2,64,128]{2,1,0:T(8,128)S(1)}, u32[]{:S(2)}, u32[]{:S(2)}) async-start(f32[2,64,128]{2,1,0:T(8,128)} %bitcast.55), calls=%async_computation | async-start | bytes 131072 | tf_op jit(solution)/shard_map/all_to_all | solution.py:241
  18.4 3.0 %all-to-all-done = f32[2,64,128]{2,1,0:T(8,128)S(1)} async-done(((f32[2,64,128]{2,1,0:T(8,128)}), f32[2,64,128]{2,1,0:T(8,128)S(1)}, u32[]{:S(2)}, u32[]{:S(2)}) %all-to-all-start) | async-done | bytes 65568 | tf_op jit(solution)/shard_map/all_to_all | solution.py:241
  22.1 3.4 %all-to-all-start.1 = ((f32[8,64,128]{2,1,0:T(8,128)}), f32[8,64,128]{2,1,0:T(8,128)S(1)}, u32[]{:S(2)}, u32[]{:S(2)}) async-start(f32[8,64,128]{2,1,0:T(8,128)} %broadcast_in_dim.13), calls=%async_computation.1 | async-start | bytes 524288 | tf_op jit(solution)/shard_map/all_to_all | solution.py:209
  25.6 1.7 collective-permute-start.6
  28.2 2.4 %collective-permute-start.7 = (bf16[256,512]{1,0:T(8,128)(2,1)S(1)}, bf16[256,512]{1,0:T(8,128)(2,1)}, u32[]{:S(2)}, u32[]{:S(2)}) collective-permute-start(bf16[256,512]{1,0:T(8,128)(2,1)S(1)} %get-tuple-element.12), channel_id=1, source_target_pairs={{0,14},{2,12},{4,10},{6,8},{8,6},{10,4},{12,2},{14,0},{1,15},{3,13... | collective-permute-start | bytes 786440 | tf_op jit(solution)/shard_map/ppermute | solution.py:229
  33.6 15.6 %all-to-all-done.1 = f32[8,64,128]{2,1,0:T(8,128)S(1)} async-done(((f32[8,64,128]{2,1,0:T(8,128)}), f32[8,64,128]{2,1,0:T(8,128)S(1)}, u32[]{:S(2)}, u32[]{:S(2)}) %all-to-all-start.1) | async-done | bytes 262176 | tf_op jit(solution)/shard_map/all_to_all | solution.py:209
  50.1 4.2 %collective-permute-done.6 = bf16[256,512]{1,0:T(8,128)(2,1)} collective-permute-done((bf16[256,512]{1,0:T(8,128)(2,1)S(1)}, bf16[256,512]{1,0:T(8,128)(2,1)}, u32[]{:S(2)}, u32[]{:S(2)}) %collective-permute-start.6) | collective-permute-done | bytes 262176 | tf_op jit(solution)/shard_map/ppermute | solution.py:229
  56.4 6.2 %shard_map.41 = (bf16[64,2048]{1,0:T(8,128)(2,1)S(1)}, f32[64,64]{1,0:T(8,128)S(1)}) custom-call(s32[1]{0:T(128)} %bitcast.at_ref, f32[2,4,2,64,128]{4,3,2,1,0:T(8,128)S(1)} %pad_maximum_fusion.z_ref), custom_call_target="tpu_custom_call" | custom-call | flops 402653184 | bytes 524288 | tf_op jit(solution)/shard_map/pallas_call | solution.py:185
  62.5 1.1 shard_map.42
  64.1 1.2 collective-permute-done.8
  65.3 17.4 %all_to_all.50 = f32[8,64,128]{2,1,0:T(8,128)S(1)} all-to-all(f32[8,64,128]{2,1,0:T(8,128)S(1)} %bitcast.58), channel_id=1, replica_groups=mesh['grp'=2,'z'=4,'core'=2,'col'=2] {'z','col'}, dimensions={0} | all-to-all | bytes 524288 | tf_op jit(solution)/shard_map/all_to_all | solution.py:203
  82.8 12.4 %all_to_all.51 = f32[8,64,128]{2,1,0:T(8,128)S(1)} all-to-all(f32[8,64,128]{2,1,0:T(8,128)S(1)} %broadcast_in_dim.14), channel_id=1, replica_groups=mesh['grp'=2,'z'=4,'core'=2,'col'=2] {'z','col'}, dimensions={0} | all-to-all | bytes 524288 | tf_op jit(solution)/shard_map/all_to_all | solution.py:209
  95.2 1.5 collective-permute-done.9
  96.8 7.2 %shard_map.43 = f32[2,4,2,64,128]{4,3,2,1,0:T(8,128)S(1)} custom-call(s32[1]{0:T(128)} %bitcast.at_ref, f32[2,4,2,64,128]{4,3,2,1,0:T(8,128)S(1)} %pad_maximum_fusion.1.z_ref, bf16[2048,512]{1,0:T(8,128)(2,1)S(1)} %constant_dynamic-update-slice_fusion.a_ref), custom_call_target="tpu_custom_call" | custom-call | flops 671088640 | bytes 2621440 | tf_op jit(solution)/shard_map/pallas_call | solution.py:185
  104.2 1.4 collective-permute-done.10
  105.7 12.6 %all_to_all.52 = f32[8,64,128]{2,1,0:T(8,128)S(1)} all-to-all(f32[8,64,128]{2,1,0:T(8,128)S(1)} %bitcast.59), channel_id=1, replica_groups=mesh['grp'=2,'z'=4,'core'=2,'col'=2] {'z','col'}, dimensions={0} | all-to-all | bytes 524288 | tf_op jit(solution)/shard_map/all_to_all | solution.py:203
  118.3 12.0 %all_to_all.53 = f32[8,64,128]{2,1,0:T(8,128)S(1)} all-to-all(f32[8,64,128]{2,1,0:T(8,128)S(1)} %broadcast_in_dim.15), channel_id=1, replica_groups=mesh['grp'=2,'z'=4,'core'=2,'col'=2] {'z','col'}, dimensions={0} | all-to-all | bytes 524288 | tf_op jit(solution)/shard_map/all_to_all | solution.py:209
  130.3 1.5 collective-permute-done.11
  131.9 7.2 %shard_map.44 = f32[2,4,2,64,128]{4,3,2,1,0:T(8,128)S(1)} custom-call(s32[1]{0:T(128)} %bitcast.at_ref, f32[2,4,2,64,128]{4,3,2,1,0:T(8,128)S(1)} %pad_maximum_fusion.2.z_ref, bf16[2048,512]{1,0:T(8,128)(2,1)S(1)} %constant_dynamic-update-slice_fusion.a_ref), custom_call_target="tpu_custom_call" | custom-call | flops 671088640 | bytes 2621440 | tf_op jit(solution)/shard_map/pallas_call | solution.py:185
  139.3 1.4 collective-permute-done.12
  140.7 12.6 %all_to_all.54 = f32[8,64,128]{2,1,0:T(8,128)S(1)} all-to-all(f32[8,64,128]{2,1,0:T(8,128)S(1)} %bitcast.60), channel_id=1, replica_groups=mesh['grp'=2,'z'=4,'core'=2,'col'=2] {'z','col'}, dimensions={0} | all-to-all | bytes 524288 | tf_op jit(solution)/shard_map/all_to_all | solution.py:203
  153.4 12.0 %all_to_all.55 = f32[8,64,128]{2,1,0:T(8,128)S(1)} all-to-all(f32[8,64,128]{2,1,0:T(8,128)S(1)} %broadcast_in_dim.16), channel_id=1, replica_groups=mesh['grp'=2,'z'=4,'core'=2,'col'=2] {'z','col'}, dimensions={0} | all-to-all | bytes 524288 | tf_op jit(solution)/shard_map/all_to_all | solution.py:209
  165.4 1.5 collective-permute-done.13
  166.9 7.2 %shard_map.45 = f32[2,4,2,64,128]{4,3,2,1,0:T(8,128)S(1)} custom-call(s32[1]{0:T(128)} %bitcast.at_ref, f32[2,4,2,64,128]{4,3,2,1,0:T(8,128)S(1)} %pad_maximum_fusion.3.z_ref, bf16[2048,512]{1,0:T(8,128)(2,1)S(1)} %constant_dynamic-update-slice_fusion.a_ref), custom_call_target="tpu_custom_call" | custom-call | flops 671088640 | bytes 2621440 | tf_op jit(solution)/shard_map/pallas_call | solution.py:185
  174.4 1.4 collective-permute-done.14
  175.8 12.6 %all_to_all.56 = f32[8,64,128]{2,1,0:T(8,128)S(1)} all-to-all(f32[8,64,128]{2,1,0:T(8,128)S(1)} %bitcast.61), channel_id=1, replica_groups=mesh['grp'=2,'z'=4,'core'=2,'col'=2] {'z','col'}, dimensions={0} | all-to-all | bytes 524288 | tf_op jit(solution)/shard_map/all_to_all | solution.py:203
  188.5 12.0 %all_to_all.57 = f32[8,64,128]{2,1,0:T(8,128)S(1)} all-to-all(f32[8,64,128]{2,1,0:T(8,128)S(1)} %broadcast_in_dim.17), channel_id=1, replica_groups=mesh['grp'=2,'z'=4,'core'=2,'col'=2] {'z','col'}, dimensions={0} | all-to-all | bytes 524288 | tf_op jit(solution)/shard_map/all_to_all | solution.py:209
  202.0 6.7 %shard_map.46 = f32[512,64]{1,0:T(8,128)S(1)} custom-call(s32[1]{0:T(128)} %bitcast.at_ref, f32[2,4,2,64,128]{4,3,2,1,0:T(8,128)S(1)} %pad_maximum_fusion.4.z_ref, bf16[2048,512]{1,0:T(8,128)(2,1)S(1)} %constant_dynamic-update-slice_fusion.a_ref), custom_call_target="tpu_custom_call" | custom-call | flops 671088640 | bytes 2621440 | tf_op jit(solution)/shard_map/pallas_call | solution.py:185
  (55 shorter events, 13.1 us)
Async XLA Ops:
  3.2 22.3 %collective-permute-start.1 = (bf16[256,512]{1,0:T(8,128)(2,1)}, bf16[256,512]{1,0:T(8,128)(2,1)}, u32[]{:S(2)}, u32[]{:S(2)}) collective-permute-start(bf16[256,512]{1,0:T(8,128)(2,1)} %get-tuple-element.17), channel_id=1, source_target_pairs={{0,4},{2,6},{4,0},{6,2},{8,12},{10,14},{12,8},{14,10},{1,5},{3,7},... | collective-permute-start | bytes 786440 | tf_op jit(solution)/shard_map/ppermute | solution.py:229
  6.3 22.0 %collective-permute-start.2 = (bf16[256,512]{1,0:T(8,128)(2,1)}, bf16[256,512]{1,0:T(8,128)(2,1)}, u32[]{:S(2)}, u32[]{:S(2)}) collective-permute-start(bf16[256,512]{1,0:T(8,128)(2,1)} %get-tuple-element.16), channel_id=1, source_target_pairs={{0,8},{2,10},{4,12},{6,14},{8,0},{10,2},{12,4},{14,6},{1,9},{3,11}... | collective-permute-start | bytes 786440 | tf_op jit(solution)/shard_map/ppermute | solution.py:229
  14.0 7.4 %all-to-all-start = ((f32[2,64,128]{2,1,0:T(8,128)}), f32[2,64,128]{2,1,0:T(8,128)S(1)}, u32[]{:S(2)}, u32[]{:S(2)}) async-start(f32[2,64,128]{2,1,0:T(8,128)} %bitcast.55), calls=%async_computation | async-start | bytes 131072 | tf_op jit(solution)/shard_map/all_to_all | solution.py:241
  17.3 14.3 %collective-permute-start.3 = (bf16[256,512]{1,0:T(8,128)(2,1)}, bf16[256,512]{1,0:T(8,128)(2,1)}, u32[]{:S(2)}, u32[]{:S(2)}) collective-permute-start(bf16[256,512]{1,0:T(8,128)(2,1)} %get-tuple-element.15), channel_id=1, source_target_pairs={{0,12},{2,14},{4,8},{6,10},{8,4},{10,6},{12,0},{14,2},{1,13},{3,15... | collective-permute-start | bytes 786440 | tf_op jit(solution)/shard_map/ppermute | solution.py:229
  17.4 15.2 %collective-permute-start.4 = (bf16[256,512]{1,0:T(8,128)(2,1)S(1)}, bf16[256,512]{1,0:T(8,128)(2,1)}, u32[]{:S(2)}, u32[]{:S(2)}) collective-permute-start(bf16[256,512]{1,0:T(8,128)(2,1)S(1)} %get-tuple-element.14), channel_id=1, source_target_pairs={{0,2},{2,0},{4,6},{6,4},{8,10},{10,8},{12,14},{14,12},{1,3},{3,1},... | collective-permute-start | bytes 786440 | tf_op jit(solution)/shard_map/ppermute | solution.py:229
  17.5 31.7 %collective-permute-start.5 = (bf16[256,512]{1,0:T(8,128)(2,1)S(1)}, bf16[256,512]{1,0:T(8,128)(2,1)}, u32[]{:S(2)}, u32[]{:S(2)}) collective-permute-start(bf16[256,512]{1,0:T(8,128)(2,1)S(1)} %get-tuple-element.13), channel_id=1, source_target_pairs={{0,6},{2,4},{4,2},{6,0},{8,14},{10,12},{12,10},{14,8},{1,7},{3,5},... | collective-permute-start | bytes 786440 | tf_op jit(solution)/shard_map/ppermute | solution.py:229
  22.1 27.0 %all-to-all-start.1 = ((f32[8,64,128]{2,1,0:T(8,128)}), f32[8,64,128]{2,1,0:T(8,128)S(1)}, u32[]{:S(2)}, u32[]{:S(2)}) async-start(f32[8,64,128]{2,1,0:T(8,128)} %broadcast_in_dim.13), calls=%async_computation.1 | async-start | bytes 524288 | tf_op jit(solution)/shard_map/all_to_all | solution.py:209
  25.6 28.8 %collective-permute-start.6 = (bf16[256,512]{1,0:T(8,128)(2,1)S(1)}, bf16[256,512]{1,0:T(8,128)(2,1)}, u32[]{:S(2)}, u32[]{:S(2)}) collective-permute-start(bf16[256,512]{1,0:T(8,128)(2,1)S(1)} %get-tuple-element.19), channel_id=1, source_target_pairs={{0,10},{2,8},{4,14},{6,12},{8,2},{10,0},{12,6},{14,4},{1,11},{3,9}... | collective-permute-start | bytes 786440 | tf_op jit(solution)/shard_map/ppermute | solution.py:229
  28.2 27.1 %collective-permute-start.7 = (bf16[256,512]{1,0:T(8,128)(2,1)S(1)}, bf16[256,512]{1,0:T(8,128)(2,1)}, u32[]{:S(2)}, u32[]{:S(2)}) collective-permute-start(bf16[256,512]{1,0:T(8,128)(2,1)S(1)} %get-tuple-element.12), channel_id=1, source_target_pairs={{0,14},{2,12},{4,10},{6,8},{8,6},{10,4},{12,2},{14,0},{1,15},{3,13... | collective-permute-start | bytes 786440 | tf_op jit(solution)/shard_map/ppermute | solution.py:229
  49.1 7.2 %collective-permute-start = (f32[4,2,64,128]{3,2,1,0:T(8,128)S(1)}, f32[4,2,64,128]{3,2,1,0:T(8,128)S(1)}, u32[]{:S(2)}, u32[]{:S(2)}) collective-permute-start(f32[4,2,64,128]{3,2,1,0:T(8,128)S(1)} %bitcast.62), channel_id=1, source_target_pairs={{0,2},{2,0},{1,3},{3,1},{4,6},{6,4},{5,7},{7,5},{8,10},{10,8},{9,1... | collective-permute-start | bytes 786440 | tf_op jit(solution)/shard_map/ppermute | solution.py:197
  63.7 1.6 collective-permute-start.8
  95.2 1.5 collective-permute-start.9
  104.0 1.6 collective-permute-start.10
  130.3 1.5 collective-permute-start.11
  139.1 1.6 collective-permute-start.12
  165.4 1.5 collective-permute-start.13
  174.2 1.6 collective-permute-start.14
  200.5 1.5 collective-permute-start.15

commit v3 on v2

--- a/solution.py
+++ b/solution.py
@@ -134,16 +134,8 @@
 
 
 def wide_of(z_ref, at_ref):
-    halves, n_z, n_col = z_ref.shape[:3]
-    return jnp.concatenate(
-        [
-            z_ref[h, at_ref[0] ^ zo, c]
-            for h in range(halves)
-            for zo in range(n_z)
-            for c in range(n_col)
-        ],
-        axis=1,
-    )
+    chunks = [z_ref[at_ref[i]].astype(jnp.float32) for i in range(z_ref.shape[0])]
+    return jnp.concatenate(chunks, axis=1)
 
 
 def narrow_basis(z_ref, at_ref):
@@ -151,40 +143,40 @@
     return small_times_wide(inverse_two, first).astype(jnp.bfloat16), upper
 
 
-def power_body(basis, a_ref, at_ref, p_ref):
+def power_body(basis, a_ref, at_ref, keep_ref, send_ref, all_ref):
     weights = dot_nn(basis, a_ref[...]).astype(jnp.bfloat16)
     forth = dot_nt(weights, a_ref[...])
-    halves, n_z, n_col, unused, width = p_ref.shape
-    for h in range(halves):
-        for zo in range(n_z):
-            for c in range(n_col):
-                i = (h * n_z + zo) * n_col + c
-                p_ref[h, at_ref[0] ^ zo, c] = forth[:, width * i : width * (i + 1)]
+    half, unused, width = keep_ref.shape
+    for i in range(2 * half):
+        all_ref[at_ref[i]] = forth[:, width * i : width * (i + 1)]
+    keep_ref[...] = all_ref[:half]
+    send_ref[...] = all_ref[half:].astype(send_ref.dtype)
 
 
 def orth_kernel(at_ref, z_ref, basis_ref, upper_ref):
     basis_ref[...], upper_ref[...] = narrow_basis(z_ref, at_ref)
 
 
-def power_kernel(at_ref, basis_ref, a_ref, p_ref):
-    power_body(basis_ref[...], a_ref, at_ref, p_ref)
-
-
-def orth_power_kernel(at_ref, z_ref, a_ref, p_ref):
+def power_kernel(at_ref, basis_ref, a_ref, keep_ref, send_ref, all_ref):
+    power_body(basis_ref[...], a_ref, at_ref, keep_ref, send_ref, all_ref)
+
+
+def orth_power_kernel(at_ref, z_ref, a_ref, keep_ref, send_ref, all_ref):
     basis, unused = narrow_basis(z_ref, at_ref)
-    power_body(basis, a_ref, at_ref, p_ref)
+    power_body(basis, a_ref, at_ref, keep_ref, send_ref, all_ref)
 
 
 def last_kernel(at_ref, z_ref, a_ref, out_ref):
     basis, unused = narrow_basis(z_ref, at_ref)
-    out_ref[...] = dot_nn(basis, a_ref[...]).T
-
-
-def call(kernel, out_shapes, flops, at, *operands):
+    out_ref[...] = dot_nn(basis, a_ref[...])
+
+
+def call(kernel, out_shapes, flops, at, *operands, scratch=()):
     moved = sum(x.size * x.dtype.itemsize for x in operands)
     return pl.pallas_call(
         kernel,
         out_shape=out_shapes,
+        scratch_shapes=scratch,
         in_specs=[pl.BlockSpec(memory_space=pltpu.SMEM)]
         + [pl.BlockSpec(memory_space=pltpu.VMEM)] * len(operands),
         out_specs=jax.tree.map(lambda _: pl.BlockSpec(memory_space=pltpu.VMEM), out_shapes),
@@ -193,75 +185,105 @@
     )(at, *operands)
 
 
-def swap_cores(value):
-    return lax.ppermute(value, "core", [(0, 1), (1, 0)])
-
-
-def sum_scatter(parts):
-    total = parts[0] + swap_cores(parts[1])
-    total = total.reshape((-1,) + total.shape[2:])
-    return jnp.sum(lax.all_to_all(total, ("z", "col"), 0, 0, tiled=True), axis=0)
-
-
-def gather_all(own):
-    n_z, n_col = lax.axis_size("z"), lax.axis_size("col")
-    copies = jnp.broadcast_to(own[None], (n_z * n_col,) + own.shape)
-    chunks = lax.all_to_all(copies, ("z", "col"), 0, 0, tiled=True)
-    chunks = chunks.reshape((n_z, n_col) + own.shape)
-    return jnp.stack([chunks, swap_cores(chunks)])
+def bits(size):
+    return [1 << k for k in range(size.bit_length() - 1)]
+
+
+def from_xor(value, axis, offset):
+    size = lax.axis_size(axis)
+    return lax.ppermute(value, axis, [(i, i ^ offset) for i in range(size)])
+
+
+def stages():
+    steps = [("col", bit) for bit in bits(lax.axis_size("col"))]
+    steps += [("z", bit) for bit in bits(lax.axis_size("z"))]
+    return [(axis, bit, (axis, bit) != steps[-1]) for axis, bit in steps]
+
+
+def sum_parts(keep, send, dtype):
+    total = keep + from_xor(send, "core", 1).astype(jnp.float32)
+    for axis, bit, halved in stages():
+        if halved:
+            half = total.shape[0] // 2
+            other = from_xor(total[half:].astype(dtype), axis, bit)
+            total = total[:half] + other.astype(jnp.float32)
+        else:
+            mine = total.astype(dtype)
+            other = from_xor(mine, axis, bit)
+            total = mine.astype(jnp.float32) + other.astype(jnp.float32)
+    return total.astype(dtype)
+
+
+def gather_parts(own):
+    for axis, bit, halved in reversed(stages()):
+        if halved:
+            own = jnp.concatenate([own, from_xor(own, axis, bit)])
+    return jnp.concatenate([own, from_xor(own, "core", 1)])
+
+
+def chunk_places(digits, n_col, n_z):
+    here = {name: lax.axis_index(name) for name in ("z", "core", "col")}
+    index = jnp.arange(n_z * 2 * n_col, dtype=jnp.int32)
+    coordinate = {"z": index // (2 * n_col), "core": index // n_col % 2, "col": index % n_col}
+    place = jnp.zeros_like(index)
+    for axis, bit, relative in digits:
+        value = coordinate[axis] ^ here[axis] if relative else coordinate[axis]
+        place = place * 2 + (value // bit) % 2
+    return place.astype(jnp.int32)
 
 
 def per_device_transposed(sketch_base, states):
     n_z, n_core, n_col = lax.axis_size("z"), lax.axis_size("core"), lax.axis_size("col")
     n_row = n_z * n_core
-    z_at, core, col = lax.axis_index("z"), lax.axis_index("core"), lax.axis_index("col")
-    row = z_at * n_core + core
     rows_local, width_local = states.shape
     rows_total, width_total = rows_local * n_row, width_local * n_col
     chunk = rows_local // n_col
     cols = width_local // n_row
-
-    def block(offset):
-        return lax.dynamic_slice_in_dim(states, (row ^ offset) * cols, cols, 1)
-
-    def to_row(value, offset):
-        pairs = [(i, i ^ offset) for i in range(n_row)]
-        return lax.ppermute(value, ("z", "core"), pairs)
-
-    received = {0: block(0)}
-    for offset in sorted(range(1, n_row), reverse=True):
-        received[offset] = to_row(block(offset), offset)
-
+    n_chunks = n_row * n_col
+
+    by_target = states.reshape(rows_local, n_row, cols).transpose(1, 0, 2)
+    a = lax.all_to_all(by_target, ("z", "core"), 0, 0, tiled=True).reshape(rows_total, cols)
+
+    col = lax.axis_index("col")
     feature_index = col * width_local + jnp.arange(width_local, dtype=jnp.int32)
     omega = sketch_table(sketch_base[0], feature_index, RANK)
-    partial = lax.dot_general(
+    z = lax.dot_general(
         omega, states, (((0,), (1,)), ((), ())), preferred_element_type=jnp.float32
     )
-    partial = partial.reshape(RANK, n_col, chunk).transpose(1, 0, 2)
-    own = jnp.sum(lax.all_to_all(partial, "col", 0, 0, tiled=True), axis=0)
-    z = gather_all(own)
-
-    a = jnp.concatenate([received[2 * zo + other] for other in range(2) for zo in range(n_z)])
-    at = z_at[None].astype(jnp.int32)
+    for bit in bits(n_col):
+        z = z + from_xor(z, "col", bit)
+    z = z.reshape(RANK, n_col, chunk).transpose(1, 0, 2)
+    z_bits = bits(n_z)[::-1]
+    for bit in z_bits:
+        z = jnp.concatenate([z, from_xor(z, "z", bit)])
+    z = jnp.concatenate([z, from_xor(z, "core", 1)])
+    digits = [("core", 1, True)] + [("z", bit, True) for bit in z_bits[::-1]]
+    at_first = chunk_places(digits + [("col", bit, False) for bit in bits(n_col)[::-1]], n_col, n_z)
+    at = chunk_places([("core", 1, True)] + stages(), n_col, n_z)
 
     f32 = jnp.float32
     square = jax.ShapeDtypeStruct((RANK, RANK), f32)
     wide = jax.ShapeDtypeStruct((RANK, rows_total), jnp.bfloat16)
-    chunks = jax.ShapeDtypeStruct((2, n_z, n_col, RANK, chunk), f32)
     orth_flops = 8 * 64 * 64 * rows_total * 6
     power_flops = 4 * 64 * rows_total * cols
 
-    basis, upper = call(orth_kernel, (wide, square), orth_flops, at, z)
+    def sent_as(dtype):
+        shape = (n_chunks // 2, RANK, chunk)
+        return jax.ShapeDtypeStruct(shape, f32), jax.ShapeDtypeStruct(shape, dtype)
+
+    basis, upper = call(orth_kernel, (wide, square), orth_flops, at_first, z)
     factor = upper.T * (1.0 / math.sqrt(rows_total * width_total))
-    parts = call(power_kernel, chunks, power_flops, at, basis, a)
+    dtype = f32
+    scratch = (pltpu.VMEM((n_chunks, RANK, chunk), f32),)
+    parts = call(power_kernel, sent_as(dtype), power_flops, at, basis, a, scratch=scratch)
     for step in range(POWER - 1):
-        z = gather_all(sum_scatter(parts))
-        parts = call(orth_power_kernel, chunks, orth_flops + power_flops, at, z, a)
-    z = gather_all(sum_scatter(parts))
-    loadings = call(
-        last_kernel, jax.ShapeDtypeStruct((cols, RANK), f32), orth_flops + power_flops, at, z, a
-    )
-    return loadings, factor
+        z = gather_parts(sum_parts(*parts, dtype))
+        dtype = jnp.bfloat16
+        flops = orth_flops + power_flops
+        parts = call(orth_power_kernel, sent_as(dtype), flops, at, z, a, scratch=scratch)
+    z = gather_parts(sum_parts(*parts, dtype))
+    loadings = jax.ShapeDtypeStruct((RANK, cols), f32)
+    return call(last_kernel, loadings, orth_flops + power_flops, at, z, a).T, factor
 
 
 def local_gram(basis):

time: 210 us -> 211 us (level)
  blocking collectives: 103 us -> 0 us
  waiting for transfers between devices: 33.7 us -> 134 us
  local copies, waits for them, and re-layouts: 12.4 us -> 3.93 us
  starting transfers between devices: 18.5 us -> 26.7 us
  Pallas kernels: 35.7 us -> 39.6 us
    ppermute x16 -> x32, waiting for transfers between devices: 15.1 us -> 134 us  [from_xor(): return lax.ppermute(value, axis, [(i, i ^ offset) for i in range(size)])]
    all_to_all x8 -> x0, blocking collectives: 103 us -> none  [the longest x4 55.2 us: sum_scatter(): lax.all_to_all(total, ('z', 'col'), 0, 0, tiled=True)]
    all_to_all x2 -> x1, waiting for transfers between devices: 18.6 us -> 0.01 us  [per_device_transposed(): lax.all_to_all(by_target, ('z', 'core'), 0, 0, tiled=True)]
    ppermute x16 -> x32, starting transfers between devices: 11.8 us -> 20.4 us  [from_xor(): return lax.ppermute(value, axis, [(i, i ^ offset) for i in range(size)])]
    unnamed x8 -> x1, local copies, waits for them, and re-layouts: 7.28 us -> 0.7 us
    pallas_call x6, Pallas kernels: 35.7 us -> 39.6 us  [call(): pl.pallas_call(kernel, out_shape=out_shapes, scratch_shapes=scratch, in_s...]
    dynamic_slice x1 -> x0, local copies, waits for them, and re-layouts: 2.55 us -> none  [block(): return lax.dynamic_slice_in_dim(states, (row ^ offset) * cols, cols, 1)]
    reshape x1, local copies, waits for them, and re-layouts: 0.67 us -> 3.16 us  [per_device_transposed(): by_target = states.reshape(rows_local, n_row, cols).transpose(1, 0, 2)]
  transfers between devices with their start and end apart: 18 -> 33, of which waited for: 11 -> 32; matrix products, arithmetic and copies ran while one was open for 6% -> 2% of each run, Pallas kernels for 0% -> 3%
where the time goes in v3:
time: 211 us
  waiting for transfers between devices  134 us (64%)
  Pallas kernels  39.6 us (19%)
  starting transfers between devices  26.7 us (13%)
  local copies, waits for them, and re-layouts  3.93 us (2%)
  matrix products  3.83 us (2%)
    ppermute x32, waiting for transfers between devices, from_xor(): return lax.ppermute(value, axis, [(i, i ^ offset) for i in range(size)])  134 us
    pallas_call x6, Pallas kernels, call(): pl.pallas_call(kernel, out_shape=out_shapes, scratch_shapes=scratch, in_s...  39.6 us
    ppermute x32, starting transfers between devices, from_xor(): return lax.ppermute(value, axis, [(i, i ^ offset) for i in range(size)])  20.4 us
    all_to_all x1, starting transfers between devices, per_device_transposed(): lax.all_to_all(by_target, ('z', 'core'), 0, 0, tiled=True)  6.33 us
  transfers between devices with their start and end apart: 33, of which 32 were waited for; matrix products, arithmetic and copies ran while one was open for 2% of the time, Pallas kernels for 3%

profile of v3, /device:TPU:0, one launch (start us, length us, event | category | flops | bytes accessed | tf_op | source)
XLA Modules:
  0.0 210.9 jit_solution(3120945526434191851)
XLA Ops:
  0.6 3.2 %copy.16 = bf16[32,8,8,512]{3,2,0,1:T(8,128)(2,1)} copy(bf16[32,8,8,512]{3,2,1,0:T(8,128)(2,1)} %bitcast.28) | data formatting | bytes 4194304 | tf_op jit(solution)/shard_map/reshape | solution.py:244
  3.8 6.3 %all-to-all-start = ((bf16[8,256,512]{2,1,0:T(8,128)(2,1)}), bf16[8,256,512]{2,1,0:T(8,128)(2,1)S(1)}, u32[]{:S(2)}, u32[]{:S(2)}) async-start(bf16[8,256,512]{2,1,0:T(8,128)(2,1)} %bitcast.27), calls=%async_computation | async-start | bytes 4194304 | tf_op jit(solution)/shard_map/all_to_all | solution.py:245
  10.8 3.8 %fusion = f32[64,256]{1,0:T(8,128)S(1)} fusion(bf16[256,4096]{1,0:T(8,128)(2,1)} %param.3, s32[]{:T(128)S(6)} %xor.77, s32[4096]{0:T(1024)S(1)} %add_multiply_fusion), kind=kOutput, calls=%fused_computation.2 | convolution fusion | flops 152043520 | bytes 2179076 | tf_op jit(solution)/shard_map/dot_general | solution.py:250
  16.2 3.0 %collective-permute-done = f32[64,256]{1,0:T(8,128)S(1)} collective-permute-done((f32[64,256]{1,0:T(8,128)S(1)}, f32[64,256]{1,0:T(8,128)S(1)}, u32[]{:S(2)}, u32[]{:S(2)}) %collective-permute-start) | collective-permute-done | bytes 65568 | tf_op jit(solution)/shard_map/ppermute | solution.py:194
  19.2 2.7 %collective-permute-start.1 = (f32[2,64,128]{2,1,0:T(8,128)S(1)}, f32[2,64,128]{2,1,0:T(8,128)S(1)}, u32[]{:S(2)}, u32[]{:S(2)}) collective-permute-start(f32[2,64,128]{2,1,0:T(8,128)S(1)} %bitcast_bitcast_fusion.1), channel_id=1, source_target_pairs={{0,8},{4,12},{8,0},{12,4},{1,9},{5,13},{9,1},{13,5},{2,10},{6,14},... | collective-permute-start | bytes 196616 | tf_op jit(solution)/shard_map/ppermute | solution.py:194
  21.9 40.1 %collective-permute-done.1 = f32[2,64,128]{2,1,0:T(8,128)S(1)} collective-permute-done((f32[2,64,128]{2,1,0:T(8,128)S(1)}, f32[2,64,128]{2,1,0:T(8,128)S(1)}, u32[]{:S(2)}, u32[]{:S(2)}) %collective-permute-start.1) | collective-permute-done | bytes 65568 | tf_op jit(solution)/shard_map/ppermute | solution.py:194
  62.1 5.0 %collective-permute-done.2 = f32[4,64,128]{2,1,0:T(8,128)S(1)} collective-permute-done((f32[4,64,128]{2,1,0:T(8,128)S(1)}, f32[4,64,128]{2,1,0:T(8,128)S(1)}, u32[]{:S(2)}, u32[]{:S(2)}) %collective-permute-start.2) | collective-permute-done | bytes 131104 | tf_op jit(solution)/shard_map/ppermute | solution.py:194
  68.8 6.7 %shard_map.41 = (bf16[64,2048]{1,0:T(8,128)(2,1)S(1)}, f32[64,64]{1,0:T(8,128)S(1)}) custom-call(s32[16]{0:T(128)S(1)} %fusion.20.at_ref, f32[16,64,128]{2,1,0:T(8,128)S(1)} %pad_maximum_fusion.z_ref), custom_call_target="tpu_custom_call" | custom-call | flops 402653184 | bytes 524288 | tf_op jit(solution)/shard_map/pallas_call | solution.py:176
  80.5 4.0 %collective-permute-done.5 = f32[4,64,128]{2,1,0:T(8,128)S(1)} collective-permute-done((f32[4,64,128]{2,1,0:T(8,128)S(1)}, f32[4,64,128]{2,1,0:T(8,128)S(1)}, u32[]{:S(2)}, u32[]{:S(2)}) %collective-permute-start.5) | collective-permute-done | bytes 131104 | tf_op jit(solution)/shard_map/ppermute | solution.py:194
  84.9 4.0 %collective-permute-done.6 = f32[2,64,128]{2,1,0:T(8,128)S(1)} collective-permute-done((f32[2,64,128]{2,1,0:T(8,128)S(1)}, f32[2,64,128]{2,1,0:T(8,128)S(1)}, u32[]{:S(2)}, u32[]{:S(2)}) %collective-permute-start.6) | collective-permute-done | bytes 65568 | tf_op jit(solution)/shard_map/ppermute | solution.py:194
  89.5 5.1 %collective-permute-done.7 = f32[2,64,128]{2,1,0:T(8,128)S(1)} collective-permute-done((f32[2,64,128]{2,1,0:T(8,128)S(1)}, f32[2,64,128]{2,1,0:T(8,128)S(1)}, u32[]{:S(2)}, u32[]{:S(2)}) %collective-permute-start.7) | collective-permute-done | bytes 65568 | tf_op jit(solution)/shard_map/ppermute | solution.py:194
  94.7 4.3 %collective-permute-done.8 = f32[2,64,128]{2,1,0:T(8,128)S(1)} collective-permute-done((f32[2,64,128]{2,1,0:T(8,128)S(1)}, f32[2,64,128]{2,1,0:T(8,128)S(1)}, u32[]{:S(2)}, u32[]{:S(2)}) %collective-permute-start.8) | collective-permute-done | bytes 65568 | tf_op jit(solution)/shard_map/ppermute | solution.py:194
  100.5 3.5 %collective-permute-done.9 = f32[4,64,128]{2,1,0:T(8,128)S(1)} collective-permute-done((f32[4,64,128]{2,1,0:T(8,128)S(1)}, f32[4,64,128]{2,1,0:T(8,128)S(1)}, u32[]{:S(2)}, u32[]{:S(2)}) %collective-permute-start.9) | collective-permute-done | bytes 131104 | tf_op jit(solution)/shard_map/ppermute | solution.py:194
  105.6 7.8 %shard_map.43 = (f32[8,64,128]{2,1,0:T(8,128)S(1)}, bf16[8,64,128]{2,1,0:T(8,128)(2,1)S(1)}) custom-call(s32[16]{0:T(128)S(1)} %fusion.18.at_ref, f32[16,64,128]{2,1,0:T(8,128)S(1)} %pad_maximum_fusion.1.z_ref, bf16[2048,512]{1,0:T(8,128)(2,1)S(1)} %bitcast.23), custom_call_target="tpu_custom_call" | custom-call | flops 671088640 | bytes 2621440 | tf_op jit(solution)/shard_map/pallas_call | solution.py:176
  116.5 2.8 %collective-permute-done.12 = bf16[4,64,128]{2,1,0:T(8,128)(2,1)S(1)} collective-permute-done((bf16[4,64,128]{2,1,0:T(8,128)(2,1)S(1)}, bf16[4,64,128]{2,1,0:T(8,128)(2,1)S(1)}, u32[]{:S(2)}, u32[]{:S(2)}) %collective-permute-start.12) | collective-permute-done | bytes 65568 | tf_op jit(solution)/shard_map/ppermute | solution.py:194
  119.4 3.9 %collective-permute-done.13 = bf16[2,64,128]{2,1,0:T(8,128)(2,1)S(1)} collective-permute-done((bf16[2,64,128]{2,1,0:T(8,128)(2,1)S(1)}, bf16[2,64,128]{2,1,0:T(8,128)(2,1)S(1)}, u32[]{:S(2)}, u32[]{:S(2)}) %collective-permute-start.13) | collective-permute-done | bytes 32800 | tf_op jit(solution)/shard_map/ppermute | solution.py:194
  123.8 4.7 %collective-permute-done.14 = bf16[2,64,128]{2,1,0:T(8,128)(2,1)S(1)} collective-permute-done((bf16[2,64,128]{2,1,0:T(8,128)(2,1)S(1)}, bf16[2,64,128]{2,1,0:T(8,128)(2,1)S(1)}, u32[]{:S(2)}, u32[]{:S(2)}) %collective-permute-start.14) | collective-permute-done | bytes 32800 | tf_op jit(solution)/shard_map/ppermute | solution.py:194
  128.6 3.9 %collective-permute-done.15 = bf16[2,64,128]{2,1,0:T(8,128)(2,1)S(1)} collective-permute-done((bf16[2,64,128]{2,1,0:T(8,128)(2,1)S(1)}, bf16[2,64,128]{2,1,0:T(8,128)(2,1)S(1)}, u32[]{:S(2)}, u32[]{:S(2)}) %collective-permute-start.15) | collective-permute-done | bytes 32800 | tf_op jit(solution)/shard_map/ppermute | solution.py:194
  134.0 2.8 %collective-permute-done.16 = bf16[4,64,128]{2,1,0:T(8,128)(2,1)S(1)} collective-permute-done((bf16[4,64,128]{2,1,0:T(8,128)(2,1)S(1)}, bf16[4,64,128]{2,1,0:T(8,128)(2,1)S(1)}, u32[]{:S(2)}, u32[]{:S(2)}) %collective-permute-start.16) | collective-permute-done | bytes 65568 | tf_op jit(solution)/shard_map/ppermute | solution.py:194
  138.3 7.8 %shard_map.44 = (f32[8,64,128]{2,1,0:T(8,128)S(1)}, bf16[8,64,128]{2,1,0:T(8,128)(2,1)S(1)}) custom-call(s32[16]{0:T(128)S(1)} %fusion.18.at_ref, bf16[16,64,128]{2,1,0:T(8,128)(2,1)S(1)} %pad_maximum_fusion.4.z_ref, bf16[2048,512]{1,0:T(8,128)(2,1)S(1)} %bitcast.24), custom_call_target="tpu_custom_call" | custom-call | flops 671088640 | bytes 2359296 | tf_op jit(solution)/shard_map/pallas_call | solution.py:176
  149.1 2.8 %collective-permute-done.19 = bf16[4,64,128]{2,1,0:T(8,128)(2,1)S(1)} collective-permute-done((bf16[4,64,128]{2,1,0:T(8,128)(2,1)S(1)}, bf16[4,64,128]{2,1,0:T(8,128)(2,1)S(1)}, u32[]{:S(2)}, u32[]{:S(2)}) %collective-permute-start.19) | collective-permute-done | bytes 65568 | tf_op jit(solution)/shard_map/ppermute | solution.py:194
  152.0 3.9 %collective-permute-done.20 = bf16[2,64,128]{2,1,0:T(8,128)(2,1)S(1)} collective-permute-done((bf16[2,64,128]{2,1,0:T(8,128)(2,1)S(1)}, bf16[2,64,128]{2,1,0:T(8,128)(2,1)S(1)}, u32[]{:S(2)}, u32[]{:S(2)}) %collective-permute-start.20) | collective-permute-done | bytes 32800 | tf_op jit(solution)/shard_map/ppermute | solution.py:194
  156.2 4.7 %collective-permute-done.21 = bf16[2,64,128]{2,1,0:T(8,128)(2,1)S(1)} collective-permute-done((bf16[2,64,128]{2,1,0:T(8,128)(2,1)S(1)}, bf16[2,64,128]{2,1,0:T(8,128)(2,1)S(1)}, u32[]{:S(2)}, u32[]{:S(2)}) %collective-permute-start.21) | collective-permute-done | bytes 32800 | tf_op jit(solution)/shard_map/ppermute | solution.py:194
  161.0 3.9 %collective-permute-done.22 = bf16[2,64,128]{2,1,0:T(8,128)(2,1)S(1)} collective-permute-done((bf16[2,64,128]{2,1,0:T(8,128)(2,1)S(1)}, bf16[2,64,128]{2,1,0:T(8,128)(2,1)S(1)}, u32[]{:S(2)}, u32[]{:S(2)}) %collective-permute-start.22) | collective-permute-done | bytes 32800 | tf_op jit(solution)/shard_map/ppermute | solution.py:194
  166.5 2.8 %collective-permute-done.23 = bf16[4,64,128]{2,1,0:T(8,128)(2,1)S(1)} collective-permute-done((bf16[4,64,128]{2,1,0:T(8,128)(2,1)S(1)}, bf16[4,64,128]{2,1,0:T(8,128)(2,1)S(1)}, u32[]{:S(2)}, u32[]{:S(2)}) %collective-permute-start.23) | collective-permute-done | bytes 65568 | tf_op jit(solution)/shard_map/ppermute | solution.py:194
  170.7 7.8 %shard_map.45 = (f32[8,64,128]{2,1,0:T(8,128)S(1)}, bf16[8,64,128]{2,1,0:T(8,128)(2,1)S(1)}) custom-call(s32[16]{0:T(128)S(1)} %fusion.18.at_ref, bf16[16,64,128]{2,1,0:T(8,128)(2,1)S(1)} %pad_maximum_fusion.5.z_ref, bf16[2048,512]{1,0:T(8,128)(2,1)S(1)} %bitcast.25), custom_call_target="tpu_custom_call" | custom-call | flops 671088640 | bytes 2359296 | tf_op jit(solution)/shard_map/pallas_call | solution.py:176
  181.5 2.8 %collective-permute-done.26 = bf16[4,64,128]{2,1,0:T(8,128)(2,1)S(1)} collective-permute-done((bf16[4,64,128]{2,1,0:T(8,128)(2,1)S(1)}, bf16[4,64,128]{2,1,0:T(8,128)(2,1)S(1)}, u32[]{:S(2)}, u32[]{:S(2)}) %collective-permute-start.26) | collective-permute-done | bytes 65568 | tf_op jit(solution)/shard_map/ppermute | solution.py:194
  184.4 3.9 %collective-permute-done.27 = bf16[2,64,128]{2,1,0:T(8,128)(2,1)S(1)} collective-permute-done((bf16[2,64,128]{2,1,0:T(8,128)(2,1)S(1)}, bf16[2,64,128]{2,1,0:T(8,128)(2,1)S(1)}, u32[]{:S(2)}, u32[]{:S(2)}) %collective-permute-start.27) | collective-permute-done | bytes 32800 | tf_op jit(solution)/shard_map/ppermute | solution.py:194
  188.6 4.7 %collective-permute-done.28 = bf16[2,64,128]{2,1,0:T(8,128)(2,1)S(1)} collective-permute-done((bf16[2,64,128]{2,1,0:T(8,128)(2,1)S(1)}, bf16[2,64,128]{2,1,0:T(8,128)(2,1)S(1)}, u32[]{:S(2)}, u32[]{:S(2)}) %collective-permute-start.28) | collective-permute-done | bytes 32800 | tf_op jit(solution)/shard_map/ppermute | solution.py:194
  193.4 3.9 %collective-permute-done.29 = bf16[2,64,128]{2,1,0:T(8,128)(2,1)S(1)} collective-permute-done((bf16[2,64,128]{2,1,0:T(8,128)(2,1)S(1)}, bf16[2,64,128]{2,1,0:T(8,128)(2,1)S(1)}, u32[]{:S(2)}, u32[]{:S(2)}) %collective-permute-start.29) | collective-permute-done | bytes 32800 | tf_op jit(solution)/shard_map/ppermute | solution.py:194
  198.9 2.8 %collective-permute-done.30 = bf16[4,64,128]{2,1,0:T(8,128)(2,1)S(1)} collective-permute-done((bf16[4,64,128]{2,1,0:T(8,128)(2,1)S(1)}, bf16[4,64,128]{2,1,0:T(8,128)(2,1)S(1)}, u32[]{:S(2)}, u32[]{:S(2)}) %collective-permute-start.30) | collective-permute-done | bytes 65568 | tf_op jit(solution)/shard_map/ppermute | solution.py:194
  203.1 7.7 %shard_map.46 = f32[64,512]{1,0:T(8,128)} custom-call(s32[16]{0:T(128)S(1)} %fusion.18.at_ref, bf16[16,64,128]{2,1,0:T(8,128)(2,1)S(1)} %pad_maximum_fusion.6.z_ref, bf16[2048,512]{1,0:T(8,128)(2,1)S(1)} %bitcast.26), custom_call_target="tpu_custom_call" | custom-call | flops 671088640 | bytes 2359296 | tf_op jit(solution)/shard_map/pallas_call | solution.py:176
  (87 shorter events, 32.1 us)
Async XLA Ops:
  3.8 71.7 %all-to-all-start = ((bf16[8,256,512]{2,1,0:T(8,128)(2,1)}), bf16[8,256,512]{2,1,0:T(8,128)(2,1)S(1)}, u32[]{:S(2)}, u32[]{:S(2)}) async-start(bf16[8,256,512]{2,1,0:T(8,128)(2,1)} %bitcast.27), calls=%async_computation | async-start | bytes 4194304 | tf_op jit(solution)/shard_map/all_to_all | solution.py:245
  14.6 4.6 %collective-permute-start = (f32[64,256]{1,0:T(8,128)S(1)}, f32[64,256]{1,0:T(8,128)S(1)}, u32[]{:S(2)}, u32[]{:S(2)}) collective-permute-start(f32[64,256]{1,0:T(8,128)S(1)} %fusion), channel_id=1, source_target_pairs={{0,1},{1,0},{2,3},{3,2},{4,5},{5,4},{6,7},{7,6},{8,9},{9,8},{10,11... | collective-permute-start | bytes 196616 | tf_op jit(solution)/shard_map/ppermute | solution.py:194
  19.2 42.8 %collective-permute-start.1 = (f32[2,64,128]{2,1,0:T(8,128)S(1)}, f32[2,64,128]{2,1,0:T(8,128)S(1)}, u32[]{:S(2)}, u32[]{:S(2)}) collective-permute-start(f32[2,64,128]{2,1,0:T(8,128)S(1)} %bitcast_bitcast_fusion.1), channel_id=1, source_target_pairs={{0,8},{4,12},{8,0},{12,4},{1,9},{5,13},{9,1},{13,5},{2,10},{6,14},... | collective-permute-start | bytes 196616 | tf_op jit(solution)/shard_map/ppermute | solution.py:194
  62.0 5.1 %collective-permute-start.2 = (f32[4,64,128]{2,1,0:T(8,128)S(1)}, f32[4,64,128]{2,1,0:T(8,128)S(1)}, u32[]{:S(2)}, u32[]{:S(2)}) collective-permute-start(f32[4,64,128]{2,1,0:T(8,128)S(1)} %pad_maximum_fusion.7), channel_id=1, source_target_pairs={{0,4},{4,0},{8,12},{12,8},{1,5},{5,1},{9,13},{13,9},{2,6},{6,2},{1... | collective-permute-start | bytes 393224 | tf_op jit(solution)/shard_map/ppermute | solution.py:194
  67.1 1.6 collective-permute-start.3
  77.2 1.6 collective-permute-start.4
  78.9 5.6 %collective-permute-start.5 = (f32[4,64,128]{2,1,0:T(8,128)S(1)}, f32[4,64,128]{2,1,0:T(8,128)S(1)}, u32[]{:S(2)}, u32[]{:S(2)}) collective-permute-start(f32[4,64,128]{2,1,0:T(8,128)S(1)} %slice.71), channel_id=1, source_target_pairs={{0,1},{1,0},{2,3},{3,2},{4,5},{5,4},{6,7},{7,6},{8,9},{9,8},{10,11... | collective-permute-start | bytes 393224 | tf_op jit(solution)/shard_map/ppermute | solution.py:194
  84.6 4.3 %collective-permute-start.6 = (f32[2,64,128]{2,1,0:T(8,128)S(1)}, f32[2,64,128]{2,1,0:T(8,128)S(1)}, u32[]{:S(2)}, u32[]{:S(2)}) collective-permute-start(f32[2,64,128]{2,1,0:T(8,128)S(1)} %slice.73), channel_id=1, source_target_pairs={{0,4},{4,0},{8,12},{12,8},{1,5},{5,1},{9,13},{13,9},{2,6},{6,2},{1... | collective-permute-start | bytes 196616 | tf_op jit(solution)/shard_map/ppermute | solution.py:194
  88.9 5.7 %collective-permute-start.7 = (f32[2,64,128]{2,1,0:T(8,128)S(1)}, f32[2,64,128]{2,1,0:T(8,128)S(1)}, u32[]{:S(2)}, u32[]{:S(2)}) collective-permute-start(f32[2,64,128]{2,1,0:T(8,128)S(1)} %slice_add_fusion.7), channel_id=1, source_target_pairs={{0,8},{4,12},{8,0},{12,4},{1,9},{5,13},{9,1},{13,5},{2,10},{6,14},... | collective-permute-start | bytes 196616 | tf_op jit(solution)/shard_map/ppermute | solution.py:194
  94.6 4.3 %collective-permute-start.8 = (f32[2,64,128]{2,1,0:T(8,128)S(1)}, f32[2,64,128]{2,1,0:T(8,128)S(1)}, u32[]{:S(2)}, u32[]{:S(2)}) collective-permute-start(f32[2,64,128]{2,1,0:T(8,128)S(1)} %add.230), channel_id=1, source_target_pairs={{0,4},{4,0},{8,12},{12,8},{1,5},{5,1},{9,13},{13,9},{2,6},{6,2},{1... | collective-permute-start | bytes 196616 | tf_op jit(solution)/shard_map/ppermute | solution.py:194
  98.9 5.0 %collective-permute-start.9 = (f32[4,64,128]{2,1,0:T(8,128)S(1)}, f32[4,64,128]{2,1,0:T(8,128)S(1)}, u32[]{:S(2)}, u32[]{:S(2)}) collective-permute-start(f32[4,64,128]{2,1,0:T(8,128)S(1)} %pad_maximum_fusion.8), channel_id=1, source_target_pairs={{0,1},{1,0},{2,3},{3,2},{4,5},{5,4},{6,7},{7,6},{8,9},{9,8},{10,11... | collective-permute-start | bytes 393224 | tf_op jit(solution)/shard_map/ppermute | solution.py:194
  104.0 1.6 collective-permute-start.10
  113.5 1.4 collective-permute-start.11
  114.9 4.3 %collective-permute-start.12 = (bf16[4,64,128]{2,1,0:T(8,128)(2,1)S(1)}, bf16[4,64,128]{2,1,0:T(8,128)(2,1)S(1)}, u32[]{:S(2)}, u32[]{:S(2)}) collective-permute-start(bf16[4,64,128]{2,1,0:T(8,128)(2,1)S(1)} %slice.108), channel_id=1, source_target_pairs={{0,1},{1,0},{2,3},{3,2},{4,5},{5,4},{6,7},{7,6},{8,9},{9,8},{10,11... | collective-permute-start | bytes 196616 | tf_op jit(solution)/shard_map/ppermute | solution.py:194
  119.3 4.0 %collective-permute-start.13 = (bf16[2,64,128]{2,1,0:T(8,128)(2,1)S(1)}, bf16[2,64,128]{2,1,0:T(8,128)(2,1)S(1)}, u32[]{:S(2)}, u32[]{:S(2)}) collective-permute-start(bf16[2,64,128]{2,1,0:T(8,128)(2,1)S(1)} %slice.111), channel_id=1, source_target_pairs={{0,4},{4,0},{8,12},{12,8},{1,5},{5,1},{9,13},{13,9},{2,6},{6,2},{1... | collective-permute-start | bytes 98312 | tf_op jit(solution)/shard_map/ppermute | solution.py:194
  123.3 5.2 %collective-permute-start.14 = (bf16[2,64,128]{2,1,0:T(8,128)(2,1)S(1)}, bf16[2,64,128]{2,1,0:T(8,128)(2,1)S(1)}, u32[]{:S(2)}, u32[]{:S(2)}) collective-permute-start(bf16[2,64,128]{2,1,0:T(8,128)(2,1)S(1)} %fusion.16), channel_id=1, source_target_pairs={{0,8},{4,12},{8,0},{12,4},{1,9},{5,13},{9,1},{13,5},{2,10},{6,14},... | collective-permute-start | bytes 98312 | tf_op jit(solution)/shard_map/ppermute | solution.py:194
  128.5 4.0 %collective-permute-start.15 = (bf16[2,64,128]{2,1,0:T(8,128)(2,1)S(1)}, bf16[2,64,128]{2,1,0:T(8,128)(2,1)S(1)}, u32[]{:S(2)}, u32[]{:S(2)}) collective-permute-start(bf16[2,64,128]{2,1,0:T(8,128)(2,1)S(1)} %add_convert_fusion.2), channel_id=1, source_target_pairs={{0,4},{4,0},{8,12},{12,8},{1,5},{5,1},{9,13},{13,9},{2,6},{6,2},{1... | collective-permute-start | bytes 98312 | tf_op jit(solution)/shard_map/ppermute | solution.py:194
  132.5 4.3 %collective-permute-start.16 = (bf16[4,64,128]{2,1,0:T(8,128)(2,1)S(1)}, bf16[4,64,128]{2,1,0:T(8,128)(2,1)S(1)}, u32[]{:S(2)}, u32[]{:S(2)}) collective-permute-start(bf16[4,64,128]{2,1,0:T(8,128)(2,1)S(1)} %pad_maximum_fusion.12), channel_id=1, source_target_pairs={{0,1},{1,0},{2,3},{3,2},{4,5},{5,4},{6,7},{7,6},{8,9},{9,8},{10,11... | collective-permute-start | bytes 196616 | tf_op jit(solution)/shard_map/ppermute | solution.py:194
  136.8 1.4 collective-permute-start.17
  146.1 1.4 collective-permute-start.18
  147.6 4.3 %collective-permute-start.19 = (bf16[4,64,128]{2,1,0:T(8,128)(2,1)S(1)}, bf16[4,64,128]{2,1,0:T(8,128)(2,1)S(1)}, u32[]{:S(2)}, u32[]{:S(2)}) collective-permute-start(bf16[4,64,128]{2,1,0:T(8,128)(2,1)S(1)} %slice.107), channel_id=1, source_target_pairs={{0,1},{1,0},{2,3},{3,2},{4,5},{5,4},{6,7},{7,6},{8,9},{9,8},{10,11... | collective-permute-start | bytes 196616 | tf_op jit(solution)/shard_map/ppermute | solution.py:194
  151.9 4.0 %collective-permute-start.20 = (bf16[2,64,128]{2,1,0:T(8,128)(2,1)S(1)}, bf16[2,64,128]{2,1,0:T(8,128)(2,1)S(1)}, u32[]{:S(2)}, u32[]{:S(2)}) collective-permute-start(bf16[2,64,128]{2,1,0:T(8,128)(2,1)S(1)} %slice.110), channel_id=1, source_target_pairs={{0,4},{4,0},{8,12},{12,8},{1,5},{5,1},{9,13},{13,9},{2,6},{6,2},{1... | collective-permute-start | bytes 98312 | tf_op jit(solution)/shard_map/ppermute | solution.py:194
  155.9 5.0 %collective-permute-start.21 = (bf16[2,64,128]{2,1,0:T(8,128)(2,1)S(1)}, bf16[2,64,128]{2,1,0:T(8,128)(2,1)S(1)}, u32[]{:S(2)}, u32[]{:S(2)}) collective-permute-start(bf16[2,64,128]{2,1,0:T(8,128)(2,1)S(1)} %fusion.15), channel_id=1, source_target_pairs={{0,8},{4,12},{8,0},{12,4},{1,9},{5,13},{9,1},{13,5},{2,10},{6,14},... | collective-permute-start | bytes 98312 | tf_op jit(solution)/shard_map/ppermute | solution.py:194
  160.9 4.0 %collective-permute-start.22 = (bf16[2,64,128]{2,1,0:T(8,128)(2,1)S(1)}, bf16[2,64,128]{2,1,0:T(8,128)(2,1)S(1)}, u32[]{:S(2)}, u32[]{:S(2)}) collective-permute-start(bf16[2,64,128]{2,1,0:T(8,128)(2,1)S(1)} %add_convert_fusion.1), channel_id=1, source_target_pairs={{0,4},{4,0},{8,12},{12,8},{1,5},{5,1},{9,13},{13,9},{2,6},{6,2},{1... | collective-permute-start | bytes 98312 | tf_op jit(solution)/shard_map/ppermute | solution.py:194
  164.9 4.3 %collective-permute-start.23 = (bf16[4,64,128]{2,1,0:T(8,128)(2,1)S(1)}, bf16[4,64,128]{2,1,0:T(8,128)(2,1)S(1)}, u32[]{:S(2)}, u32[]{:S(2)}) collective-permute-start(bf16[4,64,128]{2,1,0:T(8,128)(2,1)S(1)} %pad_maximum_fusion.13), channel_id=1, source_target_pairs={{0,1},{1,0},{2,3},{3,2},{4,5},{5,4},{6,7},{7,6},{8,9},{9,8},{10,11... | collective-permute-start | bytes 196616 | tf_op jit(solution)/shard_map/ppermute | solution.py:194
  169.3 1.4 collective-permute-start.24
  178.5 1.4 collective-permute-start.25
  180.0 4.3 %collective-permute-start.26 = (bf16[4,64,128]{2,1,0:T(8,128)(2,1)S(1)}, bf16[4,64,128]{2,1,0:T(8,128)(2,1)S(1)}, u32[]{:S(2)}, u32[]{:S(2)}) collective-permute-start(bf16[4,64,128]{2,1,0:T(8,128)(2,1)S(1)} %slice.106), channel_id=1, source_target_pairs={{0,1},{1,0},{2,3},{3,2},{4,5},{5,4},{6,7},{7,6},{8,9},{9,8},{10,11... | collective-permute-start | bytes 196616 | tf_op jit(solution)/shard_map/ppermute | solution.py:194
  184.4 4.0 %collective-permute-start.27 = (bf16[2,64,128]{2,1,0:T(8,128)(2,1)S(1)}, bf16[2,64,128]{2,1,0:T(8,128)(2,1)S(1)}, u32[]{:S(2)}, u32[]{:S(2)}) collective-permute-start(bf16[2,64,128]{2,1,0:T(8,128)(2,1)S(1)} %slice.109), channel_id=1, source_target_pairs={{0,4},{4,0},{8,12},{12,8},{1,5},{5,1},{9,13},{13,9},{2,6},{6,2},{1... | collective-permute-start | bytes 98312 | tf_op jit(solution)/shard_map/ppermute | solution.py:194
  188.4 5.0 %collective-permute-start.28 = (bf16[2,64,128]{2,1,0:T(8,128)(2,1)S(1)}, bf16[2,64,128]{2,1,0:T(8,128)(2,1)S(1)}, u32[]{:S(2)}, u32[]{:S(2)}) collective-permute-start(bf16[2,64,128]{2,1,0:T(8,128)(2,1)S(1)} %fusion.14), channel_id=1, source_target_pairs={{0,8},{4,12},{8,0},{12,4},{1,9},{5,13},{9,1},{13,5},{2,10},{6,14},... | collective-permute-start | bytes 98312 | tf_op jit(solution)/shard_map/ppermute | solution.py:194
  193.4 4.0 %collective-permute-start.29 = (bf16[2,64,128]{2,1,0:T(8,128)(2,1)S(1)}, bf16[2,64,128]{2,1,0:T(8,128)(2,1)S(1)}, u32[]{:S(2)}, u32[]{:S(2)}) collective-permute-start(bf16[2,64,128]{2,1,0:T(8,128)(2,1)S(1)} %add_convert_fusion), channel_id=1, source_target_pairs={{0,4},{4,0},{8,12},{12,8},{1,5},{5,1},{9,13},{13,9},{2,6},{6,2},{1... | collective-permute-start | bytes 98312 | tf_op jit(solution)/shard_map/ppermute | solution.py:194
  197.4 4.3 %collective-permute-start.30 = (bf16[4,64,128]{2,1,0:T(8,128)(2,1)S(1)}, bf16[4,64,128]{2,1,0:T(8,128)(2,1)S(1)}, u32[]{:S(2)}, u32[]{:S(2)}) collective-permute-start(bf16[4,64,128]{2,1,0:T(8,128)(2,1)S(1)} %pad_maximum_fusion.14), channel_id=1, source_target_pairs={{0,1},{1,0},{2,3},{3,2},{4,5},{5,4},{6,7},{7,6},{8,9},{9,8},{10,11... | collective-permute-start | bytes 196616 | tf_op jit(solution)/shard_map/ppermute | solution.py:194
  (1 other events, 1.4 us)

commit v4 on v3

v4 whole, which is shorter than its diff:
```python
import functools
import math

import jax
import jax.numpy as jnp
from jax import lax
from jax.experimental import pallas as pl
from jax.experimental.pallas import tpu as pltpu
from jax.sharding import PartitionSpec as P

RANK = 64
POWER = 4
LANES = 128
SUB = 8


shift_ratio = 0.005


def scramble(value):
    value = value ^ jnp.right_shift(value, 16) & 65535
    value = value * 73244475
    value = value ^ jnp.right_shift(value, 16) & 65535
    value = value * 73244475
    value = value ^ jnp.right_shift(value, 16) & 65535
    return value


def sketch_table(base_value, feature_index, rank):
    counter = feature_index[:, None] * rank + jnp.arange(rank, dtype=jnp.int32)[None, :]
    offset = scramble(base_value)
    total = jnp.zeros(counter.shape, jnp.float32)
    for j in range(4):
        hashed = scramble(counter * 4 + j + offset)
        total = total + (hashed & 16777215).astype(jnp.float32) * (1.0 / 16777216.0)
    return ((total - 2.0) * 1.7320508).astype(jnp.bfloat16)


def terms_of(value):
    if value.dtype == jnp.bfloat16:
        return [value]
    high = value.astype(jnp.bfloat16)
    rest = value - high.astype(jnp.float32)
    middle = rest.astype(jnp.bfloat16)
    low = (rest - middle.astype(jnp.float32)).astype(jnp.bfloat16)
    return [high, middle, low]


def dot_nn(left, right):
    return lax.dot_general(
        left, right, (((1,), (0,)), ((), ())), preferred_element_type=jnp.float32
    )


def dot_nt(left, right):
    return lax.dot_general(
        left, right, (((1,), (1,)), ((), ())), preferred_element_type=jnp.float32
    )


def small_times_wide(small, wide):
    left, right = terms_of(small), terms_of(wide)
    pairs = [(i, d - i) for d in (2, 1, 0) for i in range(d + 1)]
    pairs = [(i, j) for i, j in pairs if i < len(left) and j < len(right)]
    return dot_nn(
        jnp.concatenate([left[i] for i, unused in pairs], axis=1),
        jnp.concatenate([right[j] for unused, j in pairs], axis=0),
    )


def gram_of(wide):
    terms = terms_of(wide)
    if len(terms) == 1:
        return dot_nt(terms[0], terms[0])
    rank = wide.shape[0]
    stacked = jnp.concatenate(terms, axis=0)
    both = dot_nt(stacked, stacked)
    cross = both[rank : 2 * rank, :rank] + both[2 * rank :, :rank]
    return both[:rank, :rank] + ((cross + cross.T) + both[rank : 2 * rank, rank : 2 * rank])


def eliminate(matrix):
    size = matrix.shape[0]
    blocks = size // SUB
    row_index = lax.broadcasted_iota(jnp.int32, (SUB, 2 * size), 0)
    square_row = lax.broadcasted_iota(jnp.int32, (SUB, size), 0)
    square_col = lax.broadcasted_iota(jnp.int32, (SUB, size), 1)
    work = []
    for i in range(blocks):
        unit = jnp.where(square_col == square_row + SUB * i, 1.0, 0.0).astype(jnp.float32)
        work.append(jnp.concatenate([matrix[SUB * i : SUB * (i + 1), :], unit], axis=1))
    rows = []
    for b in range(blocks):
        columns = [
            {
                i: jnp.broadcast_to(work[i][:, SUB * b + j : SUB * b + j + 1], (SUB, 2 * size))
                for i in range(b, blocks)
            }
            for j in range(SUB)
        ]
        pivots = jnp.zeros((SUB, 2 * size), jnp.float32)
        for k in range(SUB):
            pivot = jnp.broadcast_to(columns[k][b][k : k + 1, :], (SUB, 2 * size))
            reciprocal = 1.0 / pivot
            pivots = jnp.where(row_index == k, pivot, pivots)
            work_row = jnp.broadcast_to(work[b][k : k + 1, :], (SUB, 2 * size))
            later = [
                jnp.broadcast_to(columns[j][b][k : k + 1, :], (SUB, 2 * size))
                for j in range(k + 1, SUB)
            ]
            for i in range(b, blocks):
                factor = columns[k][i] * reciprocal
                if i == b:
                    factor = jnp.where(row_index > k, factor, 0.0)
                for j in range(k + 1, SUB):
                    columns[j][i] = columns[j][i] - factor * later[j - k - 1]
                work[i] = work[i] - factor * work_row
        rows.append(work[b] * lax.rsqrt(pivots))
    both = jnp.concatenate(rows, axis=0)
    keep = lax.broadcasted_iota(jnp.int32, (size, size), 1) >= lax.broadcasted_iota(
        jnp.int32, (size, size), 0
    )
    return jnp.where(keep, both[:, :size], 0.0), both[:, size:]


def shifted(whole_gram):
    size = whole_gram.shape[0]
    diagonal = lax.broadcasted_iota(jnp.int32, (size, size), 0) == lax.broadcasted_iota(
        jnp.int32, (size, size), 1
    )
    on_diagonal = jnp.where(diagonal, whole_gram, 0.0)
    trace = jnp.sum(jnp.sum(on_diagonal, axis=1, keepdims=True), axis=0, keepdims=True)
    return jnp.where(diagonal, whole_gram + shift_ratio * trace, whole_gram)


def wide_of(at_ref, z_refs):
    half = z_refs[0].shape[0]
    n_col = at_ref.shape[0] // half
    chunks = [z_refs[i // n_col % 2][at_ref[i]] for i in range(at_ref.shape[0])]
    return jnp.concatenate(chunks, axis=1)


def narrow_basis(at_ref, z_refs):
    wide = wide_of(at_ref, z_refs)
    upper, inverse_one = eliminate(shifted(gram_of(wide)))
    first = small_times_wide(inverse_one, wide)
    unused, inverse_two = eliminate(gram_of(first))
    return small_times_wide(inverse_two, first).astype(jnp.bfloat16), upper


def times_slab(basis, a_refs):
    rows = a_refs[0].shape[0]
    pieces = [
        dot_nn(basis[:, rows * s : rows * (s + 1)], a_ref[...]) for s, a_ref in enumerate(a_refs)
    ]
    return functools.reduce(jnp.add, pieces)


def power_body(basis, a_refs, at_ref, part_refs):
    weights = times_slab(basis, a_refs).astype(jnp.bfloat16)
    width = part_refs[0].shape[2]
    n_col = at_ref.shape[0] // len(a_refs)
    for s, a_ref in enumerate(a_refs):
        forth = dot_nt(weights, a_ref[...])
        target = part_refs[s % 2]
        for c in range(n_col):
            block = forth[:, width * c : width * (c + 1)]
            target[at_ref[s * n_col + c]] = block.astype(target.dtype)


def orth_kernel(at_ref, z_ref, other_ref, basis_ref, upper_ref):
    basis_ref[...], upper_ref[...] = narrow_basis(at_ref, (z_ref, other_ref))


def power_kernel(at_ref, basis_ref, *refs):
    power_body(basis_ref[...], refs[:-2], at_ref, refs[-2:])


def orth_power_kernel(at_ref, z_ref, other_ref, *refs):
    basis, unused = narrow_basis(at_ref, (z_ref, other_ref))
    power_body(basis, refs[:-2], at_ref, refs[-2:])


def last_kernel(at_ref, z_ref, other_ref, *refs):
    basis, unused = narrow_basis(at_ref, (z_ref, other_ref))
    refs[-1][...] = times_slab(basis, refs[:-1])


def call(kernel, out_shapes, flops, at, *operands):
    moved = sum(x.size * x.dtype.itemsize for x in operands)
    return pl.pallas_call(
        kernel,
        out_shape=out_shapes,
        in_specs=[pl.BlockSpec(memory_space=pltpu.SMEM)]
        + [pl.BlockSpec(memory_space=pltpu.VMEM)] * len(operands),
        out_specs=jax.tree.map(lambda _: pl.BlockSpec(memory_space=pltpu.VMEM), out_shapes),
        compiler_params=pltpu.CompilerParams(vmem_limit_bytes=40 * 1024 * 1024),
        cost_estimate=pl.CostEstimate(flops=flops, bytes_accessed=moved, transcendentals=0),
    )(at, *operands)


def bits(size):
    return [1 << k for k in range(size.bit_length() - 1)]


def from_xor(value, axis, offset):
    size = math.prod(lax.axis_size(name) for name in axis)
    return lax.ppermute(value, axis, [(i, i ^ offset) for i in range(size)])


def sum_parts(keep, send, dtype):
    total = keep + from_xor(send, ("core",), 1).astype(jnp.float32)
    for bit in bits(lax.axis_size("col")):
        half = total.shape[0] // 2
        other = from_xor(total[half:].astype(dtype), ("col",), bit)
        total = total[:half] + other.astype(jnp.float32)
    for bit in bits(lax.axis_size("z")):
        mine = total.astype(dtype)
        total = mine.astype(jnp.float32) + from_xor(mine, ("z",), bit).astype(jnp.float32)
    return total.astype(dtype)


def gather_parts(own):
    for bit in bits(lax.axis_size("col"))[::-1]:
        own = jnp.concatenate([own, from_xor(own, ("col",), bit)])
    return own, from_xor(own, ("core",), 1)


def chunk_places(digits):
    n_z, n_col = lax.axis_size("z"), lax.axis_size("col")
    index = jnp.arange(n_z * 2 * n_col, dtype=jnp.int32)
    z_at, col_at = lax.axis_index("z"), lax.axis_index("col")
    column = index % n_col
    relative = {"z": index // (2 * n_col), "col": column ^ col_at}
    absolute = {"z": relative["z"] ^ z_at, "col": column}
    place = jnp.zeros_like(index)
    for axis, bit, is_relative in digits:
        place = place * 2 + ((relative if is_relative else absolute)[axis] // bit) % 2
    return place.astype(jnp.int32)


def per_device_transposed(sketch_base, states):
    n_z, n_core, n_col = lax.axis_size("z"), lax.axis_size("core"), lax.axis_size("col")
    n_row = n_z * n_core
    rows_local, width_local = states.shape
    rows_total, width_total = rows_local * n_row, width_local * n_col
    chunk = rows_local // n_col
    cols = width_local // n_row
    half = n_z * n_col
    row = lax.axis_index("z") * n_core + lax.axis_index("core")
    pieces = [None] * n_row

    def block(slab, offset):
        return lax.dynamic_slice_in_dim(slab, (row ^ offset) * cols, cols, 1)

    def move(slab, offsets):
        for offset in offsets:
            pieces[offset] = block(slab, offset)
            if offset:
                pieces[offset] = from_xor(pieces[offset], ("z", "core"), offset)

    far = list(range(n_row // 2, n_row))
    near = list(range(n_row // 2 - 1, -1, -1))
    move(states, far[:1])

    col = lax.axis_index("col")
    feature_index = col * width_local + jnp.arange(width_local, dtype=jnp.int32)
    omega = sketch_table(sketch_base[0], feature_index, RANK)
    z = lax.dot_general(
        omega, states, (((0,), (1,)), ((), ())), preferred_element_type=jnp.float32
    )
    for bit in bits(n_col):
        z = z + from_xor(z, ("col",), bit)
    z = z.reshape(RANK, n_col, chunk).transpose(1, 0, 2)
    z_bits = bits(n_z)[::-1]
    for k, bit in enumerate(z_bits):
        z = jnp.concatenate([z, from_xor(z, ("z",), bit)])
        slab, z = lax.optimization_barrier((states, z))
        if k == 0:
            move(slab, far[1:2])
    move(slab, far[2:] + near)
    z = z, from_xor(z, ("core",), 1)
    absolute_col = [("col", bit, False) for bit in bits(n_col)[::-1]]
    at_first = chunk_places([("z", bit, True) for bit in z_bits[::-1]] + absolute_col)
    relative_col = [("col", bit, True) for bit in bits(n_col)]
    at = chunk_places(relative_col + [("z", bit, False) for bit in z_bits])

    f32 = jnp.float32
    square = jax.ShapeDtypeStruct((RANK, RANK), f32)
    wide = jax.ShapeDtypeStruct((RANK, rows_total), jnp.bfloat16)
    orth_flops = 8 * 64 * 64 * rows_total * 6
    power_flops = 4 * 64 * rows_total * cols

    def sent_as(dtype):
        shape = (half, RANK, chunk)
        return jax.ShapeDtypeStruct(shape, f32), jax.ShapeDtypeStruct(shape, dtype)

    basis, upper = call(orth_kernel, (wide, square), orth_flops, at_first, *z)
    factor = upper.T * (1.0 / math.sqrt(rows_total * width_total))
    dtype = f32
    parts = call(power_kernel, sent_as(dtype), power_flops, at, basis, *pieces)
    for step in range(POWER - 1):
        z = gather_parts(sum_parts(*parts, dtype))
        dtype = jnp.bfloat16
        flops = orth_flops + power_flops
        parts = call(orth_power_kernel, sent_as(dtype), flops, at, *z, *pieces)
    z = gather_parts(sum_parts(*parts, dtype))
    loadings = jax.ShapeDtypeStruct((RANK, cols), f32)
    return call(last_kernel, loadings, orth_flops + power_flops, at, *z, *pieces).T, factor


def local_gram(basis):
    return jnp.dot(basis.T, basis, precision=lax.Precision.HIGHEST)


def orthonormal_block(sketch):
    whole_gram = lax.psum(local_gram(sketch), "row")
    identity = jnp.eye(RANK, dtype=jnp.float32)
    lower = jnp.linalg.cholesky(whole_gram + shift_ratio * jnp.trace(whole_gram) * identity)
    first = jax.scipy.linalg.solve_triangular(lower, sketch.T, lower=True).T
    lower_two = jnp.linalg.cholesky(lax.psum(local_gram(first), "row"))
    return jax.scipy.linalg.solve_triangular(lower_two, first.T, lower=True).T, lower


def per_device_slabs(sketch_base, states):
    width_local = states.shape[1]
    rows_total = states.shape[0] * lax.axis_size("row")
    width_total = width_local * lax.axis_size("col")
    feature_index = lax.axis_index("col") * width_local + jnp.arange(width_local, dtype=jnp.int32)
    omega = sketch_table(sketch_base[0], feature_index, RANK)

    def row_basis(right):
        partial_sketch = jnp.dot(states, right, preferred_element_type=jnp.float32)
        basis_new, lower = orthonormal_block(lax.psum(partial_sketch, "col"))
        return basis_new.astype(jnp.bfloat16), lower

    def back(basis):
        return lax.dot_general(
            states, basis, (((0,), (0,)), ((), ())), preferred_element_type=jnp.float32
        )

    basis, first_lower = row_basis(omega)
    factor = first_lower * (1.0 / math.sqrt(rows_total * width_total))
    for step in range(POWER):
        basis, unused = row_basis(lax.psum(back(basis), "row").astype(jnp.bfloat16))
    return lax.psum_scatter(back(basis), "row", scatter_dimension=0, tiled=True), factor


def solution(mesh):
    n_grp, n_row, n_col = (mesh.shape[name] for name in ("grp", "row", "col"))
    fits = n_row % 2 == 0 and n_row & (n_row - 1) == 0

    def run(sketch_base, states):
        rows_local = states.shape[0] // (n_grp * n_row)
        width_local = states.shape[1] // n_col
        tiled = rows_local % (n_col * LANES) == 0 and width_local % (n_row * LANES) == 0
        if fits and tiled:
            split = mesh.devices.reshape(n_grp, n_row // 2, 2, n_col)
            inner = jax.sharding.Mesh(split, ("grp", "z", "core", "col"))
            row, step = ("z", "core"), per_device_transposed
        else:
            inner, row, step = mesh, ("row",), per_device_slabs
        return jax.shard_map(
            step,
            mesh=inner,
            in_specs=(P("grp"), P(("grp",) + row, "col")),
            out_specs=(P(("col",) + row, "grp"), P("grp", None)),
            check_vma=False,
        )(sketch_base, states)

    return run
```

time: 211 us -> 185 us (0.88)
  waiting for transfers between devices: 134 us -> 102 us
  starting transfers between devices: 26.7 us -> 37.2 us
  Pallas kernels: 39.6 us -> 35.6 us
    ppermute x32 -> x35, waiting for transfers between devices: 134 us -> 102 us  [from_xor(): return lax.ppermute(value, axis, [(i, i ^ offset) for i in range(size)])]
    ppermute x32 -> x35, starting transfers between devices: 20.4 us -> 37.2 us  [from_xor(): return lax.ppermute(value, axis, [(i, i ^ offset) for i in range(size)])]
    all_to_all x1 -> x0, starting transfers between devices: 6.33 us -> none  [per_device_transposed(): lax.all_to_all(by_target, ('z', 'core'), 0, 0, tiled=True)]
    pallas_call x6, Pallas kernels: 39.6 us -> 35.6 us  [call(): pl.pallas_call(kernel, out_shape=out_shapes, in_specs=[pl.BlockSpec(memor...]
    dynamic_slice x0 -> x3, local copies, waits for them, and re-layouts: none -> 3.39 us  [block(): return lax.dynamic_slice_in_dim(slab, (row ^ offset) * cols, cols, 1)]
    reshape x1 -> x0, local copies, waits for them, and re-layouts: 3.16 us -> none  [per_device_transposed(): by_target = states.reshape(rows_local, n_row, cols).transpose(1, 0, 2)]
  transfers between devices with their start and end apart: 33 -> 35, of which waited for: 32 -> 29; matrix products, arithmetic and copies ran while one was open for 2% -> 2% of each run, Pallas kernels for 3% -> 3%
where the time goes in v4:
time: 185 us
  waiting for transfers between devices  102 us (55%)
  starting transfers between devices  37.2 us (20%)
  Pallas kernels  35.6 us (19%)
  local copies, waits for them, and re-layouts  4.14 us (2%)
  matrix products  3.83 us (2%)
    ppermute x35, waiting for transfers between devices, from_xor(): return lax.ppermute(value, axis, [(i, i ^ offset) for i in range(size)])  102 us
    ppermute x35, starting transfers between devices, from_xor(): return lax.ppermute(value, axis, [(i, i ^ offset) for i in range(size)])  37.2 us
    pallas_call x6, Pallas kernels, call(): pl.pallas_call(kernel, out_shape=out_shapes, in_specs=[pl.BlockSpec(memor...  35.6 us
    dot_general x1, matrix products, per_device_transposed(): lax.dot_general(omega, states, (((0,), (1,)), ((), ())), preferred_elemen...  3.83 us
  transfers between devices with their start and end apart: 35, of which 29 were waited for; matrix products, arithmetic and copies ran while one was open for 2% of the time, Pallas kernels for 3%

profile of v4, /device:TPU:0, one launch (start us, length us, event | category | flops | bytes accessed | tf_op | source)
XLA Modules:
  0.0 184.6 jit_solution(2445964522665314672)
XLA Ops:
  1.3 3.8 %fusion = f32[64,256]{1,0:T(8,128)S(1)} fusion(bf16[256,4096]{1,0:T(8,128)(2,1)} %param.3, s32[]{:T(128)S(6)} %xor.84, s32[4096]{0:T(1024)S(1)} %add_multiply_fusion), kind=kOutput, calls=%fused_computation.1 | convolution fusion | flops 152043520 | bytes 2179076 | tf_op jit(solution)/shard_map/dot_general | solution.py:269
  5.1 3.0 %collective-permute-start = (f32[64,256]{1,0:T(8,128)S(1)}, f32[64,256]{1,0:T(8,128)S(1)}, u32[]{:S(2)}, u32[]{:S(2)}) collective-permute-start(f32[64,256]{1,0:T(8,128)S(1)} %fusion), channel_id=1, source_target_pairs={{0,1},{1,0},{2,3},{3,2},{4,5},{5,4},{6,7},{7,6},{8,9},{9,8},{10,11... | collective-permute-start | bytes 196616 | tf_op jit(solution)/shard_map/ppermute | solution.py:208
  8.1 2.2 %collective-permute-done = f32[64,256]{1,0:T(8,128)S(1)} collective-permute-done((f32[64,256]{1,0:T(8,128)S(1)}, f32[64,256]{1,0:T(8,128)S(1)}, u32[]{:S(2)}, u32[]{:S(2)}) %collective-permute-start) | collective-permute-done | bytes 65568 | tf_op jit(solution)/shard_map/ppermute | solution.py:208
  10.4 3.2 %collective-permute-start.1 = (f32[2,64,128]{2,1,0:T(8,128)S(1)}, f32[2,64,128]{2,1,0:T(8,128)S(1)}, u32[]{:S(2)}, u32[]{:S(2)}) collective-permute-start(f32[2,64,128]{2,1,0:T(8,128)S(1)} %bitcast_bitcast_fusion), channel_id=1, source_target_pairs={{0,8},{4,12},{8,0},{12,4},{1,9},{5,13},{9,1},{13,5},{2,10},{6,14},... | collective-permute-start | bytes 196616 | tf_op jit(solution)/shard_map/ppermute | solution.py:208
  13.6 2.2 %collective-permute-done.1 = f32[2,64,128]{2,1,0:T(8,128)S(1)} collective-permute-done((f32[2,64,128]{2,1,0:T(8,128)S(1)}, f32[2,64,128]{2,1,0:T(8,128)S(1)}, u32[]{:S(2)}, u32[]{:S(2)}) %collective-permute-start.1) | collective-permute-done | bytes 65568 | tf_op jit(solution)/shard_map/ppermute | solution.py:208
  18.8 3.2 %collective-permute-start.7 = (bf16[256,512]{1,0:T(8,128)(2,1)S(1)}, bf16[256,512]{1,0:T(8,128)(2,1)S(1)}, u32[]{:S(2)}, u32[]{:S(2)}) collective-permute-start(bf16[256,512]{1,0:T(8,128)(2,1)S(1)} %constant_dynamic-slice_fusion.3), channel_id=1, source_target_pairs={{0,8},{2,10},{4,12},{6,14},{8,0},{10,2},{12,4},{14,6},{1,9},{3,11}... | collective-permute-start | bytes 786440 | tf_op jit(solution)/shard_map/ppermute | solution.py:208
  24.7 3.1 %collective-permute-start.10 = (bf16[256,512]{1,0:T(8,128)(2,1)S(1)}, bf16[256,512]{1,0:T(8,128)(2,1)S(1)}, u32[]{:S(2)}, u32[]{:S(2)}) collective-permute-start(bf16[256,512]{1,0:T(8,128)(2,1)S(1)} %get-tuple-element.36), channel_id=1, source_target_pairs={{0,14},{2,12},{4,10},{6,8},{8,6},{10,4},{12,2},{14,0},{1,15},{3,13... | collective-permute-start | bytes 786440 | tf_op jit(solution)/shard_map/ppermute | solution.py:208
  28.6 20.5 %collective-permute-done.7.refs_4_ = bf16[256,512]{1,0:T(8,128)(2,1)S(1)} collective-permute-done((bf16[256,512]{1,0:T(8,128)(2,1)S(1)}, bf16[256,512]{1,0:T(8,128)(2,1)S(1)}, u32[]{:S(2)}, u32[]{:S(2)}) %collective-permute-start.7) | collective-permute-done | bytes 262176 | tf_op jit(solution)/shard_map/ppermute | solution.py:208
  49.2 3.8 %collective-permute-done.8.refs_5_ = bf16[256,512]{1,0:T(8,128)(2,1)S(1)} collective-permute-done((bf16[256,512]{1,0:T(8,128)(2,1)S(1)}, bf16[256,512]{1,0:T(8,128)(2,1)S(1)}, u32[]{:S(2)}, u32[]{:S(2)}) %collective-permute-start.8) | collective-permute-done | bytes 262176 | tf_op jit(solution)/shard_map/ppermute | solution.py:208
  53.0 2.6 %collective-permute-start.5 = (bf16[256,512]{1,0:T(8,128)(2,1)S(1)}, bf16[256,512]{1,0:T(8,128)(2,1)S(1)}, u32[]{:S(2)}, u32[]{:S(2)}) collective-permute-start(bf16[256,512]{1,0:T(8,128)(2,1)S(1)} %get-tuple-element.39), channel_id=1, source_target_pairs={{0,4},{2,6},{4,0},{6,2},{8,12},{10,14},{12,8},{14,10},{1,5},{3,7},... | collective-permute-start | bytes 786440 | tf_op jit(solution)/shard_map/ppermute | solution.py:208
  55.6 6.3 %shard_map.41 = (bf16[64,2048]{1,0:T(8,128)(2,1)S(1)}, f32[64,64]{1,0:T(8,128)S(1)}) custom-call(s32[16]{0:T(128)S(1)} %fusion.20.at_ref, f32[8,64,128]{2,1,0:T(8,128)S(1)} %pad_maximum_fusion.z_ref, f32[8,64,128]{2,1,0:T(8,128)S(1)} %collective-permute-done.3.other_ref), custom_call_target="tpu_custom_call" | custom-call | flops 402653184 | bytes 524288 | tf_op jit(solution)/shard_map/pallas_call | solution.py:191
  61.9 3.1 %collective-permute-done.5.refs_2_ = bf16[256,512]{1,0:T(8,128)(2,1)S(1)} collective-permute-done((bf16[256,512]{1,0:T(8,128)(2,1)S(1)}, bf16[256,512]{1,0:T(8,128)(2,1)S(1)}, u32[]{:S(2)}, u32[]{:S(2)}) %collective-permute-start.5) | collective-permute-done | bytes 262176 | tf_op jit(solution)/shard_map/ppermute | solution.py:208
  69.9 4.0 %collective-permute-done.12 = f32[4,64,128]{2,1,0:T(8,128)S(1)} collective-permute-done((f32[4,64,128]{2,1,0:T(8,128)S(1)}, f32[4,64,128]{2,1,0:T(8,128)S(1)}, u32[]{:S(2)}, u32[]{:S(2)}) %collective-permute-start.12) | collective-permute-done | bytes 131104 | tf_op jit(solution)/shard_map/ppermute | solution.py:208
  74.7 4.3 %collective-permute-done.13 = f32[4,64,128]{2,1,0:T(8,128)S(1)} collective-permute-done((f32[4,64,128]{2,1,0:T(8,128)S(1)}, f32[4,64,128]{2,1,0:T(8,128)S(1)}, u32[]{:S(2)}, u32[]{:S(2)}) %collective-permute-start.13) | collective-permute-done | bytes 131104 | tf_op jit(solution)/shard_map/ppermute | solution.py:208
  80.7 5.7 %collective-permute-done.14 = f32[4,64,128]{2,1,0:T(8,128)S(1)} collective-permute-done((f32[4,64,128]{2,1,0:T(8,128)S(1)}, f32[4,64,128]{2,1,0:T(8,128)S(1)}, u32[]{:S(2)}, u32[]{:S(2)}) %collective-permute-start.14) | collective-permute-done | bytes 131104 | tf_op jit(solution)/shard_map/ppermute | solution.py:208
  87.9 3.5 %collective-permute-done.15 = f32[4,64,128]{2,1,0:T(8,128)S(1)} collective-permute-done((f32[4,64,128]{2,1,0:T(8,128)S(1)}, f32[4,64,128]{2,1,0:T(8,128)S(1)}, u32[]{:S(2)}, u32[]{:S(2)}) %collective-permute-start.15) | collective-permute-done | bytes 131104 | tf_op jit(solution)/shard_map/ppermute | solution.py:208
  93.0 7.4 %shard_map.43 = (f32[8,64,128]{2,1,0:T(8,128)S(1)}, bf16[8,64,128]{2,1,0:T(8,128)(2,1)S(1)}) custom-call(s32[16]{0:T(128)S(1)} %fusion.18.at_ref, f32[8,64,128]{2,1,0:T(8,128)S(1)} %pad_maximum_fusion.1.z_ref, f32[8,64,128]{2,1,0:T(8,128)S(1)} %collective-permute-done.16.other_ref, bf16[256,512]{1,0:T(8,128)(2,1)S(1)} %get-tuple-element.41.refs_0_, ...), custom_call_target="tpu_custom_call" | custom-call | flops 671088640 | bytes 2621440 | tf_op jit(solution)/shard_map/pallas_call | solution.py:191
  103.4 2.8 %collective-permute-done.18 = bf16[4,64,128]{2,1,0:T(8,128)(2,1)S(1)} collective-permute-done((bf16[4,64,128]{2,1,0:T(8,128)(2,1)S(1)}, bf16[4,64,128]{2,1,0:T(8,128)(2,1)S(1)}, u32[]{:S(2)}, u32[]{:S(2)}) %collective-permute-start.18) | collective-permute-done | bytes 65568 | tf_op jit(solution)/shard_map/ppermute | solution.py:208
  106.3 4.3 %collective-permute-done.19 = bf16[4,64,128]{2,1,0:T(8,128)(2,1)S(1)} collective-permute-done((bf16[4,64,128]{2,1,0:T(8,128)(2,1)S(1)}, bf16[4,64,128]{2,1,0:T(8,128)(2,1)S(1)}, u32[]{:S(2)}, u32[]{:S(2)}) %collective-permute-start.19) | collective-permute-done | bytes 65568 | tf_op jit(solution)/shard_map/ppermute | solution.py:208
  111.6 4.4 %collective-permute-done.20 = bf16[4,64,128]{2,1,0:T(8,128)(2,1)S(1)} collective-permute-done((bf16[4,64,128]{2,1,0:T(8,128)(2,1)S(1)}, bf16[4,64,128]{2,1,0:T(8,128)(2,1)S(1)}, u32[]{:S(2)}, u32[]{:S(2)}) %collective-permute-start.20) | collective-permute-done | bytes 65568 | tf_op jit(solution)/shard_map/ppermute | solution.py:208
  117.5 2.8 %collective-permute-done.21 = bf16[4,64,128]{2,1,0:T(8,128)(2,1)S(1)} collective-permute-done((bf16[4,64,128]{2,1,0:T(8,128)(2,1)S(1)}, bf16[4,64,128]{2,1,0:T(8,128)(2,1)S(1)}, u32[]{:S(2)}, u32[]{:S(2)}) %collective-permute-start.21) | collective-permute-done | bytes 65568 | tf_op jit(solution)/shard_map/ppermute | solution.py:208
  121.7 6.7 %shard_map.44 = (f32[8,64,128]{2,1,0:T(8,128)S(1)}, bf16[8,64,128]{2,1,0:T(8,128)(2,1)S(1)}) custom-call(s32[16]{0:T(128)S(1)} %fusion.18.at_ref, bf16[8,64,128]{2,1,0:T(8,128)(2,1)S(1)} %pad_maximum_fusion.3.z_ref, bf16[8,64,128]{2,1,0:T(8,128)(2,1)S(1)} %collective-permute-done.22.other_ref, bf16[256,512]{1,0:T(8,128)(2,1)S(1)} %get-tuple-element.41.refs_0_, ...), custom_call_target="tpu_custom_call" | custom-call | flops 671088640 | bytes 2359296 | tf_op jit(solution)/shard_map/pallas_call | solution.py:191
  131.5 2.8 %collective-permute-done.24 = bf16[4,64,128]{2,1,0:T(8,128)(2,1)S(1)} collective-permute-done((bf16[4,64,128]{2,1,0:T(8,128)(2,1)S(1)}, bf16[4,64,128]{2,1,0:T(8,128)(2,1)S(1)}, u32[]{:S(2)}, u32[]{:S(2)}) %collective-permute-start.24) | collective-permute-done | bytes 65568 | tf_op jit(solution)/shard_map/ppermute | solution.py:208
  134.4 4.3 %collective-permute-done.25 = bf16[4,64,128]{2,1,0:T(8,128)(2,1)S(1)} collective-permute-done((bf16[4,64,128]{2,1,0:T(8,128)(2,1)S(1)}, bf16[4,64,128]{2,1,0:T(8,128)(2,1)S(1)}, u32[]{:S(2)}, u32[]{:S(2)}) %collective-permute-start.25) | collective-permute-done | bytes 65568 | tf_op jit(solution)/shard_map/ppermute | solution.py:208
  139.6 4.4 %collective-permute-done.26 = bf16[4,64,128]{2,1,0:T(8,128)(2,1)S(1)} collective-permute-done((bf16[4,64,128]{2,1,0:T(8,128)(2,1)S(1)}, bf16[4,64,128]{2,1,0:T(8,128)(2,1)S(1)}, u32[]{:S(2)}, u32[]{:S(2)}) %collective-permute-start.26) | collective-permute-done | bytes 65568 | tf_op jit(solution)/shard_map/ppermute | solution.py:208
  145.6 2.8 %collective-permute-done.27 = bf16[4,64,128]{2,1,0:T(8,128)(2,1)S(1)} collective-permute-done((bf16[4,64,128]{2,1,0:T(8,128)(2,1)S(1)}, bf16[4,64,128]{2,1,0:T(8,128)(2,1)S(1)}, u32[]{:S(2)}, u32[]{:S(2)}) %collective-permute-start.27) | collective-permute-done | bytes 65568 | tf_op jit(solution)/shard_map/ppermute | solution.py:208
  149.8 6.7 %shard_map.45 = (f32[8,64,128]{2,1,0:T(8,128)S(1)}, bf16[8,64,128]{2,1,0:T(8,128)(2,1)S(1)}) custom-call(s32[16]{0:T(128)S(1)} %fusion.18.at_ref, bf16[8,64,128]{2,1,0:T(8,128)(2,1)S(1)} %pad_maximum_fusion.4.z_ref, bf16[8,64,128]{2,1,0:T(8,128)(2,1)S(1)} %collective-permute-done.28.other_ref, bf16[256,512]{1,0:T(8,128)(2,1)S(1)} %get-tuple-element.41.refs_0_, ...), custom_call_target="tpu_custom_call" | custom-call | flops 671088640 | bytes 2359296 | tf_op jit(solution)/shard_map/pallas_call | solution.py:191
  159.5 2.8 %collective-permute-done.30 = bf16[4,64,128]{2,1,0:T(8,128)(2,1)S(1)} collective-permute-done((bf16[4,64,128]{2,1,0:T(8,128)(2,1)S(1)}, bf16[4,64,128]{2,1,0:T(8,128)(2,1)S(1)}, u32[]{:S(2)}, u32[]{:S(2)}) %collective-permute-start.30) | collective-permute-done | bytes 65568 | tf_op jit(solution)/shard_map/ppermute | solution.py:208
  162.4 4.3 %collective-permute-done.31 = bf16[4,64,128]{2,1,0:T(8,128)(2,1)S(1)} collective-permute-done((bf16[4,64,128]{2,1,0:T(8,128)(2,1)S(1)}, bf16[4,64,128]{2,1,0:T(8,128)(2,1)S(1)}, u32[]{:S(2)}, u32[]{:S(2)}) %collective-permute-start.31) | collective-permute-done | bytes 65568 | tf_op jit(solution)/shard_map/ppermute | solution.py:208
  167.7 4.4 %collective-permute-done.32 = bf16[4,64,128]{2,1,0:T(8,128)(2,1)S(1)} collective-permute-done((bf16[4,64,128]{2,1,0:T(8,128)(2,1)S(1)}, bf16[4,64,128]{2,1,0:T(8,128)(2,1)S(1)}, u32[]{:S(2)}, u32[]{:S(2)}) %collective-permute-start.32) | collective-permute-done | bytes 65568 | tf_op jit(solution)/shard_map/ppermute | solution.py:208
  173.6 2.8 %collective-permute-done.33 = bf16[4,64,128]{2,1,0:T(8,128)(2,1)S(1)} collective-permute-done((bf16[4,64,128]{2,1,0:T(8,128)(2,1)S(1)}, bf16[4,64,128]{2,1,0:T(8,128)(2,1)S(1)}, u32[]{:S(2)}, u32[]{:S(2)}) %collective-permute-start.33) | collective-permute-done | bytes 65568 | tf_op jit(solution)/shard_map/ppermute | solution.py:208
  177.8 6.8 %shard_map.46 = f32[64,512]{1,0:T(8,128)} custom-call(s32[16]{0:T(128)S(1)} %fusion.18.at_ref, bf16[8,64,128]{2,1,0:T(8,128)(2,1)S(1)} %pad_maximum_fusion.5.z_ref, bf16[8,64,128]{2,1,0:T(8,128)(2,1)S(1)} %collective-permute-done.34.other_ref, bf16[256,512]{1,0:T(8,128)(2,1)S(1)} %get-tuple-element.41.refs_0_, ...), custom_call_target="tpu_custom_call" | custom-call | flops 671088640 | bytes 2359296 | tf_op jit(solution)/shard_map/pallas_call | solution.py:191
  (80 shorter events, 38.2 us)
Async XLA Ops:
  5.1 5.2 %collective-permute-start = (f32[64,256]{1,0:T(8,128)S(1)}, f32[64,256]{1,0:T(8,128)S(1)}, u32[]{:S(2)}, u32[]{:S(2)}) collective-permute-start(f32[64,256]{1,0:T(8,128)S(1)} %fusion), channel_id=1, source_target_pairs={{0,1},{1,0},{2,3},{3,2},{4,5},{5,4},{6,7},{7,6},{8,9},{9,8},{10,11... | collective-permute-start | bytes 196616 | tf_op jit(solution)/shard_map/ppermute | solution.py:208
  10.4 5.4 %collective-permute-start.1 = (f32[2,64,128]{2,1,0:T(8,128)S(1)}, f32[2,64,128]{2,1,0:T(8,128)S(1)}, u32[]{:S(2)}, u32[]{:S(2)}) collective-permute-start(f32[2,64,128]{2,1,0:T(8,128)S(1)} %bitcast_bitcast_fusion), channel_id=1, source_target_pairs={{0,8},{4,12},{8,0},{12,4},{1,9},{5,13},{9,1},{13,5},{2,10},{6,14},... | collective-permute-start | bytes 196616 | tf_op jit(solution)/shard_map/ppermute | solution.py:208
  15.8 7.2 %collective-permute-start.2 = (f32[4,64,128]{2,1,0:T(8,128)S(1)}, f32[4,64,128]{2,1,0:T(8,128)S(1)}, u32[]{:S(2)}, u32[]{:S(2)}) collective-permute-start(f32[4,64,128]{2,1,0:T(8,128)S(1)} %pad_maximum_fusion.2), channel_id=1, source_target_pairs={{0,4},{4,0},{8,12},{12,8},{1,5},{5,1},{9,13},{13,9},{2,6},{6,2},{1... | collective-permute-start | bytes 393224 | tf_op jit(solution)/shard_map/ppermute | solution.py:208
  18.8 30.4 %collective-permute-start.7 = (bf16[256,512]{1,0:T(8,128)(2,1)S(1)}, bf16[256,512]{1,0:T(8,128)(2,1)S(1)}, u32[]{:S(2)}, u32[]{:S(2)}) collective-permute-start(bf16[256,512]{1,0:T(8,128)(2,1)S(1)} %constant_dynamic-slice_fusion.3), channel_id=1, source_target_pairs={{0,8},{2,10},{4,12},{6,14},{8,0},{10,2},{12,4},{14,6},{1,9},{3,11}... | collective-permute-start | bytes 786440 | tf_op jit(solution)/shard_map/ppermute | solution.py:208
  23.0 30.0 %collective-permute-start.8 = (bf16[256,512]{1,0:T(8,128)(2,1)S(1)}, bf16[256,512]{1,0:T(8,128)(2,1)S(1)}, u32[]{:S(2)}, u32[]{:S(2)}) collective-permute-start(bf16[256,512]{1,0:T(8,128)(2,1)S(1)} %constant_dynamic-slice_fusion.2), channel_id=1, source_target_pairs={{0,10},{2,8},{4,14},{6,12},{8,2},{10,0},{12,6},{14,4},{1,11},{3,9}... | collective-permute-start | bytes 786440 | tf_op jit(solution)/shard_map/ppermute | solution.py:208
  23.1 32.5 %collective-permute-start.3 = (f32[8,64,128]{2,1,0:T(8,128)S(1)}, f32[8,64,128]{2,1,0:T(8,128)S(1)}, u32[]{:S(2)}, u32[]{:S(2)}) collective-permute-start(f32[8,64,128]{2,1,0:T(8,128)S(1)} %pad_maximum_fusion.z_ref), channel_id=1, source_target_pairs={{0,2},{2,0},{1,3},{3,1},{4,6},{6,4},{5,7},{7,5},{8,10},{10,8},{9,1... | collective-permute-start | bytes 786440 | tf_op jit(solution)/shard_map/ppermute | solution.py:208
  24.7 37.2 %collective-permute-start.10 = (bf16[256,512]{1,0:T(8,128)(2,1)S(1)}, bf16[256,512]{1,0:T(8,128)(2,1)S(1)}, u32[]{:S(2)}, u32[]{:S(2)}) collective-permute-start(bf16[256,512]{1,0:T(8,128)(2,1)S(1)} %get-tuple-element.36), channel_id=1, source_target_pairs={{0,14},{2,12},{4,10},{6,8},{8,6},{10,4},{12,2},{14,0},{1,15},{3,13... | collective-permute-start | bytes 786440 | tf_op jit(solution)/shard_map/ppermute | solution.py:208
  27.9 34.0 %collective-permute-start.9 = (bf16[256,512]{1,0:T(8,128)(2,1)S(1)}, bf16[256,512]{1,0:T(8,128)(2,1)S(1)}, u32[]{:S(2)}, u32[]{:S(2)}) collective-permute-start(bf16[256,512]{1,0:T(8,128)(2,1)S(1)} %get-tuple-element.37), channel_id=1, source_target_pairs={{0,12},{2,14},{4,8},{6,10},{8,4},{10,6},{12,0},{14,2},{1,13},{3,15... | collective-permute-start | bytes 786440 | tf_op jit(solution)/shard_map/ppermute | solution.py:208
  49.2 12.8 %collective-permute-start.6 = (bf16[256,512]{1,0:T(8,128)(2,1)S(1)}, bf16[256,512]{1,0:T(8,128)(2,1)S(1)}, u32[]{:S(2)}, u32[]{:S(2)}) collective-permute-start(bf16[256,512]{1,0:T(8,128)(2,1)S(1)} %get-tuple-element.38), channel_id=1, source_target_pairs={{0,6},{2,4},{4,2},{6,0},{8,14},{10,12},{12,10},{14,8},{1,7},{3,5},... | collective-permute-start | bytes 786440 | tf_op jit(solution)/shard_map/ppermute | solution.py:208
  53.0 12.0 %collective-permute-start.5 = (bf16[256,512]{1,0:T(8,128)(2,1)S(1)}, bf16[256,512]{1,0:T(8,128)(2,1)S(1)}, u32[]{:S(2)}, u32[]{:S(2)}) collective-permute-start(bf16[256,512]{1,0:T(8,128)(2,1)S(1)} %get-tuple-element.39), channel_id=1, source_target_pairs={{0,4},{2,6},{4,0},{6,2},{8,12},{10,14},{12,8},{14,10},{1,5},{3,7},... | collective-permute-start | bytes 786440 | tf_op jit(solution)/shard_map/ppermute | solution.py:208
  55.6 9.4 %collective-permute-start.4 = (bf16[256,512]{1,0:T(8,128)(2,1)S(1)}, bf16[256,512]{1,0:T(8,128)(2,1)S(1)}, u32[]{:S(2)}, u32[]{:S(2)}) collective-permute-start(bf16[256,512]{1,0:T(8,128)(2,1)S(1)} %get-tuple-element.40), channel_id=1, source_target_pairs={{0,2},{2,0},{4,6},{6,4},{8,10},{10,8},{12,14},{14,12},{1,3},{3,1},... | collective-permute-start | bytes 786440 | tf_op jit(solution)/shard_map/ppermute | solution.py:208
  66.7 1.6 collective-permute-start.11
  68.3 5.6 %collective-permute-start.12 = (f32[4,64,128]{2,1,0:T(8,128)S(1)}, f32[4,64,128]{2,1,0:T(8,128)S(1)}, u32[]{:S(2)}, u32[]{:S(2)}) collective-permute-start(f32[4,64,128]{2,1,0:T(8,128)S(1)} %slice.36), channel_id=1, source_target_pairs={{0,1},{1,0},{2,3},{3,2},{4,5},{5,4},{6,7},{7,6},{8,9},{9,8},{10,11... | collective-permute-start | bytes 393224 | tf_op jit(solution)/shard_map/ppermute | solution.py:208
  74.0 5.0 %collective-permute-start.13 = (f32[4,64,128]{2,1,0:T(8,128)S(1)}, f32[4,64,128]{2,1,0:T(8,128)S(1)}, u32[]{:S(2)}, u32[]{:S(2)}) collective-permute-start(f32[4,64,128]{2,1,0:T(8,128)S(1)} %slice_add_fusion.3), channel_id=1, source_target_pairs={{0,4},{4,0},{8,12},{12,8},{1,5},{5,1},{9,13},{13,9},{2,6},{6,2},{1... | collective-permute-start | bytes 393224 | tf_op jit(solution)/shard_map/ppermute | solution.py:208
  79.0 7.3 %collective-permute-start.14 = (f32[4,64,128]{2,1,0:T(8,128)S(1)}, f32[4,64,128]{2,1,0:T(8,128)S(1)}, u32[]{:S(2)}, u32[]{:S(2)}) collective-permute-start(f32[4,64,128]{2,1,0:T(8,128)S(1)} %add.245), channel_id=1, source_target_pairs={{0,8},{4,12},{8,0},{12,4},{1,9},{5,13},{9,1},{13,5},{2,10},{6,14},... | collective-permute-start | bytes 393224 | tf_op jit(solution)/shard_map/ppermute | solution.py:208
  86.4 5.0 %collective-permute-start.15 = (f32[4,64,128]{2,1,0:T(8,128)S(1)}, f32[4,64,128]{2,1,0:T(8,128)S(1)}, u32[]{:S(2)}, u32[]{:S(2)}) collective-permute-start(f32[4,64,128]{2,1,0:T(8,128)S(1)} %add.246), channel_id=1, source_target_pairs={{0,1},{1,0},{2,3},{3,2},{4,5},{5,4},{6,7},{7,6},{8,9},{9,8},{10,11... | collective-permute-start | bytes 393224 | tf_op jit(solution)/shard_map/ppermute | solution.py:208
  91.4 1.6 collective-permute-start.16
  101.9 4.3 %collective-permute-start.18 = (bf16[4,64,128]{2,1,0:T(8,128)(2,1)S(1)}, bf16[4,64,128]{2,1,0:T(8,128)(2,1)S(1)}, u32[]{:S(2)}, u32[]{:S(2)}) collective-permute-start(bf16[4,64,128]{2,1,0:T(8,128)(2,1)S(1)} %slice.58), channel_id=1, source_target_pairs={{0,1},{1,0},{2,3},{3,2},{4,5},{5,4},{6,7},{7,6},{8,9},{9,8},{10,11... | collective-permute-start | bytes 196616 | tf_op jit(solution)/shard_map/ppermute | solution.py:208
  106.2 4.3 %collective-permute-start.19 = (bf16[4,64,128]{2,1,0:T(8,128)(2,1)S(1)}, bf16[4,64,128]{2,1,0:T(8,128)(2,1)S(1)}, u32[]{:S(2)}, u32[]{:S(2)}) collective-permute-start(bf16[4,64,128]{2,1,0:T(8,128)(2,1)S(1)} %fusion.16), channel_id=1, source_target_pairs={{0,4},{4,0},{8,12},{12,8},{1,5},{5,1},{9,13},{13,9},{2,6},{6,2},{1... | collective-permute-start | bytes 196616 | tf_op jit(solution)/shard_map/ppermute | solution.py:208
  110.6 5.4 %collective-permute-start.20 = (bf16[4,64,128]{2,1,0:T(8,128)(2,1)S(1)}, bf16[4,64,128]{2,1,0:T(8,128)(2,1)S(1)}, u32[]{:S(2)}, u32[]{:S(2)}) collective-permute-start(bf16[4,64,128]{2,1,0:T(8,128)(2,1)S(1)} %add_convert_fusion.5), channel_id=1, source_target_pairs={{0,8},{4,12},{8,0},{12,4},{1,9},{5,13},{9,1},{13,5},{2,10},{6,14},... | collective-permute-start | bytes 196616 | tf_op jit(solution)/shard_map/ppermute | solution.py:208
  116.0 4.3 %collective-permute-start.21 = (bf16[4,64,128]{2,1,0:T(8,128)(2,1)S(1)}, bf16[4,64,128]{2,1,0:T(8,128)(2,1)S(1)}, u32[]{:S(2)}, u32[]{:S(2)}) collective-permute-start(bf16[4,64,128]{2,1,0:T(8,128)(2,1)S(1)} %add_convert_fusion.4), channel_id=1, source_target_pairs={{0,1},{1,0},{2,3},{3,2},{4,5},{5,4},{6,7},{7,6},{8,9},{9,8},{10,11... | collective-permute-start | bytes 196616 | tf_op jit(solution)/shard_map/ppermute | solution.py:208
  120.3 1.4 collective-permute-start.22
  128.5 1.4 collective-permute-start.23
  129.9 4.3 %collective-permute-start.24 = (bf16[4,64,128]{2,1,0:T(8,128)(2,1)S(1)}, bf16[4,64,128]{2,1,0:T(8,128)(2,1)S(1)}, u32[]{:S(2)}, u32[]{:S(2)}) collective-permute-start(bf16[4,64,128]{2,1,0:T(8,128)(2,1)S(1)} %slice.57), channel_id=1, source_target_pairs={{0,1},{1,0},{2,3},{3,2},{4,5},{5,4},{6,7},{7,6},{8,9},{9,8},{10,11... | collective-permute-start | bytes 196616 | tf_op jit(solution)/shard_map/ppermute | solution.py:208
  134.3 4.3 %collective-permute-start.25 = (bf16[4,64,128]{2,1,0:T(8,128)(2,1)S(1)}, bf16[4,64,128]{2,1,0:T(8,128)(2,1)S(1)}, u32[]{:S(2)}, u32[]{:S(2)}) collective-permute-start(bf16[4,64,128]{2,1,0:T(8,128)(2,1)S(1)} %fusion.15), channel_id=1, source_target_pairs={{0,4},{4,0},{8,12},{12,8},{1,5},{5,1},{9,13},{13,9},{2,6},{6,2},{1... | collective-permute-start | bytes 196616 | tf_op jit(solution)/shard_map/ppermute | solution.py:208
  138.6 5.4 %collective-permute-start.26 = (bf16[4,64,128]{2,1,0:T(8,128)(2,1)S(1)}, bf16[4,64,128]{2,1,0:T(8,128)(2,1)S(1)}, u32[]{:S(2)}, u32[]{:S(2)}) collective-permute-start(bf16[4,64,128]{2,1,0:T(8,128)(2,1)S(1)} %add_convert_fusion.3), channel_id=1, source_target_pairs={{0,8},{4,12},{8,0},{12,4},{1,9},{5,13},{9,1},{13,5},{2,10},{6,14},... | collective-permute-start | bytes 196616 | tf_op jit(solution)/shard_map/ppermute | solution.py:208
  144.0 4.3 %collective-permute-start.27 = (bf16[4,64,128]{2,1,0:T(8,128)(2,1)S(1)}, bf16[4,64,128]{2,1,0:T(8,128)(2,1)S(1)}, u32[]{:S(2)}, u32[]{:S(2)}) collective-permute-start(bf16[4,64,128]{2,1,0:T(8,128)(2,1)S(1)} %add_convert_fusion.2), channel_id=1, source_target_pairs={{0,1},{1,0},{2,3},{3,2},{4,5},{5,4},{6,7},{7,6},{8,9},{9,8},{10,11... | collective-permute-start | bytes 196616 | tf_op jit(solution)/shard_map/ppermute | solution.py:208
  148.4 1.4 collective-permute-start.28
  158.0 4.3 %collective-permute-start.30 = (bf16[4,64,128]{2,1,0:T(8,128)(2,1)S(1)}, bf16[4,64,128]{2,1,0:T(8,128)(2,1)S(1)}, u32[]{:S(2)}, u32[]{:S(2)}) collective-permute-start(bf16[4,64,128]{2,1,0:T(8,128)(2,1)S(1)} %slice.56), channel_id=1, source_target_pairs={{0,1},{1,0},{2,3},{3,2},{4,5},{5,4},{6,7},{7,6},{8,9},{9,8},{10,11... | collective-permute-start | bytes 196616 | tf_op jit(solution)/shard_map/ppermute | solution.py:208
  162.3 4.3 %collective-permute-start.31 = (bf16[4,64,128]{2,1,0:T(8,128)(2,1)S(1)}, bf16[4,64,128]{2,1,0:T(8,128)(2,1)S(1)}, u32[]{:S(2)}, u32[]{:S(2)}) collective-permute-start(bf16[4,64,128]{2,1,0:T(8,128)(2,1)S(1)} %fusion.14), channel_id=1, source_target_pairs={{0,4},{4,0},{8,12},{12,8},{1,5},{5,1},{9,13},{13,9},{2,6},{6,2},{1... | collective-permute-start | bytes 196616 | tf_op jit(solution)/shard_map/ppermute | solution.py:208
  166.7 5.4 %collective-permute-start.32 = (bf16[4,64,128]{2,1,0:T(8,128)(2,1)S(1)}, bf16[4,64,128]{2,1,0:T(8,128)(2,1)S(1)}, u32[]{:S(2)}, u32[]{:S(2)}) collective-permute-start(bf16[4,64,128]{2,1,0:T(8,128)(2,1)S(1)} %add_convert_fusion.1), channel_id=1, source_target_pairs={{0,8},{4,12},{8,0},{12,4},{1,9},{5,13},{9,1},{13,5},{2,10},{6,14},... | collective-permute-start | bytes 196616 | tf_op jit(solution)/shard_map/ppermute | solution.py:208
  172.1 4.3 %collective-permute-start.33 = (bf16[4,64,128]{2,1,0:T(8,128)(2,1)S(1)}, bf16[4,64,128]{2,1,0:T(8,128)(2,1)S(1)}, u32[]{:S(2)}, u32[]{:S(2)}) collective-permute-start(bf16[4,64,128]{2,1,0:T(8,128)(2,1)S(1)} %add_convert_fusion), channel_id=1, source_target_pairs={{0,1},{1,0},{2,3},{3,2},{4,5},{5,4},{6,7},{7,6},{8,9},{9,8},{10,11... | collective-permute-start | bytes 196616 | tf_op jit(solution)/shard_map/ppermute | solution.py:208
  (3 other events, 4.2 us)

commit v5 on v4

--- a/solution.py
+++ b/solution.py
@@ -89,33 +89,39 @@
     for i in range(blocks):
         unit = jnp.where(square_col == square_row + SUB * i, 1.0, 0.0).astype(jnp.float32)
         work.append(jnp.concatenate([matrix[SUB * i : SUB * (i + 1), :], unit], axis=1))
+
+    def everywhere(row):
+        return jnp.broadcast_to(row, (SUB, 2 * size))
+
     rows = []
     for b in range(blocks):
-        columns = [
-            {
-                i: jnp.broadcast_to(work[i][:, SUB * b + j : SUB * b + j + 1], (SUB, 2 * size))
-                for i in range(b, blocks)
-            }
-            for j in range(SUB)
+        columns = {
+            i: [everywhere(work[i][:, SUB * b + j : SUB * b + j + 1]) for j in range(SUB)]
+            for i in range(b, blocks)
+        }
+        entry = [
+            [everywhere(columns[b][j][i : i + 1, :]) if i <= j else None for j in range(SUB)]
+            for i in range(SUB)
         ]
-        pivots = jnp.zeros((SUB, 2 * size), jnp.float32)
+        row = [everywhere(work[b][k : k + 1, :]) for k in range(SUB)]
+        reciprocal = []
         for k in range(SUB):
-            pivot = jnp.broadcast_to(columns[k][b][k : k + 1, :], (SUB, 2 * size))
-            reciprocal = 1.0 / pivot
-            pivots = jnp.where(row_index == k, pivot, pivots)
-            work_row = jnp.broadcast_to(work[b][k : k + 1, :], (SUB, 2 * size))
-            later = [
-                jnp.broadcast_to(columns[j][b][k : k + 1, :], (SUB, 2 * size))
-                for j in range(k + 1, SUB)
-            ]
-            for i in range(b, blocks):
-                factor = columns[k][i] * reciprocal
-                if i == b:
-                    factor = jnp.where(row_index > k, factor, 0.0)
+            reciprocal.append(1.0 / entry[k][k])
+            for i in range(k + 1, SUB):
+                factor = entry[k][i] * reciprocal[k]
+                for j in range(i, SUB):
+                    entry[i][j] = entry[i][j] - factor * entry[k][j]
+                row[i] = row[i] - factor * row[k]
+        for i in range(b + 1, blocks):
+            for k in range(SUB):
+                factor = columns[i][k] * reciprocal[k]
                 for j in range(k + 1, SUB):
-                    columns[j][i] = columns[j][i] - factor * later[j - k - 1]
-                work[i] = work[i] - factor * work_row
-        rows.append(work[b] * lax.rsqrt(pivots))
+                    columns[i][j] = columns[i][j] - factor * entry[k][j]
+                work[i] = work[i] - factor * row[k]
+        scaled = row[0] * lax.rsqrt(entry[0][0])
+        for k in range(1, SUB):
+            scaled = jnp.where(row_index == k, row[k] * lax.rsqrt(entry[k][k]), scaled)
+        rows.append(scaled)
     both = jnp.concatenate(rows, axis=0)
     keep = lax.broadcasted_iota(jnp.int32, (size, size), 1) >= lax.broadcasted_iota(
         jnp.int32, (size, size), 0
@@ -123,14 +129,18 @@
     return jnp.where(keep, both[:, :size], 0.0), both[:, size:]
 
 
-def shifted(whole_gram):
+def shifted(whole_gram, trace):
     size = whole_gram.shape[0]
     diagonal = lax.broadcasted_iota(jnp.int32, (size, size), 0) == lax.broadcasted_iota(
         jnp.int32, (size, size), 1
     )
-    on_diagonal = jnp.where(diagonal, whole_gram, 0.0)
-    trace = jnp.sum(jnp.sum(on_diagonal, axis=1, keepdims=True), axis=0, keepdims=True)
     return jnp.where(diagonal, whole_gram + shift_ratio * trace, whole_gram)
+
+
+def sum_of_squares(wide):
+    wide = wide.astype(jnp.float32)
+    by_row = jnp.sum(wide * wide, axis=0, keepdims=True)
+    return jnp.sum(by_row, axis=1, keepdims=True)
 
 
 def wide_of(at_ref, z_refs):
@@ -142,7 +152,7 @@
 
 def narrow_basis(at_ref, z_refs):
     wide = wide_of(at_ref, z_refs)
-    upper, inverse_one = eliminate(shifted(gram_of(wide)))
+    upper, inverse_one = eliminate(shifted(gram_of(wide), sum_of_squares(wide)))
     first = small_times_wide(inverse_one, wide)
     unused, inverse_two = eliminate(gram_of(first))
     return small_times_wide(inverse_two, first).astype(jnp.bfloat16), upper
@@ -261,24 +271,25 @@
 
     far = list(range(n_row // 2, n_row))
     near = list(range(n_row // 2 - 1, -1, -1))
-    move(states, far[:1])
+    pieces[far[0]] = block(states, far[0])
+    slab, pieces[far[0]] = lax.optimization_barrier((states, pieces[far[0]]))
+    pieces[far[0]] = from_xor(pieces[far[0]], ("z", "core"), far[0])
 
     col = lax.axis_index("col")
     feature_index = col * width_local + jnp.arange(width_local, dtype=jnp.int32)
     omega = sketch_table(sketch_base[0], feature_index, RANK)
-    z = lax.dot_general(
-        omega, states, (((0,), (1,)), ((), ())), preferred_element_type=jnp.float32
-    )
+    z = lax.dot_general(omega, slab, (((0,), (1,)), ((), ())), preferred_element_type=jnp.float32)
     for bit in bits(n_col):
         z = z + from_xor(z, ("col",), bit)
     z = z.reshape(RANK, n_col, chunk).transpose(1, 0, 2)
+    z, pieces[far[0]], slab = lax.optimization_barrier((z, pieces[far[0]], slab))
+    move(slab, far[1:2])
     z_bits = bits(n_z)[::-1]
     for k, bit in enumerate(z_bits):
         z = jnp.concatenate([z, from_xor(z, ("z",), bit)])
-        slab, z = lax.optimization_barrier((states, z))
-        if k == 0:
-            move(slab, far[1:2])
-    move(slab, far[2:] + near)
+        z, slab = lax.optimization_barrier((z, slab))
+        move(slab, far[2:3] if k == 0 else [])
+    move(slab, far[3:])
     z = z, from_xor(z, ("core",), 1)
     absolute_col = [("col", bit, False) for bit in bits(n_col)[::-1]]
     at_first = chunk_places([("z", bit, True) for bit in z_bits[::-1]] + absolute_col)
@@ -296,6 +307,8 @@
         return jax.ShapeDtypeStruct(shape, f32), jax.ShapeDtypeStruct(shape, dtype)
 
     basis, upper = call(orth_kernel, (wide, square), orth_flops, at_first, *z)
+    basis, slab = lax.optimization_barrier((basis, slab))
+    move(slab, near)
     factor = upper.T * (1.0 / math.sqrt(rows_total * width_total))
     dtype = f32
     parts = call(power_kernel, sent_as(dtype), power_flops, at, basis, *pieces)

time: 185 us -> 193 us (1.043)
  waiting for transfers between devices: 102 us -> 126 us
  starting transfers between devices: 37.2 us -> 22.1 us
  local copies, waits for them, and re-layouts: 4.14 us -> 1.9 us
    ppermute x35, waiting for transfers between devices: 102 us -> 126 us  [from_xor(): return lax.ppermute(value, axis, [(i, i ^ offset) for i in range(size)])]
    ppermute x35, starting transfers between devices: 37.2 us -> 22.1 us  [from_xor(): return lax.ppermute(value, axis, [(i, i ^ offset) for i in range(size)])]
    dynamic_slice x3 -> x5, local copies, waits for them, and re-layouts: 3.39 us -> 1.15 us  [block(): return lax.dynamic_slice_in_dim(slab, (row ^ offset) * cols, cols, 1)]
  transfers between devices with their start and end apart: 35 -> 35, of which waited for: 29 -> 30; matrix products, arithmetic and copies ran while one was open for 2% -> 0% of each run, Pallas kernels for 3% -> 3%
where the time goes in v5:
time: 193 us
  waiting for transfers between devices  126 us (65%)
  Pallas kernels  36.4 us (19%)
  starting transfers between devices  22.1 us (11%)
  matrix products  3.97 us (2%)
    ppermute x35, waiting for transfers between devices, from_xor(): return lax.ppermute(value, axis, [(i, i ^ offset) for i in range(size)])  126 us
    pallas_call x6, Pallas kernels, call(): pl.pallas_call(kernel, out_shape=out_shapes, in_specs=[pl.BlockSpec(memor...  36.4 us
    ppermute x35, starting transfers between devices, from_xor(): return lax.ppermute(value, axis, [(i, i ^ offset) for i in range(size)])  22.1 us
    dot_general x1, matrix products, per_device_transposed(): lax.dot_general(omega, slab, (((0,), (1,)), ((), ())), preferred_element_...  3.97 us
  transfers between devices with their start and end apart: 35, of which 30 were waited for; matrix products, arithmetic and copies ran while one was open for 0% of the time, Pallas kernels for 3%

profile of v5, /device:TPU:0, one launch (start us, length us, event | category | flops | bytes accessed | tf_op | source)
XLA Modules:
  0.0 192.9 jit_solution(1522557435120838451)
XLA Ops:
  2.3 4.0 %fusion = f32[64,256]{1,0:T(8,128)S(1)} fusion(bf16[256,4096]{1,0:T(8,128)(2,1)} %param.3, s32[]{:T(128)S(6)} %xor.84, s32[4096]{0:T(1024)S(1)} %add_multiply_fusion), kind=kOutput, calls=%fused_computation.1 | convolution fusion | flops 152043520 | bytes 2179076 | tf_op jit(solution)/shard_map/dot_general | solution.py:281
  6.3 3.0 %collective-permute-start = (f32[64,256]{1,0:T(8,128)S(1)}, f32[64,256]{1,0:T(8,128)S(1)}, u32[]{:S(2)}, u32[]{:S(2)}) collective-permute-start(f32[64,256]{1,0:T(8,128)S(1)} %fusion), channel_id=1, source_target_pairs={{0,1},{1,0},{2,3},{3,2},{4,5},{5,4},{6,7},{7,6},{8,9},{9,8},{10,11... | collective-permute-start | bytes 196616 | tf_op jit(solution)/shard_map/ppermute | solution.py:218
  9.3 2.6 %collective-permute-start.1 = (bf16[256,512]{1,0:T(8,128)(2,1)S(1)}, bf16[256,512]{1,0:T(8,128)(2,1)S(1)}, u32[]{:S(2)}, u32[]{:S(2)}) collective-permute-start(bf16[256,512]{1,0:T(8,128)(2,1)S(1)} %constant_dynamic-slice_fusion.7), channel_id=1, source_target_pairs={{0,8},{2,10},{4,12},{6,14},{8,0},{10,2},{12,4},{14,6},{1,9},{3,11}... | collective-permute-start | bytes 786440 | tf_op jit(solution)/shard_map/ppermute | solution.py:218
  11.9 11.7 %collective-permute-done.1.refs_4_ = bf16[256,512]{1,0:T(8,128)(2,1)S(1)} collective-permute-done((bf16[256,512]{1,0:T(8,128)(2,1)S(1)}, bf16[256,512]{1,0:T(8,128)(2,1)S(1)}, u32[]{:S(2)}, u32[]{:S(2)}) %collective-permute-start.1) | collective-permute-done | bytes 262176 | tf_op jit(solution)/shard_map/ppermute | solution.py:218
  23.6 6.5 %collective-permute-done.2 = f32[2,64,128]{2,1,0:T(8,128)S(1)} collective-permute-done((f32[2,64,128]{2,1,0:T(8,128)S(1)}, f32[2,64,128]{2,1,0:T(8,128)S(1)}, u32[]{:S(2)}, u32[]{:S(2)}) %collective-permute-start.2) | collective-permute-done | bytes 65568 | tf_op jit(solution)/shard_map/ppermute | solution.py:218
  30.2 4.9 %collective-permute-done.3 = f32[4,64,128]{2,1,0:T(8,128)S(1)} collective-permute-done((f32[4,64,128]{2,1,0:T(8,128)S(1)}, f32[4,64,128]{2,1,0:T(8,128)S(1)}, u32[]{:S(2)}, u32[]{:S(2)}) %collective-permute-start.3) | collective-permute-done | bytes 131104 | tf_op jit(solution)/shard_map/ppermute | solution.py:218
  36.1 1.7 collective-permute-start.9
  39.4 6.4 %shard_map.41 = (bf16[64,2048]{1,0:T(8,128)(2,1)S(1)}, f32[64,64]{1,0:T(8,128)S(1)}) custom-call(s32[16]{0:T(128)S(1)} %fusion.20.at_ref, f32[8,64,128]{2,1,0:T(8,128)S(1)} %pad_maximum_fusion.z_ref, f32[8,64,128]{2,1,0:T(8,128)S(1)} %collective-permute-done.4.other_ref), custom_call_target="tpu_custom_call" | custom-call | flops 402653184 | bytes 524288 | tf_op jit(solution)/shard_map/pallas_call | solution.py:201
  46.6 1.8 collective-permute-start.6
  48.4 12.9 %collective-permute-done.8.refs_5_ = bf16[256,512]{1,0:T(8,128)(2,1)S(1)} collective-permute-done((bf16[256,512]{1,0:T(8,128)(2,1)S(1)}, bf16[256,512]{1,0:T(8,128)(2,1)S(1)}, u32[]{:S(2)}, u32[]{:S(2)}) %collective-permute-start.8) | collective-permute-done | bytes 262176 | tf_op jit(solution)/shard_map/ppermute | solution.py:218
  61.4 5.4 %collective-permute-done.7.refs_3_ = bf16[256,512]{1,0:T(8,128)(2,1)S(1)} collective-permute-done((bf16[256,512]{1,0:T(8,128)(2,1)S(1)}, bf16[256,512]{1,0:T(8,128)(2,1)S(1)}, u32[]{:S(2)}, u32[]{:S(2)}) %collective-permute-start.7) | collective-permute-done | bytes 262176 | tf_op jit(solution)/shard_map/ppermute | solution.py:218
  66.8 5.7 %collective-permute-done.6.refs_2_ = bf16[256,512]{1,0:T(8,128)(2,1)S(1)} collective-permute-done((bf16[256,512]{1,0:T(8,128)(2,1)S(1)}, bf16[256,512]{1,0:T(8,128)(2,1)S(1)}, u32[]{:S(2)}, u32[]{:S(2)}) %collective-permute-start.6) | collective-permute-done | bytes 262176 | tf_op jit(solution)/shard_map/ppermute | solution.py:218
  76.5 5.0 %collective-permute-done.12 = f32[4,64,128]{2,1,0:T(8,128)S(1)} collective-permute-done((f32[4,64,128]{2,1,0:T(8,128)S(1)}, f32[4,64,128]{2,1,0:T(8,128)S(1)}, u32[]{:S(2)}, u32[]{:S(2)}) %collective-permute-start.12) | collective-permute-done | bytes 131104 | tf_op jit(solution)/shard_map/ppermute | solution.py:218
  82.1 4.4 %collective-permute-done.13 = f32[4,64,128]{2,1,0:T(8,128)S(1)} collective-permute-done((f32[4,64,128]{2,1,0:T(8,128)S(1)}, f32[4,64,128]{2,1,0:T(8,128)S(1)}, u32[]{:S(2)}, u32[]{:S(2)}) %collective-permute-start.13) | collective-permute-done | bytes 131104 | tf_op jit(solution)/shard_map/ppermute | solution.py:218
  87.7 6.2 %collective-permute-done.14 = f32[4,64,128]{2,1,0:T(8,128)S(1)} collective-permute-done((f32[4,64,128]{2,1,0:T(8,128)S(1)}, f32[4,64,128]{2,1,0:T(8,128)S(1)}, u32[]{:S(2)}, u32[]{:S(2)}) %collective-permute-start.14) | collective-permute-done | bytes 131104 | tf_op jit(solution)/shard_map/ppermute | solution.py:218
  94.5 4.4 %collective-permute-done.15 = f32[4,64,128]{2,1,0:T(8,128)S(1)} collective-permute-done((f32[4,64,128]{2,1,0:T(8,128)S(1)}, f32[4,64,128]{2,1,0:T(8,128)S(1)}, u32[]{:S(2)}, u32[]{:S(2)}) %collective-permute-start.15) | collective-permute-done | bytes 131104 | tf_op jit(solution)/shard_map/ppermute | solution.py:218
  100.5 7.6 %shard_map.43 = (f32[8,64,128]{2,1,0:T(8,128)S(1)}, bf16[8,64,128]{2,1,0:T(8,128)(2,1)S(1)}) custom-call(s32[16]{0:T(128)S(1)} %fusion.18.at_ref, f32[8,64,128]{2,1,0:T(8,128)S(1)} %pad_maximum_fusion.1.z_ref, f32[8,64,128]{2,1,0:T(8,128)S(1)} %collective-permute-done.16.other_ref, bf16[256,512]{1,0:T(8,128)(2,1)S(1)} %get-tuple-element.53.refs_0_, ...), custom_call_target="tpu_custom_call" | custom-call | flops 671088640 | bytes 2621440 | tf_op jit(solution)/shard_map/pallas_call | solution.py:201
  110.2 3.7 %collective-permute-done.18 = bf16[4,64,128]{2,1,0:T(8,128)(2,1)S(1)} collective-permute-done((bf16[4,64,128]{2,1,0:T(8,128)(2,1)S(1)}, bf16[4,64,128]{2,1,0:T(8,128)(2,1)S(1)}, u32[]{:S(2)}, u32[]{:S(2)}) %collective-permute-start.18) | collective-permute-done | bytes 65568 | tf_op jit(solution)/shard_map/ppermute | solution.py:218
  114.0 4.3 %collective-permute-done.19 = bf16[4,64,128]{2,1,0:T(8,128)(2,1)S(1)} collective-permute-done((bf16[4,64,128]{2,1,0:T(8,128)(2,1)S(1)}, bf16[4,64,128]{2,1,0:T(8,128)(2,1)S(1)}, u32[]{:S(2)}, u32[]{:S(2)}) %collective-permute-start.19) | collective-permute-done | bytes 65568 | tf_op jit(solution)/shard_map/ppermute | solution.py:218
  118.9 4.8 %collective-permute-done.20 = bf16[4,64,128]{2,1,0:T(8,128)(2,1)S(1)} collective-permute-done((bf16[4,64,128]{2,1,0:T(8,128)(2,1)S(1)}, bf16[4,64,128]{2,1,0:T(8,128)(2,1)S(1)}, u32[]{:S(2)}, u32[]{:S(2)}) %collective-permute-start.20) | collective-permute-done | bytes 65568 | tf_op jit(solution)/shard_map/ppermute | solution.py:218
  124.3 3.7 %collective-permute-done.21 = bf16[4,64,128]{2,1,0:T(8,128)(2,1)S(1)} collective-permute-done((bf16[4,64,128]{2,1,0:T(8,128)(2,1)S(1)}, bf16[4,64,128]{2,1,0:T(8,128)(2,1)S(1)}, u32[]{:S(2)}, u32[]{:S(2)}) %collective-permute-start.21) | collective-permute-done | bytes 65568 | tf_op jit(solution)/shard_map/ppermute | solution.py:218
  129.4 6.8 %shard_map.44 = (f32[8,64,128]{2,1,0:T(8,128)S(1)}, bf16[8,64,128]{2,1,0:T(8,128)(2,1)S(1)}) custom-call(s32[16]{0:T(128)S(1)} %fusion.18.at_ref, bf16[8,64,128]{2,1,0:T(8,128)(2,1)S(1)} %pad_maximum_fusion.3.z_ref, bf16[8,64,128]{2,1,0:T(8,128)(2,1)S(1)} %collective-permute-done.22.other_ref, bf16[256,512]{1,0:T(8,128)(2,1)S(1)} %get-tuple-element.53.refs_0_, ...), custom_call_target="tpu_custom_call" | custom-call | flops 671088640 | bytes 2359296 | tf_op jit(solution)/shard_map/pallas_call | solution.py:201
  138.3 3.7 %collective-permute-done.24 = bf16[4,64,128]{2,1,0:T(8,128)(2,1)S(1)} collective-permute-done((bf16[4,64,128]{2,1,0:T(8,128)(2,1)S(1)}, bf16[4,64,128]{2,1,0:T(8,128)(2,1)S(1)}, u32[]{:S(2)}, u32[]{:S(2)}) %collective-permute-start.24) | collective-permute-done | bytes 65568 | tf_op jit(solution)/shard_map/ppermute | solution.py:218
  142.2 4.3 %collective-permute-done.25 = bf16[4,64,128]{2,1,0:T(8,128)(2,1)S(1)} collective-permute-done((bf16[4,64,128]{2,1,0:T(8,128)(2,1)S(1)}, bf16[4,64,128]{2,1,0:T(8,128)(2,1)S(1)}, u32[]{:S(2)}, u32[]{:S(2)}) %collective-permute-start.25) | collective-permute-done | bytes 65568 | tf_op jit(solution)/shard_map/ppermute | solution.py:218
  147.1 4.8 %collective-permute-done.26 = bf16[4,64,128]{2,1,0:T(8,128)(2,1)S(1)} collective-permute-done((bf16[4,64,128]{2,1,0:T(8,128)(2,1)S(1)}, bf16[4,64,128]{2,1,0:T(8,128)(2,1)S(1)}, u32[]{:S(2)}, u32[]{:S(2)}) %collective-permute-start.26) | collective-permute-done | bytes 65568 | tf_op jit(solution)/shard_map/ppermute | solution.py:218
  152.4 3.7 %collective-permute-done.27 = bf16[4,64,128]{2,1,0:T(8,128)(2,1)S(1)} collective-permute-done((bf16[4,64,128]{2,1,0:T(8,128)(2,1)S(1)}, bf16[4,64,128]{2,1,0:T(8,128)(2,1)S(1)}, u32[]{:S(2)}, u32[]{:S(2)}) %collective-permute-start.27) | collective-permute-done | bytes 65568 | tf_op jit(solution)/shard_map/ppermute | solution.py:218
  157.6 6.8 %shard_map.45 = (f32[8,64,128]{2,1,0:T(8,128)S(1)}, bf16[8,64,128]{2,1,0:T(8,128)(2,1)S(1)}) custom-call(s32[16]{0:T(128)S(1)} %fusion.18.at_ref, bf16[8,64,128]{2,1,0:T(8,128)(2,1)S(1)} %pad_maximum_fusion.4.z_ref, bf16[8,64,128]{2,1,0:T(8,128)(2,1)S(1)} %collective-permute-done.28.other_ref, bf16[256,512]{1,0:T(8,128)(2,1)S(1)} %get-tuple-element.53.refs_0_, ...), custom_call_target="tpu_custom_call" | custom-call | flops 671088640 | bytes 2359296 | tf_op jit(solution)/shard_map/pallas_call | solution.py:201
  166.5 3.7 %collective-permute-done.30 = bf16[4,64,128]{2,1,0:T(8,128)(2,1)S(1)} collective-permute-done((bf16[4,64,128]{2,1,0:T(8,128)(2,1)S(1)}, bf16[4,64,128]{2,1,0:T(8,128)(2,1)S(1)}, u32[]{:S(2)}, u32[]{:S(2)}) %collective-permute-start.30) | collective-permute-done | bytes 65568 | tf_op jit(solution)/shard_map/ppermute | solution.py:218
  170.3 4.3 %collective-permute-done.31 = bf16[4,64,128]{2,1,0:T(8,128)(2,1)S(1)} collective-permute-done((bf16[4,64,128]{2,1,0:T(8,128)(2,1)S(1)}, bf16[4,64,128]{2,1,0:T(8,128)(2,1)S(1)}, u32[]{:S(2)}, u32[]{:S(2)}) %collective-permute-start.31) | collective-permute-done | bytes 65568 | tf_op jit(solution)/shard_map/ppermute | solution.py:218
  175.2 4.8 %collective-permute-done.32 = bf16[4,64,128]{2,1,0:T(8,128)(2,1)S(1)} collective-permute-done((bf16[4,64,128]{2,1,0:T(8,128)(2,1)S(1)}, bf16[4,64,128]{2,1,0:T(8,128)(2,1)S(1)}, u32[]{:S(2)}, u32[]{:S(2)}) %collective-permute-start.32) | collective-permute-done | bytes 65568 | tf_op jit(solution)/shard_map/ppermute | solution.py:218
  180.6 3.7 %collective-permute-done.33 = bf16[4,64,128]{2,1,0:T(8,128)(2,1)S(1)} collective-permute-done((bf16[4,64,128]{2,1,0:T(8,128)(2,1)S(1)}, bf16[4,64,128]{2,1,0:T(8,128)(2,1)S(1)}, u32[]{:S(2)}, u32[]{:S(2)}) %collective-permute-start.33) | collective-permute-done | bytes 65568 | tf_op jit(solution)/shard_map/ppermute | solution.py:218
  185.8 7.2 %shard_map.46 = f32[64,512]{1,0:T(8,128)} custom-call(s32[16]{0:T(128)S(1)} %fusion.18.at_ref, bf16[8,64,128]{2,1,0:T(8,128)(2,1)S(1)} %pad_maximum_fusion.5.z_ref, bf16[8,64,128]{2,1,0:T(8,128)(2,1)S(1)} %collective-permute-done.34.other_ref, bf16[256,512]{1,0:T(8,128)(2,1)S(1)} %get-tuple-element.53.refs_0_, ...), custom_call_target="tpu_custom_call" | custom-call | flops 671088640 | bytes 2359296 | tf_op jit(solution)/shard_map/pallas_call | solution.py:201
  (84 shorter events, 27.1 us)
Async XLA Ops:
  6.3 5.6 %collective-permute-start = (f32[64,256]{1,0:T(8,128)S(1)}, f32[64,256]{1,0:T(8,128)S(1)}, u32[]{:S(2)}, u32[]{:S(2)}) collective-permute-start(f32[64,256]{1,0:T(8,128)S(1)} %fusion), channel_id=1, source_target_pairs={{0,1},{1,0},{2,3},{3,2},{4,5},{5,4},{6,7},{7,6},{8,9},{9,8},{10,11... | collective-permute-start | bytes 196616 | tf_op jit(solution)/shard_map/ppermute | solution.py:218
  9.3 14.3 %collective-permute-start.1 = (bf16[256,512]{1,0:T(8,128)(2,1)S(1)}, bf16[256,512]{1,0:T(8,128)(2,1)S(1)}, u32[]{:S(2)}, u32[]{:S(2)}) collective-permute-start(bf16[256,512]{1,0:T(8,128)(2,1)S(1)} %constant_dynamic-slice_fusion.7), channel_id=1, source_target_pairs={{0,8},{2,10},{4,12},{6,14},{8,0},{10,2},{12,4},{14,6},{1,9},{3,11}... | collective-permute-start | bytes 786440 | tf_op jit(solution)/shard_map/ppermute | solution.py:218
  23.6 6.5 %collective-permute-start.2 = (f32[2,64,128]{2,1,0:T(8,128)S(1)}, f32[2,64,128]{2,1,0:T(8,128)S(1)}, u32[]{:S(2)}, u32[]{:S(2)}) collective-permute-start(f32[2,64,128]{2,1,0:T(8,128)S(1)} %bitcast_bitcast_fusion), channel_id=1, source_target_pairs={{0,8},{4,12},{8,0},{12,4},{1,9},{5,13},{9,1},{13,5},{2,10},{6,14},... | collective-permute-start | bytes 196616 | tf_op jit(solution)/shard_map/ppermute | solution.py:218
  30.0 5.0 %collective-permute-start.3 = (f32[4,64,128]{2,1,0:T(8,128)S(1)}, f32[4,64,128]{2,1,0:T(8,128)S(1)}, u32[]{:S(2)}, u32[]{:S(2)}) collective-permute-start(f32[4,64,128]{2,1,0:T(8,128)S(1)} %pad_maximum_fusion.2), channel_id=1, source_target_pairs={{0,4},{4,0},{8,12},{12,8},{1,5},{5,1},{9,13},{13,9},{2,6},{6,2},{1... | collective-permute-start | bytes 393224 | tf_op jit(solution)/shard_map/ppermute | solution.py:218
  35.1 4.4 %collective-permute-start.4 = (f32[8,64,128]{2,1,0:T(8,128)S(1)}, f32[8,64,128]{2,1,0:T(8,128)S(1)}, u32[]{:S(2)}, u32[]{:S(2)}) collective-permute-start(f32[8,64,128]{2,1,0:T(8,128)S(1)} %pad_maximum_fusion.z_ref), channel_id=1, source_target_pairs={{0,2},{2,0},{1,3},{3,1},{4,6},{6,4},{5,7},{7,5},{8,10},{10,8},{9,1... | collective-permute-start | bytes 786440 | tf_op jit(solution)/shard_map/ppermute | solution.py:218
  35.2 26.1 %collective-permute-start.8 = (bf16[256,512]{1,0:T(8,128)(2,1)S(1)}, bf16[256,512]{1,0:T(8,128)(2,1)S(1)}, u32[]{:S(2)}, u32[]{:S(2)}) collective-permute-start(bf16[256,512]{1,0:T(8,128)(2,1)S(1)} %constant_dynamic-slice_fusion.2), channel_id=1, source_target_pairs={{0,10},{2,8},{4,14},{6,12},{8,2},{10,0},{12,6},{14,4},{1,11},{3,9}... | collective-permute-start | bytes 786440 | tf_op jit(solution)/shard_map/ppermute | solution.py:218
  36.1 25.3 %collective-permute-start.9 = (bf16[256,512]{1,0:T(8,128)(2,1)S(1)}, bf16[256,512]{1,0:T(8,128)(2,1)S(1)}, u32[]{:S(2)}, u32[]{:S(2)}) collective-permute-start(bf16[256,512]{1,0:T(8,128)(2,1)S(1)} %constant_dynamic-slice_fusion.1), channel_id=1, source_target_pairs={{0,12},{2,14},{4,8},{6,10},{8,4},{10,6},{12,0},{14,2},{1,13},{3,15... | collective-permute-start | bytes 786440 | tf_op jit(solution)/shard_map/ppermute | solution.py:218
  37.8 23.6 %collective-permute-start.10 = (bf16[256,512]{1,0:T(8,128)(2,1)S(1)}, bf16[256,512]{1,0:T(8,128)(2,1)S(1)}, u32[]{:S(2)}, u32[]{:S(2)}) collective-permute-start(bf16[256,512]{1,0:T(8,128)(2,1)S(1)} %constant_dynamic-slice_fusion), channel_id=1, source_target_pairs={{0,14},{2,12},{4,10},{6,8},{8,6},{10,4},{12,2},{14,0},{1,15},{3,13... | collective-permute-start | bytes 786440 | tf_op jit(solution)/shard_map/ppermute | solution.py:218
  46.0 20.8 %collective-permute-start.7 = (bf16[256,512]{1,0:T(8,128)(2,1)S(1)}, bf16[256,512]{1,0:T(8,128)(2,1)S(1)}, u32[]{:S(2)}, u32[]{:S(2)}) collective-permute-start(bf16[256,512]{1,0:T(8,128)(2,1)S(1)} %get-tuple-element.50), channel_id=1, source_target_pairs={{0,6},{2,4},{4,2},{6,0},{8,14},{10,12},{12,10},{14,8},{1,7},{3,5},... | collective-permute-start | bytes 786440 | tf_op jit(solution)/shard_map/ppermute | solution.py:218
  46.6 25.9 %collective-permute-start.6 = (bf16[256,512]{1,0:T(8,128)(2,1)S(1)}, bf16[256,512]{1,0:T(8,128)(2,1)S(1)}, u32[]{:S(2)}, u32[]{:S(2)}) collective-permute-start(bf16[256,512]{1,0:T(8,128)(2,1)S(1)} %get-tuple-element.51), channel_id=1, source_target_pairs={{0,4},{2,6},{4,0},{6,2},{8,12},{10,14},{12,8},{14,10},{1,5},{3,7},... | collective-permute-start | bytes 786440 | tf_op jit(solution)/shard_map/ppermute | solution.py:218
  61.3 11.2 %collective-permute-start.5 = (bf16[256,512]{1,0:T(8,128)(2,1)S(1)}, bf16[256,512]{1,0:T(8,128)(2,1)S(1)}, u32[]{:S(2)}, u32[]{:S(2)}) collective-permute-start(bf16[256,512]{1,0:T(8,128)(2,1)S(1)} %get-tuple-element.52), channel_id=1, source_target_pairs={{0,2},{2,0},{4,6},{6,4},{8,10},{10,8},{12,14},{14,12},{1,3},{3,1},... | collective-permute-start | bytes 786440 | tf_op jit(solution)/shard_map/ppermute | solution.py:218
  74.2 1.6 collective-permute-start.11
  75.9 5.6 %collective-permute-start.12 = (f32[4,64,128]{2,1,0:T(8,128)S(1)}, f32[4,64,128]{2,1,0:T(8,128)S(1)}, u32[]{:S(2)}, u32[]{:S(2)}) collective-permute-start(f32[4,64,128]{2,1,0:T(8,128)S(1)} %slice.36), channel_id=1, source_target_pairs={{0,1},{1,0},{2,3},{3,2},{4,5},{5,4},{6,7},{7,6},{8,9},{9,8},{10,11... | collective-permute-start | bytes 393224 | tf_op jit(solution)/shard_map/ppermute | solution.py:218
  81.5 5.0 %collective-permute-start.13 = (f32[4,64,128]{2,1,0:T(8,128)S(1)}, f32[4,64,128]{2,1,0:T(8,128)S(1)}, u32[]{:S(2)}, u32[]{:S(2)}) collective-permute-start(f32[4,64,128]{2,1,0:T(8,128)S(1)} %slice_add_fusion.3), channel_id=1, source_target_pairs={{0,4},{4,0},{8,12},{12,8},{1,5},{5,1},{9,13},{13,9},{2,6},{6,2},{1... | collective-permute-start | bytes 393224 | tf_op jit(solution)/shard_map/ppermute | solution.py:218
  86.5 7.3 %collective-permute-start.14 = (f32[4,64,128]{2,1,0:T(8,128)S(1)}, f32[4,64,128]{2,1,0:T(8,128)S(1)}, u32[]{:S(2)}, u32[]{:S(2)}) collective-permute-start(f32[4,64,128]{2,1,0:T(8,128)S(1)} %add.245), channel_id=1, source_target_pairs={{0,8},{4,12},{8,0},{12,4},{1,9},{5,13},{9,1},{13,5},{2,10},{6,14},... | collective-permute-start | bytes 393224 | tf_op jit(solution)/shard_map/ppermute | solution.py:218
  93.9 5.0 %collective-permute-start.15 = (f32[4,64,128]{2,1,0:T(8,128)S(1)}, f32[4,64,128]{2,1,0:T(8,128)S(1)}, u32[]{:S(2)}, u32[]{:S(2)}) collective-permute-start(f32[4,64,128]{2,1,0:T(8,128)S(1)} %add.246), channel_id=1, source_target_pairs={{0,1},{1,0},{2,3},{3,2},{4,5},{5,4},{6,7},{7,6},{8,9},{9,8},{10,11... | collective-permute-start | bytes 393224 | tf_op jit(solution)/shard_map/ppermute | solution.py:218
  98.9 1.6 collective-permute-start.16
  108.1 1.4 collective-permute-start.17
  109.6 4.3 %collective-permute-start.18 = (bf16[4,64,128]{2,1,0:T(8,128)(2,1)S(1)}, bf16[4,64,128]{2,1,0:T(8,128)(2,1)S(1)}, u32[]{:S(2)}, u32[]{:S(2)}) collective-permute-start(bf16[4,64,128]{2,1,0:T(8,128)(2,1)S(1)} %slice.58), channel_id=1, source_target_pairs={{0,1},{1,0},{2,3},{3,2},{4,5},{5,4},{6,7},{7,6},{8,9},{9,8},{10,11... | collective-permute-start | bytes 196616 | tf_op jit(solution)/shard_map/ppermute | solution.py:218
  113.9 4.3 %collective-permute-start.19 = (bf16[4,64,128]{2,1,0:T(8,128)(2,1)S(1)}, bf16[4,64,128]{2,1,0:T(8,128)(2,1)S(1)}, u32[]{:S(2)}, u32[]{:S(2)}) collective-permute-start(bf16[4,64,128]{2,1,0:T(8,128)(2,1)S(1)} %fusion.16), channel_id=1, source_target_pairs={{0,4},{4,0},{8,12},{12,8},{1,5},{5,1},{9,13},{13,9},{2,6},{6,2},{1... | collective-permute-start | bytes 196616 | tf_op jit(solution)/shard_map/ppermute | solution.py:218
  118.3 5.4 %collective-permute-start.20 = (bf16[4,64,128]{2,1,0:T(8,128)(2,1)S(1)}, bf16[4,64,128]{2,1,0:T(8,128)(2,1)S(1)}, u32[]{:S(2)}, u32[]{:S(2)}) collective-permute-start(bf16[4,64,128]{2,1,0:T(8,128)(2,1)S(1)} %add_convert_fusion.5), channel_id=1, source_target_pairs={{0,8},{4,12},{8,0},{12,4},{1,9},{5,13},{9,1},{13,5},{2,10},{6,14},... | collective-permute-start | bytes 196616 | tf_op jit(solution)/shard_map/ppermute | solution.py:218
  123.7 4.3 %collective-permute-start.21 = (bf16[4,64,128]{2,1,0:T(8,128)(2,1)S(1)}, bf16[4,64,128]{2,1,0:T(8,128)(2,1)S(1)}, u32[]{:S(2)}, u32[]{:S(2)}) collective-permute-start(bf16[4,64,128]{2,1,0:T(8,128)(2,1)S(1)} %add_convert_fusion.4), channel_id=1, source_target_pairs={{0,1},{1,0},{2,3},{3,2},{4,5},{5,4},{6,7},{7,6},{8,9},{9,8},{10,11... | collective-permute-start | bytes 196616 | tf_op jit(solution)/shard_map/ppermute | solution.py:218
  128.0 1.4 collective-permute-start.22
  137.7 4.3 %collective-permute-start.24 = (bf16[4,64,128]{2,1,0:T(8,128)(2,1)S(1)}, bf16[4,64,128]{2,1,0:T(8,128)(2,1)S(1)}, u32[]{:S(2)}, u32[]{:S(2)}) collective-permute-start(bf16[4,64,128]{2,1,0:T(8,128)(2,1)S(1)} %slice.57), channel_id=1, source_target_pairs={{0,1},{1,0},{2,3},{3,2},{4,5},{5,4},{6,7},{7,6},{8,9},{9,8},{10,11... | collective-permute-start | bytes 196616 | tf_op jit(solution)/shard_map/ppermute | solution.py:218
  142.1 4.3 %collective-permute-start.25 = (bf16[4,64,128]{2,1,0:T(8,128)(2,1)S(1)}, bf16[4,64,128]{2,1,0:T(8,128)(2,1)S(1)}, u32[]{:S(2)}, u32[]{:S(2)}) collective-permute-start(bf16[4,64,128]{2,1,0:T(8,128)(2,1)S(1)} %fusion.15), channel_id=1, source_target_pairs={{0,4},{4,0},{8,12},{12,8},{1,5},{5,1},{9,13},{13,9},{2,6},{6,2},{1... | collective-permute-start | bytes 196616 | tf_op jit(solution)/shard_map/ppermute | solution.py:218
  146.4 5.4 %collective-permute-start.26 = (bf16[4,64,128]{2,1,0:T(8,128)(2,1)S(1)}, bf16[4,64,128]{2,1,0:T(8,128)(2,1)S(1)}, u32[]{:S(2)}, u32[]{:S(2)}) collective-permute-start(bf16[4,64,128]{2,1,0:T(8,128)(2,1)S(1)} %add_convert_fusion.3), channel_id=1, source_target_pairs={{0,8},{4,12},{8,0},{12,4},{1,9},{5,13},{9,1},{13,5},{2,10},{6,14},... | collective-permute-start | bytes 196616 | tf_op jit(solution)/shard_map/ppermute | solution.py:218
  151.8 4.3 %collective-permute-start.27 = (bf16[4,64,128]{2,1,0:T(8,128)(2,1)S(1)}, bf16[4,64,128]{2,1,0:T(8,128)(2,1)S(1)}, u32[]{:S(2)}, u32[]{:S(2)}) collective-permute-start(bf16[4,64,128]{2,1,0:T(8,128)(2,1)S(1)} %add_convert_fusion.2), channel_id=1, source_target_pairs={{0,1},{1,0},{2,3},{3,2},{4,5},{5,4},{6,7},{7,6},{8,9},{9,8},{10,11... | collective-permute-start | bytes 196616 | tf_op jit(solution)/shard_map/ppermute | solution.py:218
  165.9 4.3 %collective-permute-start.30 = (bf16[4,64,128]{2,1,0:T(8,128)(2,1)S(1)}, bf16[4,64,128]{2,1,0:T(8,128)(2,1)S(1)}, u32[]{:S(2)}, u32[]{:S(2)}) collective-permute-start(bf16[4,64,128]{2,1,0:T(8,128)(2,1)S(1)} %slice.56), channel_id=1, source_target_pairs={{0,1},{1,0},{2,3},{3,2},{4,5},{5,4},{6,7},{7,6},{8,9},{9,8},{10,11... | collective-permute-start | bytes 196616 | tf_op jit(solution)/shard_map/ppermute | solution.py:218
  170.3 4.3 %collective-permute-start.31 = (bf16[4,64,128]{2,1,0:T(8,128)(2,1)S(1)}, bf16[4,64,128]{2,1,0:T(8,128)(2,1)S(1)}, u32[]{:S(2)}, u32[]{:S(2)}) collective-permute-start(bf16[4,64,128]{2,1,0:T(8,128)(2,1)S(1)} %fusion.14), channel_id=1, source_target_pairs={{0,4},{4,0},{8,12},{12,8},{1,5},{5,1},{9,13},{13,9},{2,6},{6,2},{1... | collective-permute-start | bytes 196616 | tf_op jit(solution)/shard_map/ppermute | solution.py:218
  174.6 5.4 %collective-permute-start.32 = (bf16[4,64,128]{2,1,0:T(8,128)(2,1)S(1)}, bf16[4,64,128]{2,1,0:T(8,128)(2,1)S(1)}, u32[]{:S(2)}, u32[]{:S(2)}) collective-permute-start(bf16[4,64,128]{2,1,0:T(8,128)(2,1)S(1)} %add_convert_fusion.1), channel_id=1, source_target_pairs={{0,8},{4,12},{8,0},{12,4},{1,9},{5,13},{9,1},{13,5},{2,10},{6,14},... | collective-permute-start | bytes 196616 | tf_op jit(solution)/shard_map/ppermute | solution.py:218
  180.0 4.3 %collective-permute-start.33 = (bf16[4,64,128]{2,1,0:T(8,128)(2,1)S(1)}, bf16[4,64,128]{2,1,0:T(8,128)(2,1)S(1)}, u32[]{:S(2)}, u32[]{:S(2)}) collective-permute-start(bf16[4,64,128]{2,1,0:T(8,128)(2,1)S(1)} %add_convert_fusion), channel_id=1, source_target_pairs={{0,1},{1,0},{2,3},{3,2},{4,5},{5,4},{6,7},{7,6},{8,9},{9,8},{10,11... | collective-permute-start | bytes 196616 | tf_op jit(solution)/shard_map/ppermute | solution.py:218
  184.4 1.4 collective-permute-start.34
  (4 other events, 37.1 us)

commit v6 on v4

--- a/solution.py
+++ b/solution.py
@@ -12,6 +12,7 @@
 POWER = 4
 LANES = 128
 SUB = 8
+SKETCH_FLOPS = 30_000_000_000
 
 
 shift_ratio = 0.005
@@ -34,6 +35,28 @@
         hashed = scramble(counter * 4 + j + offset)
         total = total + (hashed & 16777215).astype(jnp.float32) * (1.0 / 16777216.0)
     return ((total - 2.0) * 1.7320508).astype(jnp.bfloat16)
+
+
+def sketch_kernel(at_ref, states_ref, out_ref):
+    rank = out_ref.shape[0]
+    width = states_ref.shape[1]
+    step = math.gcd(width, 512)
+    out_ref[...] = jnp.zeros_like(out_ref)
+
+    def body(i, carry):
+        start = pl.multiple_of(i * step, step)
+        feature = lax.broadcasted_iota(jnp.int32, (rank, step), 1) + (at_ref[1] + start)
+        column = lax.broadcasted_iota(jnp.int32, (rank, step), 0)
+        counter = (feature * rank + column) * 4 + at_ref[0]
+        total = jnp.zeros((rank, step), jnp.float32)
+        for j in range(4):
+            hashed = scramble(counter + j)
+            total = total + (hashed & 16777215).astype(jnp.float32) * (1.0 / 16777216.0)
+        omega = ((total - 2.0) * 1.7320508).astype(jnp.bfloat16)
+        out_ref[...] += dot_nt(omega, states_ref[:, pl.ds(start, step)])
+        return carry
+
+    lax.fori_loop(0, width // step, body, 0)
 
 
 def terms_of(value):
@@ -261,31 +284,47 @@
 
     far = list(range(n_row // 2, n_row))
     near = list(range(n_row // 2 - 1, -1, -1))
-    move(states, far[:1])
-
-    col = lax.axis_index("col")
-    feature_index = col * width_local + jnp.arange(width_local, dtype=jnp.int32)
-    omega = sketch_table(sketch_base[0], feature_index, RANK)
-    z = lax.dot_general(
-        omega, states, (((0,), (1,)), ((), ())), preferred_element_type=jnp.float32
-    )
+    rounds = [far[:1] + near[1:], far[1:2] + near[:1]]
+    rounds += [[offset] for offset in far[2:]]
+
+    def after_round(value):
+        if not rounds:
+            return value
+        offsets = rounds.pop(0)
+        move(slab[0], offsets)
+        moved = [pieces[offset] for offset in offsets]
+        value, slab[0], moved = lax.optimization_barrier((value, slab[0], moved))
+        for offset, piece in zip(offsets, moved):
+            pieces[offset] = piece
+        return value
+
+    slab = [states]
+
+    f32 = jnp.float32
+    at_sketch = jnp.stack([scramble(sketch_base[0]), lax.axis_index("col") * width_local])
+    z = call(
+        sketch_kernel,
+        jax.ShapeDtypeStruct((RANK, rows_local), f32),
+        SKETCH_FLOPS,
+        at_sketch.astype(jnp.int32),
+        states,
+    )
+    z = after_round(z)
     for bit in bits(n_col):
         z = z + from_xor(z, ("col",), bit)
     z = z.reshape(RANK, n_col, chunk).transpose(1, 0, 2)
     z_bits = bits(n_z)[::-1]
-    for k, bit in enumerate(z_bits):
+    for bit in z_bits:
+        z = after_round(z)
         z = jnp.concatenate([z, from_xor(z, ("z",), bit)])
-        slab, z = lax.optimization_barrier((states, z))
-        if k == 0:
-            move(slab, far[1:2])
-    move(slab, far[2:] + near)
+    for offsets in rounds:
+        move(slab[0], offsets)
     z = z, from_xor(z, ("core",), 1)
     absolute_col = [("col", bit, False) for bit in bits(n_col)[::-1]]
     at_first = chunk_places([("z", bit, True) for bit in z_bits[::-1]] + absolute_col)
     relative_col = [("col", bit, True) for bit in bits(n_col)]
     at = chunk_places(relative_col + [("z", bit, False) for bit in z_bits])
 
-    f32 = jnp.float32
     square = jax.ShapeDtypeStruct((RANK, RANK), f32)
     wide = jax.ShapeDtypeStruct((RANK, rows_total), jnp.bfloat16)
     orth_flops = 8 * 64 * 64 * rows_total * 6
@@ -295,7 +334,7 @@
         shape = (half, RANK, chunk)
         return jax.ShapeDtypeStruct(shape, f32), jax.ShapeDtypeStruct(shape, dtype)
 
-    basis, upper = call(orth_kernel, (wide, square), orth_flops, at_first, *z)
+    basis, upper = call(orth_kernel, (wide, square), 1, at_first, *z)
     factor = upper.T * (1.0 / math.sqrt(rows_total * width_total))
     dtype = f32
     parts = call(power_kernel, sent_as(dtype), power_flops, at, basis, *pieces)

time: 185 us -> 194 us (1.049)
  waiting for transfers between devices: 102 us -> 115 us
  starting transfers between devices: 37.2 us -> 30.5 us
  matrix products: 3.83 us -> 0 us
  Pallas kernels: 35.6 us -> 39.2 us
  local copies, waits for them, and re-layouts: 4.14 us -> 6.65 us
    ppermute x35, waiting for transfers between devices: 102 us -> 115 us  [from_xor(): return lax.ppermute(value, axis, [(i, i ^ offset) for i in range(size)])]
    ppermute x35, starting transfers between devices: 37.2 us -> 30.5 us  [from_xor(): return lax.ppermute(value, axis, [(i, i ^ offset) for i in range(size)])]
    dot_general x1 -> x0, matrix products: 3.83 us -> none  [per_device_transposed(): lax.dot_general(omega, states, (((0,), (1,)), ((), ())), preferred_elemen...]
    pallas_call x6 -> x7, Pallas kernels: 35.6 us -> 39.2 us  [call(): pl.pallas_call(kernel, out_shape=out_shapes, in_specs=[pl.BlockSpec(memor...]
    dynamic_slice x3 -> x4, local copies, waits for them, and re-layouts: 3.39 us -> 4.29 us  [block(): return lax.dynamic_slice_in_dim(slab, (row ^ offset) * cols, cols, 1)]
  transfers between devices with their start and end apart: 35 -> 35, of which waited for: 29 -> 31; matrix products, arithmetic and copies ran while one was open for 2% -> 1% of each run, Pallas kernels for 3% -> 5%
where the time goes in v6:
time: 194 us
  waiting for transfers between devices  115 us (59%)
  Pallas kernels  39.2 us (20%)
  starting transfers between devices  30.5 us (16%)
  local copies, waits for them, and re-layouts  6.65 us (3%)
    ppermute x35, waiting for transfers between devices, from_xor(): return lax.ppermute(value, axis, [(i, i ^ offset) for i in range(size)])  115 us
    pallas_call x7, Pallas kernels, call(): pl.pallas_call(kernel, out_shape=out_shapes, in_specs=[pl.BlockSpec(memor...  39.2 us
    ppermute x35, starting transfers between devices, from_xor(): return lax.ppermute(value, axis, [(i, i ^ offset) for i in range(size)])  30.5 us
    dynamic_slice x4, local copies, waits for them, and re-layouts, block(): return lax.dynamic_slice_in_dim(slab, (row ^ offset) * cols, cols, 1)  4.29 us
  transfers between devices with their start and end apart: 35, of which 31 were waited for; matrix products, arithmetic and copies ran while one was open for 1% of the time, Pallas kernels for 5%

profile of v6, /device:TPU:0, one launch (start us, length us, event | category | flops | bytes accessed | tf_op | source)
XLA Modules:
  0.0 193.6 jit_solution(733765547270520631)
XLA Ops:
  2.5 2.6 %collective-permute-start.1 = (bf16[256,512]{1,0:T(8,128)(2,1)S(1)}, bf16[256,512]{1,0:T(8,128)(2,1)S(1)}, u32[]{:S(2)}, u32[]{:S(2)}) collective-permute-start(bf16[256,512]{1,0:T(8,128)(2,1)S(1)} %get-tuple-element.56), channel_id=1, source_target_pairs={{0,4},{2,6},{4,0},{6,2},{8,12},{10,14},{12,8},{14,10},{1,5},{3,7},... | collective-permute-start | bytes 786440 | tf_op jit(solution)/shard_map/ppermute | solution.py:231
  5.1 2.6 %collective-permute-start = (bf16[256,512]{1,0:T(8,128)(2,1)S(1)}, bf16[256,512]{1,0:T(8,128)(2,1)S(1)}, u32[]{:S(2)}, u32[]{:S(2)}) collective-permute-start(bf16[256,512]{1,0:T(8,128)(2,1)S(1)} %get-tuple-element.57), channel_id=1, source_target_pairs={{0,8},{2,10},{4,12},{6,14},{8,0},{10,2},{12,4},{14,6},{1,9},{3,11}... | collective-permute-start | bytes 786440 | tf_op jit(solution)/shard_map/ppermute | solution.py:231
  10.0 3.6 %shard_map.41 = f32[64,256]{1,0:T(8,128)S(1)} custom-call(s32[2]{0:T(128)S(1)} %pad_add_fusion.at_ref, bf16[256,4096]{1,0:T(8,128)(2,1)S(1)} %copy-done), custom_call_target="tpu_custom_call" | custom-call | flops 30000001024 | bytes 2097152 | tf_op jit(solution)/shard_map/pallas_call | solution.py:214
  13.7 3.8 %collective-permute-done.1.refs_2_ = bf16[256,512]{1,0:T(8,128)(2,1)S(1)} collective-permute-done((bf16[256,512]{1,0:T(8,128)(2,1)S(1)}, bf16[256,512]{1,0:T(8,128)(2,1)S(1)}, u32[]{:S(2)}, u32[]{:S(2)}) %collective-permute-start.1) | collective-permute-done | bytes 262176 | tf_op jit(solution)/shard_map/ppermute | solution.py:231
  22.7 2.7 %collective-permute-start.4 = (bf16[256,512]{1,0:T(8,128)(2,1)S(1)}, bf16[256,512]{1,0:T(8,128)(2,1)S(1)}, u32[]{:S(2)}, u32[]{:S(2)}) collective-permute-start(bf16[256,512]{1,0:T(8,128)(2,1)S(1)} %get-tuple-element.53), channel_id=1, source_target_pairs={{0,10},{2,8},{4,14},{6,12},{8,2},{10,0},{12,6},{14,4},{1,11},{3,9}... | collective-permute-start | bytes 786440 | tf_op jit(solution)/shard_map/ppermute | solution.py:231
  25.5 9.3 %collective-permute-done.5.refs_3_ = bf16[256,512]{1,0:T(8,128)(2,1)S(1)} collective-permute-done((bf16[256,512]{1,0:T(8,128)(2,1)S(1)}, bf16[256,512]{1,0:T(8,128)(2,1)S(1)}, u32[]{:S(2)}, u32[]{:S(2)}) %collective-permute-start.5) | collective-permute-done | bytes 262176 | tf_op jit(solution)/shard_map/ppermute | solution.py:231
  34.7 2.7 %collective-permute-done.4.refs_5_ = bf16[256,512]{1,0:T(8,128)(2,1)S(1)} collective-permute-done((bf16[256,512]{1,0:T(8,128)(2,1)S(1)}, bf16[256,512]{1,0:T(8,128)(2,1)S(1)}, u32[]{:S(2)}, u32[]{:S(2)}) %collective-permute-start.4) | collective-permute-done | bytes 262176 | tf_op jit(solution)/shard_map/ppermute | solution.py:231
  38.4 2.6 %collective-permute-start.7 = (bf16[256,512]{1,0:T(8,128)(2,1)S(1)}, bf16[256,512]{1,0:T(8,128)(2,1)S(1)}, u32[]{:S(2)}, u32[]{:S(2)}) collective-permute-start(bf16[256,512]{1,0:T(8,128)(2,1)S(1)} %constant_dynamic-slice_fusion.1), channel_id=1, source_target_pairs={{0,12},{2,14},{4,8},{6,10},{8,4},{10,6},{12,0},{14,2},{1,13},{3,15... | collective-permute-start | bytes 786440 | tf_op jit(solution)/shard_map/ppermute | solution.py:231
  41.0 13.4 %collective-permute-done.6 = f32[2,64,128]{2,1,0:T(8,128)S(1)} collective-permute-done((f32[2,64,128]{2,1,0:T(8,128)S(1)}, f32[2,64,128]{2,1,0:T(8,128)S(1)}, u32[]{:S(2)}, u32[]{:S(2)}) %collective-permute-start.6) | collective-permute-done | bytes 65568 | tf_op jit(solution)/shard_map/ppermute | solution.py:231
  54.5 5.0 %collective-permute-done.8 = f32[4,64,128]{2,1,0:T(8,128)S(1)} collective-permute-done((f32[4,64,128]{2,1,0:T(8,128)S(1)}, f32[4,64,128]{2,1,0:T(8,128)S(1)}, u32[]{:S(2)}, u32[]{:S(2)}) %collective-permute-start.8) | collective-permute-done | bytes 131104 | tf_op jit(solution)/shard_map/ppermute | solution.py:231
  63.2 6.3 %shard_map.42 = (bf16[64,2048]{1,0:T(8,128)(2,1)S(1)}, f32[64,64]{1,0:T(8,128)S(1)}) custom-call(s32[16]{0:T(128)S(1)} %fusion.6.at_ref, f32[8,64,128]{2,1,0:T(8,128)S(1)} %constant_dynamic-update-slice_fusion.z_ref, f32[8,64,128]{2,1,0:T(8,128)S(1)} %collective-permute-done.9.other_ref), custom_call_target="tpu_custom_call" | custom-call | flops 1 | bytes 524288 | tf_op jit(solution)/shard_map/pallas_call | solution.py:214
  74.6 5.2 %collective-permute-done.12 = f32[4,64,128]{2,1,0:T(8,128)S(1)} collective-permute-done((f32[4,64,128]{2,1,0:T(8,128)S(1)}, f32[4,64,128]{2,1,0:T(8,128)S(1)}, u32[]{:S(2)}, u32[]{:S(2)}) %collective-permute-start.12) | collective-permute-done | bytes 131104 | tf_op jit(solution)/shard_map/ppermute | solution.py:231
  79.8 4.1 %collective-permute-start.13 = (f32[4,64,128]{2,1,0:T(8,128)S(1)}, f32[4,64,128]{2,1,0:T(8,128)S(1)}, u32[]{:S(2)}, u32[]{:S(2)}) collective-permute-start(f32[4,64,128]{2,1,0:T(8,128)S(1)} %slice_add_fusion.3), channel_id=1, source_target_pairs={{0,4},{4,0},{8,12},{12,8},{1,5},{5,1},{9,13},{13,9},{2,6},{6,2},{1... | collective-permute-start | bytes 393224 | tf_op jit(solution)/shard_map/ppermute | solution.py:231
  83.9 3.2 %collective-permute-done.13 = f32[4,64,128]{2,1,0:T(8,128)S(1)} collective-permute-done((f32[4,64,128]{2,1,0:T(8,128)S(1)}, f32[4,64,128]{2,1,0:T(8,128)S(1)}, u32[]{:S(2)}, u32[]{:S(2)}) %collective-permute-start.13) | collective-permute-done | bytes 131104 | tf_op jit(solution)/shard_map/ppermute | solution.py:231
  89.6 5.7 %collective-permute-done.14 = f32[4,64,128]{2,1,0:T(8,128)S(1)} collective-permute-done((f32[4,64,128]{2,1,0:T(8,128)S(1)}, f32[4,64,128]{2,1,0:T(8,128)S(1)}, u32[]{:S(2)}, u32[]{:S(2)}) %collective-permute-start.14) | collective-permute-done | bytes 131104 | tf_op jit(solution)/shard_map/ppermute | solution.py:231
  95.9 4.4 %collective-permute-done.15 = f32[4,64,128]{2,1,0:T(8,128)S(1)} collective-permute-done((f32[4,64,128]{2,1,0:T(8,128)S(1)}, f32[4,64,128]{2,1,0:T(8,128)S(1)}, u32[]{:S(2)}, u32[]{:S(2)}) %collective-permute-start.15) | collective-permute-done | bytes 131104 | tf_op jit(solution)/shard_map/ppermute | solution.py:231
  102.0 7.3 %shard_map.44 = (f32[8,64,128]{2,1,0:T(8,128)S(1)}, bf16[8,64,128]{2,1,0:T(8,128)(2,1)S(1)}) custom-call(s32[16]{0:T(128)S(1)} %fusion.4.at_ref, f32[8,64,128]{2,1,0:T(8,128)S(1)} %pad_maximum_fusion.z_ref, f32[8,64,128]{2,1,0:T(8,128)S(1)} %collective-permute-done.16.other_ref, bf16[256,512]{1,0:T(8,128)(2,1)S(1)} %get-tuple-element.31.refs_0_, ...), custom_call_target="tpu_custom_call" | custom-call | flops 671088640 | bytes 2621440 | tf_op jit(solution)/shard_map/pallas_call | solution.py:214
  111.3 3.7 %collective-permute-done.18 = bf16[4,64,128]{2,1,0:T(8,128)(2,1)S(1)} collective-permute-done((bf16[4,64,128]{2,1,0:T(8,128)(2,1)S(1)}, bf16[4,64,128]{2,1,0:T(8,128)(2,1)S(1)}, u32[]{:S(2)}, u32[]{:S(2)}) %collective-permute-start.18) | collective-permute-done | bytes 65568 | tf_op jit(solution)/shard_map/ppermute | solution.py:231
  115.1 4.3 %collective-permute-done.19 = bf16[4,64,128]{2,1,0:T(8,128)(2,1)S(1)} collective-permute-done((bf16[4,64,128]{2,1,0:T(8,128)(2,1)S(1)}, bf16[4,64,128]{2,1,0:T(8,128)(2,1)S(1)}, u32[]{:S(2)}, u32[]{:S(2)}) %collective-permute-start.19) | collective-permute-done | bytes 65568 | tf_op jit(solution)/shard_map/ppermute | solution.py:231
  120.1 4.7 %collective-permute-done.20 = bf16[4,64,128]{2,1,0:T(8,128)(2,1)S(1)} collective-permute-done((bf16[4,64,128]{2,1,0:T(8,128)(2,1)S(1)}, bf16[4,64,128]{2,1,0:T(8,128)(2,1)S(1)}, u32[]{:S(2)}, u32[]{:S(2)}) %collective-permute-start.20) | collective-permute-done | bytes 65568 | tf_op jit(solution)/shard_map/ppermute | solution.py:231
  125.4 3.7 %collective-permute-done.21 = bf16[4,64,128]{2,1,0:T(8,128)(2,1)S(1)} collective-permute-done((bf16[4,64,128]{2,1,0:T(8,128)(2,1)S(1)}, bf16[4,64,128]{2,1,0:T(8,128)(2,1)S(1)}, u32[]{:S(2)}, u32[]{:S(2)}) %collective-permute-start.21) | collective-permute-done | bytes 65568 | tf_op jit(solution)/shard_map/ppermute | solution.py:231
  130.6 6.8 %shard_map.45 = (f32[8,64,128]{2,1,0:T(8,128)S(1)}, bf16[8,64,128]{2,1,0:T(8,128)(2,1)S(1)}) custom-call(s32[16]{0:T(128)S(1)} %fusion.4.at_ref, bf16[8,64,128]{2,1,0:T(8,128)(2,1)S(1)} %pad_maximum_fusion.2.z_ref, bf16[8,64,128]{2,1,0:T(8,128)(2,1)S(1)} %collective-permute-done.22.other_ref, bf16[256,512]{1,0:T(8,128)(2,1)S(1)} %get-tuple-element.31.refs_0_, ...), custom_call_target="tpu_custom_call" | custom-call | flops 671088640 | bytes 2359296 | tf_op jit(solution)/shard_map/pallas_call | solution.py:214
  139.5 3.7 %collective-permute-done.24 = bf16[4,64,128]{2,1,0:T(8,128)(2,1)S(1)} collective-permute-done((bf16[4,64,128]{2,1,0:T(8,128)(2,1)S(1)}, bf16[4,64,128]{2,1,0:T(8,128)(2,1)S(1)}, u32[]{:S(2)}, u32[]{:S(2)}) %collective-permute-start.24) | collective-permute-done | bytes 65568 | tf_op jit(solution)/shard_map/ppermute | solution.py:231
  143.3 4.3 %collective-permute-done.25 = bf16[4,64,128]{2,1,0:T(8,128)(2,1)S(1)} collective-permute-done((bf16[4,64,128]{2,1,0:T(8,128)(2,1)S(1)}, bf16[4,64,128]{2,1,0:T(8,128)(2,1)S(1)}, u32[]{:S(2)}, u32[]{:S(2)}) %collective-permute-start.25) | collective-permute-done | bytes 65568 | tf_op jit(solution)/shard_map/ppermute | solution.py:231
  148.3 4.7 %collective-permute-done.26 = bf16[4,64,128]{2,1,0:T(8,128)(2,1)S(1)} collective-permute-done((bf16[4,64,128]{2,1,0:T(8,128)(2,1)S(1)}, bf16[4,64,128]{2,1,0:T(8,128)(2,1)S(1)}, u32[]{:S(2)}, u32[]{:S(2)}) %collective-permute-start.26) | collective-permute-done | bytes 65568 | tf_op jit(solution)/shard_map/ppermute | solution.py:231
  153.6 3.7 %collective-permute-done.27 = bf16[4,64,128]{2,1,0:T(8,128)(2,1)S(1)} collective-permute-done((bf16[4,64,128]{2,1,0:T(8,128)(2,1)S(1)}, bf16[4,64,128]{2,1,0:T(8,128)(2,1)S(1)}, u32[]{:S(2)}, u32[]{:S(2)}) %collective-permute-start.27) | collective-permute-done | bytes 65568 | tf_op jit(solution)/shard_map/ppermute | solution.py:231
  158.7 6.7 %shard_map.46 = (f32[8,64,128]{2,1,0:T(8,128)S(1)}, bf16[8,64,128]{2,1,0:T(8,128)(2,1)S(1)}) custom-call(s32[16]{0:T(128)S(1)} %fusion.4.at_ref, bf16[8,64,128]{2,1,0:T(8,128)(2,1)S(1)} %pad_maximum_fusion.3.z_ref, bf16[8,64,128]{2,1,0:T(8,128)(2,1)S(1)} %collective-permute-done.28.other_ref, bf16[256,512]{1,0:T(8,128)(2,1)S(1)} %get-tuple-element.31.refs_0_, ...), custom_call_target="tpu_custom_call" | custom-call | flops 671088640 | bytes 2359296 | tf_op jit(solution)/shard_map/pallas_call | solution.py:214
  167.5 3.7 %collective-permute-done.30 = bf16[4,64,128]{2,1,0:T(8,128)(2,1)S(1)} collective-permute-done((bf16[4,64,128]{2,1,0:T(8,128)(2,1)S(1)}, bf16[4,64,128]{2,1,0:T(8,128)(2,1)S(1)}, u32[]{:S(2)}, u32[]{:S(2)}) %collective-permute-start.30) | collective-permute-done | bytes 65568 | tf_op jit(solution)/shard_map/ppermute | solution.py:231
  171.3 4.3 %collective-permute-done.31 = bf16[4,64,128]{2,1,0:T(8,128)(2,1)S(1)} collective-permute-done((bf16[4,64,128]{2,1,0:T(8,128)(2,1)S(1)}, bf16[4,64,128]{2,1,0:T(8,128)(2,1)S(1)}, u32[]{:S(2)}, u32[]{:S(2)}) %collective-permute-start.31) | collective-permute-done | bytes 65568 | tf_op jit(solution)/shard_map/ppermute | solution.py:231
  176.3 4.7 %collective-permute-done.32 = bf16[4,64,128]{2,1,0:T(8,128)(2,1)S(1)} collective-permute-done((bf16[4,64,128]{2,1,0:T(8,128)(2,1)S(1)}, bf16[4,64,128]{2,1,0:T(8,128)(2,1)S(1)}, u32[]{:S(2)}, u32[]{:S(2)}) %collective-permute-start.32) | collective-permute-done | bytes 65568 | tf_op jit(solution)/shard_map/ppermute | solution.py:231
  181.6 3.7 %collective-permute-done.33 = bf16[4,64,128]{2,1,0:T(8,128)(2,1)S(1)} collective-permute-done((bf16[4,64,128]{2,1,0:T(8,128)(2,1)S(1)}, bf16[4,64,128]{2,1,0:T(8,128)(2,1)S(1)}, u32[]{:S(2)}, u32[]{:S(2)}) %collective-permute-start.33) | collective-permute-done | bytes 65568 | tf_op jit(solution)/shard_map/ppermute | solution.py:231
  186.8 6.8 %shard_map.47 = f32[64,512]{1,0:T(8,128)} custom-call(s32[16]{0:T(128)S(1)} %fusion.4.at_ref, bf16[8,64,128]{2,1,0:T(8,128)(2,1)S(1)} %pad_maximum_fusion.4.z_ref, bf16[8,64,128]{2,1,0:T(8,128)(2,1)S(1)} %collective-permute-done.34.other_ref, bf16[256,512]{1,0:T(8,128)(2,1)S(1)} %get-tuple-element.31.refs_0_, ...), custom_call_target="tpu_custom_call" | custom-call | flops 671088640 | bytes 2359296 | tf_op jit(solution)/shard_map/pallas_call | solution.py:214
  (84 shorter events, 37.9 us)
Async XLA Ops:
  2.0 11.7 %collective-permute-start.2 = (bf16[256,512]{1,0:T(8,128)(2,1)S(1)}, bf16[256,512]{1,0:T(8,128)(2,1)S(1)}, u32[]{:S(2)}, u32[]{:S(2)}) collective-permute-start(bf16[256,512]{1,0:T(8,128)(2,1)S(1)} %get-tuple-element.55), channel_id=1, source_target_pairs={{0,2},{2,0},{4,6},{6,4},{8,10},{10,8},{12,14},{14,12},{1,3},{3,1},... | collective-permute-start | bytes 786440 | tf_op jit(solution)/shard_map/ppermute | solution.py:231
  2.5 15.1 %collective-permute-start.1 = (bf16[256,512]{1,0:T(8,128)(2,1)S(1)}, bf16[256,512]{1,0:T(8,128)(2,1)S(1)}, u32[]{:S(2)}, u32[]{:S(2)}) collective-permute-start(bf16[256,512]{1,0:T(8,128)(2,1)S(1)} %get-tuple-element.56), channel_id=1, source_target_pairs={{0,4},{2,6},{4,0},{6,2},{8,12},{10,14},{12,8},{14,10},{1,5},{3,7},... | collective-permute-start | bytes 786440 | tf_op jit(solution)/shard_map/ppermute | solution.py:231
  5.1 14.9 %collective-permute-start = (bf16[256,512]{1,0:T(8,128)(2,1)S(1)}, bf16[256,512]{1,0:T(8,128)(2,1)S(1)}, u32[]{:S(2)}, u32[]{:S(2)}) collective-permute-start(bf16[256,512]{1,0:T(8,128)(2,1)S(1)} %get-tuple-element.57), channel_id=1, source_target_pairs={{0,8},{2,10},{4,12},{6,14},{8,0},{10,2},{12,4},{14,6},{1,9},{3,11}... | collective-permute-start | bytes 786440 | tf_op jit(solution)/shard_map/ppermute | solution.py:231
  20.1 5.4 %collective-permute-start.3 = (f32[64,256]{1,0:T(8,128)S(1)}, f32[64,256]{1,0:T(8,128)S(1)}, u32[]{:S(2)}, u32[]{:S(2)}) collective-permute-start(f32[64,256]{1,0:T(8,128)S(1)} %shard_map.41), channel_id=1, source_target_pairs={{0,1},{1,0},{2,3},{3,2},{4,5},{5,4},{6,7},{7,6},{8,9},{9,8},{10,11... | collective-permute-start | bytes 196616 | tf_op jit(solution)/shard_map/ppermute | solution.py:231
  22.6 12.1 %collective-permute-start.5 = (bf16[256,512]{1,0:T(8,128)(2,1)S(1)}, bf16[256,512]{1,0:T(8,128)(2,1)S(1)}, u32[]{:S(2)}, u32[]{:S(2)}) collective-permute-start(bf16[256,512]{1,0:T(8,128)(2,1)S(1)} %get-tuple-element.52), channel_id=1, source_target_pairs={{0,6},{2,4},{4,2},{6,0},{8,14},{10,12},{12,10},{14,8},{1,7},{3,5},... | collective-permute-start | bytes 786440 | tf_op jit(solution)/shard_map/ppermute | solution.py:231
  22.7 14.7 %collective-permute-start.4 = (bf16[256,512]{1,0:T(8,128)(2,1)S(1)}, bf16[256,512]{1,0:T(8,128)(2,1)S(1)}, u32[]{:S(2)}, u32[]{:S(2)}) collective-permute-start(bf16[256,512]{1,0:T(8,128)(2,1)S(1)} %get-tuple-element.53), channel_id=1, source_target_pairs={{0,10},{2,8},{4,14},{6,12},{8,2},{10,0},{12,6},{14,4},{1,11},{3,9}... | collective-permute-start | bytes 786440 | tf_op jit(solution)/shard_map/ppermute | solution.py:231
  38.4 16.0 %collective-permute-start.7 = (bf16[256,512]{1,0:T(8,128)(2,1)S(1)}, bf16[256,512]{1,0:T(8,128)(2,1)S(1)}, u32[]{:S(2)}, u32[]{:S(2)}) collective-permute-start(bf16[256,512]{1,0:T(8,128)(2,1)S(1)} %constant_dynamic-slice_fusion.1), channel_id=1, source_target_pairs={{0,12},{2,14},{4,8},{6,10},{8,4},{10,6},{12,0},{14,2},{1,13},{3,15... | collective-permute-start | bytes 786440 | tf_op jit(solution)/shard_map/ppermute | solution.py:231
  41.0 13.4 %collective-permute-start.6 = (f32[2,64,128]{2,1,0:T(8,128)S(1)}, f32[2,64,128]{2,1,0:T(8,128)S(1)}, u32[]{:S(2)}, u32[]{:S(2)}) collective-permute-start(f32[2,64,128]{2,1,0:T(8,128)S(1)} %bitcast_bitcast_fusion), channel_id=1, source_target_pairs={{0,8},{4,12},{8,0},{12,4},{1,9},{5,13},{9,1},{13,5},{2,10},{6,14},... | collective-permute-start | bytes 196616 | tf_op jit(solution)/shard_map/ppermute | solution.py:231
  54.4 5.2 %collective-permute-start.8 = (f32[4,64,128]{2,1,0:T(8,128)S(1)}, f32[4,64,128]{2,1,0:T(8,128)S(1)}, u32[]{:S(2)}, u32[]{:S(2)}) collective-permute-start(f32[4,64,128]{2,1,0:T(8,128)S(1)} %pad_maximum_fusion.1), channel_id=1, source_target_pairs={{0,4},{4,0},{8,12},{12,8},{1,5},{5,1},{9,13},{13,9},{2,6},{6,2},{1... | collective-permute-start | bytes 393224 | tf_op jit(solution)/shard_map/ppermute | solution.py:231
  59.5 3.6 %collective-permute-start.9 = (f32[8,64,128]{2,1,0:T(8,128)S(1)}, f32[8,64,128]{2,1,0:T(8,128)S(1)}, u32[]{:S(2)}, u32[]{:S(2)}) collective-permute-start(f32[8,64,128]{2,1,0:T(8,128)S(1)} %constant_dynamic-update-slice_fusion.z_ref), channel_id=1, source_target_pairs={{0,2},{2,0},{1,3},{3,1},{4,6},{6,4},{5,7},{7,5},{8,10},{10,8},{9,1... | collective-permute-start | bytes 786440 | tf_op jit(solution)/shard_map/ppermute | solution.py:231
  60.6 10.0 %collective-permute-start.10 = (bf16[256,512]{1,0:T(8,128)(2,1)S(1)}, bf16[256,512]{1,0:T(8,128)(2,1)S(1)}, u32[]{:S(2)}, u32[]{:S(2)}) collective-permute-start(bf16[256,512]{1,0:T(8,128)(2,1)S(1)} %constant_dynamic-slice_fusion), channel_id=1, source_target_pairs={{0,14},{2,12},{4,10},{6,8},{8,6},{10,4},{12,2},{14,0},{1,15},{3,13... | collective-permute-start | bytes 786440 | tf_op jit(solution)/shard_map/ppermute | solution.py:231
  72.3 1.7 collective-permute-start.11
  74.0 5.8 %collective-permute-start.12 = (f32[4,64,128]{2,1,0:T(8,128)S(1)}, f32[4,64,128]{2,1,0:T(8,128)S(1)}, u32[]{:S(2)}, u32[]{:S(2)}) collective-permute-start(f32[4,64,128]{2,1,0:T(8,128)S(1)} %slice.36), channel_id=1, source_target_pairs={{0,1},{1,0},{2,3},{3,2},{4,5},{5,4},{6,7},{7,6},{8,9},{9,8},{10,11... | collective-permute-start | bytes 393224 | tf_op jit(solution)/shard_map/ppermute | solution.py:231
  79.8 7.3 %collective-permute-start.13 = (f32[4,64,128]{2,1,0:T(8,128)S(1)}, f32[4,64,128]{2,1,0:T(8,128)S(1)}, u32[]{:S(2)}, u32[]{:S(2)}) collective-permute-start(f32[4,64,128]{2,1,0:T(8,128)S(1)} %slice_add_fusion.3), channel_id=1, source_target_pairs={{0,4},{4,0},{8,12},{12,8},{1,5},{5,1},{9,13},{13,9},{2,6},{6,2},{1... | collective-permute-start | bytes 393224 | tf_op jit(solution)/shard_map/ppermute | solution.py:231
  87.1 8.1 %collective-permute-start.14 = (f32[4,64,128]{2,1,0:T(8,128)S(1)}, f32[4,64,128]{2,1,0:T(8,128)S(1)}, u32[]{:S(2)}, u32[]{:S(2)}) collective-permute-start(f32[4,64,128]{2,1,0:T(8,128)S(1)} %add.154), channel_id=1, source_target_pairs={{0,8},{4,12},{8,0},{12,4},{1,9},{5,13},{9,1},{13,5},{2,10},{6,14},... | collective-permute-start | bytes 393224 | tf_op jit(solution)/shard_map/ppermute | solution.py:231
  95.3 5.0 %collective-permute-start.15 = (f32[4,64,128]{2,1,0:T(8,128)S(1)}, f32[4,64,128]{2,1,0:T(8,128)S(1)}, u32[]{:S(2)}, u32[]{:S(2)}) collective-permute-start(f32[4,64,128]{2,1,0:T(8,128)S(1)} %add.155), channel_id=1, source_target_pairs={{0,1},{1,0},{2,3},{3,2},{4,5},{5,4},{6,7},{7,6},{8,9},{9,8},{10,11... | collective-permute-start | bytes 393224 | tf_op jit(solution)/shard_map/ppermute | solution.py:231
  100.4 1.6 collective-permute-start.16
  109.2 1.4 collective-permute-start.17
  110.7 4.3 %collective-permute-start.18 = (bf16[4,64,128]{2,1,0:T(8,128)(2,1)S(1)}, bf16[4,64,128]{2,1,0:T(8,128)(2,1)S(1)}, u32[]{:S(2)}, u32[]{:S(2)}) collective-permute-start(bf16[4,64,128]{2,1,0:T(8,128)(2,1)S(1)} %slice.58), channel_id=1, source_target_pairs={{0,1},{1,0},{2,3},{3,2},{4,5},{5,4},{6,7},{7,6},{8,9},{9,8},{10,11... | collective-permute-start | bytes 196616 | tf_op jit(solution)/shard_map/ppermute | solution.py:231
  115.0 4.3 %collective-permute-start.19 = (bf16[4,64,128]{2,1,0:T(8,128)(2,1)S(1)}, bf16[4,64,128]{2,1,0:T(8,128)(2,1)S(1)}, u32[]{:S(2)}, u32[]{:S(2)}) collective-permute-start(bf16[4,64,128]{2,1,0:T(8,128)(2,1)S(1)} %fusion.2), channel_id=1, source_target_pairs={{0,4},{4,0},{8,12},{12,8},{1,5},{5,1},{9,13},{13,9},{2,6},{6,2},{1... | collective-permute-start | bytes 196616 | tf_op jit(solution)/shard_map/ppermute | solution.py:231
  119.4 5.4 %collective-permute-start.20 = (bf16[4,64,128]{2,1,0:T(8,128)(2,1)S(1)}, bf16[4,64,128]{2,1,0:T(8,128)(2,1)S(1)}, u32[]{:S(2)}, u32[]{:S(2)}) collective-permute-start(bf16[4,64,128]{2,1,0:T(8,128)(2,1)S(1)} %add_convert_fusion.5), channel_id=1, source_target_pairs={{0,8},{4,12},{8,0},{12,4},{1,9},{5,13},{9,1},{13,5},{2,10},{6,14},... | collective-permute-start | bytes 196616 | tf_op jit(solution)/shard_map/ppermute | solution.py:231
  124.8 4.3 %collective-permute-start.21 = (bf16[4,64,128]{2,1,0:T(8,128)(2,1)S(1)}, bf16[4,64,128]{2,1,0:T(8,128)(2,1)S(1)}, u32[]{:S(2)}, u32[]{:S(2)}) collective-permute-start(bf16[4,64,128]{2,1,0:T(8,128)(2,1)S(1)} %add_convert_fusion.4), channel_id=1, source_target_pairs={{0,1},{1,0},{2,3},{3,2},{4,5},{5,4},{6,7},{7,6},{8,9},{9,8},{10,11... | collective-permute-start | bytes 196616 | tf_op jit(solution)/shard_map/ppermute | solution.py:231
  129.1 1.4 collective-permute-start.22
  137.4 1.4 collective-permute-start.23
  138.8 4.3 %collective-permute-start.24 = (bf16[4,64,128]{2,1,0:T(8,128)(2,1)S(1)}, bf16[4,64,128]{2,1,0:T(8,128)(2,1)S(1)}, u32[]{:S(2)}, u32[]{:S(2)}) collective-permute-start(bf16[4,64,128]{2,1,0:T(8,128)(2,1)S(1)} %slice.57), channel_id=1, source_target_pairs={{0,1},{1,0},{2,3},{3,2},{4,5},{5,4},{6,7},{7,6},{8,9},{9,8},{10,11... | collective-permute-start | bytes 196616 | tf_op jit(solution)/shard_map/ppermute | solution.py:231
  143.2 4.3 %collective-permute-start.25 = (bf16[4,64,128]{2,1,0:T(8,128)(2,1)S(1)}, bf16[4,64,128]{2,1,0:T(8,128)(2,1)S(1)}, u32[]{:S(2)}, u32[]{:S(2)}) collective-permute-start(bf16[4,64,128]{2,1,0:T(8,128)(2,1)S(1)} %fusion.1), channel_id=1, source_target_pairs={{0,4},{4,0},{8,12},{12,8},{1,5},{5,1},{9,13},{13,9},{2,6},{6,2},{1... | collective-permute-start | bytes 196616 | tf_op jit(solution)/shard_map/ppermute | solution.py:231
  147.6 5.4 %collective-permute-start.26 = (bf16[4,64,128]{2,1,0:T(8,128)(2,1)S(1)}, bf16[4,64,128]{2,1,0:T(8,128)(2,1)S(1)}, u32[]{:S(2)}, u32[]{:S(2)}) collective-permute-start(bf16[4,64,128]{2,1,0:T(8,128)(2,1)S(1)} %add_convert_fusion.3), channel_id=1, source_target_pairs={{0,8},{4,12},{8,0},{12,4},{1,9},{5,13},{9,1},{13,5},{2,10},{6,14},... | collective-permute-start | bytes 196616 | tf_op jit(solution)/shard_map/ppermute | solution.py:231
  153.0 4.3 %collective-permute-start.27 = (bf16[4,64,128]{2,1,0:T(8,128)(2,1)S(1)}, bf16[4,64,128]{2,1,0:T(8,128)(2,1)S(1)}, u32[]{:S(2)}, u32[]{:S(2)}) collective-permute-start(bf16[4,64,128]{2,1,0:T(8,128)(2,1)S(1)} %add_convert_fusion.2), channel_id=1, source_target_pairs={{0,1},{1,0},{2,3},{3,2},{4,5},{5,4},{6,7},{7,6},{8,9},{9,8},{10,11... | collective-permute-start | bytes 196616 | tf_op jit(solution)/shard_map/ppermute | solution.py:231
  166.9 4.3 %collective-permute-start.30 = (bf16[4,64,128]{2,1,0:T(8,128)(2,1)S(1)}, bf16[4,64,128]{2,1,0:T(8,128)(2,1)S(1)}, u32[]{:S(2)}, u32[]{:S(2)}) collective-permute-start(bf16[4,64,128]{2,1,0:T(8,128)(2,1)S(1)} %slice.56), channel_id=1, source_target_pairs={{0,1},{1,0},{2,3},{3,2},{4,5},{5,4},{6,7},{7,6},{8,9},{9,8},{10,11... | collective-permute-start | bytes 196616 | tf_op jit(solution)/shard_map/ppermute | solution.py:231
  171.3 4.3 %collective-permute-start.31 = (bf16[4,64,128]{2,1,0:T(8,128)(2,1)S(1)}, bf16[4,64,128]{2,1,0:T(8,128)(2,1)S(1)}, u32[]{:S(2)}, u32[]{:S(2)}) collective-permute-start(bf16[4,64,128]{2,1,0:T(8,128)(2,1)S(1)} %fusion), channel_id=1, source_target_pairs={{0,4},{4,0},{8,12},{12,8},{1,5},{5,1},{9,13},{13,9},{2,6},{6,2},{1... | collective-permute-start | bytes 196616 | tf_op jit(solution)/shard_map/ppermute | solution.py:231
  175.6 5.4 %collective-permute-start.32 = (bf16[4,64,128]{2,1,0:T(8,128)(2,1)S(1)}, bf16[4,64,128]{2,1,0:T(8,128)(2,1)S(1)}, u32[]{:S(2)}, u32[]{:S(2)}) collective-permute-start(bf16[4,64,128]{2,1,0:T(8,128)(2,1)S(1)} %add_convert_fusion.1), channel_id=1, source_target_pairs={{0,8},{4,12},{8,0},{12,4},{1,9},{5,13},{9,1},{13,5},{2,10},{6,14},... | collective-permute-start | bytes 196616 | tf_op jit(solution)/shard_map/ppermute | solution.py:231
  181.0 4.3 %collective-permute-start.33 = (bf16[4,64,128]{2,1,0:T(8,128)(2,1)S(1)}, bf16[4,64,128]{2,1,0:T(8,128)(2,1)S(1)}, u32[]{:S(2)}, u32[]{:S(2)}) collective-permute-start(bf16[4,64,128]{2,1,0:T(8,128)(2,1)S(1)} %add_convert_fusion), channel_id=1, source_target_pairs={{0,1},{1,0},{2,3},{3,2},{4,5},{5,4},{6,7},{7,6},{8,9},{9,8},{10,11... | collective-permute-start | bytes 196616 | tf_op jit(solution)/shard_map/ppermute | solution.py:231
  (4 other events, 5.8 us)

commit v7 on v4

--- a/solution.py
+++ b/solution.py
@@ -101,7 +101,8 @@
         pivots = jnp.zeros((SUB, 2 * size), jnp.float32)
         for k in range(SUB):
             pivot = jnp.broadcast_to(columns[k][b][k : k + 1, :], (SUB, 2 * size))
-            reciprocal = 1.0 / pivot
+            reciprocal = pl.reciprocal(pivot, approx=True)
+            reciprocal = reciprocal * (2.0 - pivot * reciprocal)
             pivots = jnp.where(row_index == k, pivot, pivots)
             work_row = jnp.broadcast_to(work[b][k : k + 1, :], (SUB, 2 * size))
             later = [
@@ -261,7 +262,6 @@
 
     far = list(range(n_row // 2, n_row))
     near = list(range(n_row // 2 - 1, -1, -1))
-    move(states, far[:1])
 
     col = lax.axis_index("col")
     feature_index = col * width_local + jnp.arange(width_local, dtype=jnp.int32)
@@ -275,11 +275,14 @@
     z_bits = bits(n_z)[::-1]
     for k, bit in enumerate(z_bits):
         z = jnp.concatenate([z, from_xor(z, ("z",), bit)])
-        slab, z = lax.optimization_barrier((states, z))
         if k == 0:
-            move(slab, far[1:2])
-    move(slab, far[2:] + near)
+            z, slab = lax.optimization_barrier((z, states))
+            move(slab, far + near)
     z = z, from_xor(z, ("core",), 1)
+    held = far[:1] + near[:1]
+    z, moved = lax.optimization_barrier((z, [pieces[offset] for offset in held]))
+    for offset, piece in zip(held, moved):
+        pieces[offset] = piece
     absolute_col = [("col", bit, False) for bit in bits(n_col)[::-1]]
     at_first = chunk_places([("z", bit, True) for bit in z_bits[::-1]] + absolute_col)
     relative_col = [("col", bit, True) for bit in bits(n_col)]

time: 185 us -> 191 us (1.032)
  starting transfers between devices: 37.2 us -> 56.9 us
  waiting for transfers between devices: 102 us -> 87.6 us
  Pallas kernels: 35.6 us -> 39 us
  local copies, waits for them, and re-layouts: 4.14 us -> 1.01 us
    ppermute x35, starting transfers between devices: 37.2 us -> 56.9 us  [from_xor(): return lax.ppermute(value, axis, [(i, i ^ offset) for i in range(size)])]
    ppermute x35, waiting for transfers between devices: 102 us -> 87.6 us  [from_xor(): return lax.ppermute(value, axis, [(i, i ^ offset) for i in range(size)])]
    pallas_call x6, Pallas kernels: 35.6 us -> 39 us  [call(): pl.pallas_call(kernel, out_shape=out_shapes, in_specs=[pl.BlockSpec(memor...]
    dynamic_slice x3 -> x1, local copies, waits for them, and re-layouts: 3.39 us -> 0.24 us  [block(): return lax.dynamic_slice_in_dim(slab, (row ^ offset) * cols, cols, 1)]
  transfers between devices with their start and end apart: 35 -> 35, of which waited for: 29 -> 29; matrix products, arithmetic and copies ran while one was open for 2% -> 1% of each run, Pallas kernels for 3% -> 4%
where the time goes in v7:
time: 191 us
  waiting for transfers between devices  87.6 us (46%)
  starting transfers between devices  56.9 us (30%)
  Pallas kernels  39 us (20%)
  matrix products  3.97 us (2%)
    ppermute x35, waiting for transfers between devices, from_xor(): return lax.ppermute(value, axis, [(i, i ^ offset) for i in range(size)])  87.6 us
    ppermute x35, starting transfers between devices, from_xor(): return lax.ppermute(value, axis, [(i, i ^ offset) for i in range(size)])  56.9 us
    pallas_call x6, Pallas kernels, call(): pl.pallas_call(kernel, out_shape=out_shapes, in_specs=[pl.BlockSpec(memor...  39 us
    dot_general x1, matrix products, per_device_transposed(): lax.dot_general(omega, states, (((0,), (1,)), ((), ())), preferred_elemen...  3.97 us
  transfers between devices with their start and end apart: 35, of which 29 were waited for; matrix products, arithmetic and copies ran while one was open for 1% of the time, Pallas kernels for 4%

profile of v7, /device:TPU:0, one launch (start us, length us, event | category | flops | bytes accessed | tf_op | source)
XLA Modules:
  0.0 190.6 jit_solution(10268182846264610063)
XLA Ops:
  1.3 4.0 %fusion = f32[64,256]{1,0:T(8,128)S(1)} fusion(bf16[256,4096]{1,0:T(8,128)(2,1)} %param.3, s32[]{:T(128)S(6)} %xor.84, s32[4096]{0:T(1024)S(1)} %add_multiply_fusion), kind=kOutput, calls=%fused_computation.1 | convolution fusion | flops 152043520 | bytes 2179076 | tf_op jit(solution)/shard_map/dot_general | solution.py:269
  5.3 3.0 %collective-permute-start = (f32[64,256]{1,0:T(8,128)S(1)}, f32[64,256]{1,0:T(8,128)S(1)}, u32[]{:S(2)}, u32[]{:S(2)}) collective-permute-start(f32[64,256]{1,0:T(8,128)S(1)} %fusion), channel_id=1, source_target_pairs={{0,1},{1,0},{2,3},{3,2},{4,5},{5,4},{6,7},{7,6},{8,9},{9,8},{10,11... | collective-permute-start | bytes 196616 | tf_op jit(solution)/shard_map/ppermute | solution.py:209
  8.3 2.2 %collective-permute-done = f32[64,256]{1,0:T(8,128)S(1)} collective-permute-done((f32[64,256]{1,0:T(8,128)S(1)}, f32[64,256]{1,0:T(8,128)S(1)}, u32[]{:S(2)}, u32[]{:S(2)}) %collective-permute-start) | collective-permute-done | bytes 65568 | tf_op jit(solution)/shard_map/ppermute | solution.py:209
  10.5 3.2 %collective-permute-start.1 = (f32[2,64,128]{2,1,0:T(8,128)S(1)}, f32[2,64,128]{2,1,0:T(8,128)S(1)}, u32[]{:S(2)}, u32[]{:S(2)}) collective-permute-start(f32[2,64,128]{2,1,0:T(8,128)S(1)} %bitcast_bitcast_fusion), channel_id=1, source_target_pairs={{0,8},{4,12},{8,0},{12,4},{1,9},{5,13},{9,1},{13,5},{2,10},{6,14},... | collective-permute-start | bytes 196616 | tf_op jit(solution)/shard_map/ppermute | solution.py:209
  13.7 2.2 %collective-permute-done.1 = f32[2,64,128]{2,1,0:T(8,128)S(1)} collective-permute-done((f32[2,64,128]{2,1,0:T(8,128)S(1)}, f32[2,64,128]{2,1,0:T(8,128)S(1)}, u32[]{:S(2)}, u32[]{:S(2)}) %collective-permute-start.1) | collective-permute-done | bytes 65568 | tf_op jit(solution)/shard_map/ppermute | solution.py:209
  16.0 2.0 %collective-permute-start.2 = (f32[4,64,128]{2,1,0:T(8,128)S(1)}, f32[4,64,128]{2,1,0:T(8,128)S(1)}, u32[]{:S(2)}, u32[]{:S(2)}) collective-permute-start(f32[4,64,128]{2,1,0:T(8,128)S(1)} %pad_maximum_fusion.1), channel_id=1, source_target_pairs={{0,4},{4,0},{8,12},{12,8},{1,5},{5,1},{9,13},{13,9},{2,6},{6,2},{1... | collective-permute-start | bytes 393224 | tf_op jit(solution)/shard_map/ppermute | solution.py:209
  18.3 3.2 %collective-permute-start.4 = (bf16[256,512]{1,0:T(8,128)(2,1)S(1)}, bf16[256,512]{1,0:T(8,128)(2,1)S(1)}, u32[]{:S(2)}, u32[]{:S(2)}) collective-permute-start(bf16[256,512]{1,0:T(8,128)(2,1)S(1)} %get-tuple-element.47), channel_id=1, source_target_pairs={{0,8},{2,10},{4,12},{6,14},{8,0},{10,2},{12,4},{14,6},{1,9},{3,11}... | collective-permute-start | bytes 786440 | tf_op jit(solution)/shard_map/ppermute | solution.py:209
  21.9 9.8 %collective-permute-start.10 = (bf16[256,512]{1,0:T(8,128)(2,1)S(1)}, bf16[256,512]{1,0:T(8,128)(2,1)S(1)}, u32[]{:S(2)}, u32[]{:S(2)}) collective-permute-start(bf16[256,512]{1,0:T(8,128)(2,1)S(1)} %get-tuple-element.40), channel_id=1, source_target_pairs={{0,14},{2,12},{4,10},{6,8},{8,6},{10,4},{12,2},{14,0},{1,15},{3,13... | collective-permute-start | bytes 786440 | tf_op jit(solution)/shard_map/ppermute | solution.py:209
  32.3 3.5 %collective-permute-start.7 = (bf16[256,512]{1,0:T(8,128)(2,1)S(1)}, bf16[256,512]{1,0:T(8,128)(2,1)S(1)}, u32[]{:S(2)}, u32[]{:S(2)}) collective-permute-start(bf16[256,512]{1,0:T(8,128)(2,1)S(1)} %get-tuple-element.43), channel_id=1, source_target_pairs={{0,4},{2,6},{4,0},{6,2},{8,12},{10,14},{12,8},{14,10},{1,5},{3,7},... | collective-permute-start | bytes 786440 | tf_op jit(solution)/shard_map/ppermute | solution.py:209
  35.7 15.7 %collective-permute-start.6 = (bf16[256,512]{1,0:T(8,128)(2,1)S(1)}, bf16[256,512]{1,0:T(8,128)(2,1)S(1)}, u32[]{:S(2)}, u32[]{:S(2)}) collective-permute-start(bf16[256,512]{1,0:T(8,128)(2,1)S(1)} %get-tuple-element.44), channel_id=1, source_target_pairs={{0,2},{2,0},{4,6},{6,4},{8,10},{10,8},{12,14},{14,12},{1,3},{3,1},... | collective-permute-start | bytes 786440 | tf_op jit(solution)/shard_map/ppermute | solution.py:209
  51.5 6.9 %shard_map.41 = (bf16[64,2048]{1,0:T(8,128)(2,1)S(1)}, f32[64,64]{1,0:T(8,128)S(1)}) custom-call(s32[16]{0:T(128)S(1)} %fusion.20.at_ref, f32[8,64,128]{2,1,0:T(8,128)S(1)} %constant_dynamic-update-slice_fusion.z_ref, f32[8,64,128]{2,1,0:T(8,128)S(1)} %collective-permute-done.3.other_ref), custom_call_target="tpu_custom_call" | custom-call | flops 402653184 | bytes 524288 | tf_op jit(solution)/shard_map/pallas_call | solution.py:192
  58.4 10.0 %collective-permute-done.8.refs_5_ = bf16[256,512]{1,0:T(8,128)(2,1)S(1)} collective-permute-done((bf16[256,512]{1,0:T(8,128)(2,1)S(1)}, bf16[256,512]{1,0:T(8,128)(2,1)S(1)}, u32[]{:S(2)}, u32[]{:S(2)}) %collective-permute-start.8) | collective-permute-done | bytes 262176 | tf_op jit(solution)/shard_map/ppermute | solution.py:209
  73.3 4.1 %collective-permute-done.12 = f32[4,64,128]{2,1,0:T(8,128)S(1)} collective-permute-done((f32[4,64,128]{2,1,0:T(8,128)S(1)}, f32[4,64,128]{2,1,0:T(8,128)S(1)}, u32[]{:S(2)}, u32[]{:S(2)}) %collective-permute-start.12) | collective-permute-done | bytes 131104 | tf_op jit(solution)/shard_map/ppermute | solution.py:209
  77.5 5.0 %collective-permute-done.13 = f32[4,64,128]{2,1,0:T(8,128)S(1)} collective-permute-done((f32[4,64,128]{2,1,0:T(8,128)S(1)}, f32[4,64,128]{2,1,0:T(8,128)S(1)}, u32[]{:S(2)}, u32[]{:S(2)}) %collective-permute-start.13) | collective-permute-done | bytes 131104 | tf_op jit(solution)/shard_map/ppermute | solution.py:209
  83.2 6.4 %collective-permute-done.14 = f32[4,64,128]{2,1,0:T(8,128)S(1)} collective-permute-done((f32[4,64,128]{2,1,0:T(8,128)S(1)}, f32[4,64,128]{2,1,0:T(8,128)S(1)}, u32[]{:S(2)}, u32[]{:S(2)}) %collective-permute-start.14) | collective-permute-done | bytes 131104 | tf_op jit(solution)/shard_map/ppermute | solution.py:209
  91.1 3.5 %collective-permute-done.15 = f32[4,64,128]{2,1,0:T(8,128)S(1)} collective-permute-done((f32[4,64,128]{2,1,0:T(8,128)S(1)}, f32[4,64,128]{2,1,0:T(8,128)S(1)}, u32[]{:S(2)}, u32[]{:S(2)}) %collective-permute-start.15) | collective-permute-done | bytes 131104 | tf_op jit(solution)/shard_map/ppermute | solution.py:209
  96.2 8.1 %shard_map.43 = (f32[8,64,128]{2,1,0:T(8,128)S(1)}, bf16[8,64,128]{2,1,0:T(8,128)(2,1)S(1)}) custom-call(s32[16]{0:T(128)S(1)} %fusion.18.at_ref, f32[8,64,128]{2,1,0:T(8,128)S(1)} %pad_maximum_fusion.z_ref, f32[8,64,128]{2,1,0:T(8,128)S(1)} %collective-permute-done.16.other_ref, bf16[256,512]{1,0:T(8,128)(2,1)S(1)} %get-tuple-element.45.refs_0_, ...), custom_call_target="tpu_custom_call" | custom-call | flops 671088640 | bytes 2621440 | tf_op jit(solution)/shard_map/pallas_call | solution.py:192
  107.3 2.8 %collective-permute-done.18 = bf16[4,64,128]{2,1,0:T(8,128)(2,1)S(1)} collective-permute-done((bf16[4,64,128]{2,1,0:T(8,128)(2,1)S(1)}, bf16[4,64,128]{2,1,0:T(8,128)(2,1)S(1)}, u32[]{:S(2)}, u32[]{:S(2)}) %collective-permute-start.18) | collective-permute-done | bytes 65568 | tf_op jit(solution)/shard_map/ppermute | solution.py:209
  110.2 4.3 %collective-permute-done.19 = bf16[4,64,128]{2,1,0:T(8,128)(2,1)S(1)} collective-permute-done((bf16[4,64,128]{2,1,0:T(8,128)(2,1)S(1)}, bf16[4,64,128]{2,1,0:T(8,128)(2,1)S(1)}, u32[]{:S(2)}, u32[]{:S(2)}) %collective-permute-start.19) | collective-permute-done | bytes 65568 | tf_op jit(solution)/shard_map/ppermute | solution.py:209
  115.1 4.7 %collective-permute-done.20 = bf16[4,64,128]{2,1,0:T(8,128)(2,1)S(1)} collective-permute-done((bf16[4,64,128]{2,1,0:T(8,128)(2,1)S(1)}, bf16[4,64,128]{2,1,0:T(8,128)(2,1)S(1)}, u32[]{:S(2)}, u32[]{:S(2)}) %collective-permute-start.20) | collective-permute-done | bytes 65568 | tf_op jit(solution)/shard_map/ppermute | solution.py:209
  121.4 2.8 %collective-permute-done.21 = bf16[4,64,128]{2,1,0:T(8,128)(2,1)S(1)} collective-permute-done((bf16[4,64,128]{2,1,0:T(8,128)(2,1)S(1)}, bf16[4,64,128]{2,1,0:T(8,128)(2,1)S(1)}, u32[]{:S(2)}, u32[]{:S(2)}) %collective-permute-start.21) | collective-permute-done | bytes 65568 | tf_op jit(solution)/shard_map/ppermute | solution.py:209
  125.6 7.4 %shard_map.44 = (f32[8,64,128]{2,1,0:T(8,128)S(1)}, bf16[8,64,128]{2,1,0:T(8,128)(2,1)S(1)}) custom-call(s32[16]{0:T(128)S(1)} %fusion.18.at_ref, bf16[8,64,128]{2,1,0:T(8,128)(2,1)S(1)} %pad_maximum_fusion.2.z_ref, bf16[8,64,128]{2,1,0:T(8,128)(2,1)S(1)} %collective-permute-done.22.other_ref, bf16[256,512]{1,0:T(8,128)(2,1)S(1)} %get-tuple-element.45.refs_0_, ...), custom_call_target="tpu_custom_call" | custom-call | flops 671088640 | bytes 2359296 | tf_op jit(solution)/shard_map/pallas_call | solution.py:192
  136.1 2.8 %collective-permute-done.24 = bf16[4,64,128]{2,1,0:T(8,128)(2,1)S(1)} collective-permute-done((bf16[4,64,128]{2,1,0:T(8,128)(2,1)S(1)}, bf16[4,64,128]{2,1,0:T(8,128)(2,1)S(1)}, u32[]{:S(2)}, u32[]{:S(2)}) %collective-permute-start.24) | collective-permute-done | bytes 65568 | tf_op jit(solution)/shard_map/ppermute | solution.py:209
  138.9 4.3 %collective-permute-done.25 = bf16[4,64,128]{2,1,0:T(8,128)(2,1)S(1)} collective-permute-done((bf16[4,64,128]{2,1,0:T(8,128)(2,1)S(1)}, bf16[4,64,128]{2,1,0:T(8,128)(2,1)S(1)}, u32[]{:S(2)}, u32[]{:S(2)}) %collective-permute-start.25) | collective-permute-done | bytes 65568 | tf_op jit(solution)/shard_map/ppermute | solution.py:209
  143.9 4.7 %collective-permute-done.26 = bf16[4,64,128]{2,1,0:T(8,128)(2,1)S(1)} collective-permute-done((bf16[4,64,128]{2,1,0:T(8,128)(2,1)S(1)}, bf16[4,64,128]{2,1,0:T(8,128)(2,1)S(1)}, u32[]{:S(2)}, u32[]{:S(2)}) %collective-permute-start.26) | collective-permute-done | bytes 65568 | tf_op jit(solution)/shard_map/ppermute | solution.py:209
  150.2 2.8 %collective-permute-done.27 = bf16[4,64,128]{2,1,0:T(8,128)(2,1)S(1)} collective-permute-done((bf16[4,64,128]{2,1,0:T(8,128)(2,1)S(1)}, bf16[4,64,128]{2,1,0:T(8,128)(2,1)S(1)}, u32[]{:S(2)}, u32[]{:S(2)}) %collective-permute-start.27) | collective-permute-done | bytes 65568 | tf_op jit(solution)/shard_map/ppermute | solution.py:209
  154.4 7.4 %shard_map.45 = (f32[8,64,128]{2,1,0:T(8,128)S(1)}, bf16[8,64,128]{2,1,0:T(8,128)(2,1)S(1)}) custom-call(s32[16]{0:T(128)S(1)} %fusion.18.at_ref, bf16[8,64,128]{2,1,0:T(8,128)(2,1)S(1)} %pad_maximum_fusion.3.z_ref, bf16[8,64,128]{2,1,0:T(8,128)(2,1)S(1)} %collective-permute-done.28.other_ref, bf16[256,512]{1,0:T(8,128)(2,1)S(1)} %get-tuple-element.45.refs_0_, ...), custom_call_target="tpu_custom_call" | custom-call | flops 671088640 | bytes 2359296 | tf_op jit(solution)/shard_map/pallas_call | solution.py:192
  164.8 2.8 %collective-permute-done.30 = bf16[4,64,128]{2,1,0:T(8,128)(2,1)S(1)} collective-permute-done((bf16[4,64,128]{2,1,0:T(8,128)(2,1)S(1)}, bf16[4,64,128]{2,1,0:T(8,128)(2,1)S(1)}, u32[]{:S(2)}, u32[]{:S(2)}) %collective-permute-start.30) | collective-permute-done | bytes 65568 | tf_op jit(solution)/shard_map/ppermute | solution.py:209
  167.7 4.3 %collective-permute-done.31 = bf16[4,64,128]{2,1,0:T(8,128)(2,1)S(1)} collective-permute-done((bf16[4,64,128]{2,1,0:T(8,128)(2,1)S(1)}, bf16[4,64,128]{2,1,0:T(8,128)(2,1)S(1)}, u32[]{:S(2)}, u32[]{:S(2)}) %collective-permute-start.31) | collective-permute-done | bytes 65568 | tf_op jit(solution)/shard_map/ppermute | solution.py:209
  172.6 4.7 %collective-permute-done.32 = bf16[4,64,128]{2,1,0:T(8,128)(2,1)S(1)} collective-permute-done((bf16[4,64,128]{2,1,0:T(8,128)(2,1)S(1)}, bf16[4,64,128]{2,1,0:T(8,128)(2,1)S(1)}, u32[]{:S(2)}, u32[]{:S(2)}) %collective-permute-start.32) | collective-permute-done | bytes 65568 | tf_op jit(solution)/shard_map/ppermute | solution.py:209
  178.9 2.8 %collective-permute-done.33 = bf16[4,64,128]{2,1,0:T(8,128)(2,1)S(1)} collective-permute-done((bf16[4,64,128]{2,1,0:T(8,128)(2,1)S(1)}, bf16[4,64,128]{2,1,0:T(8,128)(2,1)S(1)}, u32[]{:S(2)}, u32[]{:S(2)}) %collective-permute-start.33) | collective-permute-done | bytes 65568 | tf_op jit(solution)/shard_map/ppermute | solution.py:209
  183.1 7.5 %shard_map.46 = f32[64,512]{1,0:T(8,128)} custom-call(s32[16]{0:T(128)S(1)} %fusion.18.at_ref, bf16[8,64,128]{2,1,0:T(8,128)(2,1)S(1)} %pad_maximum_fusion.4.z_ref, bf16[8,64,128]{2,1,0:T(8,128)(2,1)S(1)} %collective-permute-done.34.other_ref, bf16[256,512]{1,0:T(8,128)(2,1)S(1)} %get-tuple-element.45.refs_0_, ...), custom_call_target="tpu_custom_call" | custom-call | flops 671088640 | bytes 2359296 | tf_op jit(solution)/shard_map/pallas_call | solution.py:192
  (81 shorter events, 30.4 us)
Async XLA Ops:
  5.3 5.2 %collective-permute-start = (f32[64,256]{1,0:T(8,128)S(1)}, f32[64,256]{1,0:T(8,128)S(1)}, u32[]{:S(2)}, u32[]{:S(2)}) collective-permute-start(f32[64,256]{1,0:T(8,128)S(1)} %fusion), channel_id=1, source_target_pairs={{0,1},{1,0},{2,3},{3,2},{4,5},{5,4},{6,7},{7,6},{8,9},{9,8},{10,11... | collective-permute-start | bytes 196616 | tf_op jit(solution)/shard_map/ppermute | solution.py:209
  10.5 5.4 %collective-permute-start.1 = (f32[2,64,128]{2,1,0:T(8,128)S(1)}, f32[2,64,128]{2,1,0:T(8,128)S(1)}, u32[]{:S(2)}, u32[]{:S(2)}) collective-permute-start(f32[2,64,128]{2,1,0:T(8,128)S(1)} %bitcast_bitcast_fusion), channel_id=1, source_target_pairs={{0,8},{4,12},{8,0},{12,4},{1,9},{5,13},{9,1},{13,5},{2,10},{6,14},... | collective-permute-start | bytes 196616 | tf_op jit(solution)/shard_map/ppermute | solution.py:209
  16.0 5.9 %collective-permute-start.2 = (f32[4,64,128]{2,1,0:T(8,128)S(1)}, f32[4,64,128]{2,1,0:T(8,128)S(1)}, u32[]{:S(2)}, u32[]{:S(2)}) collective-permute-start(f32[4,64,128]{2,1,0:T(8,128)S(1)} %pad_maximum_fusion.1), channel_id=1, source_target_pairs={{0,4},{4,0},{8,12},{12,8},{1,5},{5,1},{9,13},{13,9},{2,6},{6,2},{1... | collective-permute-start | bytes 393224 | tf_op jit(solution)/shard_map/ppermute | solution.py:209
  18.2 14.0 %collective-permute-start.5 = (bf16[256,512]{1,0:T(8,128)(2,1)S(1)}, bf16[256,512]{1,0:T(8,128)(2,1)S(1)}, u32[]{:S(2)}, u32[]{:S(2)}) collective-permute-start(bf16[256,512]{1,0:T(8,128)(2,1)S(1)} %get-tuple-element.46), channel_id=1, source_target_pairs={{0,6},{2,4},{4,2},{6,0},{8,14},{10,12},{12,10},{14,8},{1,7},{3,5},... | collective-permute-start | bytes 786440 | tf_op jit(solution)/shard_map/ppermute | solution.py:209
  18.3 14.0 %collective-permute-start.4 = (bf16[256,512]{1,0:T(8,128)(2,1)S(1)}, bf16[256,512]{1,0:T(8,128)(2,1)S(1)}, u32[]{:S(2)}, u32[]{:S(2)}) collective-permute-start(bf16[256,512]{1,0:T(8,128)(2,1)S(1)} %get-tuple-element.47), channel_id=1, source_target_pairs={{0,8},{2,10},{4,12},{6,14},{8,0},{10,2},{12,4},{14,6},{1,9},{3,11}... | collective-permute-start | bytes 786440 | tf_op jit(solution)/shard_map/ppermute | solution.py:209
  21.8 13.9 %collective-permute-start.3 = (f32[8,64,128]{2,1,0:T(8,128)S(1)}, f32[8,64,128]{2,1,0:T(8,128)S(1)}, u32[]{:S(2)}, u32[]{:S(2)}) collective-permute-start(f32[8,64,128]{2,1,0:T(8,128)S(1)} %constant_dynamic-update-slice_fusion.z_ref), channel_id=1, source_target_pairs={{0,2},{2,0},{1,3},{3,1},{4,6},{6,4},{5,7},{7,5},{8,10},{10,8},{9,1... | collective-permute-start | bytes 786440 | tf_op jit(solution)/shard_map/ppermute | solution.py:209
  21.9 36.5 %collective-permute-start.10 = (bf16[256,512]{1,0:T(8,128)(2,1)S(1)}, bf16[256,512]{1,0:T(8,128)(2,1)S(1)}, u32[]{:S(2)}, u32[]{:S(2)}) collective-permute-start(bf16[256,512]{1,0:T(8,128)(2,1)S(1)} %get-tuple-element.40), channel_id=1, source_target_pairs={{0,14},{2,12},{4,10},{6,8},{8,6},{10,4},{12,2},{14,0},{1,15},{3,13... | collective-permute-start | bytes 786440 | tf_op jit(solution)/shard_map/ppermute | solution.py:209
  31.7 26.7 %collective-permute-start.9 = (bf16[256,512]{1,0:T(8,128)(2,1)S(1)}, bf16[256,512]{1,0:T(8,128)(2,1)S(1)}, u32[]{:S(2)}, u32[]{:S(2)}) collective-permute-start(bf16[256,512]{1,0:T(8,128)(2,1)S(1)} %get-tuple-element.41), channel_id=1, source_target_pairs={{0,12},{2,14},{4,8},{6,10},{8,4},{10,6},{12,0},{14,2},{1,13},{3,15... | collective-permute-start | bytes 786440 | tf_op jit(solution)/shard_map/ppermute | solution.py:209
  32.2 36.2 %collective-permute-start.8 = (bf16[256,512]{1,0:T(8,128)(2,1)S(1)}, bf16[256,512]{1,0:T(8,128)(2,1)S(1)}, u32[]{:S(2)}, u32[]{:S(2)}) collective-permute-start(bf16[256,512]{1,0:T(8,128)(2,1)S(1)} %get-tuple-element.42), channel_id=1, source_target_pairs={{0,10},{2,8},{4,14},{6,12},{8,2},{10,0},{12,6},{14,4},{1,11},{3,9}... | collective-permute-start | bytes 786440 | tf_op jit(solution)/shard_map/ppermute | solution.py:209
  32.3 36.2 %collective-permute-start.7 = (bf16[256,512]{1,0:T(8,128)(2,1)S(1)}, bf16[256,512]{1,0:T(8,128)(2,1)S(1)}, u32[]{:S(2)}, u32[]{:S(2)}) collective-permute-start(bf16[256,512]{1,0:T(8,128)(2,1)S(1)} %get-tuple-element.43), channel_id=1, source_target_pairs={{0,4},{2,6},{4,0},{6,2},{8,12},{10,14},{12,8},{14,10},{1,5},{3,7},... | collective-permute-start | bytes 786440 | tf_op jit(solution)/shard_map/ppermute | solution.py:209
  35.7 32.7 %collective-permute-start.6 = (bf16[256,512]{1,0:T(8,128)(2,1)S(1)}, bf16[256,512]{1,0:T(8,128)(2,1)S(1)}, u32[]{:S(2)}, u32[]{:S(2)}) collective-permute-start(bf16[256,512]{1,0:T(8,128)(2,1)S(1)} %get-tuple-element.44), channel_id=1, source_target_pairs={{0,2},{2,0},{4,6},{6,4},{8,10},{10,8},{12,14},{14,12},{1,3},{3,1},... | collective-permute-start | bytes 786440 | tf_op jit(solution)/shard_map/ppermute | solution.py:209
  70.1 1.6 collective-permute-start.11
  71.8 5.6 %collective-permute-start.12 = (f32[4,64,128]{2,1,0:T(8,128)S(1)}, f32[4,64,128]{2,1,0:T(8,128)S(1)}, u32[]{:S(2)}, u32[]{:S(2)}) collective-permute-start(f32[4,64,128]{2,1,0:T(8,128)S(1)} %slice.36), channel_id=1, source_target_pairs={{0,1},{1,0},{2,3},{3,2},{4,5},{5,4},{6,7},{7,6},{8,9},{9,8},{10,11... | collective-permute-start | bytes 393224 | tf_op jit(solution)/shard_map/ppermute | solution.py:209
  77.4 5.0 %collective-permute-start.13 = (f32[4,64,128]{2,1,0:T(8,128)S(1)}, f32[4,64,128]{2,1,0:T(8,128)S(1)}, u32[]{:S(2)}, u32[]{:S(2)}) collective-permute-start(f32[4,64,128]{2,1,0:T(8,128)S(1)} %slice_add_fusion.3), channel_id=1, source_target_pairs={{0,4},{4,0},{8,12},{12,8},{1,5},{5,1},{9,13},{13,9},{2,6},{6,2},{1... | collective-permute-start | bytes 393224 | tf_op jit(solution)/shard_map/ppermute | solution.py:209
  82.5 7.1 %collective-permute-start.14 = (f32[4,64,128]{2,1,0:T(8,128)S(1)}, f32[4,64,128]{2,1,0:T(8,128)S(1)}, u32[]{:S(2)}, u32[]{:S(2)}) collective-permute-start(f32[4,64,128]{2,1,0:T(8,128)S(1)} %add.245), channel_id=1, source_target_pairs={{0,8},{4,12},{8,0},{12,4},{1,9},{5,13},{9,1},{13,5},{2,10},{6,14},... | collective-permute-start | bytes 393224 | tf_op jit(solution)/shard_map/ppermute | solution.py:209
  89.6 5.0 %collective-permute-start.15 = (f32[4,64,128]{2,1,0:T(8,128)S(1)}, f32[4,64,128]{2,1,0:T(8,128)S(1)}, u32[]{:S(2)}, u32[]{:S(2)}) collective-permute-start(f32[4,64,128]{2,1,0:T(8,128)S(1)} %add.246), channel_id=1, source_target_pairs={{0,1},{1,0},{2,3},{3,2},{4,5},{5,4},{6,7},{7,6},{8,9},{9,8},{10,11... | collective-permute-start | bytes 393224 | tf_op jit(solution)/shard_map/ppermute | solution.py:209
  94.6 1.6 collective-permute-start.16
  104.3 1.4 collective-permute-start.17
  105.8 4.3 %collective-permute-start.18 = (bf16[4,64,128]{2,1,0:T(8,128)(2,1)S(1)}, bf16[4,64,128]{2,1,0:T(8,128)(2,1)S(1)}, u32[]{:S(2)}, u32[]{:S(2)}) collective-permute-start(bf16[4,64,128]{2,1,0:T(8,128)(2,1)S(1)} %slice.58), channel_id=1, source_target_pairs={{0,1},{1,0},{2,3},{3,2},{4,5},{5,4},{6,7},{7,6},{8,9},{9,8},{10,11... | collective-permute-start | bytes 196616 | tf_op jit(solution)/shard_map/ppermute | solution.py:209
  110.1 4.3 %collective-permute-start.19 = (bf16[4,64,128]{2,1,0:T(8,128)(2,1)S(1)}, bf16[4,64,128]{2,1,0:T(8,128)(2,1)S(1)}, u32[]{:S(2)}, u32[]{:S(2)}) collective-permute-start(bf16[4,64,128]{2,1,0:T(8,128)(2,1)S(1)} %fusion.16), channel_id=1, source_target_pairs={{0,4},{4,0},{8,12},{12,8},{1,5},{5,1},{9,13},{13,9},{2,6},{6,2},{1... | collective-permute-start | bytes 196616 | tf_op jit(solution)/shard_map/ppermute | solution.py:209
  114.5 5.4 %collective-permute-start.20 = (bf16[4,64,128]{2,1,0:T(8,128)(2,1)S(1)}, bf16[4,64,128]{2,1,0:T(8,128)(2,1)S(1)}, u32[]{:S(2)}, u32[]{:S(2)}) collective-permute-start(bf16[4,64,128]{2,1,0:T(8,128)(2,1)S(1)} %add_convert_fusion.5), channel_id=1, source_target_pairs={{0,8},{4,12},{8,0},{12,4},{1,9},{5,13},{9,1},{13,5},{2,10},{6,14},... | collective-permute-start | bytes 196616 | tf_op jit(solution)/shard_map/ppermute | solution.py:209
  119.9 4.3 %collective-permute-start.21 = (bf16[4,64,128]{2,1,0:T(8,128)(2,1)S(1)}, bf16[4,64,128]{2,1,0:T(8,128)(2,1)S(1)}, u32[]{:S(2)}, u32[]{:S(2)}) collective-permute-start(bf16[4,64,128]{2,1,0:T(8,128)(2,1)S(1)} %add_convert_fusion.4), channel_id=1, source_target_pairs={{0,1},{1,0},{2,3},{3,2},{4,5},{5,4},{6,7},{7,6},{8,9},{9,8},{10,11... | collective-permute-start | bytes 196616 | tf_op jit(solution)/shard_map/ppermute | solution.py:209
  124.2 1.4 collective-permute-start.22
  133.0 1.4 collective-permute-start.23
  134.5 4.3 %collective-permute-start.24 = (bf16[4,64,128]{2,1,0:T(8,128)(2,1)S(1)}, bf16[4,64,128]{2,1,0:T(8,128)(2,1)S(1)}, u32[]{:S(2)}, u32[]{:S(2)}) collective-permute-start(bf16[4,64,128]{2,1,0:T(8,128)(2,1)S(1)} %slice.57), channel_id=1, source_target_pairs={{0,1},{1,0},{2,3},{3,2},{4,5},{5,4},{6,7},{7,6},{8,9},{9,8},{10,11... | collective-permute-start | bytes 196616 | tf_op jit(solution)/shard_map/ppermute | solution.py:209
  138.9 4.3 %collective-permute-start.25 = (bf16[4,64,128]{2,1,0:T(8,128)(2,1)S(1)}, bf16[4,64,128]{2,1,0:T(8,128)(2,1)S(1)}, u32[]{:S(2)}, u32[]{:S(2)}) collective-permute-start(bf16[4,64,128]{2,1,0:T(8,128)(2,1)S(1)} %fusion.15), channel_id=1, source_target_pairs={{0,4},{4,0},{8,12},{12,8},{1,5},{5,1},{9,13},{13,9},{2,6},{6,2},{1... | collective-permute-start | bytes 196616 | tf_op jit(solution)/shard_map/ppermute | solution.py:209
  143.2 5.4 %collective-permute-start.26 = (bf16[4,64,128]{2,1,0:T(8,128)(2,1)S(1)}, bf16[4,64,128]{2,1,0:T(8,128)(2,1)S(1)}, u32[]{:S(2)}, u32[]{:S(2)}) collective-permute-start(bf16[4,64,128]{2,1,0:T(8,128)(2,1)S(1)} %add_convert_fusion.3), channel_id=1, source_target_pairs={{0,8},{4,12},{8,0},{12,4},{1,9},{5,13},{9,1},{13,5},{2,10},{6,14},... | collective-permute-start | bytes 196616 | tf_op jit(solution)/shard_map/ppermute | solution.py:209
  148.6 4.3 %collective-permute-start.27 = (bf16[4,64,128]{2,1,0:T(8,128)(2,1)S(1)}, bf16[4,64,128]{2,1,0:T(8,128)(2,1)S(1)}, u32[]{:S(2)}, u32[]{:S(2)}) collective-permute-start(bf16[4,64,128]{2,1,0:T(8,128)(2,1)S(1)} %add_convert_fusion.2), channel_id=1, source_target_pairs={{0,1},{1,0},{2,3},{3,2},{4,5},{5,4},{6,7},{7,6},{8,9},{9,8},{10,11... | collective-permute-start | bytes 196616 | tf_op jit(solution)/shard_map/ppermute | solution.py:209
  163.2 4.3 %collective-permute-start.30 = (bf16[4,64,128]{2,1,0:T(8,128)(2,1)S(1)}, bf16[4,64,128]{2,1,0:T(8,128)(2,1)S(1)}, u32[]{:S(2)}, u32[]{:S(2)}) collective-permute-start(bf16[4,64,128]{2,1,0:T(8,128)(2,1)S(1)} %slice.56), channel_id=1, source_target_pairs={{0,1},{1,0},{2,3},{3,2},{4,5},{5,4},{6,7},{7,6},{8,9},{9,8},{10,11... | collective-permute-start | bytes 196616 | tf_op jit(solution)/shard_map/ppermute | solution.py:209
  167.6 4.3 %collective-permute-start.31 = (bf16[4,64,128]{2,1,0:T(8,128)(2,1)S(1)}, bf16[4,64,128]{2,1,0:T(8,128)(2,1)S(1)}, u32[]{:S(2)}, u32[]{:S(2)}) collective-permute-start(bf16[4,64,128]{2,1,0:T(8,128)(2,1)S(1)} %fusion.14), channel_id=1, source_target_pairs={{0,4},{4,0},{8,12},{12,8},{1,5},{5,1},{9,13},{13,9},{2,6},{6,2},{1... | collective-permute-start | bytes 196616 | tf_op jit(solution)/shard_map/ppermute | solution.py:209
  172.0 5.4 %collective-permute-start.32 = (bf16[4,64,128]{2,1,0:T(8,128)(2,1)S(1)}, bf16[4,64,128]{2,1,0:T(8,128)(2,1)S(1)}, u32[]{:S(2)}, u32[]{:S(2)}) collective-permute-start(bf16[4,64,128]{2,1,0:T(8,128)(2,1)S(1)} %add_convert_fusion.1), channel_id=1, source_target_pairs={{0,8},{4,12},{8,0},{12,4},{1,9},{5,13},{9,1},{13,5},{2,10},{6,14},... | collective-permute-start | bytes 196616 | tf_op jit(solution)/shard_map/ppermute | solution.py:209
  177.4 4.3 %collective-permute-start.33 = (bf16[4,64,128]{2,1,0:T(8,128)(2,1)S(1)}, bf16[4,64,128]{2,1,0:T(8,128)(2,1)S(1)}, u32[]{:S(2)}, u32[]{:S(2)}) collective-permute-start(bf16[4,64,128]{2,1,0:T(8,128)(2,1)S(1)} %add_convert_fusion), channel_id=1, source_target_pairs={{0,1},{1,0},{2,3},{3,2},{4,5},{5,4},{6,7},{7,6},{8,9},{9,8},{10,11... | collective-permute-start | bytes 196616 | tf_op jit(solution)/shard_map/ppermute | solution.py:209
  (4 other events, 20.9 us)

commit v8 on v4

--- a/solution.py
+++ b/solution.py
@@ -148,24 +148,14 @@
     return small_times_wide(inverse_two, first).astype(jnp.bfloat16), upper
 
 
-def times_slab(basis, a_refs):
-    rows = a_refs[0].shape[0]
-    pieces = [
-        dot_nn(basis[:, rows * s : rows * (s + 1)], a_ref[...]) for s, a_ref in enumerate(a_refs)
-    ]
-    return functools.reduce(jnp.add, pieces)
-
-
-def power_body(basis, a_refs, at_ref, part_refs):
-    weights = times_slab(basis, a_refs).astype(jnp.bfloat16)
-    width = part_refs[0].shape[2]
-    n_col = at_ref.shape[0] // len(a_refs)
-    for s, a_ref in enumerate(a_refs):
-        forth = dot_nt(weights, a_ref[...])
-        target = part_refs[s % 2]
-        for c in range(n_col):
-            block = forth[:, width * c : width * (c + 1)]
-            target[at_ref[s * n_col + c]] = block.astype(target.dtype)
+def power_body(basis, a, at_ref, part_refs):
+    weights = dot_nn(basis, a).astype(jnp.bfloat16)
+    forth = dot_nt(weights, a)
+    half, unused, width = part_refs[0].shape
+    n_col = at_ref.shape[0] // half
+    for i in range(2 * half):
+        target = part_refs[i // n_col % 2]
+        target[at_ref[i]] = forth[:, width * i : width * (i + 1)].astype(target.dtype)
 
 
 def orth_kernel(at_ref, z_ref, other_ref, basis_ref, upper_ref):
@@ -173,17 +163,21 @@
 
 
 def power_kernel(at_ref, basis_ref, *refs):
-    power_body(basis_ref[...], refs[:-2], at_ref, refs[-2:])
-
-
-def orth_power_kernel(at_ref, z_ref, other_ref, *refs):
+    piece_refs, a_ref, part_refs = refs[:-3], refs[-3], refs[-2:]
+    rows = piece_refs[0].shape[0]
+    for s, piece_ref in enumerate(piece_refs):
+        a_ref[rows * s : rows * (s + 1), :] = piece_ref[...]
+    power_body(basis_ref[...], a_ref[...], at_ref, part_refs)
+
+
+def orth_power_kernel(at_ref, z_ref, other_ref, a_ref, *part_refs):
     basis, unused = narrow_basis(at_ref, (z_ref, other_ref))
-    power_body(basis, refs[:-2], at_ref, refs[-2:])
-
-
-def last_kernel(at_ref, z_ref, other_ref, *refs):
+    power_body(basis, a_ref[...], at_ref, part_refs)
+
+
+def last_kernel(at_ref, z_ref, other_ref, a_ref, out_ref):
     basis, unused = narrow_basis(at_ref, (z_ref, other_ref))
-    refs[-1][...] = times_slab(basis, refs[:-1])
+    out_ref[...] = dot_nn(basis, a_ref[...])
 
 
 def call(kernel, out_shapes, flops, at, *operands):
@@ -260,8 +254,15 @@
                 pieces[offset] = from_xor(pieces[offset], ("z", "core"), offset)
 
     far = list(range(n_row // 2, n_row))
-    near = list(range(n_row // 2 - 1, -1, -1))
-    move(states, far[:1])
+    near = list(range(2, n_row // 2))
+    beside = [[1], near + far[:1]]
+
+    def hold(value, offsets):
+        move(states, offsets)
+        value, moved = lax.optimization_barrier((value, [pieces[o] for o in offsets]))
+        for o, piece in zip(offsets, moved):
+            pieces[o] = piece
+        return value
 
     col = lax.axis_index("col")
     feature_index = col * width_local + jnp.arange(width_local, dtype=jnp.int32)
@@ -274,11 +275,13 @@
     z = z.reshape(RANK, n_col, chunk).transpose(1, 0, 2)
     z_bits = bits(n_z)[::-1]
     for k, bit in enumerate(z_bits):
+        z = hold(z, beside.pop(0)) if beside else z
         z = jnp.concatenate([z, from_xor(z, ("z",), bit)])
-        slab, z = lax.optimization_barrier((states, z))
         if k == 0:
+            z, slab = lax.optimization_barrier((z, states))
             move(slab, far[1:2])
-    move(slab, far[2:] + near)
+    z, slab = lax.optimization_barrier((z, states))
+    move(slab, far[2:] + [0] + [o for offsets in beside for o in offsets])
     z = z, from_xor(z, ("core",), 1)
     absolute_col = [("col", bit, False) for bit in bits(n_col)[::-1]]
     at_first = chunk_places([("z", bit, True) for bit in z_bits[::-1]] + absolute_col)
@@ -298,15 +301,16 @@
     basis, upper = call(orth_kernel, (wide, square), orth_flops, at_first, *z)
     factor = upper.T * (1.0 / math.sqrt(rows_total * width_total))
     dtype = f32
-    parts = call(power_kernel, sent_as(dtype), power_flops, at, basis, *pieces)
+    slab = jax.ShapeDtypeStruct((rows_total, cols), states.dtype)
+    a, *parts = call(power_kernel, (slab,) + sent_as(dtype), power_flops, at, basis, *pieces)
     for step in range(POWER - 1):
         z = gather_parts(sum_parts(*parts, dtype))
         dtype = jnp.bfloat16
         flops = orth_flops + power_flops
-        parts = call(orth_power_kernel, sent_as(dtype), flops, at, *z, *pieces)
+        parts = call(orth_power_kernel, sent_as(dtype), flops, at, *z, a)
     z = gather_parts(sum_parts(*parts, dtype))
     loadings = jax.ShapeDtypeStruct((RANK, cols), f32)
-    return call(last_kernel, loadings, orth_flops + power_flops, at, *z, *pieces).T, factor
+    return call(last_kernel, loadings, orth_flops + power_flops, at, *z, a).T, factor
 
 
 def local_gram(basis):

time: 185 us -> 189 us (1.022)
  waiting for transfers between devices: 102 us -> 108 us
  local copies, waits for them, and re-layouts: 4.14 us -> 0.95 us
    ppermute x35, waiting for transfers between devices: 102 us -> 108 us  [from_xor(): return lax.ppermute(value, axis, [(i, i ^ offset) for i in range(size)])]
    dynamic_slice x3, local copies, waits for them, and re-layouts: 3.39 us -> 0.2 us  [block(): return lax.dynamic_slice_in_dim(slab, (row ^ offset) * cols, cols, 1)]
  transfers between devices with their start and end apart: 35 -> 35, of which waited for: 29 -> 28; matrix products, arithmetic and copies ran while one was open for 2% -> 1% of each run, Pallas kernels for 3% -> 3%
where the time goes in v8:
time: 189 us
  waiting for transfers between devices  108 us (57%)
  starting transfers between devices  38 us (20%)
  Pallas kernels  35.7 us (19%)
  matrix products  3.97 us (2%)
    ppermute x35, waiting for transfers between devices, from_xor(): return lax.ppermute(value, axis, [(i, i ^ offset) for i in range(size)])  108 us
    ppermute x35, starting transfers between devices, from_xor(): return lax.ppermute(value, axis, [(i, i ^ offset) for i in range(size)])  38 us
    pallas_call x6, Pallas kernels, call(): pl.pallas_call(kernel, out_shape=out_shapes, in_specs=[pl.BlockSpec(memor...  35.7 us
    dot_general x1, matrix products, per_device_transposed(): lax.dot_general(omega, states, (((0,), (1,)), ((), ())), preferred_elemen...  3.97 us
  transfers between devices with their start and end apart: 35, of which 28 were waited for; matrix products, arithmetic and copies ran while one was open for 1% of the time, Pallas kernels for 3%

profile of v8, /device:TPU:0, one launch (start us, length us, event | category | flops | bytes accessed | tf_op | source)
XLA Modules:
  0.0 188.5 jit_solution(2464570639717032717)
XLA Ops:
  1.3 4.0 %fusion = f32[64,256]{1,0:T(8,128)S(1)} fusion(bf16[256,4096]{1,0:T(8,128)(2,1)} %param.3, s32[]{:T(128)S(6)} %xor.84, s32[4096]{0:T(1024)S(1)} %add_multiply_fusion), kind=kOutput, calls=%fused_computation.1 | convolution fusion | flops 152043520 | bytes 2179076 | tf_op jit(solution)/shard_map/dot_general | solution.py:270
  5.3 3.0 %collective-permute-start = (f32[64,256]{1,0:T(8,128)S(1)}, f32[64,256]{1,0:T(8,128)S(1)}, u32[]{:S(2)}, u32[]{:S(2)}) collective-permute-start(f32[64,256]{1,0:T(8,128)S(1)} %fusion), channel_id=1, source_target_pairs={{0,1},{1,0},{2,3},{3,2},{4,5},{5,4},{6,7},{7,6},{8,9},{9,8},{10,11... | collective-permute-start | bytes 196616 | tf_op jit(solution)/shard_map/ppermute | solution.py:202
  8.5 2.7 %collective-permute-start.5 = (bf16[256,512]{1,0:T(8,128)(2,1)S(1)}, bf16[256,512]{1,0:T(8,128)(2,1)S(1)}, u32[]{:S(2)}, u32[]{:S(2)}) collective-permute-start(bf16[256,512]{1,0:T(8,128)(2,1)S(1)} %get-tuple-element.53), channel_id=1, source_target_pairs={{0,8},{2,10},{4,12},{6,14},{8,0},{10,2},{12,4},{14,6},{1,9},{3,11}... | collective-permute-start | bytes 786440 | tf_op jit(solution)/shard_map/ppermute | solution.py:202
  13.7 16.2 %collective-permute-done.2 = f32[2,64,128]{2,1,0:T(8,128)S(1)} collective-permute-done((f32[2,64,128]{2,1,0:T(8,128)S(1)}, f32[2,64,128]{2,1,0:T(8,128)S(1)}, u32[]{:S(2)}, u32[]{:S(2)}) %collective-permute-start.2) | collective-permute-done | bytes 65568 | tf_op jit(solution)/shard_map/ppermute | solution.py:202
  33.5 4.1 %collective-permute-done.6 = f32[4,64,128]{2,1,0:T(8,128)S(1)} collective-permute-done((f32[4,64,128]{2,1,0:T(8,128)S(1)}, f32[4,64,128]{2,1,0:T(8,128)S(1)}, u32[]{:S(2)}, u32[]{:S(2)}) %collective-permute-start.6) | collective-permute-done | bytes 131104 | tf_op jit(solution)/shard_map/ppermute | solution.py:202
  37.7 2.4 %collective-permute-start.10 = (bf16[256,512]{1,0:T(8,128)(2,1)S(1)}, bf16[256,512]{1,0:T(8,128)(2,1)S(1)}, u32[]{:S(2)}, u32[]{:S(2)}) collective-permute-start(bf16[256,512]{1,0:T(8,128)(2,1)S(1)} %get-tuple-element.50), channel_id=1, source_target_pairs={{0,14},{2,12},{4,10},{6,8},{8,6},{10,4},{12,2},{14,0},{1,15},{3,13... | collective-permute-start | bytes 786440 | tf_op jit(solution)/shard_map/ppermute | solution.py:202
  40.2 1.5 collective-permute-start.9
  41.8 6.3 %shard_map.41 = (bf16[64,2048]{1,0:T(8,128)(2,1)S(1)}, f32[64,64]{1,0:T(8,128)S(1)}) custom-call(s32[16]{0:T(128)S(1)} %fusion.20.at_ref, f32[8,64,128]{2,1,0:T(8,128)S(1)} %pad_maximum_fusion.z_ref, f32[8,64,128]{2,1,0:T(8,128)S(1)} %collective-permute-done.7.other_ref), custom_call_target="tpu_custom_call" | custom-call | flops 402653184 | bytes 524288 | tf_op jit(solution)/shard_map/pallas_call | solution.py:185
  48.1 10.7 %collective-permute-done.8.refs_5_ = bf16[256,512]{1,0:T(8,128)(2,1)S(1)} collective-permute-done((bf16[256,512]{1,0:T(8,128)(2,1)S(1)}, bf16[256,512]{1,0:T(8,128)(2,1)S(1)}, u32[]{:S(2)}, u32[]{:S(2)}) %collective-permute-start.8) | collective-permute-done | bytes 262176 | tf_op jit(solution)/shard_map/ppermute | solution.py:202
  58.8 1.8 shard_map.42
  62.9 5.0 %collective-permute-done.12 = f32[4,64,128]{2,1,0:T(8,128)S(1)} collective-permute-done((f32[4,64,128]{2,1,0:T(8,128)S(1)}, f32[4,64,128]{2,1,0:T(8,128)S(1)}, u32[]{:S(2)}, u32[]{:S(2)}) %collective-permute-start.12) | collective-permute-done | bytes 131104 | tf_op jit(solution)/shard_map/ppermute | solution.py:202
  67.9 11.2 %collective-permute-start.13 = (f32[4,64,128]{2,1,0:T(8,128)S(1)}, f32[4,64,128]{2,1,0:T(8,128)S(1)}, u32[]{:S(2)}, u32[]{:S(2)}) collective-permute-start(f32[4,64,128]{2,1,0:T(8,128)S(1)} %slice_add_fusion.3), channel_id=1, source_target_pairs={{0,4},{4,0},{8,12},{12,8},{1,5},{5,1},{9,13},{13,9},{2,6},{6,2},{1... | collective-permute-start | bytes 393224 | tf_op jit(solution)/shard_map/ppermute | solution.py:202
  79.1 3.0 %collective-permute-done.13 = f32[4,64,128]{2,1,0:T(8,128)S(1)} collective-permute-done((f32[4,64,128]{2,1,0:T(8,128)S(1)}, f32[4,64,128]{2,1,0:T(8,128)S(1)}, u32[]{:S(2)}, u32[]{:S(2)}) %collective-permute-start.13) | collective-permute-done | bytes 131104 | tf_op jit(solution)/shard_map/ppermute | solution.py:202
  82.1 3.0 %collective-permute-start.14 = (f32[4,64,128]{2,1,0:T(8,128)S(1)}, f32[4,64,128]{2,1,0:T(8,128)S(1)}, u32[]{:S(2)}, u32[]{:S(2)}) collective-permute-start(f32[4,64,128]{2,1,0:T(8,128)S(1)} %add.245), channel_id=1, source_target_pairs={{0,8},{4,12},{8,0},{12,4},{1,9},{5,13},{9,1},{13,5},{2,10},{6,14},... | collective-permute-start | bytes 393224 | tf_op jit(solution)/shard_map/ppermute | solution.py:202
  85.1 4.9 %collective-permute-done.14 = f32[4,64,128]{2,1,0:T(8,128)S(1)} collective-permute-done((f32[4,64,128]{2,1,0:T(8,128)S(1)}, f32[4,64,128]{2,1,0:T(8,128)S(1)}, u32[]{:S(2)}, u32[]{:S(2)}) %collective-permute-start.14) | collective-permute-done | bytes 131104 | tf_op jit(solution)/shard_map/ppermute | solution.py:202
  90.6 4.4 %collective-permute-done.15 = f32[4,64,128]{2,1,0:T(8,128)S(1)} collective-permute-done((f32[4,64,128]{2,1,0:T(8,128)S(1)}, f32[4,64,128]{2,1,0:T(8,128)S(1)}, u32[]{:S(2)}, u32[]{:S(2)}) %collective-permute-start.15) | collective-permute-done | bytes 131104 | tf_op jit(solution)/shard_map/ppermute | solution.py:202
  96.7 7.4 %shard_map.43 = (f32[8,64,128]{2,1,0:T(8,128)S(1)}, bf16[8,64,128]{2,1,0:T(8,128)(2,1)S(1)}) custom-call(s32[16]{0:T(128)S(1)} %fusion.18.at_ref, f32[8,64,128]{2,1,0:T(8,128)S(1)} %pad_maximum_fusion.1.z_ref, f32[8,64,128]{2,1,0:T(8,128)S(1)} %collective-permute-done.16.other_ref, bf16[2048,512]{1,0:T(8,128)(2,1)S(1)} %get-tuple-element.36.a_ref), custom_call_target="tpu_custom_call" | custom-call | flops 671088640 | bytes 2621440 | tf_op jit(solution)/shard_map/pallas_call | solution.py:185
  106.2 3.7 %collective-permute-done.18 = bf16[4,64,128]{2,1,0:T(8,128)(2,1)S(1)} collective-permute-done((bf16[4,64,128]{2,1,0:T(8,128)(2,1)S(1)}, bf16[4,64,128]{2,1,0:T(8,128)(2,1)S(1)}, u32[]{:S(2)}, u32[]{:S(2)}) %collective-permute-start.18) | collective-permute-done | bytes 65568 | tf_op jit(solution)/shard_map/ppermute | solution.py:202
  110.1 4.2 %collective-permute-done.19 = bf16[4,64,128]{2,1,0:T(8,128)(2,1)S(1)} collective-permute-done((bf16[4,64,128]{2,1,0:T(8,128)(2,1)S(1)}, bf16[4,64,128]{2,1,0:T(8,128)(2,1)S(1)}, u32[]{:S(2)}, u32[]{:S(2)}) %collective-permute-start.19) | collective-permute-done | bytes 65568 | tf_op jit(solution)/shard_map/ppermute | solution.py:202
  115.4 4.3 %collective-permute-done.20 = bf16[4,64,128]{2,1,0:T(8,128)(2,1)S(1)} collective-permute-done((bf16[4,64,128]{2,1,0:T(8,128)(2,1)S(1)}, bf16[4,64,128]{2,1,0:T(8,128)(2,1)S(1)}, u32[]{:S(2)}, u32[]{:S(2)}) %collective-permute-start.20) | collective-permute-done | bytes 65568 | tf_op jit(solution)/shard_map/ppermute | solution.py:202
  120.4 3.7 %collective-permute-done.21 = bf16[4,64,128]{2,1,0:T(8,128)(2,1)S(1)} collective-permute-done((bf16[4,64,128]{2,1,0:T(8,128)(2,1)S(1)}, bf16[4,64,128]{2,1,0:T(8,128)(2,1)S(1)}, u32[]{:S(2)}, u32[]{:S(2)}) %collective-permute-start.21) | collective-permute-done | bytes 65568 | tf_op jit(solution)/shard_map/ppermute | solution.py:202
  125.6 6.7 %shard_map.44 = (f32[8,64,128]{2,1,0:T(8,128)S(1)}, bf16[8,64,128]{2,1,0:T(8,128)(2,1)S(1)}) custom-call(s32[16]{0:T(128)S(1)} %fusion.18.at_ref, bf16[8,64,128]{2,1,0:T(8,128)(2,1)S(1)} %pad_maximum_fusion.3.z_ref, bf16[8,64,128]{2,1,0:T(8,128)(2,1)S(1)} %collective-permute-done.22.other_ref, bf16[2048,512]{1,0:T(8,128)(2,1)S(1)} %get-tuple-element.36.a_ref), custom_call_target="tpu_custom_call" | custom-call | flops 671088640 | bytes 2359296 | tf_op jit(solution)/shard_map/pallas_call | solution.py:185
  134.4 3.7 %collective-permute-done.24 = bf16[4,64,128]{2,1,0:T(8,128)(2,1)S(1)} collective-permute-done((bf16[4,64,128]{2,1,0:T(8,128)(2,1)S(1)}, bf16[4,64,128]{2,1,0:T(8,128)(2,1)S(1)}, u32[]{:S(2)}, u32[]{:S(2)}) %collective-permute-start.24) | collective-permute-done | bytes 65568 | tf_op jit(solution)/shard_map/ppermute | solution.py:202
  138.2 4.3 %collective-permute-done.25 = bf16[4,64,128]{2,1,0:T(8,128)(2,1)S(1)} collective-permute-done((bf16[4,64,128]{2,1,0:T(8,128)(2,1)S(1)}, bf16[4,64,128]{2,1,0:T(8,128)(2,1)S(1)}, u32[]{:S(2)}, u32[]{:S(2)}) %collective-permute-start.25) | collective-permute-done | bytes 65568 | tf_op jit(solution)/shard_map/ppermute | solution.py:202
  143.5 4.4 %collective-permute-done.26 = bf16[4,64,128]{2,1,0:T(8,128)(2,1)S(1)} collective-permute-done((bf16[4,64,128]{2,1,0:T(8,128)(2,1)S(1)}, bf16[4,64,128]{2,1,0:T(8,128)(2,1)S(1)}, u32[]{:S(2)}, u32[]{:S(2)}) %collective-permute-start.26) | collective-permute-done | bytes 65568 | tf_op jit(solution)/shard_map/ppermute | solution.py:202
  148.5 3.7 %collective-permute-done.27 = bf16[4,64,128]{2,1,0:T(8,128)(2,1)S(1)} collective-permute-done((bf16[4,64,128]{2,1,0:T(8,128)(2,1)S(1)}, bf16[4,64,128]{2,1,0:T(8,128)(2,1)S(1)}, u32[]{:S(2)}, u32[]{:S(2)}) %collective-permute-start.27) | collective-permute-done | bytes 65568 | tf_op jit(solution)/shard_map/ppermute | solution.py:202
  153.7 6.7 %shard_map.45 = (f32[8,64,128]{2,1,0:T(8,128)S(1)}, bf16[8,64,128]{2,1,0:T(8,128)(2,1)S(1)}) custom-call(s32[16]{0:T(128)S(1)} %fusion.18.at_ref, bf16[8,64,128]{2,1,0:T(8,128)(2,1)S(1)} %pad_maximum_fusion.4.z_ref, bf16[8,64,128]{2,1,0:T(8,128)(2,1)S(1)} %collective-permute-done.28.other_ref, bf16[2048,512]{1,0:T(8,128)(2,1)S(1)} %get-tuple-element.36.a_ref), custom_call_target="tpu_custom_call" | custom-call | flops 671088640 | bytes 2359296 | tf_op jit(solution)/shard_map/pallas_call | solution.py:185
  162.5 3.7 %collective-permute-done.30 = bf16[4,64,128]{2,1,0:T(8,128)(2,1)S(1)} collective-permute-done((bf16[4,64,128]{2,1,0:T(8,128)(2,1)S(1)}, bf16[4,64,128]{2,1,0:T(8,128)(2,1)S(1)}, u32[]{:S(2)}, u32[]{:S(2)}) %collective-permute-start.30) | collective-permute-done | bytes 65568 | tf_op jit(solution)/shard_map/ppermute | solution.py:202
  166.3 4.3 %collective-permute-done.31 = bf16[4,64,128]{2,1,0:T(8,128)(2,1)S(1)} collective-permute-done((bf16[4,64,128]{2,1,0:T(8,128)(2,1)S(1)}, bf16[4,64,128]{2,1,0:T(8,128)(2,1)S(1)}, u32[]{:S(2)}, u32[]{:S(2)}) %collective-permute-start.31) | collective-permute-done | bytes 65568 | tf_op jit(solution)/shard_map/ppermute | solution.py:202
  171.5 4.4 %collective-permute-done.32 = bf16[4,64,128]{2,1,0:T(8,128)(2,1)S(1)} collective-permute-done((bf16[4,64,128]{2,1,0:T(8,128)(2,1)S(1)}, bf16[4,64,128]{2,1,0:T(8,128)(2,1)S(1)}, u32[]{:S(2)}, u32[]{:S(2)}) %collective-permute-start.32) | collective-permute-done | bytes 65568 | tf_op jit(solution)/shard_map/ppermute | solution.py:202
  176.6 3.7 %collective-permute-done.33 = bf16[4,64,128]{2,1,0:T(8,128)(2,1)S(1)} collective-permute-done((bf16[4,64,128]{2,1,0:T(8,128)(2,1)S(1)}, bf16[4,64,128]{2,1,0:T(8,128)(2,1)S(1)}, u32[]{:S(2)}, u32[]{:S(2)}) %collective-permute-start.33) | collective-permute-done | bytes 65568 | tf_op jit(solution)/shard_map/ppermute | solution.py:202
  181.7 6.8 %shard_map.46 = f32[64,512]{1,0:T(8,128)} custom-call(s32[16]{0:T(128)S(1)} %fusion.18.at_ref, bf16[8,64,128]{2,1,0:T(8,128)(2,1)S(1)} %pad_maximum_fusion.5.z_ref, bf16[8,64,128]{2,1,0:T(8,128)(2,1)S(1)} %collective-permute-done.34.other_ref, bf16[2048,512]{1,0:T(8,128)(2,1)S(1)} %get-tuple-element.36.a_ref), custom_call_target="tpu_custom_call" | custom-call | flops 671088640 | bytes 2359296 | tf_op jit(solution)/shard_map/pallas_call | solution.py:185
  (82 shorter events, 26.9 us)
Async XLA Ops:
  5.3 7.6 %collective-permute-start = (f32[64,256]{1,0:T(8,128)S(1)}, f32[64,256]{1,0:T(8,128)S(1)}, u32[]{:S(2)}, u32[]{:S(2)}) collective-permute-start(f32[64,256]{1,0:T(8,128)S(1)} %fusion), channel_id=1, source_target_pairs={{0,1},{1,0},{2,3},{3,2},{4,5},{5,4},{6,7},{7,6},{8,9},{9,8},{10,11... | collective-permute-start | bytes 196616 | tf_op jit(solution)/shard_map/ppermute | solution.py:202
  8.4 4.5 %collective-permute-start.1 = (bf16[256,512]{1,0:T(8,128)(2,1)S(1)}, bf16[256,512]{1,0:T(8,128)(2,1)S(1)}, u32[]{:S(2)}, u32[]{:S(2)}) collective-permute-start(bf16[256,512]{1,0:T(8,128)(2,1)S(1)} %get-tuple-element.56), channel_id=1, source_target_pairs={{0,2},{2,0},{4,6},{6,4},{8,10},{10,8},{12,14},{14,12},{1,3},{3,1},... | collective-permute-start | bytes 786440 | tf_op jit(solution)/shard_map/ppermute | solution.py:202
  8.5 21.5 %collective-permute-start.5 = (bf16[256,512]{1,0:T(8,128)(2,1)S(1)}, bf16[256,512]{1,0:T(8,128)(2,1)S(1)}, u32[]{:S(2)}, u32[]{:S(2)}) collective-permute-start(bf16[256,512]{1,0:T(8,128)(2,1)S(1)} %get-tuple-element.53), channel_id=1, source_target_pairs={{0,8},{2,10},{4,12},{6,14},{8,0},{10,2},{12,4},{14,6},{1,9},{3,11}... | collective-permute-start | bytes 786440 | tf_op jit(solution)/shard_map/ppermute | solution.py:202
  11.1 18.9 %collective-permute-start.4 = (bf16[256,512]{1,0:T(8,128)(2,1)S(1)}, bf16[256,512]{1,0:T(8,128)(2,1)S(1)}, u32[]{:S(2)}, u32[]{:S(2)}) collective-permute-start(bf16[256,512]{1,0:T(8,128)(2,1)S(1)} %get-tuple-element.54), channel_id=1, source_target_pairs={{0,6},{2,4},{4,2},{6,0},{8,14},{10,12},{12,10},{14,8},{1,7},{3,5},... | collective-permute-start | bytes 786440 | tf_op jit(solution)/shard_map/ppermute | solution.py:202
  12.5 18.8 %collective-permute-start.3 = (bf16[256,512]{1,0:T(8,128)(2,1)S(1)}, bf16[256,512]{1,0:T(8,128)(2,1)S(1)}, u32[]{:S(2)}, u32[]{:S(2)}) collective-permute-start(bf16[256,512]{1,0:T(8,128)(2,1)S(1)} %get-tuple-element.55), channel_id=1, source_target_pairs={{0,4},{2,6},{4,0},{6,2},{8,12},{10,14},{12,8},{14,10},{1,5},{3,7},... | collective-permute-start | bytes 786440 | tf_op jit(solution)/shard_map/ppermute | solution.py:202
  12.9 17.0 %collective-permute-start.2 = (f32[2,64,128]{2,1,0:T(8,128)S(1)}, f32[2,64,128]{2,1,0:T(8,128)S(1)}, u32[]{:S(2)}, u32[]{:S(2)}) collective-permute-start(f32[2,64,128]{2,1,0:T(8,128)S(1)} %bitcast_bitcast_fusion), channel_id=1, source_target_pairs={{0,8},{4,12},{8,0},{12,4},{1,9},{5,13},{9,1},{13,5},{2,10},{6,14},... | collective-permute-start | bytes 196616 | tf_op jit(solution)/shard_map/ppermute | solution.py:202
  31.3 6.3 %collective-permute-start.6 = (f32[4,64,128]{2,1,0:T(8,128)S(1)}, f32[4,64,128]{2,1,0:T(8,128)S(1)}, u32[]{:S(2)}, u32[]{:S(2)}) collective-permute-start(f32[4,64,128]{2,1,0:T(8,128)S(1)} %pad_maximum_fusion.2), channel_id=1, source_target_pairs={{0,4},{4,0},{8,12},{12,8},{1,5},{5,1},{9,13},{13,9},{2,6},{6,2},{1... | collective-permute-start | bytes 393224 | tf_op jit(solution)/shard_map/ppermute | solution.py:202
  32.5 26.3 %collective-permute-start.8 = (bf16[256,512]{1,0:T(8,128)(2,1)S(1)}, bf16[256,512]{1,0:T(8,128)(2,1)S(1)}, u32[]{:S(2)}, u32[]{:S(2)}) collective-permute-start(bf16[256,512]{1,0:T(8,128)(2,1)S(1)} %constant_dynamic-slice_fusion.2), channel_id=1, source_target_pairs={{0,10},{2,8},{4,14},{6,12},{8,2},{10,0},{12,6},{14,4},{1,11},{3,9}... | collective-permute-start | bytes 786440 | tf_op jit(solution)/shard_map/ppermute | solution.py:202
  37.6 4.2 %collective-permute-start.7 = (f32[8,64,128]{2,1,0:T(8,128)S(1)}, f32[8,64,128]{2,1,0:T(8,128)S(1)}, u32[]{:S(2)}, u32[]{:S(2)}) collective-permute-start(f32[8,64,128]{2,1,0:T(8,128)S(1)} %pad_maximum_fusion.z_ref), channel_id=1, source_target_pairs={{0,2},{2,0},{1,3},{3,1},{4,6},{6,4},{5,7},{7,5},{8,10},{10,8},{9,1... | collective-permute-start | bytes 786440 | tf_op jit(solution)/shard_map/ppermute | solution.py:202
  37.7 21.1 %collective-permute-start.10 = (bf16[256,512]{1,0:T(8,128)(2,1)S(1)}, bf16[256,512]{1,0:T(8,128)(2,1)S(1)}, u32[]{:S(2)}, u32[]{:S(2)}) collective-permute-start(bf16[256,512]{1,0:T(8,128)(2,1)S(1)} %get-tuple-element.50), channel_id=1, source_target_pairs={{0,14},{2,12},{4,10},{6,8},{8,6},{10,4},{12,2},{14,0},{1,15},{3,13... | collective-permute-start | bytes 786440 | tf_op jit(solution)/shard_map/ppermute | solution.py:202
  40.2 18.6 %collective-permute-start.9 = (bf16[256,512]{1,0:T(8,128)(2,1)S(1)}, bf16[256,512]{1,0:T(8,128)(2,1)S(1)}, u32[]{:S(2)}, u32[]{:S(2)}) collective-permute-start(bf16[256,512]{1,0:T(8,128)(2,1)S(1)} %get-tuple-element.51), channel_id=1, source_target_pairs={{0,12},{2,14},{4,8},{6,10},{8,4},{10,6},{12,0},{14,2},{1,13},{3,15... | collective-permute-start | bytes 786440 | tf_op jit(solution)/shard_map/ppermute | solution.py:202
  60.6 1.6 collective-permute-start.11
  62.3 5.6 %collective-permute-start.12 = (f32[4,64,128]{2,1,0:T(8,128)S(1)}, f32[4,64,128]{2,1,0:T(8,128)S(1)}, u32[]{:S(2)}, u32[]{:S(2)}) collective-permute-start(f32[4,64,128]{2,1,0:T(8,128)S(1)} %slice.36), channel_id=1, source_target_pairs={{0,1},{1,0},{2,3},{3,2},{4,5},{5,4},{6,7},{7,6},{8,9},{9,8},{10,11... | collective-permute-start | bytes 393224 | tf_op jit(solution)/shard_map/ppermute | solution.py:202
  67.9 14.2 %collective-permute-start.13 = (f32[4,64,128]{2,1,0:T(8,128)S(1)}, f32[4,64,128]{2,1,0:T(8,128)S(1)}, u32[]{:S(2)}, u32[]{:S(2)}) collective-permute-start(f32[4,64,128]{2,1,0:T(8,128)S(1)} %slice_add_fusion.3), channel_id=1, source_target_pairs={{0,4},{4,0},{8,12},{12,8},{1,5},{5,1},{9,13},{13,9},{2,6},{6,2},{1... | collective-permute-start | bytes 393224 | tf_op jit(solution)/shard_map/ppermute | solution.py:202
  82.1 7.9 %collective-permute-start.14 = (f32[4,64,128]{2,1,0:T(8,128)S(1)}, f32[4,64,128]{2,1,0:T(8,128)S(1)}, u32[]{:S(2)}, u32[]{:S(2)}) collective-permute-start(f32[4,64,128]{2,1,0:T(8,128)S(1)} %add.245), channel_id=1, source_target_pairs={{0,8},{4,12},{8,0},{12,4},{1,9},{5,13},{9,1},{13,5},{2,10},{6,14},... | collective-permute-start | bytes 393224 | tf_op jit(solution)/shard_map/ppermute | solution.py:202
  90.0 5.0 %collective-permute-start.15 = (f32[4,64,128]{2,1,0:T(8,128)S(1)}, f32[4,64,128]{2,1,0:T(8,128)S(1)}, u32[]{:S(2)}, u32[]{:S(2)}) collective-permute-start(f32[4,64,128]{2,1,0:T(8,128)S(1)} %add.246), channel_id=1, source_target_pairs={{0,1},{1,0},{2,3},{3,2},{4,5},{5,4},{6,7},{7,6},{8,9},{9,8},{10,11... | collective-permute-start | bytes 393224 | tf_op jit(solution)/shard_map/ppermute | solution.py:202
  95.1 1.6 collective-permute-start.16
  105.6 4.3 %collective-permute-start.18 = (bf16[4,64,128]{2,1,0:T(8,128)(2,1)S(1)}, bf16[4,64,128]{2,1,0:T(8,128)(2,1)S(1)}, u32[]{:S(2)}, u32[]{:S(2)}) collective-permute-start(bf16[4,64,128]{2,1,0:T(8,128)(2,1)S(1)} %slice.58), channel_id=1, source_target_pairs={{0,1},{1,0},{2,3},{3,2},{4,5},{5,4},{6,7},{7,6},{8,9},{9,8},{10,11... | collective-permute-start | bytes 196616 | tf_op jit(solution)/shard_map/ppermute | solution.py:202
  110.0 4.3 %collective-permute-start.19 = (bf16[4,64,128]{2,1,0:T(8,128)(2,1)S(1)}, bf16[4,64,128]{2,1,0:T(8,128)(2,1)S(1)}, u32[]{:S(2)}, u32[]{:S(2)}) collective-permute-start(bf16[4,64,128]{2,1,0:T(8,128)(2,1)S(1)} %fusion.16), channel_id=1, source_target_pairs={{0,4},{4,0},{8,12},{12,8},{1,5},{5,1},{9,13},{13,9},{2,6},{6,2},{1... | collective-permute-start | bytes 196616 | tf_op jit(solution)/shard_map/ppermute | solution.py:202
  114.3 5.5 %collective-permute-start.20 = (bf16[4,64,128]{2,1,0:T(8,128)(2,1)S(1)}, bf16[4,64,128]{2,1,0:T(8,128)(2,1)S(1)}, u32[]{:S(2)}, u32[]{:S(2)}) collective-permute-start(bf16[4,64,128]{2,1,0:T(8,128)(2,1)S(1)} %add_convert_fusion.5), channel_id=1, source_target_pairs={{0,8},{4,12},{8,0},{12,4},{1,9},{5,13},{9,1},{13,5},{2,10},{6,14},... | collective-permute-start | bytes 196616 | tf_op jit(solution)/shard_map/ppermute | solution.py:202
  119.8 4.3 %collective-permute-start.21 = (bf16[4,64,128]{2,1,0:T(8,128)(2,1)S(1)}, bf16[4,64,128]{2,1,0:T(8,128)(2,1)S(1)}, u32[]{:S(2)}, u32[]{:S(2)}) collective-permute-start(bf16[4,64,128]{2,1,0:T(8,128)(2,1)S(1)} %add_convert_fusion.4), channel_id=1, source_target_pairs={{0,1},{1,0},{2,3},{3,2},{4,5},{5,4},{6,7},{7,6},{8,9},{9,8},{10,11... | collective-permute-start | bytes 196616 | tf_op jit(solution)/shard_map/ppermute | solution.py:202
  124.2 1.4 collective-permute-start.22
  133.7 4.3 %collective-permute-start.24 = (bf16[4,64,128]{2,1,0:T(8,128)(2,1)S(1)}, bf16[4,64,128]{2,1,0:T(8,128)(2,1)S(1)}, u32[]{:S(2)}, u32[]{:S(2)}) collective-permute-start(bf16[4,64,128]{2,1,0:T(8,128)(2,1)S(1)} %slice.57), channel_id=1, source_target_pairs={{0,1},{1,0},{2,3},{3,2},{4,5},{5,4},{6,7},{7,6},{8,9},{9,8},{10,11... | collective-permute-start | bytes 196616 | tf_op jit(solution)/shard_map/ppermute | solution.py:202
  138.1 4.3 %collective-permute-start.25 = (bf16[4,64,128]{2,1,0:T(8,128)(2,1)S(1)}, bf16[4,64,128]{2,1,0:T(8,128)(2,1)S(1)}, u32[]{:S(2)}, u32[]{:S(2)}) collective-permute-start(bf16[4,64,128]{2,1,0:T(8,128)(2,1)S(1)} %fusion.15), channel_id=1, source_target_pairs={{0,4},{4,0},{8,12},{12,8},{1,5},{5,1},{9,13},{13,9},{2,6},{6,2},{1... | collective-permute-start | bytes 196616 | tf_op jit(solution)/shard_map/ppermute | solution.py:202
  142.5 5.4 %collective-permute-start.26 = (bf16[4,64,128]{2,1,0:T(8,128)(2,1)S(1)}, bf16[4,64,128]{2,1,0:T(8,128)(2,1)S(1)}, u32[]{:S(2)}, u32[]{:S(2)}) collective-permute-start(bf16[4,64,128]{2,1,0:T(8,128)(2,1)S(1)} %add_convert_fusion.3), channel_id=1, source_target_pairs={{0,8},{4,12},{8,0},{12,4},{1,9},{5,13},{9,1},{13,5},{2,10},{6,14},... | collective-permute-start | bytes 196616 | tf_op jit(solution)/shard_map/ppermute | solution.py:202
  147.9 4.3 %collective-permute-start.27 = (bf16[4,64,128]{2,1,0:T(8,128)(2,1)S(1)}, bf16[4,64,128]{2,1,0:T(8,128)(2,1)S(1)}, u32[]{:S(2)}, u32[]{:S(2)}) collective-permute-start(bf16[4,64,128]{2,1,0:T(8,128)(2,1)S(1)} %add_convert_fusion.2), channel_id=1, source_target_pairs={{0,1},{1,0},{2,3},{3,2},{4,5},{5,4},{6,7},{7,6},{8,9},{9,8},{10,11... | collective-permute-start | bytes 196616 | tf_op jit(solution)/shard_map/ppermute | solution.py:202
  152.3 1.4 collective-permute-start.28
  160.4 1.4 collective-permute-start.29
  161.9 4.3 %collective-permute-start.30 = (bf16[4,64,128]{2,1,0:T(8,128)(2,1)S(1)}, bf16[4,64,128]{2,1,0:T(8,128)(2,1)S(1)}, u32[]{:S(2)}, u32[]{:S(2)}) collective-permute-start(bf16[4,64,128]{2,1,0:T(8,128)(2,1)S(1)} %slice.56), channel_id=1, source_target_pairs={{0,1},{1,0},{2,3},{3,2},{4,5},{5,4},{6,7},{7,6},{8,9},{9,8},{10,11... | collective-permute-start | bytes 196616 | tf_op jit(solution)/shard_map/ppermute | solution.py:202
  166.2 4.3 %collective-permute-start.31 = (bf16[4,64,128]{2,1,0:T(8,128)(2,1)S(1)}, bf16[4,64,128]{2,1,0:T(8,128)(2,1)S(1)}, u32[]{:S(2)}, u32[]{:S(2)}) collective-permute-start(bf16[4,64,128]{2,1,0:T(8,128)(2,1)S(1)} %fusion.14), channel_id=1, source_target_pairs={{0,4},{4,0},{8,12},{12,8},{1,5},{5,1},{9,13},{13,9},{2,6},{6,2},{1... | collective-permute-start | bytes 196616 | tf_op jit(solution)/shard_map/ppermute | solution.py:202
  170.6 5.4 %collective-permute-start.32 = (bf16[4,64,128]{2,1,0:T(8,128)(2,1)S(1)}, bf16[4,64,128]{2,1,0:T(8,128)(2,1)S(1)}, u32[]{:S(2)}, u32[]{:S(2)}) collective-permute-start(bf16[4,64,128]{2,1,0:T(8,128)(2,1)S(1)} %add_convert_fusion.1), channel_id=1, source_target_pairs={{0,8},{4,12},{8,0},{12,4},{1,9},{5,13},{9,1},{13,5},{2,10},{6,14},... | collective-permute-start | bytes 196616 | tf_op jit(solution)/shard_map/ppermute | solution.py:202
  176.0 4.3 %collective-permute-start.33 = (bf16[4,64,128]{2,1,0:T(8,128)(2,1)S(1)}, bf16[4,64,128]{2,1,0:T(8,128)(2,1)S(1)}, u32[]{:S(2)}, u32[]{:S(2)}) collective-permute-start(bf16[4,64,128]{2,1,0:T(8,128)(2,1)S(1)} %add_convert_fusion), channel_id=1, source_target_pairs={{0,1},{1,0},{2,3},{3,2},{4,5},{5,4},{6,7},{7,6},{8,9},{9,8},{10,11... | collective-permute-start | bytes 196616 | tf_op jit(solution)/shard_map/ppermute | solution.py:202
  (4 other events, 11.2 us)

commit v9 on v8

--- a/solution.py
+++ b/solution.py
@@ -254,11 +254,9 @@
                 pieces[offset] = from_xor(pieces[offset], ("z", "core"), offset)
 
     far = list(range(n_row // 2, n_row))
-    near = list(range(2, n_row // 2))
-    beside = [[1], near + far[:1]]
+    near = list(range(1, n_row // 2))
 
     def hold(value, offsets):
-        move(states, offsets)
         value, moved = lax.optimization_barrier((value, [pieces[o] for o in offsets]))
         for o, piece in zip(offsets, moved):
             pieces[o] = piece
@@ -270,19 +268,21 @@
     z = lax.dot_general(
         omega, states, (((0,), (1,)), ((), ())), preferred_element_type=jnp.float32
     )
+    move(states, far[:2] + [0])
     for bit in bits(n_col):
         z = z + from_xor(z, ("col",), bit)
     z = z.reshape(RANK, n_col, chunk).transpose(1, 0, 2)
     z_bits = bits(n_z)[::-1]
-    for k, bit in enumerate(z_bits):
-        z = hold(z, beside.pop(0)) if beside else z
+    z = jnp.concatenate([z, from_xor(z, ("z",), z_bits[0])])
+    z, slab = lax.optimization_barrier((z, states))
+    move(slab, far[2:])
+    z = hold(z, far[:1])
+    for bit in z_bits[1:]:
         z = jnp.concatenate([z, from_xor(z, ("z",), bit)])
-        if k == 0:
-            z, slab = lax.optimization_barrier((z, states))
-            move(slab, far[1:2])
-    z, slab = lax.optimization_barrier((z, states))
-    move(slab, far[2:] + [0] + [o for offsets in beside for o in offsets])
+    move(slab, near)
+    z = hold(z, far[1:2])
     z = z, from_xor(z, ("core",), 1)
+    z = hold(z, far[2:3])
     absolute_col = [("col", bit, False) for bit in bits(n_col)[::-1]]
     at_first = chunk_places([("z", bit, True) for bit in z_bits[::-1]] + absolute_col)
     relative_col = [("col", bit, True) for bit in bits(n_col)]

time: 189 us -> 187 us (0.989)
  starting transfers between devices: 38 us -> 25.5 us
  waiting for transfers between devices: 108 us -> 119 us
    ppermute x35, starting transfers between devices: 38 us -> 25.5 us  [from_xor(): return lax.ppermute(value, axis, [(i, i ^ offset) for i in range(size)])]
    ppermute x35, waiting for transfers between devices: 108 us -> 119 us  [from_xor(): return lax.ppermute(value, axis, [(i, i ^ offset) for i in range(size)])]
where the time goes in v9:
time: 187 us
  waiting for transfers between devices  119 us (64%)
  Pallas kernels  35.7 us (19%)
  starting transfers between devices  25.5 us (14%)
  matrix products  3.97 us (2%)
    ppermute x35, waiting for transfers between devices, from_xor(): return lax.ppermute(value, axis, [(i, i ^ offset) for i in range(size)])  119 us
    pallas_call x6, Pallas kernels, call(): pl.pallas_call(kernel, out_shape=out_shapes, in_specs=[pl.BlockSpec(memor...  35.7 us
    ppermute x35, starting transfers between devices, from_xor(): return lax.ppermute(value, axis, [(i, i ^ offset) for i in range(size)])  25.5 us
    dot_general x1, matrix products, per_device_transposed(): lax.dot_general(omega, states, (((0,), (1,)), ((), ())), preferred_elemen...  3.97 us
  transfers between devices with their start and end apart: 35, of which 28 were waited for; matrix products, arithmetic and copies ran while one was open for 1% of the time, Pallas kernels for 3%

profile of v9, /device:TPU:0, one launch (start us, length us, event | category | flops | bytes accessed | tf_op | source)
XLA Modules:
  0.0 187.2 jit_solution(17516175645085702555)
XLA Ops:
  1.3 4.0 %fusion = f32[64,256]{1,0:T(8,128)S(1)} fusion(bf16[256,4096]{1,0:T(8,128)(2,1)} %param.3, s32[]{:T(128)S(6)} %xor.84, s32[4096]{0:T(1024)S(1)} %add_multiply_fusion), kind=kOutput, calls=%fused_computation.1 | convolution fusion | flops 152043520 | bytes 2179076 | tf_op jit(solution)/shard_map/dot_general | solution.py:268
  5.3 3.0 %collective-permute-start = (f32[64,256]{1,0:T(8,128)S(1)}, f32[64,256]{1,0:T(8,128)S(1)}, u32[]{:S(2)}, u32[]{:S(2)}) collective-permute-start(f32[64,256]{1,0:T(8,128)S(1)} %fusion), channel_id=1, source_target_pairs={{0,1},{1,0},{2,3},{3,2},{4,5},{5,4},{6,7},{7,6},{8,9},{9,8},{10,11... | collective-permute-start | bytes 196616 | tf_op jit(solution)/shard_map/ppermute | solution.py:202
  8.4 2.7 %collective-permute-start.2 = (bf16[256,512]{1,0:T(8,128)(2,1)S(1)}, bf16[256,512]{1,0:T(8,128)(2,1)S(1)}, u32[]{:S(2)}, u32[]{:S(2)}) collective-permute-start(bf16[256,512]{1,0:T(8,128)(2,1)S(1)} %get-tuple-element.54), channel_id=1, source_target_pairs={{0,8},{2,10},{4,12},{6,14},{8,0},{10,2},{12,4},{14,6},{1,9},{3,11}... | collective-permute-start | bytes 786440 | tf_op jit(solution)/shard_map/ppermute | solution.py:202
  11.0 2.7 %collective-permute-start.1 = (f32[2,64,128]{2,1,0:T(8,128)S(1)}, f32[2,64,128]{2,1,0:T(8,128)S(1)}, u32[]{:S(2)}, u32[]{:S(2)}) collective-permute-start(f32[2,64,128]{2,1,0:T(8,128)S(1)} %bitcast_bitcast_fusion), channel_id=1, source_target_pairs={{0,8},{4,12},{8,0},{12,4},{1,9},{5,13},{9,1},{13,5},{2,10},{6,14},... | collective-permute-start | bytes 196616 | tf_op jit(solution)/shard_map/ppermute | solution.py:202
  13.7 18.6 %collective-permute-done.1 = f32[2,64,128]{2,1,0:T(8,128)S(1)} collective-permute-done((f32[2,64,128]{2,1,0:T(8,128)S(1)}, f32[2,64,128]{2,1,0:T(8,128)S(1)}, u32[]{:S(2)}, u32[]{:S(2)}) %collective-permute-start.1) | collective-permute-done | bytes 65568 | tf_op jit(solution)/shard_map/ppermute | solution.py:202
  32.6 2.5 %collective-permute-start.6 = (bf16[256,512]{1,0:T(8,128)(2,1)S(1)}, bf16[256,512]{1,0:T(8,128)(2,1)S(1)}, u32[]{:S(2)}, u32[]{:S(2)}) collective-permute-start(bf16[256,512]{1,0:T(8,128)(2,1)S(1)} %get-tuple-element.52), channel_id=1, source_target_pairs={{0,12},{2,14},{4,8},{6,10},{8,4},{10,6},{12,0},{14,2},{1,13},{3,15... | collective-permute-start | bytes 786440 | tf_op jit(solution)/shard_map/ppermute | solution.py:202
  35.0 10.1 %collective-permute-done.3 = f32[4,64,128]{2,1,0:T(8,128)S(1)} collective-permute-done((f32[4,64,128]{2,1,0:T(8,128)S(1)}, f32[4,64,128]{2,1,0:T(8,128)S(1)}, u32[]{:S(2)}, u32[]{:S(2)}) %collective-permute-start.3) | collective-permute-done | bytes 131104 | tf_op jit(solution)/shard_map/ppermute | solution.py:202
  45.3 3.6 %collective-permute-start.10 = (bf16[256,512]{1,0:T(8,128)(2,1)S(1)}, bf16[256,512]{1,0:T(8,128)(2,1)S(1)}, u32[]{:S(2)}, u32[]{:S(2)}) collective-permute-start(bf16[256,512]{1,0:T(8,128)(2,1)S(1)} %get-tuple-element.48), channel_id=1, source_target_pairs={{0,14},{2,12},{4,10},{6,8},{8,6},{10,4},{12,2},{14,0},{1,15},{3,13... | collective-permute-start | bytes 786440 | tf_op jit(solution)/shard_map/ppermute | solution.py:202
  50.8 6.3 %shard_map.41 = (bf16[64,2048]{1,0:T(8,128)(2,1)S(1)}, f32[64,64]{1,0:T(8,128)S(1)}) custom-call(s32[16]{0:T(128)S(1)} %fusion.20.at_ref, f32[8,64,128]{2,1,0:T(8,128)S(1)} %pad_maximum_fusion.z_ref, f32[8,64,128]{2,1,0:T(8,128)S(1)} %collective-permute-done.5.other_ref), custom_call_target="tpu_custom_call" | custom-call | flops 402653184 | bytes 524288 | tf_op jit(solution)/shard_map/pallas_call | solution.py:185
  57.1 4.3 %collective-permute-done.9.refs_3_ = bf16[256,512]{1,0:T(8,128)(2,1)S(1)} collective-permute-done((bf16[256,512]{1,0:T(8,128)(2,1)S(1)}, bf16[256,512]{1,0:T(8,128)(2,1)S(1)}, u32[]{:S(2)}, u32[]{:S(2)}) %collective-permute-start.9) | collective-permute-done | bytes 262176 | tf_op jit(solution)/shard_map/ppermute | solution.py:202
  61.4 5.6 %collective-permute-done.8.refs_2_ = bf16[256,512]{1,0:T(8,128)(2,1)S(1)} collective-permute-done((bf16[256,512]{1,0:T(8,128)(2,1)S(1)}, bf16[256,512]{1,0:T(8,128)(2,1)S(1)}, u32[]{:S(2)}, u32[]{:S(2)}) %collective-permute-start.8) | collective-permute-done | bytes 262176 | tf_op jit(solution)/shard_map/ppermute | solution.py:202
  67.1 1.8 shard_map.42
  71.1 5.0 %collective-permute-done.12 = f32[4,64,128]{2,1,0:T(8,128)S(1)} collective-permute-done((f32[4,64,128]{2,1,0:T(8,128)S(1)}, f32[4,64,128]{2,1,0:T(8,128)S(1)}, u32[]{:S(2)}, u32[]{:S(2)}) %collective-permute-start.12) | collective-permute-done | bytes 131104 | tf_op jit(solution)/shard_map/ppermute | solution.py:202
  77.8 3.3 %collective-permute-done.13 = f32[4,64,128]{2,1,0:T(8,128)S(1)} collective-permute-done((f32[4,64,128]{2,1,0:T(8,128)S(1)}, f32[4,64,128]{2,1,0:T(8,128)S(1)}, u32[]{:S(2)}, u32[]{:S(2)}) %collective-permute-start.13) | collective-permute-done | bytes 131104 | tf_op jit(solution)/shard_map/ppermute | solution.py:202
  81.8 6.7 %collective-permute-done.14 = f32[4,64,128]{2,1,0:T(8,128)S(1)} collective-permute-done((f32[4,64,128]{2,1,0:T(8,128)S(1)}, f32[4,64,128]{2,1,0:T(8,128)S(1)}, u32[]{:S(2)}, u32[]{:S(2)}) %collective-permute-start.14) | collective-permute-done | bytes 131104 | tf_op jit(solution)/shard_map/ppermute | solution.py:202
  89.1 4.5 %collective-permute-done.15 = f32[4,64,128]{2,1,0:T(8,128)S(1)} collective-permute-done((f32[4,64,128]{2,1,0:T(8,128)S(1)}, f32[4,64,128]{2,1,0:T(8,128)S(1)}, u32[]{:S(2)}, u32[]{:S(2)}) %collective-permute-start.15) | collective-permute-done | bytes 131104 | tf_op jit(solution)/shard_map/ppermute | solution.py:202
  95.2 7.4 %shard_map.43 = (f32[8,64,128]{2,1,0:T(8,128)S(1)}, bf16[8,64,128]{2,1,0:T(8,128)(2,1)S(1)}) custom-call(s32[16]{0:T(128)S(1)} %fusion.18.at_ref, f32[8,64,128]{2,1,0:T(8,128)S(1)} %pad_maximum_fusion.1.z_ref, f32[8,64,128]{2,1,0:T(8,128)S(1)} %collective-permute-done.16.other_ref, bf16[2048,512]{1,0:T(8,128)(2,1)S(1)} %get-tuple-element.34.a_ref), custom_call_target="tpu_custom_call" | custom-call | flops 671088640 | bytes 2621440 | tf_op jit(solution)/shard_map/pallas_call | solution.py:185
  104.7 3.8 %collective-permute-done.18 = bf16[4,64,128]{2,1,0:T(8,128)(2,1)S(1)} collective-permute-done((bf16[4,64,128]{2,1,0:T(8,128)(2,1)S(1)}, bf16[4,64,128]{2,1,0:T(8,128)(2,1)S(1)}, u32[]{:S(2)}, u32[]{:S(2)}) %collective-permute-start.18) | collective-permute-done | bytes 65568 | tf_op jit(solution)/shard_map/ppermute | solution.py:202
  108.9 3.9 %collective-permute-done.19 = bf16[4,64,128]{2,1,0:T(8,128)(2,1)S(1)} collective-permute-done((bf16[4,64,128]{2,1,0:T(8,128)(2,1)S(1)}, bf16[4,64,128]{2,1,0:T(8,128)(2,1)S(1)}, u32[]{:S(2)}, u32[]{:S(2)}) %collective-permute-start.19) | collective-permute-done | bytes 65568 | tf_op jit(solution)/shard_map/ppermute | solution.py:202
  113.1 5.4 %collective-permute-done.20 = bf16[4,64,128]{2,1,0:T(8,128)(2,1)S(1)} collective-permute-done((bf16[4,64,128]{2,1,0:T(8,128)(2,1)S(1)}, bf16[4,64,128]{2,1,0:T(8,128)(2,1)S(1)}, u32[]{:S(2)}, u32[]{:S(2)}) %collective-permute-start.20) | collective-permute-done | bytes 65568 | tf_op jit(solution)/shard_map/ppermute | solution.py:202
  119.1 3.7 %collective-permute-done.21 = bf16[4,64,128]{2,1,0:T(8,128)(2,1)S(1)} collective-permute-done((bf16[4,64,128]{2,1,0:T(8,128)(2,1)S(1)}, bf16[4,64,128]{2,1,0:T(8,128)(2,1)S(1)}, u32[]{:S(2)}, u32[]{:S(2)}) %collective-permute-start.21) | collective-permute-done | bytes 65568 | tf_op jit(solution)/shard_map/ppermute | solution.py:202
  124.3 6.7 %shard_map.44 = (f32[8,64,128]{2,1,0:T(8,128)S(1)}, bf16[8,64,128]{2,1,0:T(8,128)(2,1)S(1)}) custom-call(s32[16]{0:T(128)S(1)} %fusion.18.at_ref, bf16[8,64,128]{2,1,0:T(8,128)(2,1)S(1)} %pad_maximum_fusion.3.z_ref, bf16[8,64,128]{2,1,0:T(8,128)(2,1)S(1)} %collective-permute-done.22.other_ref, bf16[2048,512]{1,0:T(8,128)(2,1)S(1)} %get-tuple-element.34.a_ref), custom_call_target="tpu_custom_call" | custom-call | flops 671088640 | bytes 2359296 | tf_op jit(solution)/shard_map/pallas_call | solution.py:185
  133.1 3.7 %collective-permute-done.24 = bf16[4,64,128]{2,1,0:T(8,128)(2,1)S(1)} collective-permute-done((bf16[4,64,128]{2,1,0:T(8,128)(2,1)S(1)}, bf16[4,64,128]{2,1,0:T(8,128)(2,1)S(1)}, u32[]{:S(2)}, u32[]{:S(2)}) %collective-permute-start.24) | collective-permute-done | bytes 65568 | tf_op jit(solution)/shard_map/ppermute | solution.py:202
  136.9 4.3 %collective-permute-done.25 = bf16[4,64,128]{2,1,0:T(8,128)(2,1)S(1)} collective-permute-done((bf16[4,64,128]{2,1,0:T(8,128)(2,1)S(1)}, bf16[4,64,128]{2,1,0:T(8,128)(2,1)S(1)}, u32[]{:S(2)}, u32[]{:S(2)}) %collective-permute-start.25) | collective-permute-done | bytes 65568 | tf_op jit(solution)/shard_map/ppermute | solution.py:202
  141.3 5.3 %collective-permute-done.26 = bf16[4,64,128]{2,1,0:T(8,128)(2,1)S(1)} collective-permute-done((bf16[4,64,128]{2,1,0:T(8,128)(2,1)S(1)}, bf16[4,64,128]{2,1,0:T(8,128)(2,1)S(1)}, u32[]{:S(2)}, u32[]{:S(2)}) %collective-permute-start.26) | collective-permute-done | bytes 65568 | tf_op jit(solution)/shard_map/ppermute | solution.py:202
  147.2 3.7 %collective-permute-done.27 = bf16[4,64,128]{2,1,0:T(8,128)(2,1)S(1)} collective-permute-done((bf16[4,64,128]{2,1,0:T(8,128)(2,1)S(1)}, bf16[4,64,128]{2,1,0:T(8,128)(2,1)S(1)}, u32[]{:S(2)}, u32[]{:S(2)}) %collective-permute-start.27) | collective-permute-done | bytes 65568 | tf_op jit(solution)/shard_map/ppermute | solution.py:202
  152.3 6.7 %shard_map.45 = (f32[8,64,128]{2,1,0:T(8,128)S(1)}, bf16[8,64,128]{2,1,0:T(8,128)(2,1)S(1)}) custom-call(s32[16]{0:T(128)S(1)} %fusion.18.at_ref, bf16[8,64,128]{2,1,0:T(8,128)(2,1)S(1)} %pad_maximum_fusion.4.z_ref, bf16[8,64,128]{2,1,0:T(8,128)(2,1)S(1)} %collective-permute-done.28.other_ref, bf16[2048,512]{1,0:T(8,128)(2,1)S(1)} %get-tuple-element.34.a_ref), custom_call_target="tpu_custom_call" | custom-call | flops 671088640 | bytes 2359296 | tf_op jit(solution)/shard_map/pallas_call | solution.py:185
  161.1 3.7 %collective-permute-done.30 = bf16[4,64,128]{2,1,0:T(8,128)(2,1)S(1)} collective-permute-done((bf16[4,64,128]{2,1,0:T(8,128)(2,1)S(1)}, bf16[4,64,128]{2,1,0:T(8,128)(2,1)S(1)}, u32[]{:S(2)}, u32[]{:S(2)}) %collective-permute-start.30) | collective-permute-done | bytes 65568 | tf_op jit(solution)/shard_map/ppermute | solution.py:202
  165.0 4.3 %collective-permute-done.31 = bf16[4,64,128]{2,1,0:T(8,128)(2,1)S(1)} collective-permute-done((bf16[4,64,128]{2,1,0:T(8,128)(2,1)S(1)}, bf16[4,64,128]{2,1,0:T(8,128)(2,1)S(1)}, u32[]{:S(2)}, u32[]{:S(2)}) %collective-permute-start.31) | collective-permute-done | bytes 65568 | tf_op jit(solution)/shard_map/ppermute | solution.py:202
  169.3 5.3 %collective-permute-done.32 = bf16[4,64,128]{2,1,0:T(8,128)(2,1)S(1)} collective-permute-done((bf16[4,64,128]{2,1,0:T(8,128)(2,1)S(1)}, bf16[4,64,128]{2,1,0:T(8,128)(2,1)S(1)}, u32[]{:S(2)}, u32[]{:S(2)}) %collective-permute-start.32) | collective-permute-done | bytes 65568 | tf_op jit(solution)/shard_map/ppermute | solution.py:202
  175.2 3.7 %collective-permute-done.33 = bf16[4,64,128]{2,1,0:T(8,128)(2,1)S(1)} collective-permute-done((bf16[4,64,128]{2,1,0:T(8,128)(2,1)S(1)}, bf16[4,64,128]{2,1,0:T(8,128)(2,1)S(1)}, u32[]{:S(2)}, u32[]{:S(2)}) %collective-permute-start.33) | collective-permute-done | bytes 65568 | tf_op jit(solution)/shard_map/ppermute | solution.py:202
  180.4 6.8 %shard_map.46 = f32[64,512]{1,0:T(8,128)} custom-call(s32[16]{0:T(128)S(1)} %fusion.18.at_ref, bf16[8,64,128]{2,1,0:T(8,128)(2,1)S(1)} %pad_maximum_fusion.5.z_ref, bf16[8,64,128]{2,1,0:T(8,128)(2,1)S(1)} %collective-permute-done.34.other_ref, bf16[2048,512]{1,0:T(8,128)(2,1)S(1)} %get-tuple-element.34.a_ref), custom_call_target="tpu_custom_call" | custom-call | flops 671088640 | bytes 2359296 | tf_op jit(solution)/shard_map/pallas_call | solution.py:185
  (81 shorter events, 22.5 us)
Async XLA Ops:
  5.3 5.7 %collective-permute-start = (f32[64,256]{1,0:T(8,128)S(1)}, f32[64,256]{1,0:T(8,128)S(1)}, u32[]{:S(2)}, u32[]{:S(2)}) collective-permute-start(f32[64,256]{1,0:T(8,128)S(1)} %fusion), channel_id=1, source_target_pairs={{0,1},{1,0},{2,3},{3,2},{4,5},{5,4},{6,7},{7,6},{8,9},{9,8},{10,11... | collective-permute-start | bytes 196616 | tf_op jit(solution)/shard_map/ppermute | solution.py:202
  8.4 24.0 %collective-permute-start.2 = (bf16[256,512]{1,0:T(8,128)(2,1)S(1)}, bf16[256,512]{1,0:T(8,128)(2,1)S(1)}, u32[]{:S(2)}, u32[]{:S(2)}) collective-permute-start(bf16[256,512]{1,0:T(8,128)(2,1)S(1)} %get-tuple-element.54), channel_id=1, source_target_pairs={{0,8},{2,10},{4,12},{6,14},{8,0},{10,2},{12,4},{14,6},{1,9},{3,11}... | collective-permute-start | bytes 786440 | tf_op jit(solution)/shard_map/ppermute | solution.py:202
  11.0 21.3 %collective-permute-start.1 = (f32[2,64,128]{2,1,0:T(8,128)S(1)}, f32[2,64,128]{2,1,0:T(8,128)S(1)}, u32[]{:S(2)}, u32[]{:S(2)}) collective-permute-start(f32[2,64,128]{2,1,0:T(8,128)S(1)} %bitcast_bitcast_fusion), channel_id=1, source_target_pairs={{0,8},{4,12},{8,0},{12,4},{1,9},{5,13},{9,1},{13,5},{2,10},{6,14},... | collective-permute-start | bytes 196616 | tf_op jit(solution)/shard_map/ppermute | solution.py:202
  13.7 31.5 %collective-permute-start.4 = (bf16[256,512]{1,0:T(8,128)(2,1)S(1)}, bf16[256,512]{1,0:T(8,128)(2,1)S(1)}, u32[]{:S(2)}, u32[]{:S(2)}) collective-permute-start(bf16[256,512]{1,0:T(8,128)(2,1)S(1)} %get-tuple-element.55), channel_id=1, source_target_pairs={{0,10},{2,8},{4,14},{6,12},{8,2},{10,0},{12,6},{14,4},{1,11},{3,9}... | collective-permute-start | bytes 786440 | tf_op jit(solution)/shard_map/ppermute | solution.py:202
  32.3 12.9 %collective-permute-start.3 = (f32[4,64,128]{2,1,0:T(8,128)S(1)}, f32[4,64,128]{2,1,0:T(8,128)S(1)}, u32[]{:S(2)}, u32[]{:S(2)}) collective-permute-start(f32[4,64,128]{2,1,0:T(8,128)S(1)} %pad_maximum_fusion.2), channel_id=1, source_target_pairs={{0,4},{4,0},{8,12},{12,8},{1,5},{5,1},{9,13},{13,9},{2,6},{6,2},{1... | collective-permute-start | bytes 393224 | tf_op jit(solution)/shard_map/ppermute | solution.py:202
  32.6 18.0 %collective-permute-start.6 = (bf16[256,512]{1,0:T(8,128)(2,1)S(1)}, bf16[256,512]{1,0:T(8,128)(2,1)S(1)}, u32[]{:S(2)}, u32[]{:S(2)}) collective-permute-start(bf16[256,512]{1,0:T(8,128)(2,1)S(1)} %get-tuple-element.52), channel_id=1, source_target_pairs={{0,12},{2,14},{4,8},{6,10},{8,4},{10,6},{12,0},{14,2},{1,13},{3,15... | collective-permute-start | bytes 786440 | tf_op jit(solution)/shard_map/ppermute | solution.py:202
  45.2 5.6 %collective-permute-start.5 = (f32[8,64,128]{2,1,0:T(8,128)S(1)}, f32[8,64,128]{2,1,0:T(8,128)S(1)}, u32[]{:S(2)}, u32[]{:S(2)}) collective-permute-start(f32[8,64,128]{2,1,0:T(8,128)S(1)} %pad_maximum_fusion.z_ref), channel_id=1, source_target_pairs={{0,2},{2,0},{1,3},{3,1},{4,6},{6,4},{5,7},{7,5},{8,10},{10,8},{9,1... | collective-permute-start | bytes 786440 | tf_op jit(solution)/shard_map/ppermute | solution.py:202
  45.3 11.8 %collective-permute-start.10 = (bf16[256,512]{1,0:T(8,128)(2,1)S(1)}, bf16[256,512]{1,0:T(8,128)(2,1)S(1)}, u32[]{:S(2)}, u32[]{:S(2)}) collective-permute-start(bf16[256,512]{1,0:T(8,128)(2,1)S(1)} %get-tuple-element.48), channel_id=1, source_target_pairs={{0,14},{2,12},{4,10},{6,8},{8,6},{10,4},{12,2},{14,0},{1,15},{3,13... | collective-permute-start | bytes 786440 | tf_op jit(solution)/shard_map/ppermute | solution.py:202
  48.9 12.6 %collective-permute-start.9 = (bf16[256,512]{1,0:T(8,128)(2,1)S(1)}, bf16[256,512]{1,0:T(8,128)(2,1)S(1)}, u32[]{:S(2)}, u32[]{:S(2)}) collective-permute-start(bf16[256,512]{1,0:T(8,128)(2,1)S(1)} %get-tuple-element.49), channel_id=1, source_target_pairs={{0,6},{2,4},{4,2},{6,0},{8,14},{10,12},{12,10},{14,8},{1,7},{3,5},... | collective-permute-start | bytes 786440 | tf_op jit(solution)/shard_map/ppermute | solution.py:202
  48.9 18.2 %collective-permute-start.8 = (bf16[256,512]{1,0:T(8,128)(2,1)S(1)}, bf16[256,512]{1,0:T(8,128)(2,1)S(1)}, u32[]{:S(2)}, u32[]{:S(2)}) collective-permute-start(bf16[256,512]{1,0:T(8,128)(2,1)S(1)} %get-tuple-element.50), channel_id=1, source_target_pairs={{0,4},{2,6},{4,0},{6,2},{8,12},{10,14},{12,8},{14,10},{1,5},{3,7},... | collective-permute-start | bytes 786440 | tf_op jit(solution)/shard_map/ppermute | solution.py:202
  50.6 16.5 %collective-permute-start.7 = (bf16[256,512]{1,0:T(8,128)(2,1)S(1)}, bf16[256,512]{1,0:T(8,128)(2,1)S(1)}, u32[]{:S(2)}, u32[]{:S(2)}) collective-permute-start(bf16[256,512]{1,0:T(8,128)(2,1)S(1)} %get-tuple-element.51), channel_id=1, source_target_pairs={{0,2},{2,0},{4,6},{6,4},{8,10},{10,8},{12,14},{14,12},{1,3},{3,1},... | collective-permute-start | bytes 786440 | tf_op jit(solution)/shard_map/ppermute | solution.py:202
  68.9 1.6 collective-permute-start.11
  70.5 5.6 %collective-permute-start.12 = (f32[4,64,128]{2,1,0:T(8,128)S(1)}, f32[4,64,128]{2,1,0:T(8,128)S(1)}, u32[]{:S(2)}, u32[]{:S(2)}) collective-permute-start(f32[4,64,128]{2,1,0:T(8,128)S(1)} %slice.36), channel_id=1, source_target_pairs={{0,1},{1,0},{2,3},{3,2},{4,5},{5,4},{6,7},{7,6},{8,9},{9,8},{10,11... | collective-permute-start | bytes 393224 | tf_op jit(solution)/shard_map/ppermute | solution.py:202
  76.1 5.0 %collective-permute-start.13 = (f32[4,64,128]{2,1,0:T(8,128)S(1)}, f32[4,64,128]{2,1,0:T(8,128)S(1)}, u32[]{:S(2)}, u32[]{:S(2)}) collective-permute-start(f32[4,64,128]{2,1,0:T(8,128)S(1)} %slice_add_fusion.3), channel_id=1, source_target_pairs={{0,4},{4,0},{8,12},{12,8},{1,5},{5,1},{9,13},{13,9},{2,6},{6,2},{1... | collective-permute-start | bytes 393224 | tf_op jit(solution)/shard_map/ppermute | solution.py:202
  81.2 7.3 %collective-permute-start.14 = (f32[4,64,128]{2,1,0:T(8,128)S(1)}, f32[4,64,128]{2,1,0:T(8,128)S(1)}, u32[]{:S(2)}, u32[]{:S(2)}) collective-permute-start(f32[4,64,128]{2,1,0:T(8,128)S(1)} %add.245), channel_id=1, source_target_pairs={{0,8},{4,12},{8,0},{12,4},{1,9},{5,13},{9,1},{13,5},{2,10},{6,14},... | collective-permute-start | bytes 393224 | tf_op jit(solution)/shard_map/ppermute | solution.py:202
  88.6 5.0 %collective-permute-start.15 = (f32[4,64,128]{2,1,0:T(8,128)S(1)}, f32[4,64,128]{2,1,0:T(8,128)S(1)}, u32[]{:S(2)}, u32[]{:S(2)}) collective-permute-start(f32[4,64,128]{2,1,0:T(8,128)S(1)} %add.246), channel_id=1, source_target_pairs={{0,1},{1,0},{2,3},{3,2},{4,5},{5,4},{6,7},{7,6},{8,9},{9,8},{10,11... | collective-permute-start | bytes 393224 | tf_op jit(solution)/shard_map/ppermute | solution.py:202
  93.6 1.6 collective-permute-start.16
  104.1 4.3 %collective-permute-start.18 = (bf16[4,64,128]{2,1,0:T(8,128)(2,1)S(1)}, bf16[4,64,128]{2,1,0:T(8,128)(2,1)S(1)}, u32[]{:S(2)}, u32[]{:S(2)}) collective-permute-start(bf16[4,64,128]{2,1,0:T(8,128)(2,1)S(1)} %slice.58), channel_id=1, source_target_pairs={{0,1},{1,0},{2,3},{3,2},{4,5},{5,4},{6,7},{7,6},{8,9},{9,8},{10,11... | collective-permute-start | bytes 196616 | tf_op jit(solution)/shard_map/ppermute | solution.py:202
  108.5 4.3 %collective-permute-start.19 = (bf16[4,64,128]{2,1,0:T(8,128)(2,1)S(1)}, bf16[4,64,128]{2,1,0:T(8,128)(2,1)S(1)}, u32[]{:S(2)}, u32[]{:S(2)}) collective-permute-start(bf16[4,64,128]{2,1,0:T(8,128)(2,1)S(1)} %fusion.16), channel_id=1, source_target_pairs={{0,4},{4,0},{8,12},{12,8},{1,5},{5,1},{9,13},{13,9},{2,6},{6,2},{1... | collective-permute-start | bytes 196616 | tf_op jit(solution)/shard_map/ppermute | solution.py:202
  112.8 5.7 %collective-permute-start.20 = (bf16[4,64,128]{2,1,0:T(8,128)(2,1)S(1)}, bf16[4,64,128]{2,1,0:T(8,128)(2,1)S(1)}, u32[]{:S(2)}, u32[]{:S(2)}) collective-permute-start(bf16[4,64,128]{2,1,0:T(8,128)(2,1)S(1)} %add_convert_fusion.5), channel_id=1, source_target_pairs={{0,8},{4,12},{8,0},{12,4},{1,9},{5,13},{9,1},{13,5},{2,10},{6,14},... | collective-permute-start | bytes 196616 | tf_op jit(solution)/shard_map/ppermute | solution.py:202
  118.5 4.3 %collective-permute-start.21 = (bf16[4,64,128]{2,1,0:T(8,128)(2,1)S(1)}, bf16[4,64,128]{2,1,0:T(8,128)(2,1)S(1)}, u32[]{:S(2)}, u32[]{:S(2)}) collective-permute-start(bf16[4,64,128]{2,1,0:T(8,128)(2,1)S(1)} %add_convert_fusion.4), channel_id=1, source_target_pairs={{0,1},{1,0},{2,3},{3,2},{4,5},{5,4},{6,7},{7,6},{8,9},{9,8},{10,11... | collective-permute-start | bytes 196616 | tf_op jit(solution)/shard_map/ppermute | solution.py:202
  122.9 1.4 collective-permute-start.22
  131.0 1.4 collective-permute-start.23
  132.5 4.3 %collective-permute-start.24 = (bf16[4,64,128]{2,1,0:T(8,128)(2,1)S(1)}, bf16[4,64,128]{2,1,0:T(8,128)(2,1)S(1)}, u32[]{:S(2)}, u32[]{:S(2)}) collective-permute-start(bf16[4,64,128]{2,1,0:T(8,128)(2,1)S(1)} %slice.57), channel_id=1, source_target_pairs={{0,1},{1,0},{2,3},{3,2},{4,5},{5,4},{6,7},{7,6},{8,9},{9,8},{10,11... | collective-permute-start | bytes 196616 | tf_op jit(solution)/shard_map/ppermute | solution.py:202
  136.8 4.3 %collective-permute-start.25 = (bf16[4,64,128]{2,1,0:T(8,128)(2,1)S(1)}, bf16[4,64,128]{2,1,0:T(8,128)(2,1)S(1)}, u32[]{:S(2)}, u32[]{:S(2)}) collective-permute-start(bf16[4,64,128]{2,1,0:T(8,128)(2,1)S(1)} %fusion.15), channel_id=1, source_target_pairs={{0,4},{4,0},{8,12},{12,8},{1,5},{5,1},{9,13},{13,9},{2,6},{6,2},{1... | collective-permute-start | bytes 196616 | tf_op jit(solution)/shard_map/ppermute | solution.py:202
  141.2 5.4 %collective-permute-start.26 = (bf16[4,64,128]{2,1,0:T(8,128)(2,1)S(1)}, bf16[4,64,128]{2,1,0:T(8,128)(2,1)S(1)}, u32[]{:S(2)}, u32[]{:S(2)}) collective-permute-start(bf16[4,64,128]{2,1,0:T(8,128)(2,1)S(1)} %add_convert_fusion.3), channel_id=1, source_target_pairs={{0,8},{4,12},{8,0},{12,4},{1,9},{5,13},{9,1},{13,5},{2,10},{6,14},... | collective-permute-start | bytes 196616 | tf_op jit(solution)/shard_map/ppermute | solution.py:202
  146.6 4.3 %collective-permute-start.27 = (bf16[4,64,128]{2,1,0:T(8,128)(2,1)S(1)}, bf16[4,64,128]{2,1,0:T(8,128)(2,1)S(1)}, u32[]{:S(2)}, u32[]{:S(2)}) collective-permute-start(bf16[4,64,128]{2,1,0:T(8,128)(2,1)S(1)} %add_convert_fusion.2), channel_id=1, source_target_pairs={{0,1},{1,0},{2,3},{3,2},{4,5},{5,4},{6,7},{7,6},{8,9},{9,8},{10,11... | collective-permute-start | bytes 196616 | tf_op jit(solution)/shard_map/ppermute | solution.py:202
  150.9 1.4 collective-permute-start.28
  160.5 4.3 %collective-permute-start.30 = (bf16[4,64,128]{2,1,0:T(8,128)(2,1)S(1)}, bf16[4,64,128]{2,1,0:T(8,128)(2,1)S(1)}, u32[]{:S(2)}, u32[]{:S(2)}) collective-permute-start(bf16[4,64,128]{2,1,0:T(8,128)(2,1)S(1)} %slice.56), channel_id=1, source_target_pairs={{0,1},{1,0},{2,3},{3,2},{4,5},{5,4},{6,7},{7,6},{8,9},{9,8},{10,11... | collective-permute-start | bytes 196616 | tf_op jit(solution)/shard_map/ppermute | solution.py:202
  164.9 4.3 %collective-permute-start.31 = (bf16[4,64,128]{2,1,0:T(8,128)(2,1)S(1)}, bf16[4,64,128]{2,1,0:T(8,128)(2,1)S(1)}, u32[]{:S(2)}, u32[]{:S(2)}) collective-permute-start(bf16[4,64,128]{2,1,0:T(8,128)(2,1)S(1)} %fusion.14), channel_id=1, source_target_pairs={{0,4},{4,0},{8,12},{12,8},{1,5},{5,1},{9,13},{13,9},{2,6},{6,2},{1... | collective-permute-start | bytes 196616 | tf_op jit(solution)/shard_map/ppermute | solution.py:202
  169.2 5.4 %collective-permute-start.32 = (bf16[4,64,128]{2,1,0:T(8,128)(2,1)S(1)}, bf16[4,64,128]{2,1,0:T(8,128)(2,1)S(1)}, u32[]{:S(2)}, u32[]{:S(2)}) collective-permute-start(bf16[4,64,128]{2,1,0:T(8,128)(2,1)S(1)} %add_convert_fusion.1), channel_id=1, source_target_pairs={{0,8},{4,12},{8,0},{12,4},{1,9},{5,13},{9,1},{13,5},{2,10},{6,14},... | collective-permute-start | bytes 196616 | tf_op jit(solution)/shard_map/ppermute | solution.py:202
  174.6 4.3 %collective-permute-start.33 = (bf16[4,64,128]{2,1,0:T(8,128)(2,1)S(1)}, bf16[4,64,128]{2,1,0:T(8,128)(2,1)S(1)}, u32[]{:S(2)}, u32[]{:S(2)}) collective-permute-start(bf16[4,64,128]{2,1,0:T(8,128)(2,1)S(1)} %add_convert_fusion), channel_id=1, source_target_pairs={{0,1},{1,0},{2,3},{3,2},{4,5},{5,4},{6,7},{7,6},{8,9},{9,8},{10,11... | collective-permute-start | bytes 196616 | tf_op jit(solution)/shard_map/ppermute | solution.py:202
  (4 other events, 11.2 us)

commit v10 on v9

--- a/solution.py
+++ b/solution.py
@@ -134,63 +134,69 @@
 
 
 def wide_of(at_ref, z_refs):
-    half = z_refs[0].shape[0]
-    n_col = at_ref.shape[0] // half
-    chunks = [z_refs[i // n_col % 2][at_ref[i]] for i in range(at_ref.shape[0])]
+    chunks = [z_ref[at_ref[i]] for z_ref in z_refs for i in range(at_ref.shape[0])]
     return jnp.concatenate(chunks, axis=1)
 
 
-def narrow_basis(at_ref, z_refs):
+def first_pass(at_ref, z_refs):
     wide = wide_of(at_ref, z_refs)
     upper, inverse_one = eliminate(shifted(gram_of(wide)))
-    first = small_times_wide(inverse_one, wide)
+    return small_times_wide(inverse_one, wide), upper
+
+
+def back_product(at_ref, z_refs, a):
+    first, unused = first_pass(at_ref, z_refs)
+    rank = first.shape[0]
+    back = dot_nn(jnp.concatenate(terms_of(first), axis=0), a)
+    back = back[:rank] + (back[rank : 2 * rank] + back[2 * rank :])
     unused, inverse_two = eliminate(gram_of(first))
-    return small_times_wide(inverse_two, first).astype(jnp.bfloat16), upper
-
-
-def power_body(basis, a, at_ref, part_refs):
-    weights = dot_nn(basis, a).astype(jnp.bfloat16)
-    forth = dot_nt(weights, a)
-    half, unused, width = part_refs[0].shape
-    n_col = at_ref.shape[0] // half
-    for i in range(2 * half):
-        target = part_refs[i // n_col % 2]
-        target[at_ref[i]] = forth[:, width * i : width * (i + 1)].astype(target.dtype)
+    return small_times_wide(inverse_two, back)
+
+
+def forth_product(weights, a_ref, at_ref, part_ref):
+    chunks, unused, width = part_ref.shape
+    forth = dot_nt(weights.astype(jnp.bfloat16), a_ref[: chunks * width, :])
+    for i in range(chunks):
+        part_ref[at_ref[i]] = forth[:, width * i : width * (i + 1)]
 
 
 def orth_kernel(at_ref, z_ref, other_ref, basis_ref, upper_ref):
-    basis_ref[...], upper_ref[...] = narrow_basis(at_ref, (z_ref, other_ref))
+    first, upper = first_pass(at_ref, (z_ref, other_ref))
+    unused, inverse_two = eliminate(gram_of(first))
+    basis_ref[...] = small_times_wide(inverse_two, first).astype(jnp.bfloat16)
+    upper_ref[...] = upper
 
 
 def power_kernel(at_ref, basis_ref, *refs):
-    piece_refs, a_ref, part_refs = refs[:-3], refs[-3], refs[-2:]
+    piece_refs, a_ref, part_ref = refs[:-2], refs[-2], refs[-1]
     rows = piece_refs[0].shape[0]
     for s, piece_ref in enumerate(piece_refs):
         a_ref[rows * s : rows * (s + 1), :] = piece_ref[...]
-    power_body(basis_ref[...], a_ref[...], at_ref, part_refs)
-
-
-def orth_power_kernel(at_ref, z_ref, other_ref, a_ref, *part_refs):
-    basis, unused = narrow_basis(at_ref, (z_ref, other_ref))
-    power_body(basis, a_ref[...], at_ref, part_refs)
-
-
-def last_kernel(at_ref, z_ref, other_ref, a_ref, out_ref):
-    basis, unused = narrow_basis(at_ref, (z_ref, other_ref))
-    out_ref[...] = dot_nn(basis, a_ref[...])
-
-
-def call(kernel, out_shapes, flops, at, *operands):
+    forth_product(dot_nn(basis_ref[...], a_ref[...]), a_ref, at_ref, part_ref)
+
+
+def orth_power_kernel(at_ref, z_ref, other_ref, a_ref, part_ref):
+    weights = back_product(at_ref, (z_ref, other_ref), a_ref[...])
+    forth_product(weights, a_ref, at_ref, part_ref)
+
+
+def last_kernel(at_ref, core_ref, z_ref, other_ref, a_ref, out_ref):
+    cols = out_ref.shape[1]
+    start = pl.multiple_of(core_ref[0] * cols, cols)
+    out_ref[...] = back_product(at_ref, (z_ref, other_ref), a_ref[:, pl.ds(start, cols)])
+
+
+def call(kernel, out_shapes, flops, scalars, *operands):
     moved = sum(x.size * x.dtype.itemsize for x in operands)
     return pl.pallas_call(
         kernel,
         out_shape=out_shapes,
-        in_specs=[pl.BlockSpec(memory_space=pltpu.SMEM)]
+        in_specs=[pl.BlockSpec(memory_space=pltpu.SMEM)] * len(scalars)
         + [pl.BlockSpec(memory_space=pltpu.VMEM)] * len(operands),
         out_specs=jax.tree.map(lambda _: pl.BlockSpec(memory_space=pltpu.VMEM), out_shapes),
         compiler_params=pltpu.CompilerParams(vmem_limit_bytes=40 * 1024 * 1024),
         cost_estimate=pl.CostEstimate(flops=flops, bytes_accessed=moved, transcendentals=0),
-    )(at, *operands)
+    )(*scalars, *operands)
 
 
 def bits(size):
@@ -202,8 +208,7 @@
     return lax.ppermute(value, axis, [(i, i ^ offset) for i in range(size)])
 
 
-def sum_parts(keep, send, dtype):
-    total = keep + from_xor(send, ("core",), 1).astype(jnp.float32)
+def sum_parts(total, dtype):
     for bit in bits(lax.axis_size("col")):
         half = total.shape[0] // 2
         other = from_xor(total[half:].astype(dtype), ("col",), bit)
@@ -222,10 +227,10 @@
 
 def chunk_places(digits):
     n_z, n_col = lax.axis_size("z"), lax.axis_size("col")
-    index = jnp.arange(n_z * 2 * n_col, dtype=jnp.int32)
+    index = jnp.arange(n_z * n_col, dtype=jnp.int32)
     z_at, col_at = lax.axis_index("z"), lax.axis_index("col")
     column = index % n_col
-    relative = {"z": index // (2 * n_col), "col": column ^ col_at}
+    relative = {"z": index // n_col, "col": column ^ col_at}
     absolute = {"z": relative["z"] ^ z_at, "col": column}
     place = jnp.zeros_like(index)
     for axis, bit, is_relative in digits:
@@ -239,78 +244,65 @@
     rows_local, width_local = states.shape
     rows_total, width_total = rows_local * n_row, width_local * n_col
     chunk = rows_local // n_col
-    cols = width_local // n_row
-    half = n_z * n_col
-    row = lax.axis_index("z") * n_core + lax.axis_index("core")
-    pieces = [None] * n_row
-
-    def block(slab, offset):
-        return lax.dynamic_slice_in_dim(slab, (row ^ offset) * cols, cols, 1)
-
-    def move(slab, offsets):
-        for offset in offsets:
-            pieces[offset] = block(slab, offset)
-            if offset:
-                pieces[offset] = from_xor(pieces[offset], ("z", "core"), offset)
-
-    far = list(range(n_row // 2, n_row))
-    near = list(range(1, n_row // 2))
-
-    def hold(value, offsets):
-        value, moved = lax.optimization_barrier((value, [pieces[o] for o in offsets]))
-        for o, piece in zip(offsets, moved):
-            pieces[o] = piece
-        return value
-
-    col = lax.axis_index("col")
+    cols = width_local // n_z
+    chunks = n_z * n_col
+    z_at, col = lax.axis_index("z"), lax.axis_index("col")
+    pieces = {}
+
+    def move(slab, offset):
+        block = lax.dynamic_slice_in_dim(slab, (z_at ^ offset) * cols, cols, 1)
+        pieces[offset] = from_xor(block, ("z",), offset) if offset else block
+
     feature_index = col * width_local + jnp.arange(width_local, dtype=jnp.int32)
     omega = sketch_table(sketch_base[0], feature_index, RANK)
     z = lax.dot_general(
         omega, states, (((0,), (1,)), ((), ())), preferred_element_type=jnp.float32
     )
-    move(states, far[:2] + [0])
+    z_bits = bits(n_z)[::-1]
+    far = z_bits[0]
+    move(states, 0)
+    move(states, far)
     for bit in bits(n_col):
         z = z + from_xor(z, ("col",), bit)
     z = z.reshape(RANK, n_col, chunk).transpose(1, 0, 2)
-    z_bits = bits(n_z)[::-1]
-    z = jnp.concatenate([z, from_xor(z, ("z",), z_bits[0])])
+    z = jnp.concatenate([z, from_xor(z, ("z",), far)])
     z, slab = lax.optimization_barrier((z, states))
-    move(slab, far[2:])
-    z = hold(z, far[:1])
+    for offset in sorted(set(range(1, n_z)) - {far}, reverse=True):
+        move(slab, offset)
+    z, pieces[far] = lax.optimization_barrier((z, pieces[far]))
     for bit in z_bits[1:]:
         z = jnp.concatenate([z, from_xor(z, ("z",), bit)])
-    move(slab, near)
-    z = hold(z, far[1:2])
     z = z, from_xor(z, ("core",), 1)
-    z = hold(z, far[2:3])
     absolute_col = [("col", bit, False) for bit in bits(n_col)[::-1]]
     at_first = chunk_places([("z", bit, True) for bit in z_bits[::-1]] + absolute_col)
     relative_col = [("col", bit, True) for bit in bits(n_col)]
     at = chunk_places(relative_col + [("z", bit, False) for bit in z_bits])
+    early = [0, far]
+    late = [offset for offset in range(n_z) if offset not in early]
+    others = {offset: from_xor(pieces[offset], ("core",), 1) for offset in early}
 
     f32 = jnp.float32
     square = jax.ShapeDtypeStruct((RANK, RANK), f32)
     wide = jax.ShapeDtypeStruct((RANK, rows_total), jnp.bfloat16)
+    slab = jax.ShapeDtypeStruct((rows_total, cols), states.dtype)
+    parts = jax.ShapeDtypeStruct((chunks, RANK, chunk), f32)
+    loadings = jax.ShapeDtypeStruct((RANK, cols // n_core), f32)
     orth_flops = 8 * 64 * 64 * rows_total * 6
-    power_flops = 4 * 64 * rows_total * cols
-
-    def sent_as(dtype):
-        shape = (half, RANK, chunk)
-        return jax.ShapeDtypeStruct(shape, f32), jax.ShapeDtypeStruct(shape, dtype)
-
-    basis, upper = call(orth_kernel, (wide, square), orth_flops, at_first, *z)
+    flops = orth_flops + 4 * 64 * rows_total * cols
+
+    basis, upper = call(orth_kernel, (wide, square), orth_flops, (at_first,), *z)
+    basis, moved = lax.optimization_barrier((basis, [pieces[offset] for offset in late]))
+    pieces.update(zip(late, moved))
+    others.update((offset, from_xor(pieces[offset], ("core",), 1)) for offset in late)
+    blocks = [half[offset] for half in (pieces, others) for offset in range(n_z)]
     factor = upper.T * (1.0 / math.sqrt(rows_total * width_total))
-    dtype = f32
-    slab = jax.ShapeDtypeStruct((rows_total, cols), states.dtype)
-    a, *parts = call(power_kernel, (slab,) + sent_as(dtype), power_flops, at, basis, *pieces)
+    a, total = call(power_kernel, (slab, parts), flops, (at,), basis, *blocks)
+    z = gather_parts(sum_parts(total, f32))
     for step in range(POWER - 1):
-        z = gather_parts(sum_parts(*parts, dtype))
-        dtype = jnp.bfloat16
-        flops = orth_flops + power_flops
-        parts = call(orth_power_kernel, sent_as(dtype), flops, at, *z, a)
-    z = gather_parts(sum_parts(*parts, dtype))
-    loadings = jax.ShapeDtypeStruct((RANK, cols), f32)
-    return call(last_kernel, loadings, orth_flops + power_flops, at, *z, a).T, factor
+        total = call(orth_power_kernel, parts, flops, (at,), *z, a)
+        z = gather_parts(sum_parts(total, jnp.bfloat16))
+    core = lax.axis_index("core")[None].astype(jnp.int32)
+    return call(last_kernel, loadings, flops, (at, core), *z, a).T, factor
 
 
 def local_gram(basis):

time: 187 us -> 182 us (0.973)
  waiting for transfers between devices: 119 us -> 105 us
  starting transfers between devices: 25.5 us -> 30.1 us
  local copies, waits for them, and re-layouts: 0.97 us -> 5.26 us
    ppermute x35 -> x31, waiting for transfers between devices: 119 us -> 105 us  [from_xor(): return lax.ppermute(value, axis, [(i, i ^ offset) for i in range(size)])]
    ppermute x35 -> x31, starting transfers between devices: 25.5 us -> 30.1 us  [from_xor(): return lax.ppermute(value, axis, [(i, i ^ offset) for i in range(size)])]
    unnamed x3 -> x8, local copies, waits for them, and re-layouts: 0.7 us -> 2.91 us
    dynamic_slice x2, local copies, waits for them, and re-layouts: 0.22 us -> 2.3 us  [move(): block = lax.dynamic_slice_in_dim(slab, (z_at ^ offset) * cols, cols, 1)]
  transfers between devices with their start and end apart: 35 -> 31, of which waited for: 28 -> 28; matrix products, arithmetic and copies ran while one was open for 1% -> 2% of each run, Pallas kernels for 3% -> 3%
where the time goes in v10:
time: 182 us
  waiting for transfers between devices  105 us (58%)
  Pallas kernels  37.2 us (20%)
  starting transfers between devices  30.1 us (17%)
  local copies, waits for them, and re-layouts  5.26 us (3%)
  matrix products  2.24 us (1%)
    ppermute x31, waiting for transfers between devices, from_xor(): return lax.ppermute(value, axis, [(i, i ^ offset) for i in range(size)])  105 us
    pallas_call x6, Pallas kernels, call(): pl.pallas_call(kernel, out_shape=out_shapes, in_specs=[pl.BlockSpec(memor...  37.2 us
    ppermute x31, starting transfers between devices, from_xor(): return lax.ppermute(value, axis, [(i, i ^ offset) for i in range(size)])  30.1 us
  transfers between devices with their start and end apart: 31, of which 28 were waited for; matrix products, arithmetic and copies ran while one was open for 2% of the time, Pallas kernels for 3%

profile of v10, /device:TPU:0, one launch (start us, length us, event | category | flops | bytes accessed | tf_op | source)
XLA Modules:
  0.0 182.2 jit_solution(6415455809373949790)
XLA Ops:
  0.7 2.2 %constant_dynamic-slice_fusion = (bf16[256,1024]{1,0:T(8,128)(2,1)S(1)}, bf16[256,1024]{1,0:T(8,128)(2,1)}) fusion(bf16[256,4096]{1,0:T(8,128)(2,1)} %param.3, s32[]{:T(128)S(6)} %select_n.78, s32[]{:T(128)S(6)} %select_n.75), kind=kLoop, calls=%fused_computation.66 | loop fusion | bytes 2097160 | tf_op jit(solution)/shard_map/dynamic_slice | solution.py:253
  2.9 4.0 %collective-permute-start.2 = (bf16[256,1024]{1,0:T(8,128)(2,1)}, bf16[256,1024]{1,0:T(8,128)(2,1)S(1)}, u32[]{:S(2)}, u32[]{:S(2)}) collective-permute-start(bf16[256,1024]{1,0:T(8,128)(2,1)} %get-tuple-element.31), channel_id=1, source_target_pairs={{0,8},{4,12},{8,0},{12,4},{1,9},{5,13},{9,1},{13,5},{2,10},{6,14},... | collective-permute-start | bytes 1572872 | tf_op jit(solution)/shard_map/ppermute | solution.py:208
  7.6 2.2 %fusion = f32[64,256]{1,0:T(8,128)S(1)} fusion(bf16[256,4096]{1,0:T(8,128)(2,1)S(1)} %copy-done.2, s32[]{:T(128)S(6)} %xor.72, s32[4096]{0:T(1024)S(1)} %add_multiply_fusion), kind=kOutput, calls=%fused_computation.1 | convolution fusion | flops 152043520 | bytes 2179076 | tf_op jit(solution)/shard_map/dot_general | solution.py:258
  11.4 2.8 %collective-permute-done = f32[64,256]{1,0:T(8,128)S(1)} collective-permute-done((f32[64,256]{1,0:T(8,128)S(1)}, f32[64,256]{1,0:T(8,128)S(1)}, u32[]{:S(2)}, u32[]{:S(2)}) %collective-permute-start) | collective-permute-done | bytes 65568 | tf_op jit(solution)/shard_map/ppermute | solution.py:208
  14.2 18.8 %collective-permute-done.1 = f32[2,64,128]{2,1,0:T(8,128)S(1)} collective-permute-done((f32[2,64,128]{2,1,0:T(8,128)S(1)}, f32[2,64,128]{2,1,0:T(8,128)S(1)}, u32[]{:S(2)}, u32[]{:S(2)}) %collective-permute-start.1) | collective-permute-done | bytes 65568 | tf_op jit(solution)/shard_map/ppermute | solution.py:208
  34.0 2.9 %collective-permute-start.6 = (bf16[256,1024]{1,0:T(8,128)(2,1)S(1)}, bf16[256,1024]{1,0:T(8,128)(2,1)S(1)}, u32[]{:S(2)}, u32[]{:S(2)}) collective-permute-start(bf16[256,1024]{1,0:T(8,128)(2,1)S(1)} %get-tuple-element.32), channel_id=1, source_target_pairs={{0,12},{4,8},{8,4},{12,0},{1,13},{5,9},{9,5},{13,1},{2,14},{6,10},... | collective-permute-start | bytes 1572872 | tf_op jit(solution)/shard_map/ppermute | solution.py:208
  39.8 6.3 %shard_map.41 = (bf16[64,2048]{1,0:T(8,128)(2,1)S(1)}, f32[64,64]{1,0:T(8,128)S(1)}) custom-call(s32[8]{0:T(128)S(1)} %fusion.20.at_ref, f32[8,64,128]{2,1,0:T(8,128)S(1)} %constant_dynamic-update-slice_fusion.z_ref, f32[8,64,128]{2,1,0:T(8,128)S(1)} %collective-permute-done.4.other_ref), custom_call_target="tpu_custom_call" | custom-call | flops 402653184 | bytes 524288 | tf_op jit(solution)/shard_map/pallas_call | solution.py:191
  46.0 6.2 %collective-permute-done.6.refs_3_ = bf16[256,1024]{1,0:T(8,128)(2,1)S(1)} collective-permute-done((bf16[256,1024]{1,0:T(8,128)(2,1)S(1)}, bf16[256,1024]{1,0:T(8,128)(2,1)S(1)}, u32[]{:S(2)}, u32[]{:S(2)}) %collective-permute-start.6) | collective-permute-done | bytes 524320 | tf_op jit(solution)/shard_map/ppermute | solution.py:208
  52.3 9.4 %collective-permute-done.5.refs_1_ = bf16[256,1024]{1,0:T(8,128)(2,1)S(1)} collective-permute-done((bf16[256,1024]{1,0:T(8,128)(2,1)S(1)}, bf16[256,1024]{1,0:T(8,128)(2,1)S(1)}, u32[]{:S(2)}, u32[]{:S(2)}) %collective-permute-start.5) | collective-permute-done | bytes 524320 | tf_op jit(solution)/shard_map/ppermute | solution.py:208
  64.4 2.1 %shard_map.42 = (bf16[2048,1024]{1,0:T(8,128)(2,1)S(1)}, f32[8,64,128]{2,1,0:T(8,128)S(1)}) custom-call(s32[8]{0:T(128)S(1)} %fusion.18.at_ref, bf16[64,2048]{1,0:T(8,128)(2,1)S(1)} %get-tuple-element.17.basis_ref, bf16[256,1024]{1,0:T(8,128)(2,1)S(1)} %get-tuple-element.30.refs_0_, bf16[256,1024]{1,0:T(8,128)(2,1)S(1)} %collective-permute-done.5.refs_1_, ...), custom_call_target="tpu_custom_call" | custom-call | flops 939524096 | bytes 4456448 | tf_op jit(solution)/shard_map/pallas_call | solution.py:191
  68.1 4.0 %collective-permute-done.11 = f32[4,64,128]{2,1,0:T(8,128)S(1)} collective-permute-done((f32[4,64,128]{2,1,0:T(8,128)S(1)}, f32[4,64,128]{2,1,0:T(8,128)S(1)}, u32[]{:S(2)}, u32[]{:S(2)}) %collective-permute-start.11) | collective-permute-done | bytes 131104 | tf_op jit(solution)/shard_map/ppermute | solution.py:208
  72.5 4.6 %collective-permute-done.12 = f32[4,64,128]{2,1,0:T(8,128)S(1)} collective-permute-done((f32[4,64,128]{2,1,0:T(8,128)S(1)}, f32[4,64,128]{2,1,0:T(8,128)S(1)}, u32[]{:S(2)}, u32[]{:S(2)}) %collective-permute-start.12) | collective-permute-done | bytes 131104 | tf_op jit(solution)/shard_map/ppermute | solution.py:208
  77.2 1.8 %collective-permute-start.13 = (f32[4,64,128]{2,1,0:T(8,128)S(1)}, f32[4,64,128]{2,1,0:T(8,128)S(1)}, u32[]{:S(2)}, u32[]{:S(2)}) collective-permute-start(f32[4,64,128]{2,1,0:T(8,128)S(1)} %add.212), channel_id=1, source_target_pairs={{0,8},{4,12},{8,0},{12,4},{1,9},{5,13},{9,1},{13,5},{2,10},{6,14},... | collective-permute-start | bytes 393224 | tf_op jit(solution)/shard_map/ppermute | solution.py:208
  79.0 5.5 %collective-permute-done.13 = f32[4,64,128]{2,1,0:T(8,128)S(1)} collective-permute-done((f32[4,64,128]{2,1,0:T(8,128)S(1)}, f32[4,64,128]{2,1,0:T(8,128)S(1)}, u32[]{:S(2)}, u32[]{:S(2)}) %collective-permute-start.13) | collective-permute-done | bytes 131104 | tf_op jit(solution)/shard_map/ppermute | solution.py:208
  86.1 3.5 %collective-permute-done.14 = f32[4,64,128]{2,1,0:T(8,128)S(1)} collective-permute-done((f32[4,64,128]{2,1,0:T(8,128)S(1)}, f32[4,64,128]{2,1,0:T(8,128)S(1)}, u32[]{:S(2)}, u32[]{:S(2)}) %collective-permute-start.14) | collective-permute-done | bytes 131104 | tf_op jit(solution)/shard_map/ppermute | solution.py:208
  91.2 8.0 %shard_map.43 = f32[8,64,128]{2,1,0:T(8,128)S(1)} custom-call(s32[8]{0:T(128)S(1)} %fusion.18.at_ref, f32[8,64,128]{2,1,0:T(8,128)S(1)} %pad_maximum_fusion.z_ref, f32[8,64,128]{2,1,0:T(8,128)S(1)} %collective-permute-done.15.other_ref, bf16[2048,1024]{1,0:T(8,128)(2,1)S(1)} %get-tuple-element.22.a_ref), custom_call_target="tpu_custom_call" | custom-call | flops 939524096 | bytes 4718592 | tf_op jit(solution)/shard_map/pallas_call | solution.py:191
  100.8 2.8 %collective-permute-done.16 = bf16[4,64,128]{2,1,0:T(8,128)(2,1)S(1)} collective-permute-done((bf16[4,64,128]{2,1,0:T(8,128)(2,1)S(1)}, bf16[4,64,128]{2,1,0:T(8,128)(2,1)S(1)}, u32[]{:S(2)}, u32[]{:S(2)}) %collective-permute-start.16) | collective-permute-done | bytes 65568 | tf_op jit(solution)/shard_map/ppermute | solution.py:208
  103.7 4.3 %collective-permute-done.17 = bf16[4,64,128]{2,1,0:T(8,128)(2,1)S(1)} collective-permute-done((bf16[4,64,128]{2,1,0:T(8,128)(2,1)S(1)}, bf16[4,64,128]{2,1,0:T(8,128)(2,1)S(1)}, u32[]{:S(2)}, u32[]{:S(2)}) %collective-permute-start.17) | collective-permute-done | bytes 65568 | tf_op jit(solution)/shard_map/ppermute | solution.py:208
  109.2 4.4 %collective-permute-done.18 = bf16[4,64,128]{2,1,0:T(8,128)(2,1)S(1)} collective-permute-done((bf16[4,64,128]{2,1,0:T(8,128)(2,1)S(1)}, bf16[4,64,128]{2,1,0:T(8,128)(2,1)S(1)}, u32[]{:S(2)}, u32[]{:S(2)}) %collective-permute-start.18) | collective-permute-done | bytes 65568 | tf_op jit(solution)/shard_map/ppermute | solution.py:208
  115.2 2.8 %collective-permute-done.19 = bf16[4,64,128]{2,1,0:T(8,128)(2,1)S(1)} collective-permute-done((bf16[4,64,128]{2,1,0:T(8,128)(2,1)S(1)}, bf16[4,64,128]{2,1,0:T(8,128)(2,1)S(1)}, u32[]{:S(2)}, u32[]{:S(2)}) %collective-permute-start.19) | collective-permute-done | bytes 65568 | tf_op jit(solution)/shard_map/ppermute | solution.py:208
  119.4 7.1 %shard_map.44 = f32[8,64,128]{2,1,0:T(8,128)S(1)} custom-call(s32[8]{0:T(128)S(1)} %fusion.18.at_ref, bf16[8,64,128]{2,1,0:T(8,128)(2,1)S(1)} %pad_maximum_fusion.2.z_ref, bf16[8,64,128]{2,1,0:T(8,128)(2,1)S(1)} %collective-permute-done.20.other_ref, bf16[2048,1024]{1,0:T(8,128)(2,1)S(1)} %get-tuple-element.22.a_ref), custom_call_target="tpu_custom_call" | custom-call | flops 939524096 | bytes 4456448 | tf_op jit(solution)/shard_map/pallas_call | solution.py:191
  128.1 2.8 %collective-permute-done.21 = bf16[4,64,128]{2,1,0:T(8,128)(2,1)S(1)} collective-permute-done((bf16[4,64,128]{2,1,0:T(8,128)(2,1)S(1)}, bf16[4,64,128]{2,1,0:T(8,128)(2,1)S(1)}, u32[]{:S(2)}, u32[]{:S(2)}) %collective-permute-start.21) | collective-permute-done | bytes 65568 | tf_op jit(solution)/shard_map/ppermute | solution.py:208
  131.0 4.3 %collective-permute-done.22 = bf16[4,64,128]{2,1,0:T(8,128)(2,1)S(1)} collective-permute-done((bf16[4,64,128]{2,1,0:T(8,128)(2,1)S(1)}, bf16[4,64,128]{2,1,0:T(8,128)(2,1)S(1)}, u32[]{:S(2)}, u32[]{:S(2)}) %collective-permute-start.22) | collective-permute-done | bytes 65568 | tf_op jit(solution)/shard_map/ppermute | solution.py:208
  136.3 4.4 %collective-permute-done.23 = bf16[4,64,128]{2,1,0:T(8,128)(2,1)S(1)} collective-permute-done((bf16[4,64,128]{2,1,0:T(8,128)(2,1)S(1)}, bf16[4,64,128]{2,1,0:T(8,128)(2,1)S(1)}, u32[]{:S(2)}, u32[]{:S(2)}) %collective-permute-start.23) | collective-permute-done | bytes 65568 | tf_op jit(solution)/shard_map/ppermute | solution.py:208
  142.2 2.8 %collective-permute-done.24 = bf16[4,64,128]{2,1,0:T(8,128)(2,1)S(1)} collective-permute-done((bf16[4,64,128]{2,1,0:T(8,128)(2,1)S(1)}, bf16[4,64,128]{2,1,0:T(8,128)(2,1)S(1)}, u32[]{:S(2)}, u32[]{:S(2)}) %collective-permute-start.24) | collective-permute-done | bytes 65568 | tf_op jit(solution)/shard_map/ppermute | solution.py:208
  146.5 7.1 %shard_map.45 = f32[8,64,128]{2,1,0:T(8,128)S(1)} custom-call(s32[8]{0:T(128)S(1)} %fusion.18.at_ref, bf16[8,64,128]{2,1,0:T(8,128)(2,1)S(1)} %pad_maximum_fusion.3.z_ref, bf16[8,64,128]{2,1,0:T(8,128)(2,1)S(1)} %collective-permute-done.25.other_ref, bf16[2048,1024]{1,0:T(8,128)(2,1)S(1)} %get-tuple-element.22.a_ref), custom_call_target="tpu_custom_call" | custom-call | flops 939524096 | bytes 4456448 | tf_op jit(solution)/shard_map/pallas_call | solution.py:191
  155.2 2.8 %collective-permute-done.26 = bf16[4,64,128]{2,1,0:T(8,128)(2,1)S(1)} collective-permute-done((bf16[4,64,128]{2,1,0:T(8,128)(2,1)S(1)}, bf16[4,64,128]{2,1,0:T(8,128)(2,1)S(1)}, u32[]{:S(2)}, u32[]{:S(2)}) %collective-permute-start.26) | collective-permute-done | bytes 65568 | tf_op jit(solution)/shard_map/ppermute | solution.py:208
  158.1 4.3 %collective-permute-done.27 = bf16[4,64,128]{2,1,0:T(8,128)(2,1)S(1)} collective-permute-done((bf16[4,64,128]{2,1,0:T(8,128)(2,1)S(1)}, bf16[4,64,128]{2,1,0:T(8,128)(2,1)S(1)}, u32[]{:S(2)}, u32[]{:S(2)}) %collective-permute-start.27) | collective-permute-done | bytes 65568 | tf_op jit(solution)/shard_map/ppermute | solution.py:208
  163.3 4.4 %collective-permute-done.28 = bf16[4,64,128]{2,1,0:T(8,128)(2,1)S(1)} collective-permute-done((bf16[4,64,128]{2,1,0:T(8,128)(2,1)S(1)}, bf16[4,64,128]{2,1,0:T(8,128)(2,1)S(1)}, u32[]{:S(2)}, u32[]{:S(2)}) %collective-permute-start.28) | collective-permute-done | bytes 65568 | tf_op jit(solution)/shard_map/ppermute | solution.py:208
  169.3 2.8 %collective-permute-done.29 = bf16[4,64,128]{2,1,0:T(8,128)(2,1)S(1)} collective-permute-done((bf16[4,64,128]{2,1,0:T(8,128)(2,1)S(1)}, bf16[4,64,128]{2,1,0:T(8,128)(2,1)S(1)}, u32[]{:S(2)}, u32[]{:S(2)}) %collective-permute-start.29) | collective-permute-done | bytes 65568 | tf_op jit(solution)/shard_map/ppermute | solution.py:208
  173.5 2.2 %copy-done.1 = bf16[2048,1024]{1,0:T(8,128)(2,1)S(1)} copy-done((bf16[2048,1024]{1,0:T(8,128)(2,1)S(1)}, bf16[2048,1024]{1,0:T(8,128)(2,1)}, u32[]{:S(2)}) %copy-start.1) | copy-done | bytes 4194328
  175.7 6.5 %shard_map.46 = f32[64,512]{1,0:T(8,128)} custom-call(s32[8]{0:T(128)S(1)} %fusion.18.at_ref, s32[1]{0:T(128)} %bitcast.core_ref, bf16[8,64,128]{2,1,0:T(8,128)(2,1)S(1)} %pad_maximum_fusion.4.z_ref, bf16[8,64,128]{2,1,0:T(8,128)(2,1)S(1)} %collective-permute-done.30.other_ref, bf16[2048,1024]{1,0:T(8,128)(2,1)S(1)} %copy-done.1), custom_call_target="tpu_custom_call" | custom-call | flops 939524096 | bytes 4456448 | tf_op jit(solution)/shard_map/pallas_call | solution.py:191
  (74 shorter events, 30.4 us)
Async XLA Ops:
  2.9 30.2 %collective-permute-start.2 = (bf16[256,1024]{1,0:T(8,128)(2,1)}, bf16[256,1024]{1,0:T(8,128)(2,1)S(1)}, u32[]{:S(2)}, u32[]{:S(2)}) collective-permute-start(bf16[256,1024]{1,0:T(8,128)(2,1)} %get-tuple-element.31), channel_id=1, source_target_pairs={{0,8},{4,12},{8,0},{12,4},{1,9},{5,13},{9,1},{13,5},{2,10},{6,14},... | collective-permute-start | bytes 1572872 | tf_op jit(solution)/shard_map/ppermute | solution.py:208
  9.8 4.3 %collective-permute-start = (f32[64,256]{1,0:T(8,128)S(1)}, f32[64,256]{1,0:T(8,128)S(1)}, u32[]{:S(2)}, u32[]{:S(2)}) collective-permute-start(f32[64,256]{1,0:T(8,128)S(1)} %fusion), channel_id=1, source_target_pairs={{0,1},{1,0},{2,3},{3,2},{4,5},{5,4},{6,7},{7,6},{8,9},{9,8},{10,11... | collective-permute-start | bytes 196616 | tf_op jit(solution)/shard_map/ppermute | solution.py:208
  14.1 18.9 %collective-permute-start.1 = (f32[2,64,128]{2,1,0:T(8,128)S(1)}, f32[2,64,128]{2,1,0:T(8,128)S(1)}, u32[]{:S(2)}, u32[]{:S(2)}) collective-permute-start(f32[2,64,128]{2,1,0:T(8,128)S(1)} %bitcast_bitcast_fusion), channel_id=1, source_target_pairs={{0,8},{4,12},{8,0},{12,4},{1,9},{5,13},{9,1},{13,5},{2,10},{6,14},... | collective-permute-start | bytes 196616 | tf_op jit(solution)/shard_map/ppermute | solution.py:208
  33.1 5.0 %collective-permute-start.3 = (f32[4,64,128]{2,1,0:T(8,128)S(1)}, f32[4,64,128]{2,1,0:T(8,128)S(1)}, u32[]{:S(2)}, u32[]{:S(2)}) collective-permute-start(f32[4,64,128]{2,1,0:T(8,128)S(1)} %pad_maximum_fusion.1), channel_id=1, source_target_pairs={{0,4},{4,0},{8,12},{12,8},{1,5},{5,1},{9,13},{13,9},{2,6},{6,2},{1... | collective-permute-start | bytes 393224 | tf_op jit(solution)/shard_map/ppermute | solution.py:208
  34.0 18.3 %collective-permute-start.6 = (bf16[256,1024]{1,0:T(8,128)(2,1)S(1)}, bf16[256,1024]{1,0:T(8,128)(2,1)S(1)}, u32[]{:S(2)}, u32[]{:S(2)}) collective-permute-start(bf16[256,1024]{1,0:T(8,128)(2,1)S(1)} %get-tuple-element.32), channel_id=1, source_target_pairs={{0,12},{4,8},{8,4},{12,0},{1,13},{5,9},{9,5},{13,1},{2,14},{6,10},... | collective-permute-start | bytes 1572872 | tf_op jit(solution)/shard_map/ppermute | solution.py:208
  36.9 24.8 %collective-permute-start.5 = (bf16[256,1024]{1,0:T(8,128)(2,1)S(1)}, bf16[256,1024]{1,0:T(8,128)(2,1)S(1)}, u32[]{:S(2)}, u32[]{:S(2)}) collective-permute-start(bf16[256,1024]{1,0:T(8,128)(2,1)S(1)} %get-tuple-element.33), channel_id=1, source_target_pairs={{0,4},{4,0},{8,12},{12,8},{1,5},{5,1},{9,13},{13,9},{2,6},{6,2},{1... | collective-permute-start | bytes 1572872 | tf_op jit(solution)/shard_map/ppermute | solution.py:208
  38.1 1.6 collective-permute-start.4
  38.2 24.0 %collective-permute-start.7 = (bf16[256,1024]{1,0:T(8,128)(2,1)S(1)}, bf16[256,1024]{1,0:T(8,128)(2,1)S(1)}, u32[]{:S(2)}, u32[]{:S(2)}) collective-permute-start(bf16[256,1024]{1,0:T(8,128)(2,1)S(1)} %get-tuple-element.30.refs_0_), channel_id=1, source_target_pairs={{0,2},{2,0},{1,3},{3,1},{4,6},{6,4},{5,7},{7,5},{8,10},{10,8},{9,1... | collective-permute-start | bytes 1572872 | tf_op jit(solution)/shard_map/ppermute | solution.py:208
  38.7 23.5 %collective-permute-start.9 = (bf16[256,1024]{1,0:T(8,128)(2,1)S(1)}, bf16[256,1024]{1,0:T(8,128)(2,1)S(1)}, u32[]{:S(2)}, u32[]{:S(2)}) collective-permute-start(bf16[256,1024]{1,0:T(8,128)(2,1)S(1)} %collective-permute-done.2.refs_2_), channel_id=1, source_target_pairs={{0,2},{2,0},{1,3},{3,1},{4,6},{6,4},{5,7},{7,5},{8,10},{10,8},{9,1... | collective-permute-start | bytes 1572872 | tf_op jit(solution)/shard_map/ppermute | solution.py:208
  61.7 1.9 %collective-permute-start.8 = (bf16[256,1024]{1,0:T(8,128)(2,1)S(1)}, bf16[256,1024]{1,0:T(8,128)(2,1)S(1)}, u32[]{:S(2)}, u32[]{:S(2)}) collective-permute-start(bf16[256,1024]{1,0:T(8,128)(2,1)S(1)} %collective-permute-done.5.refs_1_), channel_id=1, source_target_pairs={{0,2},{2,0},{1,3},{3,1},{4,6},{6,4},{5,7},{7,5},{8,10},{10,8},{9,1... | collective-permute-start | bytes 1572872 | tf_op jit(solution)/shard_map/ppermute | solution.py:208
  61.7 2.7 %collective-permute-start.10 = (bf16[256,1024]{1,0:T(8,128)(2,1)S(1)}, bf16[256,1024]{1,0:T(8,128)(2,1)S(1)}, u32[]{:S(2)}, u32[]{:S(2)}) collective-permute-start(bf16[256,1024]{1,0:T(8,128)(2,1)S(1)} %collective-permute-done.6.refs_3_), channel_id=1, source_target_pairs={{0,2},{2,0},{1,3},{3,1},{4,6},{6,4},{5,7},{7,5},{8,10},{10,8},{9,1... | collective-permute-start | bytes 1572872 | tf_op jit(solution)/shard_map/ppermute | solution.py:208
  66.5 80.0 %copy-start = (bf16[2048,1024]{1,0:T(8,128)(2,1)}, bf16[2048,1024]{1,0:T(8,128)(2,1)S(1)}, u32[]{:S(2)}) copy-start(bf16[2048,1024]{1,0:T(8,128)(2,1)S(1)} %get-tuple-element.22.a_ref) | copy-start | bytes 12582916
  66.5 5.6 %collective-permute-start.11 = (f32[4,64,128]{2,1,0:T(8,128)S(1)}, f32[4,64,128]{2,1,0:T(8,128)S(1)}, u32[]{:S(2)}, u32[]{:S(2)}) collective-permute-start(f32[4,64,128]{2,1,0:T(8,128)S(1)} %slice.28), channel_id=1, source_target_pairs={{0,1},{1,0},{2,3},{3,2},{4,5},{5,4},{6,7},{7,6},{8,9},{9,8},{10,11... | collective-permute-start | bytes 393224 | tf_op jit(solution)/shard_map/ppermute | solution.py:208
  72.1 5.0 %collective-permute-start.12 = (f32[4,64,128]{2,1,0:T(8,128)S(1)}, f32[4,64,128]{2,1,0:T(8,128)S(1)}, u32[]{:S(2)}, u32[]{:S(2)}) collective-permute-start(f32[4,64,128]{2,1,0:T(8,128)S(1)} %slice_add_fusion.3), channel_id=1, source_target_pairs={{0,4},{4,0},{8,12},{12,8},{1,5},{5,1},{9,13},{13,9},{2,6},{6,2},{1... | collective-permute-start | bytes 393224 | tf_op jit(solution)/shard_map/ppermute | solution.py:208
  77.2 7.3 %collective-permute-start.13 = (f32[4,64,128]{2,1,0:T(8,128)S(1)}, f32[4,64,128]{2,1,0:T(8,128)S(1)}, u32[]{:S(2)}, u32[]{:S(2)}) collective-permute-start(f32[4,64,128]{2,1,0:T(8,128)S(1)} %add.212), channel_id=1, source_target_pairs={{0,8},{4,12},{8,0},{12,4},{1,9},{5,13},{9,1},{13,5},{2,10},{6,14},... | collective-permute-start | bytes 393224 | tf_op jit(solution)/shard_map/ppermute | solution.py:208
  84.6 5.0 %collective-permute-start.14 = (f32[4,64,128]{2,1,0:T(8,128)S(1)}, f32[4,64,128]{2,1,0:T(8,128)S(1)}, u32[]{:S(2)}, u32[]{:S(2)}) collective-permute-start(f32[4,64,128]{2,1,0:T(8,128)S(1)} %add.213), channel_id=1, source_target_pairs={{0,1},{1,0},{2,3},{3,2},{4,5},{5,4},{6,7},{7,6},{8,9},{9,8},{10,11... | collective-permute-start | bytes 393224 | tf_op jit(solution)/shard_map/ppermute | solution.py:208
  89.6 1.6 collective-permute-start.15
  99.2 4.3 %collective-permute-start.16 = (bf16[4,64,128]{2,1,0:T(8,128)(2,1)S(1)}, bf16[4,64,128]{2,1,0:T(8,128)(2,1)S(1)}, u32[]{:S(2)}, u32[]{:S(2)}) collective-permute-start(bf16[4,64,128]{2,1,0:T(8,128)(2,1)S(1)} %slice.56), channel_id=1, source_target_pairs={{0,1},{1,0},{2,3},{3,2},{4,5},{5,4},{6,7},{7,6},{8,9},{9,8},{10,11... | collective-permute-start | bytes 196616 | tf_op jit(solution)/shard_map/ppermute | solution.py:208
  103.6 4.3 %collective-permute-start.17 = (bf16[4,64,128]{2,1,0:T(8,128)(2,1)S(1)}, bf16[4,64,128]{2,1,0:T(8,128)(2,1)S(1)}, u32[]{:S(2)}, u32[]{:S(2)}) collective-permute-start(bf16[4,64,128]{2,1,0:T(8,128)(2,1)S(1)} %fusion.16), channel_id=1, source_target_pairs={{0,4},{4,0},{8,12},{12,8},{1,5},{5,1},{9,13},{13,9},{2,6},{6,2},{1... | collective-permute-start | bytes 196616 | tf_op jit(solution)/shard_map/ppermute | solution.py:208
  107.9 5.7 %collective-permute-start.18 = (bf16[4,64,128]{2,1,0:T(8,128)(2,1)S(1)}, bf16[4,64,128]{2,1,0:T(8,128)(2,1)S(1)}, u32[]{:S(2)}, u32[]{:S(2)}) collective-permute-start(bf16[4,64,128]{2,1,0:T(8,128)(2,1)S(1)} %add_convert_fusion.5), channel_id=1, source_target_pairs={{0,8},{4,12},{8,0},{12,4},{1,9},{5,13},{9,1},{13,5},{2,10},{6,14},... | collective-permute-start | bytes 196616 | tf_op jit(solution)/shard_map/ppermute | solution.py:208
  113.6 4.3 %collective-permute-start.19 = (bf16[4,64,128]{2,1,0:T(8,128)(2,1)S(1)}, bf16[4,64,128]{2,1,0:T(8,128)(2,1)S(1)}, u32[]{:S(2)}, u32[]{:S(2)}) collective-permute-start(bf16[4,64,128]{2,1,0:T(8,128)(2,1)S(1)} %add_convert_fusion.4), channel_id=1, source_target_pairs={{0,1},{1,0},{2,3},{3,2},{4,5},{5,4},{6,7},{7,6},{8,9},{9,8},{10,11... | collective-permute-start | bytes 196616 | tf_op jit(solution)/shard_map/ppermute | solution.py:208
  118.0 1.4 collective-permute-start.20
  126.6 4.3 %collective-permute-start.21 = (bf16[4,64,128]{2,1,0:T(8,128)(2,1)S(1)}, bf16[4,64,128]{2,1,0:T(8,128)(2,1)S(1)}, u32[]{:S(2)}, u32[]{:S(2)}) collective-permute-start(bf16[4,64,128]{2,1,0:T(8,128)(2,1)S(1)} %slice.55), channel_id=1, source_target_pairs={{0,1},{1,0},{2,3},{3,2},{4,5},{5,4},{6,7},{7,6},{8,9},{9,8},{10,11... | collective-permute-start | bytes 196616 | tf_op jit(solution)/shard_map/ppermute | solution.py:208
  130.9 4.3 %collective-permute-start.22 = (bf16[4,64,128]{2,1,0:T(8,128)(2,1)S(1)}, bf16[4,64,128]{2,1,0:T(8,128)(2,1)S(1)}, u32[]{:S(2)}, u32[]{:S(2)}) collective-permute-start(bf16[4,64,128]{2,1,0:T(8,128)(2,1)S(1)} %fusion.15), channel_id=1, source_target_pairs={{0,4},{4,0},{8,12},{12,8},{1,5},{5,1},{9,13},{13,9},{2,6},{6,2},{1... | collective-permute-start | bytes 196616 | tf_op jit(solution)/shard_map/ppermute | solution.py:208
  135.3 5.4 %collective-permute-start.23 = (bf16[4,64,128]{2,1,0:T(8,128)(2,1)S(1)}, bf16[4,64,128]{2,1,0:T(8,128)(2,1)S(1)}, u32[]{:S(2)}, u32[]{:S(2)}) collective-permute-start(bf16[4,64,128]{2,1,0:T(8,128)(2,1)S(1)} %add_convert_fusion.3), channel_id=1, source_target_pairs={{0,8},{4,12},{8,0},{12,4},{1,9},{5,13},{9,1},{13,5},{2,10},{6,14},... | collective-permute-start | bytes 196616 | tf_op jit(solution)/shard_map/ppermute | solution.py:208
  140.7 4.3 %collective-permute-start.24 = (bf16[4,64,128]{2,1,0:T(8,128)(2,1)S(1)}, bf16[4,64,128]{2,1,0:T(8,128)(2,1)S(1)}, u32[]{:S(2)}, u32[]{:S(2)}) collective-permute-start(bf16[4,64,128]{2,1,0:T(8,128)(2,1)S(1)} %add_convert_fusion.2), channel_id=1, source_target_pairs={{0,1},{1,0},{2,3},{3,2},{4,5},{5,4},{6,7},{7,6},{8,9},{9,8},{10,11... | collective-permute-start | bytes 196616 | tf_op jit(solution)/shard_map/ppermute | solution.py:208
  145.0 1.4 collective-permute-start.25
  153.6 4.3 %collective-permute-start.26 = (bf16[4,64,128]{2,1,0:T(8,128)(2,1)S(1)}, bf16[4,64,128]{2,1,0:T(8,128)(2,1)S(1)}, u32[]{:S(2)}, u32[]{:S(2)}) collective-permute-start(bf16[4,64,128]{2,1,0:T(8,128)(2,1)S(1)} %slice.54), channel_id=1, source_target_pairs={{0,1},{1,0},{2,3},{3,2},{4,5},{5,4},{6,7},{7,6},{8,9},{9,8},{10,11... | collective-permute-start | bytes 196616 | tf_op jit(solution)/shard_map/ppermute | solution.py:208
  158.0 4.3 %collective-permute-start.27 = (bf16[4,64,128]{2,1,0:T(8,128)(2,1)S(1)}, bf16[4,64,128]{2,1,0:T(8,128)(2,1)S(1)}, u32[]{:S(2)}, u32[]{:S(2)}) collective-permute-start(bf16[4,64,128]{2,1,0:T(8,128)(2,1)S(1)} %fusion.14), channel_id=1, source_target_pairs={{0,4},{4,0},{8,12},{12,8},{1,5},{5,1},{9,13},{13,9},{2,6},{6,2},{1... | collective-permute-start | bytes 196616 | tf_op jit(solution)/shard_map/ppermute | solution.py:208
  162.3 5.4 %collective-permute-start.28 = (bf16[4,64,128]{2,1,0:T(8,128)(2,1)S(1)}, bf16[4,64,128]{2,1,0:T(8,128)(2,1)S(1)}, u32[]{:S(2)}, u32[]{:S(2)}) collective-permute-start(bf16[4,64,128]{2,1,0:T(8,128)(2,1)S(1)} %add_convert_fusion.1), channel_id=1, source_target_pairs={{0,8},{4,12},{8,0},{12,4},{1,9},{5,13},{9,1},{13,5},{2,10},{6,14},... | collective-permute-start | bytes 196616 | tf_op jit(solution)/shard_map/ppermute | solution.py:208
  167.7 4.3 %collective-permute-start.29 = (bf16[4,64,128]{2,1,0:T(8,128)(2,1)S(1)}, bf16[4,64,128]{2,1,0:T(8,128)(2,1)S(1)}, u32[]{:S(2)}, u32[]{:S(2)}) collective-permute-start(bf16[4,64,128]{2,1,0:T(8,128)(2,1)S(1)} %add_convert_fusion), channel_id=1, source_target_pairs={{0,1},{1,0},{2,3},{3,2},{4,5},{5,4},{6,7},{7,6},{8,9},{9,8},{10,11... | collective-permute-start | bytes 196616 | tf_op jit(solution)/shard_map/ppermute | solution.py:208
  172.1 1.4 collective-permute-start.30
  (2 other events, 9.1 us)

commit v11 on v10

--- a/solution.py
+++ b/solution.py
@@ -12,6 +12,7 @@
 POWER = 4
 LANES = 128
 SUB = 8
+TILE = 256
 
 
 shift_ratio = 0.005
@@ -79,7 +80,8 @@
     return both[:rank, :rank] + ((cross + cross.T) + both[rank : 2 * rank, rank : 2 * rank])
 
 
-def eliminate(matrix):
+def eliminate(matrix, beside=()):
+    beside = list(beside)
     size = matrix.shape[0]
     blocks = size // SUB
     row_index = lax.broadcasted_iota(jnp.int32, (SUB, 2 * size), 0)
@@ -91,6 +93,8 @@
         work.append(jnp.concatenate([matrix[SUB * i : SUB * (i + 1), :], unit], axis=1))
     rows = []
     for b in range(blocks):
+        for unused in range(-(-len(beside) // (blocks - b))):
+            beside.pop(0)()
         columns = [
             {
                 i: jnp.broadcast_to(work[i][:, SUB * b + j : SUB * b + j + 1], (SUB, 2 * size))
@@ -147,10 +151,17 @@
 def back_product(at_ref, z_refs, a):
     first, unused = first_pass(at_ref, z_refs)
     rank = first.shape[0]
-    back = dot_nn(jnp.concatenate(terms_of(first), axis=0), a)
-    back = back[:rank] + (back[rank : 2 * rank] + back[2 * rank :])
-    unused, inverse_two = eliminate(gram_of(first))
-    return small_times_wide(inverse_two, back)
+    terms = jnp.concatenate(terms_of(first), axis=0)
+    tiles = []
+
+    def tile(start):
+        back = dot_nn(terms, a[:, start : start + TILE])
+        tiles.append(back[:rank] + (back[rank : 2 * rank] + back[2 * rank :]))
+
+    starts = range(0, a.shape[1], TILE)
+    work = [functools.partial(tile, start) for start in starts]
+    unused, inverse_two = eliminate(gram_of(first), work)
+    return small_times_wide(inverse_two, jnp.concatenate(tiles, axis=1))
 
 
 def forth_product(weights, a_ref, at_ref, part_ref):
@@ -194,7 +205,7 @@
         in_specs=[pl.BlockSpec(memory_space=pltpu.SMEM)] * len(scalars)
         + [pl.BlockSpec(memory_space=pltpu.VMEM)] * len(operands),
         out_specs=jax.tree.map(lambda _: pl.BlockSpec(memory_space=pltpu.VMEM), out_shapes),
-        compiler_params=pltpu.CompilerParams(vmem_limit_bytes=40 * 1024 * 1024),
+        compiler_params=pltpu.CompilerParams(vmem_limit_bytes=20 * 1024 * 1024),
         cost_estimate=pl.CostEstimate(flops=flops, bytes_accessed=moved, transcendentals=0),
     )(*scalars, *operands)
 
@@ -258,20 +269,21 @@
     z = lax.dot_general(
         omega, states, (((0,), (1,)), ((), ())), preferred_element_type=jnp.float32
     )
+    z = z.reshape(RANK, n_col, chunk).transpose(1, 0, 2)
     z_bits = bits(n_z)[::-1]
     far = z_bits[0]
     move(states, 0)
-    move(states, far)
+    z, slab = lax.optimization_barrier((z, states))
+    move(slab, far)
+    z = jnp.concatenate([z, from_xor(z, ("z",), far)])
+    z, slab = lax.optimization_barrier((z, slab))
+    for offset in sorted(set(range(1, n_z)) - {far}, reverse=True):
+        move(slab, offset)
+    for bit in z_bits[1:]:
+        z = jnp.concatenate([z, from_xor(z, ("z",), bit)])
     for bit in bits(n_col):
         z = z + from_xor(z, ("col",), bit)
-    z = z.reshape(RANK, n_col, chunk).transpose(1, 0, 2)
-    z = jnp.concatenate([z, from_xor(z, ("z",), far)])
-    z, slab = lax.optimization_barrier((z, states))
-    for offset in sorted(set(range(1, n_z)) - {far}, reverse=True):
-        move(slab, offset)
     z, pieces[far] = lax.optimization_barrier((z, pieces[far]))
-    for bit in z_bits[1:]:
-        z = jnp.concatenate([z, from_xor(z, ("z",), bit)])
     z = z, from_xor(z, ("core",), 1)
     absolute_col = [("col", bit, False) for bit in bits(n_col)[::-1]]
     at_first = chunk_places([("z", bit, True) for bit in z_bits[::-1]] + absolute_col)

time: 182 us -> 179 us (0.984)
  waiting for transfers between devices: 105 us -> 98.1 us
  starting transfers between devices: 30.1 us -> 35.5 us
  Pallas kernels: 37.2 us -> 34.2 us
    ppermute x31, waiting for transfers between devices: 105 us -> 98.1 us  [from_xor(): return lax.ppermute(value, axis, [(i, i ^ offset) for i in range(size)])]
    ppermute x31, starting transfers between devices: 30.1 us -> 35.5 us  [from_xor(): return lax.ppermute(value, axis, [(i, i ^ offset) for i in range(size)])]
    pallas_call x6, Pallas kernels: 37.2 us -> 34.2 us  [call(): pl.pallas_call(kernel, out_shape=out_shapes, in_specs=[pl.BlockSpec(memor...]
  transfers between devices with their start and end apart: 31 -> 31, of which waited for: 28 -> 26; matrix products, arithmetic and copies ran while one was open for 2% -> 2% of each run, Pallas kernels for 3% -> 4%
where the time goes in v11:
time: 179 us
  waiting for transfers between devices  98.1 us (55%)
  starting transfers between devices  35.5 us (20%)
  Pallas kernels  34.2 us (19%)
  local copies, waits for them, and re-layouts  5.19 us (3%)
  matrix products  3.97 us (2%)
    ppermute x31, waiting for transfers between devices, from_xor(): return lax.ppermute(value, axis, [(i, i ^ offset) for i in range(size)])  98.1 us
    ppermute x31, starting transfers between devices, from_xor(): return lax.ppermute(value, axis, [(i, i ^ offset) for i in range(size)])  35.5 us
    pallas_call x6, Pallas kernels, call(): pl.pallas_call(kernel, out_shape=out_shapes, in_specs=[pl.BlockSpec(memor...  34.2 us
    dot_general x1, matrix products, per_device_transposed(): lax.dot_general(omega, states, (((0,), (1,)), ((), ())), preferred_elemen...  3.97 us
  transfers between devices with their start and end apart: 31, of which 26 were waited for; matrix products, arithmetic and copies ran while one was open for 2% of the time, Pallas kernels for 4%

profile of v11, /device:TPU:0, one launch (start us, length us, event | category | flops | bytes accessed | tf_op | source)
XLA Modules:
  0.0 179.0 jit_solution(12494359926152353353)
XLA Ops:
  1.3 4.0 %convolution_bitcast_fusion = f32[8,2,8,128]{3,2,1,0:T(8,128)S(1)} fusion(bf16[256,4096]{1,0:T(8,128)(2,1)} %param.3, s32[]{:T(128)S(6)} %xor.72, s32[4096]{0:T(1024)S(1)} %add_multiply_fusion), kind=kOutput, calls=%fused_computation | convolution fusion | flops 152043520 | bytes 2179076 | tf_op jit(solution)/shard_map/dot_general | solution.py:269
  5.3 4.1 %collective-permute-start = (f32[2,64,128]{2,1,0:T(8,128)S(1)}, f32[2,64,128]{2,1,0:T(8,128)S(1)}, u32[]{:S(2)}, u32[]{:S(2)}) collective-permute-start(f32[2,64,128]{2,1,0:T(8,128)S(1)} %bitcast.16), channel_id=1, source_target_pairs={{0,8},{4,12},{8,0},{12,4},{1,9},{5,13},{9,1},{13,5},{2,10},{6,14},... | collective-permute-start | bytes 196616 | tf_op jit(solution)/shard_map/ppermute | solution.py:219
  9.4 3.6 %collective-permute-done = f32[2,64,128]{2,1,0:T(8,128)S(1)} collective-permute-done((f32[2,64,128]{2,1,0:T(8,128)S(1)}, f32[2,64,128]{2,1,0:T(8,128)S(1)}, u32[]{:S(2)}, u32[]{:S(2)}) %collective-permute-start) | collective-permute-done | bytes 65568 | tf_op jit(solution)/shard_map/ppermute | solution.py:219
  13.8 3.4 %collective-permute-start.3 = (bf16[256,1024]{1,0:T(8,128)(2,1)S(1)}, bf16[256,1024]{1,0:T(8,128)(2,1)S(1)}, u32[]{:S(2)}, u32[]{:S(2)}) collective-permute-start(bf16[256,1024]{1,0:T(8,128)(2,1)S(1)} %constant_dynamic-slice_fusion.3), channel_id=1, source_target_pairs={{0,8},{4,12},{8,0},{12,4},{1,9},{5,13},{9,1},{13,5},{2,10},{6,14},... | collective-permute-start | bytes 1572872 | tf_op jit(solution)/shard_map/ppermute | solution.py:219
  17.2 2.9 %collective-permute-done.1 = f32[4,64,128]{2,1,0:T(8,128)S(1)} collective-permute-done((f32[4,64,128]{2,1,0:T(8,128)S(1)}, f32[4,64,128]{2,1,0:T(8,128)S(1)}, u32[]{:S(2)}, u32[]{:S(2)}) %collective-permute-start.1) | collective-permute-done | bytes 131104 | tf_op jit(solution)/shard_map/ppermute | solution.py:219
  23.2 2.3 %collective-permute-start.6 = (bf16[256,1024]{1,0:T(8,128)(2,1)}, bf16[256,1024]{1,0:T(8,128)(2,1)S(1)}, u32[]{:S(2)}, u32[]{:S(2)}) collective-permute-start(bf16[256,1024]{1,0:T(8,128)(2,1)} %get-tuple-element.34), channel_id=1, source_target_pairs={{0,12},{4,8},{8,4},{12,0},{1,13},{5,9},{9,5},{13,1},{2,14},{6,10},... | collective-permute-start | bytes 1572872 | tf_op jit(solution)/shard_map/ppermute | solution.py:219
  26.6 26.0 %collective-permute-done.3.refs_2_ = bf16[256,1024]{1,0:T(8,128)(2,1)S(1)} collective-permute-done((bf16[256,1024]{1,0:T(8,128)(2,1)S(1)}, bf16[256,1024]{1,0:T(8,128)(2,1)S(1)}, u32[]{:S(2)}, u32[]{:S(2)}) %collective-permute-start.3) | collective-permute-done | bytes 524320 | tf_op jit(solution)/shard_map/ppermute | solution.py:219
  54.3 6.3 %shard_map.41 = (bf16[64,2048]{1,0:T(8,128)(2,1)S(1)}, f32[64,64]{1,0:T(8,128)S(1)}) custom-call(s32[8]{0:T(128)S(1)} %fusion.19.at_ref, f32[8,64,128]{2,1,0:T(8,128)S(1)} %add.206.z_ref, f32[8,64,128]{2,1,0:T(8,128)S(1)} %collective-permute-done.4.other_ref), custom_call_target="tpu_custom_call" | custom-call | flops 402653184 | bytes 524288 | tf_op jit(solution)/shard_map/pallas_call | solution.py:202
  63.5 2.1 %shard_map.42 = (bf16[2048,1024]{1,0:T(8,128)(2,1)S(1)}, f32[8,64,128]{2,1,0:T(8,128)S(1)}) custom-call(s32[8]{0:T(128)S(1)} %fusion.17.at_ref, bf16[64,2048]{1,0:T(8,128)(2,1)S(1)} %get-tuple-element.21.basis_ref, bf16[256,1024]{1,0:T(8,128)(2,1)S(1)} %constant_dynamic-slice_fusion.refs_0_, bf16[256,1024]{1,0:T(8,128)(2,1)S(1)} %collective-permute-done.5.refs_1_, ...), custom_call_target="tpu_custom_call" | custom-call | flops 939524096 | bytes 4456448 | tf_op jit(solution)/shard_map/pallas_call | solution.py:202
  67.2 4.3 %collective-permute-done.11 = f32[4,64,128]{2,1,0:T(8,128)S(1)} collective-permute-done((f32[4,64,128]{2,1,0:T(8,128)S(1)}, f32[4,64,128]{2,1,0:T(8,128)S(1)}, u32[]{:S(2)}, u32[]{:S(2)}) %collective-permute-start.11) | collective-permute-done | bytes 131104 | tf_op jit(solution)/shard_map/ppermute | solution.py:219
  71.5 2.1 %collective-permute-start.12 = (f32[4,64,128]{2,1,0:T(8,128)S(1)}, f32[4,64,128]{2,1,0:T(8,128)S(1)}, u32[]{:S(2)}, u32[]{:S(2)}) collective-permute-start(f32[4,64,128]{2,1,0:T(8,128)S(1)} %slice_add_fusion.3), channel_id=1, source_target_pairs={{0,4},{4,0},{8,12},{12,8},{1,5},{5,1},{9,13},{13,9},{2,6},{6,2},{1... | collective-permute-start | bytes 393224 | tf_op jit(solution)/shard_map/ppermute | solution.py:219
  73.6 3.0 %collective-permute-done.12 = f32[4,64,128]{2,1,0:T(8,128)S(1)} collective-permute-done((f32[4,64,128]{2,1,0:T(8,128)S(1)}, f32[4,64,128]{2,1,0:T(8,128)S(1)}, u32[]{:S(2)}, u32[]{:S(2)}) %collective-permute-start.12) | collective-permute-done | bytes 131104 | tf_op jit(solution)/shard_map/ppermute | solution.py:219
  76.5 3.0 %collective-permute-start.13 = (f32[4,64,128]{2,1,0:T(8,128)S(1)}, f32[4,64,128]{2,1,0:T(8,128)S(1)}, u32[]{:S(2)}, u32[]{:S(2)}) collective-permute-start(f32[4,64,128]{2,1,0:T(8,128)S(1)} %add.212), channel_id=1, source_target_pairs={{0,8},{4,12},{8,0},{12,4},{1,9},{5,13},{9,1},{13,5},{2,10},{6,14},... | collective-permute-start | bytes 393224 | tf_op jit(solution)/shard_map/ppermute | solution.py:219
  79.5 4.6 %collective-permute-done.13 = f32[4,64,128]{2,1,0:T(8,128)S(1)} collective-permute-done((f32[4,64,128]{2,1,0:T(8,128)S(1)}, f32[4,64,128]{2,1,0:T(8,128)S(1)}, u32[]{:S(2)}, u32[]{:S(2)}) %collective-permute-start.13) | collective-permute-done | bytes 131104 | tf_op jit(solution)/shard_map/ppermute | solution.py:219
  85.7 3.5 %collective-permute-done.14 = f32[4,64,128]{2,1,0:T(8,128)S(1)} collective-permute-done((f32[4,64,128]{2,1,0:T(8,128)S(1)}, f32[4,64,128]{2,1,0:T(8,128)S(1)}, u32[]{:S(2)}, u32[]{:S(2)}) %collective-permute-start.14) | collective-permute-done | bytes 131104 | tf_op jit(solution)/shard_map/ppermute | solution.py:219
  90.8 7.0 %shard_map.43 = f32[8,64,128]{2,1,0:T(8,128)S(1)} custom-call(s32[8]{0:T(128)S(1)} %fusion.17.at_ref, f32[8,64,128]{2,1,0:T(8,128)S(1)} %pad_maximum_fusion.z_ref, f32[8,64,128]{2,1,0:T(8,128)S(1)} %collective-permute-done.15.other_ref, bf16[2048,1024]{1,0:T(8,128)(2,1)S(1)} %get-tuple-element.26.a_ref), custom_call_target="tpu_custom_call" | custom-call | flops 939524096 | bytes 4718592 | tf_op jit(solution)/shard_map/pallas_call | solution.py:202
  99.4 2.8 %collective-permute-done.16 = bf16[4,64,128]{2,1,0:T(8,128)(2,1)S(1)} collective-permute-done((bf16[4,64,128]{2,1,0:T(8,128)(2,1)S(1)}, bf16[4,64,128]{2,1,0:T(8,128)(2,1)S(1)}, u32[]{:S(2)}, u32[]{:S(2)}) %collective-permute-start.16) | collective-permute-done | bytes 65568 | tf_op jit(solution)/shard_map/ppermute | solution.py:219
  102.7 3.8 %collective-permute-done.17 = bf16[4,64,128]{2,1,0:T(8,128)(2,1)S(1)} collective-permute-done((bf16[4,64,128]{2,1,0:T(8,128)(2,1)S(1)}, bf16[4,64,128]{2,1,0:T(8,128)(2,1)S(1)}, u32[]{:S(2)}, u32[]{:S(2)}) %collective-permute-start.17) | collective-permute-done | bytes 65568 | tf_op jit(solution)/shard_map/ppermute | solution.py:219
  107.9 4.4 %collective-permute-done.18 = bf16[4,64,128]{2,1,0:T(8,128)(2,1)S(1)} collective-permute-done((bf16[4,64,128]{2,1,0:T(8,128)(2,1)S(1)}, bf16[4,64,128]{2,1,0:T(8,128)(2,1)S(1)}, u32[]{:S(2)}, u32[]{:S(2)}) %collective-permute-start.18) | collective-permute-done | bytes 65568 | tf_op jit(solution)/shard_map/ppermute | solution.py:219
  113.9 2.8 %collective-permute-done.19 = bf16[4,64,128]{2,1,0:T(8,128)(2,1)S(1)} collective-permute-done((bf16[4,64,128]{2,1,0:T(8,128)(2,1)S(1)}, bf16[4,64,128]{2,1,0:T(8,128)(2,1)S(1)}, u32[]{:S(2)}, u32[]{:S(2)}) %collective-permute-start.19) | collective-permute-done | bytes 65568 | tf_op jit(solution)/shard_map/ppermute | solution.py:219
  118.1 6.4 %shard_map.44 = f32[8,64,128]{2,1,0:T(8,128)S(1)} custom-call(s32[8]{0:T(128)S(1)} %fusion.17.at_ref, bf16[8,64,128]{2,1,0:T(8,128)(2,1)S(1)} %pad_maximum_fusion.2.z_ref, bf16[8,64,128]{2,1,0:T(8,128)(2,1)S(1)} %collective-permute-done.20.other_ref, bf16[2048,1024]{1,0:T(8,128)(2,1)S(1)} %get-tuple-element.26.a_ref), custom_call_target="tpu_custom_call" | custom-call | flops 939524096 | bytes 4456448 | tf_op jit(solution)/shard_map/pallas_call | solution.py:202
  126.1 2.8 %collective-permute-done.21 = bf16[4,64,128]{2,1,0:T(8,128)(2,1)S(1)} collective-permute-done((bf16[4,64,128]{2,1,0:T(8,128)(2,1)S(1)}, bf16[4,64,128]{2,1,0:T(8,128)(2,1)S(1)}, u32[]{:S(2)}, u32[]{:S(2)}) %collective-permute-start.21) | collective-permute-done | bytes 65568 | tf_op jit(solution)/shard_map/ppermute | solution.py:219
  128.9 4.3 %collective-permute-done.22 = bf16[4,64,128]{2,1,0:T(8,128)(2,1)S(1)} collective-permute-done((bf16[4,64,128]{2,1,0:T(8,128)(2,1)S(1)}, bf16[4,64,128]{2,1,0:T(8,128)(2,1)S(1)}, u32[]{:S(2)}, u32[]{:S(2)}) %collective-permute-start.22) | collective-permute-done | bytes 65568 | tf_op jit(solution)/shard_map/ppermute | solution.py:219
  134.2 4.4 %collective-permute-done.23 = bf16[4,64,128]{2,1,0:T(8,128)(2,1)S(1)} collective-permute-done((bf16[4,64,128]{2,1,0:T(8,128)(2,1)S(1)}, bf16[4,64,128]{2,1,0:T(8,128)(2,1)S(1)}, u32[]{:S(2)}, u32[]{:S(2)}) %collective-permute-start.23) | collective-permute-done | bytes 65568 | tf_op jit(solution)/shard_map/ppermute | solution.py:219
  140.2 2.8 %collective-permute-done.24 = bf16[4,64,128]{2,1,0:T(8,128)(2,1)S(1)} collective-permute-done((bf16[4,64,128]{2,1,0:T(8,128)(2,1)S(1)}, bf16[4,64,128]{2,1,0:T(8,128)(2,1)S(1)}, u32[]{:S(2)}, u32[]{:S(2)}) %collective-permute-start.24) | collective-permute-done | bytes 65568 | tf_op jit(solution)/shard_map/ppermute | solution.py:219
  144.4 6.4 %shard_map.45 = f32[8,64,128]{2,1,0:T(8,128)S(1)} custom-call(s32[8]{0:T(128)S(1)} %fusion.17.at_ref, bf16[8,64,128]{2,1,0:T(8,128)(2,1)S(1)} %pad_maximum_fusion.3.z_ref, bf16[8,64,128]{2,1,0:T(8,128)(2,1)S(1)} %collective-permute-done.25.other_ref, bf16[2048,1024]{1,0:T(8,128)(2,1)S(1)} %get-tuple-element.26.a_ref), custom_call_target="tpu_custom_call" | custom-call | flops 939524096 | bytes 4456448 | tf_op jit(solution)/shard_map/pallas_call | solution.py:202
  152.3 2.8 %collective-permute-done.26 = bf16[4,64,128]{2,1,0:T(8,128)(2,1)S(1)} collective-permute-done((bf16[4,64,128]{2,1,0:T(8,128)(2,1)S(1)}, bf16[4,64,128]{2,1,0:T(8,128)(2,1)S(1)}, u32[]{:S(2)}, u32[]{:S(2)}) %collective-permute-start.26) | collective-permute-done | bytes 65568 | tf_op jit(solution)/shard_map/ppermute | solution.py:219
  155.2 4.3 %collective-permute-done.27 = bf16[4,64,128]{2,1,0:T(8,128)(2,1)S(1)} collective-permute-done((bf16[4,64,128]{2,1,0:T(8,128)(2,1)S(1)}, bf16[4,64,128]{2,1,0:T(8,128)(2,1)S(1)}, u32[]{:S(2)}, u32[]{:S(2)}) %collective-permute-start.27) | collective-permute-done | bytes 65568 | tf_op jit(solution)/shard_map/ppermute | solution.py:219
  160.5 4.4 %collective-permute-done.28 = bf16[4,64,128]{2,1,0:T(8,128)(2,1)S(1)} collective-permute-done((bf16[4,64,128]{2,1,0:T(8,128)(2,1)S(1)}, bf16[4,64,128]{2,1,0:T(8,128)(2,1)S(1)}, u32[]{:S(2)}, u32[]{:S(2)}) %collective-permute-start.28) | collective-permute-done | bytes 65568 | tf_op jit(solution)/shard_map/ppermute | solution.py:219
  166.4 2.8 %collective-permute-done.29 = bf16[4,64,128]{2,1,0:T(8,128)(2,1)S(1)} collective-permute-done((bf16[4,64,128]{2,1,0:T(8,128)(2,1)S(1)}, bf16[4,64,128]{2,1,0:T(8,128)(2,1)S(1)}, u32[]{:S(2)}, u32[]{:S(2)}) %collective-permute-start.29) | collective-permute-done | bytes 65568 | tf_op jit(solution)/shard_map/ppermute | solution.py:219
  170.6 2.2 %copy-done.1 = bf16[2048,1024]{1,0:T(8,128)(2,1)S(1)} copy-done((bf16[2048,1024]{1,0:T(8,128)(2,1)S(1)}, bf16[2048,1024]{1,0:T(8,128)(2,1)}, u32[]{:S(2)}) %copy-start.1) | copy-done | bytes 4194328
  172.8 6.1 %shard_map.46 = f32[64,512]{1,0:T(8,128)} custom-call(s32[8]{0:T(128)S(1)} %fusion.17.at_ref, s32[1]{0:T(128)} %bitcast.core_ref, bf16[8,64,128]{2,1,0:T(8,128)(2,1)S(1)} %pad_maximum_fusion.4.z_ref, bf16[8,64,128]{2,1,0:T(8,128)(2,1)S(1)} %collective-permute-done.30.other_ref, bf16[2048,1024]{1,0:T(8,128)(2,1)S(1)} %copy-done.1), custom_call_target="tpu_custom_call" | custom-call | flops 939524096 | bytes 4456448 | tf_op jit(solution)/shard_map/pallas_call | solution.py:202
  (76 shorter events, 32.1 us)
Async XLA Ops:
  5.3 7.8 %collective-permute-start = (f32[2,64,128]{2,1,0:T(8,128)S(1)}, f32[2,64,128]{2,1,0:T(8,128)S(1)}, u32[]{:S(2)}, u32[]{:S(2)}) collective-permute-start(f32[2,64,128]{2,1,0:T(8,128)S(1)} %bitcast.16), channel_id=1, source_target_pairs={{0,8},{4,12},{8,0},{12,4},{1,9},{5,13},{9,1},{13,5},{2,10},{6,14},... | collective-permute-start | bytes 196616 | tf_op jit(solution)/shard_map/ppermute | solution.py:219
  13.1 7.0 %collective-permute-start.1 = (f32[4,64,128]{2,1,0:T(8,128)S(1)}, f32[4,64,128]{2,1,0:T(8,128)S(1)}, u32[]{:S(2)}, u32[]{:S(2)}) collective-permute-start(f32[4,64,128]{2,1,0:T(8,128)S(1)} %pad_maximum_fusion.1), channel_id=1, source_target_pairs={{0,4},{4,0},{8,12},{12,8},{1,5},{5,1},{9,13},{13,9},{2,6},{6,2},{1... | collective-permute-start | bytes 393224 | tf_op jit(solution)/shard_map/ppermute | solution.py:219
  13.8 38.8 %collective-permute-start.3 = (bf16[256,1024]{1,0:T(8,128)(2,1)S(1)}, bf16[256,1024]{1,0:T(8,128)(2,1)S(1)}, u32[]{:S(2)}, u32[]{:S(2)}) collective-permute-start(bf16[256,1024]{1,0:T(8,128)(2,1)S(1)} %constant_dynamic-slice_fusion.3), channel_id=1, source_target_pairs={{0,8},{4,12},{8,0},{12,4},{1,9},{5,13},{9,1},{13,5},{2,10},{6,14},... | collective-permute-start | bytes 1572872 | tf_op jit(solution)/shard_map/ppermute | solution.py:219
  20.1 6.4 %collective-permute-start.2 = (f32[8,64,128]{2,1,0:T(8,128)S(1)}, f32[8,64,128]{2,1,0:T(8,128)S(1)}, u32[]{:S(2)}, u32[]{:S(2)}) collective-permute-start(f32[8,64,128]{2,1,0:T(8,128)S(1)} %constant_dynamic-update-slice_fusion), channel_id=1, source_target_pairs={{0,1},{1,0},{2,3},{3,2},{4,5},{5,4},{6,7},{7,6},{8,9},{9,8},{10,11... | collective-permute-start | bytes 786440 | tf_op jit(solution)/shard_map/ppermute | solution.py:219
  23.2 37.5 %collective-permute-start.6 = (bf16[256,1024]{1,0:T(8,128)(2,1)}, bf16[256,1024]{1,0:T(8,128)(2,1)S(1)}, u32[]{:S(2)}, u32[]{:S(2)}) collective-permute-start(bf16[256,1024]{1,0:T(8,128)(2,1)} %get-tuple-element.34), channel_id=1, source_target_pairs={{0,12},{4,8},{8,4},{12,0},{1,13},{5,9},{9,5},{13,1},{2,14},{6,10},... | collective-permute-start | bytes 1572872 | tf_op jit(solution)/shard_map/ppermute | solution.py:219
  25.5 35.2 %collective-permute-start.5 = (bf16[256,1024]{1,0:T(8,128)(2,1)}, bf16[256,1024]{1,0:T(8,128)(2,1)S(1)}, u32[]{:S(2)}, u32[]{:S(2)}) collective-permute-start(bf16[256,1024]{1,0:T(8,128)(2,1)} %get-tuple-element.35), channel_id=1, source_target_pairs={{0,4},{4,0},{8,12},{12,8},{1,5},{5,1},{9,13},{13,9},{2,6},{6,2},{1... | collective-permute-start | bytes 1572872 | tf_op jit(solution)/shard_map/ppermute | solution.py:219
  52.6 1.8 collective-permute-start.4
  53.6 7.7 %collective-permute-start.7 = (bf16[256,1024]{1,0:T(8,128)(2,1)S(1)}, bf16[256,1024]{1,0:T(8,128)(2,1)S(1)}, u32[]{:S(2)}, u32[]{:S(2)}) collective-permute-start(bf16[256,1024]{1,0:T(8,128)(2,1)S(1)} %constant_dynamic-slice_fusion.refs_0_), channel_id=1, source_target_pairs={{0,2},{2,0},{1,3},{3,1},{4,6},{6,4},{5,7},{7,5},{8,10},{10,8},{9,1... | collective-permute-start | bytes 1572872 | tf_op jit(solution)/shard_map/ppermute | solution.py:219
  54.2 7.1 %collective-permute-start.9 = (bf16[256,1024]{1,0:T(8,128)(2,1)S(1)}, bf16[256,1024]{1,0:T(8,128)(2,1)S(1)}, u32[]{:S(2)}, u32[]{:S(2)}) collective-permute-start(bf16[256,1024]{1,0:T(8,128)(2,1)S(1)} %collective-permute-done.3.refs_2_), channel_id=1, source_target_pairs={{0,2},{2,0},{1,3},{3,1},{4,6},{6,4},{5,7},{7,5},{8,10},{10,8},{9,1... | collective-permute-start | bytes 1572872 | tf_op jit(solution)/shard_map/ppermute | solution.py:219
  60.6 2.1 %collective-permute-start.8 = (bf16[256,1024]{1,0:T(8,128)(2,1)S(1)}, bf16[256,1024]{1,0:T(8,128)(2,1)S(1)}, u32[]{:S(2)}, u32[]{:S(2)}) collective-permute-start(bf16[256,1024]{1,0:T(8,128)(2,1)S(1)} %collective-permute-done.5.refs_1_), channel_id=1, source_target_pairs={{0,2},{2,0},{1,3},{3,1},{4,6},{6,4},{5,7},{7,5},{8,10},{10,8},{9,1... | collective-permute-start | bytes 1572872 | tf_op jit(solution)/shard_map/ppermute | solution.py:219
  61.2 2.3 %collective-permute-start.10 = (bf16[256,1024]{1,0:T(8,128)(2,1)S(1)}, bf16[256,1024]{1,0:T(8,128)(2,1)S(1)}, u32[]{:S(2)}, u32[]{:S(2)}) collective-permute-start(bf16[256,1024]{1,0:T(8,128)(2,1)S(1)} %collective-permute-done.6.refs_3_), channel_id=1, source_target_pairs={{0,2},{2,0},{1,3},{3,1},{4,6},{6,4},{5,7},{7,5},{8,10},{10,8},{9,1... | collective-permute-start | bytes 1572872 | tf_op jit(solution)/shard_map/ppermute | solution.py:219
  65.6 78.8 %copy-start = (bf16[2048,1024]{1,0:T(8,128)(2,1)}, bf16[2048,1024]{1,0:T(8,128)(2,1)S(1)}, u32[]{:S(2)}) copy-start(bf16[2048,1024]{1,0:T(8,128)(2,1)S(1)} %get-tuple-element.26.a_ref) | copy-start | bytes 12582916
  65.6 5.8 %collective-permute-start.11 = (f32[4,64,128]{2,1,0:T(8,128)S(1)}, f32[4,64,128]{2,1,0:T(8,128)S(1)}, u32[]{:S(2)}, u32[]{:S(2)}) collective-permute-start(f32[4,64,128]{2,1,0:T(8,128)S(1)} %slice.28), channel_id=1, source_target_pairs={{0,1},{1,0},{2,3},{3,2},{4,5},{5,4},{6,7},{7,6},{8,9},{9,8},{10,11... | collective-permute-start | bytes 393224 | tf_op jit(solution)/shard_map/ppermute | solution.py:219
  71.5 5.0 %collective-permute-start.12 = (f32[4,64,128]{2,1,0:T(8,128)S(1)}, f32[4,64,128]{2,1,0:T(8,128)S(1)}, u32[]{:S(2)}, u32[]{:S(2)}) collective-permute-start(f32[4,64,128]{2,1,0:T(8,128)S(1)} %slice_add_fusion.3), channel_id=1, source_target_pairs={{0,4},{4,0},{8,12},{12,8},{1,5},{5,1},{9,13},{13,9},{2,6},{6,2},{1... | collective-permute-start | bytes 393224 | tf_op jit(solution)/shard_map/ppermute | solution.py:219
  76.5 7.6 %collective-permute-start.13 = (f32[4,64,128]{2,1,0:T(8,128)S(1)}, f32[4,64,128]{2,1,0:T(8,128)S(1)}, u32[]{:S(2)}, u32[]{:S(2)}) collective-permute-start(f32[4,64,128]{2,1,0:T(8,128)S(1)} %add.212), channel_id=1, source_target_pairs={{0,8},{4,12},{8,0},{12,4},{1,9},{5,13},{9,1},{13,5},{2,10},{6,14},... | collective-permute-start | bytes 393224 | tf_op jit(solution)/shard_map/ppermute | solution.py:219
  84.2 5.0 %collective-permute-start.14 = (f32[4,64,128]{2,1,0:T(8,128)S(1)}, f32[4,64,128]{2,1,0:T(8,128)S(1)}, u32[]{:S(2)}, u32[]{:S(2)}) collective-permute-start(f32[4,64,128]{2,1,0:T(8,128)S(1)} %add.213), channel_id=1, source_target_pairs={{0,1},{1,0},{2,3},{3,2},{4,5},{5,4},{6,7},{7,6},{8,9},{9,8},{10,11... | collective-permute-start | bytes 393224 | tf_op jit(solution)/shard_map/ppermute | solution.py:219
  89.2 1.6 collective-permute-start.15
  97.8 4.3 %collective-permute-start.16 = (bf16[4,64,128]{2,1,0:T(8,128)(2,1)S(1)}, bf16[4,64,128]{2,1,0:T(8,128)(2,1)S(1)}, u32[]{:S(2)}, u32[]{:S(2)}) collective-permute-start(bf16[4,64,128]{2,1,0:T(8,128)(2,1)S(1)} %slice.56), channel_id=1, source_target_pairs={{0,1},{1,0},{2,3},{3,2},{4,5},{5,4},{6,7},{7,6},{8,9},{9,8},{10,11... | collective-permute-start | bytes 196616 | tf_op jit(solution)/shard_map/ppermute | solution.py:219
  102.2 4.3 %collective-permute-start.17 = (bf16[4,64,128]{2,1,0:T(8,128)(2,1)S(1)}, bf16[4,64,128]{2,1,0:T(8,128)(2,1)S(1)}, u32[]{:S(2)}, u32[]{:S(2)}) collective-permute-start(bf16[4,64,128]{2,1,0:T(8,128)(2,1)S(1)} %fusion.15), channel_id=1, source_target_pairs={{0,4},{4,0},{8,12},{12,8},{1,5},{5,1},{9,13},{13,9},{2,6},{6,2},{1... | collective-permute-start | bytes 196616 | tf_op jit(solution)/shard_map/ppermute | solution.py:219
  106.5 5.8 %collective-permute-start.18 = (bf16[4,64,128]{2,1,0:T(8,128)(2,1)S(1)}, bf16[4,64,128]{2,1,0:T(8,128)(2,1)S(1)}, u32[]{:S(2)}, u32[]{:S(2)}) collective-permute-start(bf16[4,64,128]{2,1,0:T(8,128)(2,1)S(1)} %add_convert_fusion.5), channel_id=1, source_target_pairs={{0,8},{4,12},{8,0},{12,4},{1,9},{5,13},{9,1},{13,5},{2,10},{6,14},... | collective-permute-start | bytes 196616 | tf_op jit(solution)/shard_map/ppermute | solution.py:219
  112.4 4.3 %collective-permute-start.19 = (bf16[4,64,128]{2,1,0:T(8,128)(2,1)S(1)}, bf16[4,64,128]{2,1,0:T(8,128)(2,1)S(1)}, u32[]{:S(2)}, u32[]{:S(2)}) collective-permute-start(bf16[4,64,128]{2,1,0:T(8,128)(2,1)S(1)} %add_convert_fusion.4), channel_id=1, source_target_pairs={{0,1},{1,0},{2,3},{3,2},{4,5},{5,4},{6,7},{7,6},{8,9},{9,8},{10,11... | collective-permute-start | bytes 196616 | tf_op jit(solution)/shard_map/ppermute | solution.py:219
  116.7 1.4 collective-permute-start.20
  124.5 4.3 %collective-permute-start.21 = (bf16[4,64,128]{2,1,0:T(8,128)(2,1)S(1)}, bf16[4,64,128]{2,1,0:T(8,128)(2,1)S(1)}, u32[]{:S(2)}, u32[]{:S(2)}) collective-permute-start(bf16[4,64,128]{2,1,0:T(8,128)(2,1)S(1)} %slice.55), channel_id=1, source_target_pairs={{0,1},{1,0},{2,3},{3,2},{4,5},{5,4},{6,7},{7,6},{8,9},{9,8},{10,11... | collective-permute-start | bytes 196616 | tf_op jit(solution)/shard_map/ppermute | solution.py:219
  128.9 4.3 %collective-permute-start.22 = (bf16[4,64,128]{2,1,0:T(8,128)(2,1)S(1)}, bf16[4,64,128]{2,1,0:T(8,128)(2,1)S(1)}, u32[]{:S(2)}, u32[]{:S(2)}) collective-permute-start(bf16[4,64,128]{2,1,0:T(8,128)(2,1)S(1)} %fusion.14), channel_id=1, source_target_pairs={{0,4},{4,0},{8,12},{12,8},{1,5},{5,1},{9,13},{13,9},{2,6},{6,2},{1... | collective-permute-start | bytes 196616 | tf_op jit(solution)/shard_map/ppermute | solution.py:219
  133.2 5.4 %collective-permute-start.23 = (bf16[4,64,128]{2,1,0:T(8,128)(2,1)S(1)}, bf16[4,64,128]{2,1,0:T(8,128)(2,1)S(1)}, u32[]{:S(2)}, u32[]{:S(2)}) collective-permute-start(bf16[4,64,128]{2,1,0:T(8,128)(2,1)S(1)} %add_convert_fusion.3), channel_id=1, source_target_pairs={{0,8},{4,12},{8,0},{12,4},{1,9},{5,13},{9,1},{13,5},{2,10},{6,14},... | collective-permute-start | bytes 196616 | tf_op jit(solution)/shard_map/ppermute | solution.py:219
  138.6 4.3 %collective-permute-start.24 = (bf16[4,64,128]{2,1,0:T(8,128)(2,1)S(1)}, bf16[4,64,128]{2,1,0:T(8,128)(2,1)S(1)}, u32[]{:S(2)}, u32[]{:S(2)}) collective-permute-start(bf16[4,64,128]{2,1,0:T(8,128)(2,1)S(1)} %add_convert_fusion.2), channel_id=1, source_target_pairs={{0,1},{1,0},{2,3},{3,2},{4,5},{5,4},{6,7},{7,6},{8,9},{9,8},{10,11... | collective-permute-start | bytes 196616 | tf_op jit(solution)/shard_map/ppermute | solution.py:219
  143.0 1.4 collective-permute-start.25
  150.8 4.3 %collective-permute-start.26 = (bf16[4,64,128]{2,1,0:T(8,128)(2,1)S(1)}, bf16[4,64,128]{2,1,0:T(8,128)(2,1)S(1)}, u32[]{:S(2)}, u32[]{:S(2)}) collective-permute-start(bf16[4,64,128]{2,1,0:T(8,128)(2,1)S(1)} %slice.54), channel_id=1, source_target_pairs={{0,1},{1,0},{2,3},{3,2},{4,5},{5,4},{6,7},{7,6},{8,9},{9,8},{10,11... | collective-permute-start | bytes 196616 | tf_op jit(solution)/shard_map/ppermute | solution.py:219
  155.1 4.3 %collective-permute-start.27 = (bf16[4,64,128]{2,1,0:T(8,128)(2,1)S(1)}, bf16[4,64,128]{2,1,0:T(8,128)(2,1)S(1)}, u32[]{:S(2)}, u32[]{:S(2)}) collective-permute-start(bf16[4,64,128]{2,1,0:T(8,128)(2,1)S(1)} %fusion.13), channel_id=1, source_target_pairs={{0,4},{4,0},{8,12},{12,8},{1,5},{5,1},{9,13},{13,9},{2,6},{6,2},{1... | collective-permute-start | bytes 196616 | tf_op jit(solution)/shard_map/ppermute | solution.py:219
  159.5 5.4 %collective-permute-start.28 = (bf16[4,64,128]{2,1,0:T(8,128)(2,1)S(1)}, bf16[4,64,128]{2,1,0:T(8,128)(2,1)S(1)}, u32[]{:S(2)}, u32[]{:S(2)}) collective-permute-start(bf16[4,64,128]{2,1,0:T(8,128)(2,1)S(1)} %add_convert_fusion.1), channel_id=1, source_target_pairs={{0,8},{4,12},{8,0},{12,4},{1,9},{5,13},{9,1},{13,5},{2,10},{6,14},... | collective-permute-start | bytes 196616 | tf_op jit(solution)/shard_map/ppermute | solution.py:219
  164.9 4.3 %collective-permute-start.29 = (bf16[4,64,128]{2,1,0:T(8,128)(2,1)S(1)}, bf16[4,64,128]{2,1,0:T(8,128)(2,1)S(1)}, u32[]{:S(2)}, u32[]{:S(2)}) collective-permute-start(bf16[4,64,128]{2,1,0:T(8,128)(2,1)S(1)} %add_convert_fusion), channel_id=1, source_target_pairs={{0,1},{1,0},{2,3},{3,2},{4,5},{5,4},{6,7},{7,6},{8,9},{9,8},{10,11... | collective-permute-start | bytes 196616 | tf_op jit(solution)/shard_map/ppermute | solution.py:219
  169.2 1.4 collective-permute-start.30
  (2 other events, 14.6 us)

commit v12 on v11

--- a/solution.py
+++ b/solution.py
@@ -91,6 +91,10 @@
     for i in range(blocks):
         unit = jnp.where(square_col == square_row + SUB * i, 1.0, 0.0).astype(jnp.float32)
         work.append(jnp.concatenate([matrix[SUB * i : SUB * (i + 1), :], unit], axis=1))
+
+    def fill(register, k):
+        return jnp.broadcast_to(register[k : k + 1, :], (SUB, 2 * size))
+
     rows = []
     for b in range(blocks):
         for unused in range(-(-len(beside) // (blocks - b))):
@@ -102,23 +106,31 @@
             }
             for j in range(SUB)
         ]
-        pivots = jnp.zeros((SUB, 2 * size), jnp.float32)
-        for k in range(SUB):
-            pivot = jnp.broadcast_to(columns[k][b][k : k + 1, :], (SUB, 2 * size))
-            reciprocal = 1.0 / pivot
-            pivots = jnp.where(row_index == k, pivot, pivots)
-            work_row = jnp.broadcast_to(work[b][k : k + 1, :], (SUB, 2 * size))
-            later = [
-                jnp.broadcast_to(columns[j][b][k : k + 1, :], (SUB, 2 * size))
-                for j in range(k + 1, SUB)
-            ]
-            for i in range(b, blocks):
-                factor = columns[k][i] * reciprocal
-                if i == b:
-                    factor = jnp.where(row_index > k, factor, 0.0)
-                for j in range(k + 1, SUB):
-                    columns[j][i] = columns[j][i] - factor * later[j - k - 1]
-                work[i] = work[i] - factor * work_row
+        pivots = jnp.ones((SUB, 2 * size), jnp.float32)
+        for k in range(0, SUB, 2):
+            col_0, col_1 = columns[k], columns[k + 1]
+            a, h, d = fill(col_0[b], k), fill(col_1[b], k), fill(col_1[b], k + 1)
+            det = a * d - h * h
+            over_det, over_a = 1.0 / det, 1.0 / a
+            below_0 = jnp.where(row_index > k + 1, col_0[b], 0.0)
+            below_1 = jnp.where(row_index > k + 1, col_1[b], 0.0)
+            for j in range(k + 2, SUB):
+                entry_0, entry_1 = fill(columns[j][b], k), fill(columns[j][b], k + 1)
+                up_0 = d * entry_0 - h * entry_1
+                up_1 = a * entry_1 - h * entry_0
+                columns[j][b] = columns[j][b] - over_det * (below_0 * up_0 + below_1 * up_1)
+                up_0, up_1 = over_det * up_0, over_det * up_1
+                for i in range(b + 1, blocks):
+                    columns[j][i] = columns[j][i] - (col_0[i] * up_0 + col_1[i] * up_1)
+            row_0, row_1 = fill(work[b], k), fill(work[b], k + 1)
+            up_0 = over_det * (d * row_0 - h * row_1)
+            up_1 = over_det * (a * row_1 - h * row_0)
+            for i in range(b + 1, blocks):
+                work[i] = work[i] - (col_0[i] * up_0 + col_1[i] * up_1)
+            second = jnp.where(row_index == k + 1, h * over_a, 0.0)
+            work[b] = work[b] - (below_0 * up_0 + below_1 * up_1 + second * row_0)
+            pivots = jnp.where(row_index == k, a, pivots)
+            pivots = jnp.where(row_index == k + 1, det * over_a, pivots)
         rows.append(work[b] * lax.rsqrt(pivots))
     both = jnp.concatenate(rows, axis=0)
     keep = lax.broadcasted_iota(jnp.int32, (size, size), 1) >= lax.broadcasted_iota(
@@ -127,14 +139,17 @@
     return jnp.where(keep, both[:, :size], 0.0), both[:, size:]
 
 
-def shifted(whole_gram):
+def shifted_factor(whole_gram):
     size = whole_gram.shape[0]
     diagonal = lax.broadcasted_iota(jnp.int32, (size, size), 0) == lax.broadcasted_iota(
         jnp.int32, (size, size), 1
     )
     on_diagonal = jnp.where(diagonal, whole_gram, 0.0)
     trace = jnp.sum(jnp.sum(on_diagonal, axis=1, keepdims=True), axis=0, keepdims=True)
-    return jnp.where(diagonal, whole_gram + shift_ratio * trace, whole_gram)
+    scaled = whole_gram * (1.0 / trace)
+    upper, inverse = eliminate(jnp.where(diagonal, scaled + shift_ratio, scaled))
+    root = jnp.sqrt(trace)
+    return upper * root, inverse * (1.0 / root)
 
 
 def wide_of(at_ref, z_refs):
@@ -144,7 +159,7 @@
 
 def first_pass(at_ref, z_refs):
     wide = wide_of(at_ref, z_refs)
-    upper, inverse_one = eliminate(shifted(gram_of(wide)))
+    upper, inverse_one = shifted_factor(gram_of(wide))
     return small_times_wide(inverse_one, wide), upper
 
 

time: 179 us -> 178 us (level)
  transfers between devices with their start and end apart: 31 -> 31, of which waited for: 26 -> 26; matrix products, arithmetic and copies ran while one was open for 2% -> 2% of each run, Pallas kernels for 4% -> 3%
where the time goes in v12:
time: 178 us
  waiting for transfers between devices  98.1 us (55%)
  starting transfers between devices  35.8 us (20%)
  Pallas kernels  32.7 us (18%)
  local copies, waits for them, and re-layouts  5.19 us (3%)
  matrix products  3.97 us (2%)
    ppermute x31, waiting for transfers between devices, from_xor(): return lax.ppermute(value, axis, [(i, i ^ offset) for i in range(size)])  98.1 us
    ppermute x31, starting transfers between devices, from_xor(): return lax.ppermute(value, axis, [(i, i ^ offset) for i in range(size)])  35.8 us
    pallas_call x6, Pallas kernels, call(): pl.pallas_call(kernel, out_shape=out_shapes, in_specs=[pl.BlockSpec(memor...  32.7 us
    dot_general x1, matrix products, per_device_transposed(): lax.dot_general(omega, states, (((0,), (1,)), ((), ())), preferred_elemen...  3.97 us
  transfers between devices with their start and end apart: 31, of which 26 were waited for; matrix products, arithmetic and copies ran while one was open for 2% of the time, Pallas kernels for 3%

profile of v12, /device:TPU:0, one launch (start us, length us, event | category | flops | bytes accessed | tf_op | source)
XLA Modules:
  0.0 177.7 jit_solution(11190451364681485150)
XLA Ops:
  1.3 4.0 %convolution_bitcast_fusion = f32[8,2,8,128]{3,2,1,0:T(8,128)S(1)} fusion(bf16[256,4096]{1,0:T(8,128)(2,1)} %param.3, s32[]{:T(128)S(6)} %xor.72, s32[4096]{0:T(1024)S(1)} %add_multiply_fusion), kind=kOutput, calls=%fused_computation | convolution fusion | flops 152043520 | bytes 2179076 | tf_op jit(solution)/shard_map/dot_general | solution.py:284
  5.3 4.1 %collective-permute-start = (f32[2,64,128]{2,1,0:T(8,128)S(1)}, f32[2,64,128]{2,1,0:T(8,128)S(1)}, u32[]{:S(2)}, u32[]{:S(2)}) collective-permute-start(f32[2,64,128]{2,1,0:T(8,128)S(1)} %bitcast.16), channel_id=1, source_target_pairs={{0,8},{4,12},{8,0},{12,4},{1,9},{5,13},{9,1},{13,5},{2,10},{6,14},... | collective-permute-start | bytes 196616 | tf_op jit(solution)/shard_map/ppermute | solution.py:234
  9.4 3.6 %collective-permute-done = f32[2,64,128]{2,1,0:T(8,128)S(1)} collective-permute-done((f32[2,64,128]{2,1,0:T(8,128)S(1)}, f32[2,64,128]{2,1,0:T(8,128)S(1)}, u32[]{:S(2)}, u32[]{:S(2)}) %collective-permute-start) | collective-permute-done | bytes 65568 | tf_op jit(solution)/shard_map/ppermute | solution.py:234
  13.8 3.4 %collective-permute-start.3 = (bf16[256,1024]{1,0:T(8,128)(2,1)S(1)}, bf16[256,1024]{1,0:T(8,128)(2,1)S(1)}, u32[]{:S(2)}, u32[]{:S(2)}) collective-permute-start(bf16[256,1024]{1,0:T(8,128)(2,1)S(1)} %constant_dynamic-slice_fusion.3), channel_id=1, source_target_pairs={{0,8},{4,12},{8,0},{12,4},{1,9},{5,13},{9,1},{13,5},{2,10},{6,14},... | collective-permute-start | bytes 1572872 | tf_op jit(solution)/shard_map/ppermute | solution.py:234
  17.2 2.9 %collective-permute-done.1 = f32[4,64,128]{2,1,0:T(8,128)S(1)} collective-permute-done((f32[4,64,128]{2,1,0:T(8,128)S(1)}, f32[4,64,128]{2,1,0:T(8,128)S(1)}, u32[]{:S(2)}, u32[]{:S(2)}) %collective-permute-start.1) | collective-permute-done | bytes 131104 | tf_op jit(solution)/shard_map/ppermute | solution.py:234
  23.2 2.3 %collective-permute-start.6 = (bf16[256,1024]{1,0:T(8,128)(2,1)}, bf16[256,1024]{1,0:T(8,128)(2,1)S(1)}, u32[]{:S(2)}, u32[]{:S(2)}) collective-permute-start(bf16[256,1024]{1,0:T(8,128)(2,1)} %get-tuple-element.34), channel_id=1, source_target_pairs={{0,12},{4,8},{8,4},{12,0},{1,13},{5,9},{9,5},{13,1},{2,14},{6,10},... | collective-permute-start | bytes 1572872 | tf_op jit(solution)/shard_map/ppermute | solution.py:234
  26.6 26.0 %collective-permute-done.3.refs_2_ = bf16[256,1024]{1,0:T(8,128)(2,1)S(1)} collective-permute-done((bf16[256,1024]{1,0:T(8,128)(2,1)S(1)}, bf16[256,1024]{1,0:T(8,128)(2,1)S(1)}, u32[]{:S(2)}, u32[]{:S(2)}) %collective-permute-start.3) | collective-permute-done | bytes 524320 | tf_op jit(solution)/shard_map/ppermute | solution.py:234
  54.3 6.0 %shard_map.41 = (bf16[64,2048]{1,0:T(8,128)(2,1)S(1)}, f32[64,64]{1,0:T(8,128)S(1)}) custom-call(s32[8]{0:T(128)S(1)} %fusion.19.at_ref, f32[8,64,128]{2,1,0:T(8,128)S(1)} %add.206.z_ref, f32[8,64,128]{2,1,0:T(8,128)S(1)} %collective-permute-done.4.other_ref), custom_call_target="tpu_custom_call" | custom-call | flops 402653184 | bytes 524288 | tf_op jit(solution)/shard_map/pallas_call | solution.py:217
  63.2 2.1 %shard_map.42 = (bf16[2048,1024]{1,0:T(8,128)(2,1)S(1)}, f32[8,64,128]{2,1,0:T(8,128)S(1)}) custom-call(s32[8]{0:T(128)S(1)} %fusion.17.at_ref, bf16[64,2048]{1,0:T(8,128)(2,1)S(1)} %get-tuple-element.21.basis_ref, bf16[256,1024]{1,0:T(8,128)(2,1)S(1)} %constant_dynamic-slice_fusion.refs_0_, bf16[256,1024]{1,0:T(8,128)(2,1)S(1)} %collective-permute-done.5.refs_1_, ...), custom_call_target="tpu_custom_call" | custom-call | flops 939524096 | bytes 4456448 | tf_op jit(solution)/shard_map/pallas_call | solution.py:217
  66.9 4.3 %collective-permute-done.11 = f32[4,64,128]{2,1,0:T(8,128)S(1)} collective-permute-done((f32[4,64,128]{2,1,0:T(8,128)S(1)}, f32[4,64,128]{2,1,0:T(8,128)S(1)}, u32[]{:S(2)}, u32[]{:S(2)}) %collective-permute-start.11) | collective-permute-done | bytes 131104 | tf_op jit(solution)/shard_map/ppermute | solution.py:234
  71.2 2.4 %collective-permute-start.12 = (f32[4,64,128]{2,1,0:T(8,128)S(1)}, f32[4,64,128]{2,1,0:T(8,128)S(1)}, u32[]{:S(2)}, u32[]{:S(2)}) collective-permute-start(f32[4,64,128]{2,1,0:T(8,128)S(1)} %slice_add_fusion.3), channel_id=1, source_target_pairs={{0,4},{4,0},{8,12},{12,8},{1,5},{5,1},{9,13},{13,9},{2,6},{6,2},{1... | collective-permute-start | bytes 393224 | tf_op jit(solution)/shard_map/ppermute | solution.py:234
  73.6 3.0 %collective-permute-done.12 = f32[4,64,128]{2,1,0:T(8,128)S(1)} collective-permute-done((f32[4,64,128]{2,1,0:T(8,128)S(1)}, f32[4,64,128]{2,1,0:T(8,128)S(1)}, u32[]{:S(2)}, u32[]{:S(2)}) %collective-permute-start.12) | collective-permute-done | bytes 131104 | tf_op jit(solution)/shard_map/ppermute | solution.py:234
  76.5 3.0 %collective-permute-start.13 = (f32[4,64,128]{2,1,0:T(8,128)S(1)}, f32[4,64,128]{2,1,0:T(8,128)S(1)}, u32[]{:S(2)}, u32[]{:S(2)}) collective-permute-start(f32[4,64,128]{2,1,0:T(8,128)S(1)} %add.212), channel_id=1, source_target_pairs={{0,8},{4,12},{8,0},{12,4},{1,9},{5,13},{9,1},{13,5},{2,10},{6,14},... | collective-permute-start | bytes 393224 | tf_op jit(solution)/shard_map/ppermute | solution.py:234
  79.5 4.6 %collective-permute-done.13 = f32[4,64,128]{2,1,0:T(8,128)S(1)} collective-permute-done((f32[4,64,128]{2,1,0:T(8,128)S(1)}, f32[4,64,128]{2,1,0:T(8,128)S(1)}, u32[]{:S(2)}, u32[]{:S(2)}) %collective-permute-start.13) | collective-permute-done | bytes 131104 | tf_op jit(solution)/shard_map/ppermute | solution.py:234
  85.7 3.5 %collective-permute-done.14 = f32[4,64,128]{2,1,0:T(8,128)S(1)} collective-permute-done((f32[4,64,128]{2,1,0:T(8,128)S(1)}, f32[4,64,128]{2,1,0:T(8,128)S(1)}, u32[]{:S(2)}, u32[]{:S(2)}) %collective-permute-start.14) | collective-permute-done | bytes 131104 | tf_op jit(solution)/shard_map/ppermute | solution.py:234
  90.8 6.7 %shard_map.43 = f32[8,64,128]{2,1,0:T(8,128)S(1)} custom-call(s32[8]{0:T(128)S(1)} %fusion.17.at_ref, f32[8,64,128]{2,1,0:T(8,128)S(1)} %pad_maximum_fusion.z_ref, f32[8,64,128]{2,1,0:T(8,128)S(1)} %collective-permute-done.15.other_ref, bf16[2048,1024]{1,0:T(8,128)(2,1)S(1)} %get-tuple-element.26.a_ref), custom_call_target="tpu_custom_call" | custom-call | flops 939524096 | bytes 4718592 | tf_op jit(solution)/shard_map/pallas_call | solution.py:217
  99.1 2.8 %collective-permute-done.16 = bf16[4,64,128]{2,1,0:T(8,128)(2,1)S(1)} collective-permute-done((bf16[4,64,128]{2,1,0:T(8,128)(2,1)S(1)}, bf16[4,64,128]{2,1,0:T(8,128)(2,1)S(1)}, u32[]{:S(2)}, u32[]{:S(2)}) %collective-permute-start.16) | collective-permute-done | bytes 65568 | tf_op jit(solution)/shard_map/ppermute | solution.py:234
  102.4 3.8 %collective-permute-done.17 = bf16[4,64,128]{2,1,0:T(8,128)(2,1)S(1)} collective-permute-done((bf16[4,64,128]{2,1,0:T(8,128)(2,1)S(1)}, bf16[4,64,128]{2,1,0:T(8,128)(2,1)S(1)}, u32[]{:S(2)}, u32[]{:S(2)}) %collective-permute-start.17) | collective-permute-done | bytes 65568 | tf_op jit(solution)/shard_map/ppermute | solution.py:234
  107.6 4.4 %collective-permute-done.18 = bf16[4,64,128]{2,1,0:T(8,128)(2,1)S(1)} collective-permute-done((bf16[4,64,128]{2,1,0:T(8,128)(2,1)S(1)}, bf16[4,64,128]{2,1,0:T(8,128)(2,1)S(1)}, u32[]{:S(2)}, u32[]{:S(2)}) %collective-permute-start.18) | collective-permute-done | bytes 65568 | tf_op jit(solution)/shard_map/ppermute | solution.py:234
  113.6 2.8 %collective-permute-done.19 = bf16[4,64,128]{2,1,0:T(8,128)(2,1)S(1)} collective-permute-done((bf16[4,64,128]{2,1,0:T(8,128)(2,1)S(1)}, bf16[4,64,128]{2,1,0:T(8,128)(2,1)S(1)}, u32[]{:S(2)}, u32[]{:S(2)}) %collective-permute-start.19) | collective-permute-done | bytes 65568 | tf_op jit(solution)/shard_map/ppermute | solution.py:234
  117.8 6.0 %shard_map.44 = f32[8,64,128]{2,1,0:T(8,128)S(1)} custom-call(s32[8]{0:T(128)S(1)} %fusion.17.at_ref, bf16[8,64,128]{2,1,0:T(8,128)(2,1)S(1)} %pad_maximum_fusion.2.z_ref, bf16[8,64,128]{2,1,0:T(8,128)(2,1)S(1)} %collective-permute-done.20.other_ref, bf16[2048,1024]{1,0:T(8,128)(2,1)S(1)} %get-tuple-element.26.a_ref), custom_call_target="tpu_custom_call" | custom-call | flops 939524096 | bytes 4456448 | tf_op jit(solution)/shard_map/pallas_call | solution.py:217
  125.4 2.8 %collective-permute-done.21 = bf16[4,64,128]{2,1,0:T(8,128)(2,1)S(1)} collective-permute-done((bf16[4,64,128]{2,1,0:T(8,128)(2,1)S(1)}, bf16[4,64,128]{2,1,0:T(8,128)(2,1)S(1)}, u32[]{:S(2)}, u32[]{:S(2)}) %collective-permute-start.21) | collective-permute-done | bytes 65568 | tf_op jit(solution)/shard_map/ppermute | solution.py:234
  128.3 4.3 %collective-permute-done.22 = bf16[4,64,128]{2,1,0:T(8,128)(2,1)S(1)} collective-permute-done((bf16[4,64,128]{2,1,0:T(8,128)(2,1)S(1)}, bf16[4,64,128]{2,1,0:T(8,128)(2,1)S(1)}, u32[]{:S(2)}, u32[]{:S(2)}) %collective-permute-start.22) | collective-permute-done | bytes 65568 | tf_op jit(solution)/shard_map/ppermute | solution.py:234
  133.6 4.4 %collective-permute-done.23 = bf16[4,64,128]{2,1,0:T(8,128)(2,1)S(1)} collective-permute-done((bf16[4,64,128]{2,1,0:T(8,128)(2,1)S(1)}, bf16[4,64,128]{2,1,0:T(8,128)(2,1)S(1)}, u32[]{:S(2)}, u32[]{:S(2)}) %collective-permute-start.23) | collective-permute-done | bytes 65568 | tf_op jit(solution)/shard_map/ppermute | solution.py:234
  139.6 2.8 %collective-permute-done.24 = bf16[4,64,128]{2,1,0:T(8,128)(2,1)S(1)} collective-permute-done((bf16[4,64,128]{2,1,0:T(8,128)(2,1)S(1)}, bf16[4,64,128]{2,1,0:T(8,128)(2,1)S(1)}, u32[]{:S(2)}, u32[]{:S(2)}) %collective-permute-start.24) | collective-permute-done | bytes 65568 | tf_op jit(solution)/shard_map/ppermute | solution.py:234
  143.8 6.0 %shard_map.45 = f32[8,64,128]{2,1,0:T(8,128)S(1)} custom-call(s32[8]{0:T(128)S(1)} %fusion.17.at_ref, bf16[8,64,128]{2,1,0:T(8,128)(2,1)S(1)} %pad_maximum_fusion.3.z_ref, bf16[8,64,128]{2,1,0:T(8,128)(2,1)S(1)} %collective-permute-done.25.other_ref, bf16[2048,1024]{1,0:T(8,128)(2,1)S(1)} %get-tuple-element.26.a_ref), custom_call_target="tpu_custom_call" | custom-call | flops 939524096 | bytes 4456448 | tf_op jit(solution)/shard_map/pallas_call | solution.py:217
  151.4 2.8 %collective-permute-done.26 = bf16[4,64,128]{2,1,0:T(8,128)(2,1)S(1)} collective-permute-done((bf16[4,64,128]{2,1,0:T(8,128)(2,1)S(1)}, bf16[4,64,128]{2,1,0:T(8,128)(2,1)S(1)}, u32[]{:S(2)}, u32[]{:S(2)}) %collective-permute-start.26) | collective-permute-done | bytes 65568 | tf_op jit(solution)/shard_map/ppermute | solution.py:234
  154.3 4.3 %collective-permute-done.27 = bf16[4,64,128]{2,1,0:T(8,128)(2,1)S(1)} collective-permute-done((bf16[4,64,128]{2,1,0:T(8,128)(2,1)S(1)}, bf16[4,64,128]{2,1,0:T(8,128)(2,1)S(1)}, u32[]{:S(2)}, u32[]{:S(2)}) %collective-permute-start.27) | collective-permute-done | bytes 65568 | tf_op jit(solution)/shard_map/ppermute | solution.py:234
  159.5 4.4 %collective-permute-done.28 = bf16[4,64,128]{2,1,0:T(8,128)(2,1)S(1)} collective-permute-done((bf16[4,64,128]{2,1,0:T(8,128)(2,1)S(1)}, bf16[4,64,128]{2,1,0:T(8,128)(2,1)S(1)}, u32[]{:S(2)}, u32[]{:S(2)}) %collective-permute-start.28) | collective-permute-done | bytes 65568 | tf_op jit(solution)/shard_map/ppermute | solution.py:234
  165.5 2.8 %collective-permute-done.29 = bf16[4,64,128]{2,1,0:T(8,128)(2,1)S(1)} collective-permute-done((bf16[4,64,128]{2,1,0:T(8,128)(2,1)S(1)}, bf16[4,64,128]{2,1,0:T(8,128)(2,1)S(1)}, u32[]{:S(2)}, u32[]{:S(2)}) %collective-permute-start.29) | collective-permute-done | bytes 65568 | tf_op jit(solution)/shard_map/ppermute | solution.py:234
  169.7 2.2 %copy-done.1 = bf16[2048,1024]{1,0:T(8,128)(2,1)S(1)} copy-done((bf16[2048,1024]{1,0:T(8,128)(2,1)S(1)}, bf16[2048,1024]{1,0:T(8,128)(2,1)}, u32[]{:S(2)}) %copy-start.1) | copy-done | bytes 4194328
  171.9 5.8 %shard_map.46 = f32[64,512]{1,0:T(8,128)} custom-call(s32[8]{0:T(128)S(1)} %fusion.17.at_ref, s32[1]{0:T(128)} %bitcast.core_ref, bf16[8,64,128]{2,1,0:T(8,128)(2,1)S(1)} %pad_maximum_fusion.4.z_ref, bf16[8,64,128]{2,1,0:T(8,128)(2,1)S(1)} %collective-permute-done.30.other_ref, bf16[2048,1024]{1,0:T(8,128)(2,1)S(1)} %copy-done.1), custom_call_target="tpu_custom_call" | custom-call | flops 939524096 | bytes 4456448 | tf_op jit(solution)/shard_map/pallas_call | solution.py:217
  (76 shorter events, 32.1 us)
Async XLA Ops:
  5.3 7.8 %collective-permute-start = (f32[2,64,128]{2,1,0:T(8,128)S(1)}, f32[2,64,128]{2,1,0:T(8,128)S(1)}, u32[]{:S(2)}, u32[]{:S(2)}) collective-permute-start(f32[2,64,128]{2,1,0:T(8,128)S(1)} %bitcast.16), channel_id=1, source_target_pairs={{0,8},{4,12},{8,0},{12,4},{1,9},{5,13},{9,1},{13,5},{2,10},{6,14},... | collective-permute-start | bytes 196616 | tf_op jit(solution)/shard_map/ppermute | solution.py:234
  13.1 7.0 %collective-permute-start.1 = (f32[4,64,128]{2,1,0:T(8,128)S(1)}, f32[4,64,128]{2,1,0:T(8,128)S(1)}, u32[]{:S(2)}, u32[]{:S(2)}) collective-permute-start(f32[4,64,128]{2,1,0:T(8,128)S(1)} %pad_maximum_fusion.1), channel_id=1, source_target_pairs={{0,4},{4,0},{8,12},{12,8},{1,5},{5,1},{9,13},{13,9},{2,6},{6,2},{1... | collective-permute-start | bytes 393224 | tf_op jit(solution)/shard_map/ppermute | solution.py:234
  13.8 38.8 %collective-permute-start.3 = (bf16[256,1024]{1,0:T(8,128)(2,1)S(1)}, bf16[256,1024]{1,0:T(8,128)(2,1)S(1)}, u32[]{:S(2)}, u32[]{:S(2)}) collective-permute-start(bf16[256,1024]{1,0:T(8,128)(2,1)S(1)} %constant_dynamic-slice_fusion.3), channel_id=1, source_target_pairs={{0,8},{4,12},{8,0},{12,4},{1,9},{5,13},{9,1},{13,5},{2,10},{6,14},... | collective-permute-start | bytes 1572872 | tf_op jit(solution)/shard_map/ppermute | solution.py:234
  20.1 6.4 %collective-permute-start.2 = (f32[8,64,128]{2,1,0:T(8,128)S(1)}, f32[8,64,128]{2,1,0:T(8,128)S(1)}, u32[]{:S(2)}, u32[]{:S(2)}) collective-permute-start(f32[8,64,128]{2,1,0:T(8,128)S(1)} %constant_dynamic-update-slice_fusion), channel_id=1, source_target_pairs={{0,1},{1,0},{2,3},{3,2},{4,5},{5,4},{6,7},{7,6},{8,9},{9,8},{10,11... | collective-permute-start | bytes 786440 | tf_op jit(solution)/shard_map/ppermute | solution.py:234
  23.2 37.2 %collective-permute-start.6 = (bf16[256,1024]{1,0:T(8,128)(2,1)}, bf16[256,1024]{1,0:T(8,128)(2,1)S(1)}, u32[]{:S(2)}, u32[]{:S(2)}) collective-permute-start(bf16[256,1024]{1,0:T(8,128)(2,1)} %get-tuple-element.34), channel_id=1, source_target_pairs={{0,12},{4,8},{8,4},{12,0},{1,13},{5,9},{9,5},{13,1},{2,14},{6,10},... | collective-permute-start | bytes 1572872 | tf_op jit(solution)/shard_map/ppermute | solution.py:234
  25.5 34.9 %collective-permute-start.5 = (bf16[256,1024]{1,0:T(8,128)(2,1)}, bf16[256,1024]{1,0:T(8,128)(2,1)S(1)}, u32[]{:S(2)}, u32[]{:S(2)}) collective-permute-start(bf16[256,1024]{1,0:T(8,128)(2,1)} %get-tuple-element.35), channel_id=1, source_target_pairs={{0,4},{4,0},{8,12},{12,8},{1,5},{5,1},{9,13},{13,9},{2,6},{6,2},{1... | collective-permute-start | bytes 1572872 | tf_op jit(solution)/shard_map/ppermute | solution.py:234
  52.6 1.8 collective-permute-start.4
  53.6 7.4 %collective-permute-start.7 = (bf16[256,1024]{1,0:T(8,128)(2,1)S(1)}, bf16[256,1024]{1,0:T(8,128)(2,1)S(1)}, u32[]{:S(2)}, u32[]{:S(2)}) collective-permute-start(bf16[256,1024]{1,0:T(8,128)(2,1)S(1)} %constant_dynamic-slice_fusion.refs_0_), channel_id=1, source_target_pairs={{0,2},{2,0},{1,3},{3,1},{4,6},{6,4},{5,7},{7,5},{8,10},{10,8},{9,1... | collective-permute-start | bytes 1572872 | tf_op jit(solution)/shard_map/ppermute | solution.py:234
  54.2 6.8 %collective-permute-start.9 = (bf16[256,1024]{1,0:T(8,128)(2,1)S(1)}, bf16[256,1024]{1,0:T(8,128)(2,1)S(1)}, u32[]{:S(2)}, u32[]{:S(2)}) collective-permute-start(bf16[256,1024]{1,0:T(8,128)(2,1)S(1)} %collective-permute-done.3.refs_2_), channel_id=1, source_target_pairs={{0,2},{2,0},{1,3},{3,1},{4,6},{6,4},{5,7},{7,5},{8,10},{10,8},{9,1... | collective-permute-start | bytes 1572872 | tf_op jit(solution)/shard_map/ppermute | solution.py:234
  60.4 2.1 %collective-permute-start.8 = (bf16[256,1024]{1,0:T(8,128)(2,1)S(1)}, bf16[256,1024]{1,0:T(8,128)(2,1)S(1)}, u32[]{:S(2)}, u32[]{:S(2)}) collective-permute-start(bf16[256,1024]{1,0:T(8,128)(2,1)S(1)} %collective-permute-done.5.refs_1_), channel_id=1, source_target_pairs={{0,2},{2,0},{1,3},{3,1},{4,6},{6,4},{5,7},{7,5},{8,10},{10,8},{9,1... | collective-permute-start | bytes 1572872 | tf_op jit(solution)/shard_map/ppermute | solution.py:234
  60.9 2.3 %collective-permute-start.10 = (bf16[256,1024]{1,0:T(8,128)(2,1)S(1)}, bf16[256,1024]{1,0:T(8,128)(2,1)S(1)}, u32[]{:S(2)}, u32[]{:S(2)}) collective-permute-start(bf16[256,1024]{1,0:T(8,128)(2,1)S(1)} %collective-permute-done.6.refs_3_), channel_id=1, source_target_pairs={{0,2},{2,0},{1,3},{3,1},{4,6},{6,4},{5,7},{7,5},{8,10},{10,8},{9,1... | collective-permute-start | bytes 1572872 | tf_op jit(solution)/shard_map/ppermute | solution.py:234
  65.3 78.5 %copy-start = (bf16[2048,1024]{1,0:T(8,128)(2,1)}, bf16[2048,1024]{1,0:T(8,128)(2,1)S(1)}, u32[]{:S(2)}) copy-start(bf16[2048,1024]{1,0:T(8,128)(2,1)S(1)} %get-tuple-element.26.a_ref) | copy-start | bytes 12582916
  65.3 5.8 %collective-permute-start.11 = (f32[4,64,128]{2,1,0:T(8,128)S(1)}, f32[4,64,128]{2,1,0:T(8,128)S(1)}, u32[]{:S(2)}, u32[]{:S(2)}) collective-permute-start(f32[4,64,128]{2,1,0:T(8,128)S(1)} %slice.28), channel_id=1, source_target_pairs={{0,1},{1,0},{2,3},{3,2},{4,5},{5,4},{6,7},{7,6},{8,9},{9,8},{10,11... | collective-permute-start | bytes 393224 | tf_op jit(solution)/shard_map/ppermute | solution.py:234
  71.2 5.3 %collective-permute-start.12 = (f32[4,64,128]{2,1,0:T(8,128)S(1)}, f32[4,64,128]{2,1,0:T(8,128)S(1)}, u32[]{:S(2)}, u32[]{:S(2)}) collective-permute-start(f32[4,64,128]{2,1,0:T(8,128)S(1)} %slice_add_fusion.3), channel_id=1, source_target_pairs={{0,4},{4,0},{8,12},{12,8},{1,5},{5,1},{9,13},{13,9},{2,6},{6,2},{1... | collective-permute-start | bytes 393224 | tf_op jit(solution)/shard_map/ppermute | solution.py:234
  76.5 7.6 %collective-permute-start.13 = (f32[4,64,128]{2,1,0:T(8,128)S(1)}, f32[4,64,128]{2,1,0:T(8,128)S(1)}, u32[]{:S(2)}, u32[]{:S(2)}) collective-permute-start(f32[4,64,128]{2,1,0:T(8,128)S(1)} %add.212), channel_id=1, source_target_pairs={{0,8},{4,12},{8,0},{12,4},{1,9},{5,13},{9,1},{13,5},{2,10},{6,14},... | collective-permute-start | bytes 393224 | tf_op jit(solution)/shard_map/ppermute | solution.py:234
  84.2 5.0 %collective-permute-start.14 = (f32[4,64,128]{2,1,0:T(8,128)S(1)}, f32[4,64,128]{2,1,0:T(8,128)S(1)}, u32[]{:S(2)}, u32[]{:S(2)}) collective-permute-start(f32[4,64,128]{2,1,0:T(8,128)S(1)} %add.213), channel_id=1, source_target_pairs={{0,1},{1,0},{2,3},{3,2},{4,5},{5,4},{6,7},{7,6},{8,9},{9,8},{10,11... | collective-permute-start | bytes 393224 | tf_op jit(solution)/shard_map/ppermute | solution.py:234
  89.2 1.6 collective-permute-start.15
  97.5 4.3 %collective-permute-start.16 = (bf16[4,64,128]{2,1,0:T(8,128)(2,1)S(1)}, bf16[4,64,128]{2,1,0:T(8,128)(2,1)S(1)}, u32[]{:S(2)}, u32[]{:S(2)}) collective-permute-start(bf16[4,64,128]{2,1,0:T(8,128)(2,1)S(1)} %slice.56), channel_id=1, source_target_pairs={{0,1},{1,0},{2,3},{3,2},{4,5},{5,4},{6,7},{7,6},{8,9},{9,8},{10,11... | collective-permute-start | bytes 196616 | tf_op jit(solution)/shard_map/ppermute | solution.py:234
  101.9 4.3 %collective-permute-start.17 = (bf16[4,64,128]{2,1,0:T(8,128)(2,1)S(1)}, bf16[4,64,128]{2,1,0:T(8,128)(2,1)S(1)}, u32[]{:S(2)}, u32[]{:S(2)}) collective-permute-start(bf16[4,64,128]{2,1,0:T(8,128)(2,1)S(1)} %fusion.15), channel_id=1, source_target_pairs={{0,4},{4,0},{8,12},{12,8},{1,5},{5,1},{9,13},{13,9},{2,6},{6,2},{1... | collective-permute-start | bytes 196616 | tf_op jit(solution)/shard_map/ppermute | solution.py:234
  106.2 5.8 %collective-permute-start.18 = (bf16[4,64,128]{2,1,0:T(8,128)(2,1)S(1)}, bf16[4,64,128]{2,1,0:T(8,128)(2,1)S(1)}, u32[]{:S(2)}, u32[]{:S(2)}) collective-permute-start(bf16[4,64,128]{2,1,0:T(8,128)(2,1)S(1)} %add_convert_fusion.5), channel_id=1, source_target_pairs={{0,8},{4,12},{8,0},{12,4},{1,9},{5,13},{9,1},{13,5},{2,10},{6,14},... | collective-permute-start | bytes 196616 | tf_op jit(solution)/shard_map/ppermute | solution.py:234
  112.0 4.3 %collective-permute-start.19 = (bf16[4,64,128]{2,1,0:T(8,128)(2,1)S(1)}, bf16[4,64,128]{2,1,0:T(8,128)(2,1)S(1)}, u32[]{:S(2)}, u32[]{:S(2)}) collective-permute-start(bf16[4,64,128]{2,1,0:T(8,128)(2,1)S(1)} %add_convert_fusion.4), channel_id=1, source_target_pairs={{0,1},{1,0},{2,3},{3,2},{4,5},{5,4},{6,7},{7,6},{8,9},{9,8},{10,11... | collective-permute-start | bytes 196616 | tf_op jit(solution)/shard_map/ppermute | solution.py:234
  116.4 1.4 collective-permute-start.20
  123.9 4.3 %collective-permute-start.21 = (bf16[4,64,128]{2,1,0:T(8,128)(2,1)S(1)}, bf16[4,64,128]{2,1,0:T(8,128)(2,1)S(1)}, u32[]{:S(2)}, u32[]{:S(2)}) collective-permute-start(bf16[4,64,128]{2,1,0:T(8,128)(2,1)S(1)} %slice.55), channel_id=1, source_target_pairs={{0,1},{1,0},{2,3},{3,2},{4,5},{5,4},{6,7},{7,6},{8,9},{9,8},{10,11... | collective-permute-start | bytes 196616 | tf_op jit(solution)/shard_map/ppermute | solution.py:234
  128.2 4.3 %collective-permute-start.22 = (bf16[4,64,128]{2,1,0:T(8,128)(2,1)S(1)}, bf16[4,64,128]{2,1,0:T(8,128)(2,1)S(1)}, u32[]{:S(2)}, u32[]{:S(2)}) collective-permute-start(bf16[4,64,128]{2,1,0:T(8,128)(2,1)S(1)} %fusion.14), channel_id=1, source_target_pairs={{0,4},{4,0},{8,12},{12,8},{1,5},{5,1},{9,13},{13,9},{2,6},{6,2},{1... | collective-permute-start | bytes 196616 | tf_op jit(solution)/shard_map/ppermute | solution.py:234
  132.6 5.4 %collective-permute-start.23 = (bf16[4,64,128]{2,1,0:T(8,128)(2,1)S(1)}, bf16[4,64,128]{2,1,0:T(8,128)(2,1)S(1)}, u32[]{:S(2)}, u32[]{:S(2)}) collective-permute-start(bf16[4,64,128]{2,1,0:T(8,128)(2,1)S(1)} %add_convert_fusion.3), channel_id=1, source_target_pairs={{0,8},{4,12},{8,0},{12,4},{1,9},{5,13},{9,1},{13,5},{2,10},{6,14},... | collective-permute-start | bytes 196616 | tf_op jit(solution)/shard_map/ppermute | solution.py:234
  138.0 4.3 %collective-permute-start.24 = (bf16[4,64,128]{2,1,0:T(8,128)(2,1)S(1)}, bf16[4,64,128]{2,1,0:T(8,128)(2,1)S(1)}, u32[]{:S(2)}, u32[]{:S(2)}) collective-permute-start(bf16[4,64,128]{2,1,0:T(8,128)(2,1)S(1)} %add_convert_fusion.2), channel_id=1, source_target_pairs={{0,1},{1,0},{2,3},{3,2},{4,5},{5,4},{6,7},{7,6},{8,9},{9,8},{10,11... | collective-permute-start | bytes 196616 | tf_op jit(solution)/shard_map/ppermute | solution.py:234
  142.4 1.4 collective-permute-start.25
  149.8 4.3 %collective-permute-start.26 = (bf16[4,64,128]{2,1,0:T(8,128)(2,1)S(1)}, bf16[4,64,128]{2,1,0:T(8,128)(2,1)S(1)}, u32[]{:S(2)}, u32[]{:S(2)}) collective-permute-start(bf16[4,64,128]{2,1,0:T(8,128)(2,1)S(1)} %slice.54), channel_id=1, source_target_pairs={{0,1},{1,0},{2,3},{3,2},{4,5},{5,4},{6,7},{7,6},{8,9},{9,8},{10,11... | collective-permute-start | bytes 196616 | tf_op jit(solution)/shard_map/ppermute | solution.py:234
  154.2 4.3 %collective-permute-start.27 = (bf16[4,64,128]{2,1,0:T(8,128)(2,1)S(1)}, bf16[4,64,128]{2,1,0:T(8,128)(2,1)S(1)}, u32[]{:S(2)}, u32[]{:S(2)}) collective-permute-start(bf16[4,64,128]{2,1,0:T(8,128)(2,1)S(1)} %fusion.13), channel_id=1, source_target_pairs={{0,4},{4,0},{8,12},{12,8},{1,5},{5,1},{9,13},{13,9},{2,6},{6,2},{1... | collective-permute-start | bytes 196616 | tf_op jit(solution)/shard_map/ppermute | solution.py:234
  158.6 5.4 %collective-permute-start.28 = (bf16[4,64,128]{2,1,0:T(8,128)(2,1)S(1)}, bf16[4,64,128]{2,1,0:T(8,128)(2,1)S(1)}, u32[]{:S(2)}, u32[]{:S(2)}) collective-permute-start(bf16[4,64,128]{2,1,0:T(8,128)(2,1)S(1)} %add_convert_fusion.1), channel_id=1, source_target_pairs={{0,8},{4,12},{8,0},{12,4},{1,9},{5,13},{9,1},{13,5},{2,10},{6,14},... | collective-permute-start | bytes 196616 | tf_op jit(solution)/shard_map/ppermute | solution.py:234
  164.0 4.3 %collective-permute-start.29 = (bf16[4,64,128]{2,1,0:T(8,128)(2,1)S(1)}, bf16[4,64,128]{2,1,0:T(8,128)(2,1)S(1)}, u32[]{:S(2)}, u32[]{:S(2)}) collective-permute-start(bf16[4,64,128]{2,1,0:T(8,128)(2,1)S(1)} %add_convert_fusion), channel_id=1, source_target_pairs={{0,1},{1,0},{2,3},{3,2},{4,5},{5,4},{6,7},{7,6},{8,9},{9,8},{10,11... | collective-permute-start | bytes 196616 | tf_op jit(solution)/shard_map/ppermute | solution.py:234
  168.3 1.4 collective-permute-start.30
  (2 other events, 14.6 us)

commit v13 on v12

--- a/solution.py
+++ b/solution.py
@@ -195,9 +195,10 @@
 
 def power_kernel(at_ref, basis_ref, *refs):
     piece_refs, a_ref, part_ref = refs[:-2], refs[-2], refs[-1]
-    rows = piece_refs[0].shape[0]
-    for s, piece_ref in enumerate(piece_refs):
-        a_ref[rows * s : rows * (s + 1), :] = piece_ref[...]
+    start = 0
+    for piece_ref in piece_refs:
+        a_ref[start : start + piece_ref.shape[0], :] = piece_ref[...]
+        start += piece_ref.shape[0]
     forth_product(dot_nn(basis_ref[...], a_ref[...]), a_ref, at_ref, part_ref)
 
 
@@ -275,9 +276,16 @@
     z_at, col = lax.axis_index("z"), lax.axis_index("col")
     pieces = {}
 
-    def move(slab, offset):
-        block = lax.dynamic_slice_in_dim(slab, (z_at ^ offset) * cols, cols, 1)
-        pieces[offset] = from_xor(block, ("z",), offset) if offset else block
+    def move(slab, offset, part=0, parts=1):
+        rows = rows_local // parts
+        start = (part * rows, (z_at ^ offset) * cols)
+        block = lax.dynamic_slice(slab, start, (rows, cols))
+        pieces[offset, part] = from_xor(block, ("z",), offset) if offset else block
+
+    def hold(value, names):
+        value, moved = lax.optimization_barrier((value, [pieces[name] for name in names]))
+        pieces.update(zip(names, moved))
+        return value
 
     feature_index = col * width_local + jnp.arange(width_local, dtype=jnp.int32)
     omega = sketch_table(sketch_base[0], feature_index, RANK)
@@ -287,26 +295,27 @@
     z = z.reshape(RANK, n_col, chunk).transpose(1, 0, 2)
     z_bits = bits(n_z)[::-1]
     far = z_bits[0]
-    move(states, 0)
+    for offset in [0, far, *range(1, far)]:
+        move(states, offset)
+    first = list(pieces)
+    z = jnp.concatenate([z, from_xor(z, ("z",), far)])
     z, slab = lax.optimization_barrier((z, states))
-    move(slab, far)
-    z = jnp.concatenate([z, from_xor(z, ("z",), far)])
-    z, slab = lax.optimization_barrier((z, slab))
-    for offset in sorted(set(range(1, n_z)) - {far}, reverse=True):
-        move(slab, offset)
+    for offset in range(far + 1, n_z):
+        move(slab, offset, 0, 2)
+        move(slab, offset, 1, 2)
+    for bit in bits(n_col):
+        z = z + from_xor(z, ("col",), bit)
+    z = hold(z, first)
     for bit in z_bits[1:]:
         z = jnp.concatenate([z, from_xor(z, ("z",), bit)])
-    for bit in bits(n_col):
-        z = z + from_xor(z, ("col",), bit)
-    z, pieces[far] = lax.optimization_barrier((z, pieces[far]))
+    z = hold(z, [(offset, 0) for offset in range(far + 1, n_z)])
     z = z, from_xor(z, ("core",), 1)
     absolute_col = [("col", bit, False) for bit in bits(n_col)[::-1]]
     at_first = chunk_places([("z", bit, True) for bit in z_bits[::-1]] + absolute_col)
     relative_col = [("col", bit, True) for bit in bits(n_col)]
     at = chunk_places(relative_col + [("z", bit, False) for bit in z_bits])
-    early = [0, far]
-    late = [offset for offset in range(n_z) if offset not in early]
-    others = {offset: from_xor(pieces[offset], ("core",), 1) for offset in early}
+    late = [name for name in pieces if name[0] > far]
+    others = {name: from_xor(pieces[name], ("core",), 1) for name in first}
 
     f32 = jnp.float32
     square = jax.ShapeDtypeStruct((RANK, RANK), f32)
@@ -318,10 +327,9 @@
     flops = orth_flops + 4 * 64 * rows_total * cols
 
     basis, upper = call(orth_kernel, (wide, square), orth_flops, (at_first,), *z)
-    basis, moved = lax.optimization_barrier((basis, [pieces[offset] for offset in late]))
-    pieces.update(zip(late, moved))
-    others.update((offset, from_xor(pieces[offset], ("core",), 1)) for offset in late)
-    blocks = [half[offset] for half in (pieces, others) for offset in range(n_z)]
+    basis = hold(basis, late)
+    others.update((name, from_xor(pieces[name], ("core",), 1)) for name in late)
+    blocks = [half[name] for half in (pieces, others) for name in sorted(half)]
     factor = upper.T * (1.0 / math.sqrt(rows_total * width_total))
     a, total = call(power_kernel, (slab, parts), flops, (at,), basis, *blocks)
     z = gather_parts(sum_parts(total, f32))
@@ -371,7 +379,7 @@
 
 def solution(mesh):
     n_grp, n_row, n_col = (mesh.shape[name] for name in ("grp", "row", "col"))
-    fits = n_row % 2 == 0 and n_row & (n_row - 1) == 0
+    fits = n_row >= 4 and n_row & (n_row - 1) == 0
 
     def run(sketch_base, states):
         rows_local = states.shape[0] // (n_grp * n_row)

time: 178 us -> 177 us (level)
  starting transfers between devices: 35.8 us -> 26.4 us
  waiting for transfers between devices: 98.1 us -> 106 us
    ppermute x31 -> x33, starting transfers between devices: 35.8 us -> 26.4 us  [from_xor(): return lax.ppermute(value, axis, [(i, i ^ offset) for i in range(size)])]
    ppermute x31 -> x33, waiting for transfers between devices: 98.1 us -> 106 us  [from_xor(): return lax.ppermute(value, axis, [(i, i ^ offset) for i in range(size)])]
  transfers between devices with their start and end apart: 31 -> 33, of which waited for: 26 -> 25; matrix products, arithmetic and copies ran while one was open for 2% -> 3% of each run, Pallas kernels for 3% -> 3%
where the time goes in v13:
time: 177 us
  waiting for transfers between devices  106 us (60%)
  Pallas kernels  32.7 us (18%)
  starting transfers between devices  26.4 us (15%)
  local copies, waits for them, and re-layouts  5.53 us (3%)
  matrix products  3.83 us (2%)
    ppermute x33, waiting for transfers between devices, from_xor(): return lax.ppermute(value, axis, [(i, i ^ offset) for i in range(size)])  106 us
    pallas_call x6, Pallas kernels, call(): pl.pallas_call(kernel, out_shape=out_shapes, in_specs=[pl.BlockSpec(memor...  32.7 us
    ppermute x33, starting transfers between devices, from_xor(): return lax.ppermute(value, axis, [(i, i ^ offset) for i in range(size)])  26.4 us
    dot_general x1, matrix products, per_device_transposed(): lax.dot_general(omega, states, (((0,), (1,)), ((), ())), preferred_elemen...  3.83 us
  transfers between devices with their start and end apart: 33, of which 25 were waited for; matrix products, arithmetic and copies ran while one was open for 3% of the time, Pallas kernels for 3%

profile of v13, /device:TPU:0, one launch (start us, length us, event | category | flops | bytes accessed | tf_op | source)
XLA Modules:
  0.0 176.6 jit_solution(16160960437589164832)
XLA Ops:
  2.1 3.1 %collective-permute-start.3 = (bf16[256,1024]{1,0:T(8,128)(2,1)S(1)}, bf16[256,1024]{1,0:T(8,128)(2,1)S(1)}, u32[]{:S(2)}, u32[]{:S(2)}) collective-permute-start(bf16[256,1024]{1,0:T(8,128)(2,1)S(1)} %get-tuple-element.40), channel_id=1, source_target_pairs={{0,4},{4,0},{8,12},{12,8},{1,5},{5,1},{9,13},{13,9},{2,6},{6,2},{1... | collective-permute-start | bytes 1572872 | tf_op jit(solution)/shard_map/ppermute | solution.py:235
  5.2 2.6 %collective-permute-start.2 = (bf16[256,1024]{1,0:T(8,128)(2,1)S(1)}, bf16[256,1024]{1,0:T(8,128)(2,1)S(1)}, u32[]{:S(2)}, u32[]{:S(2)}) collective-permute-start(bf16[256,1024]{1,0:T(8,128)(2,1)S(1)} %get-tuple-element.42), channel_id=1, source_target_pairs={{0,8},{4,12},{8,0},{12,4},{1,9},{5,13},{9,1},{13,5},{2,10},{6,14},... | collective-permute-start | bytes 1572872 | tf_op jit(solution)/shard_map/ppermute | solution.py:235
  8.5 3.8 %convolution_bitcast_fusion = f32[8,2,8,128]{3,2,1,0:T(8,128)S(1)} fusion(bf16[256,4096]{1,0:T(8,128)(2,1)} %param.3, s32[]{:T(128)S(6)} %xor.73, s32[4096]{0:T(1024)S(1)} %add_multiply_fusion), kind=kOutput, calls=%fused_computation | convolution fusion | flops 152043520 | bytes 2179076 | tf_op jit(solution)/shard_map/dot_general | solution.py:292
  12.8 20.8 %collective-permute-done = f32[2,64,128]{2,1,0:T(8,128)S(1)} collective-permute-done((f32[2,64,128]{2,1,0:T(8,128)S(1)}, f32[2,64,128]{2,1,0:T(8,128)S(1)}, u32[]{:S(2)}, u32[]{:S(2)}) %collective-permute-start) | collective-permute-done | bytes 65568 | tf_op jit(solution)/shard_map/ppermute | solution.py:235
  36.2 2.5 %collective-permute-start.5 = (bf16[128,1024]{1,0:T(8,128)(2,1)S(1)}, bf16[128,1024]{1,0:T(8,128)(2,1)S(1)}, u32[]{:S(2)}, u32[]{:S(2)}) collective-permute-start(bf16[128,1024]{1,0:T(8,128)(2,1)S(1)} %get-tuple-element.39), channel_id=1, source_target_pairs={{0,12},{4,8},{8,4},{12,0},{1,13},{5,9},{9,5},{13,1},{2,14},{6,10},... | collective-permute-start | bytes 786440 | tf_op jit(solution)/shard_map/ppermute | solution.py:235
  38.9 8.7 %collective-permute-done.4 = f32[4,64,128]{2,1,0:T(8,128)S(1)} collective-permute-done((f32[4,64,128]{2,1,0:T(8,128)S(1)}, f32[4,64,128]{2,1,0:T(8,128)S(1)}, u32[]{:S(2)}, u32[]{:S(2)}) %collective-permute-start.4) | collective-permute-done | bytes 131104 | tf_op jit(solution)/shard_map/ppermute | solution.py:235
  47.7 2.2 %collective-permute-start.7 = (bf16[128,1024]{1,0:T(8,128)(2,1)S(1)}, bf16[128,1024]{1,0:T(8,128)(2,1)S(1)}, u32[]{:S(2)}, u32[]{:S(2)}) collective-permute-start(bf16[128,1024]{1,0:T(8,128)(2,1)S(1)} %get-tuple-element.38), channel_id=1, source_target_pairs={{0,12},{4,8},{8,4},{12,0},{1,13},{5,9},{9,5},{13,1},{2,14},{6,10},... | collective-permute-start | bytes 786440 | tf_op jit(solution)/shard_map/ppermute | solution.py:235
  50.7 6.0 %shard_map.41 = (bf16[64,2048]{1,0:T(8,128)(2,1)S(1)}, f32[64,64]{1,0:T(8,128)S(1)}) custom-call(s32[8]{0:T(128)S(1)} %fusion.19.at_ref, f32[8,64,128]{2,1,0:T(8,128)S(1)} %pad_maximum_fusion.z_ref, f32[8,64,128]{2,1,0:T(8,128)S(1)} %collective-permute-done.6.other_ref), custom_call_target="tpu_custom_call" | custom-call | flops 402653184 | bytes 524288 | tf_op jit(solution)/shard_map/pallas_call | solution.py:218
  60.3 2.1 %shard_map.42 = (bf16[2048,1024]{1,0:T(8,128)(2,1)S(1)}, f32[8,64,128]{2,1,0:T(8,128)S(1)}) custom-call(s32[8]{0:T(128)S(1)} %fusion.17.at_ref, bf16[64,2048]{1,0:T(8,128)(2,1)S(1)} %get-tuple-element.23.basis_ref, bf16[256,1024]{1,0:T(8,128)(2,1)S(1)} %get-tuple-element.24.refs_0_, bf16[256,1024]{1,0:T(8,128)(2,1)S(1)} %collective-permute-done.3.refs_1_, ...), custom_call_target="tpu_custom_call" | custom-call | flops 939524096 | bytes 4456448 | tf_op jit(solution)/shard_map/pallas_call | solution.py:218
  63.0 5.0 %collective-permute-done.13 = f32[4,64,128]{2,1,0:T(8,128)S(1)} collective-permute-done((f32[4,64,128]{2,1,0:T(8,128)S(1)}, f32[4,64,128]{2,1,0:T(8,128)S(1)}, u32[]{:S(2)}, u32[]{:S(2)}) %collective-permute-start.13) | collective-permute-done | bytes 131104 | tf_op jit(solution)/shard_map/ppermute | solution.py:235
  68.0 4.4 %collective-permute-start.14 = (f32[4,64,128]{2,1,0:T(8,128)S(1)}, f32[4,64,128]{2,1,0:T(8,128)S(1)}, u32[]{:S(2)}, u32[]{:S(2)}) collective-permute-start(f32[4,64,128]{2,1,0:T(8,128)S(1)} %slice_add_fusion.3), channel_id=1, source_target_pairs={{0,4},{4,0},{8,12},{12,8},{1,5},{5,1},{9,13},{13,9},{2,6},{6,2},{1... | collective-permute-start | bytes 393224 | tf_op jit(solution)/shard_map/ppermute | solution.py:235
  72.4 3.0 %collective-permute-done.14 = f32[4,64,128]{2,1,0:T(8,128)S(1)} collective-permute-done((f32[4,64,128]{2,1,0:T(8,128)S(1)}, f32[4,64,128]{2,1,0:T(8,128)S(1)}, u32[]{:S(2)}, u32[]{:S(2)}) %collective-permute-start.14) | collective-permute-done | bytes 131104 | tf_op jit(solution)/shard_map/ppermute | solution.py:235
  75.4 2.0 %collective-permute-start.15 = (f32[4,64,128]{2,1,0:T(8,128)S(1)}, f32[4,64,128]{2,1,0:T(8,128)S(1)}, u32[]{:S(2)}, u32[]{:S(2)}) collective-permute-start(f32[4,64,128]{2,1,0:T(8,128)S(1)} %add.213), channel_id=1, source_target_pairs={{0,8},{4,12},{8,0},{12,4},{1,9},{5,13},{9,1},{13,5},{2,10},{6,14},... | collective-permute-start | bytes 393224 | tf_op jit(solution)/shard_map/ppermute | solution.py:235
  77.4 5.6 %collective-permute-done.15 = f32[4,64,128]{2,1,0:T(8,128)S(1)} collective-permute-done((f32[4,64,128]{2,1,0:T(8,128)S(1)}, f32[4,64,128]{2,1,0:T(8,128)S(1)}, u32[]{:S(2)}, u32[]{:S(2)}) %collective-permute-start.15) | collective-permute-done | bytes 131104 | tf_op jit(solution)/shard_map/ppermute | solution.py:235
  83.6 4.4 %collective-permute-done.16 = f32[4,64,128]{2,1,0:T(8,128)S(1)} collective-permute-done((f32[4,64,128]{2,1,0:T(8,128)S(1)}, f32[4,64,128]{2,1,0:T(8,128)S(1)}, u32[]{:S(2)}, u32[]{:S(2)}) %collective-permute-start.16) | collective-permute-done | bytes 131104 | tf_op jit(solution)/shard_map/ppermute | solution.py:235
  89.7 6.7 %shard_map.43 = f32[8,64,128]{2,1,0:T(8,128)S(1)} custom-call(s32[8]{0:T(128)S(1)} %fusion.17.at_ref, f32[8,64,128]{2,1,0:T(8,128)S(1)} %pad_maximum_fusion.1.z_ref, f32[8,64,128]{2,1,0:T(8,128)S(1)} %collective-permute-done.17.other_ref, bf16[2048,1024]{1,0:T(8,128)(2,1)S(1)} %get-tuple-element.30.a_ref), custom_call_target="tpu_custom_call" | custom-call | flops 939524096 | bytes 4718592 | tf_op jit(solution)/shard_map/pallas_call | solution.py:218
  97.0 3.7 %collective-permute-done.18 = bf16[4,64,128]{2,1,0:T(8,128)(2,1)S(1)} collective-permute-done((bf16[4,64,128]{2,1,0:T(8,128)(2,1)S(1)}, bf16[4,64,128]{2,1,0:T(8,128)(2,1)S(1)}, u32[]{:S(2)}, u32[]{:S(2)}) %collective-permute-start.18) | collective-permute-done | bytes 65568 | tf_op jit(solution)/shard_map/ppermute | solution.py:235
  101.3 3.8 %collective-permute-done.19 = bf16[4,64,128]{2,1,0:T(8,128)(2,1)S(1)} collective-permute-done((bf16[4,64,128]{2,1,0:T(8,128)(2,1)S(1)}, bf16[4,64,128]{2,1,0:T(8,128)(2,1)S(1)}, u32[]{:S(2)}, u32[]{:S(2)}) %collective-permute-start.19) | collective-permute-done | bytes 65568 | tf_op jit(solution)/shard_map/ppermute | solution.py:235
  105.5 5.4 %collective-permute-done.20 = bf16[4,64,128]{2,1,0:T(8,128)(2,1)S(1)} collective-permute-done((bf16[4,64,128]{2,1,0:T(8,128)(2,1)S(1)}, bf16[4,64,128]{2,1,0:T(8,128)(2,1)S(1)}, u32[]{:S(2)}, u32[]{:S(2)}) %collective-permute-start.20) | collective-permute-done | bytes 65568 | tf_op jit(solution)/shard_map/ppermute | solution.py:235
  111.5 3.7 %collective-permute-done.21 = bf16[4,64,128]{2,1,0:T(8,128)(2,1)S(1)} collective-permute-done((bf16[4,64,128]{2,1,0:T(8,128)(2,1)S(1)}, bf16[4,64,128]{2,1,0:T(8,128)(2,1)S(1)}, u32[]{:S(2)}, u32[]{:S(2)}) %collective-permute-start.21) | collective-permute-done | bytes 65568 | tf_op jit(solution)/shard_map/ppermute | solution.py:235
  116.7 6.0 %shard_map.44 = f32[8,64,128]{2,1,0:T(8,128)S(1)} custom-call(s32[8]{0:T(128)S(1)} %fusion.17.at_ref, bf16[8,64,128]{2,1,0:T(8,128)(2,1)S(1)} %pad_maximum_fusion.3.z_ref, bf16[8,64,128]{2,1,0:T(8,128)(2,1)S(1)} %collective-permute-done.22.other_ref, bf16[2048,1024]{1,0:T(8,128)(2,1)S(1)} %get-tuple-element.30.a_ref), custom_call_target="tpu_custom_call" | custom-call | flops 939524096 | bytes 4456448 | tf_op jit(solution)/shard_map/pallas_call | solution.py:218
  123.4 3.7 %collective-permute-done.23 = bf16[4,64,128]{2,1,0:T(8,128)(2,1)S(1)} collective-permute-done((bf16[4,64,128]{2,1,0:T(8,128)(2,1)S(1)}, bf16[4,64,128]{2,1,0:T(8,128)(2,1)S(1)}, u32[]{:S(2)}, u32[]{:S(2)}) %collective-permute-start.23) | collective-permute-done | bytes 65568 | tf_op jit(solution)/shard_map/ppermute | solution.py:235
  127.2 4.3 %collective-permute-done.24 = bf16[4,64,128]{2,1,0:T(8,128)(2,1)S(1)} collective-permute-done((bf16[4,64,128]{2,1,0:T(8,128)(2,1)S(1)}, bf16[4,64,128]{2,1,0:T(8,128)(2,1)S(1)}, u32[]{:S(2)}, u32[]{:S(2)}) %collective-permute-start.24) | collective-permute-done | bytes 65568 | tf_op jit(solution)/shard_map/ppermute | solution.py:235
  131.6 5.3 %collective-permute-done.25 = bf16[4,64,128]{2,1,0:T(8,128)(2,1)S(1)} collective-permute-done((bf16[4,64,128]{2,1,0:T(8,128)(2,1)S(1)}, bf16[4,64,128]{2,1,0:T(8,128)(2,1)S(1)}, u32[]{:S(2)}, u32[]{:S(2)}) %collective-permute-start.25) | collective-permute-done | bytes 65568 | tf_op jit(solution)/shard_map/ppermute | solution.py:235
  137.5 3.7 %collective-permute-done.26 = bf16[4,64,128]{2,1,0:T(8,128)(2,1)S(1)} collective-permute-done((bf16[4,64,128]{2,1,0:T(8,128)(2,1)S(1)}, bf16[4,64,128]{2,1,0:T(8,128)(2,1)S(1)}, u32[]{:S(2)}, u32[]{:S(2)}) %collective-permute-start.26) | collective-permute-done | bytes 65568 | tf_op jit(solution)/shard_map/ppermute | solution.py:235
  142.6 6.0 %shard_map.45 = f32[8,64,128]{2,1,0:T(8,128)S(1)} custom-call(s32[8]{0:T(128)S(1)} %fusion.17.at_ref, bf16[8,64,128]{2,1,0:T(8,128)(2,1)S(1)} %pad_maximum_fusion.4.z_ref, bf16[8,64,128]{2,1,0:T(8,128)(2,1)S(1)} %collective-permute-done.27.other_ref, bf16[2048,1024]{1,0:T(8,128)(2,1)S(1)} %get-tuple-element.30.a_ref), custom_call_target="tpu_custom_call" | custom-call | flops 939524096 | bytes 4456448 | tf_op jit(solution)/shard_map/pallas_call | solution.py:218
  149.3 3.7 %collective-permute-done.28 = bf16[4,64,128]{2,1,0:T(8,128)(2,1)S(1)} collective-permute-done((bf16[4,64,128]{2,1,0:T(8,128)(2,1)S(1)}, bf16[4,64,128]{2,1,0:T(8,128)(2,1)S(1)}, u32[]{:S(2)}, u32[]{:S(2)}) %collective-permute-start.28) | collective-permute-done | bytes 65568 | tf_op jit(solution)/shard_map/ppermute | solution.py:235
  153.1 4.3 %collective-permute-done.29 = bf16[4,64,128]{2,1,0:T(8,128)(2,1)S(1)} collective-permute-done((bf16[4,64,128]{2,1,0:T(8,128)(2,1)S(1)}, bf16[4,64,128]{2,1,0:T(8,128)(2,1)S(1)}, u32[]{:S(2)}, u32[]{:S(2)}) %collective-permute-start.29) | collective-permute-done | bytes 65568 | tf_op jit(solution)/shard_map/ppermute | solution.py:235
  157.5 5.3 %collective-permute-done.30 = bf16[4,64,128]{2,1,0:T(8,128)(2,1)S(1)} collective-permute-done((bf16[4,64,128]{2,1,0:T(8,128)(2,1)S(1)}, bf16[4,64,128]{2,1,0:T(8,128)(2,1)S(1)}, u32[]{:S(2)}, u32[]{:S(2)}) %collective-permute-start.30) | collective-permute-done | bytes 65568 | tf_op jit(solution)/shard_map/ppermute | solution.py:235
  163.4 3.7 %collective-permute-done.31 = bf16[4,64,128]{2,1,0:T(8,128)(2,1)S(1)} collective-permute-done((bf16[4,64,128]{2,1,0:T(8,128)(2,1)S(1)}, bf16[4,64,128]{2,1,0:T(8,128)(2,1)S(1)}, u32[]{:S(2)}, u32[]{:S(2)}) %collective-permute-start.31) | collective-permute-done | bytes 65568 | tf_op jit(solution)/shard_map/ppermute | solution.py:235
  168.6 2.2 %copy-done.1 = bf16[2048,1024]{1,0:T(8,128)(2,1)S(1)} copy-done((bf16[2048,1024]{1,0:T(8,128)(2,1)S(1)}, bf16[2048,1024]{1,0:T(8,128)(2,1)}, u32[]{:S(2)}) %copy-start.1) | copy-done | bytes 4194328
  170.8 5.8 %shard_map.46 = f32[64,512]{1,0:T(8,128)} custom-call(s32[8]{0:T(128)S(1)} %fusion.17.at_ref, s32[1]{0:T(128)} %bitcast.core_ref, bf16[8,64,128]{2,1,0:T(8,128)(2,1)S(1)} %pad_maximum_fusion.5.z_ref, bf16[8,64,128]{2,1,0:T(8,128)(2,1)S(1)} %collective-permute-done.32.other_ref, bf16[2048,1024]{1,0:T(8,128)(2,1)S(1)} %copy-done.1), custom_call_target="tpu_custom_call" | custom-call | flops 939524096 | bytes 4456448 | tf_op jit(solution)/shard_map/pallas_call | solution.py:218
  (76 shorter events, 21.2 us)
Async XLA Ops:
  2.1 36.7 %collective-permute-start.3 = (bf16[256,1024]{1,0:T(8,128)(2,1)S(1)}, bf16[256,1024]{1,0:T(8,128)(2,1)S(1)}, u32[]{:S(2)}, u32[]{:S(2)}) collective-permute-start(bf16[256,1024]{1,0:T(8,128)(2,1)S(1)} %get-tuple-element.40), channel_id=1, source_target_pairs={{0,4},{4,0},{8,12},{12,8},{1,5},{5,1},{9,13},{13,9},{2,6},{6,2},{1... | collective-permute-start | bytes 1572872 | tf_op jit(solution)/shard_map/ppermute | solution.py:235
  5.2 33.6 %collective-permute-start.2 = (bf16[256,1024]{1,0:T(8,128)(2,1)S(1)}, bf16[256,1024]{1,0:T(8,128)(2,1)S(1)}, u32[]{:S(2)}, u32[]{:S(2)}) collective-permute-start(bf16[256,1024]{1,0:T(8,128)(2,1)S(1)} %get-tuple-element.42), channel_id=1, source_target_pairs={{0,8},{4,12},{8,0},{12,4},{1,9},{5,13},{9,1},{13,5},{2,10},{6,14},... | collective-permute-start | bytes 1572872 | tf_op jit(solution)/shard_map/ppermute | solution.py:235
  12.4 21.2 %collective-permute-start = (f32[2,64,128]{2,1,0:T(8,128)S(1)}, f32[2,64,128]{2,1,0:T(8,128)S(1)}, u32[]{:S(2)}, u32[]{:S(2)}) collective-permute-start(f32[2,64,128]{2,1,0:T(8,128)S(1)} %bitcast.16), channel_id=1, source_target_pairs={{0,8},{4,12},{8,0},{12,4},{1,9},{5,13},{9,1},{13,5},{2,10},{6,14},... | collective-permute-start | bytes 196616 | tf_op jit(solution)/shard_map/ppermute | solution.py:235
  33.6 5.2 %collective-permute-start.1 = (f32[4,64,128]{2,1,0:T(8,128)S(1)}, f32[4,64,128]{2,1,0:T(8,128)S(1)}, u32[]{:S(2)}, u32[]{:S(2)}) collective-permute-start(f32[4,64,128]{2,1,0:T(8,128)S(1)} %pad_maximum_fusion.2), channel_id=1, source_target_pairs={{0,1},{1,0},{2,3},{3,2},{4,5},{5,4},{6,7},{7,6},{8,9},{9,8},{10,11... | collective-permute-start | bytes 393224 | tf_op jit(solution)/shard_map/ppermute | solution.py:235
  36.2 11.4 %collective-permute-start.5 = (bf16[128,1024]{1,0:T(8,128)(2,1)S(1)}, bf16[128,1024]{1,0:T(8,128)(2,1)S(1)}, u32[]{:S(2)}, u32[]{:S(2)}) collective-permute-start(bf16[128,1024]{1,0:T(8,128)(2,1)S(1)} %get-tuple-element.39), channel_id=1, source_target_pairs={{0,12},{4,8},{8,4},{12,0},{1,13},{5,9},{9,5},{13,1},{2,14},{6,10},... | collective-permute-start | bytes 786440 | tf_op jit(solution)/shard_map/ppermute | solution.py:235
  38.8 8.8 %collective-permute-start.4 = (f32[4,64,128]{2,1,0:T(8,128)S(1)}, f32[4,64,128]{2,1,0:T(8,128)S(1)}, u32[]{:S(2)}, u32[]{:S(2)}) collective-permute-start(f32[4,64,128]{2,1,0:T(8,128)S(1)} %add.207), channel_id=1, source_target_pairs={{0,4},{4,0},{8,12},{12,8},{1,5},{5,1},{9,13},{13,9},{2,6},{6,2},{1... | collective-permute-start | bytes 393224 | tf_op jit(solution)/shard_map/ppermute | solution.py:235
  47.7 3.0 %collective-permute-start.6 = (f32[8,64,128]{2,1,0:T(8,128)S(1)}, f32[8,64,128]{2,1,0:T(8,128)S(1)}, u32[]{:S(2)}, u32[]{:S(2)}) collective-permute-start(f32[8,64,128]{2,1,0:T(8,128)S(1)} %pad_maximum_fusion.z_ref), channel_id=1, source_target_pairs={{0,2},{2,0},{1,3},{3,1},{4,6},{6,4},{5,7},{7,5},{8,10},{10,8},{9,1... | collective-permute-start | bytes 786440 | tf_op jit(solution)/shard_map/ppermute | solution.py:235
  47.7 10.6 %collective-permute-start.7 = (bf16[128,1024]{1,0:T(8,128)(2,1)S(1)}, bf16[128,1024]{1,0:T(8,128)(2,1)S(1)}, u32[]{:S(2)}, u32[]{:S(2)}) collective-permute-start(bf16[128,1024]{1,0:T(8,128)(2,1)S(1)} %get-tuple-element.38), channel_id=1, source_target_pairs={{0,12},{4,8},{8,4},{12,0},{1,13},{5,9},{9,5},{13,1},{2,14},{6,10},... | collective-permute-start | bytes 786440 | tf_op jit(solution)/shard_map/ppermute | solution.py:235
  50.0 8.9 %collective-permute-start.8 = (bf16[256,1024]{1,0:T(8,128)(2,1)S(1)}, bf16[256,1024]{1,0:T(8,128)(2,1)S(1)}, u32[]{:S(2)}, u32[]{:S(2)}) collective-permute-start(bf16[256,1024]{1,0:T(8,128)(2,1)S(1)} %get-tuple-element.24.refs_0_), channel_id=1, source_target_pairs={{0,2},{2,0},{1,3},{3,1},{4,6},{6,4},{5,7},{7,5},{8,10},{10,8},{9,1... | collective-permute-start | bytes 1572872 | tf_op jit(solution)/shard_map/ppermute | solution.py:235
  50.1 8.8 %collective-permute-start.9 = (bf16[256,1024]{1,0:T(8,128)(2,1)S(1)}, bf16[256,1024]{1,0:T(8,128)(2,1)S(1)}, u32[]{:S(2)}, u32[]{:S(2)}) collective-permute-start(bf16[256,1024]{1,0:T(8,128)(2,1)S(1)} %collective-permute-done.3.refs_1_), channel_id=1, source_target_pairs={{0,2},{2,0},{1,3},{3,1},{4,6},{6,4},{5,7},{7,5},{8,10},{10,8},{9,1... | collective-permute-start | bytes 1572872 | tf_op jit(solution)/shard_map/ppermute | solution.py:235
  50.5 8.5 %collective-permute-start.10 = (bf16[256,1024]{1,0:T(8,128)(2,1)S(1)}, bf16[256,1024]{1,0:T(8,128)(2,1)S(1)}, u32[]{:S(2)}, u32[]{:S(2)}) collective-permute-start(bf16[256,1024]{1,0:T(8,128)(2,1)S(1)} %collective-permute-done.2.refs_2_), channel_id=1, source_target_pairs={{0,2},{2,0},{1,3},{3,1},{4,6},{6,4},{5,7},{7,5},{8,10},{10,8},{9,1... | collective-permute-start | bytes 1572872 | tf_op jit(solution)/shard_map/ppermute | solution.py:235
  58.4 1.5 collective-permute-start.11
  58.4 1.9 %collective-permute-start.12 = (bf16[128,1024]{1,0:T(8,128)(2,1)S(1)}, bf16[128,1024]{1,0:T(8,128)(2,1)S(1)}, u32[]{:S(2)}, u32[]{:S(2)}) collective-permute-start(bf16[128,1024]{1,0:T(8,128)(2,1)S(1)} %collective-permute-done.7.refs_4_), channel_id=1, source_target_pairs={{0,2},{2,0},{1,3},{3,1},{4,6},{6,4},{5,7},{7,5},{8,10},{10,8},{9,1... | collective-permute-start | bytes 786440 | tf_op jit(solution)/shard_map/ppermute | solution.py:235
  62.4 5.6 %collective-permute-start.13 = (f32[4,64,128]{2,1,0:T(8,128)S(1)}, f32[4,64,128]{2,1,0:T(8,128)S(1)}, u32[]{:S(2)}, u32[]{:S(2)}) collective-permute-start(f32[4,64,128]{2,1,0:T(8,128)S(1)} %slice.28), channel_id=1, source_target_pairs={{0,1},{1,0},{2,3},{3,2},{4,5},{5,4},{6,7},{7,6},{8,9},{9,8},{10,11... | collective-permute-start | bytes 393224 | tf_op jit(solution)/shard_map/ppermute | solution.py:235
  68.0 7.4 %collective-permute-start.14 = (f32[4,64,128]{2,1,0:T(8,128)S(1)}, f32[4,64,128]{2,1,0:T(8,128)S(1)}, u32[]{:S(2)}, u32[]{:S(2)}) collective-permute-start(f32[4,64,128]{2,1,0:T(8,128)S(1)} %slice_add_fusion.3), channel_id=1, source_target_pairs={{0,4},{4,0},{8,12},{12,8},{1,5},{5,1},{9,13},{13,9},{2,6},{6,2},{1... | collective-permute-start | bytes 393224 | tf_op jit(solution)/shard_map/ppermute | solution.py:235
  75.4 7.6 %collective-permute-start.15 = (f32[4,64,128]{2,1,0:T(8,128)S(1)}, f32[4,64,128]{2,1,0:T(8,128)S(1)}, u32[]{:S(2)}, u32[]{:S(2)}) collective-permute-start(f32[4,64,128]{2,1,0:T(8,128)S(1)} %add.213), channel_id=1, source_target_pairs={{0,8},{4,12},{8,0},{12,4},{1,9},{5,13},{9,1},{13,5},{2,10},{6,14},... | collective-permute-start | bytes 393224 | tf_op jit(solution)/shard_map/ppermute | solution.py:235
  83.0 5.0 %collective-permute-start.16 = (f32[4,64,128]{2,1,0:T(8,128)S(1)}, f32[4,64,128]{2,1,0:T(8,128)S(1)}, u32[]{:S(2)}, u32[]{:S(2)}) collective-permute-start(f32[4,64,128]{2,1,0:T(8,128)S(1)} %add.214), channel_id=1, source_target_pairs={{0,1},{1,0},{2,3},{3,2},{4,5},{5,4},{6,7},{7,6},{8,9},{9,8},{10,11... | collective-permute-start | bytes 393224 | tf_op jit(solution)/shard_map/ppermute | solution.py:235
  88.1 1.6 collective-permute-start.17
  96.4 4.3 %collective-permute-start.18 = (bf16[4,64,128]{2,1,0:T(8,128)(2,1)S(1)}, bf16[4,64,128]{2,1,0:T(8,128)(2,1)S(1)}, u32[]{:S(2)}, u32[]{:S(2)}) collective-permute-start(bf16[4,64,128]{2,1,0:T(8,128)(2,1)S(1)} %slice.56), channel_id=1, source_target_pairs={{0,1},{1,0},{2,3},{3,2},{4,5},{5,4},{6,7},{7,6},{8,9},{9,8},{10,11... | collective-permute-start | bytes 196616 | tf_op jit(solution)/shard_map/ppermute | solution.py:235
  100.7 4.3 %collective-permute-start.19 = (bf16[4,64,128]{2,1,0:T(8,128)(2,1)S(1)}, bf16[4,64,128]{2,1,0:T(8,128)(2,1)S(1)}, u32[]{:S(2)}, u32[]{:S(2)}) collective-permute-start(bf16[4,64,128]{2,1,0:T(8,128)(2,1)S(1)} %fusion.15), channel_id=1, source_target_pairs={{0,4},{4,0},{8,12},{12,8},{1,5},{5,1},{9,13},{13,9},{2,6},{6,2},{1... | collective-permute-start | bytes 196616 | tf_op jit(solution)/shard_map/ppermute | solution.py:235
  105.1 5.8 %collective-permute-start.20 = (bf16[4,64,128]{2,1,0:T(8,128)(2,1)S(1)}, bf16[4,64,128]{2,1,0:T(8,128)(2,1)S(1)}, u32[]{:S(2)}, u32[]{:S(2)}) collective-permute-start(bf16[4,64,128]{2,1,0:T(8,128)(2,1)S(1)} %add_convert_fusion.5), channel_id=1, source_target_pairs={{0,8},{4,12},{8,0},{12,4},{1,9},{5,13},{9,1},{13,5},{2,10},{6,14},... | collective-permute-start | bytes 196616 | tf_op jit(solution)/shard_map/ppermute | solution.py:235
  110.9 4.3 %collective-permute-start.21 = (bf16[4,64,128]{2,1,0:T(8,128)(2,1)S(1)}, bf16[4,64,128]{2,1,0:T(8,128)(2,1)S(1)}, u32[]{:S(2)}, u32[]{:S(2)}) collective-permute-start(bf16[4,64,128]{2,1,0:T(8,128)(2,1)S(1)} %add_convert_fusion.4), channel_id=1, source_target_pairs={{0,1},{1,0},{2,3},{3,2},{4,5},{5,4},{6,7},{7,6},{8,9},{9,8},{10,11... | collective-permute-start | bytes 196616 | tf_op jit(solution)/shard_map/ppermute | solution.py:235
  115.3 1.4 collective-permute-start.22
  122.8 4.3 %collective-permute-start.23 = (bf16[4,64,128]{2,1,0:T(8,128)(2,1)S(1)}, bf16[4,64,128]{2,1,0:T(8,128)(2,1)S(1)}, u32[]{:S(2)}, u32[]{:S(2)}) collective-permute-start(bf16[4,64,128]{2,1,0:T(8,128)(2,1)S(1)} %slice.55), channel_id=1, source_target_pairs={{0,1},{1,0},{2,3},{3,2},{4,5},{5,4},{6,7},{7,6},{8,9},{9,8},{10,11... | collective-permute-start | bytes 196616 | tf_op jit(solution)/shard_map/ppermute | solution.py:235
  127.1 4.3 %collective-permute-start.24 = (bf16[4,64,128]{2,1,0:T(8,128)(2,1)S(1)}, bf16[4,64,128]{2,1,0:T(8,128)(2,1)S(1)}, u32[]{:S(2)}, u32[]{:S(2)}) collective-permute-start(bf16[4,64,128]{2,1,0:T(8,128)(2,1)S(1)} %fusion.14), channel_id=1, source_target_pairs={{0,4},{4,0},{8,12},{12,8},{1,5},{5,1},{9,13},{13,9},{2,6},{6,2},{1... | collective-permute-start | bytes 196616 | tf_op jit(solution)/shard_map/ppermute | solution.py:235
  131.5 5.4 %collective-permute-start.25 = (bf16[4,64,128]{2,1,0:T(8,128)(2,1)S(1)}, bf16[4,64,128]{2,1,0:T(8,128)(2,1)S(1)}, u32[]{:S(2)}, u32[]{:S(2)}) collective-permute-start(bf16[4,64,128]{2,1,0:T(8,128)(2,1)S(1)} %add_convert_fusion.3), channel_id=1, source_target_pairs={{0,8},{4,12},{8,0},{12,4},{1,9},{5,13},{9,1},{13,5},{2,10},{6,14},... | collective-permute-start | bytes 196616 | tf_op jit(solution)/shard_map/ppermute | solution.py:235
  136.9 4.3 %collective-permute-start.26 = (bf16[4,64,128]{2,1,0:T(8,128)(2,1)S(1)}, bf16[4,64,128]{2,1,0:T(8,128)(2,1)S(1)}, u32[]{:S(2)}, u32[]{:S(2)}) collective-permute-start(bf16[4,64,128]{2,1,0:T(8,128)(2,1)S(1)} %add_convert_fusion.2), channel_id=1, source_target_pairs={{0,1},{1,0},{2,3},{3,2},{4,5},{5,4},{6,7},{7,6},{8,9},{9,8},{10,11... | collective-permute-start | bytes 196616 | tf_op jit(solution)/shard_map/ppermute | solution.py:235
  141.2 1.4 collective-permute-start.27
  148.7 4.3 %collective-permute-start.28 = (bf16[4,64,128]{2,1,0:T(8,128)(2,1)S(1)}, bf16[4,64,128]{2,1,0:T(8,128)(2,1)S(1)}, u32[]{:S(2)}, u32[]{:S(2)}) collective-permute-start(bf16[4,64,128]{2,1,0:T(8,128)(2,1)S(1)} %slice.54), channel_id=1, source_target_pairs={{0,1},{1,0},{2,3},{3,2},{4,5},{5,4},{6,7},{7,6},{8,9},{9,8},{10,11... | collective-permute-start | bytes 196616 | tf_op jit(solution)/shard_map/ppermute | solution.py:235
  153.1 4.3 %collective-permute-start.29 = (bf16[4,64,128]{2,1,0:T(8,128)(2,1)S(1)}, bf16[4,64,128]{2,1,0:T(8,128)(2,1)S(1)}, u32[]{:S(2)}, u32[]{:S(2)}) collective-permute-start(bf16[4,64,128]{2,1,0:T(8,128)(2,1)S(1)} %fusion.13), channel_id=1, source_target_pairs={{0,4},{4,0},{8,12},{12,8},{1,5},{5,1},{9,13},{13,9},{2,6},{6,2},{1... | collective-permute-start | bytes 196616 | tf_op jit(solution)/shard_map/ppermute | solution.py:235
  157.4 5.4 %collective-permute-start.30 = (bf16[4,64,128]{2,1,0:T(8,128)(2,1)S(1)}, bf16[4,64,128]{2,1,0:T(8,128)(2,1)S(1)}, u32[]{:S(2)}, u32[]{:S(2)}) collective-permute-start(bf16[4,64,128]{2,1,0:T(8,128)(2,1)S(1)} %add_convert_fusion.1), channel_id=1, source_target_pairs={{0,8},{4,12},{8,0},{12,4},{1,9},{5,13},{9,1},{13,5},{2,10},{6,14},... | collective-permute-start | bytes 196616 | tf_op jit(solution)/shard_map/ppermute | solution.py:235
  162.8 4.3 %collective-permute-start.31 = (bf16[4,64,128]{2,1,0:T(8,128)(2,1)S(1)}, bf16[4,64,128]{2,1,0:T(8,128)(2,1)S(1)}, u32[]{:S(2)}, u32[]{:S(2)}) collective-permute-start(bf16[4,64,128]{2,1,0:T(8,128)(2,1)S(1)} %add_convert_fusion), channel_id=1, source_target_pairs={{0,1},{1,0},{2,3},{3,2},{4,5},{5,4},{6,7},{7,6},{8,9},{9,8},{10,11... | collective-permute-start | bytes 196616 | tf_op jit(solution)/shard_map/ppermute | solution.py:235
  (3 other events, 83.8 us)

commit v14 on v13

--- a/solution.py
+++ b/solution.py
@@ -295,7 +295,7 @@
     z = z.reshape(RANK, n_col, chunk).transpose(1, 0, 2)
     z_bits = bits(n_z)[::-1]
     far = z_bits[0]
-    for offset in [0, far, *range(1, far)]:
+    for offset in [0, far]:
         move(states, offset)
     first = list(pieces)
     z = jnp.concatenate([z, from_xor(z, ("z",), far)])
@@ -303,6 +303,8 @@
     for offset in range(far + 1, n_z):
         move(slab, offset, 0, 2)
         move(slab, offset, 1, 2)
+    for offset in range(1, far):
+        move(slab, offset)
     for bit in bits(n_col):
         z = z + from_xor(z, ("col",), bit)
     z = hold(z, first)
@@ -314,7 +316,7 @@
     at_first = chunk_places([("z", bit, True) for bit in z_bits[::-1]] + absolute_col)
     relative_col = [("col", bit, True) for bit in bits(n_col)]
     at = chunk_places(relative_col + [("z", bit, False) for bit in z_bits])
-    late = [name for name in pieces if name[0] > far]
+    late = [name for name in pieces if name not in first]
     others = {name: from_xor(pieces[name], ("core",), 1) for name in first}
 
     f32 = jnp.float32

time: 177 us -> 181 us (1.023)
  waiting for transfers between devices: 106 us -> 111 us
    ppermute x33, waiting for transfers between devices: 106 us -> 111 us  [from_xor(): return lax.ppermute(value, axis, [(i, i ^ offset) for i in range(size)])]
    ppermute x33, starting transfers between devices: 26.4 us -> 28.2 us  [from_xor(): return lax.ppermute(value, axis, [(i, i ^ offset) for i in range(size)])]
  transfers between devices with their start and end apart: 33 -> 33, of which waited for: 25 -> 25; matrix products, arithmetic and copies ran while one was open for 3% -> 2% of each run, Pallas kernels for 3% -> 3%
where the time goes in v14:
time: 181 us
  waiting for transfers between devices  111 us (61%)
  Pallas kernels  32.8 us (18%)
  starting transfers between devices  28.2 us (16%)
  local copies, waits for them, and re-layouts  5.25 us (3%)
  matrix products  2.24 us (1%)
    ppermute x33, waiting for transfers between devices, from_xor(): return lax.ppermute(value, axis, [(i, i ^ offset) for i in range(size)])  111 us
    pallas_call x6, Pallas kernels, call(): pl.pallas_call(kernel, out_shape=out_shapes, in_specs=[pl.BlockSpec(memor...  32.8 us
    ppermute x33, starting transfers between devices, from_xor(): return lax.ppermute(value, axis, [(i, i ^ offset) for i in range(size)])  28.2 us
  transfers between devices with their start and end apart: 33, of which 25 were waited for; matrix products, arithmetic and copies ran while one was open for 2% of the time, Pallas kernels for 3%

profile of v14, /device:TPU:0, one launch (start us, length us, event | category | flops | bytes accessed | tf_op | source)
XLA Modules:
  0.0 181.3 jit_solution(9936557471886214483)
XLA Ops:
  0.7 2.2 %constant_dynamic-slice_fusion.2 = (bf16[256,1024]{1,0:T(8,128)(2,1)}, bf16[256,1024]{1,0:T(8,128)(2,1)S(1)}) fusion(bf16[256,4096]{1,0:T(8,128)(2,1)} %param.3, s32[]{:T(128)S(6)} %select_n.77, s32[]{:T(128)S(6)} %select_n.76), kind=kLoop, calls=%fused_computation.66 | loop fusion | bytes 2097160 | tf_op jit(solution)/shard_map/dynamic_slice | solution.py:282
  2.9 4.0 %collective-permute-start.2 = (bf16[256,1024]{1,0:T(8,128)(2,1)}, bf16[256,1024]{1,0:T(8,128)(2,1)S(1)}, u32[]{:S(2)}, u32[]{:S(2)}) collective-permute-start(bf16[256,1024]{1,0:T(8,128)(2,1)} %get-tuple-element.40), channel_id=1, source_target_pairs={{0,8},{4,12},{8,0},{12,4},{1,9},{5,13},{9,1},{13,5},{2,10},{6,14},... | collective-permute-start | bytes 1572872 | tf_op jit(solution)/shard_map/ppermute | solution.py:235
  7.6 2.2 %convolution_bitcast_fusion = f32[8,2,8,128]{3,2,1,0:T(8,128)S(1)} fusion(bf16[256,4096]{1,0:T(8,128)(2,1)S(1)} %copy-done.2, s32[]{:T(128)S(6)} %xor.73, s32[4096]{0:T(1024)S(1)} %add_multiply_fusion), kind=kOutput, calls=%fused_computation | convolution fusion | flops 152043520 | bytes 2179076 | tf_op jit(solution)/shard_map/dot_general | solution.py:292
  9.9 23.1 %collective-permute-done = f32[2,64,128]{2,1,0:T(8,128)S(1)} collective-permute-done((f32[2,64,128]{2,1,0:T(8,128)S(1)}, f32[2,64,128]{2,1,0:T(8,128)S(1)}, u32[]{:S(2)}, u32[]{:S(2)}) %collective-permute-start) | collective-permute-done | bytes 65568 | tf_op jit(solution)/shard_map/ppermute | solution.py:235
  34.7 3.6 %collective-permute-start.4 = (bf16[128,1024]{1,0:T(8,128)(2,1)S(1)}, bf16[128,1024]{1,0:T(8,128)(2,1)S(1)}, u32[]{:S(2)}, u32[]{:S(2)}) collective-permute-start(bf16[128,1024]{1,0:T(8,128)(2,1)S(1)} %get-tuple-element.39), channel_id=1, source_target_pairs={{0,12},{4,8},{8,4},{12,0},{1,13},{5,9},{9,5},{13,1},{2,14},{6,10},... | collective-permute-start | bytes 786440 | tf_op jit(solution)/shard_map/ppermute | solution.py:235
  40.5 7.3 %collective-permute-done.3 = f32[4,64,128]{2,1,0:T(8,128)S(1)} collective-permute-done((f32[4,64,128]{2,1,0:T(8,128)S(1)}, f32[4,64,128]{2,1,0:T(8,128)S(1)}, u32[]{:S(2)}, u32[]{:S(2)}) %collective-permute-start.3) | collective-permute-done | bytes 131104 | tf_op jit(solution)/shard_map/ppermute | solution.py:235
  48.0 3.2 %collective-permute-start.6 = (bf16[128,1024]{1,0:T(8,128)(2,1)S(1)}, bf16[128,1024]{1,0:T(8,128)(2,1)S(1)}, u32[]{:S(2)}, u32[]{:S(2)}) collective-permute-start(bf16[128,1024]{1,0:T(8,128)(2,1)S(1)} %get-tuple-element.38), channel_id=1, source_target_pairs={{0,12},{4,8},{8,4},{12,0},{1,13},{5,9},{9,5},{13,1},{2,14},{6,10},... | collective-permute-start | bytes 786440 | tf_op jit(solution)/shard_map/ppermute | solution.py:235
  51.8 6.0 %shard_map.41 = (bf16[64,2048]{1,0:T(8,128)(2,1)S(1)}, f32[64,64]{1,0:T(8,128)S(1)}) custom-call(s32[8]{0:T(128)S(1)} %fusion.19.at_ref, f32[8,64,128]{2,1,0:T(8,128)S(1)} %pad_maximum_fusion.z_ref, f32[8,64,128]{2,1,0:T(8,128)S(1)} %collective-permute-done.5.other_ref), custom_call_target="tpu_custom_call" | custom-call | flops 402653184 | bytes 524288 | tf_op jit(solution)/shard_map/pallas_call | solution.py:218
  57.8 6.4 %collective-permute-done.6.refs_4_ = bf16[128,1024]{1,0:T(8,128)(2,1)S(1)} collective-permute-done((bf16[128,1024]{1,0:T(8,128)(2,1)S(1)}, bf16[128,1024]{1,0:T(8,128)(2,1)S(1)}, u32[]{:S(2)}, u32[]{:S(2)}) %collective-permute-start.6) | collective-permute-done | bytes 262176 | tf_op jit(solution)/shard_map/ppermute | solution.py:235
  66.9 2.1 %shard_map.42 = (bf16[2048,1024]{1,0:T(8,128)(2,1)S(1)}, f32[8,64,128]{2,1,0:T(8,128)S(1)}) custom-call(s32[8]{0:T(128)S(1)} %fusion.17.at_ref, bf16[64,2048]{1,0:T(8,128)(2,1)S(1)} %get-tuple-element.23.basis_ref, bf16[256,1024]{1,0:T(8,128)(2,1)S(1)} %get-tuple-element.24.refs_0_, bf16[256,1024]{1,0:T(8,128)(2,1)S(1)} %collective-permute-done.7.refs_1_, ...), custom_call_target="tpu_custom_call" | custom-call | flops 939524096 | bytes 4456448 | tf_op jit(solution)/shard_map/pallas_call | solution.py:218
  69.7 5.0 %collective-permute-done.13 = f32[4,64,128]{2,1,0:T(8,128)S(1)} collective-permute-done((f32[4,64,128]{2,1,0:T(8,128)S(1)}, f32[4,64,128]{2,1,0:T(8,128)S(1)}, u32[]{:S(2)}, u32[]{:S(2)}) %collective-permute-start.13) | collective-permute-done | bytes 131104 | tf_op jit(solution)/shard_map/ppermute | solution.py:235
  74.8 5.0 %collective-permute-done.14 = f32[4,64,128]{2,1,0:T(8,128)S(1)} collective-permute-done((f32[4,64,128]{2,1,0:T(8,128)S(1)}, f32[4,64,128]{2,1,0:T(8,128)S(1)}, u32[]{:S(2)}, u32[]{:S(2)}) %collective-permute-start.14) | collective-permute-done | bytes 131104 | tf_op jit(solution)/shard_map/ppermute | solution.py:235
  79.8 2.2 %collective-permute-start.15 = (f32[4,64,128]{2,1,0:T(8,128)S(1)}, f32[4,64,128]{2,1,0:T(8,128)S(1)}, u32[]{:S(2)}, u32[]{:S(2)}) collective-permute-start(f32[4,64,128]{2,1,0:T(8,128)S(1)} %add.213), channel_id=1, source_target_pairs={{0,8},{4,12},{8,0},{12,4},{1,9},{5,13},{9,1},{13,5},{2,10},{6,14},... | collective-permute-start | bytes 393224 | tf_op jit(solution)/shard_map/ppermute | solution.py:235
  81.9 5.2 %collective-permute-done.15 = f32[4,64,128]{2,1,0:T(8,128)S(1)} collective-permute-done((f32[4,64,128]{2,1,0:T(8,128)S(1)}, f32[4,64,128]{2,1,0:T(8,128)S(1)}, u32[]{:S(2)}, u32[]{:S(2)}) %collective-permute-start.15) | collective-permute-done | bytes 131104 | tf_op jit(solution)/shard_map/ppermute | solution.py:235
  87.7 4.4 %collective-permute-done.16 = f32[4,64,128]{2,1,0:T(8,128)S(1)} collective-permute-done((f32[4,64,128]{2,1,0:T(8,128)S(1)}, f32[4,64,128]{2,1,0:T(8,128)S(1)}, u32[]{:S(2)}, u32[]{:S(2)}) %collective-permute-start.16) | collective-permute-done | bytes 131104 | tf_op jit(solution)/shard_map/ppermute | solution.py:235
  93.8 6.7 %shard_map.43 = f32[8,64,128]{2,1,0:T(8,128)S(1)} custom-call(s32[8]{0:T(128)S(1)} %fusion.17.at_ref, f32[8,64,128]{2,1,0:T(8,128)S(1)} %pad_maximum_fusion.1.z_ref, f32[8,64,128]{2,1,0:T(8,128)S(1)} %collective-permute-done.17.other_ref, bf16[2048,1024]{1,0:T(8,128)(2,1)S(1)} %get-tuple-element.30.a_ref), custom_call_target="tpu_custom_call" | custom-call | flops 939524096 | bytes 4718592 | tf_op jit(solution)/shard_map/pallas_call | solution.py:218
  101.1 3.7 %collective-permute-done.18 = bf16[4,64,128]{2,1,0:T(8,128)(2,1)S(1)} collective-permute-done((bf16[4,64,128]{2,1,0:T(8,128)(2,1)S(1)}, bf16[4,64,128]{2,1,0:T(8,128)(2,1)S(1)}, u32[]{:S(2)}, u32[]{:S(2)}) %collective-permute-start.18) | collective-permute-done | bytes 65568 | tf_op jit(solution)/shard_map/ppermute | solution.py:235
  105.4 3.8 %collective-permute-done.19 = bf16[4,64,128]{2,1,0:T(8,128)(2,1)S(1)} collective-permute-done((bf16[4,64,128]{2,1,0:T(8,128)(2,1)S(1)}, bf16[4,64,128]{2,1,0:T(8,128)(2,1)S(1)}, u32[]{:S(2)}, u32[]{:S(2)}) %collective-permute-start.19) | collective-permute-done | bytes 65568 | tf_op jit(solution)/shard_map/ppermute | solution.py:235
  111.1 4.1 %collective-permute-done.20 = bf16[4,64,128]{2,1,0:T(8,128)(2,1)S(1)} collective-permute-done((bf16[4,64,128]{2,1,0:T(8,128)(2,1)S(1)}, bf16[4,64,128]{2,1,0:T(8,128)(2,1)S(1)}, u32[]{:S(2)}, u32[]{:S(2)}) %collective-permute-start.20) | collective-permute-done | bytes 65568 | tf_op jit(solution)/shard_map/ppermute | solution.py:235
  115.8 3.7 %collective-permute-done.21 = bf16[4,64,128]{2,1,0:T(8,128)(2,1)S(1)} collective-permute-done((bf16[4,64,128]{2,1,0:T(8,128)(2,1)S(1)}, bf16[4,64,128]{2,1,0:T(8,128)(2,1)S(1)}, u32[]{:S(2)}, u32[]{:S(2)}) %collective-permute-start.21) | collective-permute-done | bytes 65568 | tf_op jit(solution)/shard_map/ppermute | solution.py:235
  121.0 6.1 %shard_map.44 = f32[8,64,128]{2,1,0:T(8,128)S(1)} custom-call(s32[8]{0:T(128)S(1)} %fusion.17.at_ref, bf16[8,64,128]{2,1,0:T(8,128)(2,1)S(1)} %pad_maximum_fusion.3.z_ref, bf16[8,64,128]{2,1,0:T(8,128)(2,1)S(1)} %collective-permute-done.22.other_ref, bf16[2048,1024]{1,0:T(8,128)(2,1)S(1)} %get-tuple-element.30.a_ref), custom_call_target="tpu_custom_call" | custom-call | flops 939524096 | bytes 4456448 | tf_op jit(solution)/shard_map/pallas_call | solution.py:218
  127.6 3.7 %collective-permute-done.23 = bf16[4,64,128]{2,1,0:T(8,128)(2,1)S(1)} collective-permute-done((bf16[4,64,128]{2,1,0:T(8,128)(2,1)S(1)}, bf16[4,64,128]{2,1,0:T(8,128)(2,1)S(1)}, u32[]{:S(2)}, u32[]{:S(2)}) %collective-permute-start.23) | collective-permute-done | bytes 65568 | tf_op jit(solution)/shard_map/ppermute | solution.py:235
  131.8 4.0 %collective-permute-done.24 = bf16[4,64,128]{2,1,0:T(8,128)(2,1)S(1)} collective-permute-done((bf16[4,64,128]{2,1,0:T(8,128)(2,1)S(1)}, bf16[4,64,128]{2,1,0:T(8,128)(2,1)S(1)}, u32[]{:S(2)}, u32[]{:S(2)}) %collective-permute-start.24) | collective-permute-done | bytes 65568 | tf_op jit(solution)/shard_map/ppermute | solution.py:235
  137.1 4.4 %collective-permute-done.25 = bf16[4,64,128]{2,1,0:T(8,128)(2,1)S(1)} collective-permute-done((bf16[4,64,128]{2,1,0:T(8,128)(2,1)S(1)}, bf16[4,64,128]{2,1,0:T(8,128)(2,1)S(1)}, u32[]{:S(2)}, u32[]{:S(2)}) %collective-permute-start.25) | collective-permute-done | bytes 65568 | tf_op jit(solution)/shard_map/ppermute | solution.py:235
  142.1 3.7 %collective-permute-done.26 = bf16[4,64,128]{2,1,0:T(8,128)(2,1)S(1)} collective-permute-done((bf16[4,64,128]{2,1,0:T(8,128)(2,1)S(1)}, bf16[4,64,128]{2,1,0:T(8,128)(2,1)S(1)}, u32[]{:S(2)}, u32[]{:S(2)}) %collective-permute-start.26) | collective-permute-done | bytes 65568 | tf_op jit(solution)/shard_map/ppermute | solution.py:235
  147.3 6.1 %shard_map.45 = f32[8,64,128]{2,1,0:T(8,128)S(1)} custom-call(s32[8]{0:T(128)S(1)} %fusion.17.at_ref, bf16[8,64,128]{2,1,0:T(8,128)(2,1)S(1)} %pad_maximum_fusion.4.z_ref, bf16[8,64,128]{2,1,0:T(8,128)(2,1)S(1)} %collective-permute-done.27.other_ref, bf16[2048,1024]{1,0:T(8,128)(2,1)S(1)} %get-tuple-element.30.a_ref), custom_call_target="tpu_custom_call" | custom-call | flops 939524096 | bytes 4456448 | tf_op jit(solution)/shard_map/pallas_call | solution.py:218
  153.9 3.7 %collective-permute-done.28 = bf16[4,64,128]{2,1,0:T(8,128)(2,1)S(1)} collective-permute-done((bf16[4,64,128]{2,1,0:T(8,128)(2,1)S(1)}, bf16[4,64,128]{2,1,0:T(8,128)(2,1)S(1)}, u32[]{:S(2)}, u32[]{:S(2)}) %collective-permute-start.28) | collective-permute-done | bytes 65568 | tf_op jit(solution)/shard_map/ppermute | solution.py:235
  157.8 4.3 %collective-permute-done.29 = bf16[4,64,128]{2,1,0:T(8,128)(2,1)S(1)} collective-permute-done((bf16[4,64,128]{2,1,0:T(8,128)(2,1)S(1)}, bf16[4,64,128]{2,1,0:T(8,128)(2,1)S(1)}, u32[]{:S(2)}, u32[]{:S(2)}) %collective-permute-start.29) | collective-permute-done | bytes 65568 | tf_op jit(solution)/shard_map/ppermute | solution.py:235
  163.0 4.4 %collective-permute-done.30 = bf16[4,64,128]{2,1,0:T(8,128)(2,1)S(1)} collective-permute-done((bf16[4,64,128]{2,1,0:T(8,128)(2,1)S(1)}, bf16[4,64,128]{2,1,0:T(8,128)(2,1)S(1)}, u32[]{:S(2)}, u32[]{:S(2)}) %collective-permute-start.30) | collective-permute-done | bytes 65568 | tf_op jit(solution)/shard_map/ppermute | solution.py:235
  168.1 3.7 %collective-permute-done.31 = bf16[4,64,128]{2,1,0:T(8,128)(2,1)S(1)} collective-permute-done((bf16[4,64,128]{2,1,0:T(8,128)(2,1)S(1)}, bf16[4,64,128]{2,1,0:T(8,128)(2,1)S(1)}, u32[]{:S(2)}, u32[]{:S(2)}) %collective-permute-start.31) | collective-permute-done | bytes 65568 | tf_op jit(solution)/shard_map/ppermute | solution.py:235
  173.2 2.2 %copy-done.1 = bf16[2048,1024]{1,0:T(8,128)(2,1)S(1)} copy-done((bf16[2048,1024]{1,0:T(8,128)(2,1)S(1)}, bf16[2048,1024]{1,0:T(8,128)(2,1)}, u32[]{:S(2)}) %copy-start.1) | copy-done | bytes 4194328
  175.4 5.9 %shard_map.46 = f32[64,512]{1,0:T(8,128)} custom-call(s32[8]{0:T(128)S(1)} %fusion.17.at_ref, s32[1]{0:T(128)} %bitcast.core_ref, bf16[8,64,128]{2,1,0:T(8,128)(2,1)S(1)} %pad_maximum_fusion.5.z_ref, bf16[8,64,128]{2,1,0:T(8,128)(2,1)S(1)} %collective-permute-done.32.other_ref, bf16[2048,1024]{1,0:T(8,128)(2,1)S(1)} %copy-done.1), custom_call_target="tpu_custom_call" | custom-call | flops 939524096 | bytes 4456448 | tf_op jit(solution)/shard_map/pallas_call | solution.py:218
  (79 shorter events, 23.4 us)
Async XLA Ops:
  2.9 35.5 %collective-permute-start.2 = (bf16[256,1024]{1,0:T(8,128)(2,1)}, bf16[256,1024]{1,0:T(8,128)(2,1)S(1)}, u32[]{:S(2)}, u32[]{:S(2)}) collective-permute-start(bf16[256,1024]{1,0:T(8,128)(2,1)} %get-tuple-element.40), channel_id=1, source_target_pairs={{0,8},{4,12},{8,0},{12,4},{1,9},{5,13},{9,1},{13,5},{2,10},{6,14},... | collective-permute-start | bytes 1572872 | tf_op jit(solution)/shard_map/ppermute | solution.py:235
  9.9 23.2 %collective-permute-start = (f32[2,64,128]{2,1,0:T(8,128)S(1)}, f32[2,64,128]{2,1,0:T(8,128)S(1)}, u32[]{:S(2)}, u32[]{:S(2)}) collective-permute-start(f32[2,64,128]{2,1,0:T(8,128)S(1)} %bitcast.16), channel_id=1, source_target_pairs={{0,8},{4,12},{8,0},{12,4},{1,9},{5,13},{9,1},{13,5},{2,10},{6,14},... | collective-permute-start | bytes 196616 | tf_op jit(solution)/shard_map/ppermute | solution.py:235
  33.1 5.2 %collective-permute-start.1 = (f32[4,64,128]{2,1,0:T(8,128)S(1)}, f32[4,64,128]{2,1,0:T(8,128)S(1)}, u32[]{:S(2)}, u32[]{:S(2)}) collective-permute-start(f32[4,64,128]{2,1,0:T(8,128)S(1)} %pad_maximum_fusion.2), channel_id=1, source_target_pairs={{0,1},{1,0},{2,3},{3,2},{4,5},{5,4},{6,7},{7,6},{8,9},{9,8},{10,11... | collective-permute-start | bytes 393224 | tf_op jit(solution)/shard_map/ppermute | solution.py:235
  34.7 13.2 %collective-permute-start.4 = (bf16[128,1024]{1,0:T(8,128)(2,1)S(1)}, bf16[128,1024]{1,0:T(8,128)(2,1)S(1)}, u32[]{:S(2)}, u32[]{:S(2)}) collective-permute-start(bf16[128,1024]{1,0:T(8,128)(2,1)S(1)} %get-tuple-element.39), channel_id=1, source_target_pairs={{0,12},{4,8},{8,4},{12,0},{1,13},{5,9},{9,5},{13,1},{2,14},{6,10},... | collective-permute-start | bytes 786440 | tf_op jit(solution)/shard_map/ppermute | solution.py:235
  38.3 9.5 %collective-permute-start.3 = (f32[4,64,128]{2,1,0:T(8,128)S(1)}, f32[4,64,128]{2,1,0:T(8,128)S(1)}, u32[]{:S(2)}, u32[]{:S(2)}) collective-permute-start(f32[4,64,128]{2,1,0:T(8,128)S(1)} %add.207), channel_id=1, source_target_pairs={{0,4},{4,0},{8,12},{12,8},{1,5},{5,1},{9,13},{13,9},{2,6},{6,2},{1... | collective-permute-start | bytes 393224 | tf_op jit(solution)/shard_map/ppermute | solution.py:235
  39.4 24.8 %collective-permute-start.7 = (bf16[256,1024]{1,0:T(8,128)(2,1)S(1)}, bf16[256,1024]{1,0:T(8,128)(2,1)S(1)}, u32[]{:S(2)}, u32[]{:S(2)}) collective-permute-start(bf16[256,1024]{1,0:T(8,128)(2,1)S(1)} %constant_dynamic-slice_fusion), channel_id=1, source_target_pairs={{0,4},{4,0},{8,12},{12,8},{1,5},{5,1},{9,13},{13,9},{2,6},{6,2},{1... | collective-permute-start | bytes 1572872 | tf_op jit(solution)/shard_map/ppermute | solution.py:235
  47.9 3.9 %collective-permute-start.5 = (f32[8,64,128]{2,1,0:T(8,128)S(1)}, f32[8,64,128]{2,1,0:T(8,128)S(1)}, u32[]{:S(2)}, u32[]{:S(2)}) collective-permute-start(f32[8,64,128]{2,1,0:T(8,128)S(1)} %pad_maximum_fusion.z_ref), channel_id=1, source_target_pairs={{0,2},{2,0},{1,3},{3,1},{4,6},{6,4},{5,7},{7,5},{8,10},{10,8},{9,1... | collective-permute-start | bytes 786440 | tf_op jit(solution)/shard_map/ppermute | solution.py:235
  48.0 16.3 %collective-permute-start.6 = (bf16[128,1024]{1,0:T(8,128)(2,1)S(1)}, bf16[128,1024]{1,0:T(8,128)(2,1)S(1)}, u32[]{:S(2)}, u32[]{:S(2)}) collective-permute-start(bf16[128,1024]{1,0:T(8,128)(2,1)S(1)} %get-tuple-element.38), channel_id=1, source_target_pairs={{0,12},{4,8},{8,4},{12,0},{1,13},{5,9},{9,5},{13,1},{2,14},{6,10},... | collective-permute-start | bytes 786440 | tf_op jit(solution)/shard_map/ppermute | solution.py:235
  51.2 13.6 %collective-permute-start.8 = (bf16[256,1024]{1,0:T(8,128)(2,1)S(1)}, bf16[256,1024]{1,0:T(8,128)(2,1)S(1)}, u32[]{:S(2)}, u32[]{:S(2)}) collective-permute-start(bf16[256,1024]{1,0:T(8,128)(2,1)S(1)} %get-tuple-element.24.refs_0_), channel_id=1, source_target_pairs={{0,2},{2,0},{1,3},{3,1},{4,6},{6,4},{5,7},{7,5},{8,10},{10,8},{9,1... | collective-permute-start | bytes 1572872 | tf_op jit(solution)/shard_map/ppermute | solution.py:235
  51.5 13.4 %collective-permute-start.10 = (bf16[256,1024]{1,0:T(8,128)(2,1)S(1)}, bf16[256,1024]{1,0:T(8,128)(2,1)S(1)}, u32[]{:S(2)}, u32[]{:S(2)}) collective-permute-start(bf16[256,1024]{1,0:T(8,128)(2,1)S(1)} %collective-permute-done.2.refs_2_), channel_id=1, source_target_pairs={{0,2},{2,0},{1,3},{3,1},{4,6},{6,4},{5,7},{7,5},{8,10},{10,8},{9,1... | collective-permute-start | bytes 1572872 | tf_op jit(solution)/shard_map/ppermute | solution.py:235
  64.3 2.7 %collective-permute-start.9 = (bf16[256,1024]{1,0:T(8,128)(2,1)S(1)}, bf16[256,1024]{1,0:T(8,128)(2,1)S(1)}, u32[]{:S(2)}, u32[]{:S(2)}) collective-permute-start(bf16[256,1024]{1,0:T(8,128)(2,1)S(1)} %collective-permute-done.7.refs_1_), channel_id=1, source_target_pairs={{0,2},{2,0},{1,3},{3,1},{4,6},{6,4},{5,7},{7,5},{8,10},{10,8},{9,1... | collective-permute-start | bytes 1572872 | tf_op jit(solution)/shard_map/ppermute | solution.py:235
  64.3 2.3 %collective-permute-start.11 = (bf16[128,1024]{1,0:T(8,128)(2,1)S(1)}, bf16[128,1024]{1,0:T(8,128)(2,1)S(1)}, u32[]{:S(2)}, u32[]{:S(2)}) collective-permute-start(bf16[128,1024]{1,0:T(8,128)(2,1)S(1)} %collective-permute-done.4.refs_3_), channel_id=1, source_target_pairs={{0,2},{2,0},{1,3},{3,1},{4,6},{6,4},{5,7},{7,5},{8,10},{10,8},{9,1... | collective-permute-start | bytes 786440 | tf_op jit(solution)/shard_map/ppermute | solution.py:235
  64.8 2.1 %collective-permute-start.12 = (bf16[128,1024]{1,0:T(8,128)(2,1)S(1)}, bf16[128,1024]{1,0:T(8,128)(2,1)S(1)}, u32[]{:S(2)}, u32[]{:S(2)}) collective-permute-start(bf16[128,1024]{1,0:T(8,128)(2,1)S(1)} %collective-permute-done.6.refs_4_), channel_id=1, source_target_pairs={{0,2},{2,0},{1,3},{3,1},{4,6},{6,4},{5,7},{7,5},{8,10},{10,8},{9,1... | collective-permute-start | bytes 786440 | tf_op jit(solution)/shard_map/ppermute | solution.py:235
  69.1 5.6 %collective-permute-start.13 = (f32[4,64,128]{2,1,0:T(8,128)S(1)}, f32[4,64,128]{2,1,0:T(8,128)S(1)}, u32[]{:S(2)}, u32[]{:S(2)}) collective-permute-start(f32[4,64,128]{2,1,0:T(8,128)S(1)} %slice.28), channel_id=1, source_target_pairs={{0,1},{1,0},{2,3},{3,2},{4,5},{5,4},{6,7},{7,6},{8,9},{9,8},{10,11... | collective-permute-start | bytes 393224 | tf_op jit(solution)/shard_map/ppermute | solution.py:235
  74.7 5.0 %collective-permute-start.14 = (f32[4,64,128]{2,1,0:T(8,128)S(1)}, f32[4,64,128]{2,1,0:T(8,128)S(1)}, u32[]{:S(2)}, u32[]{:S(2)}) collective-permute-start(f32[4,64,128]{2,1,0:T(8,128)S(1)} %slice_add_fusion.3), channel_id=1, source_target_pairs={{0,4},{4,0},{8,12},{12,8},{1,5},{5,1},{9,13},{13,9},{2,6},{6,2},{1... | collective-permute-start | bytes 393224 | tf_op jit(solution)/shard_map/ppermute | solution.py:235
  79.8 7.3 %collective-permute-start.15 = (f32[4,64,128]{2,1,0:T(8,128)S(1)}, f32[4,64,128]{2,1,0:T(8,128)S(1)}, u32[]{:S(2)}, u32[]{:S(2)}) collective-permute-start(f32[4,64,128]{2,1,0:T(8,128)S(1)} %add.213), channel_id=1, source_target_pairs={{0,8},{4,12},{8,0},{12,4},{1,9},{5,13},{9,1},{13,5},{2,10},{6,14},... | collective-permute-start | bytes 393224 | tf_op jit(solution)/shard_map/ppermute | solution.py:235
  87.1 5.0 %collective-permute-start.16 = (f32[4,64,128]{2,1,0:T(8,128)S(1)}, f32[4,64,128]{2,1,0:T(8,128)S(1)}, u32[]{:S(2)}, u32[]{:S(2)}) collective-permute-start(f32[4,64,128]{2,1,0:T(8,128)S(1)} %add.214), channel_id=1, source_target_pairs={{0,1},{1,0},{2,3},{3,2},{4,5},{5,4},{6,7},{7,6},{8,9},{9,8},{10,11... | collective-permute-start | bytes 393224 | tf_op jit(solution)/shard_map/ppermute | solution.py:235
  92.2 1.6 collective-permute-start.17
  100.5 4.3 %collective-permute-start.18 = (bf16[4,64,128]{2,1,0:T(8,128)(2,1)S(1)}, bf16[4,64,128]{2,1,0:T(8,128)(2,1)S(1)}, u32[]{:S(2)}, u32[]{:S(2)}) collective-permute-start(bf16[4,64,128]{2,1,0:T(8,128)(2,1)S(1)} %slice.56), channel_id=1, source_target_pairs={{0,1},{1,0},{2,3},{3,2},{4,5},{5,4},{6,7},{7,6},{8,9},{9,8},{10,11... | collective-permute-start | bytes 196616 | tf_op jit(solution)/shard_map/ppermute | solution.py:235
  104.9 4.3 %collective-permute-start.19 = (bf16[4,64,128]{2,1,0:T(8,128)(2,1)S(1)}, bf16[4,64,128]{2,1,0:T(8,128)(2,1)S(1)}, u32[]{:S(2)}, u32[]{:S(2)}) collective-permute-start(bf16[4,64,128]{2,1,0:T(8,128)(2,1)S(1)} %fusion.15), channel_id=1, source_target_pairs={{0,4},{4,0},{8,12},{12,8},{1,5},{5,1},{9,13},{13,9},{2,6},{6,2},{1... | collective-permute-start | bytes 196616 | tf_op jit(solution)/shard_map/ppermute | solution.py:235
  109.2 5.9 %collective-permute-start.20 = (bf16[4,64,128]{2,1,0:T(8,128)(2,1)S(1)}, bf16[4,64,128]{2,1,0:T(8,128)(2,1)S(1)}, u32[]{:S(2)}, u32[]{:S(2)}) collective-permute-start(bf16[4,64,128]{2,1,0:T(8,128)(2,1)S(1)} %add_convert_fusion.5), channel_id=1, source_target_pairs={{0,8},{4,12},{8,0},{12,4},{1,9},{5,13},{9,1},{13,5},{2,10},{6,14},... | collective-permute-start | bytes 196616 | tf_op jit(solution)/shard_map/ppermute | solution.py:235
  115.2 4.3 %collective-permute-start.21 = (bf16[4,64,128]{2,1,0:T(8,128)(2,1)S(1)}, bf16[4,64,128]{2,1,0:T(8,128)(2,1)S(1)}, u32[]{:S(2)}, u32[]{:S(2)}) collective-permute-start(bf16[4,64,128]{2,1,0:T(8,128)(2,1)S(1)} %add_convert_fusion.4), channel_id=1, source_target_pairs={{0,1},{1,0},{2,3},{3,2},{4,5},{5,4},{6,7},{7,6},{8,9},{9,8},{10,11... | collective-permute-start | bytes 196616 | tf_op jit(solution)/shard_map/ppermute | solution.py:235
  119.5 1.4 collective-permute-start.22
  127.0 4.3 %collective-permute-start.23 = (bf16[4,64,128]{2,1,0:T(8,128)(2,1)S(1)}, bf16[4,64,128]{2,1,0:T(8,128)(2,1)S(1)}, u32[]{:S(2)}, u32[]{:S(2)}) collective-permute-start(bf16[4,64,128]{2,1,0:T(8,128)(2,1)S(1)} %slice.55), channel_id=1, source_target_pairs={{0,1},{1,0},{2,3},{3,2},{4,5},{5,4},{6,7},{7,6},{8,9},{9,8},{10,11... | collective-permute-start | bytes 196616 | tf_op jit(solution)/shard_map/ppermute | solution.py:235
  131.4 4.3 %collective-permute-start.24 = (bf16[4,64,128]{2,1,0:T(8,128)(2,1)S(1)}, bf16[4,64,128]{2,1,0:T(8,128)(2,1)S(1)}, u32[]{:S(2)}, u32[]{:S(2)}) collective-permute-start(bf16[4,64,128]{2,1,0:T(8,128)(2,1)S(1)} %fusion.14), channel_id=1, source_target_pairs={{0,4},{4,0},{8,12},{12,8},{1,5},{5,1},{9,13},{13,9},{2,6},{6,2},{1... | collective-permute-start | bytes 196616 | tf_op jit(solution)/shard_map/ppermute | solution.py:235
  135.8 5.7 %collective-permute-start.25 = (bf16[4,64,128]{2,1,0:T(8,128)(2,1)S(1)}, bf16[4,64,128]{2,1,0:T(8,128)(2,1)S(1)}, u32[]{:S(2)}, u32[]{:S(2)}) collective-permute-start(bf16[4,64,128]{2,1,0:T(8,128)(2,1)S(1)} %add_convert_fusion.3), channel_id=1, source_target_pairs={{0,8},{4,12},{8,0},{12,4},{1,9},{5,13},{9,1},{13,5},{2,10},{6,14},... | collective-permute-start | bytes 196616 | tf_op jit(solution)/shard_map/ppermute | solution.py:235
  141.5 4.3 %collective-permute-start.26 = (bf16[4,64,128]{2,1,0:T(8,128)(2,1)S(1)}, bf16[4,64,128]{2,1,0:T(8,128)(2,1)S(1)}, u32[]{:S(2)}, u32[]{:S(2)}) collective-permute-start(bf16[4,64,128]{2,1,0:T(8,128)(2,1)S(1)} %add_convert_fusion.2), channel_id=1, source_target_pairs={{0,1},{1,0},{2,3},{3,2},{4,5},{5,4},{6,7},{7,6},{8,9},{9,8},{10,11... | collective-permute-start | bytes 196616 | tf_op jit(solution)/shard_map/ppermute | solution.py:235
  145.8 1.4 collective-permute-start.27
  153.3 4.3 %collective-permute-start.28 = (bf16[4,64,128]{2,1,0:T(8,128)(2,1)S(1)}, bf16[4,64,128]{2,1,0:T(8,128)(2,1)S(1)}, u32[]{:S(2)}, u32[]{:S(2)}) collective-permute-start(bf16[4,64,128]{2,1,0:T(8,128)(2,1)S(1)} %slice.54), channel_id=1, source_target_pairs={{0,1},{1,0},{2,3},{3,2},{4,5},{5,4},{6,7},{7,6},{8,9},{9,8},{10,11... | collective-permute-start | bytes 196616 | tf_op jit(solution)/shard_map/ppermute | solution.py:235
  157.7 4.3 %collective-permute-start.29 = (bf16[4,64,128]{2,1,0:T(8,128)(2,1)S(1)}, bf16[4,64,128]{2,1,0:T(8,128)(2,1)S(1)}, u32[]{:S(2)}, u32[]{:S(2)}) collective-permute-start(bf16[4,64,128]{2,1,0:T(8,128)(2,1)S(1)} %fusion.13), channel_id=1, source_target_pairs={{0,4},{4,0},{8,12},{12,8},{1,5},{5,1},{9,13},{13,9},{2,6},{6,2},{1... | collective-permute-start | bytes 196616 | tf_op jit(solution)/shard_map/ppermute | solution.py:235
  162.1 5.4 %collective-permute-start.30 = (bf16[4,64,128]{2,1,0:T(8,128)(2,1)S(1)}, bf16[4,64,128]{2,1,0:T(8,128)(2,1)S(1)}, u32[]{:S(2)}, u32[]{:S(2)}) collective-permute-start(bf16[4,64,128]{2,1,0:T(8,128)(2,1)S(1)} %add_convert_fusion.1), channel_id=1, source_target_pairs={{0,8},{4,12},{8,0},{12,4},{1,9},{5,13},{9,1},{13,5},{2,10},{6,14},... | collective-permute-start | bytes 196616 | tf_op jit(solution)/shard_map/ppermute | solution.py:235
  167.5 4.3 %collective-permute-start.31 = (bf16[4,64,128]{2,1,0:T(8,128)(2,1)S(1)}, bf16[4,64,128]{2,1,0:T(8,128)(2,1)S(1)}, u32[]{:S(2)}, u32[]{:S(2)}) collective-permute-start(bf16[4,64,128]{2,1,0:T(8,128)(2,1)S(1)} %add_convert_fusion), channel_id=1, source_target_pairs={{0,1},{1,0},{2,3},{3,2},{4,5},{5,4},{6,7},{7,6},{8,9},{9,8},{10,11... | collective-permute-start | bytes 196616 | tf_op jit(solution)/shard_map/ppermute | solution.py:235
  (4 other events, 88.7 us)

commit v15 on v13

--- a/solution.py
+++ b/solution.py
@@ -235,21 +235,36 @@
     return lax.ppermute(value, axis, [(i, i ^ offset) for i in range(size)])
 
 
+def square_devices():
+    n_z, n_col = lax.axis_size("z"), lax.axis_size("col")
+    sides = [(z, col) for z in range(2 if n_z > 2 else 1) for col in range(n_col)]
+    return [(z * n_col + col, col * (2 if n_z > 2 else 1) + z) for z, col in sides[:0:-1]]
+
+
 def sum_parts(total, dtype):
-    for bit in bits(lax.axis_size("col")):
-        half = total.shape[0] // 2
-        other = from_xor(total[half:].astype(dtype), ("col",), bit)
-        total = total[:half] + other.astype(jnp.float32)
-    for bit in bits(lax.axis_size("z")):
+    offsets = square_devices()
+    step = total.shape[0] // (len(offsets) + 1)
+    others = [
+        from_xor(total[step * place : step * (place + 1)].astype(dtype), ("z", "col"), offset)
+        for offset, place in offsets
+    ]
+    total = functools.reduce(jnp.add, [x.astype(jnp.float32) for x in others], total[:step])
+    for bit in far_bits():
         mine = total.astype(dtype)
         total = mine.astype(jnp.float32) + from_xor(mine, ("z",), bit).astype(jnp.float32)
     return total.astype(dtype)
 
 
 def gather_parts(own):
-    for bit in bits(lax.axis_size("col"))[::-1]:
-        own = jnp.concatenate([own, from_xor(own, ("col",), bit)])
+    placed = {0: own}
+    for offset, place in square_devices():
+        placed[place] = from_xor(own, ("z", "col"), offset)
+    own = jnp.concatenate([placed[place] for place in sorted(placed)])
     return own, from_xor(own, ("core",), 1)
+
+
+def far_bits():
+    return bits(lax.axis_size("z"))[1 if lax.axis_size("z") > 2 else 0 :]
 
 
 def chunk_places(digits):
@@ -312,8 +327,9 @@
     z = z, from_xor(z, ("core",), 1)
     absolute_col = [("col", bit, False) for bit in bits(n_col)[::-1]]
     at_first = chunk_places([("z", bit, True) for bit in z_bits[::-1]] + absolute_col)
-    relative_col = [("col", bit, True) for bit in bits(n_col)]
-    at = chunk_places(relative_col + [("z", bit, False) for bit in z_bits])
+    digits = [("col", bit, True) for bit in bits(n_col)[::-1]]
+    digits += [("z", 1, True)] if n_z > 2 else []
+    at = chunk_places(digits + [("z", bit, False) for bit in far_bits()])
     late = [name for name in pieces if name[0] > far]
     others = {name: from_xor(pieces[name], ("core",), 1) for name in first}
 
@@ -379,7 +395,7 @@
 
 def solution(mesh):
     n_grp, n_row, n_col = (mesh.shape[name] for name in ("grp", "row", "col"))
-    fits = n_row >= 4 and n_row & (n_row - 1) == 0
+    fits = n_row >= 4 and n_row & (n_row - 1) == 0 and n_col & (n_col - 1) == 0
 
     def run(sketch_base, states):
         rows_local = states.shape[0] // (n_grp * n_row)

time: 177 us -> 171 us (0.966)
  waiting for transfers between devices: 106 us -> 81.1 us
  starting transfers between devices: 26.4 us -> 45 us
    ppermute x33 -> x45, waiting for transfers between devices: 106 us -> 81.1 us  [from_xor(): return lax.ppermute(value, axis, [(i, i ^ offset) for i in range(size)])]
    ppermute x33 -> x45, starting transfers between devices: 26.4 us -> 45 us  [from_xor(): return lax.ppermute(value, axis, [(i, i ^ offset) for i in range(size)])]
  transfers between devices with their start and end apart: 33 -> 45, of which waited for: 25 -> 34; matrix products, arithmetic and copies ran while one was open for 3% -> 3% of each run, Pallas kernels for 3% -> 4%
where the time goes in v15:
time: 171 us; the launch traced here: 170 us
  waiting for transfers between devices  81.1 us (47%)
  starting transfers between devices  45 us (26%)
  Pallas kernels  32.8 us (19%)
  local copies, waits for them, and re-layouts  5.53 us (3%)
  matrix products  3.83 us (2%)
    ppermute x45, waiting for transfers between devices, from_xor(): return lax.ppermute(value, axis, [(i, i ^ offset) for i in range(size)])  81.1 us
    ppermute x45, starting transfers between devices, from_xor(): return lax.ppermute(value, axis, [(i, i ^ offset) for i in range(size)])  45 us
    pallas_call x6, Pallas kernels, call(): pl.pallas_call(kernel, out_shape=out_shapes, in_specs=[pl.BlockSpec(memor...  32.8 us
    dot_general x1, matrix products, per_device_transposed(): lax.dot_general(omega, states, (((0,), (1,)), ((), ())), preferred_elemen...  3.83 us
  transfers between devices with their start and end apart: 45, of which 34 were waited for; matrix products, arithmetic and copies ran while one was open for 3% of the time, Pallas kernels for 4%

profile of v15, /device:TPU:0, one launch (start us, length us, event | category | flops | bytes accessed | tf_op | source)
XLA Modules:
  0.0 170.3 jit_solution(16403515067923838110)
XLA Ops:
  2.1 3.1 %collective-permute-start.3 = (bf16[256,1024]{1,0:T(8,128)(2,1)S(1)}, bf16[256,1024]{1,0:T(8,128)(2,1)S(1)}, u32[]{:S(2)}, u32[]{:S(2)}) collective-permute-start(bf16[256,1024]{1,0:T(8,128)(2,1)S(1)} %get-tuple-element.40), channel_id=1, source_target_pairs={{0,4},{4,0},{8,12},{12,8},{1,5},{5,1},{9,13},{13,9},{2,6},{6,2},{1... | collective-permute-start | bytes 1572872 | tf_op jit(solution)/shard_map/ppermute | solution.py:235
  5.2 2.6 %collective-permute-start.2 = (bf16[256,1024]{1,0:T(8,128)(2,1)S(1)}, bf16[256,1024]{1,0:T(8,128)(2,1)S(1)}, u32[]{:S(2)}, u32[]{:S(2)}) collective-permute-start(bf16[256,1024]{1,0:T(8,128)(2,1)S(1)} %get-tuple-element.42), channel_id=1, source_target_pairs={{0,8},{4,12},{8,0},{12,4},{1,9},{5,13},{9,1},{13,5},{2,10},{6,14},... | collective-permute-start | bytes 1572872 | tf_op jit(solution)/shard_map/ppermute | solution.py:235
  8.5 3.8 %convolution_bitcast_fusion = f32[8,2,8,128]{3,2,1,0:T(8,128)S(1)} fusion(bf16[256,4096]{1,0:T(8,128)(2,1)} %param.3, s32[]{:T(128)S(6)} %xor.73, s32[4096]{0:T(1024)S(1)} %add_multiply_fusion), kind=kOutput, calls=%fused_computation | convolution fusion | flops 152043520 | bytes 2179076 | tf_op jit(solution)/shard_map/dot_general | solution.py:307
  12.8 20.8 %collective-permute-done = f32[2,64,128]{2,1,0:T(8,128)S(1)} collective-permute-done((f32[2,64,128]{2,1,0:T(8,128)S(1)}, f32[2,64,128]{2,1,0:T(8,128)S(1)}, u32[]{:S(2)}, u32[]{:S(2)}) %collective-permute-start) | collective-permute-done | bytes 65568 | tf_op jit(solution)/shard_map/ppermute | solution.py:235
  36.2 2.5 %collective-permute-start.5 = (bf16[128,1024]{1,0:T(8,128)(2,1)S(1)}, bf16[128,1024]{1,0:T(8,128)(2,1)S(1)}, u32[]{:S(2)}, u32[]{:S(2)}) collective-permute-start(bf16[128,1024]{1,0:T(8,128)(2,1)S(1)} %get-tuple-element.39), channel_id=1, source_target_pairs={{0,12},{4,8},{8,4},{12,0},{1,13},{5,9},{9,5},{13,1},{2,14},{6,10},... | collective-permute-start | bytes 786440 | tf_op jit(solution)/shard_map/ppermute | solution.py:235
  38.9 8.7 %collective-permute-done.4 = f32[4,64,128]{2,1,0:T(8,128)S(1)} collective-permute-done((f32[4,64,128]{2,1,0:T(8,128)S(1)}, f32[4,64,128]{2,1,0:T(8,128)S(1)}, u32[]{:S(2)}, u32[]{:S(2)}) %collective-permute-start.4) | collective-permute-done | bytes 131104 | tf_op jit(solution)/shard_map/ppermute | solution.py:235
  47.7 2.2 %collective-permute-start.7 = (bf16[128,1024]{1,0:T(8,128)(2,1)S(1)}, bf16[128,1024]{1,0:T(8,128)(2,1)S(1)}, u32[]{:S(2)}, u32[]{:S(2)}) collective-permute-start(bf16[128,1024]{1,0:T(8,128)(2,1)S(1)} %get-tuple-element.38), channel_id=1, source_target_pairs={{0,12},{4,8},{8,4},{12,0},{1,13},{5,9},{9,5},{13,1},{2,14},{6,10},... | collective-permute-start | bytes 786440 | tf_op jit(solution)/shard_map/ppermute | solution.py:235
  50.7 6.0 %shard_map.41 = (bf16[64,2048]{1,0:T(8,128)(2,1)S(1)}, f32[64,64]{1,0:T(8,128)S(1)}) custom-call(s32[8]{0:T(128)S(1)} %fusion.24.at_ref, f32[8,64,128]{2,1,0:T(8,128)S(1)} %pad_maximum_fusion.z_ref, f32[8,64,128]{2,1,0:T(8,128)S(1)} %collective-permute-done.6.other_ref), custom_call_target="tpu_custom_call" | custom-call | flops 402653184 | bytes 524288 | tf_op jit(solution)/shard_map/pallas_call | solution.py:218
  56.7 1.7 collective-permute-done.7.refs_4_
  60.3 2.1 %shard_map.42 = (bf16[2048,1024]{1,0:T(8,128)(2,1)S(1)}, f32[8,64,128]{2,1,0:T(8,128)S(1)}) custom-call(s32[8]{0:T(128)S(1)} %fusion.22.at_ref, bf16[64,2048]{1,0:T(8,128)(2,1)S(1)} %get-tuple-element.23.basis_ref, bf16[256,1024]{1,0:T(8,128)(2,1)S(1)} %get-tuple-element.24.refs_0_, bf16[256,1024]{1,0:T(8,128)(2,1)S(1)} %collective-permute-done.3.refs_1_, ...), custom_call_target="tpu_custom_call" | custom-call | flops 939524096 | bytes 4456448 | tf_op jit(solution)/shard_map/pallas_call | solution.py:218
  62.5 4.4 %collective-permute-start.13 = (f32[2,64,128]{2,1,0:T(8,128)S(1)}, f32[2,64,128]{2,1,0:T(8,128)S(1)}, u32[]{:S(2)}, u32[]{:S(2)}) collective-permute-start(f32[2,64,128]{2,1,0:T(8,128)S(1)} %get-tuple-element.43), channel_id=1, source_target_pairs={{0,5},{1,4},{4,1},{5,0},{8,13},{9,12},{12,9},{13,8},{2,7},{3,6},{6... | collective-permute-start | bytes 196616 | tf_op jit(solution)/shard_map/ppermute | solution.py:235
  69.2 1.9 %collective-permute-done.15 = f32[2,64,128]{2,1,0:T(8,128)S(1)} collective-permute-done((f32[2,64,128]{2,1,0:T(8,128)S(1)}, f32[2,64,128]{2,1,0:T(8,128)S(1)}, u32[]{:S(2)}, u32[]{:S(2)}) %collective-permute-start.15) | collective-permute-done | bytes 65568 | tf_op jit(solution)/shard_map/ppermute | solution.py:235
  72.7 5.3 %collective-permute-done.16 = f32[2,64,128]{2,1,0:T(8,128)S(1)} collective-permute-done((f32[2,64,128]{2,1,0:T(8,128)S(1)}, f32[2,64,128]{2,1,0:T(8,128)S(1)}, u32[]{:S(2)}, u32[]{:S(2)}) %collective-permute-start.16) | collective-permute-done | bytes 65568 | tf_op jit(solution)/shard_map/ppermute | solution.py:235
  79.4 2.2 %collective-permute-start.17 = (f32[2,64,128]{2,1,0:T(8,128)S(1)}, f32[2,64,128]{2,1,0:T(8,128)S(1)}, u32[]{:S(2)}, u32[]{:S(2)}) collective-permute-start(f32[2,64,128]{2,1,0:T(8,128)S(1)} %add.225), channel_id=1, source_target_pairs={{0,4},{1,5},{4,0},{5,1},{8,12},{9,13},{12,8},{13,9},{2,6},{3,7},{6... | collective-permute-start | bytes 196616 | tf_op jit(solution)/shard_map/ppermute | solution.py:235
  81.6 1.8 %collective-permute-done.19 = f32[2,64,128]{2,1,0:T(8,128)S(1)} collective-permute-done((f32[2,64,128]{2,1,0:T(8,128)S(1)}, f32[2,64,128]{2,1,0:T(8,128)S(1)}, u32[]{:S(2)}, u32[]{:S(2)}) %collective-permute-start.19) | collective-permute-done | bytes 65568 | tf_op jit(solution)/shard_map/ppermute | solution.py:235
  85.5 6.7 %shard_map.43 = f32[8,64,128]{2,1,0:T(8,128)S(1)} custom-call(s32[8]{0:T(128)S(1)} %fusion.22.at_ref, f32[8,64,128]{2,1,0:T(8,128)S(1)} %pad_maximum_fusion.1.z_ref, f32[8,64,128]{2,1,0:T(8,128)S(1)} %collective-permute-done.20.other_ref, bf16[2048,1024]{1,0:T(8,128)(2,1)S(1)} %get-tuple-element.30.a_ref), custom_call_target="tpu_custom_call" | custom-call | flops 939524096 | bytes 4718592 | tf_op jit(solution)/shard_map/pallas_call | solution.py:218
  92.2 2.6 %collective-permute-start.21 = (bf16[2,64,128]{2,1,0:T(8,128)(2,1)S(1)}, bf16[2,64,128]{2,1,0:T(8,128)(2,1)S(1)}, u32[]{:S(2)}, u32[]{:S(2)}) collective-permute-start(bf16[2,64,128]{2,1,0:T(8,128)(2,1)S(1)} %get-tuple-element.52), channel_id=1, source_target_pairs={{0,5},{1,4},{4,1},{5,0},{8,13},{9,12},{12,9},{13,8},{2,7},{3,6},{6... | collective-permute-start | bytes 98312 | tf_op jit(solution)/shard_map/ppermute | solution.py:235
  97.1 1.6 collective-permute-done.23
  99.8 4.8 %collective-permute-done.24 = bf16[2,64,128]{2,1,0:T(8,128)(2,1)S(1)} collective-permute-done((bf16[2,64,128]{2,1,0:T(8,128)(2,1)S(1)}, bf16[2,64,128]{2,1,0:T(8,128)(2,1)S(1)}, u32[]{:S(2)}, u32[]{:S(2)}) %collective-permute-start.24) | collective-permute-done | bytes 32800 | tf_op jit(solution)/shard_map/ppermute | solution.py:235
  106.1 2.0 %collective-permute-start.25 = (bf16[2,64,128]{2,1,0:T(8,128)(2,1)S(1)}, bf16[2,64,128]{2,1,0:T(8,128)(2,1)S(1)}, u32[]{:S(2)}, u32[]{:S(2)}) collective-permute-start(bf16[2,64,128]{2,1,0:T(8,128)(2,1)S(1)} %add_convert_fusion.2), channel_id=1, source_target_pairs={{0,4},{1,5},{4,0},{5,1},{8,12},{9,13},{12,8},{13,9},{2,6},{3,7},{6... | collective-permute-start | bytes 98312 | tf_op jit(solution)/shard_map/ppermute | solution.py:235
  111.5 6.1 %shard_map.44 = f32[8,64,128]{2,1,0:T(8,128)S(1)} custom-call(s32[8]{0:T(128)S(1)} %fusion.22.at_ref, bf16[8,64,128]{2,1,0:T(8,128)(2,1)S(1)} %pad_maximum_fusion.3.z_ref, bf16[8,64,128]{2,1,0:T(8,128)(2,1)S(1)} %collective-permute-done.28.other_ref, bf16[2048,1024]{1,0:T(8,128)(2,1)S(1)} %get-tuple-element.30.a_ref), custom_call_target="tpu_custom_call" | custom-call | flops 939524096 | bytes 4456448 | tf_op jit(solution)/shard_map/pallas_call | solution.py:218
  117.6 2.6 %collective-permute-start.29 = (bf16[2,64,128]{2,1,0:T(8,128)(2,1)S(1)}, bf16[2,64,128]{2,1,0:T(8,128)(2,1)S(1)}, u32[]{:S(2)}, u32[]{:S(2)}) collective-permute-start(bf16[2,64,128]{2,1,0:T(8,128)(2,1)S(1)} %get-tuple-element.49), channel_id=1, source_target_pairs={{0,5},{1,4},{4,1},{5,0},{8,13},{9,12},{12,9},{13,8},{2,7},{3,6},{6... | collective-permute-start | bytes 98312 | tf_op jit(solution)/shard_map/ppermute | solution.py:235
  122.5 1.6 collective-permute-done.31
  125.2 4.8 %collective-permute-done.32 = bf16[2,64,128]{2,1,0:T(8,128)(2,1)S(1)} collective-permute-done((bf16[2,64,128]{2,1,0:T(8,128)(2,1)S(1)}, bf16[2,64,128]{2,1,0:T(8,128)(2,1)S(1)}, u32[]{:S(2)}, u32[]{:S(2)}) %collective-permute-start.32) | collective-permute-done | bytes 32800 | tf_op jit(solution)/shard_map/ppermute | solution.py:235
  131.5 2.0 %collective-permute-start.33 = (bf16[2,64,128]{2,1,0:T(8,128)(2,1)S(1)}, bf16[2,64,128]{2,1,0:T(8,128)(2,1)S(1)}, u32[]{:S(2)}, u32[]{:S(2)}) collective-permute-start(bf16[2,64,128]{2,1,0:T(8,128)(2,1)S(1)} %add_convert_fusion.1), channel_id=1, source_target_pairs={{0,4},{1,5},{4,0},{5,1},{8,12},{9,13},{12,8},{13,9},{2,6},{3,7},{6... | collective-permute-start | bytes 98312 | tf_op jit(solution)/shard_map/ppermute | solution.py:235
  136.9 6.1 %shard_map.45 = f32[8,64,128]{2,1,0:T(8,128)S(1)} custom-call(s32[8]{0:T(128)S(1)} %fusion.22.at_ref, bf16[8,64,128]{2,1,0:T(8,128)(2,1)S(1)} %pad_maximum_fusion.4.z_ref, bf16[8,64,128]{2,1,0:T(8,128)(2,1)S(1)} %collective-permute-done.36.other_ref, bf16[2048,1024]{1,0:T(8,128)(2,1)S(1)} %get-tuple-element.30.a_ref), custom_call_target="tpu_custom_call" | custom-call | flops 939524096 | bytes 4456448 | tf_op jit(solution)/shard_map/pallas_call | solution.py:218
  143.0 2.6 %collective-permute-start.37 = (bf16[2,64,128]{2,1,0:T(8,128)(2,1)S(1)}, bf16[2,64,128]{2,1,0:T(8,128)(2,1)S(1)}, u32[]{:S(2)}, u32[]{:S(2)}) collective-permute-start(bf16[2,64,128]{2,1,0:T(8,128)(2,1)S(1)} %get-tuple-element.46), channel_id=1, source_target_pairs={{0,5},{1,4},{4,1},{5,0},{8,13},{9,12},{12,9},{13,8},{2,7},{3,6},{6... | collective-permute-start | bytes 98312 | tf_op jit(solution)/shard_map/ppermute | solution.py:235
  147.9 1.6 collective-permute-done.39
  150.6 4.8 %collective-permute-done.40 = bf16[2,64,128]{2,1,0:T(8,128)(2,1)S(1)} collective-permute-done((bf16[2,64,128]{2,1,0:T(8,128)(2,1)S(1)}, bf16[2,64,128]{2,1,0:T(8,128)(2,1)S(1)}, u32[]{:S(2)}, u32[]{:S(2)}) %collective-permute-start.40) | collective-permute-done | bytes 32800 | tf_op jit(solution)/shard_map/ppermute | solution.py:235
  156.9 2.0 %collective-permute-start.41 = (bf16[2,64,128]{2,1,0:T(8,128)(2,1)S(1)}, bf16[2,64,128]{2,1,0:T(8,128)(2,1)S(1)}, u32[]{:S(2)}, u32[]{:S(2)}) collective-permute-start(bf16[2,64,128]{2,1,0:T(8,128)(2,1)S(1)} %add_convert_fusion), channel_id=1, source_target_pairs={{0,4},{1,5},{4,0},{5,1},{8,12},{9,13},{12,8},{13,9},{2,6},{3,7},{6... | collective-permute-start | bytes 98312 | tf_op jit(solution)/shard_map/ppermute | solution.py:235
  162.3 2.2 %copy-done.1 = bf16[2048,1024]{1,0:T(8,128)(2,1)S(1)} copy-done((bf16[2048,1024]{1,0:T(8,128)(2,1)S(1)}, bf16[2048,1024]{1,0:T(8,128)(2,1)}, u32[]{:S(2)}) %copy-start.1) | copy-done | bytes 4194328
  164.5 5.9 %shard_map.46 = f32[64,512]{1,0:T(8,128)} custom-call(s32[8]{0:T(128)S(1)} %fusion.22.at_ref, s32[1]{0:T(128)} %bitcast.core_ref, bf16[8,64,128]{2,1,0:T(8,128)(2,1)S(1)} %pad_maximum_fusion.5.z_ref, bf16[8,64,128]{2,1,0:T(8,128)(2,1)S(1)} %collective-permute-done.44.other_ref, bf16[2048,1024]{1,0:T(8,128)(2,1)S(1)} %copy-done.1), custom_call_target="tpu_custom_call" | custom-call | flops 939524096 | bytes 4456448 | tf_op jit(solution)/shard_map/pallas_call | solution.py:218
  (99 shorter events, 39.5 us)
Async XLA Ops:
  2.1 36.7 %collective-permute-start.3 = (bf16[256,1024]{1,0:T(8,128)(2,1)S(1)}, bf16[256,1024]{1,0:T(8,128)(2,1)S(1)}, u32[]{:S(2)}, u32[]{:S(2)}) collective-permute-start(bf16[256,1024]{1,0:T(8,128)(2,1)S(1)} %get-tuple-element.40), channel_id=1, source_target_pairs={{0,4},{4,0},{8,12},{12,8},{1,5},{5,1},{9,13},{13,9},{2,6},{6,2},{1... | collective-permute-start | bytes 1572872 | tf_op jit(solution)/shard_map/ppermute | solution.py:235
  5.2 33.6 %collective-permute-start.2 = (bf16[256,1024]{1,0:T(8,128)(2,1)S(1)}, bf16[256,1024]{1,0:T(8,128)(2,1)S(1)}, u32[]{:S(2)}, u32[]{:S(2)}) collective-permute-start(bf16[256,1024]{1,0:T(8,128)(2,1)S(1)} %get-tuple-element.42), channel_id=1, source_target_pairs={{0,8},{4,12},{8,0},{12,4},{1,9},{5,13},{9,1},{13,5},{2,10},{6,14},... | collective-permute-start | bytes 1572872 | tf_op jit(solution)/shard_map/ppermute | solution.py:235
  12.4 21.2 %collective-permute-start = (f32[2,64,128]{2,1,0:T(8,128)S(1)}, f32[2,64,128]{2,1,0:T(8,128)S(1)}, u32[]{:S(2)}, u32[]{:S(2)}) collective-permute-start(f32[2,64,128]{2,1,0:T(8,128)S(1)} %bitcast.16), channel_id=1, source_target_pairs={{0,8},{4,12},{8,0},{12,4},{1,9},{5,13},{9,1},{13,5},{2,10},{6,14},... | collective-permute-start | bytes 196616 | tf_op jit(solution)/shard_map/ppermute | solution.py:235
  33.6 5.2 %collective-permute-start.1 = (f32[4,64,128]{2,1,0:T(8,128)S(1)}, f32[4,64,128]{2,1,0:T(8,128)S(1)}, u32[]{:S(2)}, u32[]{:S(2)}) collective-permute-start(f32[4,64,128]{2,1,0:T(8,128)S(1)} %pad_maximum_fusion.2), channel_id=1, source_target_pairs={{0,1},{1,0},{2,3},{3,2},{4,5},{5,4},{6,7},{7,6},{8,9},{9,8},{10,11... | collective-permute-start | bytes 393224 | tf_op jit(solution)/shard_map/ppermute | solution.py:235
  36.2 11.4 %collective-permute-start.5 = (bf16[128,1024]{1,0:T(8,128)(2,1)S(1)}, bf16[128,1024]{1,0:T(8,128)(2,1)S(1)}, u32[]{:S(2)}, u32[]{:S(2)}) collective-permute-start(bf16[128,1024]{1,0:T(8,128)(2,1)S(1)} %get-tuple-element.39), channel_id=1, source_target_pairs={{0,12},{4,8},{8,4},{12,0},{1,13},{5,9},{9,5},{13,1},{2,14},{6,10},... | collective-permute-start | bytes 786440 | tf_op jit(solution)/shard_map/ppermute | solution.py:235
  38.8 8.8 %collective-permute-start.4 = (f32[4,64,128]{2,1,0:T(8,128)S(1)}, f32[4,64,128]{2,1,0:T(8,128)S(1)}, u32[]{:S(2)}, u32[]{:S(2)}) collective-permute-start(f32[4,64,128]{2,1,0:T(8,128)S(1)} %add.217), channel_id=1, source_target_pairs={{0,4},{4,0},{8,12},{12,8},{1,5},{5,1},{9,13},{13,9},{2,6},{6,2},{1... | collective-permute-start | bytes 393224 | tf_op jit(solution)/shard_map/ppermute | solution.py:235
  47.7 10.6 %collective-permute-start.7 = (bf16[128,1024]{1,0:T(8,128)(2,1)S(1)}, bf16[128,1024]{1,0:T(8,128)(2,1)S(1)}, u32[]{:S(2)}, u32[]{:S(2)}) collective-permute-start(bf16[128,1024]{1,0:T(8,128)(2,1)S(1)} %get-tuple-element.38), channel_id=1, source_target_pairs={{0,12},{4,8},{8,4},{12,0},{1,13},{5,9},{9,5},{13,1},{2,14},{6,10},... | collective-permute-start | bytes 786440 | tf_op jit(solution)/shard_map/ppermute | solution.py:235
  50.0 8.9 %collective-permute-start.8 = (bf16[256,1024]{1,0:T(8,128)(2,1)S(1)}, bf16[256,1024]{1,0:T(8,128)(2,1)S(1)}, u32[]{:S(2)}, u32[]{:S(2)}) collective-permute-start(bf16[256,1024]{1,0:T(8,128)(2,1)S(1)} %get-tuple-element.24.refs_0_), channel_id=1, source_target_pairs={{0,2},{2,0},{1,3},{3,1},{4,6},{6,4},{5,7},{7,5},{8,10},{10,8},{9,1... | collective-permute-start | bytes 1572872 | tf_op jit(solution)/shard_map/ppermute | solution.py:235
  50.1 8.8 %collective-permute-start.9 = (bf16[256,1024]{1,0:T(8,128)(2,1)S(1)}, bf16[256,1024]{1,0:T(8,128)(2,1)S(1)}, u32[]{:S(2)}, u32[]{:S(2)}) collective-permute-start(bf16[256,1024]{1,0:T(8,128)(2,1)S(1)} %collective-permute-done.3.refs_1_), channel_id=1, source_target_pairs={{0,2},{2,0},{1,3},{3,1},{4,6},{6,4},{5,7},{7,5},{8,10},{10,8},{9,1... | collective-permute-start | bytes 1572872 | tf_op jit(solution)/shard_map/ppermute | solution.py:235
  50.5 8.5 %collective-permute-start.10 = (bf16[256,1024]{1,0:T(8,128)(2,1)S(1)}, bf16[256,1024]{1,0:T(8,128)(2,1)S(1)}, u32[]{:S(2)}, u32[]{:S(2)}) collective-permute-start(bf16[256,1024]{1,0:T(8,128)(2,1)S(1)} %collective-permute-done.2.refs_2_), channel_id=1, source_target_pairs={{0,2},{2,0},{1,3},{3,1},{4,6},{6,4},{5,7},{7,5},{8,10},{10,8},{9,1... | collective-permute-start | bytes 1572872 | tf_op jit(solution)/shard_map/ppermute | solution.py:235
  62.5 6.8 %collective-permute-start.13 = (f32[2,64,128]{2,1,0:T(8,128)S(1)}, f32[2,64,128]{2,1,0:T(8,128)S(1)}, u32[]{:S(2)}, u32[]{:S(2)}) collective-permute-start(f32[2,64,128]{2,1,0:T(8,128)S(1)} %get-tuple-element.43), channel_id=1, source_target_pairs={{0,5},{1,4},{4,1},{5,0},{8,13},{9,12},{12,9},{13,8},{2,7},{3,6},{6... | collective-permute-start | bytes 196616 | tf_op jit(solution)/shard_map/ppermute | solution.py:235
  66.8 4.3 %collective-permute-start.15 = (f32[2,64,128]{2,1,0:T(8,128)S(1)}, f32[2,64,128]{2,1,0:T(8,128)S(1)}, u32[]{:S(2)}, u32[]{:S(2)}) collective-permute-start(f32[2,64,128]{2,1,0:T(8,128)S(1)} %get-tuple-element.44), channel_id=1, source_target_pairs={{0,1},{1,0},{4,5},{5,4},{8,9},{9,8},{12,13},{13,12},{2,3},{3,2},{6... | collective-permute-start | bytes 196616 | tf_op jit(solution)/shard_map/ppermute | solution.py:235
  68.3 4.3 %collective-permute-start.14 = (f32[2,64,128]{2,1,0:T(8,128)S(1)}, f32[2,64,128]{2,1,0:T(8,128)S(1)}, u32[]{:S(2)}, u32[]{:S(2)}) collective-permute-start(f32[2,64,128]{2,1,0:T(8,128)S(1)} %get-tuple-element.45), channel_id=1, source_target_pairs={{0,4},{1,5},{4,0},{5,1},{8,12},{9,13},{12,8},{13,9},{2,6},{3,7},{6... | collective-permute-start | bytes 196616 | tf_op jit(solution)/shard_map/ppermute | solution.py:235
  72.6 5.4 %collective-permute-start.16 = (f32[2,64,128]{2,1,0:T(8,128)S(1)}, f32[2,64,128]{2,1,0:T(8,128)S(1)}, u32[]{:S(2)}, u32[]{:S(2)}) collective-permute-start(f32[2,64,128]{2,1,0:T(8,128)S(1)} %add_add_fusion), channel_id=1, source_target_pairs={{0,8},{4,12},{8,0},{12,4},{1,9},{5,13},{9,1},{13,5},{2,10},{6,14},... | collective-permute-start | bytes 196616 | tf_op jit(solution)/shard_map/ppermute | solution.py:235
  78.0 5.3 %collective-permute-start.19 = (f32[2,64,128]{2,1,0:T(8,128)S(1)}, f32[2,64,128]{2,1,0:T(8,128)S(1)}, u32[]{:S(2)}, u32[]{:S(2)}) collective-permute-start(f32[2,64,128]{2,1,0:T(8,128)S(1)} %add.225), channel_id=1, source_target_pairs={{0,5},{1,4},{4,1},{5,0},{8,13},{9,12},{12,9},{13,8},{2,7},{3,6},{6... | collective-permute-start | bytes 196616 | tf_op jit(solution)/shard_map/ppermute | solution.py:235
  78.7 5.0 %collective-permute-start.18 = (f32[2,64,128]{2,1,0:T(8,128)S(1)}, f32[2,64,128]{2,1,0:T(8,128)S(1)}, u32[]{:S(2)}, u32[]{:S(2)}) collective-permute-start(f32[2,64,128]{2,1,0:T(8,128)S(1)} %add.225), channel_id=1, source_target_pairs={{0,1},{1,0},{4,5},{5,4},{8,9},{9,8},{12,13},{13,12},{2,3},{3,2},{6... | collective-permute-start | bytes 196616 | tf_op jit(solution)/shard_map/ppermute | solution.py:235
  79.4 4.4 %collective-permute-start.17 = (f32[2,64,128]{2,1,0:T(8,128)S(1)}, f32[2,64,128]{2,1,0:T(8,128)S(1)}, u32[]{:S(2)}, u32[]{:S(2)}) collective-permute-start(f32[2,64,128]{2,1,0:T(8,128)S(1)} %add.225), channel_id=1, source_target_pairs={{0,4},{1,5},{4,0},{5,1},{8,12},{9,13},{12,8},{13,9},{2,6},{3,7},{6... | collective-permute-start | bytes 196616 | tf_op jit(solution)/shard_map/ppermute | solution.py:235
  92.2 4.9 %collective-permute-start.21 = (bf16[2,64,128]{2,1,0:T(8,128)(2,1)S(1)}, bf16[2,64,128]{2,1,0:T(8,128)(2,1)S(1)}, u32[]{:S(2)}, u32[]{:S(2)}) collective-permute-start(bf16[2,64,128]{2,1,0:T(8,128)(2,1)S(1)} %get-tuple-element.52), channel_id=1, source_target_pairs={{0,5},{1,4},{4,1},{5,0},{8,13},{9,12},{12,9},{13,8},{2,7},{3,6},{6... | collective-permute-start | bytes 98312 | tf_op jit(solution)/shard_map/ppermute | solution.py:235
  94.8 3.9 %collective-permute-start.23 = (bf16[2,64,128]{2,1,0:T(8,128)(2,1)S(1)}, bf16[2,64,128]{2,1,0:T(8,128)(2,1)S(1)}, u32[]{:S(2)}, u32[]{:S(2)}) collective-permute-start(bf16[2,64,128]{2,1,0:T(8,128)(2,1)S(1)} %get-tuple-element.53), channel_id=1, source_target_pairs={{0,1},{1,0},{4,5},{5,4},{8,9},{9,8},{12,13},{13,12},{2,3},{3,2},{6... | collective-permute-start | bytes 98312 | tf_op jit(solution)/shard_map/ppermute | solution.py:235
  95.8 3.9 %collective-permute-start.22 = (bf16[2,64,128]{2,1,0:T(8,128)(2,1)S(1)}, bf16[2,64,128]{2,1,0:T(8,128)(2,1)S(1)}, u32[]{:S(2)}, u32[]{:S(2)}) collective-permute-start(bf16[2,64,128]{2,1,0:T(8,128)(2,1)S(1)} %get-tuple-element.54), channel_id=1, source_target_pairs={{0,4},{1,5},{4,0},{5,1},{8,12},{9,13},{12,8},{13,9},{2,6},{3,7},{6... | collective-permute-start | bytes 98312 | tf_op jit(solution)/shard_map/ppermute | solution.py:235
  99.7 4.9 %collective-permute-start.24 = (bf16[2,64,128]{2,1,0:T(8,128)(2,1)S(1)}, bf16[2,64,128]{2,1,0:T(8,128)(2,1)S(1)}, u32[]{:S(2)}, u32[]{:S(2)}) collective-permute-start(bf16[2,64,128]{2,1,0:T(8,128)(2,1)S(1)} %fusion.21), channel_id=1, source_target_pairs={{0,8},{4,12},{8,0},{12,4},{1,9},{5,13},{9,1},{13,5},{2,10},{6,14},... | collective-permute-start | bytes 98312 | tf_op jit(solution)/shard_map/ppermute | solution.py:235
  104.6 5.0 %collective-permute-start.27 = (bf16[2,64,128]{2,1,0:T(8,128)(2,1)S(1)}, bf16[2,64,128]{2,1,0:T(8,128)(2,1)S(1)}, u32[]{:S(2)}, u32[]{:S(2)}) collective-permute-start(bf16[2,64,128]{2,1,0:T(8,128)(2,1)S(1)} %add_convert_fusion.2), channel_id=1, source_target_pairs={{0,5},{1,4},{4,1},{5,0},{8,13},{9,12},{12,9},{13,8},{2,7},{3,6},{6... | collective-permute-start | bytes 98312 | tf_op jit(solution)/shard_map/ppermute | solution.py:235
  105.3 4.3 %collective-permute-start.26 = (bf16[2,64,128]{2,1,0:T(8,128)(2,1)S(1)}, bf16[2,64,128]{2,1,0:T(8,128)(2,1)S(1)}, u32[]{:S(2)}, u32[]{:S(2)}) collective-permute-start(bf16[2,64,128]{2,1,0:T(8,128)(2,1)S(1)} %add_convert_fusion.2), channel_id=1, source_target_pairs={{0,1},{1,0},{4,5},{5,4},{8,9},{9,8},{12,13},{13,12},{2,3},{3,2},{6... | collective-permute-start | bytes 98312 | tf_op jit(solution)/shard_map/ppermute | solution.py:235
  106.1 3.9 %collective-permute-start.25 = (bf16[2,64,128]{2,1,0:T(8,128)(2,1)S(1)}, bf16[2,64,128]{2,1,0:T(8,128)(2,1)S(1)}, u32[]{:S(2)}, u32[]{:S(2)}) collective-permute-start(bf16[2,64,128]{2,1,0:T(8,128)(2,1)S(1)} %add_convert_fusion.2), channel_id=1, source_target_pairs={{0,4},{1,5},{4,0},{5,1},{8,12},{9,13},{12,8},{13,9},{2,6},{3,7},{6... | collective-permute-start | bytes 98312 | tf_op jit(solution)/shard_map/ppermute | solution.py:235
  117.6 4.9 %collective-permute-start.29 = (bf16[2,64,128]{2,1,0:T(8,128)(2,1)S(1)}, bf16[2,64,128]{2,1,0:T(8,128)(2,1)S(1)}, u32[]{:S(2)}, u32[]{:S(2)}) collective-permute-start(bf16[2,64,128]{2,1,0:T(8,128)(2,1)S(1)} %get-tuple-element.49), channel_id=1, source_target_pairs={{0,5},{1,4},{4,1},{5,0},{8,13},{9,12},{12,9},{13,8},{2,7},{3,6},{6... | collective-permute-start | bytes 98312 | tf_op jit(solution)/shard_map/ppermute | solution.py:235
  125.1 4.9 %collective-permute-start.32 = (bf16[2,64,128]{2,1,0:T(8,128)(2,1)S(1)}, bf16[2,64,128]{2,1,0:T(8,128)(2,1)S(1)}, u32[]{:S(2)}, u32[]{:S(2)}) collective-permute-start(bf16[2,64,128]{2,1,0:T(8,128)(2,1)S(1)} %fusion.18), channel_id=1, source_target_pairs={{0,8},{4,12},{8,0},{12,4},{1,9},{5,13},{9,1},{13,5},{2,10},{6,14},... | collective-permute-start | bytes 98312 | tf_op jit(solution)/shard_map/ppermute | solution.py:235
  130.0 5.0 %collective-permute-start.35 = (bf16[2,64,128]{2,1,0:T(8,128)(2,1)S(1)}, bf16[2,64,128]{2,1,0:T(8,128)(2,1)S(1)}, u32[]{:S(2)}, u32[]{:S(2)}) collective-permute-start(bf16[2,64,128]{2,1,0:T(8,128)(2,1)S(1)} %add_convert_fusion.1), channel_id=1, source_target_pairs={{0,5},{1,4},{4,1},{5,0},{8,13},{9,12},{12,9},{13,8},{2,7},{3,6},{6... | collective-permute-start | bytes 98312 | tf_op jit(solution)/shard_map/ppermute | solution.py:235
  130.7 4.3 %collective-permute-start.34 = (bf16[2,64,128]{2,1,0:T(8,128)(2,1)S(1)}, bf16[2,64,128]{2,1,0:T(8,128)(2,1)S(1)}, u32[]{:S(2)}, u32[]{:S(2)}) collective-permute-start(bf16[2,64,128]{2,1,0:T(8,128)(2,1)S(1)} %add_convert_fusion.1), channel_id=1, source_target_pairs={{0,1},{1,0},{4,5},{5,4},{8,9},{9,8},{12,13},{13,12},{2,3},{3,2},{6... | collective-permute-start | bytes 98312 | tf_op jit(solution)/shard_map/ppermute | solution.py:235
  143.0 4.9 %collective-permute-start.37 = (bf16[2,64,128]{2,1,0:T(8,128)(2,1)S(1)}, bf16[2,64,128]{2,1,0:T(8,128)(2,1)S(1)}, u32[]{:S(2)}, u32[]{:S(2)}) collective-permute-start(bf16[2,64,128]{2,1,0:T(8,128)(2,1)S(1)} %get-tuple-element.46), channel_id=1, source_target_pairs={{0,5},{1,4},{4,1},{5,0},{8,13},{9,12},{12,9},{13,8},{2,7},{3,6},{6... | collective-permute-start | bytes 98312 | tf_op jit(solution)/shard_map/ppermute | solution.py:235
  150.5 4.9 %collective-permute-start.40 = (bf16[2,64,128]{2,1,0:T(8,128)(2,1)S(1)}, bf16[2,64,128]{2,1,0:T(8,128)(2,1)S(1)}, u32[]{:S(2)}, u32[]{:S(2)}) collective-permute-start(bf16[2,64,128]{2,1,0:T(8,128)(2,1)S(1)} %fusion.15), channel_id=1, source_target_pairs={{0,8},{4,12},{8,0},{12,4},{1,9},{5,13},{9,1},{13,5},{2,10},{6,14},... | collective-permute-start | bytes 98312 | tf_op jit(solution)/shard_map/ppermute | solution.py:235
  155.4 5.0 %collective-permute-start.43 = (bf16[2,64,128]{2,1,0:T(8,128)(2,1)S(1)}, bf16[2,64,128]{2,1,0:T(8,128)(2,1)S(1)}, u32[]{:S(2)}, u32[]{:S(2)}) collective-permute-start(bf16[2,64,128]{2,1,0:T(8,128)(2,1)S(1)} %add_convert_fusion), channel_id=1, source_target_pairs={{0,5},{1,4},{4,1},{5,0},{8,13},{9,12},{12,9},{13,8},{2,7},{3,6},{6... | collective-permute-start | bytes 98312 | tf_op jit(solution)/shard_map/ppermute | solution.py:235
  156.1 4.3 %collective-permute-start.42 = (bf16[2,64,128]{2,1,0:T(8,128)(2,1)S(1)}, bf16[2,64,128]{2,1,0:T(8,128)(2,1)S(1)}, u32[]{:S(2)}, u32[]{:S(2)}) collective-permute-start(bf16[2,64,128]{2,1,0:T(8,128)(2,1)S(1)} %add_convert_fusion), channel_id=1, source_target_pairs={{0,1},{1,0},{4,5},{5,4},{8,9},{9,8},{12,13},{13,12},{2,3},{3,2},{6... | collective-permute-start | bytes 98312 | tf_op jit(solution)/shard_map/ppermute | solution.py:235
  (15 other events, 112.4 us)

commit v16 on v15

--- a/solution.py
+++ b/solution.py
@@ -181,7 +181,7 @@
 
 def forth_product(weights, a_ref, at_ref, part_ref):
     chunks, unused, width = part_ref.shape
-    forth = dot_nt(weights.astype(jnp.bfloat16), a_ref[: chunks * width, :])
+    forth = dot_nt(weights.astype(jnp.bfloat16), a_ref[...])
     for i in range(chunks):
         part_ref[at_ref[i]] = forth[:, width * i : width * (i + 1)]
 
@@ -202,15 +202,15 @@
     forth_product(dot_nn(basis_ref[...], a_ref[...]), a_ref, at_ref, part_ref)
 
 
-def orth_power_kernel(at_ref, z_ref, other_ref, a_ref, part_ref):
-    weights = back_product(at_ref, (z_ref, other_ref), a_ref[...])
+def orth_power_kernel(at_ref, z_ref, a_ref, part_ref):
+    weights = back_product(at_ref, (z_ref,), a_ref[...])
     forth_product(weights, a_ref, at_ref, part_ref)
 
 
-def last_kernel(at_ref, core_ref, z_ref, other_ref, a_ref, out_ref):
+def last_kernel(at_ref, core_ref, z_ref, a_ref, out_ref):
     cols = out_ref.shape[1]
     start = pl.multiple_of(core_ref[0] * cols, cols)
-    out_ref[...] = back_product(at_ref, (z_ref, other_ref), a_ref[:, pl.ds(start, cols)])
+    out_ref[...] = back_product(at_ref, (z_ref,), a_ref[:, pl.ds(start, cols)])
 
 
 def call(kernel, out_shapes, flops, scalars, *operands):
@@ -235,45 +235,57 @@
     return lax.ppermute(value, axis, [(i, i ^ offset) for i in range(size)])
 
 
-def square_devices():
-    n_z, n_col = lax.axis_size("z"), lax.axis_size("col")
-    sides = [(z, col) for z in range(2 if n_z > 2 else 1) for col in range(n_col)]
-    return [(z * n_col + col, col * (2 if n_z > 2 else 1) + z) for z, col in sides[:0:-1]]
+def from_chip(value, z_offset, col_offset):
+    n_z, n_core, n_col = lax.axis_size("z"), lax.axis_size("core"), lax.axis_size("col")
+
+    def device(z, col):
+        return (z * n_core + 1) * n_col + col
+
+    pairs = [
+        (device(z, col), device(z ^ z_offset, col ^ col_offset))
+        for z in range(n_z)
+        for col in range(n_col)
+    ]
+    return lax.ppermute(value, ("z", "core", "col"), pairs)
+
+
+def square_chips():
+    near = 2 if lax.axis_size("z") > 2 else 1
+    sides = [(z, col) for z in range(near) for col in range(lax.axis_size("col"))]
+    return [((z, col), col * near + z) for z, col in sides[:0:-1]]
 
 
 def sum_parts(total, dtype):
-    offsets = square_devices()
-    step = total.shape[0] // (len(offsets) + 1)
+    chips = square_chips()
+    step = total.shape[0] // (len(chips) + 1)
     others = [
-        from_xor(total[step * place : step * (place + 1)].astype(dtype), ("z", "col"), offset)
-        for offset, place in offsets
+        from_chip(total[step * place : step * (place + 1)].astype(dtype), *offsets)
+        for offsets, place in chips
     ]
     total = functools.reduce(jnp.add, [x.astype(jnp.float32) for x in others], total[:step])
     for bit in far_bits():
         mine = total.astype(dtype)
-        total = mine.astype(jnp.float32) + from_xor(mine, ("z",), bit).astype(jnp.float32)
+        total = mine.astype(jnp.float32) + from_chip(mine, bit, 0).astype(jnp.float32)
     return total.astype(dtype)
 
 
 def gather_parts(own):
     placed = {0: own}
-    for offset, place in square_devices():
-        placed[place] = from_xor(own, ("z", "col"), offset)
-    own = jnp.concatenate([placed[place] for place in sorted(placed)])
-    return own, from_xor(own, ("core",), 1)
+    for offsets, place in square_chips():
+        placed[place] = from_chip(own, *offsets)
+    return jnp.concatenate([placed[place] for place in sorted(placed)])
 
 
 def far_bits():
     return bits(lax.axis_size("z"))[1 if lax.axis_size("z") > 2 else 0 :]
 
 
-def chunk_places(digits):
+def chunk_places(digits, halves):
     n_z, n_col = lax.axis_size("z"), lax.axis_size("col")
-    index = jnp.arange(n_z * n_col, dtype=jnp.int32)
-    z_at, col_at = lax.axis_index("z"), lax.axis_index("col")
-    column = index % n_col
-    relative = {"z": index // n_col, "col": column ^ col_at}
-    absolute = {"z": relative["z"] ^ z_at, "col": column}
+    index = jnp.arange(halves * n_z * n_col, dtype=jnp.int32)
+    relative = {"core": index // (n_col * n_z), "z": index // n_col % n_z, "col": index % n_col}
+    absolute = {name: value ^ lax.axis_index(name) for name, value in relative.items()}
+    relative["col"], absolute["col"] = absolute["col"], relative["col"]
     place = jnp.zeros_like(index)
     for axis, bit, is_relative in digits:
         place = place * 2 + ((relative if is_relative else absolute)[axis] // bit) % 2
@@ -287,7 +299,7 @@
     rows_total, width_total = rows_local * n_row, width_local * n_col
     chunk = rows_local // n_col
     cols = width_local // n_z
-    chunks = n_z * n_col
+    chunks = n_row * n_col
     z_at, col = lax.axis_index("z"), lax.axis_index("col")
     pieces = {}
 
@@ -326,10 +338,11 @@
     z = hold(z, [(offset, 0) for offset in range(far + 1, n_z)])
     z = z, from_xor(z, ("core",), 1)
     absolute_col = [("col", bit, False) for bit in bits(n_col)[::-1]]
-    at_first = chunk_places([("z", bit, True) for bit in z_bits[::-1]] + absolute_col)
+    at_first = chunk_places([("z", bit, True) for bit in z_bits[::-1]] + absolute_col, 1)
     digits = [("col", bit, True) for bit in bits(n_col)[::-1]]
     digits += [("z", 1, True)] if n_z > 2 else []
-    at = chunk_places(digits + [("z", bit, False) for bit in far_bits()])
+    digits += [("core", 1, False)] + [("z", bit, False) for bit in far_bits()]
+    at = chunk_places(digits, 2)
     late = [name for name in pieces if name[0] > far]
     others = {name: from_xor(pieces[name], ("core",), 1) for name in first}
 
@@ -350,10 +363,12 @@
     a, total = call(power_kernel, (slab, parts), flops, (at,), basis, *blocks)
     z = gather_parts(sum_parts(total, f32))
     for step in range(POWER - 1):
-        total = call(orth_power_kernel, parts, flops, (at,), *z, a)
+        total = call(orth_power_kernel, parts, flops, (at,), z, a)
         z = gather_parts(sum_parts(total, jnp.bfloat16))
-    core = lax.axis_index("core")[None].astype(jnp.int32)
-    return call(last_kernel, loadings, flops, (at, core), *z, a).T, factor
+    core = lax.axis_index("core")
+    z = jnp.where(core == 1, z, lax.ppermute(z, "core", [(1, 0)]))
+    at_core = core[None].astype(jnp.int32)
+    return call(last_kernel, loadings, flops, (at, at_core), z, a).T, factor
 
 
 def local_gram(basis):

time: 171 us -> 217 us (1.27)
  waiting for transfers between devices: 81.1 us -> 130 us
  starting transfers between devices: 45 us -> 36.5 us
  Pallas kernels: 32.8 us -> 35.6 us
    ppermute x0 -> x29, waiting for transfers between devices: none -> 99.9 us  [the longest x1 99.8 us: per_device_transposed(): z = jnp.where(core == 1, z, lax.ppermute(z, 'core', [(1, 0)]))]
    ppermute x45 -> x13, waiting for transfers between devices: 81.1 us -> 30.2 us  [from_xor(): return lax.ppermute(value, axis, [(i, i ^ offset) for i in range(size)])]
    ppermute x45 -> x13, starting transfers between devices: 45 us -> 16.1 us  [from_xor(): return lax.ppermute(value, axis, [(i, i ^ offset) for i in range(size)])]
    ppermute x0 -> x29, starting transfers between devices: none -> 20.3 us  [the longest x28 19 us: from_chip(): return lax.ppermute(value, ('z', 'core', 'col'), pairs)]
    pallas_call x6, Pallas kernels: 32.8 us -> 35.6 us  [call(): pl.pallas_call(kernel, out_shape=out_shapes, in_specs=[pl.BlockSpec(memor...]
    unnamed x5 -> x9, local copies, waits for them, and re-layouts: 2.89 us -> 4.52 us
  transfers between devices with their start and end apart: 45 -> 42, of which waited for: 34 -> 5; matrix products, arithmetic and copies ran while one was open for 3% -> 3% of each run, Pallas kernels for 4% -> 3%
where the time goes in v16:
time: 217 us; the launch traced here: 216 us
  waiting for transfers between devices  130 us (60%)
  starting transfers between devices  36.5 us (17%)
  Pallas kernels  35.6 us (16%)
  local copies, waits for them, and re-layouts  7.19 us (3%)
  matrix products  3.83 us (2%)
    ppermute x1, waiting for transfers between devices, per_device_transposed(): z = jnp.where(core == 1, z, lax.ppermute(z, 'core', [(1, 0)]))  99.8 us
    pallas_call x6, Pallas kernels, call(): pl.pallas_call(kernel, out_shape=out_shapes, in_specs=[pl.BlockSpec(memor...  35.6 us
    ppermute x13, waiting for transfers between devices, from_xor(): return lax.ppermute(value, axis, [(i, i ^ offset) for i in range(size)])  30.2 us
    ppermute x28, starting transfers between devices, from_chip(): return lax.ppermute(value, ('z', 'core', 'col'), pairs)  19 us
    ppermute x13, starting transfers between devices, from_xor(): return lax.ppermute(value, axis, [(i, i ^ offset) for i in range(size)])  16.1 us
    unnamed x9, local copies, waits for them, and re-layouts  4.52 us
  transfers between devices with their start and end apart: 42, of which 5 were waited for; matrix products, arithmetic and copies ran while one was open for 3% of the time, Pallas kernels for 3%

profile of v16, /device:TPU:0, one launch (start us, length us, event | category | flops | bytes accessed | tf_op | source)
XLA Modules:
  0.0 215.9 jit_solution(3276374607372226703)
XLA Ops:
  0.6 1.5 constant_dynamic-slice_fusion.1
  2.1 4.1 %collective-permute-start.2 = (bf16[256,1024]{1,0:T(8,128)(2,1)S(1)}, bf16[256,1024]{1,0:T(8,128)(2,1)S(1)}, u32[]{:S(2)}, u32[]{:S(2)}) collective-permute-start(bf16[256,1024]{1,0:T(8,128)(2,1)S(1)} %get-tuple-element.42), channel_id=1, source_target_pairs={{0,8},{4,12},{8,0},{12,4},{1,9},{5,13},{9,1},{13,5},{2,10},{6,14},... | collective-permute-start | bytes 1572872 | tf_op jit(solution)/shard_map/ppermute | solution.py:235
  6.2 1.6 collective-permute-start.3
  8.5 3.8 %convolution_bitcast_fusion = f32[8,2,8,128]{3,2,1,0:T(8,128)S(1)} fusion(bf16[256,4096]{1,0:T(8,128)(2,1)} %param.3, s32[]{:T(128)S(6)} %xor.81, s32[4096]{0:T(1024)S(1)} %add_multiply_fusion), kind=kOutput, calls=%fused_computation | convolution fusion | flops 152043520 | bytes 2179076 | tf_op jit(solution)/shard_map/dot_general | solution.py:319
  12.8 19.5 %collective-permute-done = f32[2,64,128]{2,1,0:T(8,128)S(1)} collective-permute-done((f32[2,64,128]{2,1,0:T(8,128)S(1)}, f32[2,64,128]{2,1,0:T(8,128)S(1)}, u32[]{:S(2)}, u32[]{:S(2)}) %collective-permute-start) | collective-permute-done | bytes 65568 | tf_op jit(solution)/shard_map/ppermute | solution.py:235
  32.3 1.6 collective-permute-start.1
  33.9 1.1 constant_dynamic-slice_fusion.4
  34.9 3.5 %collective-permute-start.5 = (bf16[128,1024]{1,0:T(8,128)(2,1)S(1)}, bf16[128,1024]{1,0:T(8,128)(2,1)S(1)}, u32[]{:S(2)}, u32[]{:S(2)}) collective-permute-start(bf16[128,1024]{1,0:T(8,128)(2,1)S(1)} %get-tuple-element.39), channel_id=1, source_target_pairs={{0,12},{4,8},{8,4},{12,0},{1,13},{5,9},{9,5},{13,1},{2,14},{6,10},... | collective-permute-start | bytes 786440 | tf_op jit(solution)/shard_map/ppermute | solution.py:235
  38.6 9.0 %collective-permute-done.4 = f32[4,64,128]{2,1,0:T(8,128)S(1)} collective-permute-done((f32[4,64,128]{2,1,0:T(8,128)S(1)}, f32[4,64,128]{2,1,0:T(8,128)S(1)}, u32[]{:S(2)}, u32[]{:S(2)}) %collective-permute-start.4) | collective-permute-done | bytes 131104 | tf_op jit(solution)/shard_map/ppermute | solution.py:235
  47.7 3.6 %collective-permute-start.7 = (bf16[128,1024]{1,0:T(8,128)(2,1)S(1)}, bf16[128,1024]{1,0:T(8,128)(2,1)}, u32[]{:S(2)}, u32[]{:S(2)}) collective-permute-start(bf16[128,1024]{1,0:T(8,128)(2,1)S(1)} %get-tuple-element.38), channel_id=1, source_target_pairs={{0,12},{4,8},{8,4},{12,0},{1,13},{5,9},{9,5},{13,1},{2,14},{6,10},... | collective-permute-start | bytes 786440 | tf_op jit(solution)/shard_map/ppermute | solution.py:235
  52.0 6.0 %shard_map.41 = (bf16[64,2048]{1,0:T(8,128)(2,1)S(1)}, f32[64,64]{1,0:T(8,128)S(1)}) custom-call(s32[8]{0:T(128)S(1)} %fusion.26.at_ref, f32[8,64,128]{2,1,0:T(8,128)S(1)} %pad_maximum_fusion.1.z_ref, f32[8,64,128]{2,1,0:T(8,128)S(1)} %collective-permute-done.6.other_ref), custom_call_target="tpu_custom_call" | custom-call | flops 402653184 | bytes 524288 | tf_op jit(solution)/shard_map/pallas_call | solution.py:218
  58.0 0.7 copy-done.2
  59.3 1.1 collective-permute-done.11.refs_8_
  61.0 0.9 copy-done.3
  61.9 3.4 %shard_map.42 = (bf16[2048,1024]{1,0:T(8,128)(2,1)S(1)}, f32[16,64,128]{2,1,0:T(8,128)S(1)}) custom-call(s32[16]{0:T(128)S(1)} %fusion.24.at_ref, bf16[64,2048]{1,0:T(8,128)(2,1)S(1)} %copy-done.3, bf16[256,1024]{1,0:T(8,128)(2,1)S(1)} %get-tuple-element.24.refs_0_, bf16[256,1024]{1,0:T(8,128)(2,1)S(1)} %collective-permute-done.3.refs_1_, ...), custom_call_target="tpu_custom_call" | custom-call | flops 939524096 | bytes 4456448 | tf_op jit(solution)/shard_map/pallas_call | solution.py:218
  65.3 0.7 collective-permute-start.13
  66.0 0.7 collective-permute-start.14
  66.7 0.7 collective-permute-start.15
  67.4 0.7 collective-permute-start.16
  68.1 0.7 collective-permute-start.17
  68.8 0.7 collective-permute-start.18
  69.5 0.8 collective-permute-start.19
  70.4 7.1 %shard_map.43 = f32[16,64,128]{2,1,0:T(8,128)S(1)} custom-call(s32[16]{0:T(128)S(1)} %fusion.24.at_ref, f32[16,64,128]{2,1,0:T(8,128)S(1)} %pad_maximum_fusion.z_ref, bf16[2048,1024]{1,0:T(8,128)(2,1)S(1)} %get-tuple-element.30.a_ref), custom_call_target="tpu_custom_call" | custom-call | flops 939524096 | bytes 4718592 | tf_op jit(solution)/shard_map/pallas_call | solution.py:218
  77.6 0.7 collective-permute-start.20
  82.5 6.6 %shard_map.44 = f32[16,64,128]{2,1,0:T(8,128)S(1)} custom-call(s32[16]{0:T(128)S(1)} %fusion.24.at_ref, bf16[16,64,128]{2,1,0:T(8,128)(2,1)S(1)} %pad_maximum_fusion.2.z_ref, bf16[2048,1024]{1,0:T(8,128)(2,1)S(1)} %get-tuple-element.30.a_ref), custom_call_target="tpu_custom_call" | custom-call | flops 939524096 | bytes 4456448 | tf_op jit(solution)/shard_map/pallas_call | solution.py:218
  93.4 0.9 collective-permute-start.33
  94.4 6.6 %shard_map.45 = f32[16,64,128]{2,1,0:T(8,128)S(1)} custom-call(s32[16]{0:T(128)S(1)} %fusion.24.at_ref, bf16[16,64,128]{2,1,0:T(8,128)(2,1)S(1)} %pad_maximum_fusion.3.z_ref, bf16[2048,1024]{1,0:T(8,128)(2,1)S(1)} %get-tuple-element.30.a_ref), custom_call_target="tpu_custom_call" | custom-call | flops 939524096 | bytes 4456448 | tf_op jit(solution)/shard_map/pallas_call | solution.py:218
  106.0 1.3 collective-permute-start.41
  107.3 0.7 copy.8
  108.0 99.8 %collective-permute-done.41 = bf16[16,64,128]{2,1,0:T(8,128)(2,1)S(1)} collective-permute-done((bf16[16,64,128]{2,1,0:T(8,128)(2,1)S(1)}, bf16[16,64,128]{2,1,0:T(8,128)(2,1)S(1)}, u32[]{:S(2)}, u32[]{:S(2)}) %collective-permute-start.41) | collective-permute-done | bytes 262176 | tf_op jit(solution)/shard_map/ppermute | solution.py:369
  207.9 2.2 %copy-done.1 = bf16[2048,1024]{1,0:T(8,128)(2,1)S(1)} copy-done((bf16[2048,1024]{1,0:T(8,128)(2,1)S(1)}, bf16[2048,1024]{1,0:T(8,128)(2,1)}, u32[]{:S(2)}) %copy-start.1) | copy-done | bytes 4194328
  210.1 5.8 %shard_map.46 = f32[64,512]{1,0:T(8,128)} custom-call(s32[16]{0:T(128)S(1)} %fusion.24.at_ref, s32[1]{0:T(128)} %bitcast.core_ref, bf16[16,64,128]{2,1,0:T(8,128)(2,1)S(1)} %broadcast_select_fusion.z_ref, bf16[2048,1024]{1,0:T(8,128)(2,1)S(1)} %copy-done.1), custom_call_target="tpu_custom_call" | custom-call | flops 939524096 | bytes 4456448 | tf_op jit(solution)/shard_map/pallas_call | solution.py:218
  (98 shorter events, 15.8 us)
Async XLA Ops:
  2.1 36.3 %collective-permute-start.2 = (bf16[256,1024]{1,0:T(8,128)(2,1)S(1)}, bf16[256,1024]{1,0:T(8,128)(2,1)S(1)}, u32[]{:S(2)}, u32[]{:S(2)}) collective-permute-start(bf16[256,1024]{1,0:T(8,128)(2,1)S(1)} %get-tuple-element.42), channel_id=1, source_target_pairs={{0,8},{4,12},{8,0},{12,4},{1,9},{5,13},{9,1},{13,5},{2,10},{6,14},... | collective-permute-start | bytes 1572872 | tf_op jit(solution)/shard_map/ppermute | solution.py:235
  6.2 32.2 %collective-permute-start.3 = (bf16[256,1024]{1,0:T(8,128)(2,1)S(1)}, bf16[256,1024]{1,0:T(8,128)(2,1)S(1)}, u32[]{:S(2)}, u32[]{:S(2)}) collective-permute-start(bf16[256,1024]{1,0:T(8,128)(2,1)S(1)} %get-tuple-element.40), channel_id=1, source_target_pairs={{0,4},{4,0},{8,12},{12,8},{1,5},{5,1},{9,13},{13,9},{2,6},{6,2},{1... | collective-permute-start | bytes 1572872 | tf_op jit(solution)/shard_map/ppermute | solution.py:235
  12.4 19.9 %collective-permute-start = (f32[2,64,128]{2,1,0:T(8,128)S(1)}, f32[2,64,128]{2,1,0:T(8,128)S(1)}, u32[]{:S(2)}, u32[]{:S(2)}) collective-permute-start(f32[2,64,128]{2,1,0:T(8,128)S(1)} %bitcast.16), channel_id=1, source_target_pairs={{0,8},{4,12},{8,0},{12,4},{1,9},{5,13},{9,1},{13,5},{2,10},{6,14},... | collective-permute-start | bytes 196616 | tf_op jit(solution)/shard_map/ppermute | solution.py:235
  32.3 6.2 %collective-permute-start.1 = (f32[4,64,128]{2,1,0:T(8,128)S(1)}, f32[4,64,128]{2,1,0:T(8,128)S(1)}, u32[]{:S(2)}, u32[]{:S(2)}) collective-permute-start(f32[4,64,128]{2,1,0:T(8,128)S(1)} %pad_maximum_fusion.5), channel_id=1, source_target_pairs={{0,1},{1,0},{2,3},{3,2},{4,5},{5,4},{6,7},{7,6},{8,9},{9,8},{10,11... | collective-permute-start | bytes 393224 | tf_op jit(solution)/shard_map/ppermute | solution.py:235
  34.9 12.7 %collective-permute-start.5 = (bf16[128,1024]{1,0:T(8,128)(2,1)S(1)}, bf16[128,1024]{1,0:T(8,128)(2,1)S(1)}, u32[]{:S(2)}, u32[]{:S(2)}) collective-permute-start(bf16[128,1024]{1,0:T(8,128)(2,1)S(1)} %get-tuple-element.39), channel_id=1, source_target_pairs={{0,12},{4,8},{8,4},{12,0},{1,13},{5,9},{9,5},{13,1},{2,14},{6,10},... | collective-permute-start | bytes 786440 | tf_op jit(solution)/shard_map/ppermute | solution.py:235
  38.5 9.1 %collective-permute-start.4 = (f32[4,64,128]{2,1,0:T(8,128)S(1)}, f32[4,64,128]{2,1,0:T(8,128)S(1)}, u32[]{:S(2)}, u32[]{:S(2)}) collective-permute-start(f32[4,64,128]{2,1,0:T(8,128)S(1)} %add.246), channel_id=1, source_target_pairs={{0,4},{4,0},{8,12},{12,8},{1,5},{5,1},{9,13},{13,9},{2,6},{6,2},{1... | collective-permute-start | bytes 393224 | tf_op jit(solution)/shard_map/ppermute | solution.py:235
  47.6 4.4 %collective-permute-start.6 = (f32[8,64,128]{2,1,0:T(8,128)S(1)}, f32[8,64,128]{2,1,0:T(8,128)S(1)}, u32[]{:S(2)}, u32[]{:S(2)}) collective-permute-start(f32[8,64,128]{2,1,0:T(8,128)S(1)} %pad_maximum_fusion.1.z_ref), channel_id=1, source_target_pairs={{0,2},{2,0},{1,3},{3,1},{4,6},{6,4},{5,7},{7,5},{8,10},{10,8},{9,1... | collective-permute-start | bytes 786440 | tf_op jit(solution)/shard_map/ppermute | solution.py:235
  47.7 11.0 %collective-permute-start.7 = (bf16[128,1024]{1,0:T(8,128)(2,1)S(1)}, bf16[128,1024]{1,0:T(8,128)(2,1)}, u32[]{:S(2)}, u32[]{:S(2)}) collective-permute-start(bf16[128,1024]{1,0:T(8,128)(2,1)S(1)} %get-tuple-element.38), channel_id=1, source_target_pairs={{0,12},{4,8},{8,4},{12,0},{1,13},{5,9},{9,5},{13,1},{2,14},{6,10},... | collective-permute-start | bytes 786440 | tf_op jit(solution)/shard_map/ppermute | solution.py:235
  51.3 8.0 %collective-permute-start.10 = (bf16[256,1024]{1,0:T(8,128)(2,1)S(1)}, bf16[256,1024]{1,0:T(8,128)(2,1)S(1)}, u32[]{:S(2)}, u32[]{:S(2)}) collective-permute-start(bf16[256,1024]{1,0:T(8,128)(2,1)S(1)} %collective-permute-done.2.refs_2_), channel_id=1, source_target_pairs={{0,2},{2,0},{1,3},{3,1},{4,6},{6,4},{5,7},{7,5},{8,10},{10,8},{9,1... | collective-permute-start | bytes 1572872 | tf_op jit(solution)/shard_map/ppermute | solution.py:235
  51.4 7.8 %collective-permute-start.8 = (bf16[256,1024]{1,0:T(8,128)(2,1)S(1)}, bf16[256,1024]{1,0:T(8,128)(2,1)S(1)}, u32[]{:S(2)}, u32[]{:S(2)}) collective-permute-start(bf16[256,1024]{1,0:T(8,128)(2,1)S(1)} %get-tuple-element.24.refs_0_), channel_id=1, source_target_pairs={{0,2},{2,0},{1,3},{3,1},{4,6},{6,4},{5,7},{7,5},{8,10},{10,8},{9,1... | collective-permute-start | bytes 1572872 | tf_op jit(solution)/shard_map/ppermute | solution.py:235
  51.8 7.5 %collective-permute-start.9 = (bf16[256,1024]{1,0:T(8,128)(2,1)S(1)}, bf16[256,1024]{1,0:T(8,128)(2,1)S(1)}, u32[]{:S(2)}, u32[]{:S(2)}) collective-permute-start(bf16[256,1024]{1,0:T(8,128)(2,1)S(1)} %collective-permute-done.3.refs_1_), channel_id=1, source_target_pairs={{0,2},{2,0},{1,3},{3,1},{4,6},{6,4},{5,7},{7,5},{8,10},{10,8},{9,1... | collective-permute-start | bytes 1572872 | tf_op jit(solution)/shard_map/ppermute | solution.py:235
  58.7 1.7 collective-permute-start.11
  59.0 1.9 collective-permute-start.12
  65.3 2.0 collective-permute-start.13
  66.0 1.4 collective-permute-start.14
  68.1 2.2 %collective-permute-start.17 = (f32[4,64,128]{2,1,0:T(8,128)S(1)}, f32[4,64,128]{2,1,0:T(8,128)S(1)}, u32[]{:S(2)}, u32[]{:S(2)}) collective-permute-start(f32[4,64,128]{2,1,0:T(8,128)S(1)} %add.254), channel_id=1, source_target_pairs={{2,6},{3,7},{6,2},{7,3},{10,14},{11,15},{14,10},{15,11},{18,22},{1... | collective-permute-start | bytes 393224 | tf_op jit(solution)/shard_map/ppermute | solution.py:249
  68.8 1.5 collective-permute-start.18
  69.5 0.9 collective-permute-start.19
  77.6 2.0 collective-permute-start.20
  78.3 1.4 collective-permute-start.21
  80.4 2.0 collective-permute-start.24
  81.1 1.4 collective-permute-start.25
  89.2 2.0 collective-permute-start.27
  89.9 1.4 collective-permute-start.28
  92.0 2.2 %collective-permute-start.31 = (bf16[4,64,128]{2,1,0:T(8,128)(2,1)S(1)}, bf16[4,64,128]{2,1,0:T(8,128)(2,1)S(1)}, u32[]{:S(2)}, u32[]{:S(2)}) collective-permute-start(bf16[4,64,128]{2,1,0:T(8,128)(2,1)S(1)} %add_convert_fusion.1), channel_id=1, source_target_pairs={{2,6},{3,7},{6,2},{7,3},{10,14},{11,15},{14,10},{15,11},{18,22},{1... | collective-permute-start | bytes 196616 | tf_op jit(solution)/shard_map/ppermute | solution.py:249
  92.7 1.6 collective-permute-start.32
  93.4 0.9 collective-permute-start.33
  101.1 2.0 collective-permute-start.34
  101.8 1.4 collective-permute-start.35
  103.9 2.0 collective-permute-start.38
  104.6 1.4 collective-permute-start.39
  106.0 101.8 %collective-permute-start.41 = (bf16[16,64,128]{2,1,0:T(8,128)(2,1)S(1)}, bf16[16,64,128]{2,1,0:T(8,128)(2,1)S(1)}, u32[]{:S(2)}, u32[]{:S(2)}) collective-permute-start(bf16[16,64,128]{2,1,0:T(8,128)(2,1)S(1)} %pad_maximum_fusion.4), channel_id=1, source_target_pairs={{2,0},{3,1},{6,4},{7,5},{10,8},{11,9},{14,12},{15,13},{18,16},{19,... | collective-permute-start | bytes 786440 | tf_op jit(solution)/shard_map/ppermute | solution.py:369
  (14 other events, 39.8 us)

commit v17 on v15

--- a/solution.py
+++ b/solution.py
@@ -153,7 +153,8 @@
 
 
 def wide_of(at_ref, z_refs):
-    chunks = [z_ref[at_ref[i]] for z_ref in z_refs for i in range(at_ref.shape[0])]
+    half = at_ref.shape[0] // len(z_refs)
+    chunks = [z_ref[at_ref[half * s + i]] for s, z_ref in enumerate(z_refs) for i in range(half)]
     return jnp.concatenate(chunks, axis=1)
 
 
@@ -236,17 +237,30 @@
 
 
 def square_devices():
-    n_z, n_col = lax.axis_size("z"), lax.axis_size("col")
-    sides = [(z, col) for z in range(2 if n_z > 2 else 1) for col in range(n_col)]
-    return [(z * n_col + col, col * (2 if n_z > 2 else 1) + z) for z, col in sides[:0:-1]]
+    near = 2 if lax.axis_size("z") > 2 else 1
+    by_z = [(z, col) for z in range(near) for col in range(lax.axis_size("col"))]
+    by_col = [(z, col) for col in range(lax.axis_size("col")) for z in range(near)]
+    return by_z, by_col if near == lax.axis_size("col") else by_z
+
+
+def from_square(value, place):
+    n_z, n_core, n_col = lax.axis_size("z"), lax.axis_size("core"), lax.axis_size("col")
+    pairs = []
+    for core, offsets in enumerate(square_devices()):
+        z_offset, col_offset = offsets[place]
+        for z in range(n_z):
+            for col in range(n_col):
+                target = ((z ^ z_offset) * n_core + core) * n_col + (col ^ col_offset)
+                pairs.append(((z * n_core + core) * n_col + col, target))
+    return lax.ppermute(value, ("z", "core", "col"), pairs)
 
 
 def sum_parts(total, dtype):
-    offsets = square_devices()
-    step = total.shape[0] // (len(offsets) + 1)
+    places = len(square_devices()[0])
+    step = total.shape[0] // places
     others = [
-        from_xor(total[step * place : step * (place + 1)].astype(dtype), ("z", "col"), offset)
-        for offset, place in offsets
+        from_square(total[step * place : step * (place + 1)].astype(dtype), place)
+        for place in range(1, places)
     ]
     total = functools.reduce(jnp.add, [x.astype(jnp.float32) for x in others], total[:step])
     for bit in far_bits():
@@ -256,10 +270,8 @@
 
 
 def gather_parts(own):
-    placed = {0: own}
-    for offset, place in square_devices():
-        placed[place] = from_xor(own, ("z", "col"), offset)
-    own = jnp.concatenate([placed[place] for place in sorted(placed)])
+    others = [from_square(own, place) for place in range(1, len(square_devices()[0]))]
+    own = jnp.concatenate([own] + others)
     return own, from_xor(own, ("core",), 1)
 
 
@@ -310,7 +322,9 @@
     z = z.reshape(RANK, n_col, chunk).transpose(1, 0, 2)
     z_bits = bits(n_z)[::-1]
     far = z_bits[0]
-    for offset in [0, far, *range(1, far)]:
+    move(states, far)
+    move(states, 0)
+    for offset in range(1, far):
         move(states, offset)
     first = list(pieces)
     z = jnp.concatenate([z, from_xor(z, ("z",), far)])
@@ -318,18 +332,25 @@
     for offset in range(far + 1, n_z):
         move(slab, offset, 0, 2)
         move(slab, offset, 1, 2)
+    z = hold(z, [(far, 0)])
     for bit in bits(n_col):
         z = z + from_xor(z, ("col",), bit)
-    z = hold(z, first)
+    z = hold(z, [(offset, 0) for offset in range(1, far)])
     for bit in z_bits[1:]:
         z = jnp.concatenate([z, from_xor(z, ("z",), bit)])
     z = hold(z, [(offset, 0) for offset in range(far + 1, n_z)])
     z = z, from_xor(z, ("core",), 1)
     absolute_col = [("col", bit, False) for bit in bits(n_col)[::-1]]
     at_first = chunk_places([("z", bit, True) for bit in z_bits[::-1]] + absolute_col)
-    digits = [("col", bit, True) for bit in bits(n_col)[::-1]]
-    digits += [("z", 1, True)] if n_z > 2 else []
-    at = chunk_places(digits + [("z", bit, False) for bit in far_bits()])
+    far_digits = [("z", bit, False) for bit in far_bits()]
+    col_digits = [("col", bit, True) for bit in bits(n_col)[::-1]]
+    near_digit = [("z", 1, True)] if n_z > 2 else []
+    by_z, by_col = square_devices()
+    at_0 = chunk_places(near_digit + col_digits + far_digits)
+    at_1 = at_0 if by_z == by_col else chunk_places(col_digits + near_digit + far_digits)
+    core = lax.axis_index("core")
+    at_first = jnp.concatenate([at_first, at_first])
+    at = jnp.concatenate([jnp.where(core == 0, at_0, at_1), jnp.where(core == 0, at_1, at_0)])
     late = [name for name in pieces if name[0] > far]
     others = {name: from_xor(pieces[name], ("core",), 1) for name in first}
 
@@ -352,8 +373,8 @@
     for step in range(POWER - 1):
         total = call(orth_power_kernel, parts, flops, (at,), *z, a)
         z = gather_parts(sum_parts(total, jnp.bfloat16))
-    core = lax.axis_index("core")[None].astype(jnp.int32)
-    return call(last_kernel, loadings, flops, (at, core), *z, a).T, factor
+    at_core = core[None].astype(jnp.int32)
+    return call(last_kernel, loadings, flops, (at, at_core), *z, a).T, factor
 
 
 def local_gram(basis):

time: 171 us -> 175 us (1.023)
  starting transfers between devices: 45 us -> 50.8 us
  waiting for transfers between devices: 81.1 us -> 77 us
    ppermute x0 -> x24, starting transfers between devices: none -> 31.5 us  [from_square(): return lax.ppermute(value, ('z', 'core', 'col'), pairs)]
    ppermute x45 -> x21, waiting for transfers between devices: 81.1 us -> 52.7 us  [from_xor(): return lax.ppermute(value, axis, [(i, i ^ offset) for i in range(size)])]
    ppermute x45 -> x21, starting transfers between devices: 45 us -> 19.4 us  [from_xor(): return lax.ppermute(value, axis, [(i, i ^ offset) for i in range(size)])]
    ppermute x0 -> x24, waiting for transfers between devices: none -> 24.3 us  [from_square(): return lax.ppermute(value, ('z', 'core', 'col'), pairs)]
    unnamed x5 -> x9, local copies, waits for them, and re-layouts: 2.89 us -> 4.53 us
  transfers between devices with their start and end apart: 45 -> 45, of which waited for: 34 -> 31; matrix products, arithmetic and copies ran while one was open for 3% -> 3% of each run, Pallas kernels for 4% -> 3%
where the time goes in v17:
time: 175 us; the launch traced here: 174 us
  waiting for transfers between devices  77 us (44%)
  starting transfers between devices  50.8 us (29%)
  Pallas kernels  33.4 us (19%)
  local copies, waits for them, and re-layouts  7.16 us (4%)
  matrix products  3.83 us (2%)
    ppermute x21, waiting for transfers between devices, from_xor(): return lax.ppermute(value, axis, [(i, i ^ offset) for i in range(size)])  52.7 us
    pallas_call x6, Pallas kernels, call(): pl.pallas_call(kernel, out_shape=out_shapes, in_specs=[pl.BlockSpec(memor...  33.4 us
    ppermute x24, starting transfers between devices, from_square(): return lax.ppermute(value, ('z', 'core', 'col'), pairs)  31.5 us
    ppermute x24, waiting for transfers between devices, from_square(): return lax.ppermute(value, ('z', 'core', 'col'), pairs)  24.3 us
    ppermute x21, starting transfers between devices, from_xor(): return lax.ppermute(value, axis, [(i, i ^ offset) for i in range(size)])  19.4 us
    unnamed x9, local copies, waits for them, and re-layouts  4.53 us
    dot_general x1, matrix products, per_device_transposed(): lax.dot_general(omega, states, (((0,), (1,)), ((), ())), preferred_elemen...  3.83 us
  transfers between devices with their start and end apart: 45, of which 31 were waited for; matrix products, arithmetic and copies ran while one was open for 3% of the time, Pallas kernels for 3%

profile of v17, /device:TPU:0, one launch (start us, length us, event | category | flops | bytes accessed | tf_op | source)
XLA Modules:
  0.0 174.4 jit_solution(12607830571638013774)
XLA Ops:
  2.1 4.1 %collective-permute-start.1 = (bf16[256,1024]{1,0:T(8,128)(2,1)S(1)}, bf16[256,1024]{1,0:T(8,128)(2,1)S(1)}, u32[]{:S(2)}, u32[]{:S(2)}) collective-permute-start(bf16[256,1024]{1,0:T(8,128)(2,1)S(1)} %get-tuple-element.39), channel_id=1, source_target_pairs={{0,8},{4,12},{8,0},{12,4},{1,9},{5,13},{9,1},{13,5},{2,10},{6,14},... | collective-permute-start | bytes 1572872 | tf_op jit(solution)/shard_map/ppermute | solution.py:236
  6.2 1.6 collective-permute-start.3
  8.5 3.8 %convolution_bitcast_fusion = f32[8,2,8,128]{3,2,1,0:T(8,128)S(1)} fusion(bf16[256,4096]{1,0:T(8,128)(2,1)} %param.3, s32[]{:T(128)S(6)} %xor.77, s32[4096]{0:T(1024)S(1)} %add_multiply_fusion), kind=kOutput, calls=%fused_computation | convolution fusion | flops 152043520 | bytes 2179076 | tf_op jit(solution)/shard_map/dot_general | solution.py:319
  12.8 19.5 %collective-permute-done = f32[2,64,128]{2,1,0:T(8,128)S(1)} collective-permute-done((f32[2,64,128]{2,1,0:T(8,128)S(1)}, f32[2,64,128]{2,1,0:T(8,128)S(1)}, u32[]{:S(2)}, u32[]{:S(2)}) %collective-permute-start) | collective-permute-done | bytes 65568 | tf_op jit(solution)/shard_map/ppermute | solution.py:236
  32.3 1.6 collective-permute-start.2
  35.0 3.5 %collective-permute-start.5 = (bf16[128,1024]{1,0:T(8,128)(2,1)S(1)}, bf16[128,1024]{1,0:T(8,128)(2,1)S(1)}, u32[]{:S(2)}, u32[]{:S(2)}) collective-permute-start(bf16[128,1024]{1,0:T(8,128)(2,1)S(1)} %get-tuple-element.42), channel_id=1, source_target_pairs={{0,12},{4,8},{8,4},{12,0},{1,13},{5,9},{9,5},{13,1},{2,14},{6,10},... | collective-permute-start | bytes 786440 | tf_op jit(solution)/shard_map/ppermute | solution.py:236
  38.6 9.0 %collective-permute-done.4 = f32[4,64,128]{2,1,0:T(8,128)S(1)} collective-permute-done((f32[4,64,128]{2,1,0:T(8,128)S(1)}, f32[4,64,128]{2,1,0:T(8,128)S(1)}, u32[]{:S(2)}, u32[]{:S(2)}) %collective-permute-start.4) | collective-permute-done | bytes 131104 | tf_op jit(solution)/shard_map/ppermute | solution.py:236
  47.7 3.6 %collective-permute-start.7 = (bf16[128,1024]{1,0:T(8,128)(2,1)S(1)}, bf16[128,1024]{1,0:T(8,128)(2,1)}, u32[]{:S(2)}, u32[]{:S(2)}) collective-permute-start(bf16[128,1024]{1,0:T(8,128)(2,1)S(1)} %get-tuple-element.41), channel_id=1, source_target_pairs={{0,12},{4,8},{8,4},{12,0},{1,13},{5,9},{9,5},{13,1},{2,14},{6,10},... | collective-permute-start | bytes 786440 | tf_op jit(solution)/shard_map/ppermute | solution.py:236
  52.1 6.0 %shard_map.41 = (bf16[64,2048]{1,0:T(8,128)(2,1)S(1)}, f32[64,64]{1,0:T(8,128)S(1)}) custom-call(s32[16]{0:T(128)S(1)} %pad_add_fusion.1.at_ref, f32[8,64,128]{2,1,0:T(8,128)S(1)} %pad_maximum_fusion.z_ref, f32[8,64,128]{2,1,0:T(8,128)S(1)} %collective-permute-done.6.other_ref), custom_call_target="tpu_custom_call" | custom-call | flops 402653184 | bytes 524288 | tf_op jit(solution)/shard_map/pallas_call | solution.py:219
  62.0 2.7 %shard_map.42 = (bf16[2048,1024]{1,0:T(8,128)(2,1)S(1)}, f32[8,64,128]{2,1,0:T(8,128)S(1)}) custom-call(s32[16]{0:T(128)S(1)} %pad_add_fusion.at_ref, bf16[64,2048]{1,0:T(8,128)(2,1)S(1)} %copy-done.3, bf16[256,1024]{1,0:T(8,128)(2,1)S(1)} %get-tuple-element.38.refs_0_, bf16[256,1024]{1,0:T(8,128)(2,1)S(1)} %collective-permute-done.3.refs_1_, ...), custom_call_target="tpu_custom_call" | custom-call | flops 939524096 | bytes 4456448 | tf_op jit(solution)/shard_map/pallas_call | solution.py:219
  65.3 6.0 %collective-permute-start.15 = (f32[2,64,128]{2,1,0:T(8,128)S(1)}, f32[2,64,128]{2,1,0:T(8,128)S(1)}, u32[]{:S(2)}, u32[]{:S(2)}) collective-permute-start(f32[2,64,128]{2,1,0:T(8,128)S(1)} %get-tuple-element.44), channel_id=1, source_target_pairs={{0,5},{1,4},{4,1},{5,0},{8,13},{9,12},{12,9},{13,8},{2,7},{3,6},{6... | collective-permute-start | bytes 196616 | tf_op jit(solution)/shard_map/ppermute | solution.py:255
  71.4 2.8 %collective-permute-done.15 = f32[2,64,128]{2,1,0:T(8,128)S(1)} collective-permute-done((f32[2,64,128]{2,1,0:T(8,128)S(1)}, f32[2,64,128]{2,1,0:T(8,128)S(1)}, u32[]{:S(2)}, u32[]{:S(2)}) %collective-permute-start.15) | collective-permute-done | bytes 65568 | tf_op jit(solution)/shard_map/ppermute | solution.py:255
  76.3 5.3 %collective-permute-done.16 = f32[2,64,128]{2,1,0:T(8,128)S(1)} collective-permute-done((f32[2,64,128]{2,1,0:T(8,128)S(1)}, f32[2,64,128]{2,1,0:T(8,128)S(1)}, u32[]{:S(2)}, u32[]{:S(2)}) %collective-permute-start.16) | collective-permute-done | bytes 65568 | tf_op jit(solution)/shard_map/ppermute | solution.py:236
  81.9 1.7 collective-permute-start.18
  85.1 1.7 collective-permute-done.19
  89.5 6.7 %shard_map.43 = f32[8,64,128]{2,1,0:T(8,128)S(1)} custom-call(s32[16]{0:T(128)S(1)} %pad_add_fusion.at_ref, f32[8,64,128]{2,1,0:T(8,128)S(1)} %pad_maximum_fusion.1.z_ref, f32[8,64,128]{2,1,0:T(8,128)S(1)} %collective-permute-done.20.other_ref, bf16[2048,1024]{1,0:T(8,128)(2,1)S(1)} %get-tuple-element.30.a_ref), custom_call_target="tpu_custom_call" | custom-call | flops 939524096 | bytes 4718592 | tf_op jit(solution)/shard_map/pallas_call | solution.py:219
  98.2 1.7 collective-permute-start.22
  100.3 2.4 %collective-permute-done.23 = bf16[2,64,128]{2,1,0:T(8,128)(2,1)S(1)} collective-permute-done((bf16[2,64,128]{2,1,0:T(8,128)(2,1)S(1)}, bf16[2,64,128]{2,1,0:T(8,128)(2,1)S(1)}, u32[]{:S(2)}, u32[]{:S(2)}) %collective-permute-start.23) | collective-permute-done | bytes 32800 | tf_op jit(solution)/shard_map/ppermute | solution.py:255
  103.8 3.8 %collective-permute-done.24 = bf16[2,64,128]{2,1,0:T(8,128)(2,1)S(1)} collective-permute-done((bf16[2,64,128]{2,1,0:T(8,128)(2,1)S(1)}, bf16[2,64,128]{2,1,0:T(8,128)(2,1)S(1)}, u32[]{:S(2)}, u32[]{:S(2)}) %collective-permute-start.24) | collective-permute-done | bytes 32800 | tf_op jit(solution)/shard_map/ppermute | solution.py:236
  107.6 2.1 %collective-permute-start.27 = (bf16[2,64,128]{2,1,0:T(8,128)(2,1)S(1)}, bf16[2,64,128]{2,1,0:T(8,128)(2,1)S(1)}, u32[]{:S(2)}, u32[]{:S(2)}) collective-permute-start(bf16[2,64,128]{2,1,0:T(8,128)(2,1)S(1)} %add_convert_fusion.2), channel_id=1, source_target_pairs={{0,5},{1,4},{4,1},{5,0},{8,13},{9,12},{12,9},{13,8},{2,7},{3,6},{6... | collective-permute-start | bytes 98312 | tf_op jit(solution)/shard_map/ppermute | solution.py:255
  115.4 6.1 %shard_map.44 = f32[8,64,128]{2,1,0:T(8,128)S(1)} custom-call(s32[16]{0:T(128)S(1)} %pad_add_fusion.at_ref, bf16[8,64,128]{2,1,0:T(8,128)(2,1)S(1)} %pad_maximum_fusion.3.z_ref, bf16[8,64,128]{2,1,0:T(8,128)(2,1)S(1)} %collective-permute-done.28.other_ref, bf16[2048,1024]{1,0:T(8,128)(2,1)S(1)} %get-tuple-element.30.a_ref), custom_call_target="tpu_custom_call" | custom-call | flops 939524096 | bytes 4456448 | tf_op jit(solution)/shard_map/pallas_call | solution.py:219
  122.7 2.0 %collective-permute-start.31 = (bf16[2,64,128]{2,1,0:T(8,128)(2,1)S(1)}, bf16[2,64,128]{2,1,0:T(8,128)(2,1)S(1)}, u32[]{:S(2)}, u32[]{:S(2)}) collective-permute-start(bf16[2,64,128]{2,1,0:T(8,128)(2,1)S(1)} %get-tuple-element.50), channel_id=1, source_target_pairs={{0,5},{1,4},{4,1},{5,0},{8,13},{9,12},{12,9},{13,8},{2,7},{3,6},{6... | collective-permute-start | bytes 98312 | tf_op jit(solution)/shard_map/ppermute | solution.py:255
  125.5 2.0 %collective-permute-done.31 = bf16[2,64,128]{2,1,0:T(8,128)(2,1)S(1)} collective-permute-done((bf16[2,64,128]{2,1,0:T(8,128)(2,1)S(1)}, bf16[2,64,128]{2,1,0:T(8,128)(2,1)S(1)}, u32[]{:S(2)}, u32[]{:S(2)}) %collective-permute-start.31) | collective-permute-done | bytes 32800 | tf_op jit(solution)/shard_map/ppermute | solution.py:255
  129.0 4.7 %collective-permute-done.32 = bf16[2,64,128]{2,1,0:T(8,128)(2,1)S(1)} collective-permute-done((bf16[2,64,128]{2,1,0:T(8,128)(2,1)S(1)}, bf16[2,64,128]{2,1,0:T(8,128)(2,1)S(1)}, u32[]{:S(2)}, u32[]{:S(2)}) %collective-permute-start.32) | collective-permute-done | bytes 32800 | tf_op jit(solution)/shard_map/ppermute | solution.py:236
  135.6 1.6 collective-permute-start.33
  141.0 6.1 %shard_map.45 = f32[8,64,128]{2,1,0:T(8,128)S(1)} custom-call(s32[16]{0:T(128)S(1)} %pad_add_fusion.at_ref, bf16[8,64,128]{2,1,0:T(8,128)(2,1)S(1)} %pad_maximum_fusion.4.z_ref, bf16[8,64,128]{2,1,0:T(8,128)(2,1)S(1)} %collective-permute-done.36.other_ref, bf16[2048,1024]{1,0:T(8,128)(2,1)S(1)} %get-tuple-element.30.a_ref), custom_call_target="tpu_custom_call" | custom-call | flops 939524096 | bytes 4456448 | tf_op jit(solution)/shard_map/pallas_call | solution.py:219
  147.1 1.7 collective-permute-start.37
  151.1 2.5 %collective-permute-done.39 = bf16[2,64,128]{2,1,0:T(8,128)(2,1)S(1)} collective-permute-done((bf16[2,64,128]{2,1,0:T(8,128)(2,1)S(1)}, bf16[2,64,128]{2,1,0:T(8,128)(2,1)S(1)}, u32[]{:S(2)}, u32[]{:S(2)}) %collective-permute-start.39) | collective-permute-done | bytes 32800 | tf_op jit(solution)/shard_map/ppermute | solution.py:255
  154.5 4.0 %collective-permute-done.40 = bf16[2,64,128]{2,1,0:T(8,128)(2,1)S(1)} collective-permute-done((bf16[2,64,128]{2,1,0:T(8,128)(2,1)S(1)}, bf16[2,64,128]{2,1,0:T(8,128)(2,1)S(1)}, u32[]{:S(2)}, u32[]{:S(2)}) %collective-permute-start.40) | collective-permute-done | bytes 32800 | tf_op jit(solution)/shard_map/ppermute | solution.py:236
  158.5 2.3 %collective-permute-start.43 = (bf16[2,64,128]{2,1,0:T(8,128)(2,1)S(1)}, bf16[2,64,128]{2,1,0:T(8,128)(2,1)S(1)}, u32[]{:S(2)}, u32[]{:S(2)}) collective-permute-start(bf16[2,64,128]{2,1,0:T(8,128)(2,1)S(1)} %add_convert_fusion), channel_id=1, source_target_pairs={{0,5},{1,4},{4,1},{5,0},{8,13},{9,12},{12,9},{13,8},{2,7},{3,6},{6... | collective-permute-start | bytes 98312 | tf_op jit(solution)/shard_map/ppermute | solution.py:255
  166.3 2.2 %copy-done.1 = bf16[2048,1024]{1,0:T(8,128)(2,1)S(1)} copy-done((bf16[2048,1024]{1,0:T(8,128)(2,1)S(1)}, bf16[2048,1024]{1,0:T(8,128)(2,1)}, u32[]{:S(2)}) %copy-start.1) | copy-done | bytes 4194328
  168.5 5.8 %shard_map.46 = f32[64,512]{1,0:T(8,128)} custom-call(s32[16]{0:T(128)S(1)} %pad_add_fusion.at_ref, s32[1]{0:T(128)} %bitcast.core_ref, bf16[8,64,128]{2,1,0:T(8,128)(2,1)S(1)} %pad_maximum_fusion.5.z_ref, bf16[8,64,128]{2,1,0:T(8,128)(2,1)S(1)} %collective-permute-done.44.other_ref, bf16[2048,1024]{1,0:T(8,128)(2,1)S(1)} %copy-done.1), custom_call_target="tpu_custom_call" | custom-call | flops 939524096 | bytes 4456448 | tf_op jit(solution)/shard_map/pallas_call | solution.py:219
  (105 shorter events, 42.1 us)
Async XLA Ops:
  2.1 30.1 %collective-permute-start.1 = (bf16[256,1024]{1,0:T(8,128)(2,1)S(1)}, bf16[256,1024]{1,0:T(8,128)(2,1)S(1)}, u32[]{:S(2)}, u32[]{:S(2)}) collective-permute-start(bf16[256,1024]{1,0:T(8,128)(2,1)S(1)} %get-tuple-element.39), channel_id=1, source_target_pairs={{0,8},{4,12},{8,0},{12,4},{1,9},{5,13},{9,1},{13,5},{2,10},{6,14},... | collective-permute-start | bytes 1572872 | tf_op jit(solution)/shard_map/ppermute | solution.py:236
  6.2 32.2 %collective-permute-start.3 = (bf16[256,1024]{1,0:T(8,128)(2,1)S(1)}, bf16[256,1024]{1,0:T(8,128)(2,1)S(1)}, u32[]{:S(2)}, u32[]{:S(2)}) collective-permute-start(bf16[256,1024]{1,0:T(8,128)(2,1)S(1)} %get-tuple-element.40), channel_id=1, source_target_pairs={{0,4},{4,0},{8,12},{12,8},{1,5},{5,1},{9,13},{13,9},{2,6},{6,2},{1... | collective-permute-start | bytes 1572872 | tf_op jit(solution)/shard_map/ppermute | solution.py:236
  12.4 19.9 %collective-permute-start = (f32[2,64,128]{2,1,0:T(8,128)S(1)}, f32[2,64,128]{2,1,0:T(8,128)S(1)}, u32[]{:S(2)}, u32[]{:S(2)}) collective-permute-start(f32[2,64,128]{2,1,0:T(8,128)S(1)} %bitcast.16), channel_id=1, source_target_pairs={{0,8},{4,12},{8,0},{12,4},{1,9},{5,13},{9,1},{13,5},{2,10},{6,14},... | collective-permute-start | bytes 196616 | tf_op jit(solution)/shard_map/ppermute | solution.py:236
  32.3 6.2 %collective-permute-start.2 = (f32[4,64,128]{2,1,0:T(8,128)S(1)}, f32[4,64,128]{2,1,0:T(8,128)S(1)}, u32[]{:S(2)}, u32[]{:S(2)}) collective-permute-start(f32[4,64,128]{2,1,0:T(8,128)S(1)} %pad_maximum_fusion.2), channel_id=1, source_target_pairs={{0,1},{1,0},{2,3},{3,2},{4,5},{5,4},{6,7},{7,6},{8,9},{9,8},{10,11... | collective-permute-start | bytes 393224 | tf_op jit(solution)/shard_map/ppermute | solution.py:236
  35.0 12.7 %collective-permute-start.5 = (bf16[128,1024]{1,0:T(8,128)(2,1)S(1)}, bf16[128,1024]{1,0:T(8,128)(2,1)S(1)}, u32[]{:S(2)}, u32[]{:S(2)}) collective-permute-start(bf16[128,1024]{1,0:T(8,128)(2,1)S(1)} %get-tuple-element.42), channel_id=1, source_target_pairs={{0,12},{4,8},{8,4},{12,0},{1,13},{5,9},{9,5},{13,1},{2,14},{6,10},... | collective-permute-start | bytes 786440 | tf_op jit(solution)/shard_map/ppermute | solution.py:236
  38.5 9.1 %collective-permute-start.4 = (f32[4,64,128]{2,1,0:T(8,128)S(1)}, f32[4,64,128]{2,1,0:T(8,128)S(1)}, u32[]{:S(2)}, u32[]{:S(2)}) collective-permute-start(f32[4,64,128]{2,1,0:T(8,128)S(1)} %add.248), channel_id=1, source_target_pairs={{0,4},{4,0},{8,12},{12,8},{1,5},{5,1},{9,13},{13,9},{2,6},{6,2},{1... | collective-permute-start | bytes 393224 | tf_op jit(solution)/shard_map/ppermute | solution.py:236
  47.6 4.5 %collective-permute-start.6 = (f32[8,64,128]{2,1,0:T(8,128)S(1)}, f32[8,64,128]{2,1,0:T(8,128)S(1)}, u32[]{:S(2)}, u32[]{:S(2)}) collective-permute-start(f32[8,64,128]{2,1,0:T(8,128)S(1)} %pad_maximum_fusion.z_ref), channel_id=1, source_target_pairs={{0,2},{2,0},{1,3},{3,1},{4,6},{6,4},{5,7},{7,5},{8,10},{10,8},{9,1... | collective-permute-start | bytes 786440 | tf_op jit(solution)/shard_map/ppermute | solution.py:236
  47.7 11.1 %collective-permute-start.7 = (bf16[128,1024]{1,0:T(8,128)(2,1)S(1)}, bf16[128,1024]{1,0:T(8,128)(2,1)}, u32[]{:S(2)}, u32[]{:S(2)}) collective-permute-start(bf16[128,1024]{1,0:T(8,128)(2,1)S(1)} %get-tuple-element.41), channel_id=1, source_target_pairs={{0,12},{4,8},{8,4},{12,0},{1,13},{5,9},{9,5},{13,1},{2,14},{6,10},... | collective-permute-start | bytes 786440 | tf_op jit(solution)/shard_map/ppermute | solution.py:236
  51.3 8.1 %collective-permute-start.8 = (bf16[256,1024]{1,0:T(8,128)(2,1)S(1)}, bf16[256,1024]{1,0:T(8,128)(2,1)S(1)}, u32[]{:S(2)}, u32[]{:S(2)}) collective-permute-start(bf16[256,1024]{1,0:T(8,128)(2,1)S(1)} %get-tuple-element.38.refs_0_), channel_id=1, source_target_pairs={{0,2},{2,0},{1,3},{3,1},{4,6},{6,4},{5,7},{7,5},{8,10},{10,8},{9,1... | collective-permute-start | bytes 1572872 | tf_op jit(solution)/shard_map/ppermute | solution.py:236
  51.5 7.9 %collective-permute-start.10 = (bf16[256,1024]{1,0:T(8,128)(2,1)S(1)}, bf16[256,1024]{1,0:T(8,128)(2,1)S(1)}, u32[]{:S(2)}, u32[]{:S(2)}) collective-permute-start(bf16[256,1024]{1,0:T(8,128)(2,1)S(1)} %collective-permute-done.1.refs_2_), channel_id=1, source_target_pairs={{0,2},{2,0},{1,3},{3,1},{4,6},{6,4},{5,7},{7,5},{8,10},{10,8},{9,1... | collective-permute-start | bytes 1572872 | tf_op jit(solution)/shard_map/ppermute | solution.py:236
  51.8 7.6 %collective-permute-start.9 = (bf16[256,1024]{1,0:T(8,128)(2,1)S(1)}, bf16[256,1024]{1,0:T(8,128)(2,1)S(1)}, u32[]{:S(2)}, u32[]{:S(2)}) collective-permute-start(bf16[256,1024]{1,0:T(8,128)(2,1)S(1)} %collective-permute-done.3.refs_1_), channel_id=1, source_target_pairs={{0,2},{2,0},{1,3},{3,1},{4,6},{6,4},{5,7},{7,5},{8,10},{10,8},{9,1... | collective-permute-start | bytes 1572872 | tf_op jit(solution)/shard_map/ppermute | solution.py:236
  64.7 6.6 %collective-permute-start.13 = (f32[2,64,128]{2,1,0:T(8,128)S(1)}, f32[2,64,128]{2,1,0:T(8,128)S(1)}, u32[]{:S(2)}, u32[]{:S(2)}) collective-permute-start(f32[2,64,128]{2,1,0:T(8,128)S(1)} %get-tuple-element.43), channel_id=1, source_target_pairs={{0,1},{1,0},{4,5},{5,4},{8,9},{9,8},{12,13},{13,12},{2,6},{3,7},{6... | collective-permute-start | bytes 196616 | tf_op jit(solution)/shard_map/ppermute | solution.py:255
  65.3 8.8 %collective-permute-start.15 = (f32[2,64,128]{2,1,0:T(8,128)S(1)}, f32[2,64,128]{2,1,0:T(8,128)S(1)}, u32[]{:S(2)}, u32[]{:S(2)}) collective-permute-start(f32[2,64,128]{2,1,0:T(8,128)S(1)} %get-tuple-element.44), channel_id=1, source_target_pairs={{0,5},{1,4},{4,1},{5,0},{8,13},{9,12},{12,9},{13,8},{2,7},{3,6},{6... | collective-permute-start | bytes 196616 | tf_op jit(solution)/shard_map/ppermute | solution.py:255
  71.3 4.3 %collective-permute-start.14 = (f32[2,64,128]{2,1,0:T(8,128)S(1)}, f32[2,64,128]{2,1,0:T(8,128)S(1)}, u32[]{:S(2)}, u32[]{:S(2)}) collective-permute-start(f32[2,64,128]{2,1,0:T(8,128)S(1)} %get-tuple-element.45), channel_id=1, source_target_pairs={{0,4},{1,5},{4,0},{5,1},{8,12},{9,13},{12,8},{13,9},{2,3},{3,2},{6... | collective-permute-start | bytes 196616 | tf_op jit(solution)/shard_map/ppermute | solution.py:255
  75.6 5.9 %collective-permute-start.16 = (f32[2,64,128]{2,1,0:T(8,128)S(1)}, f32[2,64,128]{2,1,0:T(8,128)S(1)}, u32[]{:S(2)}, u32[]{:S(2)}) collective-permute-start(f32[2,64,128]{2,1,0:T(8,128)S(1)} %add_add_fusion), channel_id=1, source_target_pairs={{0,8},{4,12},{8,0},{12,4},{1,9},{5,13},{9,1},{13,5},{2,10},{6,14},... | collective-permute-start | bytes 196616 | tf_op jit(solution)/shard_map/ppermute | solution.py:236
  81.6 5.2 %collective-permute-start.19 = (f32[2,64,128]{2,1,0:T(8,128)S(1)}, f32[2,64,128]{2,1,0:T(8,128)S(1)}, u32[]{:S(2)}, u32[]{:S(2)}) collective-permute-start(f32[2,64,128]{2,1,0:T(8,128)S(1)} %add.255), channel_id=1, source_target_pairs={{0,5},{1,4},{4,1},{5,0},{8,13},{9,12},{12,9},{13,8},{2,7},{3,6},{6... | collective-permute-start | bytes 196616 | tf_op jit(solution)/shard_map/ppermute | solution.py:255
  81.9 4.9 %collective-permute-start.18 = (f32[2,64,128]{2,1,0:T(8,128)S(1)}, f32[2,64,128]{2,1,0:T(8,128)S(1)}, u32[]{:S(2)}, u32[]{:S(2)}) collective-permute-start(f32[2,64,128]{2,1,0:T(8,128)S(1)} %add.255), channel_id=1, source_target_pairs={{0,4},{1,5},{4,0},{5,1},{8,12},{9,13},{12,8},{13,9},{2,3},{3,2},{6... | collective-permute-start | bytes 196616 | tf_op jit(solution)/shard_map/ppermute | solution.py:255
  83.6 4.3 %collective-permute-start.17 = (f32[2,64,128]{2,1,0:T(8,128)S(1)}, f32[2,64,128]{2,1,0:T(8,128)S(1)}, u32[]{:S(2)}, u32[]{:S(2)}) collective-permute-start(f32[2,64,128]{2,1,0:T(8,128)S(1)} %add.255), channel_id=1, source_target_pairs={{0,1},{1,0},{4,5},{5,4},{8,9},{9,8},{12,13},{13,12},{2,6},{3,7},{6... | collective-permute-start | bytes 196616 | tf_op jit(solution)/shard_map/ppermute | solution.py:255
  96.3 4.0 %collective-permute-start.21 = (bf16[2,64,128]{2,1,0:T(8,128)(2,1)S(1)}, bf16[2,64,128]{2,1,0:T(8,128)(2,1)S(1)}, u32[]{:S(2)}, u32[]{:S(2)}) collective-permute-start(bf16[2,64,128]{2,1,0:T(8,128)(2,1)S(1)} %get-tuple-element.52), channel_id=1, source_target_pairs={{0,1},{1,0},{4,5},{5,4},{8,9},{9,8},{12,13},{13,12},{2,6},{3,7},{6... | collective-permute-start | bytes 98312 | tf_op jit(solution)/shard_map/ppermute | solution.py:255
  97.9 4.8 %collective-permute-start.23 = (bf16[2,64,128]{2,1,0:T(8,128)(2,1)S(1)}, bf16[2,64,128]{2,1,0:T(8,128)(2,1)S(1)}, u32[]{:S(2)}, u32[]{:S(2)}) collective-permute-start(bf16[2,64,128]{2,1,0:T(8,128)(2,1)S(1)} %get-tuple-element.53), channel_id=1, source_target_pairs={{0,5},{1,4},{4,1},{5,0},{8,13},{9,12},{12,9},{13,8},{2,7},{3,6},{6... | collective-permute-start | bytes 98312 | tf_op jit(solution)/shard_map/ppermute | solution.py:255
  98.2 4.5 %collective-permute-start.22 = (bf16[2,64,128]{2,1,0:T(8,128)(2,1)S(1)}, bf16[2,64,128]{2,1,0:T(8,128)(2,1)S(1)}, u32[]{:S(2)}, u32[]{:S(2)}) collective-permute-start(bf16[2,64,128]{2,1,0:T(8,128)(2,1)S(1)} %get-tuple-element.54), channel_id=1, source_target_pairs={{0,4},{1,5},{4,0},{5,1},{8,12},{9,13},{12,8},{13,9},{2,3},{3,2},{6... | collective-permute-start | bytes 98312 | tf_op jit(solution)/shard_map/ppermute | solution.py:255
  102.7 4.9 %collective-permute-start.24 = (bf16[2,64,128]{2,1,0:T(8,128)(2,1)S(1)}, bf16[2,64,128]{2,1,0:T(8,128)(2,1)S(1)}, u32[]{:S(2)}, u32[]{:S(2)}) collective-permute-start(bf16[2,64,128]{2,1,0:T(8,128)(2,1)S(1)} %fusion.21), channel_id=1, source_target_pairs={{0,8},{4,12},{8,0},{12,4},{1,9},{5,13},{9,1},{13,5},{2,10},{6,14},... | collective-permute-start | bytes 98312 | tf_op jit(solution)/shard_map/ppermute | solution.py:236
  107.6 4.9 %collective-permute-start.27 = (bf16[2,64,128]{2,1,0:T(8,128)(2,1)S(1)}, bf16[2,64,128]{2,1,0:T(8,128)(2,1)S(1)}, u32[]{:S(2)}, u32[]{:S(2)}) collective-permute-start(bf16[2,64,128]{2,1,0:T(8,128)(2,1)S(1)} %add_convert_fusion.2), channel_id=1, source_target_pairs={{0,5},{1,4},{4,1},{5,0},{8,13},{9,12},{12,9},{13,8},{2,7},{3,6},{6... | collective-permute-start | bytes 98312 | tf_op jit(solution)/shard_map/ppermute | solution.py:255
  121.5 4.0 %collective-permute-start.29 = (bf16[2,64,128]{2,1,0:T(8,128)(2,1)S(1)}, bf16[2,64,128]{2,1,0:T(8,128)(2,1)S(1)}, u32[]{:S(2)}, u32[]{:S(2)}) collective-permute-start(bf16[2,64,128]{2,1,0:T(8,128)(2,1)S(1)} %get-tuple-element.49), channel_id=1, source_target_pairs={{0,1},{1,0},{4,5},{5,4},{8,9},{9,8},{12,13},{13,12},{2,6},{3,7},{6... | collective-permute-start | bytes 98312 | tf_op jit(solution)/shard_map/ppermute | solution.py:255
  122.7 4.8 %collective-permute-start.31 = (bf16[2,64,128]{2,1,0:T(8,128)(2,1)S(1)}, bf16[2,64,128]{2,1,0:T(8,128)(2,1)S(1)}, u32[]{:S(2)}, u32[]{:S(2)}) collective-permute-start(bf16[2,64,128]{2,1,0:T(8,128)(2,1)S(1)} %get-tuple-element.50), channel_id=1, source_target_pairs={{0,5},{1,4},{4,1},{5,0},{8,13},{9,12},{12,9},{13,8},{2,7},{3,6},{6... | collective-permute-start | bytes 98312 | tf_op jit(solution)/shard_map/ppermute | solution.py:255
  128.6 5.0 %collective-permute-start.32 = (bf16[2,64,128]{2,1,0:T(8,128)(2,1)S(1)}, bf16[2,64,128]{2,1,0:T(8,128)(2,1)S(1)}, u32[]{:S(2)}, u32[]{:S(2)}) collective-permute-start(bf16[2,64,128]{2,1,0:T(8,128)(2,1)S(1)} %fusion.18), channel_id=1, source_target_pairs={{0,8},{4,12},{8,0},{12,4},{1,9},{5,13},{9,1},{13,5},{2,10},{6,14},... | collective-permute-start | bytes 98312 | tf_op jit(solution)/shard_map/ppermute | solution.py:236
  133.7 4.9 %collective-permute-start.35 = (bf16[2,64,128]{2,1,0:T(8,128)(2,1)S(1)}, bf16[2,64,128]{2,1,0:T(8,128)(2,1)S(1)}, u32[]{:S(2)}, u32[]{:S(2)}) collective-permute-start(bf16[2,64,128]{2,1,0:T(8,128)(2,1)S(1)} %add_convert_fusion.1), channel_id=1, source_target_pairs={{0,5},{1,4},{4,1},{5,0},{8,13},{9,12},{12,9},{13,8},{2,7},{3,6},{6... | collective-permute-start | bytes 98312 | tf_op jit(solution)/shard_map/ppermute | solution.py:255
  134.5 4.1 %collective-permute-start.34 = (bf16[2,64,128]{2,1,0:T(8,128)(2,1)S(1)}, bf16[2,64,128]{2,1,0:T(8,128)(2,1)S(1)}, u32[]{:S(2)}, u32[]{:S(2)}) collective-permute-start(bf16[2,64,128]{2,1,0:T(8,128)(2,1)S(1)} %add_convert_fusion.1), channel_id=1, source_target_pairs={{0,4},{1,5},{4,0},{5,1},{8,12},{9,13},{12,8},{13,9},{2,3},{3,2},{6... | collective-permute-start | bytes 98312 | tf_op jit(solution)/shard_map/ppermute | solution.py:255
  148.8 4.8 %collective-permute-start.39 = (bf16[2,64,128]{2,1,0:T(8,128)(2,1)S(1)}, bf16[2,64,128]{2,1,0:T(8,128)(2,1)S(1)}, u32[]{:S(2)}, u32[]{:S(2)}) collective-permute-start(bf16[2,64,128]{2,1,0:T(8,128)(2,1)S(1)} %get-tuple-element.47), channel_id=1, source_target_pairs={{0,5},{1,4},{4,1},{5,0},{8,13},{9,12},{12,9},{13,8},{2,7},{3,6},{6... | collective-permute-start | bytes 98312 | tf_op jit(solution)/shard_map/ppermute | solution.py:255
  149.5 4.1 %collective-permute-start.38 = (bf16[2,64,128]{2,1,0:T(8,128)(2,1)S(1)}, bf16[2,64,128]{2,1,0:T(8,128)(2,1)S(1)}, u32[]{:S(2)}, u32[]{:S(2)}) collective-permute-start(bf16[2,64,128]{2,1,0:T(8,128)(2,1)S(1)} %get-tuple-element.48), channel_id=1, source_target_pairs={{0,4},{1,5},{4,0},{5,1},{8,12},{9,13},{12,8},{13,9},{2,3},{3,2},{6... | collective-permute-start | bytes 98312 | tf_op jit(solution)/shard_map/ppermute | solution.py:255
  153.6 4.9 %collective-permute-start.40 = (bf16[2,64,128]{2,1,0:T(8,128)(2,1)S(1)}, bf16[2,64,128]{2,1,0:T(8,128)(2,1)S(1)}, u32[]{:S(2)}, u32[]{:S(2)}) collective-permute-start(bf16[2,64,128]{2,1,0:T(8,128)(2,1)S(1)} %fusion.15), channel_id=1, source_target_pairs={{0,8},{4,12},{8,0},{12,4},{1,9},{5,13},{9,1},{13,5},{2,10},{6,14},... | collective-permute-start | bytes 98312 | tf_op jit(solution)/shard_map/ppermute | solution.py:236
  158.5 4.9 %collective-permute-start.43 = (bf16[2,64,128]{2,1,0:T(8,128)(2,1)S(1)}, bf16[2,64,128]{2,1,0:T(8,128)(2,1)S(1)}, u32[]{:S(2)}, u32[]{:S(2)}) collective-permute-start(bf16[2,64,128]{2,1,0:T(8,128)(2,1)S(1)} %add_convert_fusion), channel_id=1, source_target_pairs={{0,5},{1,4},{4,1},{5,0},{8,13},{9,12},{12,9},{13,8},{2,7},{3,6},{6... | collective-permute-start | bytes 98312 | tf_op jit(solution)/shard_map/ppermute | solution.py:255
  (17 other events, 117.0 us)

commit v18 on v15

--- a/solution.py
+++ b/solution.py
@@ -139,13 +139,15 @@
     return jnp.where(keep, both[:, :size], 0.0), both[:, size:]
 
 
-def shifted_factor(whole_gram):
+def shifted_factor(wide):
+    whole_gram = gram_of(wide)
+    squares = wide.astype(jnp.float32)
+    squares = jnp.sum(squares * squares, axis=0, keepdims=True)
+    trace = jnp.sum(squares, axis=1, keepdims=True)
     size = whole_gram.shape[0]
     diagonal = lax.broadcasted_iota(jnp.int32, (size, size), 0) == lax.broadcasted_iota(
         jnp.int32, (size, size), 1
     )
-    on_diagonal = jnp.where(diagonal, whole_gram, 0.0)
-    trace = jnp.sum(jnp.sum(on_diagonal, axis=1, keepdims=True), axis=0, keepdims=True)
     scaled = whole_gram * (1.0 / trace)
     upper, inverse = eliminate(jnp.where(diagonal, scaled + shift_ratio, scaled))
     root = jnp.sqrt(trace)
@@ -159,7 +161,7 @@
 
 def first_pass(at_ref, z_refs):
     wide = wide_of(at_ref, z_refs)
-    upper, inverse_one = shifted_factor(gram_of(wide))
+    upper, inverse_one = shifted_factor(wide)
     return small_times_wide(inverse_one, wide), upper
 
 
@@ -179,9 +181,8 @@
     return small_times_wide(inverse_two, jnp.concatenate(tiles, axis=1))
 
 
-def forth_product(weights, a_ref, at_ref, part_ref):
+def store_parts(forth, at_ref, part_ref):
     chunks, unused, width = part_ref.shape
-    forth = dot_nt(weights.astype(jnp.bfloat16), a_ref[: chunks * width, :])
     for i in range(chunks):
         part_ref[at_ref[i]] = forth[:, width * i : width * (i + 1)]
 
@@ -199,12 +200,18 @@
     for piece_ref in piece_refs:
         a_ref[start : start + piece_ref.shape[0], :] = piece_ref[...]
         start += piece_ref.shape[0]
-    forth_product(dot_nn(basis_ref[...], a_ref[...]), a_ref, at_ref, part_ref)
-
-
-def orth_power_kernel(at_ref, z_ref, other_ref, a_ref, part_ref):
-    weights = back_product(at_ref, (z_ref, other_ref), a_ref[...])
-    forth_product(weights, a_ref, at_ref, part_ref)
+    weights = dot_nn(basis_ref[...], a_ref[...]).astype(jnp.bfloat16)
+    forth = dot_nt(weights, a_ref[: part_ref.shape[0] * part_ref.shape[2], :])
+    store_parts(forth, at_ref, part_ref)
+
+
+def turn_kernel(a_ref, turned_ref):
+    turned_ref[...] = a_ref[: turned_ref.shape[1], :].T
+
+
+def orth_power_kernel(at_ref, z_ref, other_ref, a_ref, turned_ref, part_ref):
+    weights = back_product(at_ref, (z_ref, other_ref), a_ref[...]).astype(jnp.bfloat16)
+    store_parts(dot_nn(weights, turned_ref[...]), at_ref, part_ref)
 
 
 def last_kernel(at_ref, core_ref, z_ref, other_ref, a_ref, out_ref):
@@ -348,9 +355,12 @@
     blocks = [half[name] for half in (pieces, others) for name in sorted(half)]
     factor = upper.T * (1.0 / math.sqrt(rows_total * width_total))
     a, total = call(power_kernel, (slab, parts), flops, (at,), basis, *blocks)
-    z = gather_parts(sum_parts(total, f32))
+    turned = jax.ShapeDtypeStruct((cols, rows_total // n_core), states.dtype)
+    turned = call(turn_kernel, turned, flops, (), a)
+    share, turned = lax.optimization_barrier((sum_parts(total, f32), turned))
+    z = gather_parts(share)
     for step in range(POWER - 1):
-        total = call(orth_power_kernel, parts, flops, (at,), *z, a)
+        total = call(orth_power_kernel, parts, flops, (at,), *z, a, turned)
         z = gather_parts(sum_parts(total, jnp.bfloat16))
     core = lax.axis_index("core")[None].astype(jnp.int32)
     return call(last_kernel, loadings, flops, (at, core), *z, a).T, factor

time: 171 us -> 170 us (level)
    pallas_call x6 -> x7, Pallas kernels: 32.8 us -> 32.5 us  [call(): pl.pallas_call(kernel, out_shape=out_shapes, in_specs=[pl.BlockSpec(memor...]
  transfers between devices with their start and end apart: 45 -> 45, of which waited for: 34 -> 32; matrix products, arithmetic and copies ran while one was open for 3% -> 3% of each run, Pallas kernels for 4% -> 4%
where the time goes in v18:
time: 170 us
  waiting for transfers between devices  80.6 us (47%)
  starting transfers between devices  45 us (26%)
  Pallas kernels  32.5 us (19%)
  local copies, waits for them, and re-layouts  5.55 us (3%)
  matrix products  3.83 us (2%)
  between operations  1.7 us (1%)
    ppermute x45, waiting for transfers between devices, from_xor(): return lax.ppermute(value, axis, [(i, i ^ offset) for i in range(size)])  80.6 us
    ppermute x45, starting transfers between devices, from_xor(): return lax.ppermute(value, axis, [(i, i ^ offset) for i in range(size)])  45 us
    pallas_call x7, Pallas kernels, call(): pl.pallas_call(kernel, out_shape=out_shapes, in_specs=[pl.BlockSpec(memor...  32.5 us
    dot_general x1, matrix products, per_device_transposed(): lax.dot_general(omega, states, (((0,), (1,)), ((), ())), preferred_elemen...  3.83 us
  transfers between devices with their start and end apart: 45, of which 32 were waited for; matrix products, arithmetic and copies ran while one was open for 3% of the time, Pallas kernels for 4%

profile of v18, /device:TPU:0, one launch (start us, length us, event | category | flops | bytes accessed | tf_op | source)
XLA Modules:
  0.0 169.5 jit_solution(18225223048327772936)
XLA Ops:
  2.1 3.1 %collective-permute-start.3 = (bf16[256,1024]{1,0:T(8,128)(2,1)S(1)}, bf16[256,1024]{1,0:T(8,128)(2,1)S(1)}, u32[]{:S(2)}, u32[]{:S(2)}) collective-permute-start(bf16[256,1024]{1,0:T(8,128)(2,1)S(1)} %get-tuple-element.44), channel_id=1, source_target_pairs={{0,4},{4,0},{8,12},{12,8},{1,5},{5,1},{9,13},{13,9},{2,6},{6,2},{1... | collective-permute-start | bytes 1572872 | tf_op jit(solution)/shard_map/ppermute | solution.py:242
  5.2 2.6 %collective-permute-start.2 = (bf16[256,1024]{1,0:T(8,128)(2,1)S(1)}, bf16[256,1024]{1,0:T(8,128)(2,1)S(1)}, u32[]{:S(2)}, u32[]{:S(2)}) collective-permute-start(bf16[256,1024]{1,0:T(8,128)(2,1)S(1)} %get-tuple-element.46), channel_id=1, source_target_pairs={{0,8},{4,12},{8,0},{12,4},{1,9},{5,13},{9,1},{13,5},{2,10},{6,14},... | collective-permute-start | bytes 1572872 | tf_op jit(solution)/shard_map/ppermute | solution.py:242
  8.5 3.8 %convolution_bitcast_fusion = f32[8,2,8,128]{3,2,1,0:T(8,128)S(1)} fusion(bf16[256,4096]{1,0:T(8,128)(2,1)} %param.3, s32[]{:T(128)S(6)} %xor.73, s32[4096]{0:T(1024)S(1)} %add_multiply_fusion), kind=kOutput, calls=%fused_computation | convolution fusion | flops 152043520 | bytes 2179076 | tf_op jit(solution)/shard_map/dot_general | solution.py:314
  12.8 20.8 %collective-permute-done = f32[2,64,128]{2,1,0:T(8,128)S(1)} collective-permute-done((f32[2,64,128]{2,1,0:T(8,128)S(1)}, f32[2,64,128]{2,1,0:T(8,128)S(1)}, u32[]{:S(2)}, u32[]{:S(2)}) %collective-permute-start) | collective-permute-done | bytes 65568 | tf_op jit(solution)/shard_map/ppermute | solution.py:242
  36.2 2.5 %collective-permute-start.5 = (bf16[128,1024]{1,0:T(8,128)(2,1)S(1)}, bf16[128,1024]{1,0:T(8,128)(2,1)S(1)}, u32[]{:S(2)}, u32[]{:S(2)}) collective-permute-start(bf16[128,1024]{1,0:T(8,128)(2,1)S(1)} %get-tuple-element.43), channel_id=1, source_target_pairs={{0,12},{4,8},{8,4},{12,0},{1,13},{5,9},{9,5},{13,1},{2,14},{6,10},... | collective-permute-start | bytes 786440 | tf_op jit(solution)/shard_map/ppermute | solution.py:242
  38.9 8.7 %collective-permute-done.4 = f32[4,64,128]{2,1,0:T(8,128)S(1)} collective-permute-done((f32[4,64,128]{2,1,0:T(8,128)S(1)}, f32[4,64,128]{2,1,0:T(8,128)S(1)}, u32[]{:S(2)}, u32[]{:S(2)}) %collective-permute-start.4) | collective-permute-done | bytes 131104 | tf_op jit(solution)/shard_map/ppermute | solution.py:242
  47.7 2.2 %collective-permute-start.7 = (bf16[128,1024]{1,0:T(8,128)(2,1)S(1)}, bf16[128,1024]{1,0:T(8,128)(2,1)S(1)}, u32[]{:S(2)}, u32[]{:S(2)}) collective-permute-start(bf16[128,1024]{1,0:T(8,128)(2,1)S(1)} %get-tuple-element.42), channel_id=1, source_target_pairs={{0,12},{4,8},{8,4},{12,0},{1,13},{5,9},{9,5},{13,1},{2,14},{6,10},... | collective-permute-start | bytes 786440 | tf_op jit(solution)/shard_map/ppermute | solution.py:242
  50.7 5.9 %shard_map.41 = (bf16[64,2048]{1,0:T(8,128)(2,1)S(1)}, f32[64,64]{1,0:T(8,128)S(1)}) custom-call(s32[8]{0:T(128)S(1)} %fusion.24.at_ref, f32[8,64,128]{2,1,0:T(8,128)S(1)} %pad_maximum_fusion.z_ref, f32[8,64,128]{2,1,0:T(8,128)S(1)} %collective-permute-done.6.other_ref), custom_call_target="tpu_custom_call" | custom-call | flops 402653184 | bytes 524288 | tf_op jit(solution)/shard_map/pallas_call | solution.py:225
  56.6 1.8 %collective-permute-done.7.refs_4_ = bf16[128,1024]{1,0:T(8,128)(2,1)S(1)} collective-permute-done((bf16[128,1024]{1,0:T(8,128)(2,1)S(1)}, bf16[128,1024]{1,0:T(8,128)(2,1)S(1)}, u32[]{:S(2)}, u32[]{:S(2)}) %collective-permute-start.7) | collective-permute-done | bytes 262176 | tf_op jit(solution)/shard_map/ppermute | solution.py:242
  60.3 2.1 %shard_map.42 = (bf16[2048,1024]{1,0:T(8,128)(2,1)S(1)}, f32[8,64,128]{2,1,0:T(8,128)S(1)}) custom-call(s32[8]{0:T(128)S(1)} %fusion.22.at_ref, bf16[64,2048]{1,0:T(8,128)(2,1)S(1)} %get-tuple-element.25.basis_ref, bf16[256,1024]{1,0:T(8,128)(2,1)S(1)} %get-tuple-element.26.refs_0_, bf16[256,1024]{1,0:T(8,128)(2,1)S(1)} %collective-permute-done.3.refs_1_, ...), custom_call_target="tpu_custom_call" | custom-call | flops 939524096 | bytes 4456448 | tf_op jit(solution)/shard_map/pallas_call | solution.py:225
  62.5 4.4 %collective-permute-start.13 = (f32[2,64,128]{2,1,0:T(8,128)S(1)}, f32[2,64,128]{2,1,0:T(8,128)S(1)}, u32[]{:S(2)}, u32[]{:S(2)}) collective-permute-start(f32[2,64,128]{2,1,0:T(8,128)S(1)} %get-tuple-element.47), channel_id=1, source_target_pairs={{0,5},{1,4},{4,1},{5,0},{8,13},{9,12},{12,9},{13,8},{2,7},{3,6},{6... | collective-permute-start | bytes 196616 | tf_op jit(solution)/shard_map/ppermute | solution.py:242
  69.2 1.9 %collective-permute-done.15 = f32[2,64,128]{2,1,0:T(8,128)S(1)} collective-permute-done((f32[2,64,128]{2,1,0:T(8,128)S(1)}, f32[2,64,128]{2,1,0:T(8,128)S(1)}, u32[]{:S(2)}, u32[]{:S(2)}) %collective-permute-start.15) | collective-permute-done | bytes 65568 | tf_op jit(solution)/shard_map/ppermute | solution.py:242
  73.3 4.7 %collective-permute-done.16 = f32[2,64,128]{2,1,0:T(8,128)S(1)} collective-permute-done((f32[2,64,128]{2,1,0:T(8,128)S(1)}, f32[2,64,128]{2,1,0:T(8,128)S(1)}, u32[]{:S(2)}, u32[]{:S(2)}) %collective-permute-start.16) | collective-permute-done | bytes 65568 | tf_op jit(solution)/shard_map/ppermute | solution.py:242
  79.4 2.2 %collective-permute-start.17 = (f32[2,64,128]{2,1,0:T(8,128)S(1)}, f32[2,64,128]{2,1,0:T(8,128)S(1)}, u32[]{:S(2)}, u32[]{:S(2)}) collective-permute-start(f32[2,64,128]{2,1,0:T(8,128)S(1)} %add.225), channel_id=1, source_target_pairs={{0,4},{1,5},{4,0},{5,1},{8,12},{9,13},{12,8},{13,9},{2,6},{3,7},{6... | collective-permute-start | bytes 196616 | tf_op jit(solution)/shard_map/ppermute | solution.py:242
  81.6 2.2 %collective-permute-done.17 = f32[2,64,128]{2,1,0:T(8,128)S(1)} collective-permute-done((f32[2,64,128]{2,1,0:T(8,128)S(1)}, f32[2,64,128]{2,1,0:T(8,128)S(1)}, u32[]{:S(2)}, u32[]{:S(2)}) %collective-permute-start.17) | collective-permute-done | bytes 65568 | tf_op jit(solution)/shard_map/ppermute | solution.py:242
  85.5 6.4 %shard_map.44 = f32[8,64,128]{2,1,0:T(8,128)S(1)} custom-call(s32[8]{0:T(128)S(1)} %fusion.22.at_ref, f32[8,64,128]{2,1,0:T(8,128)S(1)} %constant_dynamic-update-slice_fusion.z_ref, f32[8,64,128]{2,1,0:T(8,128)S(1)} %collective-permute-done.20.other_ref, bf16[2048,1024]{1,0:T(8,128)(2,1)S(1)} %get-tuple-element.32.a_ref, ...), custom_call_target="tpu_custom_call" | custom-call | flops 939524096 | bytes 6815744 | tf_op jit(solution)/shard_map/pallas_call | solution.py:225
  91.9 2.6 %collective-permute-start.21 = (bf16[2,64,128]{2,1,0:T(8,128)(2,1)S(1)}, bf16[2,64,128]{2,1,0:T(8,128)(2,1)S(1)}, u32[]{:S(2)}, u32[]{:S(2)}) collective-permute-start(bf16[2,64,128]{2,1,0:T(8,128)(2,1)S(1)} %get-tuple-element.56), channel_id=1, source_target_pairs={{0,5},{1,4},{4,1},{5,0},{8,13},{9,12},{12,9},{13,8},{2,7},{3,6},{6... | collective-permute-start | bytes 98312 | tf_op jit(solution)/shard_map/ppermute | solution.py:242
  96.8 1.6 collective-permute-done.23
  99.5 4.8 %collective-permute-done.24 = bf16[2,64,128]{2,1,0:T(8,128)(2,1)S(1)} collective-permute-done((bf16[2,64,128]{2,1,0:T(8,128)(2,1)S(1)}, bf16[2,64,128]{2,1,0:T(8,128)(2,1)S(1)}, u32[]{:S(2)}, u32[]{:S(2)}) %collective-permute-start.24) | collective-permute-done | bytes 32800 | tf_op jit(solution)/shard_map/ppermute | solution.py:242
  105.8 2.0 %collective-permute-start.25 = (bf16[2,64,128]{2,1,0:T(8,128)(2,1)S(1)}, bf16[2,64,128]{2,1,0:T(8,128)(2,1)S(1)}, u32[]{:S(2)}, u32[]{:S(2)}) collective-permute-start(bf16[2,64,128]{2,1,0:T(8,128)(2,1)S(1)} %add_convert_fusion.2), channel_id=1, source_target_pairs={{0,4},{1,5},{4,0},{5,1},{8,12},{9,13},{12,8},{13,9},{2,6},{3,7},{6... | collective-permute-start | bytes 98312 | tf_op jit(solution)/shard_map/ppermute | solution.py:242
  111.2 5.8 %shard_map.45 = f32[8,64,128]{2,1,0:T(8,128)S(1)} custom-call(s32[8]{0:T(128)S(1)} %fusion.22.at_ref, bf16[8,64,128]{2,1,0:T(8,128)(2,1)S(1)} %pad_maximum_fusion.2.z_ref, bf16[8,64,128]{2,1,0:T(8,128)(2,1)S(1)} %collective-permute-done.28.other_ref, bf16[2048,1024]{1,0:T(8,128)(2,1)S(1)} %get-tuple-element.32.a_ref, bf16[1024,1024]{1,0:T(8,128)(2,1)S(1)} %shard_map.43.turned_ref), custom_call_target="tpu_custom_call" | custom-call | flops 939524096 | bytes 6553600 | tf_op jit(solution)/shard_map/pallas_call | solution.py:225
  117.0 2.6 %collective-permute-start.29 = (bf16[2,64,128]{2,1,0:T(8,128)(2,1)S(1)}, bf16[2,64,128]{2,1,0:T(8,128)(2,1)S(1)}, u32[]{:S(2)}, u32[]{:S(2)}) collective-permute-start(bf16[2,64,128]{2,1,0:T(8,128)(2,1)S(1)} %get-tuple-element.53), channel_id=1, source_target_pairs={{0,5},{1,4},{4,1},{5,0},{8,13},{9,12},{12,9},{13,8},{2,7},{3,6},{6... | collective-permute-start | bytes 98312 | tf_op jit(solution)/shard_map/ppermute | solution.py:242
  121.9 1.6 collective-permute-done.31
  124.6 4.8 %collective-permute-done.32 = bf16[2,64,128]{2,1,0:T(8,128)(2,1)S(1)} collective-permute-done((bf16[2,64,128]{2,1,0:T(8,128)(2,1)S(1)}, bf16[2,64,128]{2,1,0:T(8,128)(2,1)S(1)}, u32[]{:S(2)}, u32[]{:S(2)}) %collective-permute-start.32) | collective-permute-done | bytes 32800 | tf_op jit(solution)/shard_map/ppermute | solution.py:242
  130.9 2.0 %collective-permute-start.33 = (bf16[2,64,128]{2,1,0:T(8,128)(2,1)S(1)}, bf16[2,64,128]{2,1,0:T(8,128)(2,1)S(1)}, u32[]{:S(2)}, u32[]{:S(2)}) collective-permute-start(bf16[2,64,128]{2,1,0:T(8,128)(2,1)S(1)} %add_convert_fusion.1), channel_id=1, source_target_pairs={{0,4},{1,5},{4,0},{5,1},{8,12},{9,13},{12,8},{13,9},{2,6},{3,7},{6... | collective-permute-start | bytes 98312 | tf_op jit(solution)/shard_map/ppermute | solution.py:242
  136.3 5.8 %shard_map.46 = f32[8,64,128]{2,1,0:T(8,128)S(1)} custom-call(s32[8]{0:T(128)S(1)} %fusion.22.at_ref, bf16[8,64,128]{2,1,0:T(8,128)(2,1)S(1)} %pad_maximum_fusion.3.z_ref, bf16[8,64,128]{2,1,0:T(8,128)(2,1)S(1)} %collective-permute-done.36.other_ref, bf16[2048,1024]{1,0:T(8,128)(2,1)S(1)} %get-tuple-element.32.a_ref, bf16[1024,1024]{1,0:T(8,128)(2,1)S(1)} %shard_map.43.turned_ref), custom_call_target="tpu_custom_call" | custom-call | flops 939524096 | bytes 6553600 | tf_op jit(solution)/shard_map/pallas_call | solution.py:225
  142.1 2.6 %collective-permute-start.37 = (bf16[2,64,128]{2,1,0:T(8,128)(2,1)S(1)}, bf16[2,64,128]{2,1,0:T(8,128)(2,1)S(1)}, u32[]{:S(2)}, u32[]{:S(2)}) collective-permute-start(bf16[2,64,128]{2,1,0:T(8,128)(2,1)S(1)} %get-tuple-element.50), channel_id=1, source_target_pairs={{0,5},{1,4},{4,1},{5,0},{8,13},{9,12},{12,9},{13,8},{2,7},{3,6},{6... | collective-permute-start | bytes 98312 | tf_op jit(solution)/shard_map/ppermute | solution.py:242
  147.0 1.6 collective-permute-done.39
  149.7 4.8 %collective-permute-done.40 = bf16[2,64,128]{2,1,0:T(8,128)(2,1)S(1)} collective-permute-done((bf16[2,64,128]{2,1,0:T(8,128)(2,1)S(1)}, bf16[2,64,128]{2,1,0:T(8,128)(2,1)S(1)}, u32[]{:S(2)}, u32[]{:S(2)}) %collective-permute-start.40) | collective-permute-done | bytes 32800 | tf_op jit(solution)/shard_map/ppermute | solution.py:242
  156.0 2.0 %collective-permute-start.41 = (bf16[2,64,128]{2,1,0:T(8,128)(2,1)S(1)}, bf16[2,64,128]{2,1,0:T(8,128)(2,1)S(1)}, u32[]{:S(2)}, u32[]{:S(2)}) collective-permute-start(bf16[2,64,128]{2,1,0:T(8,128)(2,1)S(1)} %add_convert_fusion), channel_id=1, source_target_pairs={{0,4},{1,5},{4,0},{5,1},{8,12},{9,13},{12,8},{13,9},{2,6},{3,7},{6... | collective-permute-start | bytes 98312 | tf_op jit(solution)/shard_map/ppermute | solution.py:242
  161.4 2.2 %copy-done.1 = bf16[2048,1024]{1,0:T(8,128)(2,1)S(1)} copy-done((bf16[2048,1024]{1,0:T(8,128)(2,1)S(1)}, bf16[2048,1024]{1,0:T(8,128)(2,1)}, u32[]{:S(2)}) %copy-start.1) | copy-done | bytes 4194328
  163.6 6.0 %shard_map.47 = f32[64,512]{1,0:T(8,128)} custom-call(s32[8]{0:T(128)S(1)} %fusion.22.at_ref, s32[1]{0:T(128)} %bitcast.core_ref, bf16[8,64,128]{2,1,0:T(8,128)(2,1)S(1)} %pad_maximum_fusion.4.z_ref, bf16[8,64,128]{2,1,0:T(8,128)(2,1)S(1)} %collective-permute-done.44.other_ref, bf16[2048,1024]{1,0:T(8,128)(2,1)S(1)} %copy-done.1), custom_call_target="tpu_custom_call" | custom-call | flops 939524096 | bytes 4456448 | tf_op jit(solution)/shard_map/pallas_call | solution.py:225
  (103 shorter events, 39.7 us)
Async XLA Ops:
  2.1 36.7 %collective-permute-start.3 = (bf16[256,1024]{1,0:T(8,128)(2,1)S(1)}, bf16[256,1024]{1,0:T(8,128)(2,1)S(1)}, u32[]{:S(2)}, u32[]{:S(2)}) collective-permute-start(bf16[256,1024]{1,0:T(8,128)(2,1)S(1)} %get-tuple-element.44), channel_id=1, source_target_pairs={{0,4},{4,0},{8,12},{12,8},{1,5},{5,1},{9,13},{13,9},{2,6},{6,2},{1... | collective-permute-start | bytes 1572872 | tf_op jit(solution)/shard_map/ppermute | solution.py:242
  5.2 33.6 %collective-permute-start.2 = (bf16[256,1024]{1,0:T(8,128)(2,1)S(1)}, bf16[256,1024]{1,0:T(8,128)(2,1)S(1)}, u32[]{:S(2)}, u32[]{:S(2)}) collective-permute-start(bf16[256,1024]{1,0:T(8,128)(2,1)S(1)} %get-tuple-element.46), channel_id=1, source_target_pairs={{0,8},{4,12},{8,0},{12,4},{1,9},{5,13},{9,1},{13,5},{2,10},{6,14},... | collective-permute-start | bytes 1572872 | tf_op jit(solution)/shard_map/ppermute | solution.py:242
  12.4 21.2 %collective-permute-start = (f32[2,64,128]{2,1,0:T(8,128)S(1)}, f32[2,64,128]{2,1,0:T(8,128)S(1)}, u32[]{:S(2)}, u32[]{:S(2)}) collective-permute-start(f32[2,64,128]{2,1,0:T(8,128)S(1)} %bitcast.16), channel_id=1, source_target_pairs={{0,8},{4,12},{8,0},{12,4},{1,9},{5,13},{9,1},{13,5},{2,10},{6,14},... | collective-permute-start | bytes 196616 | tf_op jit(solution)/shard_map/ppermute | solution.py:242
  33.6 5.2 %collective-permute-start.1 = (f32[4,64,128]{2,1,0:T(8,128)S(1)}, f32[4,64,128]{2,1,0:T(8,128)S(1)}, u32[]{:S(2)}, u32[]{:S(2)}) collective-permute-start(f32[4,64,128]{2,1,0:T(8,128)S(1)} %pad_maximum_fusion.1), channel_id=1, source_target_pairs={{0,1},{1,0},{2,3},{3,2},{4,5},{5,4},{6,7},{7,6},{8,9},{9,8},{10,11... | collective-permute-start | bytes 393224 | tf_op jit(solution)/shard_map/ppermute | solution.py:242
  36.2 11.4 %collective-permute-start.5 = (bf16[128,1024]{1,0:T(8,128)(2,1)S(1)}, bf16[128,1024]{1,0:T(8,128)(2,1)S(1)}, u32[]{:S(2)}, u32[]{:S(2)}) collective-permute-start(bf16[128,1024]{1,0:T(8,128)(2,1)S(1)} %get-tuple-element.43), channel_id=1, source_target_pairs={{0,12},{4,8},{8,4},{12,0},{1,13},{5,9},{9,5},{13,1},{2,14},{6,10},... | collective-permute-start | bytes 786440 | tf_op jit(solution)/shard_map/ppermute | solution.py:242
  38.8 8.8 %collective-permute-start.4 = (f32[4,64,128]{2,1,0:T(8,128)S(1)}, f32[4,64,128]{2,1,0:T(8,128)S(1)}, u32[]{:S(2)}, u32[]{:S(2)}) collective-permute-start(f32[4,64,128]{2,1,0:T(8,128)S(1)} %add.217), channel_id=1, source_target_pairs={{0,4},{4,0},{8,12},{12,8},{1,5},{5,1},{9,13},{13,9},{2,6},{6,2},{1... | collective-permute-start | bytes 393224 | tf_op jit(solution)/shard_map/ppermute | solution.py:242
  47.7 10.6 %collective-permute-start.7 = (bf16[128,1024]{1,0:T(8,128)(2,1)S(1)}, bf16[128,1024]{1,0:T(8,128)(2,1)S(1)}, u32[]{:S(2)}, u32[]{:S(2)}) collective-permute-start(bf16[128,1024]{1,0:T(8,128)(2,1)S(1)} %get-tuple-element.42), channel_id=1, source_target_pairs={{0,12},{4,8},{8,4},{12,0},{1,13},{5,9},{9,5},{13,1},{2,14},{6,10},... | collective-permute-start | bytes 786440 | tf_op jit(solution)/shard_map/ppermute | solution.py:242
  50.0 8.9 %collective-permute-start.8 = (bf16[256,1024]{1,0:T(8,128)(2,1)S(1)}, bf16[256,1024]{1,0:T(8,128)(2,1)S(1)}, u32[]{:S(2)}, u32[]{:S(2)}) collective-permute-start(bf16[256,1024]{1,0:T(8,128)(2,1)S(1)} %get-tuple-element.26.refs_0_), channel_id=1, source_target_pairs={{0,2},{2,0},{1,3},{3,1},{4,6},{6,4},{5,7},{7,5},{8,10},{10,8},{9,1... | collective-permute-start | bytes 1572872 | tf_op jit(solution)/shard_map/ppermute | solution.py:242
  50.1 8.8 %collective-permute-start.9 = (bf16[256,1024]{1,0:T(8,128)(2,1)S(1)}, bf16[256,1024]{1,0:T(8,128)(2,1)S(1)}, u32[]{:S(2)}, u32[]{:S(2)}) collective-permute-start(bf16[256,1024]{1,0:T(8,128)(2,1)S(1)} %collective-permute-done.3.refs_1_), channel_id=1, source_target_pairs={{0,2},{2,0},{1,3},{3,1},{4,6},{6,4},{5,7},{7,5},{8,10},{10,8},{9,1... | collective-permute-start | bytes 1572872 | tf_op jit(solution)/shard_map/ppermute | solution.py:242
  50.5 8.5 %collective-permute-start.10 = (bf16[256,1024]{1,0:T(8,128)(2,1)S(1)}, bf16[256,1024]{1,0:T(8,128)(2,1)S(1)}, u32[]{:S(2)}, u32[]{:S(2)}) collective-permute-start(bf16[256,1024]{1,0:T(8,128)(2,1)S(1)} %collective-permute-done.2.refs_2_), channel_id=1, source_target_pairs={{0,2},{2,0},{1,3},{3,1},{4,6},{6,4},{5,7},{7,5},{8,10},{10,8},{9,1... | collective-permute-start | bytes 1572872 | tf_op jit(solution)/shard_map/ppermute | solution.py:242
  62.5 6.8 %collective-permute-start.13 = (f32[2,64,128]{2,1,0:T(8,128)S(1)}, f32[2,64,128]{2,1,0:T(8,128)S(1)}, u32[]{:S(2)}, u32[]{:S(2)}) collective-permute-start(f32[2,64,128]{2,1,0:T(8,128)S(1)} %get-tuple-element.47), channel_id=1, source_target_pairs={{0,5},{1,4},{4,1},{5,0},{8,13},{9,12},{12,9},{13,8},{2,7},{3,6},{6... | collective-permute-start | bytes 196616 | tf_op jit(solution)/shard_map/ppermute | solution.py:242
  66.8 4.3 %collective-permute-start.15 = (f32[2,64,128]{2,1,0:T(8,128)S(1)}, f32[2,64,128]{2,1,0:T(8,128)S(1)}, u32[]{:S(2)}, u32[]{:S(2)}) collective-permute-start(f32[2,64,128]{2,1,0:T(8,128)S(1)} %get-tuple-element.48), channel_id=1, source_target_pairs={{0,1},{1,0},{4,5},{5,4},{8,9},{9,8},{12,13},{13,12},{2,3},{3,2},{6... | collective-permute-start | bytes 196616 | tf_op jit(solution)/shard_map/ppermute | solution.py:242
  68.3 4.3 %collective-permute-start.14 = (f32[2,64,128]{2,1,0:T(8,128)S(1)}, f32[2,64,128]{2,1,0:T(8,128)S(1)}, u32[]{:S(2)}, u32[]{:S(2)}) collective-permute-start(f32[2,64,128]{2,1,0:T(8,128)S(1)} %get-tuple-element.49), channel_id=1, source_target_pairs={{0,4},{1,5},{4,0},{5,1},{8,12},{9,13},{12,8},{13,9},{2,6},{3,7},{6... | collective-permute-start | bytes 196616 | tf_op jit(solution)/shard_map/ppermute | solution.py:242
  72.6 5.4 %collective-permute-start.16 = (f32[2,64,128]{2,1,0:T(8,128)S(1)}, f32[2,64,128]{2,1,0:T(8,128)S(1)}, u32[]{:S(2)}, u32[]{:S(2)}) collective-permute-start(f32[2,64,128]{2,1,0:T(8,128)S(1)} %add_add_fusion), channel_id=1, source_target_pairs={{0,8},{4,12},{8,0},{12,4},{1,9},{5,13},{9,1},{13,5},{2,10},{6,14},... | collective-permute-start | bytes 196616 | tf_op jit(solution)/shard_map/ppermute | solution.py:242
  78.0 5.8 %collective-permute-start.19 = (f32[2,64,128]{2,1,0:T(8,128)S(1)}, f32[2,64,128]{2,1,0:T(8,128)S(1)}, u32[]{:S(2)}, u32[]{:S(2)}) collective-permute-start(f32[2,64,128]{2,1,0:T(8,128)S(1)} %add.225), channel_id=1, source_target_pairs={{0,5},{1,4},{4,1},{5,0},{8,13},{9,12},{12,9},{13,8},{2,7},{3,6},{6... | collective-permute-start | bytes 196616 | tf_op jit(solution)/shard_map/ppermute | solution.py:242
  78.7 5.1 %collective-permute-start.18 = (f32[2,64,128]{2,1,0:T(8,128)S(1)}, f32[2,64,128]{2,1,0:T(8,128)S(1)}, u32[]{:S(2)}, u32[]{:S(2)}) collective-permute-start(f32[2,64,128]{2,1,0:T(8,128)S(1)} %add.225), channel_id=1, source_target_pairs={{0,1},{1,0},{4,5},{5,4},{8,9},{9,8},{12,13},{13,12},{2,3},{3,2},{6... | collective-permute-start | bytes 196616 | tf_op jit(solution)/shard_map/ppermute | solution.py:242
  79.4 4.4 %collective-permute-start.17 = (f32[2,64,128]{2,1,0:T(8,128)S(1)}, f32[2,64,128]{2,1,0:T(8,128)S(1)}, u32[]{:S(2)}, u32[]{:S(2)}) collective-permute-start(f32[2,64,128]{2,1,0:T(8,128)S(1)} %add.225), channel_id=1, source_target_pairs={{0,4},{1,5},{4,0},{5,1},{8,12},{9,13},{12,8},{13,9},{2,6},{3,7},{6... | collective-permute-start | bytes 196616 | tf_op jit(solution)/shard_map/ppermute | solution.py:242
  91.9 4.9 %collective-permute-start.21 = (bf16[2,64,128]{2,1,0:T(8,128)(2,1)S(1)}, bf16[2,64,128]{2,1,0:T(8,128)(2,1)S(1)}, u32[]{:S(2)}, u32[]{:S(2)}) collective-permute-start(bf16[2,64,128]{2,1,0:T(8,128)(2,1)S(1)} %get-tuple-element.56), channel_id=1, source_target_pairs={{0,5},{1,4},{4,1},{5,0},{8,13},{9,12},{12,9},{13,8},{2,7},{3,6},{6... | collective-permute-start | bytes 98312 | tf_op jit(solution)/shard_map/ppermute | solution.py:242
  94.5 3.9 %collective-permute-start.23 = (bf16[2,64,128]{2,1,0:T(8,128)(2,1)S(1)}, bf16[2,64,128]{2,1,0:T(8,128)(2,1)S(1)}, u32[]{:S(2)}, u32[]{:S(2)}) collective-permute-start(bf16[2,64,128]{2,1,0:T(8,128)(2,1)S(1)} %get-tuple-element.57), channel_id=1, source_target_pairs={{0,1},{1,0},{4,5},{5,4},{8,9},{9,8},{12,13},{13,12},{2,3},{3,2},{6... | collective-permute-start | bytes 98312 | tf_op jit(solution)/shard_map/ppermute | solution.py:242
  95.5 3.9 %collective-permute-start.22 = (bf16[2,64,128]{2,1,0:T(8,128)(2,1)S(1)}, bf16[2,64,128]{2,1,0:T(8,128)(2,1)S(1)}, u32[]{:S(2)}, u32[]{:S(2)}) collective-permute-start(bf16[2,64,128]{2,1,0:T(8,128)(2,1)S(1)} %get-tuple-element.58), channel_id=1, source_target_pairs={{0,4},{1,5},{4,0},{5,1},{8,12},{9,13},{12,8},{13,9},{2,6},{3,7},{6... | collective-permute-start | bytes 98312 | tf_op jit(solution)/shard_map/ppermute | solution.py:242
  99.4 4.9 %collective-permute-start.24 = (bf16[2,64,128]{2,1,0:T(8,128)(2,1)S(1)}, bf16[2,64,128]{2,1,0:T(8,128)(2,1)S(1)}, u32[]{:S(2)}, u32[]{:S(2)}) collective-permute-start(bf16[2,64,128]{2,1,0:T(8,128)(2,1)S(1)} %fusion.21), channel_id=1, source_target_pairs={{0,8},{4,12},{8,0},{12,4},{1,9},{5,13},{9,1},{13,5},{2,10},{6,14},... | collective-permute-start | bytes 98312 | tf_op jit(solution)/shard_map/ppermute | solution.py:242
  104.3 5.0 %collective-permute-start.27 = (bf16[2,64,128]{2,1,0:T(8,128)(2,1)S(1)}, bf16[2,64,128]{2,1,0:T(8,128)(2,1)S(1)}, u32[]{:S(2)}, u32[]{:S(2)}) collective-permute-start(bf16[2,64,128]{2,1,0:T(8,128)(2,1)S(1)} %add_convert_fusion.2), channel_id=1, source_target_pairs={{0,5},{1,4},{4,1},{5,0},{8,13},{9,12},{12,9},{13,8},{2,7},{3,6},{6... | collective-permute-start | bytes 98312 | tf_op jit(solution)/shard_map/ppermute | solution.py:242
  105.0 4.3 %collective-permute-start.26 = (bf16[2,64,128]{2,1,0:T(8,128)(2,1)S(1)}, bf16[2,64,128]{2,1,0:T(8,128)(2,1)S(1)}, u32[]{:S(2)}, u32[]{:S(2)}) collective-permute-start(bf16[2,64,128]{2,1,0:T(8,128)(2,1)S(1)} %add_convert_fusion.2), channel_id=1, source_target_pairs={{0,1},{1,0},{4,5},{5,4},{8,9},{9,8},{12,13},{13,12},{2,3},{3,2},{6... | collective-permute-start | bytes 98312 | tf_op jit(solution)/shard_map/ppermute | solution.py:242
  117.0 4.9 %collective-permute-start.29 = (bf16[2,64,128]{2,1,0:T(8,128)(2,1)S(1)}, bf16[2,64,128]{2,1,0:T(8,128)(2,1)S(1)}, u32[]{:S(2)}, u32[]{:S(2)}) collective-permute-start(bf16[2,64,128]{2,1,0:T(8,128)(2,1)S(1)} %get-tuple-element.53), channel_id=1, source_target_pairs={{0,5},{1,4},{4,1},{5,0},{8,13},{9,12},{12,9},{13,8},{2,7},{3,6},{6... | collective-permute-start | bytes 98312 | tf_op jit(solution)/shard_map/ppermute | solution.py:242
  119.6 3.9 %collective-permute-start.31 = (bf16[2,64,128]{2,1,0:T(8,128)(2,1)S(1)}, bf16[2,64,128]{2,1,0:T(8,128)(2,1)S(1)}, u32[]{:S(2)}, u32[]{:S(2)}) collective-permute-start(bf16[2,64,128]{2,1,0:T(8,128)(2,1)S(1)} %get-tuple-element.54), channel_id=1, source_target_pairs={{0,1},{1,0},{4,5},{5,4},{8,9},{9,8},{12,13},{13,12},{2,3},{3,2},{6... | collective-permute-start | bytes 98312 | tf_op jit(solution)/shard_map/ppermute | solution.py:242
  124.5 4.9 %collective-permute-start.32 = (bf16[2,64,128]{2,1,0:T(8,128)(2,1)S(1)}, bf16[2,64,128]{2,1,0:T(8,128)(2,1)S(1)}, u32[]{:S(2)}, u32[]{:S(2)}) collective-permute-start(bf16[2,64,128]{2,1,0:T(8,128)(2,1)S(1)} %fusion.18), channel_id=1, source_target_pairs={{0,8},{4,12},{8,0},{12,4},{1,9},{5,13},{9,1},{13,5},{2,10},{6,14},... | collective-permute-start | bytes 98312 | tf_op jit(solution)/shard_map/ppermute | solution.py:242
  129.4 5.0 %collective-permute-start.35 = (bf16[2,64,128]{2,1,0:T(8,128)(2,1)S(1)}, bf16[2,64,128]{2,1,0:T(8,128)(2,1)S(1)}, u32[]{:S(2)}, u32[]{:S(2)}) collective-permute-start(bf16[2,64,128]{2,1,0:T(8,128)(2,1)S(1)} %add_convert_fusion.1), channel_id=1, source_target_pairs={{0,5},{1,4},{4,1},{5,0},{8,13},{9,12},{12,9},{13,8},{2,7},{3,6},{6... | collective-permute-start | bytes 98312 | tf_op jit(solution)/shard_map/ppermute | solution.py:242
  130.1 4.3 %collective-permute-start.34 = (bf16[2,64,128]{2,1,0:T(8,128)(2,1)S(1)}, bf16[2,64,128]{2,1,0:T(8,128)(2,1)S(1)}, u32[]{:S(2)}, u32[]{:S(2)}) collective-permute-start(bf16[2,64,128]{2,1,0:T(8,128)(2,1)S(1)} %add_convert_fusion.1), channel_id=1, source_target_pairs={{0,1},{1,0},{4,5},{5,4},{8,9},{9,8},{12,13},{13,12},{2,3},{3,2},{6... | collective-permute-start | bytes 98312 | tf_op jit(solution)/shard_map/ppermute | solution.py:242
  142.1 4.9 %collective-permute-start.37 = (bf16[2,64,128]{2,1,0:T(8,128)(2,1)S(1)}, bf16[2,64,128]{2,1,0:T(8,128)(2,1)S(1)}, u32[]{:S(2)}, u32[]{:S(2)}) collective-permute-start(bf16[2,64,128]{2,1,0:T(8,128)(2,1)S(1)} %get-tuple-element.50), channel_id=1, source_target_pairs={{0,5},{1,4},{4,1},{5,0},{8,13},{9,12},{12,9},{13,8},{2,7},{3,6},{6... | collective-permute-start | bytes 98312 | tf_op jit(solution)/shard_map/ppermute | solution.py:242
  149.6 4.9 %collective-permute-start.40 = (bf16[2,64,128]{2,1,0:T(8,128)(2,1)S(1)}, bf16[2,64,128]{2,1,0:T(8,128)(2,1)S(1)}, u32[]{:S(2)}, u32[]{:S(2)}) collective-permute-start(bf16[2,64,128]{2,1,0:T(8,128)(2,1)S(1)} %fusion.15), channel_id=1, source_target_pairs={{0,8},{4,12},{8,0},{12,4},{1,9},{5,13},{9,1},{13,5},{2,10},{6,14},... | collective-permute-start | bytes 98312 | tf_op jit(solution)/shard_map/ppermute | solution.py:242
  154.5 5.0 %collective-permute-start.43 = (bf16[2,64,128]{2,1,0:T(8,128)(2,1)S(1)}, bf16[2,64,128]{2,1,0:T(8,128)(2,1)S(1)}, u32[]{:S(2)}, u32[]{:S(2)}) collective-permute-start(bf16[2,64,128]{2,1,0:T(8,128)(2,1)S(1)} %add_convert_fusion), channel_id=1, source_target_pairs={{0,5},{1,4},{4,1},{5,0},{8,13},{9,12},{12,9},{13,8},{2,7},{3,6},{6... | collective-permute-start | bytes 98312 | tf_op jit(solution)/shard_map/ppermute | solution.py:242
  155.2 4.3 %collective-permute-start.42 = (bf16[2,64,128]{2,1,0:T(8,128)(2,1)S(1)}, bf16[2,64,128]{2,1,0:T(8,128)(2,1)S(1)}, u32[]{:S(2)}, u32[]{:S(2)}) collective-permute-start(bf16[2,64,128]{2,1,0:T(8,128)(2,1)S(1)} %add_convert_fusion), channel_id=1, source_target_pairs={{0,1},{1,0},{4,5},{5,4},{8,9},{9,8},{12,13},{13,12},{2,3},{3,2},{6... | collective-permute-start | bytes 98312 | tf_op jit(solution)/shard_map/ppermute | solution.py:242
  (15 other events, 111.8 us)

commit v19 on v18

--- a/solution.py
+++ b/solution.py
@@ -298,11 +298,14 @@
     z_at, col = lax.axis_index("z"), lax.axis_index("col")
     pieces = {}
 
-    def move(slab, offset, part=0, parts=1):
+    def block(offset, part=0, parts=1):
         rows = rows_local // parts
         start = (part * rows, (z_at ^ offset) * cols)
-        block = lax.dynamic_slice(slab, start, (rows, cols))
-        pieces[offset, part] = from_xor(block, ("z",), offset) if offset else block
+        return lax.dynamic_slice(states, start, (rows, cols))
+
+    def move(blocks):
+        for name, value in blocks.items():
+            pieces[name] = from_xor(value, ("z",), name[0]) if name[0] else value
 
     def hold(value, names):
         value, moved = lax.optimization_barrier((value, [pieces[name] for name in names]))
@@ -317,14 +320,12 @@
     z = z.reshape(RANK, n_col, chunk).transpose(1, 0, 2)
     z_bits = bits(n_z)[::-1]
     far = z_bits[0]
-    for offset in [0, far, *range(1, far)]:
-        move(states, offset)
+    move({(offset, 0): block(offset) for offset in [0, far, *range(1, far)]})
     first = list(pieces)
+    late = {(o, part): block(o, part, 2) for o in range(far + 1, n_z) for part in range(2)}
     z = jnp.concatenate([z, from_xor(z, ("z",), far)])
-    z, slab = lax.optimization_barrier((z, states))
-    for offset in range(far + 1, n_z):
-        move(slab, offset, 0, 2)
-        move(slab, offset, 1, 2)
+    z, late = lax.optimization_barrier((z, late))
+    move(late)
     for bit in bits(n_col):
         z = z + from_xor(z, ("col",), bit)
     z = hold(z, first)
@@ -337,7 +338,7 @@
     digits = [("col", bit, True) for bit in bits(n_col)[::-1]]
     digits += [("z", 1, True)] if n_z > 2 else []
     at = chunk_places(digits + [("z", bit, False) for bit in far_bits()])
-    late = [name for name in pieces if name[0] > far]
+    late = list(late)
     others = {name: from_xor(pieces[name], ("core",), 1) for name in first}
 
     f32 = jnp.float32

time: 170 us -> 169 us (level)
  waiting for transfers between devices: 80.6 us -> 78.6 us
    ppermute x45, waiting for transfers between devices: 80.6 us -> 78.6 us  [from_xor(): return lax.ppermute(value, axis, [(i, i ^ offset) for i in range(size)])]
  transfers between devices with their start and end apart: 45 -> 45, of which waited for: 32 -> 33; matrix products, arithmetic and copies ran while one was open for 3% -> 3% of each run, Pallas kernels for 4% -> 4%
where the time goes in v19:
time: 169 us; the launch traced here: 168 us
  waiting for transfers between devices  78.6 us (47%)
  starting transfers between devices  45.9 us (27%)
  Pallas kernels  32.5 us (19%)
  local copies, waits for them, and re-layouts  5.55 us (3%)
  matrix products  3.83 us (2%)
    ppermute x45, waiting for transfers between devices, from_xor(): return lax.ppermute(value, axis, [(i, i ^ offset) for i in range(size)])  78.6 us
    ppermute x45, starting transfers between devices, from_xor(): return lax.ppermute(value, axis, [(i, i ^ offset) for i in range(size)])  45.9 us
    pallas_call x7, Pallas kernels, call(): pl.pallas_call(kernel, out_shape=out_shapes, in_specs=[pl.BlockSpec(memor...  32.5 us
    dot_general x1, matrix products, per_device_transposed(): lax.dot_general(omega, states, (((0,), (1,)), ((), ())), preferred_elemen...  3.83 us
  transfers between devices with their start and end apart: 45, of which 33 were waited for; matrix products, arithmetic and copies ran while one was open for 3% of the time, Pallas kernels for 4%

profile of v19, /device:TPU:0, one launch (start us, length us, event | category | flops | bytes accessed | tf_op | source)
XLA Modules:
  0.0 168.4 jit_solution(5801735217717452690)
XLA Ops:
  2.1 3.1 %collective-permute-start.3 = (bf16[256,1024]{1,0:T(8,128)(2,1)S(1)}, bf16[256,1024]{1,0:T(8,128)(2,1)S(1)}, u32[]{:S(2)}, u32[]{:S(2)}) collective-permute-start(bf16[256,1024]{1,0:T(8,128)(2,1)S(1)} %get-tuple-element.44), channel_id=1, source_target_pairs={{0,4},{4,0},{8,12},{12,8},{1,5},{5,1},{9,13},{13,9},{2,6},{6,2},{1... | collective-permute-start | bytes 1572872 | tf_op jit(solution)/shard_map/ppermute | solution.py:242
  5.2 2.6 %collective-permute-start.2 = (bf16[256,1024]{1,0:T(8,128)(2,1)S(1)}, bf16[256,1024]{1,0:T(8,128)(2,1)S(1)}, u32[]{:S(2)}, u32[]{:S(2)}) collective-permute-start(bf16[256,1024]{1,0:T(8,128)(2,1)S(1)} %get-tuple-element.46), channel_id=1, source_target_pairs={{0,8},{4,12},{8,0},{12,4},{1,9},{5,13},{9,1},{13,5},{2,10},{6,14},... | collective-permute-start | bytes 1572872 | tf_op jit(solution)/shard_map/ppermute | solution.py:242
  8.5 3.8 %convolution_bitcast_fusion = f32[8,2,8,128]{3,2,1,0:T(8,128)S(1)} fusion(bf16[256,4096]{1,0:T(8,128)(2,1)} %param.3, s32[]{:T(128)S(6)} %xor.73, s32[4096]{0:T(1024)S(1)} %add_multiply_fusion), kind=kOutput, calls=%fused_computation | convolution fusion | flops 152043520 | bytes 2179076 | tf_op jit(solution)/shard_map/dot_general | solution.py:317
  13.8 19.8 %collective-permute-done = f32[2,64,128]{2,1,0:T(8,128)S(1)} collective-permute-done((f32[2,64,128]{2,1,0:T(8,128)S(1)}, f32[2,64,128]{2,1,0:T(8,128)S(1)}, u32[]{:S(2)}, u32[]{:S(2)}) %collective-permute-start) | collective-permute-done | bytes 65568 | tf_op jit(solution)/shard_map/ppermute | solution.py:242
  33.6 1.6 collective-permute-start.1
  35.2 3.0 %collective-permute-start.5 = (bf16[128,1024]{1,0:T(8,128)(2,1)S(1)}, bf16[128,1024]{1,0:T(8,128)(2,1)S(1)}, u32[]{:S(2)}, u32[]{:S(2)}) collective-permute-start(bf16[128,1024]{1,0:T(8,128)(2,1)S(1)} %get-tuple-element.22), channel_id=1, source_target_pairs={{0,12},{4,8},{8,4},{12,0},{1,13},{5,9},{9,5},{13,1},{2,14},{6,10},... | collective-permute-start | bytes 786440 | tf_op jit(solution)/shard_map/ppermute | solution.py:242
  38.8 7.7 %collective-permute-done.4 = f32[4,64,128]{2,1,0:T(8,128)S(1)} collective-permute-done((f32[4,64,128]{2,1,0:T(8,128)S(1)}, f32[4,64,128]{2,1,0:T(8,128)S(1)}, u32[]{:S(2)}, u32[]{:S(2)}) %collective-permute-start.4) | collective-permute-done | bytes 131104 | tf_op jit(solution)/shard_map/ppermute | solution.py:242
  46.6 2.5 %collective-permute-start.7 = (bf16[128,1024]{1,0:T(8,128)(2,1)S(1)}, bf16[128,1024]{1,0:T(8,128)(2,1)S(1)}, u32[]{:S(2)}, u32[]{:S(2)}) collective-permute-start(bf16[128,1024]{1,0:T(8,128)(2,1)S(1)} %get-tuple-element.26), channel_id=1, source_target_pairs={{0,12},{4,8},{8,4},{12,0},{1,13},{5,9},{9,5},{13,1},{2,14},{6,10},... | collective-permute-start | bytes 786440 | tf_op jit(solution)/shard_map/ppermute | solution.py:242
  49.9 5.9 %shard_map.41 = (bf16[64,2048]{1,0:T(8,128)(2,1)S(1)}, f32[64,64]{1,0:T(8,128)S(1)}) custom-call(s32[8]{0:T(128)S(1)} %fusion.24.at_ref, f32[8,64,128]{2,1,0:T(8,128)S(1)} %pad_maximum_fusion.z_ref, f32[8,64,128]{2,1,0:T(8,128)S(1)} %collective-permute-done.6.other_ref), custom_call_target="tpu_custom_call" | custom-call | flops 402653184 | bytes 524288 | tf_op jit(solution)/shard_map/pallas_call | solution.py:225
  59.2 2.1 %shard_map.42 = (bf16[2048,1024]{1,0:T(8,128)(2,1)S(1)}, f32[8,64,128]{2,1,0:T(8,128)S(1)}) custom-call(s32[8]{0:T(128)S(1)} %fusion.22.at_ref, bf16[64,2048]{1,0:T(8,128)(2,1)S(1)} %get-tuple-element.27.basis_ref, bf16[256,1024]{1,0:T(8,128)(2,1)S(1)} %get-tuple-element.28.refs_0_, bf16[256,1024]{1,0:T(8,128)(2,1)S(1)} %collective-permute-done.3.refs_1_, ...), custom_call_target="tpu_custom_call" | custom-call | flops 939524096 | bytes 4456448 | tf_op jit(solution)/shard_map/pallas_call | solution.py:225
  61.3 4.4 %collective-permute-start.13 = (f32[2,64,128]{2,1,0:T(8,128)S(1)}, f32[2,64,128]{2,1,0:T(8,128)S(1)}, u32[]{:S(2)}, u32[]{:S(2)}) collective-permute-start(f32[2,64,128]{2,1,0:T(8,128)S(1)} %get-tuple-element.49), channel_id=1, source_target_pairs={{0,5},{1,4},{4,1},{5,0},{8,13},{9,12},{12,9},{13,8},{2,7},{3,6},{6... | collective-permute-start | bytes 196616 | tf_op jit(solution)/shard_map/ppermute | solution.py:242
  68.1 1.9 %collective-permute-done.15 = f32[2,64,128]{2,1,0:T(8,128)S(1)} collective-permute-done((f32[2,64,128]{2,1,0:T(8,128)S(1)}, f32[2,64,128]{2,1,0:T(8,128)S(1)}, u32[]{:S(2)}, u32[]{:S(2)}) %collective-permute-start.15) | collective-permute-done | bytes 65568 | tf_op jit(solution)/shard_map/ppermute | solution.py:242
  72.2 4.7 %collective-permute-done.16 = f32[2,64,128]{2,1,0:T(8,128)S(1)} collective-permute-done((f32[2,64,128]{2,1,0:T(8,128)S(1)}, f32[2,64,128]{2,1,0:T(8,128)S(1)}, u32[]{:S(2)}, u32[]{:S(2)}) %collective-permute-start.16) | collective-permute-done | bytes 65568 | tf_op jit(solution)/shard_map/ppermute | solution.py:242
  78.3 2.2 %collective-permute-start.17 = (f32[2,64,128]{2,1,0:T(8,128)S(1)}, f32[2,64,128]{2,1,0:T(8,128)S(1)}, u32[]{:S(2)}, u32[]{:S(2)}) collective-permute-start(f32[2,64,128]{2,1,0:T(8,128)S(1)} %add.225), channel_id=1, source_target_pairs={{0,4},{1,5},{4,0},{5,1},{8,12},{9,13},{12,8},{13,9},{2,6},{3,7},{6... | collective-permute-start | bytes 196616 | tf_op jit(solution)/shard_map/ppermute | solution.py:242
  80.5 2.2 %collective-permute-done.17 = f32[2,64,128]{2,1,0:T(8,128)S(1)} collective-permute-done((f32[2,64,128]{2,1,0:T(8,128)S(1)}, f32[2,64,128]{2,1,0:T(8,128)S(1)}, u32[]{:S(2)}, u32[]{:S(2)}) %collective-permute-start.17) | collective-permute-done | bytes 65568 | tf_op jit(solution)/shard_map/ppermute | solution.py:242
  84.4 6.4 %shard_map.44 = f32[8,64,128]{2,1,0:T(8,128)S(1)} custom-call(s32[8]{0:T(128)S(1)} %fusion.22.at_ref, f32[8,64,128]{2,1,0:T(8,128)S(1)} %constant_dynamic-update-slice_fusion.z_ref, f32[8,64,128]{2,1,0:T(8,128)S(1)} %collective-permute-done.20.other_ref, bf16[2048,1024]{1,0:T(8,128)(2,1)S(1)} %get-tuple-element.34.a_ref, ...), custom_call_target="tpu_custom_call" | custom-call | flops 939524096 | bytes 6815744 | tf_op jit(solution)/shard_map/pallas_call | solution.py:225
  90.8 2.6 %collective-permute-start.21 = (bf16[2,64,128]{2,1,0:T(8,128)(2,1)S(1)}, bf16[2,64,128]{2,1,0:T(8,128)(2,1)S(1)}, u32[]{:S(2)}, u32[]{:S(2)}) collective-permute-start(bf16[2,64,128]{2,1,0:T(8,128)(2,1)S(1)} %get-tuple-element.58), channel_id=1, source_target_pairs={{0,5},{1,4},{4,1},{5,0},{8,13},{9,12},{12,9},{13,8},{2,7},{3,6},{6... | collective-permute-start | bytes 98312 | tf_op jit(solution)/shard_map/ppermute | solution.py:242
  95.7 1.6 collective-permute-done.23
  98.4 4.8 %collective-permute-done.24 = bf16[2,64,128]{2,1,0:T(8,128)(2,1)S(1)} collective-permute-done((bf16[2,64,128]{2,1,0:T(8,128)(2,1)S(1)}, bf16[2,64,128]{2,1,0:T(8,128)(2,1)S(1)}, u32[]{:S(2)}, u32[]{:S(2)}) %collective-permute-start.24) | collective-permute-done | bytes 32800 | tf_op jit(solution)/shard_map/ppermute | solution.py:242
  104.7 2.0 %collective-permute-start.25 = (bf16[2,64,128]{2,1,0:T(8,128)(2,1)S(1)}, bf16[2,64,128]{2,1,0:T(8,128)(2,1)S(1)}, u32[]{:S(2)}, u32[]{:S(2)}) collective-permute-start(bf16[2,64,128]{2,1,0:T(8,128)(2,1)S(1)} %add_convert_fusion.2), channel_id=1, source_target_pairs={{0,4},{1,5},{4,0},{5,1},{8,12},{9,13},{12,8},{13,9},{2,6},{3,7},{6... | collective-permute-start | bytes 98312 | tf_op jit(solution)/shard_map/ppermute | solution.py:242
  110.1 5.8 %shard_map.45 = f32[8,64,128]{2,1,0:T(8,128)S(1)} custom-call(s32[8]{0:T(128)S(1)} %fusion.22.at_ref, bf16[8,64,128]{2,1,0:T(8,128)(2,1)S(1)} %pad_maximum_fusion.2.z_ref, bf16[8,64,128]{2,1,0:T(8,128)(2,1)S(1)} %collective-permute-done.28.other_ref, bf16[2048,1024]{1,0:T(8,128)(2,1)S(1)} %get-tuple-element.34.a_ref, bf16[1024,1024]{1,0:T(8,128)(2,1)S(1)} %shard_map.43.turned_ref), custom_call_target="tpu_custom_call" | custom-call | flops 939524096 | bytes 6553600 | tf_op jit(solution)/shard_map/pallas_call | solution.py:225
  115.9 2.6 %collective-permute-start.29 = (bf16[2,64,128]{2,1,0:T(8,128)(2,1)S(1)}, bf16[2,64,128]{2,1,0:T(8,128)(2,1)S(1)}, u32[]{:S(2)}, u32[]{:S(2)}) collective-permute-start(bf16[2,64,128]{2,1,0:T(8,128)(2,1)S(1)} %get-tuple-element.55), channel_id=1, source_target_pairs={{0,5},{1,4},{4,1},{5,0},{8,13},{9,12},{12,9},{13,8},{2,7},{3,6},{6... | collective-permute-start | bytes 98312 | tf_op jit(solution)/shard_map/ppermute | solution.py:242
  120.8 1.6 collective-permute-done.31
  123.4 4.8 %collective-permute-done.32 = bf16[2,64,128]{2,1,0:T(8,128)(2,1)S(1)} collective-permute-done((bf16[2,64,128]{2,1,0:T(8,128)(2,1)S(1)}, bf16[2,64,128]{2,1,0:T(8,128)(2,1)S(1)}, u32[]{:S(2)}, u32[]{:S(2)}) %collective-permute-start.32) | collective-permute-done | bytes 32800 | tf_op jit(solution)/shard_map/ppermute | solution.py:242
  129.8 2.0 %collective-permute-start.33 = (bf16[2,64,128]{2,1,0:T(8,128)(2,1)S(1)}, bf16[2,64,128]{2,1,0:T(8,128)(2,1)S(1)}, u32[]{:S(2)}, u32[]{:S(2)}) collective-permute-start(bf16[2,64,128]{2,1,0:T(8,128)(2,1)S(1)} %add_convert_fusion.1), channel_id=1, source_target_pairs={{0,4},{1,5},{4,0},{5,1},{8,12},{9,13},{12,8},{13,9},{2,6},{3,7},{6... | collective-permute-start | bytes 98312 | tf_op jit(solution)/shard_map/ppermute | solution.py:242
  135.2 5.8 %shard_map.46 = f32[8,64,128]{2,1,0:T(8,128)S(1)} custom-call(s32[8]{0:T(128)S(1)} %fusion.22.at_ref, bf16[8,64,128]{2,1,0:T(8,128)(2,1)S(1)} %pad_maximum_fusion.3.z_ref, bf16[8,64,128]{2,1,0:T(8,128)(2,1)S(1)} %collective-permute-done.36.other_ref, bf16[2048,1024]{1,0:T(8,128)(2,1)S(1)} %get-tuple-element.34.a_ref, bf16[1024,1024]{1,0:T(8,128)(2,1)S(1)} %shard_map.43.turned_ref), custom_call_target="tpu_custom_call" | custom-call | flops 939524096 | bytes 6553600 | tf_op jit(solution)/shard_map/pallas_call | solution.py:225
  141.0 2.6 %collective-permute-start.37 = (bf16[2,64,128]{2,1,0:T(8,128)(2,1)S(1)}, bf16[2,64,128]{2,1,0:T(8,128)(2,1)S(1)}, u32[]{:S(2)}, u32[]{:S(2)}) collective-permute-start(bf16[2,64,128]{2,1,0:T(8,128)(2,1)S(1)} %get-tuple-element.52), channel_id=1, source_target_pairs={{0,5},{1,4},{4,1},{5,0},{8,13},{9,12},{12,9},{13,8},{2,7},{3,6},{6... | collective-permute-start | bytes 98312 | tf_op jit(solution)/shard_map/ppermute | solution.py:242
  145.8 1.6 collective-permute-done.39
  148.5 4.8 %collective-permute-done.40 = bf16[2,64,128]{2,1,0:T(8,128)(2,1)S(1)} collective-permute-done((bf16[2,64,128]{2,1,0:T(8,128)(2,1)S(1)}, bf16[2,64,128]{2,1,0:T(8,128)(2,1)S(1)}, u32[]{:S(2)}, u32[]{:S(2)}) %collective-permute-start.40) | collective-permute-done | bytes 32800 | tf_op jit(solution)/shard_map/ppermute | solution.py:242
  154.9 2.0 %collective-permute-start.41 = (bf16[2,64,128]{2,1,0:T(8,128)(2,1)S(1)}, bf16[2,64,128]{2,1,0:T(8,128)(2,1)S(1)}, u32[]{:S(2)}, u32[]{:S(2)}) collective-permute-start(bf16[2,64,128]{2,1,0:T(8,128)(2,1)S(1)} %add_convert_fusion), channel_id=1, source_target_pairs={{0,4},{1,5},{4,0},{5,1},{8,12},{9,13},{12,8},{13,9},{2,6},{3,7},{6... | collective-permute-start | bytes 98312 | tf_op jit(solution)/shard_map/ppermute | solution.py:242
  160.2 2.2 %copy-done.1 = bf16[2048,1024]{1,0:T(8,128)(2,1)S(1)} copy-done((bf16[2048,1024]{1,0:T(8,128)(2,1)S(1)}, bf16[2048,1024]{1,0:T(8,128)(2,1)}, u32[]{:S(2)}) %copy-start.1) | copy-done | bytes 4194328
  162.4 6.0 %shard_map.47 = f32[64,512]{1,0:T(8,128)} custom-call(s32[8]{0:T(128)S(1)} %fusion.22.at_ref, s32[1]{0:T(128)} %bitcast.core_ref, bf16[8,64,128]{2,1,0:T(8,128)(2,1)S(1)} %pad_maximum_fusion.4.z_ref, bf16[8,64,128]{2,1,0:T(8,128)(2,1)S(1)} %collective-permute-done.44.other_ref, bf16[2048,1024]{1,0:T(8,128)(2,1)S(1)} %copy-done.1), custom_call_target="tpu_custom_call" | custom-call | flops 939524096 | bytes 4456448 | tf_op jit(solution)/shard_map/pallas_call | solution.py:225
  (103 shorter events, 40.2 us)
Async XLA Ops:
  2.1 36.5 %collective-permute-start.3 = (bf16[256,1024]{1,0:T(8,128)(2,1)S(1)}, bf16[256,1024]{1,0:T(8,128)(2,1)S(1)}, u32[]{:S(2)}, u32[]{:S(2)}) collective-permute-start(bf16[256,1024]{1,0:T(8,128)(2,1)S(1)} %get-tuple-element.44), channel_id=1, source_target_pairs={{0,4},{4,0},{8,12},{12,8},{1,5},{5,1},{9,13},{13,9},{2,6},{6,2},{1... | collective-permute-start | bytes 1572872 | tf_op jit(solution)/shard_map/ppermute | solution.py:242
  5.2 33.5 %collective-permute-start.2 = (bf16[256,1024]{1,0:T(8,128)(2,1)S(1)}, bf16[256,1024]{1,0:T(8,128)(2,1)S(1)}, u32[]{:S(2)}, u32[]{:S(2)}) collective-permute-start(bf16[256,1024]{1,0:T(8,128)(2,1)S(1)} %get-tuple-element.46), channel_id=1, source_target_pairs={{0,8},{4,12},{8,0},{12,4},{1,9},{5,13},{9,1},{13,5},{2,10},{6,14},... | collective-permute-start | bytes 1572872 | tf_op jit(solution)/shard_map/ppermute | solution.py:242
  12.4 21.2 %collective-permute-start = (f32[2,64,128]{2,1,0:T(8,128)S(1)}, f32[2,64,128]{2,1,0:T(8,128)S(1)}, u32[]{:S(2)}, u32[]{:S(2)}) collective-permute-start(f32[2,64,128]{2,1,0:T(8,128)S(1)} %bitcast.16), channel_id=1, source_target_pairs={{0,8},{4,12},{8,0},{12,4},{1,9},{5,13},{9,1},{13,5},{2,10},{6,14},... | collective-permute-start | bytes 196616 | tf_op jit(solution)/shard_map/ppermute | solution.py:242
  33.6 5.0 %collective-permute-start.1 = (f32[4,64,128]{2,1,0:T(8,128)S(1)}, f32[4,64,128]{2,1,0:T(8,128)S(1)}, u32[]{:S(2)}, u32[]{:S(2)}) collective-permute-start(f32[4,64,128]{2,1,0:T(8,128)S(1)} %pad_maximum_fusion.1), channel_id=1, source_target_pairs={{0,1},{1,0},{2,3},{3,2},{4,5},{5,4},{6,7},{7,6},{8,9},{9,8},{10,11... | collective-permute-start | bytes 393224 | tf_op jit(solution)/shard_map/ppermute | solution.py:242
  35.2 11.4 %collective-permute-start.5 = (bf16[128,1024]{1,0:T(8,128)(2,1)S(1)}, bf16[128,1024]{1,0:T(8,128)(2,1)S(1)}, u32[]{:S(2)}, u32[]{:S(2)}) collective-permute-start(bf16[128,1024]{1,0:T(8,128)(2,1)S(1)} %get-tuple-element.22), channel_id=1, source_target_pairs={{0,12},{4,8},{8,4},{12,0},{1,13},{5,9},{9,5},{13,1},{2,14},{6,10},... | collective-permute-start | bytes 786440 | tf_op jit(solution)/shard_map/ppermute | solution.py:242
  38.7 7.8 %collective-permute-start.4 = (f32[4,64,128]{2,1,0:T(8,128)S(1)}, f32[4,64,128]{2,1,0:T(8,128)S(1)}, u32[]{:S(2)}, u32[]{:S(2)}) collective-permute-start(f32[4,64,128]{2,1,0:T(8,128)S(1)} %add.218), channel_id=1, source_target_pairs={{0,4},{4,0},{8,12},{12,8},{1,5},{5,1},{9,13},{13,9},{2,6},{6,2},{1... | collective-permute-start | bytes 393224 | tf_op jit(solution)/shard_map/ppermute | solution.py:242
  46.6 10.6 %collective-permute-start.7 = (bf16[128,1024]{1,0:T(8,128)(2,1)S(1)}, bf16[128,1024]{1,0:T(8,128)(2,1)S(1)}, u32[]{:S(2)}, u32[]{:S(2)}) collective-permute-start(bf16[128,1024]{1,0:T(8,128)(2,1)S(1)} %get-tuple-element.26), channel_id=1, source_target_pairs={{0,12},{4,8},{8,4},{12,0},{1,13},{5,9},{9,5},{13,1},{2,14},{6,10},... | collective-permute-start | bytes 786440 | tf_op jit(solution)/shard_map/ppermute | solution.py:242
  49.2 8.6 %collective-permute-start.8 = (bf16[256,1024]{1,0:T(8,128)(2,1)S(1)}, bf16[256,1024]{1,0:T(8,128)(2,1)S(1)}, u32[]{:S(2)}, u32[]{:S(2)}) collective-permute-start(bf16[256,1024]{1,0:T(8,128)(2,1)S(1)} %get-tuple-element.28.refs_0_), channel_id=1, source_target_pairs={{0,2},{2,0},{1,3},{3,1},{4,6},{6,4},{5,7},{7,5},{8,10},{10,8},{9,1... | collective-permute-start | bytes 1572872 | tf_op jit(solution)/shard_map/ppermute | solution.py:242
  49.3 8.5 %collective-permute-start.9 = (bf16[256,1024]{1,0:T(8,128)(2,1)S(1)}, bf16[256,1024]{1,0:T(8,128)(2,1)S(1)}, u32[]{:S(2)}, u32[]{:S(2)}) collective-permute-start(bf16[256,1024]{1,0:T(8,128)(2,1)S(1)} %collective-permute-done.3.refs_1_), channel_id=1, source_target_pairs={{0,2},{2,0},{1,3},{3,1},{4,6},{6,4},{5,7},{7,5},{8,10},{10,8},{9,1... | collective-permute-start | bytes 1572872 | tf_op jit(solution)/shard_map/ppermute | solution.py:242
  49.7 8.1 %collective-permute-start.10 = (bf16[256,1024]{1,0:T(8,128)(2,1)S(1)}, bf16[256,1024]{1,0:T(8,128)(2,1)S(1)}, u32[]{:S(2)}, u32[]{:S(2)}) collective-permute-start(bf16[256,1024]{1,0:T(8,128)(2,1)S(1)} %collective-permute-done.2.refs_2_), channel_id=1, source_target_pairs={{0,2},{2,0},{1,3},{3,1},{4,6},{6,4},{5,7},{7,5},{8,10},{10,8},{9,1... | collective-permute-start | bytes 1572872 | tf_op jit(solution)/shard_map/ppermute | solution.py:242
  61.3 6.8 %collective-permute-start.13 = (f32[2,64,128]{2,1,0:T(8,128)S(1)}, f32[2,64,128]{2,1,0:T(8,128)S(1)}, u32[]{:S(2)}, u32[]{:S(2)}) collective-permute-start(f32[2,64,128]{2,1,0:T(8,128)S(1)} %get-tuple-element.49), channel_id=1, source_target_pairs={{0,5},{1,4},{4,1},{5,0},{8,13},{9,12},{12,9},{13,8},{2,7},{3,6},{6... | collective-permute-start | bytes 196616 | tf_op jit(solution)/shard_map/ppermute | solution.py:242
  65.7 4.3 %collective-permute-start.15 = (f32[2,64,128]{2,1,0:T(8,128)S(1)}, f32[2,64,128]{2,1,0:T(8,128)S(1)}, u32[]{:S(2)}, u32[]{:S(2)}) collective-permute-start(f32[2,64,128]{2,1,0:T(8,128)S(1)} %get-tuple-element.50), channel_id=1, source_target_pairs={{0,1},{1,0},{4,5},{5,4},{8,9},{9,8},{12,13},{13,12},{2,3},{3,2},{6... | collective-permute-start | bytes 196616 | tf_op jit(solution)/shard_map/ppermute | solution.py:242
  67.2 4.3 %collective-permute-start.14 = (f32[2,64,128]{2,1,0:T(8,128)S(1)}, f32[2,64,128]{2,1,0:T(8,128)S(1)}, u32[]{:S(2)}, u32[]{:S(2)}) collective-permute-start(f32[2,64,128]{2,1,0:T(8,128)S(1)} %get-tuple-element.51), channel_id=1, source_target_pairs={{0,4},{1,5},{4,0},{5,1},{8,12},{9,13},{12,8},{13,9},{2,6},{3,7},{6... | collective-permute-start | bytes 196616 | tf_op jit(solution)/shard_map/ppermute | solution.py:242
  71.5 5.4 %collective-permute-start.16 = (f32[2,64,128]{2,1,0:T(8,128)S(1)}, f32[2,64,128]{2,1,0:T(8,128)S(1)}, u32[]{:S(2)}, u32[]{:S(2)}) collective-permute-start(f32[2,64,128]{2,1,0:T(8,128)S(1)} %add_add_fusion), channel_id=1, source_target_pairs={{0,8},{4,12},{8,0},{12,4},{1,9},{5,13},{9,1},{13,5},{2,10},{6,14},... | collective-permute-start | bytes 196616 | tf_op jit(solution)/shard_map/ppermute | solution.py:242
  76.9 5.8 %collective-permute-start.19 = (f32[2,64,128]{2,1,0:T(8,128)S(1)}, f32[2,64,128]{2,1,0:T(8,128)S(1)}, u32[]{:S(2)}, u32[]{:S(2)}) collective-permute-start(f32[2,64,128]{2,1,0:T(8,128)S(1)} %add.225), channel_id=1, source_target_pairs={{0,5},{1,4},{4,1},{5,0},{8,13},{9,12},{12,9},{13,8},{2,7},{3,6},{6... | collective-permute-start | bytes 196616 | tf_op jit(solution)/shard_map/ppermute | solution.py:242
  77.6 5.1 %collective-permute-start.18 = (f32[2,64,128]{2,1,0:T(8,128)S(1)}, f32[2,64,128]{2,1,0:T(8,128)S(1)}, u32[]{:S(2)}, u32[]{:S(2)}) collective-permute-start(f32[2,64,128]{2,1,0:T(8,128)S(1)} %add.225), channel_id=1, source_target_pairs={{0,1},{1,0},{4,5},{5,4},{8,9},{9,8},{12,13},{13,12},{2,3},{3,2},{6... | collective-permute-start | bytes 196616 | tf_op jit(solution)/shard_map/ppermute | solution.py:242
  78.3 4.4 %collective-permute-start.17 = (f32[2,64,128]{2,1,0:T(8,128)S(1)}, f32[2,64,128]{2,1,0:T(8,128)S(1)}, u32[]{:S(2)}, u32[]{:S(2)}) collective-permute-start(f32[2,64,128]{2,1,0:T(8,128)S(1)} %add.225), channel_id=1, source_target_pairs={{0,4},{1,5},{4,0},{5,1},{8,12},{9,13},{12,8},{13,9},{2,6},{3,7},{6... | collective-permute-start | bytes 196616 | tf_op jit(solution)/shard_map/ppermute | solution.py:242
  90.8 4.9 %collective-permute-start.21 = (bf16[2,64,128]{2,1,0:T(8,128)(2,1)S(1)}, bf16[2,64,128]{2,1,0:T(8,128)(2,1)S(1)}, u32[]{:S(2)}, u32[]{:S(2)}) collective-permute-start(bf16[2,64,128]{2,1,0:T(8,128)(2,1)S(1)} %get-tuple-element.58), channel_id=1, source_target_pairs={{0,5},{1,4},{4,1},{5,0},{8,13},{9,12},{12,9},{13,8},{2,7},{3,6},{6... | collective-permute-start | bytes 98312 | tf_op jit(solution)/shard_map/ppermute | solution.py:242
  93.4 3.9 %collective-permute-start.23 = (bf16[2,64,128]{2,1,0:T(8,128)(2,1)S(1)}, bf16[2,64,128]{2,1,0:T(8,128)(2,1)S(1)}, u32[]{:S(2)}, u32[]{:S(2)}) collective-permute-start(bf16[2,64,128]{2,1,0:T(8,128)(2,1)S(1)} %get-tuple-element.59), channel_id=1, source_target_pairs={{0,1},{1,0},{4,5},{5,4},{8,9},{9,8},{12,13},{13,12},{2,3},{3,2},{6... | collective-permute-start | bytes 98312 | tf_op jit(solution)/shard_map/ppermute | solution.py:242
  94.3 3.9 %collective-permute-start.22 = (bf16[2,64,128]{2,1,0:T(8,128)(2,1)S(1)}, bf16[2,64,128]{2,1,0:T(8,128)(2,1)S(1)}, u32[]{:S(2)}, u32[]{:S(2)}) collective-permute-start(bf16[2,64,128]{2,1,0:T(8,128)(2,1)S(1)} %get-tuple-element.60), channel_id=1, source_target_pairs={{0,4},{1,5},{4,0},{5,1},{8,12},{9,13},{12,8},{13,9},{2,6},{3,7},{6... | collective-permute-start | bytes 98312 | tf_op jit(solution)/shard_map/ppermute | solution.py:242
  98.3 4.9 %collective-permute-start.24 = (bf16[2,64,128]{2,1,0:T(8,128)(2,1)S(1)}, bf16[2,64,128]{2,1,0:T(8,128)(2,1)S(1)}, u32[]{:S(2)}, u32[]{:S(2)}) collective-permute-start(bf16[2,64,128]{2,1,0:T(8,128)(2,1)S(1)} %fusion.21), channel_id=1, source_target_pairs={{0,8},{4,12},{8,0},{12,4},{1,9},{5,13},{9,1},{13,5},{2,10},{6,14},... | collective-permute-start | bytes 98312 | tf_op jit(solution)/shard_map/ppermute | solution.py:242
  103.2 5.0 %collective-permute-start.27 = (bf16[2,64,128]{2,1,0:T(8,128)(2,1)S(1)}, bf16[2,64,128]{2,1,0:T(8,128)(2,1)S(1)}, u32[]{:S(2)}, u32[]{:S(2)}) collective-permute-start(bf16[2,64,128]{2,1,0:T(8,128)(2,1)S(1)} %add_convert_fusion.2), channel_id=1, source_target_pairs={{0,5},{1,4},{4,1},{5,0},{8,13},{9,12},{12,9},{13,8},{2,7},{3,6},{6... | collective-permute-start | bytes 98312 | tf_op jit(solution)/shard_map/ppermute | solution.py:242
  103.9 4.3 %collective-permute-start.26 = (bf16[2,64,128]{2,1,0:T(8,128)(2,1)S(1)}, bf16[2,64,128]{2,1,0:T(8,128)(2,1)S(1)}, u32[]{:S(2)}, u32[]{:S(2)}) collective-permute-start(bf16[2,64,128]{2,1,0:T(8,128)(2,1)S(1)} %add_convert_fusion.2), channel_id=1, source_target_pairs={{0,1},{1,0},{4,5},{5,4},{8,9},{9,8},{12,13},{13,12},{2,3},{3,2},{6... | collective-permute-start | bytes 98312 | tf_op jit(solution)/shard_map/ppermute | solution.py:242
  104.7 3.9 %collective-permute-start.25 = (bf16[2,64,128]{2,1,0:T(8,128)(2,1)S(1)}, bf16[2,64,128]{2,1,0:T(8,128)(2,1)S(1)}, u32[]{:S(2)}, u32[]{:S(2)}) collective-permute-start(bf16[2,64,128]{2,1,0:T(8,128)(2,1)S(1)} %add_convert_fusion.2), channel_id=1, source_target_pairs={{0,4},{1,5},{4,0},{5,1},{8,12},{9,13},{12,8},{13,9},{2,6},{3,7},{6... | collective-permute-start | bytes 98312 | tf_op jit(solution)/shard_map/ppermute | solution.py:242
  115.9 4.9 %collective-permute-start.29 = (bf16[2,64,128]{2,1,0:T(8,128)(2,1)S(1)}, bf16[2,64,128]{2,1,0:T(8,128)(2,1)S(1)}, u32[]{:S(2)}, u32[]{:S(2)}) collective-permute-start(bf16[2,64,128]{2,1,0:T(8,128)(2,1)S(1)} %get-tuple-element.55), channel_id=1, source_target_pairs={{0,5},{1,4},{4,1},{5,0},{8,13},{9,12},{12,9},{13,8},{2,7},{3,6},{6... | collective-permute-start | bytes 98312 | tf_op jit(solution)/shard_map/ppermute | solution.py:242
  123.4 4.9 %collective-permute-start.32 = (bf16[2,64,128]{2,1,0:T(8,128)(2,1)S(1)}, bf16[2,64,128]{2,1,0:T(8,128)(2,1)S(1)}, u32[]{:S(2)}, u32[]{:S(2)}) collective-permute-start(bf16[2,64,128]{2,1,0:T(8,128)(2,1)S(1)} %fusion.18), channel_id=1, source_target_pairs={{0,8},{4,12},{8,0},{12,4},{1,9},{5,13},{9,1},{13,5},{2,10},{6,14},... | collective-permute-start | bytes 98312 | tf_op jit(solution)/shard_map/ppermute | solution.py:242
  128.3 5.0 %collective-permute-start.35 = (bf16[2,64,128]{2,1,0:T(8,128)(2,1)S(1)}, bf16[2,64,128]{2,1,0:T(8,128)(2,1)S(1)}, u32[]{:S(2)}, u32[]{:S(2)}) collective-permute-start(bf16[2,64,128]{2,1,0:T(8,128)(2,1)S(1)} %add_convert_fusion.1), channel_id=1, source_target_pairs={{0,5},{1,4},{4,1},{5,0},{8,13},{9,12},{12,9},{13,8},{2,7},{3,6},{6... | collective-permute-start | bytes 98312 | tf_op jit(solution)/shard_map/ppermute | solution.py:242
  129.0 4.3 %collective-permute-start.34 = (bf16[2,64,128]{2,1,0:T(8,128)(2,1)S(1)}, bf16[2,64,128]{2,1,0:T(8,128)(2,1)S(1)}, u32[]{:S(2)}, u32[]{:S(2)}) collective-permute-start(bf16[2,64,128]{2,1,0:T(8,128)(2,1)S(1)} %add_convert_fusion.1), channel_id=1, source_target_pairs={{0,1},{1,0},{4,5},{5,4},{8,9},{9,8},{12,13},{13,12},{2,3},{3,2},{6... | collective-permute-start | bytes 98312 | tf_op jit(solution)/shard_map/ppermute | solution.py:242
  141.0 4.9 %collective-permute-start.37 = (bf16[2,64,128]{2,1,0:T(8,128)(2,1)S(1)}, bf16[2,64,128]{2,1,0:T(8,128)(2,1)S(1)}, u32[]{:S(2)}, u32[]{:S(2)}) collective-permute-start(bf16[2,64,128]{2,1,0:T(8,128)(2,1)S(1)} %get-tuple-element.52), channel_id=1, source_target_pairs={{0,5},{1,4},{4,1},{5,0},{8,13},{9,12},{12,9},{13,8},{2,7},{3,6},{6... | collective-permute-start | bytes 98312 | tf_op jit(solution)/shard_map/ppermute | solution.py:242
  148.5 4.9 %collective-permute-start.40 = (bf16[2,64,128]{2,1,0:T(8,128)(2,1)S(1)}, bf16[2,64,128]{2,1,0:T(8,128)(2,1)S(1)}, u32[]{:S(2)}, u32[]{:S(2)}) collective-permute-start(bf16[2,64,128]{2,1,0:T(8,128)(2,1)S(1)} %fusion.15), channel_id=1, source_target_pairs={{0,8},{4,12},{8,0},{12,4},{1,9},{5,13},{9,1},{13,5},{2,10},{6,14},... | collective-permute-start | bytes 98312 | tf_op jit(solution)/shard_map/ppermute | solution.py:242
  153.3 5.0 %collective-permute-start.43 = (bf16[2,64,128]{2,1,0:T(8,128)(2,1)S(1)}, bf16[2,64,128]{2,1,0:T(8,128)(2,1)S(1)}, u32[]{:S(2)}, u32[]{:S(2)}) collective-permute-start(bf16[2,64,128]{2,1,0:T(8,128)(2,1)S(1)} %add_convert_fusion), channel_id=1, source_target_pairs={{0,5},{1,4},{4,1},{5,0},{8,13},{9,12},{12,9},{13,8},{2,7},{3,6},{6... | collective-permute-start | bytes 98312 | tf_op jit(solution)/shard_map/ppermute | solution.py:242
  154.0 4.3 %collective-permute-start.42 = (bf16[2,64,128]{2,1,0:T(8,128)(2,1)S(1)}, bf16[2,64,128]{2,1,0:T(8,128)(2,1)S(1)}, u32[]{:S(2)}, u32[]{:S(2)}) collective-permute-start(bf16[2,64,128]{2,1,0:T(8,128)(2,1)S(1)} %add_convert_fusion), channel_id=1, source_target_pairs={{0,1},{1,0},{4,5},{5,4},{8,9},{9,8},{12,13},{13,12},{2,3},{3,2},{6... | collective-permute-start | bytes 98312 | tf_op jit(solution)/shard_map/ppermute | solution.py:242
  (15 other events, 112.1 us)

commit v20 on v19

--- a/solution.py
+++ b/solution.py
@@ -59,8 +59,8 @@
     )
 
 
-def small_times_wide(small, wide):
-    left, right = terms_of(small), terms_of(wide)
+def small_times_wide(small, right):
+    left = terms_of(small)
     pairs = [(i, d - i) for d in (2, 1, 0) for i in range(d + 1)]
     pairs = [(i, j) for i, j in pairs if i < len(left) and j < len(right)]
     return dot_nn(
@@ -69,11 +69,10 @@
     )
 
 
-def gram_of(wide):
-    terms = terms_of(wide)
+def gram_of(terms):
     if len(terms) == 1:
         return dot_nt(terms[0], terms[0])
-    rank = wide.shape[0]
+    rank = terms[0].shape[0]
     stacked = jnp.concatenate(terms, axis=0)
     both = dot_nt(stacked, stacked)
     cross = both[rank : 2 * rank, :rank] + both[2 * rank :, :rank]
@@ -139,8 +138,8 @@
     return jnp.where(keep, both[:, :size], 0.0), both[:, size:]
 
 
-def shifted_factor(wide):
-    whole_gram = gram_of(wide)
+def shifted_factor(wide, terms):
+    whole_gram = gram_of(terms)
     squares = wide.astype(jnp.float32)
     squares = jnp.sum(squares * squares, axis=0, keepdims=True)
     trace = jnp.sum(squares, axis=1, keepdims=True)
@@ -161,24 +160,25 @@
 
 def first_pass(at_ref, z_refs):
     wide = wide_of(at_ref, z_refs)
-    upper, inverse_one = shifted_factor(wide)
-    return small_times_wide(inverse_one, wide), upper
+    terms = terms_of(wide)
+    upper, inverse_one = shifted_factor(wide, terms)
+    return terms_of(small_times_wide(inverse_one, terms)), upper
 
 
 def back_product(at_ref, z_refs, a):
-    first, unused = first_pass(at_ref, z_refs)
-    rank = first.shape[0]
-    terms = jnp.concatenate(terms_of(first), axis=0)
+    terms, unused = first_pass(at_ref, z_refs)
+    rank = terms[0].shape[0]
+    stacked = jnp.concatenate(terms, axis=0)
     tiles = []
 
     def tile(start):
-        back = dot_nn(terms, a[:, start : start + TILE])
+        back = dot_nn(stacked, a[:, start : start + TILE])
         tiles.append(back[:rank] + (back[rank : 2 * rank] + back[2 * rank :]))
 
     starts = range(0, a.shape[1], TILE)
     work = [functools.partial(tile, start) for start in starts]
-    unused, inverse_two = eliminate(gram_of(first), work)
-    return small_times_wide(inverse_two, jnp.concatenate(tiles, axis=1))
+    unused, inverse_two = eliminate(gram_of(terms), work)
+    return small_times_wide(inverse_two, terms_of(jnp.concatenate(tiles, axis=1)))
 
 
 def store_parts(forth, at_ref, part_ref):
@@ -188,9 +188,9 @@
 
 
 def orth_kernel(at_ref, z_ref, other_ref, basis_ref, upper_ref):
-    first, upper = first_pass(at_ref, (z_ref, other_ref))
-    unused, inverse_two = eliminate(gram_of(first))
-    basis_ref[...] = small_times_wide(inverse_two, first).astype(jnp.bfloat16)
+    terms, upper = first_pass(at_ref, (z_ref, other_ref))
+    unused, inverse_two = eliminate(gram_of(terms))
+    basis_ref[...] = small_times_wide(inverse_two, terms).astype(jnp.bfloat16)
     upper_ref[...] = upper
 
 
@@ -245,7 +245,7 @@
 def square_devices():
     n_z, n_col = lax.axis_size("z"), lax.axis_size("col")
     sides = [(z, col) for z in range(2 if n_z > 2 else 1) for col in range(n_col)]
-    return [(z * n_col + col, col * (2 if n_z > 2 else 1) + z) for z, col in sides[:0:-1]]
+    return [(z * n_col + col, col * (2 if n_z > 2 else 1) + z) for z, col in sides[1:]]
 
 
 def sum_parts(total, dtype):

time: 169 us -> 170 us (level)
  starting transfers between devices: 45.9 us -> 47.7 us
    ppermute x45, starting transfers between devices: 45.9 us -> 47.7 us  [from_xor(): return lax.ppermute(value, axis, [(i, i ^ offset) for i in range(size)])]
  transfers between devices with their start and end apart: 45 -> 45, of which waited for: 33 -> 35; matrix products, arithmetic and copies ran while one was open for 3% -> 3% of each run, Pallas kernels for 4% -> 4%
where the time goes in v20:
time: 170 us
  waiting for transfers between devices  78 us (46%)
  starting transfers between devices  47.7 us (28%)
  Pallas kernels  32.5 us (19%)
  local copies, waits for them, and re-layouts  5.55 us (3%)
  matrix products  3.83 us (2%)
    ppermute x45, waiting for transfers between devices, from_xor(): return lax.ppermute(value, axis, [(i, i ^ offset) for i in range(size)])  78 us
    ppermute x45, starting transfers between devices, from_xor(): return lax.ppermute(value, axis, [(i, i ^ offset) for i in range(size)])  47.7 us
    pallas_call x7, Pallas kernels, call(): pl.pallas_call(kernel, out_shape=out_shapes, in_specs=[pl.BlockSpec(memor...  32.5 us
    dot_general x1, matrix products, per_device_transposed(): lax.dot_general(omega, states, (((0,), (1,)), ((), ())), preferred_elemen...  3.83 us
  transfers between devices with their start and end apart: 45, of which 35 were waited for; matrix products, arithmetic and copies ran while one was open for 3% of the time, Pallas kernels for 4%

profile of v20, /device:TPU:0, one launch (start us, length us, event | category | flops | bytes accessed | tf_op | source)
XLA Modules:
  0.0 169.6 jit_solution(1592503169172518735)
XLA Ops:
  2.1 3.1 %collective-permute-start.3 = (bf16[256,1024]{1,0:T(8,128)(2,1)S(1)}, bf16[256,1024]{1,0:T(8,128)(2,1)S(1)}, u32[]{:S(2)}, u32[]{:S(2)}) collective-permute-start(bf16[256,1024]{1,0:T(8,128)(2,1)S(1)} %get-tuple-element.44), channel_id=1, source_target_pairs={{0,4},{4,0},{8,12},{12,8},{1,5},{5,1},{9,13},{13,9},{2,6},{6,2},{1... | collective-permute-start | bytes 1572872 | tf_op jit(solution)/shard_map/ppermute | solution.py:242
  5.2 2.6 %collective-permute-start.2 = (bf16[256,1024]{1,0:T(8,128)(2,1)S(1)}, bf16[256,1024]{1,0:T(8,128)(2,1)S(1)}, u32[]{:S(2)}, u32[]{:S(2)}) collective-permute-start(bf16[256,1024]{1,0:T(8,128)(2,1)S(1)} %get-tuple-element.46), channel_id=1, source_target_pairs={{0,8},{4,12},{8,0},{12,4},{1,9},{5,13},{9,1},{13,5},{2,10},{6,14},... | collective-permute-start | bytes 1572872 | tf_op jit(solution)/shard_map/ppermute | solution.py:242
  8.5 3.8 %convolution_bitcast_fusion = f32[8,2,8,128]{3,2,1,0:T(8,128)S(1)} fusion(bf16[256,4096]{1,0:T(8,128)(2,1)} %param.3, s32[]{:T(128)S(6)} %xor.73, s32[4096]{0:T(1024)S(1)} %add_multiply_fusion), kind=kOutput, calls=%fused_computation | convolution fusion | flops 152043520 | bytes 2179076 | tf_op jit(solution)/shard_map/dot_general | solution.py:317
  13.8 19.8 %collective-permute-done = f32[2,64,128]{2,1,0:T(8,128)S(1)} collective-permute-done((f32[2,64,128]{2,1,0:T(8,128)S(1)}, f32[2,64,128]{2,1,0:T(8,128)S(1)}, u32[]{:S(2)}, u32[]{:S(2)}) %collective-permute-start) | collective-permute-done | bytes 65568 | tf_op jit(solution)/shard_map/ppermute | solution.py:242
  35.2 3.0 %collective-permute-start.5 = (bf16[128,1024]{1,0:T(8,128)(2,1)S(1)}, bf16[128,1024]{1,0:T(8,128)(2,1)S(1)}, u32[]{:S(2)}, u32[]{:S(2)}) collective-permute-start(bf16[128,1024]{1,0:T(8,128)(2,1)S(1)} %get-tuple-element.22), channel_id=1, source_target_pairs={{0,12},{4,8},{8,4},{12,0},{1,13},{5,9},{9,5},{13,1},{2,14},{6,10},... | collective-permute-start | bytes 786440 | tf_op jit(solution)/shard_map/ppermute | solution.py:242
  38.8 7.7 %collective-permute-done.4 = f32[4,64,128]{2,1,0:T(8,128)S(1)} collective-permute-done((f32[4,64,128]{2,1,0:T(8,128)S(1)}, f32[4,64,128]{2,1,0:T(8,128)S(1)}, u32[]{:S(2)}, u32[]{:S(2)}) %collective-permute-start.4) | collective-permute-done | bytes 131104 | tf_op jit(solution)/shard_map/ppermute | solution.py:242
  46.6 2.5 %collective-permute-start.7 = (bf16[128,1024]{1,0:T(8,128)(2,1)S(1)}, bf16[128,1024]{1,0:T(8,128)(2,1)S(1)}, u32[]{:S(2)}, u32[]{:S(2)}) collective-permute-start(bf16[128,1024]{1,0:T(8,128)(2,1)S(1)} %get-tuple-element.26), channel_id=1, source_target_pairs={{0,12},{4,8},{8,4},{12,0},{1,13},{5,9},{9,5},{13,1},{2,14},{6,10},... | collective-permute-start | bytes 786440 | tf_op jit(solution)/shard_map/ppermute | solution.py:242
  49.9 5.9 %shard_map.41 = (bf16[64,2048]{1,0:T(8,128)(2,1)S(1)}, f32[64,64]{1,0:T(8,128)S(1)}) custom-call(s32[8]{0:T(128)S(1)} %fusion.24.at_ref, f32[8,64,128]{2,1,0:T(8,128)S(1)} %pad_maximum_fusion.z_ref, f32[8,64,128]{2,1,0:T(8,128)S(1)} %collective-permute-done.6.other_ref), custom_call_target="tpu_custom_call" | custom-call | flops 402653184 | bytes 524288 | tf_op jit(solution)/shard_map/pallas_call | solution.py:225
  59.2 2.1 %shard_map.42 = (bf16[2048,1024]{1,0:T(8,128)(2,1)S(1)}, f32[8,64,128]{2,1,0:T(8,128)S(1)}) custom-call(s32[8]{0:T(128)S(1)} %fusion.22.at_ref, bf16[64,2048]{1,0:T(8,128)(2,1)S(1)} %get-tuple-element.27.basis_ref, bf16[256,1024]{1,0:T(8,128)(2,1)S(1)} %get-tuple-element.28.refs_0_, bf16[256,1024]{1,0:T(8,128)(2,1)S(1)} %collective-permute-done.3.refs_1_, ...), custom_call_target="tpu_custom_call" | custom-call | flops 939524096 | bytes 4456448 | tf_op jit(solution)/shard_map/pallas_call | solution.py:225
  61.9 5.3 %collective-permute-start.15 = (f32[2,64,128]{2,1,0:T(8,128)S(1)}, f32[2,64,128]{2,1,0:T(8,128)S(1)}, u32[]{:S(2)}, u32[]{:S(2)}) collective-permute-start(f32[2,64,128]{2,1,0:T(8,128)S(1)} %get-tuple-element.50), channel_id=1, source_target_pairs={{0,5},{1,4},{4,1},{5,0},{8,13},{9,12},{12,9},{13,8},{2,7},{3,6},{6... | collective-permute-start | bytes 196616 | tf_op jit(solution)/shard_map/ppermute | solution.py:242
  67.2 2.4 %collective-permute-done.15 = f32[2,64,128]{2,1,0:T(8,128)S(1)} collective-permute-done((f32[2,64,128]{2,1,0:T(8,128)S(1)}, f32[2,64,128]{2,1,0:T(8,128)S(1)}, u32[]{:S(2)}, u32[]{:S(2)}) %collective-permute-start.15) | collective-permute-done | bytes 65568 | tf_op jit(solution)/shard_map/ppermute | solution.py:242
  69.6 1.9 %collective-permute-done.14 = f32[2,64,128]{2,1,0:T(8,128)S(1)} collective-permute-done((f32[2,64,128]{2,1,0:T(8,128)S(1)}, f32[2,64,128]{2,1,0:T(8,128)S(1)}, u32[]{:S(2)}, u32[]{:S(2)}) %collective-permute-start.14) | collective-permute-done | bytes 65568 | tf_op jit(solution)/shard_map/ppermute | solution.py:242
  73.1 4.3 %collective-permute-done.16 = f32[2,64,128]{2,1,0:T(8,128)S(1)} collective-permute-done((f32[2,64,128]{2,1,0:T(8,128)S(1)}, f32[2,64,128]{2,1,0:T(8,128)S(1)}, u32[]{:S(2)}, u32[]{:S(2)}) %collective-permute-start.16) | collective-permute-done | bytes 65568 | tf_op jit(solution)/shard_map/ppermute | solution.py:242
  79.3 1.6 collective-permute-start.17
  81.0 2.6 %collective-permute-done.17 = f32[2,64,128]{2,1,0:T(8,128)S(1)} collective-permute-done((f32[2,64,128]{2,1,0:T(8,128)S(1)}, f32[2,64,128]{2,1,0:T(8,128)S(1)}, u32[]{:S(2)}, u32[]{:S(2)}) %collective-permute-start.17) | collective-permute-done | bytes 65568 | tf_op jit(solution)/shard_map/ppermute | solution.py:242
  85.3 6.4 %shard_map.44 = f32[8,64,128]{2,1,0:T(8,128)S(1)} custom-call(s32[8]{0:T(128)S(1)} %fusion.22.at_ref, f32[8,64,128]{2,1,0:T(8,128)S(1)} %constant_dynamic-update-slice_fusion.z_ref, f32[8,64,128]{2,1,0:T(8,128)S(1)} %collective-permute-done.20.other_ref, bf16[2048,1024]{1,0:T(8,128)(2,1)S(1)} %get-tuple-element.34.a_ref, ...), custom_call_target="tpu_custom_call" | custom-call | flops 939524096 | bytes 6815744 | tf_op jit(solution)/shard_map/pallas_call | solution.py:225
  92.5 2.4 %collective-permute-start.23 = (bf16[2,64,128]{2,1,0:T(8,128)(2,1)S(1)}, bf16[2,64,128]{2,1,0:T(8,128)(2,1)S(1)}, u32[]{:S(2)}, u32[]{:S(2)}) collective-permute-start(bf16[2,64,128]{2,1,0:T(8,128)(2,1)S(1)} %get-tuple-element.59), channel_id=1, source_target_pairs={{0,5},{1,4},{4,1},{5,0},{8,13},{9,12},{12,9},{13,8},{2,7},{3,6},{6... | collective-permute-start | bytes 98312 | tf_op jit(solution)/shard_map/ppermute | solution.py:242
  95.7 1.8 %collective-permute-done.23 = bf16[2,64,128]{2,1,0:T(8,128)(2,1)S(1)} collective-permute-done((bf16[2,64,128]{2,1,0:T(8,128)(2,1)S(1)}, bf16[2,64,128]{2,1,0:T(8,128)(2,1)S(1)}, u32[]{:S(2)}, u32[]{:S(2)}) %collective-permute-start.23) | collective-permute-done | bytes 32800 | tf_op jit(solution)/shard_map/ppermute | solution.py:242
  99.3 4.6 %collective-permute-done.24 = bf16[2,64,128]{2,1,0:T(8,128)(2,1)S(1)} collective-permute-done((bf16[2,64,128]{2,1,0:T(8,128)(2,1)S(1)}, bf16[2,64,128]{2,1,0:T(8,128)(2,1)S(1)}, u32[]{:S(2)}, u32[]{:S(2)}) %collective-permute-start.24) | collective-permute-done | bytes 32800 | tf_op jit(solution)/shard_map/ppermute | solution.py:242
  105.6 1.8 %collective-permute-start.25 = (bf16[2,64,128]{2,1,0:T(8,128)(2,1)S(1)}, bf16[2,64,128]{2,1,0:T(8,128)(2,1)S(1)}, u32[]{:S(2)}, u32[]{:S(2)}) collective-permute-start(bf16[2,64,128]{2,1,0:T(8,128)(2,1)S(1)} %add_convert_fusion.2), channel_id=1, source_target_pairs={{0,4},{1,5},{4,0},{5,1},{8,12},{9,13},{12,8},{13,9},{2,6},{3,7},{6... | collective-permute-start | bytes 98312 | tf_op jit(solution)/shard_map/ppermute | solution.py:242
  111.0 5.8 %shard_map.45 = f32[8,64,128]{2,1,0:T(8,128)S(1)} custom-call(s32[8]{0:T(128)S(1)} %fusion.22.at_ref, bf16[8,64,128]{2,1,0:T(8,128)(2,1)S(1)} %pad_maximum_fusion.2.z_ref, bf16[8,64,128]{2,1,0:T(8,128)(2,1)S(1)} %collective-permute-done.28.other_ref, bf16[2048,1024]{1,0:T(8,128)(2,1)S(1)} %get-tuple-element.34.a_ref, bf16[1024,1024]{1,0:T(8,128)(2,1)S(1)} %shard_map.43.turned_ref), custom_call_target="tpu_custom_call" | custom-call | flops 939524096 | bytes 6553600 | tf_op jit(solution)/shard_map/pallas_call | solution.py:225
  117.9 2.2 %collective-permute-start.31 = (bf16[2,64,128]{2,1,0:T(8,128)(2,1)S(1)}, bf16[2,64,128]{2,1,0:T(8,128)(2,1)S(1)}, u32[]{:S(2)}, u32[]{:S(2)}) collective-permute-start(bf16[2,64,128]{2,1,0:T(8,128)(2,1)S(1)} %get-tuple-element.56), channel_id=1, source_target_pairs={{0,5},{1,4},{4,1},{5,0},{8,13},{9,12},{12,9},{13,8},{2,7},{3,6},{6... | collective-permute-start | bytes 98312 | tf_op jit(solution)/shard_map/ppermute | solution.py:242
  120.8 2.0 %collective-permute-done.31 = bf16[2,64,128]{2,1,0:T(8,128)(2,1)S(1)} collective-permute-done((bf16[2,64,128]{2,1,0:T(8,128)(2,1)S(1)}, bf16[2,64,128]{2,1,0:T(8,128)(2,1)S(1)}, u32[]{:S(2)}, u32[]{:S(2)}) %collective-permute-start.31) | collective-permute-done | bytes 32800 | tf_op jit(solution)/shard_map/ppermute | solution.py:242
  124.5 4.7 %collective-permute-done.32 = bf16[2,64,128]{2,1,0:T(8,128)(2,1)S(1)} collective-permute-done((bf16[2,64,128]{2,1,0:T(8,128)(2,1)S(1)}, bf16[2,64,128]{2,1,0:T(8,128)(2,1)S(1)}, u32[]{:S(2)}, u32[]{:S(2)}) %collective-permute-start.32) | collective-permute-done | bytes 32800 | tf_op jit(solution)/shard_map/ppermute | solution.py:242
  130.9 1.8 %collective-permute-start.33 = (bf16[2,64,128]{2,1,0:T(8,128)(2,1)S(1)}, bf16[2,64,128]{2,1,0:T(8,128)(2,1)S(1)}, u32[]{:S(2)}, u32[]{:S(2)}) collective-permute-start(bf16[2,64,128]{2,1,0:T(8,128)(2,1)S(1)} %add_convert_fusion.1), channel_id=1, source_target_pairs={{0,4},{1,5},{4,0},{5,1},{8,12},{9,13},{12,8},{13,9},{2,6},{3,7},{6... | collective-permute-start | bytes 98312 | tf_op jit(solution)/shard_map/ppermute | solution.py:242
  136.2 5.8 %shard_map.46 = f32[8,64,128]{2,1,0:T(8,128)S(1)} custom-call(s32[8]{0:T(128)S(1)} %fusion.22.at_ref, bf16[8,64,128]{2,1,0:T(8,128)(2,1)S(1)} %pad_maximum_fusion.3.z_ref, bf16[8,64,128]{2,1,0:T(8,128)(2,1)S(1)} %collective-permute-done.36.other_ref, bf16[2048,1024]{1,0:T(8,128)(2,1)S(1)} %get-tuple-element.34.a_ref, bf16[1024,1024]{1,0:T(8,128)(2,1)S(1)} %shard_map.43.turned_ref), custom_call_target="tpu_custom_call" | custom-call | flops 939524096 | bytes 6553600 | tf_op jit(solution)/shard_map/pallas_call | solution.py:225
  143.2 2.2 %collective-permute-start.39 = (bf16[2,64,128]{2,1,0:T(8,128)(2,1)S(1)}, bf16[2,64,128]{2,1,0:T(8,128)(2,1)S(1)}, u32[]{:S(2)}, u32[]{:S(2)}) collective-permute-start(bf16[2,64,128]{2,1,0:T(8,128)(2,1)S(1)} %get-tuple-element.53), channel_id=1, source_target_pairs={{0,5},{1,4},{4,1},{5,0},{8,13},{9,12},{12,9},{13,8},{2,7},{3,6},{6... | collective-permute-start | bytes 98312 | tf_op jit(solution)/shard_map/ppermute | solution.py:242
  146.0 2.1 %collective-permute-done.39 = bf16[2,64,128]{2,1,0:T(8,128)(2,1)S(1)} collective-permute-done((bf16[2,64,128]{2,1,0:T(8,128)(2,1)S(1)}, bf16[2,64,128]{2,1,0:T(8,128)(2,1)S(1)}, u32[]{:S(2)}, u32[]{:S(2)}) %collective-permute-start.39) | collective-permute-done | bytes 32800 | tf_op jit(solution)/shard_map/ppermute | solution.py:242
  149.7 4.7 %collective-permute-done.40 = bf16[2,64,128]{2,1,0:T(8,128)(2,1)S(1)} collective-permute-done((bf16[2,64,128]{2,1,0:T(8,128)(2,1)S(1)}, bf16[2,64,128]{2,1,0:T(8,128)(2,1)S(1)}, u32[]{:S(2)}, u32[]{:S(2)}) %collective-permute-start.40) | collective-permute-done | bytes 32800 | tf_op jit(solution)/shard_map/ppermute | solution.py:242
  156.1 1.8 %collective-permute-start.41 = (bf16[2,64,128]{2,1,0:T(8,128)(2,1)S(1)}, bf16[2,64,128]{2,1,0:T(8,128)(2,1)S(1)}, u32[]{:S(2)}, u32[]{:S(2)}) collective-permute-start(bf16[2,64,128]{2,1,0:T(8,128)(2,1)S(1)} %add_convert_fusion), channel_id=1, source_target_pairs={{0,4},{1,5},{4,0},{5,1},{8,12},{9,13},{12,8},{13,9},{2,6},{3,7},{6... | collective-permute-start | bytes 98312 | tf_op jit(solution)/shard_map/ppermute | solution.py:242
  161.5 2.2 %copy-done.1 = bf16[2048,1024]{1,0:T(8,128)(2,1)S(1)} copy-done((bf16[2048,1024]{1,0:T(8,128)(2,1)S(1)}, bf16[2048,1024]{1,0:T(8,128)(2,1)}, u32[]{:S(2)}) %copy-start.1) | copy-done | bytes 4194328
  163.7 6.0 %shard_map.47 = f32[64,512]{1,0:T(8,128)} custom-call(s32[8]{0:T(128)S(1)} %fusion.22.at_ref, s32[1]{0:T(128)} %bitcast.core_ref, bf16[8,64,128]{2,1,0:T(8,128)(2,1)S(1)} %pad_maximum_fusion.4.z_ref, bf16[8,64,128]{2,1,0:T(8,128)(2,1)S(1)} %collective-permute-done.44.other_ref, bf16[2048,1024]{1,0:T(8,128)(2,1)S(1)} %copy-done.1), custom_call_target="tpu_custom_call" | custom-call | flops 939524096 | bytes 4456448 | tf_op jit(solution)/shard_map/pallas_call | solution.py:225
  (103 shorter events, 41.1 us)
Async XLA Ops:
  2.1 36.5 %collective-permute-start.3 = (bf16[256,1024]{1,0:T(8,128)(2,1)S(1)}, bf16[256,1024]{1,0:T(8,128)(2,1)S(1)}, u32[]{:S(2)}, u32[]{:S(2)}) collective-permute-start(bf16[256,1024]{1,0:T(8,128)(2,1)S(1)} %get-tuple-element.44), channel_id=1, source_target_pairs={{0,4},{4,0},{8,12},{12,8},{1,5},{5,1},{9,13},{13,9},{2,6},{6,2},{1... | collective-permute-start | bytes 1572872 | tf_op jit(solution)/shard_map/ppermute | solution.py:242
  5.2 33.5 %collective-permute-start.2 = (bf16[256,1024]{1,0:T(8,128)(2,1)S(1)}, bf16[256,1024]{1,0:T(8,128)(2,1)S(1)}, u32[]{:S(2)}, u32[]{:S(2)}) collective-permute-start(bf16[256,1024]{1,0:T(8,128)(2,1)S(1)} %get-tuple-element.46), channel_id=1, source_target_pairs={{0,8},{4,12},{8,0},{12,4},{1,9},{5,13},{9,1},{13,5},{2,10},{6,14},... | collective-permute-start | bytes 1572872 | tf_op jit(solution)/shard_map/ppermute | solution.py:242
  12.4 21.2 %collective-permute-start = (f32[2,64,128]{2,1,0:T(8,128)S(1)}, f32[2,64,128]{2,1,0:T(8,128)S(1)}, u32[]{:S(2)}, u32[]{:S(2)}) collective-permute-start(f32[2,64,128]{2,1,0:T(8,128)S(1)} %bitcast.16), channel_id=1, source_target_pairs={{0,8},{4,12},{8,0},{12,4},{1,9},{5,13},{9,1},{13,5},{2,10},{6,14},... | collective-permute-start | bytes 196616 | tf_op jit(solution)/shard_map/ppermute | solution.py:242
  33.6 5.0 %collective-permute-start.1 = (f32[4,64,128]{2,1,0:T(8,128)S(1)}, f32[4,64,128]{2,1,0:T(8,128)S(1)}, u32[]{:S(2)}, u32[]{:S(2)}) collective-permute-start(f32[4,64,128]{2,1,0:T(8,128)S(1)} %pad_maximum_fusion.1), channel_id=1, source_target_pairs={{0,1},{1,0},{2,3},{3,2},{4,5},{5,4},{6,7},{7,6},{8,9},{9,8},{10,11... | collective-permute-start | bytes 393224 | tf_op jit(solution)/shard_map/ppermute | solution.py:242
  35.2 11.4 %collective-permute-start.5 = (bf16[128,1024]{1,0:T(8,128)(2,1)S(1)}, bf16[128,1024]{1,0:T(8,128)(2,1)S(1)}, u32[]{:S(2)}, u32[]{:S(2)}) collective-permute-start(bf16[128,1024]{1,0:T(8,128)(2,1)S(1)} %get-tuple-element.22), channel_id=1, source_target_pairs={{0,12},{4,8},{8,4},{12,0},{1,13},{5,9},{9,5},{13,1},{2,14},{6,10},... | collective-permute-start | bytes 786440 | tf_op jit(solution)/shard_map/ppermute | solution.py:242
  38.7 7.8 %collective-permute-start.4 = (f32[4,64,128]{2,1,0:T(8,128)S(1)}, f32[4,64,128]{2,1,0:T(8,128)S(1)}, u32[]{:S(2)}, u32[]{:S(2)}) collective-permute-start(f32[4,64,128]{2,1,0:T(8,128)S(1)} %add.218), channel_id=1, source_target_pairs={{0,4},{4,0},{8,12},{12,8},{1,5},{5,1},{9,13},{13,9},{2,6},{6,2},{1... | collective-permute-start | bytes 393224 | tf_op jit(solution)/shard_map/ppermute | solution.py:242
  46.6 10.6 %collective-permute-start.7 = (bf16[128,1024]{1,0:T(8,128)(2,1)S(1)}, bf16[128,1024]{1,0:T(8,128)(2,1)S(1)}, u32[]{:S(2)}, u32[]{:S(2)}) collective-permute-start(bf16[128,1024]{1,0:T(8,128)(2,1)S(1)} %get-tuple-element.26), channel_id=1, source_target_pairs={{0,12},{4,8},{8,4},{12,0},{1,13},{5,9},{9,5},{13,1},{2,14},{6,10},... | collective-permute-start | bytes 786440 | tf_op jit(solution)/shard_map/ppermute | solution.py:242
  49.2 8.6 %collective-permute-start.8 = (bf16[256,1024]{1,0:T(8,128)(2,1)S(1)}, bf16[256,1024]{1,0:T(8,128)(2,1)S(1)}, u32[]{:S(2)}, u32[]{:S(2)}) collective-permute-start(bf16[256,1024]{1,0:T(8,128)(2,1)S(1)} %get-tuple-element.28.refs_0_), channel_id=1, source_target_pairs={{0,2},{2,0},{1,3},{3,1},{4,6},{6,4},{5,7},{7,5},{8,10},{10,8},{9,1... | collective-permute-start | bytes 1572872 | tf_op jit(solution)/shard_map/ppermute | solution.py:242
  49.3 8.5 %collective-permute-start.9 = (bf16[256,1024]{1,0:T(8,128)(2,1)S(1)}, bf16[256,1024]{1,0:T(8,128)(2,1)S(1)}, u32[]{:S(2)}, u32[]{:S(2)}) collective-permute-start(bf16[256,1024]{1,0:T(8,128)(2,1)S(1)} %collective-permute-done.3.refs_1_), channel_id=1, source_target_pairs={{0,2},{2,0},{1,3},{3,1},{4,6},{6,4},{5,7},{7,5},{8,10},{10,8},{9,1... | collective-permute-start | bytes 1572872 | tf_op jit(solution)/shard_map/ppermute | solution.py:242
  49.7 8.1 %collective-permute-start.10 = (bf16[256,1024]{1,0:T(8,128)(2,1)S(1)}, bf16[256,1024]{1,0:T(8,128)(2,1)S(1)}, u32[]{:S(2)}, u32[]{:S(2)}) collective-permute-start(bf16[256,1024]{1,0:T(8,128)(2,1)S(1)} %collective-permute-done.2.refs_2_), channel_id=1, source_target_pairs={{0,2},{2,0},{1,3},{3,1},{4,6},{6,4},{5,7},{7,5},{8,10},{10,8},{9,1... | collective-permute-start | bytes 1572872 | tf_op jit(solution)/shard_map/ppermute | solution.py:242
  61.3 5.9 %collective-permute-start.13 = (f32[2,64,128]{2,1,0:T(8,128)S(1)}, f32[2,64,128]{2,1,0:T(8,128)S(1)}, u32[]{:S(2)}, u32[]{:S(2)}) collective-permute-start(f32[2,64,128]{2,1,0:T(8,128)S(1)} %get-tuple-element.49), channel_id=1, source_target_pairs={{0,1},{1,0},{4,5},{5,4},{8,9},{9,8},{12,13},{13,12},{2,3},{3,2},{6... | collective-permute-start | bytes 196616 | tf_op jit(solution)/shard_map/ppermute | solution.py:242
  61.9 7.7 %collective-permute-start.15 = (f32[2,64,128]{2,1,0:T(8,128)S(1)}, f32[2,64,128]{2,1,0:T(8,128)S(1)}, u32[]{:S(2)}, u32[]{:S(2)}) collective-permute-start(f32[2,64,128]{2,1,0:T(8,128)S(1)} %get-tuple-element.50), channel_id=1, source_target_pairs={{0,5},{1,4},{4,1},{5,0},{8,13},{9,12},{12,9},{13,8},{2,7},{3,6},{6... | collective-permute-start | bytes 196616 | tf_op jit(solution)/shard_map/ppermute | solution.py:242
  67.2 4.3 %collective-permute-start.14 = (f32[2,64,128]{2,1,0:T(8,128)S(1)}, f32[2,64,128]{2,1,0:T(8,128)S(1)}, u32[]{:S(2)}, u32[]{:S(2)}) collective-permute-start(f32[2,64,128]{2,1,0:T(8,128)S(1)} %get-tuple-element.51), channel_id=1, source_target_pairs={{0,4},{1,5},{4,0},{5,1},{8,12},{9,13},{12,8},{13,9},{2,6},{3,7},{6... | collective-permute-start | bytes 196616 | tf_op jit(solution)/shard_map/ppermute | solution.py:242
  71.5 5.9 %collective-permute-start.16 = (f32[2,64,128]{2,1,0:T(8,128)S(1)}, f32[2,64,128]{2,1,0:T(8,128)S(1)}, u32[]{:S(2)}, u32[]{:S(2)}) collective-permute-start(f32[2,64,128]{2,1,0:T(8,128)S(1)} %add_add_fusion), channel_id=1, source_target_pairs={{0,8},{4,12},{8,0},{12,4},{1,9},{5,13},{9,1},{13,5},{2,10},{6,14},... | collective-permute-start | bytes 196616 | tf_op jit(solution)/shard_map/ppermute | solution.py:242
  77.4 6.2 %collective-permute-start.19 = (f32[2,64,128]{2,1,0:T(8,128)S(1)}, f32[2,64,128]{2,1,0:T(8,128)S(1)}, u32[]{:S(2)}, u32[]{:S(2)}) collective-permute-start(f32[2,64,128]{2,1,0:T(8,128)S(1)} %add.225), channel_id=1, source_target_pairs={{0,5},{1,4},{4,1},{5,0},{8,13},{9,12},{12,9},{13,8},{2,7},{3,6},{6... | collective-permute-start | bytes 196616 | tf_op jit(solution)/shard_map/ppermute | solution.py:242
  78.0 5.6 %collective-permute-start.18 = (f32[2,64,128]{2,1,0:T(8,128)S(1)}, f32[2,64,128]{2,1,0:T(8,128)S(1)}, u32[]{:S(2)}, u32[]{:S(2)}) collective-permute-start(f32[2,64,128]{2,1,0:T(8,128)S(1)} %add.225), channel_id=1, source_target_pairs={{0,1},{1,0},{4,5},{5,4},{8,9},{9,8},{12,13},{13,12},{2,3},{3,2},{6... | collective-permute-start | bytes 196616 | tf_op jit(solution)/shard_map/ppermute | solution.py:242
  79.3 4.3 %collective-permute-start.17 = (f32[2,64,128]{2,1,0:T(8,128)S(1)}, f32[2,64,128]{2,1,0:T(8,128)S(1)}, u32[]{:S(2)}, u32[]{:S(2)}) collective-permute-start(f32[2,64,128]{2,1,0:T(8,128)S(1)} %add.225), channel_id=1, source_target_pairs={{0,4},{1,5},{4,0},{5,1},{8,12},{9,13},{12,8},{13,9},{2,6},{3,7},{6... | collective-permute-start | bytes 196616 | tf_op jit(solution)/shard_map/ppermute | solution.py:242
  91.7 4.0 %collective-permute-start.21 = (bf16[2,64,128]{2,1,0:T(8,128)(2,1)S(1)}, bf16[2,64,128]{2,1,0:T(8,128)(2,1)S(1)}, u32[]{:S(2)}, u32[]{:S(2)}) collective-permute-start(bf16[2,64,128]{2,1,0:T(8,128)(2,1)S(1)} %get-tuple-element.58), channel_id=1, source_target_pairs={{0,1},{1,0},{4,5},{5,4},{8,9},{9,8},{12,13},{13,12},{2,3},{3,2},{6... | collective-permute-start | bytes 98312 | tf_op jit(solution)/shard_map/ppermute | solution.py:242
  92.5 5.1 %collective-permute-start.23 = (bf16[2,64,128]{2,1,0:T(8,128)(2,1)S(1)}, bf16[2,64,128]{2,1,0:T(8,128)(2,1)S(1)}, u32[]{:S(2)}, u32[]{:S(2)}) collective-permute-start(bf16[2,64,128]{2,1,0:T(8,128)(2,1)S(1)} %get-tuple-element.59), channel_id=1, source_target_pairs={{0,5},{1,4},{4,1},{5,0},{8,13},{9,12},{12,9},{13,8},{2,7},{3,6},{6... | collective-permute-start | bytes 98312 | tf_op jit(solution)/shard_map/ppermute | solution.py:242
  98.8 5.1 %collective-permute-start.24 = (bf16[2,64,128]{2,1,0:T(8,128)(2,1)S(1)}, bf16[2,64,128]{2,1,0:T(8,128)(2,1)S(1)}, u32[]{:S(2)}, u32[]{:S(2)}) collective-permute-start(bf16[2,64,128]{2,1,0:T(8,128)(2,1)S(1)} %fusion.21), channel_id=1, source_target_pairs={{0,8},{4,12},{8,0},{12,4},{1,9},{5,13},{9,1},{13,5},{2,10},{6,14},... | collective-permute-start | bytes 98312 | tf_op jit(solution)/shard_map/ppermute | solution.py:242
  103.9 5.0 %collective-permute-start.27 = (bf16[2,64,128]{2,1,0:T(8,128)(2,1)S(1)}, bf16[2,64,128]{2,1,0:T(8,128)(2,1)S(1)}, u32[]{:S(2)}, u32[]{:S(2)}) collective-permute-start(bf16[2,64,128]{2,1,0:T(8,128)(2,1)S(1)} %add_convert_fusion.2), channel_id=1, source_target_pairs={{0,5},{1,4},{4,1},{5,0},{8,13},{9,12},{12,9},{13,8},{2,7},{3,6},{6... | collective-permute-start | bytes 98312 | tf_op jit(solution)/shard_map/ppermute | solution.py:242
  104.7 4.3 %collective-permute-start.26 = (bf16[2,64,128]{2,1,0:T(8,128)(2,1)S(1)}, bf16[2,64,128]{2,1,0:T(8,128)(2,1)S(1)}, u32[]{:S(2)}, u32[]{:S(2)}) collective-permute-start(bf16[2,64,128]{2,1,0:T(8,128)(2,1)S(1)} %add_convert_fusion.2), channel_id=1, source_target_pairs={{0,1},{1,0},{4,5},{5,4},{8,9},{9,8},{12,13},{13,12},{2,3},{3,2},{6... | collective-permute-start | bytes 98312 | tf_op jit(solution)/shard_map/ppermute | solution.py:242
  116.8 4.0 %collective-permute-start.29 = (bf16[2,64,128]{2,1,0:T(8,128)(2,1)S(1)}, bf16[2,64,128]{2,1,0:T(8,128)(2,1)S(1)}, u32[]{:S(2)}, u32[]{:S(2)}) collective-permute-start(bf16[2,64,128]{2,1,0:T(8,128)(2,1)S(1)} %get-tuple-element.55), channel_id=1, source_target_pairs={{0,1},{1,0},{4,5},{5,4},{8,9},{9,8},{12,13},{13,12},{2,3},{3,2},{6... | collective-permute-start | bytes 98312 | tf_op jit(solution)/shard_map/ppermute | solution.py:242
  117.9 4.9 %collective-permute-start.31 = (bf16[2,64,128]{2,1,0:T(8,128)(2,1)S(1)}, bf16[2,64,128]{2,1,0:T(8,128)(2,1)S(1)}, u32[]{:S(2)}, u32[]{:S(2)}) collective-permute-start(bf16[2,64,128]{2,1,0:T(8,128)(2,1)S(1)} %get-tuple-element.56), channel_id=1, source_target_pairs={{0,5},{1,4},{4,1},{5,0},{8,13},{9,12},{12,9},{13,8},{2,7},{3,6},{6... | collective-permute-start | bytes 98312 | tf_op jit(solution)/shard_map/ppermute | solution.py:242
  124.1 5.0 %collective-permute-start.32 = (bf16[2,64,128]{2,1,0:T(8,128)(2,1)S(1)}, bf16[2,64,128]{2,1,0:T(8,128)(2,1)S(1)}, u32[]{:S(2)}, u32[]{:S(2)}) collective-permute-start(bf16[2,64,128]{2,1,0:T(8,128)(2,1)S(1)} %fusion.18), channel_id=1, source_target_pairs={{0,8},{4,12},{8,0},{12,4},{1,9},{5,13},{9,1},{13,5},{2,10},{6,14},... | collective-permute-start | bytes 98312 | tf_op jit(solution)/shard_map/ppermute | solution.py:242
  129.2 5.0 %collective-permute-start.35 = (bf16[2,64,128]{2,1,0:T(8,128)(2,1)S(1)}, bf16[2,64,128]{2,1,0:T(8,128)(2,1)S(1)}, u32[]{:S(2)}, u32[]{:S(2)}) collective-permute-start(bf16[2,64,128]{2,1,0:T(8,128)(2,1)S(1)} %add_convert_fusion.1), channel_id=1, source_target_pairs={{0,5},{1,4},{4,1},{5,0},{8,13},{9,12},{12,9},{13,8},{2,7},{3,6},{6... | collective-permute-start | bytes 98312 | tf_op jit(solution)/shard_map/ppermute | solution.py:242
  130.0 4.3 %collective-permute-start.34 = (bf16[2,64,128]{2,1,0:T(8,128)(2,1)S(1)}, bf16[2,64,128]{2,1,0:T(8,128)(2,1)S(1)}, u32[]{:S(2)}, u32[]{:S(2)}) collective-permute-start(bf16[2,64,128]{2,1,0:T(8,128)(2,1)S(1)} %add_convert_fusion.1), channel_id=1, source_target_pairs={{0,1},{1,0},{4,5},{5,4},{8,9},{9,8},{12,13},{13,12},{2,3},{3,2},{6... | collective-permute-start | bytes 98312 | tf_op jit(solution)/shard_map/ppermute | solution.py:242
  142.0 4.0 %collective-permute-start.37 = (bf16[2,64,128]{2,1,0:T(8,128)(2,1)S(1)}, bf16[2,64,128]{2,1,0:T(8,128)(2,1)S(1)}, u32[]{:S(2)}, u32[]{:S(2)}) collective-permute-start(bf16[2,64,128]{2,1,0:T(8,128)(2,1)S(1)} %get-tuple-element.52), channel_id=1, source_target_pairs={{0,1},{1,0},{4,5},{5,4},{8,9},{9,8},{12,13},{13,12},{2,3},{3,2},{6... | collective-permute-start | bytes 98312 | tf_op jit(solution)/shard_map/ppermute | solution.py:242
  143.2 4.9 %collective-permute-start.39 = (bf16[2,64,128]{2,1,0:T(8,128)(2,1)S(1)}, bf16[2,64,128]{2,1,0:T(8,128)(2,1)S(1)}, u32[]{:S(2)}, u32[]{:S(2)}) collective-permute-start(bf16[2,64,128]{2,1,0:T(8,128)(2,1)S(1)} %get-tuple-element.53), channel_id=1, source_target_pairs={{0,5},{1,4},{4,1},{5,0},{8,13},{9,12},{12,9},{13,8},{2,7},{3,6},{6... | collective-permute-start | bytes 98312 | tf_op jit(solution)/shard_map/ppermute | solution.py:242
  149.3 5.0 %collective-permute-start.40 = (bf16[2,64,128]{2,1,0:T(8,128)(2,1)S(1)}, bf16[2,64,128]{2,1,0:T(8,128)(2,1)S(1)}, u32[]{:S(2)}, u32[]{:S(2)}) collective-permute-start(bf16[2,64,128]{2,1,0:T(8,128)(2,1)S(1)} %fusion.15), channel_id=1, source_target_pairs={{0,8},{4,12},{8,0},{12,4},{1,9},{5,13},{9,1},{13,5},{2,10},{6,14},... | collective-permute-start | bytes 98312 | tf_op jit(solution)/shard_map/ppermute | solution.py:242
  154.4 5.0 %collective-permute-start.43 = (bf16[2,64,128]{2,1,0:T(8,128)(2,1)S(1)}, bf16[2,64,128]{2,1,0:T(8,128)(2,1)S(1)}, u32[]{:S(2)}, u32[]{:S(2)}) collective-permute-start(bf16[2,64,128]{2,1,0:T(8,128)(2,1)S(1)} %add_convert_fusion), channel_id=1, source_target_pairs={{0,5},{1,4},{4,1},{5,0},{8,13},{9,12},{12,9},{13,8},{2,7},{3,6},{6... | collective-permute-start | bytes 98312 | tf_op jit(solution)/shard_map/ppermute | solution.py:242
  155.2 4.3 %collective-permute-start.42 = (bf16[2,64,128]{2,1,0:T(8,128)(2,1)S(1)}, bf16[2,64,128]{2,1,0:T(8,128)(2,1)S(1)}, u32[]{:S(2)}, u32[]{:S(2)}) collective-permute-start(bf16[2,64,128]{2,1,0:T(8,128)(2,1)S(1)} %add_convert_fusion), channel_id=1, source_target_pairs={{0,1},{1,0},{4,5},{5,4},{8,9},{9,8},{12,13},{13,12},{2,3},{3,2},{6... | collective-permute-start | bytes 98312 | tf_op jit(solution)/shard_map/ppermute | solution.py:242
  (15 other events, 113.2 us)

commit v21 on v20

--- a/solution.py
+++ b/solution.py
@@ -13,6 +13,7 @@
 LANES = 128
 SUB = 8
 TILE = 256
+ROW_TILE = 512
 
 
 shift_ratio = 0.005
@@ -72,9 +73,12 @@
 def gram_of(terms):
     if len(terms) == 1:
         return dot_nt(terms[0], terms[0])
-    rank = terms[0].shape[0]
     stacked = jnp.concatenate(terms, axis=0)
-    both = dot_nt(stacked, stacked)
+    return fold_gram(dot_nt(stacked, stacked))
+
+
+def fold_gram(both):
+    rank = both.shape[0] // 3
     cross = both[rank : 2 * rank, :rank] + both[2 * rank :, :rank]
     return both[:rank, :rank] + ((cross + cross.T) + both[rank : 2 * rank, rank : 2 * rank])
 
@@ -162,13 +166,17 @@
     wide = wide_of(at_ref, z_refs)
     terms = terms_of(wide)
     upper, inverse_one = shifted_factor(wide, terms)
-    return terms_of(small_times_wide(inverse_one, terms)), upper
+    tiles, both = [], 0.0
+    for start in range(0, wide.shape[1], ROW_TILE):
+        part = small_times_wide(inverse_one, [term[:, start : start + ROW_TILE] for term in terms])
+        tiles.append(jnp.concatenate(terms_of(part), axis=0))
+        both = both + dot_nt(tiles[-1], tiles[-1])
+    return jnp.concatenate(tiles, axis=1), fold_gram(both), upper
 
 
 def back_product(at_ref, z_refs, a):
-    terms, unused = first_pass(at_ref, z_refs)
-    rank = terms[0].shape[0]
-    stacked = jnp.concatenate(terms, axis=0)
+    stacked, gram, unused = first_pass(at_ref, z_refs)
+    rank = gram.shape[0]
     tiles = []
 
     def tile(start):
@@ -177,7 +185,7 @@
 
     starts = range(0, a.shape[1], TILE)
     work = [functools.partial(tile, start) for start in starts]
-    unused, inverse_two = eliminate(gram_of(terms), work)
+    unused, inverse_two = eliminate(gram, work)
     return small_times_wide(inverse_two, terms_of(jnp.concatenate(tiles, axis=1)))
 
 
@@ -188,8 +196,10 @@
 
 
 def orth_kernel(at_ref, z_ref, other_ref, basis_ref, upper_ref):
-    terms, upper = first_pass(at_ref, (z_ref, other_ref))
-    unused, inverse_two = eliminate(gram_of(terms))
+    stacked, gram, upper = first_pass(at_ref, (z_ref, other_ref))
+    unused, inverse_two = eliminate(gram)
+    rank = gram.shape[0]
+    terms = [stacked[rank * i : rank * (i + 1)] for i in range(3)]
     basis_ref[...] = small_times_wide(inverse_two, terms).astype(jnp.bfloat16)
     upper_ref[...] = upper
 
@@ -245,7 +255,7 @@
 def square_devices():
     n_z, n_col = lax.axis_size("z"), lax.axis_size("col")
     sides = [(z, col) for z in range(2 if n_z > 2 else 1) for col in range(n_col)]
-    return [(z * n_col + col, col * (2 if n_z > 2 else 1) + z) for z, col in sides[1:]]
+    return [(z * n_col + col, col * (2 if n_z > 2 else 1) + z) for z, col in sides[:0:-1]]
 
 
 def sum_parts(total, dtype):

time: 170 us -> 169 us (level)
  starting transfers between devices: 47.7 us -> 45.9 us
    ppermute x45, starting transfers between devices: 47.7 us -> 45.9 us  [from_xor(): return lax.ppermute(value, axis, [(i, i ^ offset) for i in range(size)])]
  transfers between devices with their start and end apart: 45 -> 45, of which waited for: 35 -> 33; matrix products, arithmetic and copies ran while one was open for 3% -> 3% of each run, Pallas kernels for 4% -> 4%
where the time goes in v21:
time: 169 us; the launch traced here: 168 us
  waiting for transfers between devices  78.4 us (46%)
  starting transfers between devices  45.9 us (27%)
  Pallas kernels  32.8 us (19%)
  local copies, waits for them, and re-layouts  5.55 us (3%)
  matrix products  3.83 us (2%)
    ppermute x45, waiting for transfers between devices, from_xor(): return lax.ppermute(value, axis, [(i, i ^ offset) for i in range(size)])  78.4 us
    ppermute x45, starting transfers between devices, from_xor(): return lax.ppermute(value, axis, [(i, i ^ offset) for i in range(size)])  45.9 us
    pallas_call x7, Pallas kernels, call(): pl.pallas_call(kernel, out_shape=out_shapes, in_specs=[pl.BlockSpec(memor...  32.8 us
    dot_general x1, matrix products, per_device_transposed(): lax.dot_general(omega, states, (((0,), (1,)), ((), ())), preferred_elemen...  3.83 us
  transfers between devices with their start and end apart: 45, of which 33 were waited for; matrix products, arithmetic and copies ran while one was open for 3% of the time, Pallas kernels for 4%

profile of v21, /device:TPU:0, one launch (start us, length us, event | category | flops | bytes accessed | tf_op | source)
XLA Modules:
  0.0 168.5 jit_solution(14754215082787914023)
XLA Ops:
  2.1 3.1 %collective-permute-start.3 = (bf16[256,1024]{1,0:T(8,128)(2,1)S(1)}, bf16[256,1024]{1,0:T(8,128)(2,1)S(1)}, u32[]{:S(2)}, u32[]{:S(2)}) collective-permute-start(bf16[256,1024]{1,0:T(8,128)(2,1)S(1)} %get-tuple-element.44), channel_id=1, source_target_pairs={{0,4},{4,0},{8,12},{12,8},{1,5},{5,1},{9,13},{13,9},{2,6},{6,2},{1... | collective-permute-start | bytes 1572872 | tf_op jit(solution)/shard_map/ppermute | solution.py:252
  5.2 2.6 %collective-permute-start.2 = (bf16[256,1024]{1,0:T(8,128)(2,1)S(1)}, bf16[256,1024]{1,0:T(8,128)(2,1)S(1)}, u32[]{:S(2)}, u32[]{:S(2)}) collective-permute-start(bf16[256,1024]{1,0:T(8,128)(2,1)S(1)} %get-tuple-element.46), channel_id=1, source_target_pairs={{0,8},{4,12},{8,0},{12,4},{1,9},{5,13},{9,1},{13,5},{2,10},{6,14},... | collective-permute-start | bytes 1572872 | tf_op jit(solution)/shard_map/ppermute | solution.py:252
  8.5 3.8 %convolution_bitcast_fusion = f32[8,2,8,128]{3,2,1,0:T(8,128)S(1)} fusion(bf16[256,4096]{1,0:T(8,128)(2,1)} %param.3, s32[]{:T(128)S(6)} %xor.73, s32[4096]{0:T(1024)S(1)} %add_multiply_fusion), kind=kOutput, calls=%fused_computation | convolution fusion | flops 152043520 | bytes 2179076 | tf_op jit(solution)/shard_map/dot_general | solution.py:327
  13.8 19.8 %collective-permute-done = f32[2,64,128]{2,1,0:T(8,128)S(1)} collective-permute-done((f32[2,64,128]{2,1,0:T(8,128)S(1)}, f32[2,64,128]{2,1,0:T(8,128)S(1)}, u32[]{:S(2)}, u32[]{:S(2)}) %collective-permute-start) | collective-permute-done | bytes 65568 | tf_op jit(solution)/shard_map/ppermute | solution.py:252
  33.6 1.6 collective-permute-start.1
  35.2 3.0 %collective-permute-start.5 = (bf16[128,1024]{1,0:T(8,128)(2,1)S(1)}, bf16[128,1024]{1,0:T(8,128)(2,1)S(1)}, u32[]{:S(2)}, u32[]{:S(2)}) collective-permute-start(bf16[128,1024]{1,0:T(8,128)(2,1)S(1)} %get-tuple-element.22), channel_id=1, source_target_pairs={{0,12},{4,8},{8,4},{12,0},{1,13},{5,9},{9,5},{13,1},{2,14},{6,10},... | collective-permute-start | bytes 786440 | tf_op jit(solution)/shard_map/ppermute | solution.py:252
  38.8 7.7 %collective-permute-done.4 = f32[4,64,128]{2,1,0:T(8,128)S(1)} collective-permute-done((f32[4,64,128]{2,1,0:T(8,128)S(1)}, f32[4,64,128]{2,1,0:T(8,128)S(1)}, u32[]{:S(2)}, u32[]{:S(2)}) %collective-permute-start.4) | collective-permute-done | bytes 131104 | tf_op jit(solution)/shard_map/ppermute | solution.py:252
  46.6 2.5 %collective-permute-start.7 = (bf16[128,1024]{1,0:T(8,128)(2,1)S(1)}, bf16[128,1024]{1,0:T(8,128)(2,1)S(1)}, u32[]{:S(2)}, u32[]{:S(2)}) collective-permute-start(bf16[128,1024]{1,0:T(8,128)(2,1)S(1)} %get-tuple-element.26), channel_id=1, source_target_pairs={{0,12},{4,8},{8,4},{12,0},{1,13},{5,9},{9,5},{13,1},{2,14},{6,10},... | collective-permute-start | bytes 786440 | tf_op jit(solution)/shard_map/ppermute | solution.py:252
  49.9 6.1 %shard_map.41 = (bf16[64,2048]{1,0:T(8,128)(2,1)S(1)}, f32[64,64]{1,0:T(8,128)S(1)}) custom-call(s32[8]{0:T(128)S(1)} %fusion.24.at_ref, f32[8,64,128]{2,1,0:T(8,128)S(1)} %pad_maximum_fusion.z_ref, f32[8,64,128]{2,1,0:T(8,128)S(1)} %collective-permute-done.6.other_ref), custom_call_target="tpu_custom_call" | custom-call | flops 402653184 | bytes 524288 | tf_op jit(solution)/shard_map/pallas_call | solution.py:235
  59.2 2.1 %shard_map.42 = (bf16[2048,1024]{1,0:T(8,128)(2,1)S(1)}, f32[8,64,128]{2,1,0:T(8,128)S(1)}) custom-call(s32[8]{0:T(128)S(1)} %fusion.22.at_ref, bf16[64,2048]{1,0:T(8,128)(2,1)S(1)} %get-tuple-element.27.basis_ref, bf16[256,1024]{1,0:T(8,128)(2,1)S(1)} %get-tuple-element.28.refs_0_, bf16[256,1024]{1,0:T(8,128)(2,1)S(1)} %collective-permute-done.3.refs_1_, ...), custom_call_target="tpu_custom_call" | custom-call | flops 939524096 | bytes 4456448 | tf_op jit(solution)/shard_map/pallas_call | solution.py:235
  61.3 4.4 %collective-permute-start.13 = (f32[2,64,128]{2,1,0:T(8,128)S(1)}, f32[2,64,128]{2,1,0:T(8,128)S(1)}, u32[]{:S(2)}, u32[]{:S(2)}) collective-permute-start(f32[2,64,128]{2,1,0:T(8,128)S(1)} %get-tuple-element.49), channel_id=1, source_target_pairs={{0,5},{1,4},{4,1},{5,0},{8,13},{9,12},{12,9},{13,8},{2,7},{3,6},{6... | collective-permute-start | bytes 196616 | tf_op jit(solution)/shard_map/ppermute | solution.py:252
  68.1 1.9 %collective-permute-done.15 = f32[2,64,128]{2,1,0:T(8,128)S(1)} collective-permute-done((f32[2,64,128]{2,1,0:T(8,128)S(1)}, f32[2,64,128]{2,1,0:T(8,128)S(1)}, u32[]{:S(2)}, u32[]{:S(2)}) %collective-permute-start.15) | collective-permute-done | bytes 65568 | tf_op jit(solution)/shard_map/ppermute | solution.py:252
  72.2 4.7 %collective-permute-done.16 = f32[2,64,128]{2,1,0:T(8,128)S(1)} collective-permute-done((f32[2,64,128]{2,1,0:T(8,128)S(1)}, f32[2,64,128]{2,1,0:T(8,128)S(1)}, u32[]{:S(2)}, u32[]{:S(2)}) %collective-permute-start.16) | collective-permute-done | bytes 65568 | tf_op jit(solution)/shard_map/ppermute | solution.py:252
  78.3 2.2 %collective-permute-start.17 = (f32[2,64,128]{2,1,0:T(8,128)S(1)}, f32[2,64,128]{2,1,0:T(8,128)S(1)}, u32[]{:S(2)}, u32[]{:S(2)}) collective-permute-start(f32[2,64,128]{2,1,0:T(8,128)S(1)} %add.225), channel_id=1, source_target_pairs={{0,4},{1,5},{4,0},{5,1},{8,12},{9,13},{12,8},{13,9},{2,6},{3,7},{6... | collective-permute-start | bytes 196616 | tf_op jit(solution)/shard_map/ppermute | solution.py:252
  80.5 2.2 %collective-permute-done.17 = f32[2,64,128]{2,1,0:T(8,128)S(1)} collective-permute-done((f32[2,64,128]{2,1,0:T(8,128)S(1)}, f32[2,64,128]{2,1,0:T(8,128)S(1)}, u32[]{:S(2)}, u32[]{:S(2)}) %collective-permute-start.17) | collective-permute-done | bytes 65568 | tf_op jit(solution)/shard_map/ppermute | solution.py:252
  84.4 6.5 %shard_map.44 = f32[8,64,128]{2,1,0:T(8,128)S(1)} custom-call(s32[8]{0:T(128)S(1)} %fusion.22.at_ref, f32[8,64,128]{2,1,0:T(8,128)S(1)} %constant_dynamic-update-slice_fusion.z_ref, f32[8,64,128]{2,1,0:T(8,128)S(1)} %collective-permute-done.20.other_ref, bf16[2048,1024]{1,0:T(8,128)(2,1)S(1)} %get-tuple-element.34.a_ref, ...), custom_call_target="tpu_custom_call" | custom-call | flops 939524096 | bytes 6815744 | tf_op jit(solution)/shard_map/pallas_call | solution.py:235
  90.9 2.6 %collective-permute-start.21 = (bf16[2,64,128]{2,1,0:T(8,128)(2,1)S(1)}, bf16[2,64,128]{2,1,0:T(8,128)(2,1)S(1)}, u32[]{:S(2)}, u32[]{:S(2)}) collective-permute-start(bf16[2,64,128]{2,1,0:T(8,128)(2,1)S(1)} %get-tuple-element.58), channel_id=1, source_target_pairs={{0,5},{1,4},{4,1},{5,0},{8,13},{9,12},{12,9},{13,8},{2,7},{3,6},{6... | collective-permute-start | bytes 98312 | tf_op jit(solution)/shard_map/ppermute | solution.py:252
  95.8 1.6 collective-permute-done.23
  98.5 4.8 %collective-permute-done.24 = bf16[2,64,128]{2,1,0:T(8,128)(2,1)S(1)} collective-permute-done((bf16[2,64,128]{2,1,0:T(8,128)(2,1)S(1)}, bf16[2,64,128]{2,1,0:T(8,128)(2,1)S(1)}, u32[]{:S(2)}, u32[]{:S(2)}) %collective-permute-start.24) | collective-permute-done | bytes 32800 | tf_op jit(solution)/shard_map/ppermute | solution.py:252
  104.9 2.0 %collective-permute-start.25 = (bf16[2,64,128]{2,1,0:T(8,128)(2,1)S(1)}, bf16[2,64,128]{2,1,0:T(8,128)(2,1)S(1)}, u32[]{:S(2)}, u32[]{:S(2)}) collective-permute-start(bf16[2,64,128]{2,1,0:T(8,128)(2,1)S(1)} %add_convert_fusion.2), channel_id=1, source_target_pairs={{0,4},{1,5},{4,0},{5,1},{8,12},{9,13},{12,8},{13,9},{2,6},{3,7},{6... | collective-permute-start | bytes 98312 | tf_op jit(solution)/shard_map/ppermute | solution.py:252
  110.2 5.7 %shard_map.45 = f32[8,64,128]{2,1,0:T(8,128)S(1)} custom-call(s32[8]{0:T(128)S(1)} %fusion.22.at_ref, bf16[8,64,128]{2,1,0:T(8,128)(2,1)S(1)} %pad_maximum_fusion.2.z_ref, bf16[8,64,128]{2,1,0:T(8,128)(2,1)S(1)} %collective-permute-done.28.other_ref, bf16[2048,1024]{1,0:T(8,128)(2,1)S(1)} %get-tuple-element.34.a_ref, bf16[1024,1024]{1,0:T(8,128)(2,1)S(1)} %shard_map.43.turned_ref), custom_call_target="tpu_custom_call" | custom-call | flops 939524096 | bytes 6553600 | tf_op jit(solution)/shard_map/pallas_call | solution.py:235
  115.9 2.6 %collective-permute-start.29 = (bf16[2,64,128]{2,1,0:T(8,128)(2,1)S(1)}, bf16[2,64,128]{2,1,0:T(8,128)(2,1)S(1)}, u32[]{:S(2)}, u32[]{:S(2)}) collective-permute-start(bf16[2,64,128]{2,1,0:T(8,128)(2,1)S(1)} %get-tuple-element.55), channel_id=1, source_target_pairs={{0,5},{1,4},{4,1},{5,0},{8,13},{9,12},{12,9},{13,8},{2,7},{3,6},{6... | collective-permute-start | bytes 98312 | tf_op jit(solution)/shard_map/ppermute | solution.py:252
  120.8 1.6 collective-permute-done.31
  123.5 4.8 %collective-permute-done.32 = bf16[2,64,128]{2,1,0:T(8,128)(2,1)S(1)} collective-permute-done((bf16[2,64,128]{2,1,0:T(8,128)(2,1)S(1)}, bf16[2,64,128]{2,1,0:T(8,128)(2,1)S(1)}, u32[]{:S(2)}, u32[]{:S(2)}) %collective-permute-start.32) | collective-permute-done | bytes 32800 | tf_op jit(solution)/shard_map/ppermute | solution.py:252
  129.9 2.0 %collective-permute-start.33 = (bf16[2,64,128]{2,1,0:T(8,128)(2,1)S(1)}, bf16[2,64,128]{2,1,0:T(8,128)(2,1)S(1)}, u32[]{:S(2)}, u32[]{:S(2)}) collective-permute-start(bf16[2,64,128]{2,1,0:T(8,128)(2,1)S(1)} %add_convert_fusion.1), channel_id=1, source_target_pairs={{0,4},{1,5},{4,0},{5,1},{8,12},{9,13},{12,8},{13,9},{2,6},{3,7},{6... | collective-permute-start | bytes 98312 | tf_op jit(solution)/shard_map/ppermute | solution.py:252
  135.2 5.7 %shard_map.46 = f32[8,64,128]{2,1,0:T(8,128)S(1)} custom-call(s32[8]{0:T(128)S(1)} %fusion.22.at_ref, bf16[8,64,128]{2,1,0:T(8,128)(2,1)S(1)} %pad_maximum_fusion.3.z_ref, bf16[8,64,128]{2,1,0:T(8,128)(2,1)S(1)} %collective-permute-done.36.other_ref, bf16[2048,1024]{1,0:T(8,128)(2,1)S(1)} %get-tuple-element.34.a_ref, bf16[1024,1024]{1,0:T(8,128)(2,1)S(1)} %shard_map.43.turned_ref), custom_call_target="tpu_custom_call" | custom-call | flops 939524096 | bytes 6553600 | tf_op jit(solution)/shard_map/pallas_call | solution.py:235
  140.9 2.6 %collective-permute-start.37 = (bf16[2,64,128]{2,1,0:T(8,128)(2,1)S(1)}, bf16[2,64,128]{2,1,0:T(8,128)(2,1)S(1)}, u32[]{:S(2)}, u32[]{:S(2)}) collective-permute-start(bf16[2,64,128]{2,1,0:T(8,128)(2,1)S(1)} %get-tuple-element.52), channel_id=1, source_target_pairs={{0,5},{1,4},{4,1},{5,0},{8,13},{9,12},{12,9},{13,8},{2,7},{3,6},{6... | collective-permute-start | bytes 98312 | tf_op jit(solution)/shard_map/ppermute | solution.py:252
  145.8 1.6 collective-permute-done.39
  148.5 4.8 %collective-permute-done.40 = bf16[2,64,128]{2,1,0:T(8,128)(2,1)S(1)} collective-permute-done((bf16[2,64,128]{2,1,0:T(8,128)(2,1)S(1)}, bf16[2,64,128]{2,1,0:T(8,128)(2,1)S(1)}, u32[]{:S(2)}, u32[]{:S(2)}) %collective-permute-start.40) | collective-permute-done | bytes 32800 | tf_op jit(solution)/shard_map/ppermute | solution.py:252
  154.9 2.0 %collective-permute-start.41 = (bf16[2,64,128]{2,1,0:T(8,128)(2,1)S(1)}, bf16[2,64,128]{2,1,0:T(8,128)(2,1)S(1)}, u32[]{:S(2)}, u32[]{:S(2)}) collective-permute-start(bf16[2,64,128]{2,1,0:T(8,128)(2,1)S(1)} %add_convert_fusion), channel_id=1, source_target_pairs={{0,4},{1,5},{4,0},{5,1},{8,12},{9,13},{12,8},{13,9},{2,6},{3,7},{6... | collective-permute-start | bytes 98312 | tf_op jit(solution)/shard_map/ppermute | solution.py:252
  160.2 2.2 %copy-done.1 = bf16[2048,1024]{1,0:T(8,128)(2,1)S(1)} copy-done((bf16[2048,1024]{1,0:T(8,128)(2,1)S(1)}, bf16[2048,1024]{1,0:T(8,128)(2,1)}, u32[]{:S(2)}) %copy-start.1) | copy-done | bytes 4194328
  162.4 6.1 %shard_map.47 = f32[64,512]{1,0:T(8,128)} custom-call(s32[8]{0:T(128)S(1)} %fusion.22.at_ref, s32[1]{0:T(128)} %bitcast.core_ref, bf16[8,64,128]{2,1,0:T(8,128)(2,1)S(1)} %pad_maximum_fusion.4.z_ref, bf16[8,64,128]{2,1,0:T(8,128)(2,1)S(1)} %collective-permute-done.44.other_ref, bf16[2048,1024]{1,0:T(8,128)(2,1)S(1)} %copy-done.1), custom_call_target="tpu_custom_call" | custom-call | flops 939524096 | bytes 4456448 | tf_op jit(solution)/shard_map/pallas_call | solution.py:235
  (103 shorter events, 40.0 us)
Async XLA Ops:
  2.1 36.5 %collective-permute-start.3 = (bf16[256,1024]{1,0:T(8,128)(2,1)S(1)}, bf16[256,1024]{1,0:T(8,128)(2,1)S(1)}, u32[]{:S(2)}, u32[]{:S(2)}) collective-permute-start(bf16[256,1024]{1,0:T(8,128)(2,1)S(1)} %get-tuple-element.44), channel_id=1, source_target_pairs={{0,4},{4,0},{8,12},{12,8},{1,5},{5,1},{9,13},{13,9},{2,6},{6,2},{1... | collective-permute-start | bytes 1572872 | tf_op jit(solution)/shard_map/ppermute | solution.py:252
  5.2 33.5 %collective-permute-start.2 = (bf16[256,1024]{1,0:T(8,128)(2,1)S(1)}, bf16[256,1024]{1,0:T(8,128)(2,1)S(1)}, u32[]{:S(2)}, u32[]{:S(2)}) collective-permute-start(bf16[256,1024]{1,0:T(8,128)(2,1)S(1)} %get-tuple-element.46), channel_id=1, source_target_pairs={{0,8},{4,12},{8,0},{12,4},{1,9},{5,13},{9,1},{13,5},{2,10},{6,14},... | collective-permute-start | bytes 1572872 | tf_op jit(solution)/shard_map/ppermute | solution.py:252
  12.4 21.2 %collective-permute-start = (f32[2,64,128]{2,1,0:T(8,128)S(1)}, f32[2,64,128]{2,1,0:T(8,128)S(1)}, u32[]{:S(2)}, u32[]{:S(2)}) collective-permute-start(f32[2,64,128]{2,1,0:T(8,128)S(1)} %bitcast.16), channel_id=1, source_target_pairs={{0,8},{4,12},{8,0},{12,4},{1,9},{5,13},{9,1},{13,5},{2,10},{6,14},... | collective-permute-start | bytes 196616 | tf_op jit(solution)/shard_map/ppermute | solution.py:252
  33.6 5.0 %collective-permute-start.1 = (f32[4,64,128]{2,1,0:T(8,128)S(1)}, f32[4,64,128]{2,1,0:T(8,128)S(1)}, u32[]{:S(2)}, u32[]{:S(2)}) collective-permute-start(f32[4,64,128]{2,1,0:T(8,128)S(1)} %pad_maximum_fusion.1), channel_id=1, source_target_pairs={{0,1},{1,0},{2,3},{3,2},{4,5},{5,4},{6,7},{7,6},{8,9},{9,8},{10,11... | collective-permute-start | bytes 393224 | tf_op jit(solution)/shard_map/ppermute | solution.py:252
  35.2 11.4 %collective-permute-start.5 = (bf16[128,1024]{1,0:T(8,128)(2,1)S(1)}, bf16[128,1024]{1,0:T(8,128)(2,1)S(1)}, u32[]{:S(2)}, u32[]{:S(2)}) collective-permute-start(bf16[128,1024]{1,0:T(8,128)(2,1)S(1)} %get-tuple-element.22), channel_id=1, source_target_pairs={{0,12},{4,8},{8,4},{12,0},{1,13},{5,9},{9,5},{13,1},{2,14},{6,10},... | collective-permute-start | bytes 786440 | tf_op jit(solution)/shard_map/ppermute | solution.py:252
  38.7 7.8 %collective-permute-start.4 = (f32[4,64,128]{2,1,0:T(8,128)S(1)}, f32[4,64,128]{2,1,0:T(8,128)S(1)}, u32[]{:S(2)}, u32[]{:S(2)}) collective-permute-start(f32[4,64,128]{2,1,0:T(8,128)S(1)} %add.218), channel_id=1, source_target_pairs={{0,4},{4,0},{8,12},{12,8},{1,5},{5,1},{9,13},{13,9},{2,6},{6,2},{1... | collective-permute-start | bytes 393224 | tf_op jit(solution)/shard_map/ppermute | solution.py:252
  46.6 10.6 %collective-permute-start.7 = (bf16[128,1024]{1,0:T(8,128)(2,1)S(1)}, bf16[128,1024]{1,0:T(8,128)(2,1)S(1)}, u32[]{:S(2)}, u32[]{:S(2)}) collective-permute-start(bf16[128,1024]{1,0:T(8,128)(2,1)S(1)} %get-tuple-element.26), channel_id=1, source_target_pairs={{0,12},{4,8},{8,4},{12,0},{1,13},{5,9},{9,5},{13,1},{2,14},{6,10},... | collective-permute-start | bytes 786440 | tf_op jit(solution)/shard_map/ppermute | solution.py:252
  49.2 8.6 %collective-permute-start.8 = (bf16[256,1024]{1,0:T(8,128)(2,1)S(1)}, bf16[256,1024]{1,0:T(8,128)(2,1)S(1)}, u32[]{:S(2)}, u32[]{:S(2)}) collective-permute-start(bf16[256,1024]{1,0:T(8,128)(2,1)S(1)} %get-tuple-element.28.refs_0_), channel_id=1, source_target_pairs={{0,2},{2,0},{1,3},{3,1},{4,6},{6,4},{5,7},{7,5},{8,10},{10,8},{9,1... | collective-permute-start | bytes 1572872 | tf_op jit(solution)/shard_map/ppermute | solution.py:252
  49.3 8.5 %collective-permute-start.9 = (bf16[256,1024]{1,0:T(8,128)(2,1)S(1)}, bf16[256,1024]{1,0:T(8,128)(2,1)S(1)}, u32[]{:S(2)}, u32[]{:S(2)}) collective-permute-start(bf16[256,1024]{1,0:T(8,128)(2,1)S(1)} %collective-permute-done.3.refs_1_), channel_id=1, source_target_pairs={{0,2},{2,0},{1,3},{3,1},{4,6},{6,4},{5,7},{7,5},{8,10},{10,8},{9,1... | collective-permute-start | bytes 1572872 | tf_op jit(solution)/shard_map/ppermute | solution.py:252
  49.7 8.1 %collective-permute-start.10 = (bf16[256,1024]{1,0:T(8,128)(2,1)S(1)}, bf16[256,1024]{1,0:T(8,128)(2,1)S(1)}, u32[]{:S(2)}, u32[]{:S(2)}) collective-permute-start(bf16[256,1024]{1,0:T(8,128)(2,1)S(1)} %collective-permute-done.2.refs_2_), channel_id=1, source_target_pairs={{0,2},{2,0},{1,3},{3,1},{4,6},{6,4},{5,7},{7,5},{8,10},{10,8},{9,1... | collective-permute-start | bytes 1572872 | tf_op jit(solution)/shard_map/ppermute | solution.py:252
  61.3 6.8 %collective-permute-start.13 = (f32[2,64,128]{2,1,0:T(8,128)S(1)}, f32[2,64,128]{2,1,0:T(8,128)S(1)}, u32[]{:S(2)}, u32[]{:S(2)}) collective-permute-start(f32[2,64,128]{2,1,0:T(8,128)S(1)} %get-tuple-element.49), channel_id=1, source_target_pairs={{0,5},{1,4},{4,1},{5,0},{8,13},{9,12},{12,9},{13,8},{2,7},{3,6},{6... | collective-permute-start | bytes 196616 | tf_op jit(solution)/shard_map/ppermute | solution.py:252
  65.7 4.3 %collective-permute-start.15 = (f32[2,64,128]{2,1,0:T(8,128)S(1)}, f32[2,64,128]{2,1,0:T(8,128)S(1)}, u32[]{:S(2)}, u32[]{:S(2)}) collective-permute-start(f32[2,64,128]{2,1,0:T(8,128)S(1)} %get-tuple-element.50), channel_id=1, source_target_pairs={{0,1},{1,0},{4,5},{5,4},{8,9},{9,8},{12,13},{13,12},{2,3},{3,2},{6... | collective-permute-start | bytes 196616 | tf_op jit(solution)/shard_map/ppermute | solution.py:252
  67.2 4.3 %collective-permute-start.14 = (f32[2,64,128]{2,1,0:T(8,128)S(1)}, f32[2,64,128]{2,1,0:T(8,128)S(1)}, u32[]{:S(2)}, u32[]{:S(2)}) collective-permute-start(f32[2,64,128]{2,1,0:T(8,128)S(1)} %get-tuple-element.51), channel_id=1, source_target_pairs={{0,4},{1,5},{4,0},{5,1},{8,12},{9,13},{12,8},{13,9},{2,6},{3,7},{6... | collective-permute-start | bytes 196616 | tf_op jit(solution)/shard_map/ppermute | solution.py:252
  71.5 5.4 %collective-permute-start.16 = (f32[2,64,128]{2,1,0:T(8,128)S(1)}, f32[2,64,128]{2,1,0:T(8,128)S(1)}, u32[]{:S(2)}, u32[]{:S(2)}) collective-permute-start(f32[2,64,128]{2,1,0:T(8,128)S(1)} %add_add_fusion), channel_id=1, source_target_pairs={{0,8},{4,12},{8,0},{12,4},{1,9},{5,13},{9,1},{13,5},{2,10},{6,14},... | collective-permute-start | bytes 196616 | tf_op jit(solution)/shard_map/ppermute | solution.py:252
  76.9 5.8 %collective-permute-start.19 = (f32[2,64,128]{2,1,0:T(8,128)S(1)}, f32[2,64,128]{2,1,0:T(8,128)S(1)}, u32[]{:S(2)}, u32[]{:S(2)}) collective-permute-start(f32[2,64,128]{2,1,0:T(8,128)S(1)} %add.225), channel_id=1, source_target_pairs={{0,5},{1,4},{4,1},{5,0},{8,13},{9,12},{12,9},{13,8},{2,7},{3,6},{6... | collective-permute-start | bytes 196616 | tf_op jit(solution)/shard_map/ppermute | solution.py:252
  77.6 5.1 %collective-permute-start.18 = (f32[2,64,128]{2,1,0:T(8,128)S(1)}, f32[2,64,128]{2,1,0:T(8,128)S(1)}, u32[]{:S(2)}, u32[]{:S(2)}) collective-permute-start(f32[2,64,128]{2,1,0:T(8,128)S(1)} %add.225), channel_id=1, source_target_pairs={{0,1},{1,0},{4,5},{5,4},{8,9},{9,8},{12,13},{13,12},{2,3},{3,2},{6... | collective-permute-start | bytes 196616 | tf_op jit(solution)/shard_map/ppermute | solution.py:252
  78.3 4.4 %collective-permute-start.17 = (f32[2,64,128]{2,1,0:T(8,128)S(1)}, f32[2,64,128]{2,1,0:T(8,128)S(1)}, u32[]{:S(2)}, u32[]{:S(2)}) collective-permute-start(f32[2,64,128]{2,1,0:T(8,128)S(1)} %add.225), channel_id=1, source_target_pairs={{0,4},{1,5},{4,0},{5,1},{8,12},{9,13},{12,8},{13,9},{2,6},{3,7},{6... | collective-permute-start | bytes 196616 | tf_op jit(solution)/shard_map/ppermute | solution.py:252
  90.9 4.9 %collective-permute-start.21 = (bf16[2,64,128]{2,1,0:T(8,128)(2,1)S(1)}, bf16[2,64,128]{2,1,0:T(8,128)(2,1)S(1)}, u32[]{:S(2)}, u32[]{:S(2)}) collective-permute-start(bf16[2,64,128]{2,1,0:T(8,128)(2,1)S(1)} %get-tuple-element.58), channel_id=1, source_target_pairs={{0,5},{1,4},{4,1},{5,0},{8,13},{9,12},{12,9},{13,8},{2,7},{3,6},{6... | collective-permute-start | bytes 98312 | tf_op jit(solution)/shard_map/ppermute | solution.py:252
  93.5 3.9 %collective-permute-start.23 = (bf16[2,64,128]{2,1,0:T(8,128)(2,1)S(1)}, bf16[2,64,128]{2,1,0:T(8,128)(2,1)S(1)}, u32[]{:S(2)}, u32[]{:S(2)}) collective-permute-start(bf16[2,64,128]{2,1,0:T(8,128)(2,1)S(1)} %get-tuple-element.59), channel_id=1, source_target_pairs={{0,1},{1,0},{4,5},{5,4},{8,9},{9,8},{12,13},{13,12},{2,3},{3,2},{6... | collective-permute-start | bytes 98312 | tf_op jit(solution)/shard_map/ppermute | solution.py:252
  94.5 3.9 %collective-permute-start.22 = (bf16[2,64,128]{2,1,0:T(8,128)(2,1)S(1)}, bf16[2,64,128]{2,1,0:T(8,128)(2,1)S(1)}, u32[]{:S(2)}, u32[]{:S(2)}) collective-permute-start(bf16[2,64,128]{2,1,0:T(8,128)(2,1)S(1)} %get-tuple-element.60), channel_id=1, source_target_pairs={{0,4},{1,5},{4,0},{5,1},{8,12},{9,13},{12,8},{13,9},{2,6},{3,7},{6... | collective-permute-start | bytes 98312 | tf_op jit(solution)/shard_map/ppermute | solution.py:252
  98.4 4.9 %collective-permute-start.24 = (bf16[2,64,128]{2,1,0:T(8,128)(2,1)S(1)}, bf16[2,64,128]{2,1,0:T(8,128)(2,1)S(1)}, u32[]{:S(2)}, u32[]{:S(2)}) collective-permute-start(bf16[2,64,128]{2,1,0:T(8,128)(2,1)S(1)} %fusion.21), channel_id=1, source_target_pairs={{0,8},{4,12},{8,0},{12,4},{1,9},{5,13},{9,1},{13,5},{2,10},{6,14},... | collective-permute-start | bytes 98312 | tf_op jit(solution)/shard_map/ppermute | solution.py:252
  103.3 5.0 %collective-permute-start.27 = (bf16[2,64,128]{2,1,0:T(8,128)(2,1)S(1)}, bf16[2,64,128]{2,1,0:T(8,128)(2,1)S(1)}, u32[]{:S(2)}, u32[]{:S(2)}) collective-permute-start(bf16[2,64,128]{2,1,0:T(8,128)(2,1)S(1)} %add_convert_fusion.2), channel_id=1, source_target_pairs={{0,5},{1,4},{4,1},{5,0},{8,13},{9,12},{12,9},{13,8},{2,7},{3,6},{6... | collective-permute-start | bytes 98312 | tf_op jit(solution)/shard_map/ppermute | solution.py:252
  104.0 4.3 %collective-permute-start.26 = (bf16[2,64,128]{2,1,0:T(8,128)(2,1)S(1)}, bf16[2,64,128]{2,1,0:T(8,128)(2,1)S(1)}, u32[]{:S(2)}, u32[]{:S(2)}) collective-permute-start(bf16[2,64,128]{2,1,0:T(8,128)(2,1)S(1)} %add_convert_fusion.2), channel_id=1, source_target_pairs={{0,1},{1,0},{4,5},{5,4},{8,9},{9,8},{12,13},{13,12},{2,3},{3,2},{6... | collective-permute-start | bytes 98312 | tf_op jit(solution)/shard_map/ppermute | solution.py:252
  104.9 3.9 %collective-permute-start.25 = (bf16[2,64,128]{2,1,0:T(8,128)(2,1)S(1)}, bf16[2,64,128]{2,1,0:T(8,128)(2,1)S(1)}, u32[]{:S(2)}, u32[]{:S(2)}) collective-permute-start(bf16[2,64,128]{2,1,0:T(8,128)(2,1)S(1)} %add_convert_fusion.2), channel_id=1, source_target_pairs={{0,4},{1,5},{4,0},{5,1},{8,12},{9,13},{12,8},{13,9},{2,6},{3,7},{6... | collective-permute-start | bytes 98312 | tf_op jit(solution)/shard_map/ppermute | solution.py:252
  115.9 4.9 %collective-permute-start.29 = (bf16[2,64,128]{2,1,0:T(8,128)(2,1)S(1)}, bf16[2,64,128]{2,1,0:T(8,128)(2,1)S(1)}, u32[]{:S(2)}, u32[]{:S(2)}) collective-permute-start(bf16[2,64,128]{2,1,0:T(8,128)(2,1)S(1)} %get-tuple-element.55), channel_id=1, source_target_pairs={{0,5},{1,4},{4,1},{5,0},{8,13},{9,12},{12,9},{13,8},{2,7},{3,6},{6... | collective-permute-start | bytes 98312 | tf_op jit(solution)/shard_map/ppermute | solution.py:252
  123.4 4.9 %collective-permute-start.32 = (bf16[2,64,128]{2,1,0:T(8,128)(2,1)S(1)}, bf16[2,64,128]{2,1,0:T(8,128)(2,1)S(1)}, u32[]{:S(2)}, u32[]{:S(2)}) collective-permute-start(bf16[2,64,128]{2,1,0:T(8,128)(2,1)S(1)} %fusion.18), channel_id=1, source_target_pairs={{0,8},{4,12},{8,0},{12,4},{1,9},{5,13},{9,1},{13,5},{2,10},{6,14},... | collective-permute-start | bytes 98312 | tf_op jit(solution)/shard_map/ppermute | solution.py:252
  128.3 5.0 %collective-permute-start.35 = (bf16[2,64,128]{2,1,0:T(8,128)(2,1)S(1)}, bf16[2,64,128]{2,1,0:T(8,128)(2,1)S(1)}, u32[]{:S(2)}, u32[]{:S(2)}) collective-permute-start(bf16[2,64,128]{2,1,0:T(8,128)(2,1)S(1)} %add_convert_fusion.1), channel_id=1, source_target_pairs={{0,5},{1,4},{4,1},{5,0},{8,13},{9,12},{12,9},{13,8},{2,7},{3,6},{6... | collective-permute-start | bytes 98312 | tf_op jit(solution)/shard_map/ppermute | solution.py:252
  129.0 4.3 %collective-permute-start.34 = (bf16[2,64,128]{2,1,0:T(8,128)(2,1)S(1)}, bf16[2,64,128]{2,1,0:T(8,128)(2,1)S(1)}, u32[]{:S(2)}, u32[]{:S(2)}) collective-permute-start(bf16[2,64,128]{2,1,0:T(8,128)(2,1)S(1)} %add_convert_fusion.1), channel_id=1, source_target_pairs={{0,1},{1,0},{4,5},{5,4},{8,9},{9,8},{12,13},{13,12},{2,3},{3,2},{6... | collective-permute-start | bytes 98312 | tf_op jit(solution)/shard_map/ppermute | solution.py:252
  140.9 4.9 %collective-permute-start.37 = (bf16[2,64,128]{2,1,0:T(8,128)(2,1)S(1)}, bf16[2,64,128]{2,1,0:T(8,128)(2,1)S(1)}, u32[]{:S(2)}, u32[]{:S(2)}) collective-permute-start(bf16[2,64,128]{2,1,0:T(8,128)(2,1)S(1)} %get-tuple-element.52), channel_id=1, source_target_pairs={{0,5},{1,4},{4,1},{5,0},{8,13},{9,12},{12,9},{13,8},{2,7},{3,6},{6... | collective-permute-start | bytes 98312 | tf_op jit(solution)/shard_map/ppermute | solution.py:252
  148.4 4.9 %collective-permute-start.40 = (bf16[2,64,128]{2,1,0:T(8,128)(2,1)S(1)}, bf16[2,64,128]{2,1,0:T(8,128)(2,1)S(1)}, u32[]{:S(2)}, u32[]{:S(2)}) collective-permute-start(bf16[2,64,128]{2,1,0:T(8,128)(2,1)S(1)} %fusion.15), channel_id=1, source_target_pairs={{0,8},{4,12},{8,0},{12,4},{1,9},{5,13},{9,1},{13,5},{2,10},{6,14},... | collective-permute-start | bytes 98312 | tf_op jit(solution)/shard_map/ppermute | solution.py:252
  153.3 5.0 %collective-permute-start.43 = (bf16[2,64,128]{2,1,0:T(8,128)(2,1)S(1)}, bf16[2,64,128]{2,1,0:T(8,128)(2,1)S(1)}, u32[]{:S(2)}, u32[]{:S(2)}) collective-permute-start(bf16[2,64,128]{2,1,0:T(8,128)(2,1)S(1)} %add_convert_fusion), channel_id=1, source_target_pairs={{0,5},{1,4},{4,1},{5,0},{8,13},{9,12},{12,9},{13,8},{2,7},{3,6},{6... | collective-permute-start | bytes 98312 | tf_op jit(solution)/shard_map/ppermute | solution.py:252
  154.0 4.3 %collective-permute-start.42 = (bf16[2,64,128]{2,1,0:T(8,128)(2,1)S(1)}, bf16[2,64,128]{2,1,0:T(8,128)(2,1)S(1)}, u32[]{:S(2)}, u32[]{:S(2)}) collective-permute-start(bf16[2,64,128]{2,1,0:T(8,128)(2,1)S(1)} %add_convert_fusion), channel_id=1, source_target_pairs={{0,1},{1,0},{4,5},{5,4},{8,9},{9,8},{12,13},{13,12},{2,3},{3,2},{6... | collective-permute-start | bytes 98312 | tf_op jit(solution)/shard_map/ppermute | solution.py:252
  (15 other events, 112.2 us)

commit v22 on v19

--- a/solution.py
+++ b/solution.py
@@ -81,7 +81,7 @@
 
 
 def eliminate(matrix, beside=()):
-    beside = list(beside)
+    share = len(beside) / (matrix.shape[0] // SUB)
     size = matrix.shape[0]
     blocks = size // SUB
     row_index = lax.broadcasted_iota(jnp.int32, (SUB, 2 * size), 0)
@@ -97,8 +97,8 @@
 
     rows = []
     for b in range(blocks):
-        for unused in range(-(-len(beside) // (blocks - b))):
-            beside.pop(0)()
+        for extra in beside[math.ceil(b * share) : math.ceil((b + 1) * share)]:
+            extra()
         columns = [
             {
                 i: jnp.broadcast_to(work[i][:, SUB * b + j : SUB * b + j + 1], (SUB, 2 * size))

time: 169 us -> 169 us (level)
  no operation moved by 1% of the time
where the time goes in v22:
time: 169 us; the launch traced here: 168 us
  waiting for transfers between devices  78.6 us (47%)
  starting transfers between devices  45.9 us (27%)
  Pallas kernels  32.5 us (19%)
  local copies, waits for them, and re-layouts  5.55 us (3%)
  matrix products  3.83 us (2%)
    ppermute x45, waiting for transfers between devices, from_xor(): return lax.ppermute(value, axis, [(i, i ^ offset) for i in range(size)])  78.6 us
    ppermute x45, starting transfers between devices, from_xor(): return lax.ppermute(value, axis, [(i, i ^ offset) for i in range(size)])  45.9 us
    pallas_call x7, Pallas kernels, call(): pl.pallas_call(kernel, out_shape=out_shapes, in_specs=[pl.BlockSpec(memor...  32.5 us
    dot_general x1, matrix products, per_device_transposed(): lax.dot_general(omega, states, (((0,), (1,)), ((), ())), preferred_elemen...  3.83 us
  transfers between devices with their start and end apart: 45, of which 33 were waited for; matrix products, arithmetic and copies ran while one was open for 3% of the time, Pallas kernels for 4%

profile of v22, /device:TPU:0, one launch (start us, length us, event | category | flops | bytes accessed | tf_op | source)
XLA Modules:
  0.0 168.4 jit_solution(5394577054686669809)
XLA Ops:
  2.1 3.1 %collective-permute-start.3 = (bf16[256,1024]{1,0:T(8,128)(2,1)S(1)}, bf16[256,1024]{1,0:T(8,128)(2,1)S(1)}, u32[]{:S(2)}, u32[]{:S(2)}) collective-permute-start(bf16[256,1024]{1,0:T(8,128)(2,1)S(1)} %get-tuple-element.44), channel_id=1, source_target_pairs={{0,4},{4,0},{8,12},{12,8},{1,5},{5,1},{9,13},{13,9},{2,6},{6,2},{1... | collective-permute-start | bytes 1572872 | tf_op jit(solution)/shard_map/ppermute | solution.py:242
  5.2 2.6 %collective-permute-start.2 = (bf16[256,1024]{1,0:T(8,128)(2,1)S(1)}, bf16[256,1024]{1,0:T(8,128)(2,1)S(1)}, u32[]{:S(2)}, u32[]{:S(2)}) collective-permute-start(bf16[256,1024]{1,0:T(8,128)(2,1)S(1)} %get-tuple-element.46), channel_id=1, source_target_pairs={{0,8},{4,12},{8,0},{12,4},{1,9},{5,13},{9,1},{13,5},{2,10},{6,14},... | collective-permute-start | bytes 1572872 | tf_op jit(solution)/shard_map/ppermute | solution.py:242
  8.5 3.8 %convolution_bitcast_fusion = f32[8,2,8,128]{3,2,1,0:T(8,128)S(1)} fusion(bf16[256,4096]{1,0:T(8,128)(2,1)} %param.3, s32[]{:T(128)S(6)} %xor.73, s32[4096]{0:T(1024)S(1)} %add_multiply_fusion), kind=kOutput, calls=%fused_computation | convolution fusion | flops 152043520 | bytes 2179076 | tf_op jit(solution)/shard_map/dot_general | solution.py:317
  13.8 19.8 %collective-permute-done = f32[2,64,128]{2,1,0:T(8,128)S(1)} collective-permute-done((f32[2,64,128]{2,1,0:T(8,128)S(1)}, f32[2,64,128]{2,1,0:T(8,128)S(1)}, u32[]{:S(2)}, u32[]{:S(2)}) %collective-permute-start) | collective-permute-done | bytes 65568 | tf_op jit(solution)/shard_map/ppermute | solution.py:242
  33.6 1.6 collective-permute-start.1
  35.2 3.0 %collective-permute-start.5 = (bf16[128,1024]{1,0:T(8,128)(2,1)S(1)}, bf16[128,1024]{1,0:T(8,128)(2,1)S(1)}, u32[]{:S(2)}, u32[]{:S(2)}) collective-permute-start(bf16[128,1024]{1,0:T(8,128)(2,1)S(1)} %get-tuple-element.22), channel_id=1, source_target_pairs={{0,12},{4,8},{8,4},{12,0},{1,13},{5,9},{9,5},{13,1},{2,14},{6,10},... | collective-permute-start | bytes 786440 | tf_op jit(solution)/shard_map/ppermute | solution.py:242
  38.8 7.7 %collective-permute-done.4 = f32[4,64,128]{2,1,0:T(8,128)S(1)} collective-permute-done((f32[4,64,128]{2,1,0:T(8,128)S(1)}, f32[4,64,128]{2,1,0:T(8,128)S(1)}, u32[]{:S(2)}, u32[]{:S(2)}) %collective-permute-start.4) | collective-permute-done | bytes 131104 | tf_op jit(solution)/shard_map/ppermute | solution.py:242
  46.6 2.5 %collective-permute-start.7 = (bf16[128,1024]{1,0:T(8,128)(2,1)S(1)}, bf16[128,1024]{1,0:T(8,128)(2,1)S(1)}, u32[]{:S(2)}, u32[]{:S(2)}) collective-permute-start(bf16[128,1024]{1,0:T(8,128)(2,1)S(1)} %get-tuple-element.26), channel_id=1, source_target_pairs={{0,12},{4,8},{8,4},{12,0},{1,13},{5,9},{9,5},{13,1},{2,14},{6,10},... | collective-permute-start | bytes 786440 | tf_op jit(solution)/shard_map/ppermute | solution.py:242
  49.9 5.9 %shard_map.41 = (bf16[64,2048]{1,0:T(8,128)(2,1)S(1)}, f32[64,64]{1,0:T(8,128)S(1)}) custom-call(s32[8]{0:T(128)S(1)} %fusion.24.at_ref, f32[8,64,128]{2,1,0:T(8,128)S(1)} %pad_maximum_fusion.z_ref, f32[8,64,128]{2,1,0:T(8,128)S(1)} %collective-permute-done.6.other_ref), custom_call_target="tpu_custom_call" | custom-call | flops 402653184 | bytes 524288 | tf_op jit(solution)/shard_map/pallas_call | solution.py:225
  59.2 2.1 %shard_map.42 = (bf16[2048,1024]{1,0:T(8,128)(2,1)S(1)}, f32[8,64,128]{2,1,0:T(8,128)S(1)}) custom-call(s32[8]{0:T(128)S(1)} %fusion.22.at_ref, bf16[64,2048]{1,0:T(8,128)(2,1)S(1)} %get-tuple-element.27.basis_ref, bf16[256,1024]{1,0:T(8,128)(2,1)S(1)} %get-tuple-element.28.refs_0_, bf16[256,1024]{1,0:T(8,128)(2,1)S(1)} %collective-permute-done.3.refs_1_, ...), custom_call_target="tpu_custom_call" | custom-call | flops 939524096 | bytes 4456448 | tf_op jit(solution)/shard_map/pallas_call | solution.py:225
  61.3 4.4 %collective-permute-start.13 = (f32[2,64,128]{2,1,0:T(8,128)S(1)}, f32[2,64,128]{2,1,0:T(8,128)S(1)}, u32[]{:S(2)}, u32[]{:S(2)}) collective-permute-start(f32[2,64,128]{2,1,0:T(8,128)S(1)} %get-tuple-element.49), channel_id=1, source_target_pairs={{0,5},{1,4},{4,1},{5,0},{8,13},{9,12},{12,9},{13,8},{2,7},{3,6},{6... | collective-permute-start | bytes 196616 | tf_op jit(solution)/shard_map/ppermute | solution.py:242
  68.1 1.9 %collective-permute-done.15 = f32[2,64,128]{2,1,0:T(8,128)S(1)} collective-permute-done((f32[2,64,128]{2,1,0:T(8,128)S(1)}, f32[2,64,128]{2,1,0:T(8,128)S(1)}, u32[]{:S(2)}, u32[]{:S(2)}) %collective-permute-start.15) | collective-permute-done | bytes 65568 | tf_op jit(solution)/shard_map/ppermute | solution.py:242
  72.2 4.7 %collective-permute-done.16 = f32[2,64,128]{2,1,0:T(8,128)S(1)} collective-permute-done((f32[2,64,128]{2,1,0:T(8,128)S(1)}, f32[2,64,128]{2,1,0:T(8,128)S(1)}, u32[]{:S(2)}, u32[]{:S(2)}) %collective-permute-start.16) | collective-permute-done | bytes 65568 | tf_op jit(solution)/shard_map/ppermute | solution.py:242
  78.3 2.2 %collective-permute-start.17 = (f32[2,64,128]{2,1,0:T(8,128)S(1)}, f32[2,64,128]{2,1,0:T(8,128)S(1)}, u32[]{:S(2)}, u32[]{:S(2)}) collective-permute-start(f32[2,64,128]{2,1,0:T(8,128)S(1)} %add.225), channel_id=1, source_target_pairs={{0,4},{1,5},{4,0},{5,1},{8,12},{9,13},{12,8},{13,9},{2,6},{3,7},{6... | collective-permute-start | bytes 196616 | tf_op jit(solution)/shard_map/ppermute | solution.py:242
  80.5 2.2 %collective-permute-done.17 = f32[2,64,128]{2,1,0:T(8,128)S(1)} collective-permute-done((f32[2,64,128]{2,1,0:T(8,128)S(1)}, f32[2,64,128]{2,1,0:T(8,128)S(1)}, u32[]{:S(2)}, u32[]{:S(2)}) %collective-permute-start.17) | collective-permute-done | bytes 65568 | tf_op jit(solution)/shard_map/ppermute | solution.py:242
  84.4 6.4 %shard_map.44 = f32[8,64,128]{2,1,0:T(8,128)S(1)} custom-call(s32[8]{0:T(128)S(1)} %fusion.22.at_ref, f32[8,64,128]{2,1,0:T(8,128)S(1)} %constant_dynamic-update-slice_fusion.z_ref, f32[8,64,128]{2,1,0:T(8,128)S(1)} %collective-permute-done.20.other_ref, bf16[2048,1024]{1,0:T(8,128)(2,1)S(1)} %get-tuple-element.34.a_ref, ...), custom_call_target="tpu_custom_call" | custom-call | flops 939524096 | bytes 6815744 | tf_op jit(solution)/shard_map/pallas_call | solution.py:225
  90.8 2.6 %collective-permute-start.21 = (bf16[2,64,128]{2,1,0:T(8,128)(2,1)S(1)}, bf16[2,64,128]{2,1,0:T(8,128)(2,1)S(1)}, u32[]{:S(2)}, u32[]{:S(2)}) collective-permute-start(bf16[2,64,128]{2,1,0:T(8,128)(2,1)S(1)} %get-tuple-element.58), channel_id=1, source_target_pairs={{0,5},{1,4},{4,1},{5,0},{8,13},{9,12},{12,9},{13,8},{2,7},{3,6},{6... | collective-permute-start | bytes 98312 | tf_op jit(solution)/shard_map/ppermute | solution.py:242
  95.7 1.6 collective-permute-done.23
  98.4 4.8 %collective-permute-done.24 = bf16[2,64,128]{2,1,0:T(8,128)(2,1)S(1)} collective-permute-done((bf16[2,64,128]{2,1,0:T(8,128)(2,1)S(1)}, bf16[2,64,128]{2,1,0:T(8,128)(2,1)S(1)}, u32[]{:S(2)}, u32[]{:S(2)}) %collective-permute-start.24) | collective-permute-done | bytes 32800 | tf_op jit(solution)/shard_map/ppermute | solution.py:242
  104.7 2.0 %collective-permute-start.25 = (bf16[2,64,128]{2,1,0:T(8,128)(2,1)S(1)}, bf16[2,64,128]{2,1,0:T(8,128)(2,1)S(1)}, u32[]{:S(2)}, u32[]{:S(2)}) collective-permute-start(bf16[2,64,128]{2,1,0:T(8,128)(2,1)S(1)} %add_convert_fusion.2), channel_id=1, source_target_pairs={{0,4},{1,5},{4,0},{5,1},{8,12},{9,13},{12,8},{13,9},{2,6},{3,7},{6... | collective-permute-start | bytes 98312 | tf_op jit(solution)/shard_map/ppermute | solution.py:242
  110.1 5.8 %shard_map.45 = f32[8,64,128]{2,1,0:T(8,128)S(1)} custom-call(s32[8]{0:T(128)S(1)} %fusion.22.at_ref, bf16[8,64,128]{2,1,0:T(8,128)(2,1)S(1)} %pad_maximum_fusion.2.z_ref, bf16[8,64,128]{2,1,0:T(8,128)(2,1)S(1)} %collective-permute-done.28.other_ref, bf16[2048,1024]{1,0:T(8,128)(2,1)S(1)} %get-tuple-element.34.a_ref, bf16[1024,1024]{1,0:T(8,128)(2,1)S(1)} %shard_map.43.turned_ref), custom_call_target="tpu_custom_call" | custom-call | flops 939524096 | bytes 6553600 | tf_op jit(solution)/shard_map/pallas_call | solution.py:225
  115.9 2.6 %collective-permute-start.29 = (bf16[2,64,128]{2,1,0:T(8,128)(2,1)S(1)}, bf16[2,64,128]{2,1,0:T(8,128)(2,1)S(1)}, u32[]{:S(2)}, u32[]{:S(2)}) collective-permute-start(bf16[2,64,128]{2,1,0:T(8,128)(2,1)S(1)} %get-tuple-element.55), channel_id=1, source_target_pairs={{0,5},{1,4},{4,1},{5,0},{8,13},{9,12},{12,9},{13,8},{2,7},{3,6},{6... | collective-permute-start | bytes 98312 | tf_op jit(solution)/shard_map/ppermute | solution.py:242
  120.8 1.6 collective-permute-done.31
  123.4 4.8 %collective-permute-done.32 = bf16[2,64,128]{2,1,0:T(8,128)(2,1)S(1)} collective-permute-done((bf16[2,64,128]{2,1,0:T(8,128)(2,1)S(1)}, bf16[2,64,128]{2,1,0:T(8,128)(2,1)S(1)}, u32[]{:S(2)}, u32[]{:S(2)}) %collective-permute-start.32) | collective-permute-done | bytes 32800 | tf_op jit(solution)/shard_map/ppermute | solution.py:242
  129.8 2.0 %collective-permute-start.33 = (bf16[2,64,128]{2,1,0:T(8,128)(2,1)S(1)}, bf16[2,64,128]{2,1,0:T(8,128)(2,1)S(1)}, u32[]{:S(2)}, u32[]{:S(2)}) collective-permute-start(bf16[2,64,128]{2,1,0:T(8,128)(2,1)S(1)} %add_convert_fusion.1), channel_id=1, source_target_pairs={{0,4},{1,5},{4,0},{5,1},{8,12},{9,13},{12,8},{13,9},{2,6},{3,7},{6... | collective-permute-start | bytes 98312 | tf_op jit(solution)/shard_map/ppermute | solution.py:242
  135.2 5.8 %shard_map.46 = f32[8,64,128]{2,1,0:T(8,128)S(1)} custom-call(s32[8]{0:T(128)S(1)} %fusion.22.at_ref, bf16[8,64,128]{2,1,0:T(8,128)(2,1)S(1)} %pad_maximum_fusion.3.z_ref, bf16[8,64,128]{2,1,0:T(8,128)(2,1)S(1)} %collective-permute-done.36.other_ref, bf16[2048,1024]{1,0:T(8,128)(2,1)S(1)} %get-tuple-element.34.a_ref, bf16[1024,1024]{1,0:T(8,128)(2,1)S(1)} %shard_map.43.turned_ref), custom_call_target="tpu_custom_call" | custom-call | flops 939524096 | bytes 6553600 | tf_op jit(solution)/shard_map/pallas_call | solution.py:225
  141.0 2.6 %collective-permute-start.37 = (bf16[2,64,128]{2,1,0:T(8,128)(2,1)S(1)}, bf16[2,64,128]{2,1,0:T(8,128)(2,1)S(1)}, u32[]{:S(2)}, u32[]{:S(2)}) collective-permute-start(bf16[2,64,128]{2,1,0:T(8,128)(2,1)S(1)} %get-tuple-element.52), channel_id=1, source_target_pairs={{0,5},{1,4},{4,1},{5,0},{8,13},{9,12},{12,9},{13,8},{2,7},{3,6},{6... | collective-permute-start | bytes 98312 | tf_op jit(solution)/shard_map/ppermute | solution.py:242
  145.8 1.6 collective-permute-done.39
  148.5 4.8 %collective-permute-done.40 = bf16[2,64,128]{2,1,0:T(8,128)(2,1)S(1)} collective-permute-done((bf16[2,64,128]{2,1,0:T(8,128)(2,1)S(1)}, bf16[2,64,128]{2,1,0:T(8,128)(2,1)S(1)}, u32[]{:S(2)}, u32[]{:S(2)}) %collective-permute-start.40) | collective-permute-done | bytes 32800 | tf_op jit(solution)/shard_map/ppermute | solution.py:242
  154.9 2.0 %collective-permute-start.41 = (bf16[2,64,128]{2,1,0:T(8,128)(2,1)S(1)}, bf16[2,64,128]{2,1,0:T(8,128)(2,1)S(1)}, u32[]{:S(2)}, u32[]{:S(2)}) collective-permute-start(bf16[2,64,128]{2,1,0:T(8,128)(2,1)S(1)} %add_convert_fusion), channel_id=1, source_target_pairs={{0,4},{1,5},{4,0},{5,1},{8,12},{9,13},{12,8},{13,9},{2,6},{3,7},{6... | collective-permute-start | bytes 98312 | tf_op jit(solution)/shard_map/ppermute | solution.py:242
  160.2 2.2 %copy-done.1 = bf16[2048,1024]{1,0:T(8,128)(2,1)S(1)} copy-done((bf16[2048,1024]{1,0:T(8,128)(2,1)S(1)}, bf16[2048,1024]{1,0:T(8,128)(2,1)}, u32[]{:S(2)}) %copy-start.1) | copy-done | bytes 4194328
  162.4 6.0 %shard_map.47 = f32[64,512]{1,0:T(8,128)} custom-call(s32[8]{0:T(128)S(1)} %fusion.22.at_ref, s32[1]{0:T(128)} %bitcast.core_ref, bf16[8,64,128]{2,1,0:T(8,128)(2,1)S(1)} %pad_maximum_fusion.4.z_ref, bf16[8,64,128]{2,1,0:T(8,128)(2,1)S(1)} %collective-permute-done.44.other_ref, bf16[2048,1024]{1,0:T(8,128)(2,1)S(1)} %copy-done.1), custom_call_target="tpu_custom_call" | custom-call | flops 939524096 | bytes 4456448 | tf_op jit(solution)/shard_map/pallas_call | solution.py:225
  (103 shorter events, 40.2 us)
Async XLA Ops:
  2.1 36.5 %collective-permute-start.3 = (bf16[256,1024]{1,0:T(8,128)(2,1)S(1)}, bf16[256,1024]{1,0:T(8,128)(2,1)S(1)}, u32[]{:S(2)}, u32[]{:S(2)}) collective-permute-start(bf16[256,1024]{1,0:T(8,128)(2,1)S(1)} %get-tuple-element.44), channel_id=1, source_target_pairs={{0,4},{4,0},{8,12},{12,8},{1,5},{5,1},{9,13},{13,9},{2,6},{6,2},{1... | collective-permute-start | bytes 1572872 | tf_op jit(solution)/shard_map/ppermute | solution.py:242
  5.2 33.5 %collective-permute-start.2 = (bf16[256,1024]{1,0:T(8,128)(2,1)S(1)}, bf16[256,1024]{1,0:T(8,128)(2,1)S(1)}, u32[]{:S(2)}, u32[]{:S(2)}) collective-permute-start(bf16[256,1024]{1,0:T(8,128)(2,1)S(1)} %get-tuple-element.46), channel_id=1, source_target_pairs={{0,8},{4,12},{8,0},{12,4},{1,9},{5,13},{9,1},{13,5},{2,10},{6,14},... | collective-permute-start | bytes 1572872 | tf_op jit(solution)/shard_map/ppermute | solution.py:242
  12.4 21.2 %collective-permute-start = (f32[2,64,128]{2,1,0:T(8,128)S(1)}, f32[2,64,128]{2,1,0:T(8,128)S(1)}, u32[]{:S(2)}, u32[]{:S(2)}) collective-permute-start(f32[2,64,128]{2,1,0:T(8,128)S(1)} %bitcast.16), channel_id=1, source_target_pairs={{0,8},{4,12},{8,0},{12,4},{1,9},{5,13},{9,1},{13,5},{2,10},{6,14},... | collective-permute-start | bytes 196616 | tf_op jit(solution)/shard_map/ppermute | solution.py:242
  33.6 5.0 %collective-permute-start.1 = (f32[4,64,128]{2,1,0:T(8,128)S(1)}, f32[4,64,128]{2,1,0:T(8,128)S(1)}, u32[]{:S(2)}, u32[]{:S(2)}) collective-permute-start(f32[4,64,128]{2,1,0:T(8,128)S(1)} %pad_maximum_fusion.1), channel_id=1, source_target_pairs={{0,1},{1,0},{2,3},{3,2},{4,5},{5,4},{6,7},{7,6},{8,9},{9,8},{10,11... | collective-permute-start | bytes 393224 | tf_op jit(solution)/shard_map/ppermute | solution.py:242
  35.2 11.4 %collective-permute-start.5 = (bf16[128,1024]{1,0:T(8,128)(2,1)S(1)}, bf16[128,1024]{1,0:T(8,128)(2,1)S(1)}, u32[]{:S(2)}, u32[]{:S(2)}) collective-permute-start(bf16[128,1024]{1,0:T(8,128)(2,1)S(1)} %get-tuple-element.22), channel_id=1, source_target_pairs={{0,12},{4,8},{8,4},{12,0},{1,13},{5,9},{9,5},{13,1},{2,14},{6,10},... | collective-permute-start | bytes 786440 | tf_op jit(solution)/shard_map/ppermute | solution.py:242
  38.7 7.8 %collective-permute-start.4 = (f32[4,64,128]{2,1,0:T(8,128)S(1)}, f32[4,64,128]{2,1,0:T(8,128)S(1)}, u32[]{:S(2)}, u32[]{:S(2)}) collective-permute-start(f32[4,64,128]{2,1,0:T(8,128)S(1)} %add.218), channel_id=1, source_target_pairs={{0,4},{4,0},{8,12},{12,8},{1,5},{5,1},{9,13},{13,9},{2,6},{6,2},{1... | collective-permute-start | bytes 393224 | tf_op jit(solution)/shard_map/ppermute | solution.py:242
  46.6 10.6 %collective-permute-start.7 = (bf16[128,1024]{1,0:T(8,128)(2,1)S(1)}, bf16[128,1024]{1,0:T(8,128)(2,1)S(1)}, u32[]{:S(2)}, u32[]{:S(2)}) collective-permute-start(bf16[128,1024]{1,0:T(8,128)(2,1)S(1)} %get-tuple-element.26), channel_id=1, source_target_pairs={{0,12},{4,8},{8,4},{12,0},{1,13},{5,9},{9,5},{13,1},{2,14},{6,10},... | collective-permute-start | bytes 786440 | tf_op jit(solution)/shard_map/ppermute | solution.py:242
  49.2 8.6 %collective-permute-start.8 = (bf16[256,1024]{1,0:T(8,128)(2,1)S(1)}, bf16[256,1024]{1,0:T(8,128)(2,1)S(1)}, u32[]{:S(2)}, u32[]{:S(2)}) collective-permute-start(bf16[256,1024]{1,0:T(8,128)(2,1)S(1)} %get-tuple-element.28.refs_0_), channel_id=1, source_target_pairs={{0,2},{2,0},{1,3},{3,1},{4,6},{6,4},{5,7},{7,5},{8,10},{10,8},{9,1... | collective-permute-start | bytes 1572872 | tf_op jit(solution)/shard_map/ppermute | solution.py:242
  49.3 8.5 %collective-permute-start.9 = (bf16[256,1024]{1,0:T(8,128)(2,1)S(1)}, bf16[256,1024]{1,0:T(8,128)(2,1)S(1)}, u32[]{:S(2)}, u32[]{:S(2)}) collective-permute-start(bf16[256,1024]{1,0:T(8,128)(2,1)S(1)} %collective-permute-done.3.refs_1_), channel_id=1, source_target_pairs={{0,2},{2,0},{1,3},{3,1},{4,6},{6,4},{5,7},{7,5},{8,10},{10,8},{9,1... | collective-permute-start | bytes 1572872 | tf_op jit(solution)/shard_map/ppermute | solution.py:242
  49.7 8.1 %collective-permute-start.10 = (bf16[256,1024]{1,0:T(8,128)(2,1)S(1)}, bf16[256,1024]{1,0:T(8,128)(2,1)S(1)}, u32[]{:S(2)}, u32[]{:S(2)}) collective-permute-start(bf16[256,1024]{1,0:T(8,128)(2,1)S(1)} %collective-permute-done.2.refs_2_), channel_id=1, source_target_pairs={{0,2},{2,0},{1,3},{3,1},{4,6},{6,4},{5,7},{7,5},{8,10},{10,8},{9,1... | collective-permute-start | bytes 1572872 | tf_op jit(solution)/shard_map/ppermute | solution.py:242
  61.3 6.8 %collective-permute-start.13 = (f32[2,64,128]{2,1,0:T(8,128)S(1)}, f32[2,64,128]{2,1,0:T(8,128)S(1)}, u32[]{:S(2)}, u32[]{:S(2)}) collective-permute-start(f32[2,64,128]{2,1,0:T(8,128)S(1)} %get-tuple-element.49), channel_id=1, source_target_pairs={{0,5},{1,4},{4,1},{5,0},{8,13},{9,12},{12,9},{13,8},{2,7},{3,6},{6... | collective-permute-start | bytes 196616 | tf_op jit(solution)/shard_map/ppermute | solution.py:242
  65.7 4.3 %collective-permute-start.15 = (f32[2,64,128]{2,1,0:T(8,128)S(1)}, f32[2,64,128]{2,1,0:T(8,128)S(1)}, u32[]{:S(2)}, u32[]{:S(2)}) collective-permute-start(f32[2,64,128]{2,1,0:T(8,128)S(1)} %get-tuple-element.50), channel_id=1, source_target_pairs={{0,1},{1,0},{4,5},{5,4},{8,9},{9,8},{12,13},{13,12},{2,3},{3,2},{6... | collective-permute-start | bytes 196616 | tf_op jit(solution)/shard_map/ppermute | solution.py:242
  67.2 4.3 %collective-permute-start.14 = (f32[2,64,128]{2,1,0:T(8,128)S(1)}, f32[2,64,128]{2,1,0:T(8,128)S(1)}, u32[]{:S(2)}, u32[]{:S(2)}) collective-permute-start(f32[2,64,128]{2,1,0:T(8,128)S(1)} %get-tuple-element.51), channel_id=1, source_target_pairs={{0,4},{1,5},{4,0},{5,1},{8,12},{9,13},{12,8},{13,9},{2,6},{3,7},{6... | collective-permute-start | bytes 196616 | tf_op jit(solution)/shard_map/ppermute | solution.py:242
  71.5 5.4 %collective-permute-start.16 = (f32[2,64,128]{2,1,0:T(8,128)S(1)}, f32[2,64,128]{2,1,0:T(8,128)S(1)}, u32[]{:S(2)}, u32[]{:S(2)}) collective-permute-start(f32[2,64,128]{2,1,0:T(8,128)S(1)} %add_add_fusion), channel_id=1, source_target_pairs={{0,8},{4,12},{8,0},{12,4},{1,9},{5,13},{9,1},{13,5},{2,10},{6,14},... | collective-permute-start | bytes 196616 | tf_op jit(solution)/shard_map/ppermute | solution.py:242
  76.9 5.8 %collective-permute-start.19 = (f32[2,64,128]{2,1,0:T(8,128)S(1)}, f32[2,64,128]{2,1,0:T(8,128)S(1)}, u32[]{:S(2)}, u32[]{:S(2)}) collective-permute-start(f32[2,64,128]{2,1,0:T(8,128)S(1)} %add.225), channel_id=1, source_target_pairs={{0,5},{1,4},{4,1},{5,0},{8,13},{9,12},{12,9},{13,8},{2,7},{3,6},{6... | collective-permute-start | bytes 196616 | tf_op jit(solution)/shard_map/ppermute | solution.py:242
  77.6 5.1 %collective-permute-start.18 = (f32[2,64,128]{2,1,0:T(8,128)S(1)}, f32[2,64,128]{2,1,0:T(8,128)S(1)}, u32[]{:S(2)}, u32[]{:S(2)}) collective-permute-start(f32[2,64,128]{2,1,0:T(8,128)S(1)} %add.225), channel_id=1, source_target_pairs={{0,1},{1,0},{4,5},{5,4},{8,9},{9,8},{12,13},{13,12},{2,3},{3,2},{6... | collective-permute-start | bytes 196616 | tf_op jit(solution)/shard_map/ppermute | solution.py:242
  78.3 4.4 %collective-permute-start.17 = (f32[2,64,128]{2,1,0:T(8,128)S(1)}, f32[2,64,128]{2,1,0:T(8,128)S(1)}, u32[]{:S(2)}, u32[]{:S(2)}) collective-permute-start(f32[2,64,128]{2,1,0:T(8,128)S(1)} %add.225), channel_id=1, source_target_pairs={{0,4},{1,5},{4,0},{5,1},{8,12},{9,13},{12,8},{13,9},{2,6},{3,7},{6... | collective-permute-start | bytes 196616 | tf_op jit(solution)/shard_map/ppermute | solution.py:242
  90.8 4.9 %collective-permute-start.21 = (bf16[2,64,128]{2,1,0:T(8,128)(2,1)S(1)}, bf16[2,64,128]{2,1,0:T(8,128)(2,1)S(1)}, u32[]{:S(2)}, u32[]{:S(2)}) collective-permute-start(bf16[2,64,128]{2,1,0:T(8,128)(2,1)S(1)} %get-tuple-element.58), channel_id=1, source_target_pairs={{0,5},{1,4},{4,1},{5,0},{8,13},{9,12},{12,9},{13,8},{2,7},{3,6},{6... | collective-permute-start | bytes 98312 | tf_op jit(solution)/shard_map/ppermute | solution.py:242
  93.4 3.9 %collective-permute-start.23 = (bf16[2,64,128]{2,1,0:T(8,128)(2,1)S(1)}, bf16[2,64,128]{2,1,0:T(8,128)(2,1)S(1)}, u32[]{:S(2)}, u32[]{:S(2)}) collective-permute-start(bf16[2,64,128]{2,1,0:T(8,128)(2,1)S(1)} %get-tuple-element.59), channel_id=1, source_target_pairs={{0,1},{1,0},{4,5},{5,4},{8,9},{9,8},{12,13},{13,12},{2,3},{3,2},{6... | collective-permute-start | bytes 98312 | tf_op jit(solution)/shard_map/ppermute | solution.py:242
  94.3 3.9 %collective-permute-start.22 = (bf16[2,64,128]{2,1,0:T(8,128)(2,1)S(1)}, bf16[2,64,128]{2,1,0:T(8,128)(2,1)S(1)}, u32[]{:S(2)}, u32[]{:S(2)}) collective-permute-start(bf16[2,64,128]{2,1,0:T(8,128)(2,1)S(1)} %get-tuple-element.60), channel_id=1, source_target_pairs={{0,4},{1,5},{4,0},{5,1},{8,12},{9,13},{12,8},{13,9},{2,6},{3,7},{6... | collective-permute-start | bytes 98312 | tf_op jit(solution)/shard_map/ppermute | solution.py:242
  98.3 4.9 %collective-permute-start.24 = (bf16[2,64,128]{2,1,0:T(8,128)(2,1)S(1)}, bf16[2,64,128]{2,1,0:T(8,128)(2,1)S(1)}, u32[]{:S(2)}, u32[]{:S(2)}) collective-permute-start(bf16[2,64,128]{2,1,0:T(8,128)(2,1)S(1)} %fusion.21), channel_id=1, source_target_pairs={{0,8},{4,12},{8,0},{12,4},{1,9},{5,13},{9,1},{13,5},{2,10},{6,14},... | collective-permute-start | bytes 98312 | tf_op jit(solution)/shard_map/ppermute | solution.py:242
  103.2 5.0 %collective-permute-start.27 = (bf16[2,64,128]{2,1,0:T(8,128)(2,1)S(1)}, bf16[2,64,128]{2,1,0:T(8,128)(2,1)S(1)}, u32[]{:S(2)}, u32[]{:S(2)}) collective-permute-start(bf16[2,64,128]{2,1,0:T(8,128)(2,1)S(1)} %add_convert_fusion.2), channel_id=1, source_target_pairs={{0,5},{1,4},{4,1},{5,0},{8,13},{9,12},{12,9},{13,8},{2,7},{3,6},{6... | collective-permute-start | bytes 98312 | tf_op jit(solution)/shard_map/ppermute | solution.py:242
  103.9 4.3 %collective-permute-start.26 = (bf16[2,64,128]{2,1,0:T(8,128)(2,1)S(1)}, bf16[2,64,128]{2,1,0:T(8,128)(2,1)S(1)}, u32[]{:S(2)}, u32[]{:S(2)}) collective-permute-start(bf16[2,64,128]{2,1,0:T(8,128)(2,1)S(1)} %add_convert_fusion.2), channel_id=1, source_target_pairs={{0,1},{1,0},{4,5},{5,4},{8,9},{9,8},{12,13},{13,12},{2,3},{3,2},{6... | collective-permute-start | bytes 98312 | tf_op jit(solution)/shard_map/ppermute | solution.py:242
  104.7 3.9 %collective-permute-start.25 = (bf16[2,64,128]{2,1,0:T(8,128)(2,1)S(1)}, bf16[2,64,128]{2,1,0:T(8,128)(2,1)S(1)}, u32[]{:S(2)}, u32[]{:S(2)}) collective-permute-start(bf16[2,64,128]{2,1,0:T(8,128)(2,1)S(1)} %add_convert_fusion.2), channel_id=1, source_target_pairs={{0,4},{1,5},{4,0},{5,1},{8,12},{9,13},{12,8},{13,9},{2,6},{3,7},{6... | collective-permute-start | bytes 98312 | tf_op jit(solution)/shard_map/ppermute | solution.py:242
  115.9 4.9 %collective-permute-start.29 = (bf16[2,64,128]{2,1,0:T(8,128)(2,1)S(1)}, bf16[2,64,128]{2,1,0:T(8,128)(2,1)S(1)}, u32[]{:S(2)}, u32[]{:S(2)}) collective-permute-start(bf16[2,64,128]{2,1,0:T(8,128)(2,1)S(1)} %get-tuple-element.55), channel_id=1, source_target_pairs={{0,5},{1,4},{4,1},{5,0},{8,13},{9,12},{12,9},{13,8},{2,7},{3,6},{6... | collective-permute-start | bytes 98312 | tf_op jit(solution)/shard_map/ppermute | solution.py:242
  123.4 4.9 %collective-permute-start.32 = (bf16[2,64,128]{2,1,0:T(8,128)(2,1)S(1)}, bf16[2,64,128]{2,1,0:T(8,128)(2,1)S(1)}, u32[]{:S(2)}, u32[]{:S(2)}) collective-permute-start(bf16[2,64,128]{2,1,0:T(8,128)(2,1)S(1)} %fusion.18), channel_id=1, source_target_pairs={{0,8},{4,12},{8,0},{12,4},{1,9},{5,13},{9,1},{13,5},{2,10},{6,14},... | collective-permute-start | bytes 98312 | tf_op jit(solution)/shard_map/ppermute | solution.py:242
  128.3 5.0 %collective-permute-start.35 = (bf16[2,64,128]{2,1,0:T(8,128)(2,1)S(1)}, bf16[2,64,128]{2,1,0:T(8,128)(2,1)S(1)}, u32[]{:S(2)}, u32[]{:S(2)}) collective-permute-start(bf16[2,64,128]{2,1,0:T(8,128)(2,1)S(1)} %add_convert_fusion.1), channel_id=1, source_target_pairs={{0,5},{1,4},{4,1},{5,0},{8,13},{9,12},{12,9},{13,8},{2,7},{3,6},{6... | collective-permute-start | bytes 98312 | tf_op jit(solution)/shard_map/ppermute | solution.py:242
  129.0 4.3 %collective-permute-start.34 = (bf16[2,64,128]{2,1,0:T(8,128)(2,1)S(1)}, bf16[2,64,128]{2,1,0:T(8,128)(2,1)S(1)}, u32[]{:S(2)}, u32[]{:S(2)}) collective-permute-start(bf16[2,64,128]{2,1,0:T(8,128)(2,1)S(1)} %add_convert_fusion.1), channel_id=1, source_target_pairs={{0,1},{1,0},{4,5},{5,4},{8,9},{9,8},{12,13},{13,12},{2,3},{3,2},{6... | collective-permute-start | bytes 98312 | tf_op jit(solution)/shard_map/ppermute | solution.py:242
  141.0 4.9 %collective-permute-start.37 = (bf16[2,64,128]{2,1,0:T(8,128)(2,1)S(1)}, bf16[2,64,128]{2,1,0:T(8,128)(2,1)S(1)}, u32[]{:S(2)}, u32[]{:S(2)}) collective-permute-start(bf16[2,64,128]{2,1,0:T(8,128)(2,1)S(1)} %get-tuple-element.52), channel_id=1, source_target_pairs={{0,5},{1,4},{4,1},{5,0},{8,13},{9,12},{12,9},{13,8},{2,7},{3,6},{6... | collective-permute-start | bytes 98312 | tf_op jit(solution)/shard_map/ppermute | solution.py:242
  148.5 4.9 %collective-permute-start.40 = (bf16[2,64,128]{2,1,0:T(8,128)(2,1)S(1)}, bf16[2,64,128]{2,1,0:T(8,128)(2,1)S(1)}, u32[]{:S(2)}, u32[]{:S(2)}) collective-permute-start(bf16[2,64,128]{2,1,0:T(8,128)(2,1)S(1)} %fusion.15), channel_id=1, source_target_pairs={{0,8},{4,12},{8,0},{12,4},{1,9},{5,13},{9,1},{13,5},{2,10},{6,14},... | collective-permute-start | bytes 98312 | tf_op jit(solution)/shard_map/ppermute | solution.py:242
  153.3 5.0 %collective-permute-start.43 = (bf16[2,64,128]{2,1,0:T(8,128)(2,1)S(1)}, bf16[2,64,128]{2,1,0:T(8,128)(2,1)S(1)}, u32[]{:S(2)}, u32[]{:S(2)}) collective-permute-start(bf16[2,64,128]{2,1,0:T(8,128)(2,1)S(1)} %add_convert_fusion), channel_id=1, source_target_pairs={{0,5},{1,4},{4,1},{5,0},{8,13},{9,12},{12,9},{13,8},{2,7},{3,6},{6... | collective-permute-start | bytes 98312 | tf_op jit(solution)/shard_map/ppermute | solution.py:242
  154.0 4.3 %collective-permute-start.42 = (bf16[2,64,128]{2,1,0:T(8,128)(2,1)S(1)}, bf16[2,64,128]{2,1,0:T(8,128)(2,1)S(1)}, u32[]{:S(2)}, u32[]{:S(2)}) collective-permute-start(bf16[2,64,128]{2,1,0:T(8,128)(2,1)S(1)} %add_convert_fusion), channel_id=1, source_target_pairs={{0,1},{1,0},{4,5},{5,4},{8,9},{9,8},{12,13},{13,12},{2,3},{3,2},{6... | collective-permute-start | bytes 98312 | tf_op jit(solution)/shard_map/ppermute | solution.py:242
  (15 other events, 112.1 us)

commit v23 on v21

--- a/solution.py
+++ b/solution.py
@@ -166,9 +166,10 @@
     wide = wide_of(at_ref, z_refs)
     terms = terms_of(wide)
     upper, inverse_one = shifted_factor(wide, terms)
+    rows = ROW_TILE if len(terms) == 1 else wide.shape[1]
     tiles, both = [], 0.0
-    for start in range(0, wide.shape[1], ROW_TILE):
-        part = small_times_wide(inverse_one, [term[:, start : start + ROW_TILE] for term in terms])
+    for start in range(0, wide.shape[1], rows):
+        part = small_times_wide(inverse_one, [term[:, start : start + rows] for term in terms])
         tiles.append(jnp.concatenate(terms_of(part), axis=0))
         both = both + dot_nt(tiles[-1], tiles[-1])
     return jnp.concatenate(tiles, axis=1), fold_gram(both), upper

time: 169 us -> 169 us (level)
  no operation moved by 1% of the time
where the time goes in v23:
time: 169 us; the launch traced here: 168 us
  waiting for transfers between devices  78.6 us (47%)
  starting transfers between devices  45.9 us (27%)
  Pallas kernels  32.5 us (19%)
  local copies, waits for them, and re-layouts  5.55 us (3%)
  matrix products  3.83 us (2%)
    ppermute x45, waiting for transfers between devices, from_xor(): return lax.ppermute(value, axis, [(i, i ^ offset) for i in range(size)])  78.6 us
    ppermute x45, starting transfers between devices, from_xor(): return lax.ppermute(value, axis, [(i, i ^ offset) for i in range(size)])  45.9 us
    pallas_call x7, Pallas kernels, call(): pl.pallas_call(kernel, out_shape=out_shapes, in_specs=[pl.BlockSpec(memor...  32.5 us
    dot_general x1, matrix products, per_device_transposed(): lax.dot_general(omega, states, (((0,), (1,)), ((), ())), preferred_elemen...  3.83 us
  transfers between devices with their start and end apart: 45, of which 33 were waited for; matrix products, arithmetic and copies ran while one was open for 3% of the time, Pallas kernels for 4%

profile of v23, /device:TPU:0, one launch (start us, length us, event | category | flops | bytes accessed | tf_op | source)
XLA Modules:
  0.0 168.4 jit_solution(4262874514641395195)
XLA Ops:
  2.1 3.1 %collective-permute-start.3 = (bf16[256,1024]{1,0:T(8,128)(2,1)S(1)}, bf16[256,1024]{1,0:T(8,128)(2,1)S(1)}, u32[]{:S(2)}, u32[]{:S(2)}) collective-permute-start(bf16[256,1024]{1,0:T(8,128)(2,1)S(1)} %get-tuple-element.44), channel_id=1, source_target_pairs={{0,4},{4,0},{8,12},{12,8},{1,5},{5,1},{9,13},{13,9},{2,6},{6,2},{1... | collective-permute-start | bytes 1572872 | tf_op jit(solution)/shard_map/ppermute | solution.py:253
  5.2 2.6 %collective-permute-start.2 = (bf16[256,1024]{1,0:T(8,128)(2,1)S(1)}, bf16[256,1024]{1,0:T(8,128)(2,1)S(1)}, u32[]{:S(2)}, u32[]{:S(2)}) collective-permute-start(bf16[256,1024]{1,0:T(8,128)(2,1)S(1)} %get-tuple-element.46), channel_id=1, source_target_pairs={{0,8},{4,12},{8,0},{12,4},{1,9},{5,13},{9,1},{13,5},{2,10},{6,14},... | collective-permute-start | bytes 1572872 | tf_op jit(solution)/shard_map/ppermute | solution.py:253
  8.5 3.8 %convolution_bitcast_fusion = f32[8,2,8,128]{3,2,1,0:T(8,128)S(1)} fusion(bf16[256,4096]{1,0:T(8,128)(2,1)} %param.3, s32[]{:T(128)S(6)} %xor.73, s32[4096]{0:T(1024)S(1)} %add_multiply_fusion), kind=kOutput, calls=%fused_computation | convolution fusion | flops 152043520 | bytes 2179076 | tf_op jit(solution)/shard_map/dot_general | solution.py:328
  13.8 19.8 %collective-permute-done = f32[2,64,128]{2,1,0:T(8,128)S(1)} collective-permute-done((f32[2,64,128]{2,1,0:T(8,128)S(1)}, f32[2,64,128]{2,1,0:T(8,128)S(1)}, u32[]{:S(2)}, u32[]{:S(2)}) %collective-permute-start) | collective-permute-done | bytes 65568 | tf_op jit(solution)/shard_map/ppermute | solution.py:253
  33.6 1.6 collective-permute-start.1
  35.2 3.0 %collective-permute-start.5 = (bf16[128,1024]{1,0:T(8,128)(2,1)S(1)}, bf16[128,1024]{1,0:T(8,128)(2,1)S(1)}, u32[]{:S(2)}, u32[]{:S(2)}) collective-permute-start(bf16[128,1024]{1,0:T(8,128)(2,1)S(1)} %get-tuple-element.22), channel_id=1, source_target_pairs={{0,12},{4,8},{8,4},{12,0},{1,13},{5,9},{9,5},{13,1},{2,14},{6,10},... | collective-permute-start | bytes 786440 | tf_op jit(solution)/shard_map/ppermute | solution.py:253
  38.8 7.7 %collective-permute-done.4 = f32[4,64,128]{2,1,0:T(8,128)S(1)} collective-permute-done((f32[4,64,128]{2,1,0:T(8,128)S(1)}, f32[4,64,128]{2,1,0:T(8,128)S(1)}, u32[]{:S(2)}, u32[]{:S(2)}) %collective-permute-start.4) | collective-permute-done | bytes 131104 | tf_op jit(solution)/shard_map/ppermute | solution.py:253
  46.6 2.5 %collective-permute-start.7 = (bf16[128,1024]{1,0:T(8,128)(2,1)S(1)}, bf16[128,1024]{1,0:T(8,128)(2,1)S(1)}, u32[]{:S(2)}, u32[]{:S(2)}) collective-permute-start(bf16[128,1024]{1,0:T(8,128)(2,1)S(1)} %get-tuple-element.26), channel_id=1, source_target_pairs={{0,12},{4,8},{8,4},{12,0},{1,13},{5,9},{9,5},{13,1},{2,14},{6,10},... | collective-permute-start | bytes 786440 | tf_op jit(solution)/shard_map/ppermute | solution.py:253
  49.9 5.9 %shard_map.41 = (bf16[64,2048]{1,0:T(8,128)(2,1)S(1)}, f32[64,64]{1,0:T(8,128)S(1)}) custom-call(s32[8]{0:T(128)S(1)} %fusion.24.at_ref, f32[8,64,128]{2,1,0:T(8,128)S(1)} %pad_maximum_fusion.z_ref, f32[8,64,128]{2,1,0:T(8,128)S(1)} %collective-permute-done.6.other_ref), custom_call_target="tpu_custom_call" | custom-call | flops 402653184 | bytes 524288 | tf_op jit(solution)/shard_map/pallas_call | solution.py:236
  59.2 2.1 %shard_map.42 = (bf16[2048,1024]{1,0:T(8,128)(2,1)S(1)}, f32[8,64,128]{2,1,0:T(8,128)S(1)}) custom-call(s32[8]{0:T(128)S(1)} %fusion.22.at_ref, bf16[64,2048]{1,0:T(8,128)(2,1)S(1)} %get-tuple-element.27.basis_ref, bf16[256,1024]{1,0:T(8,128)(2,1)S(1)} %get-tuple-element.28.refs_0_, bf16[256,1024]{1,0:T(8,128)(2,1)S(1)} %collective-permute-done.3.refs_1_, ...), custom_call_target="tpu_custom_call" | custom-call | flops 939524096 | bytes 4456448 | tf_op jit(solution)/shard_map/pallas_call | solution.py:236
  61.3 4.4 %collective-permute-start.13 = (f32[2,64,128]{2,1,0:T(8,128)S(1)}, f32[2,64,128]{2,1,0:T(8,128)S(1)}, u32[]{:S(2)}, u32[]{:S(2)}) collective-permute-start(f32[2,64,128]{2,1,0:T(8,128)S(1)} %get-tuple-element.49), channel_id=1, source_target_pairs={{0,5},{1,4},{4,1},{5,0},{8,13},{9,12},{12,9},{13,8},{2,7},{3,6},{6... | collective-permute-start | bytes 196616 | tf_op jit(solution)/shard_map/ppermute | solution.py:253
  68.1 1.9 %collective-permute-done.15 = f32[2,64,128]{2,1,0:T(8,128)S(1)} collective-permute-done((f32[2,64,128]{2,1,0:T(8,128)S(1)}, f32[2,64,128]{2,1,0:T(8,128)S(1)}, u32[]{:S(2)}, u32[]{:S(2)}) %collective-permute-start.15) | collective-permute-done | bytes 65568 | tf_op jit(solution)/shard_map/ppermute | solution.py:253
  72.2 4.7 %collective-permute-done.16 = f32[2,64,128]{2,1,0:T(8,128)S(1)} collective-permute-done((f32[2,64,128]{2,1,0:T(8,128)S(1)}, f32[2,64,128]{2,1,0:T(8,128)S(1)}, u32[]{:S(2)}, u32[]{:S(2)}) %collective-permute-start.16) | collective-permute-done | bytes 65568 | tf_op jit(solution)/shard_map/ppermute | solution.py:253
  78.3 2.2 %collective-permute-start.17 = (f32[2,64,128]{2,1,0:T(8,128)S(1)}, f32[2,64,128]{2,1,0:T(8,128)S(1)}, u32[]{:S(2)}, u32[]{:S(2)}) collective-permute-start(f32[2,64,128]{2,1,0:T(8,128)S(1)} %add.225), channel_id=1, source_target_pairs={{0,4},{1,5},{4,0},{5,1},{8,12},{9,13},{12,8},{13,9},{2,6},{3,7},{6... | collective-permute-start | bytes 196616 | tf_op jit(solution)/shard_map/ppermute | solution.py:253
  80.5 2.2 %collective-permute-done.17 = f32[2,64,128]{2,1,0:T(8,128)S(1)} collective-permute-done((f32[2,64,128]{2,1,0:T(8,128)S(1)}, f32[2,64,128]{2,1,0:T(8,128)S(1)}, u32[]{:S(2)}, u32[]{:S(2)}) %collective-permute-start.17) | collective-permute-done | bytes 65568 | tf_op jit(solution)/shard_map/ppermute | solution.py:253
  84.4 6.4 %shard_map.44 = f32[8,64,128]{2,1,0:T(8,128)S(1)} custom-call(s32[8]{0:T(128)S(1)} %fusion.22.at_ref, f32[8,64,128]{2,1,0:T(8,128)S(1)} %constant_dynamic-update-slice_fusion.z_ref, f32[8,64,128]{2,1,0:T(8,128)S(1)} %collective-permute-done.20.other_ref, bf16[2048,1024]{1,0:T(8,128)(2,1)S(1)} %get-tuple-element.34.a_ref, ...), custom_call_target="tpu_custom_call" | custom-call | flops 939524096 | bytes 6815744 | tf_op jit(solution)/shard_map/pallas_call | solution.py:236
  90.8 2.6 %collective-permute-start.21 = (bf16[2,64,128]{2,1,0:T(8,128)(2,1)S(1)}, bf16[2,64,128]{2,1,0:T(8,128)(2,1)S(1)}, u32[]{:S(2)}, u32[]{:S(2)}) collective-permute-start(bf16[2,64,128]{2,1,0:T(8,128)(2,1)S(1)} %get-tuple-element.58), channel_id=1, source_target_pairs={{0,5},{1,4},{4,1},{5,0},{8,13},{9,12},{12,9},{13,8},{2,7},{3,6},{6... | collective-permute-start | bytes 98312 | tf_op jit(solution)/shard_map/ppermute | solution.py:253
  95.7 1.6 collective-permute-done.23
  98.4 4.8 %collective-permute-done.24 = bf16[2,64,128]{2,1,0:T(8,128)(2,1)S(1)} collective-permute-done((bf16[2,64,128]{2,1,0:T(8,128)(2,1)S(1)}, bf16[2,64,128]{2,1,0:T(8,128)(2,1)S(1)}, u32[]{:S(2)}, u32[]{:S(2)}) %collective-permute-start.24) | collective-permute-done | bytes 32800 | tf_op jit(solution)/shard_map/ppermute | solution.py:253
  104.7 2.0 %collective-permute-start.25 = (bf16[2,64,128]{2,1,0:T(8,128)(2,1)S(1)}, bf16[2,64,128]{2,1,0:T(8,128)(2,1)S(1)}, u32[]{:S(2)}, u32[]{:S(2)}) collective-permute-start(bf16[2,64,128]{2,1,0:T(8,128)(2,1)S(1)} %add_convert_fusion.2), channel_id=1, source_target_pairs={{0,4},{1,5},{4,0},{5,1},{8,12},{9,13},{12,8},{13,9},{2,6},{3,7},{6... | collective-permute-start | bytes 98312 | tf_op jit(solution)/shard_map/ppermute | solution.py:253
  110.1 5.7 %shard_map.45 = f32[8,64,128]{2,1,0:T(8,128)S(1)} custom-call(s32[8]{0:T(128)S(1)} %fusion.22.at_ref, bf16[8,64,128]{2,1,0:T(8,128)(2,1)S(1)} %pad_maximum_fusion.2.z_ref, bf16[8,64,128]{2,1,0:T(8,128)(2,1)S(1)} %collective-permute-done.28.other_ref, bf16[2048,1024]{1,0:T(8,128)(2,1)S(1)} %get-tuple-element.34.a_ref, bf16[1024,1024]{1,0:T(8,128)(2,1)S(1)} %shard_map.43.turned_ref), custom_call_target="tpu_custom_call" | custom-call | flops 939524096 | bytes 6553600 | tf_op jit(solution)/shard_map/pallas_call | solution.py:236
  115.8 2.6 %collective-permute-start.29 = (bf16[2,64,128]{2,1,0:T(8,128)(2,1)S(1)}, bf16[2,64,128]{2,1,0:T(8,128)(2,1)S(1)}, u32[]{:S(2)}, u32[]{:S(2)}) collective-permute-start(bf16[2,64,128]{2,1,0:T(8,128)(2,1)S(1)} %get-tuple-element.55), channel_id=1, source_target_pairs={{0,5},{1,4},{4,1},{5,0},{8,13},{9,12},{12,9},{13,8},{2,7},{3,6},{6... | collective-permute-start | bytes 98312 | tf_op jit(solution)/shard_map/ppermute | solution.py:253
  120.7 1.6 collective-permute-done.31
  123.4 4.8 %collective-permute-done.32 = bf16[2,64,128]{2,1,0:T(8,128)(2,1)S(1)} collective-permute-done((bf16[2,64,128]{2,1,0:T(8,128)(2,1)S(1)}, bf16[2,64,128]{2,1,0:T(8,128)(2,1)S(1)}, u32[]{:S(2)}, u32[]{:S(2)}) %collective-permute-start.32) | collective-permute-done | bytes 32800 | tf_op jit(solution)/shard_map/ppermute | solution.py:253
  129.7 2.0 %collective-permute-start.33 = (bf16[2,64,128]{2,1,0:T(8,128)(2,1)S(1)}, bf16[2,64,128]{2,1,0:T(8,128)(2,1)S(1)}, u32[]{:S(2)}, u32[]{:S(2)}) collective-permute-start(bf16[2,64,128]{2,1,0:T(8,128)(2,1)S(1)} %add_convert_fusion.1), channel_id=1, source_target_pairs={{0,4},{1,5},{4,0},{5,1},{8,12},{9,13},{12,8},{13,9},{2,6},{3,7},{6... | collective-permute-start | bytes 98312 | tf_op jit(solution)/shard_map/ppermute | solution.py:253
  135.1 5.7 %shard_map.46 = f32[8,64,128]{2,1,0:T(8,128)S(1)} custom-call(s32[8]{0:T(128)S(1)} %fusion.22.at_ref, bf16[8,64,128]{2,1,0:T(8,128)(2,1)S(1)} %pad_maximum_fusion.3.z_ref, bf16[8,64,128]{2,1,0:T(8,128)(2,1)S(1)} %collective-permute-done.36.other_ref, bf16[2048,1024]{1,0:T(8,128)(2,1)S(1)} %get-tuple-element.34.a_ref, bf16[1024,1024]{1,0:T(8,128)(2,1)S(1)} %shard_map.43.turned_ref), custom_call_target="tpu_custom_call" | custom-call | flops 939524096 | bytes 6553600 | tf_op jit(solution)/shard_map/pallas_call | solution.py:236
  140.8 2.6 %collective-permute-start.37 = (bf16[2,64,128]{2,1,0:T(8,128)(2,1)S(1)}, bf16[2,64,128]{2,1,0:T(8,128)(2,1)S(1)}, u32[]{:S(2)}, u32[]{:S(2)}) collective-permute-start(bf16[2,64,128]{2,1,0:T(8,128)(2,1)S(1)} %get-tuple-element.52), channel_id=1, source_target_pairs={{0,5},{1,4},{4,1},{5,0},{8,13},{9,12},{12,9},{13,8},{2,7},{3,6},{6... | collective-permute-start | bytes 98312 | tf_op jit(solution)/shard_map/ppermute | solution.py:253
  145.7 1.6 collective-permute-done.39
  148.4 4.8 %collective-permute-done.40 = bf16[2,64,128]{2,1,0:T(8,128)(2,1)S(1)} collective-permute-done((bf16[2,64,128]{2,1,0:T(8,128)(2,1)S(1)}, bf16[2,64,128]{2,1,0:T(8,128)(2,1)S(1)}, u32[]{:S(2)}, u32[]{:S(2)}) %collective-permute-start.40) | collective-permute-done | bytes 32800 | tf_op jit(solution)/shard_map/ppermute | solution.py:253
  154.7 2.0 %collective-permute-start.41 = (bf16[2,64,128]{2,1,0:T(8,128)(2,1)S(1)}, bf16[2,64,128]{2,1,0:T(8,128)(2,1)S(1)}, u32[]{:S(2)}, u32[]{:S(2)}) collective-permute-start(bf16[2,64,128]{2,1,0:T(8,128)(2,1)S(1)} %add_convert_fusion), channel_id=1, source_target_pairs={{0,4},{1,5},{4,0},{5,1},{8,12},{9,13},{12,8},{13,9},{2,6},{3,7},{6... | collective-permute-start | bytes 98312 | tf_op jit(solution)/shard_map/ppermute | solution.py:253
  160.1 2.2 %copy-done.1 = bf16[2048,1024]{1,0:T(8,128)(2,1)S(1)} copy-done((bf16[2048,1024]{1,0:T(8,128)(2,1)S(1)}, bf16[2048,1024]{1,0:T(8,128)(2,1)}, u32[]{:S(2)}) %copy-start.1) | copy-done | bytes 4194328
  162.3 6.1 %shard_map.47 = f32[64,512]{1,0:T(8,128)} custom-call(s32[8]{0:T(128)S(1)} %fusion.22.at_ref, s32[1]{0:T(128)} %bitcast.core_ref, bf16[8,64,128]{2,1,0:T(8,128)(2,1)S(1)} %pad_maximum_fusion.4.z_ref, bf16[8,64,128]{2,1,0:T(8,128)(2,1)S(1)} %collective-permute-done.44.other_ref, bf16[2048,1024]{1,0:T(8,128)(2,1)S(1)} %copy-done.1), custom_call_target="tpu_custom_call" | custom-call | flops 939524096 | bytes 4456448 | tf_op jit(solution)/shard_map/pallas_call | solution.py:236
  (103 shorter events, 40.2 us)
Async XLA Ops:
  2.1 36.5 %collective-permute-start.3 = (bf16[256,1024]{1,0:T(8,128)(2,1)S(1)}, bf16[256,1024]{1,0:T(8,128)(2,1)S(1)}, u32[]{:S(2)}, u32[]{:S(2)}) collective-permute-start(bf16[256,1024]{1,0:T(8,128)(2,1)S(1)} %get-tuple-element.44), channel_id=1, source_target_pairs={{0,4},{4,0},{8,12},{12,8},{1,5},{5,1},{9,13},{13,9},{2,6},{6,2},{1... | collective-permute-start | bytes 1572872 | tf_op jit(solution)/shard_map/ppermute | solution.py:253
  5.2 33.5 %collective-permute-start.2 = (bf16[256,1024]{1,0:T(8,128)(2,1)S(1)}, bf16[256,1024]{1,0:T(8,128)(2,1)S(1)}, u32[]{:S(2)}, u32[]{:S(2)}) collective-permute-start(bf16[256,1024]{1,0:T(8,128)(2,1)S(1)} %get-tuple-element.46), channel_id=1, source_target_pairs={{0,8},{4,12},{8,0},{12,4},{1,9},{5,13},{9,1},{13,5},{2,10},{6,14},... | collective-permute-start | bytes 1572872 | tf_op jit(solution)/shard_map/ppermute | solution.py:253
  12.4 21.2 %collective-permute-start = (f32[2,64,128]{2,1,0:T(8,128)S(1)}, f32[2,64,128]{2,1,0:T(8,128)S(1)}, u32[]{:S(2)}, u32[]{:S(2)}) collective-permute-start(f32[2,64,128]{2,1,0:T(8,128)S(1)} %bitcast.16), channel_id=1, source_target_pairs={{0,8},{4,12},{8,0},{12,4},{1,9},{5,13},{9,1},{13,5},{2,10},{6,14},... | collective-permute-start | bytes 196616 | tf_op jit(solution)/shard_map/ppermute | solution.py:253
  33.6 5.0 %collective-permute-start.1 = (f32[4,64,128]{2,1,0:T(8,128)S(1)}, f32[4,64,128]{2,1,0:T(8,128)S(1)}, u32[]{:S(2)}, u32[]{:S(2)}) collective-permute-start(f32[4,64,128]{2,1,0:T(8,128)S(1)} %pad_maximum_fusion.1), channel_id=1, source_target_pairs={{0,1},{1,0},{2,3},{3,2},{4,5},{5,4},{6,7},{7,6},{8,9},{9,8},{10,11... | collective-permute-start | bytes 393224 | tf_op jit(solution)/shard_map/ppermute | solution.py:253
  35.2 11.4 %collective-permute-start.5 = (bf16[128,1024]{1,0:T(8,128)(2,1)S(1)}, bf16[128,1024]{1,0:T(8,128)(2,1)S(1)}, u32[]{:S(2)}, u32[]{:S(2)}) collective-permute-start(bf16[128,1024]{1,0:T(8,128)(2,1)S(1)} %get-tuple-element.22), channel_id=1, source_target_pairs={{0,12},{4,8},{8,4},{12,0},{1,13},{5,9},{9,5},{13,1},{2,14},{6,10},... | collective-permute-start | bytes 786440 | tf_op jit(solution)/shard_map/ppermute | solution.py:253
  38.7 7.8 %collective-permute-start.4 = (f32[4,64,128]{2,1,0:T(8,128)S(1)}, f32[4,64,128]{2,1,0:T(8,128)S(1)}, u32[]{:S(2)}, u32[]{:S(2)}) collective-permute-start(f32[4,64,128]{2,1,0:T(8,128)S(1)} %add.218), channel_id=1, source_target_pairs={{0,4},{4,0},{8,12},{12,8},{1,5},{5,1},{9,13},{13,9},{2,6},{6,2},{1... | collective-permute-start | bytes 393224 | tf_op jit(solution)/shard_map/ppermute | solution.py:253
  46.6 10.6 %collective-permute-start.7 = (bf16[128,1024]{1,0:T(8,128)(2,1)S(1)}, bf16[128,1024]{1,0:T(8,128)(2,1)S(1)}, u32[]{:S(2)}, u32[]{:S(2)}) collective-permute-start(bf16[128,1024]{1,0:T(8,128)(2,1)S(1)} %get-tuple-element.26), channel_id=1, source_target_pairs={{0,12},{4,8},{8,4},{12,0},{1,13},{5,9},{9,5},{13,1},{2,14},{6,10},... | collective-permute-start | bytes 786440 | tf_op jit(solution)/shard_map/ppermute | solution.py:253
  49.2 8.6 %collective-permute-start.8 = (bf16[256,1024]{1,0:T(8,128)(2,1)S(1)}, bf16[256,1024]{1,0:T(8,128)(2,1)S(1)}, u32[]{:S(2)}, u32[]{:S(2)}) collective-permute-start(bf16[256,1024]{1,0:T(8,128)(2,1)S(1)} %get-tuple-element.28.refs_0_), channel_id=1, source_target_pairs={{0,2},{2,0},{1,3},{3,1},{4,6},{6,4},{5,7},{7,5},{8,10},{10,8},{9,1... | collective-permute-start | bytes 1572872 | tf_op jit(solution)/shard_map/ppermute | solution.py:253
  49.3 8.5 %collective-permute-start.9 = (bf16[256,1024]{1,0:T(8,128)(2,1)S(1)}, bf16[256,1024]{1,0:T(8,128)(2,1)S(1)}, u32[]{:S(2)}, u32[]{:S(2)}) collective-permute-start(bf16[256,1024]{1,0:T(8,128)(2,1)S(1)} %collective-permute-done.3.refs_1_), channel_id=1, source_target_pairs={{0,2},{2,0},{1,3},{3,1},{4,6},{6,4},{5,7},{7,5},{8,10},{10,8},{9,1... | collective-permute-start | bytes 1572872 | tf_op jit(solution)/shard_map/ppermute | solution.py:253
  49.7 8.1 %collective-permute-start.10 = (bf16[256,1024]{1,0:T(8,128)(2,1)S(1)}, bf16[256,1024]{1,0:T(8,128)(2,1)S(1)}, u32[]{:S(2)}, u32[]{:S(2)}) collective-permute-start(bf16[256,1024]{1,0:T(8,128)(2,1)S(1)} %collective-permute-done.2.refs_2_), channel_id=1, source_target_pairs={{0,2},{2,0},{1,3},{3,1},{4,6},{6,4},{5,7},{7,5},{8,10},{10,8},{9,1... | collective-permute-start | bytes 1572872 | tf_op jit(solution)/shard_map/ppermute | solution.py:253
  61.3 6.8 %collective-permute-start.13 = (f32[2,64,128]{2,1,0:T(8,128)S(1)}, f32[2,64,128]{2,1,0:T(8,128)S(1)}, u32[]{:S(2)}, u32[]{:S(2)}) collective-permute-start(f32[2,64,128]{2,1,0:T(8,128)S(1)} %get-tuple-element.49), channel_id=1, source_target_pairs={{0,5},{1,4},{4,1},{5,0},{8,13},{9,12},{12,9},{13,8},{2,7},{3,6},{6... | collective-permute-start | bytes 196616 | tf_op jit(solution)/shard_map/ppermute | solution.py:253
  65.7 4.3 %collective-permute-start.15 = (f32[2,64,128]{2,1,0:T(8,128)S(1)}, f32[2,64,128]{2,1,0:T(8,128)S(1)}, u32[]{:S(2)}, u32[]{:S(2)}) collective-permute-start(f32[2,64,128]{2,1,0:T(8,128)S(1)} %get-tuple-element.50), channel_id=1, source_target_pairs={{0,1},{1,0},{4,5},{5,4},{8,9},{9,8},{12,13},{13,12},{2,3},{3,2},{6... | collective-permute-start | bytes 196616 | tf_op jit(solution)/shard_map/ppermute | solution.py:253
  67.2 4.3 %collective-permute-start.14 = (f32[2,64,128]{2,1,0:T(8,128)S(1)}, f32[2,64,128]{2,1,0:T(8,128)S(1)}, u32[]{:S(2)}, u32[]{:S(2)}) collective-permute-start(f32[2,64,128]{2,1,0:T(8,128)S(1)} %get-tuple-element.51), channel_id=1, source_target_pairs={{0,4},{1,5},{4,0},{5,1},{8,12},{9,13},{12,8},{13,9},{2,6},{3,7},{6... | collective-permute-start | bytes 196616 | tf_op jit(solution)/shard_map/ppermute | solution.py:253
  71.5 5.4 %collective-permute-start.16 = (f32[2,64,128]{2,1,0:T(8,128)S(1)}, f32[2,64,128]{2,1,0:T(8,128)S(1)}, u32[]{:S(2)}, u32[]{:S(2)}) collective-permute-start(f32[2,64,128]{2,1,0:T(8,128)S(1)} %add_add_fusion), channel_id=1, source_target_pairs={{0,8},{4,12},{8,0},{12,4},{1,9},{5,13},{9,1},{13,5},{2,10},{6,14},... | collective-permute-start | bytes 196616 | tf_op jit(solution)/shard_map/ppermute | solution.py:253
  76.9 5.8 %collective-permute-start.19 = (f32[2,64,128]{2,1,0:T(8,128)S(1)}, f32[2,64,128]{2,1,0:T(8,128)S(1)}, u32[]{:S(2)}, u32[]{:S(2)}) collective-permute-start(f32[2,64,128]{2,1,0:T(8,128)S(1)} %add.225), channel_id=1, source_target_pairs={{0,5},{1,4},{4,1},{5,0},{8,13},{9,12},{12,9},{13,8},{2,7},{3,6},{6... | collective-permute-start | bytes 196616 | tf_op jit(solution)/shard_map/ppermute | solution.py:253
  77.6 5.1 %collective-permute-start.18 = (f32[2,64,128]{2,1,0:T(8,128)S(1)}, f32[2,64,128]{2,1,0:T(8,128)S(1)}, u32[]{:S(2)}, u32[]{:S(2)}) collective-permute-start(f32[2,64,128]{2,1,0:T(8,128)S(1)} %add.225), channel_id=1, source_target_pairs={{0,1},{1,0},{4,5},{5,4},{8,9},{9,8},{12,13},{13,12},{2,3},{3,2},{6... | collective-permute-start | bytes 196616 | tf_op jit(solution)/shard_map/ppermute | solution.py:253
  78.3 4.4 %collective-permute-start.17 = (f32[2,64,128]{2,1,0:T(8,128)S(1)}, f32[2,64,128]{2,1,0:T(8,128)S(1)}, u32[]{:S(2)}, u32[]{:S(2)}) collective-permute-start(f32[2,64,128]{2,1,0:T(8,128)S(1)} %add.225), channel_id=1, source_target_pairs={{0,4},{1,5},{4,0},{5,1},{8,12},{9,13},{12,8},{13,9},{2,6},{3,7},{6... | collective-permute-start | bytes 196616 | tf_op jit(solution)/shard_map/ppermute | solution.py:253
  90.8 4.9 %collective-permute-start.21 = (bf16[2,64,128]{2,1,0:T(8,128)(2,1)S(1)}, bf16[2,64,128]{2,1,0:T(8,128)(2,1)S(1)}, u32[]{:S(2)}, u32[]{:S(2)}) collective-permute-start(bf16[2,64,128]{2,1,0:T(8,128)(2,1)S(1)} %get-tuple-element.58), channel_id=1, source_target_pairs={{0,5},{1,4},{4,1},{5,0},{8,13},{9,12},{12,9},{13,8},{2,7},{3,6},{6... | collective-permute-start | bytes 98312 | tf_op jit(solution)/shard_map/ppermute | solution.py:253
  93.4 3.9 %collective-permute-start.23 = (bf16[2,64,128]{2,1,0:T(8,128)(2,1)S(1)}, bf16[2,64,128]{2,1,0:T(8,128)(2,1)S(1)}, u32[]{:S(2)}, u32[]{:S(2)}) collective-permute-start(bf16[2,64,128]{2,1,0:T(8,128)(2,1)S(1)} %get-tuple-element.59), channel_id=1, source_target_pairs={{0,1},{1,0},{4,5},{5,4},{8,9},{9,8},{12,13},{13,12},{2,3},{3,2},{6... | collective-permute-start | bytes 98312 | tf_op jit(solution)/shard_map/ppermute | solution.py:253
  94.3 3.9 %collective-permute-start.22 = (bf16[2,64,128]{2,1,0:T(8,128)(2,1)S(1)}, bf16[2,64,128]{2,1,0:T(8,128)(2,1)S(1)}, u32[]{:S(2)}, u32[]{:S(2)}) collective-permute-start(bf16[2,64,128]{2,1,0:T(8,128)(2,1)S(1)} %get-tuple-element.60), channel_id=1, source_target_pairs={{0,4},{1,5},{4,0},{5,1},{8,12},{9,13},{12,8},{13,9},{2,6},{3,7},{6... | collective-permute-start | bytes 98312 | tf_op jit(solution)/shard_map/ppermute | solution.py:253
  98.3 4.9 %collective-permute-start.24 = (bf16[2,64,128]{2,1,0:T(8,128)(2,1)S(1)}, bf16[2,64,128]{2,1,0:T(8,128)(2,1)S(1)}, u32[]{:S(2)}, u32[]{:S(2)}) collective-permute-start(bf16[2,64,128]{2,1,0:T(8,128)(2,1)S(1)} %fusion.21), channel_id=1, source_target_pairs={{0,8},{4,12},{8,0},{12,4},{1,9},{5,13},{9,1},{13,5},{2,10},{6,14},... | collective-permute-start | bytes 98312 | tf_op jit(solution)/shard_map/ppermute | solution.py:253
  103.2 5.0 %collective-permute-start.27 = (bf16[2,64,128]{2,1,0:T(8,128)(2,1)S(1)}, bf16[2,64,128]{2,1,0:T(8,128)(2,1)S(1)}, u32[]{:S(2)}, u32[]{:S(2)}) collective-permute-start(bf16[2,64,128]{2,1,0:T(8,128)(2,1)S(1)} %add_convert_fusion.2), channel_id=1, source_target_pairs={{0,5},{1,4},{4,1},{5,0},{8,13},{9,12},{12,9},{13,8},{2,7},{3,6},{6... | collective-permute-start | bytes 98312 | tf_op jit(solution)/shard_map/ppermute | solution.py:253
  103.9 4.3 %collective-permute-start.26 = (bf16[2,64,128]{2,1,0:T(8,128)(2,1)S(1)}, bf16[2,64,128]{2,1,0:T(8,128)(2,1)S(1)}, u32[]{:S(2)}, u32[]{:S(2)}) collective-permute-start(bf16[2,64,128]{2,1,0:T(8,128)(2,1)S(1)} %add_convert_fusion.2), channel_id=1, source_target_pairs={{0,1},{1,0},{4,5},{5,4},{8,9},{9,8},{12,13},{13,12},{2,3},{3,2},{6... | collective-permute-start | bytes 98312 | tf_op jit(solution)/shard_map/ppermute | solution.py:253
  104.7 3.9 %collective-permute-start.25 = (bf16[2,64,128]{2,1,0:T(8,128)(2,1)S(1)}, bf16[2,64,128]{2,1,0:T(8,128)(2,1)S(1)}, u32[]{:S(2)}, u32[]{:S(2)}) collective-permute-start(bf16[2,64,128]{2,1,0:T(8,128)(2,1)S(1)} %add_convert_fusion.2), channel_id=1, source_target_pairs={{0,4},{1,5},{4,0},{5,1},{8,12},{9,13},{12,8},{13,9},{2,6},{3,7},{6... | collective-permute-start | bytes 98312 | tf_op jit(solution)/shard_map/ppermute | solution.py:253
  115.8 4.9 %collective-permute-start.29 = (bf16[2,64,128]{2,1,0:T(8,128)(2,1)S(1)}, bf16[2,64,128]{2,1,0:T(8,128)(2,1)S(1)}, u32[]{:S(2)}, u32[]{:S(2)}) collective-permute-start(bf16[2,64,128]{2,1,0:T(8,128)(2,1)S(1)} %get-tuple-element.55), channel_id=1, source_target_pairs={{0,5},{1,4},{4,1},{5,0},{8,13},{9,12},{12,9},{13,8},{2,7},{3,6},{6... | collective-permute-start | bytes 98312 | tf_op jit(solution)/shard_map/ppermute | solution.py:253
  123.3 4.9 %collective-permute-start.32 = (bf16[2,64,128]{2,1,0:T(8,128)(2,1)S(1)}, bf16[2,64,128]{2,1,0:T(8,128)(2,1)S(1)}, u32[]{:S(2)}, u32[]{:S(2)}) collective-permute-start(bf16[2,64,128]{2,1,0:T(8,128)(2,1)S(1)} %fusion.18), channel_id=1, source_target_pairs={{0,8},{4,12},{8,0},{12,4},{1,9},{5,13},{9,1},{13,5},{2,10},{6,14},... | collective-permute-start | bytes 98312 | tf_op jit(solution)/shard_map/ppermute | solution.py:253
  128.2 5.0 %collective-permute-start.35 = (bf16[2,64,128]{2,1,0:T(8,128)(2,1)S(1)}, bf16[2,64,128]{2,1,0:T(8,128)(2,1)S(1)}, u32[]{:S(2)}, u32[]{:S(2)}) collective-permute-start(bf16[2,64,128]{2,1,0:T(8,128)(2,1)S(1)} %add_convert_fusion.1), channel_id=1, source_target_pairs={{0,5},{1,4},{4,1},{5,0},{8,13},{9,12},{12,9},{13,8},{2,7},{3,6},{6... | collective-permute-start | bytes 98312 | tf_op jit(solution)/shard_map/ppermute | solution.py:253
  128.9 4.3 %collective-permute-start.34 = (bf16[2,64,128]{2,1,0:T(8,128)(2,1)S(1)}, bf16[2,64,128]{2,1,0:T(8,128)(2,1)S(1)}, u32[]{:S(2)}, u32[]{:S(2)}) collective-permute-start(bf16[2,64,128]{2,1,0:T(8,128)(2,1)S(1)} %add_convert_fusion.1), channel_id=1, source_target_pairs={{0,1},{1,0},{4,5},{5,4},{8,9},{9,8},{12,13},{13,12},{2,3},{3,2},{6... | collective-permute-start | bytes 98312 | tf_op jit(solution)/shard_map/ppermute | solution.py:253
  140.8 4.9 %collective-permute-start.37 = (bf16[2,64,128]{2,1,0:T(8,128)(2,1)S(1)}, bf16[2,64,128]{2,1,0:T(8,128)(2,1)S(1)}, u32[]{:S(2)}, u32[]{:S(2)}) collective-permute-start(bf16[2,64,128]{2,1,0:T(8,128)(2,1)S(1)} %get-tuple-element.52), channel_id=1, source_target_pairs={{0,5},{1,4},{4,1},{5,0},{8,13},{9,12},{12,9},{13,8},{2,7},{3,6},{6... | collective-permute-start | bytes 98312 | tf_op jit(solution)/shard_map/ppermute | solution.py:253
  148.3 4.9 %collective-permute-start.40 = (bf16[2,64,128]{2,1,0:T(8,128)(2,1)S(1)}, bf16[2,64,128]{2,1,0:T(8,128)(2,1)S(1)}, u32[]{:S(2)}, u32[]{:S(2)}) collective-permute-start(bf16[2,64,128]{2,1,0:T(8,128)(2,1)S(1)} %fusion.15), channel_id=1, source_target_pairs={{0,8},{4,12},{8,0},{12,4},{1,9},{5,13},{9,1},{13,5},{2,10},{6,14},... | collective-permute-start | bytes 98312 | tf_op jit(solution)/shard_map/ppermute | solution.py:253
  153.2 5.0 %collective-permute-start.43 = (bf16[2,64,128]{2,1,0:T(8,128)(2,1)S(1)}, bf16[2,64,128]{2,1,0:T(8,128)(2,1)S(1)}, u32[]{:S(2)}, u32[]{:S(2)}) collective-permute-start(bf16[2,64,128]{2,1,0:T(8,128)(2,1)S(1)} %add_convert_fusion), channel_id=1, source_target_pairs={{0,5},{1,4},{4,1},{5,0},{8,13},{9,12},{12,9},{13,8},{2,7},{3,6},{6... | collective-permute-start | bytes 98312 | tf_op jit(solution)/shard_map/ppermute | solution.py:253
  153.9 4.3 %collective-permute-start.42 = (bf16[2,64,128]{2,1,0:T(8,128)(2,1)S(1)}, bf16[2,64,128]{2,1,0:T(8,128)(2,1)S(1)}, u32[]{:S(2)}, u32[]{:S(2)}) collective-permute-start(bf16[2,64,128]{2,1,0:T(8,128)(2,1)S(1)} %add_convert_fusion), channel_id=1, source_target_pairs={{0,1},{1,0},{4,5},{5,4},{8,9},{9,8},{12,13},{13,12},{2,3},{3,2},{6... | collective-permute-start | bytes 98312 | tf_op jit(solution)/shard_map/ppermute | solution.py:253
  (15 other events, 112.0 us)
